TPU v7x, 32 devices: a whole 2x2x4 slice. The times are simulated.
32 devices in a mesh: seq: 2 (over x), mp: 4 (over y, core), dp: 4 (over z).
Axes of the slice: x: 2, y: 2, z: 4, core: 2. Of those that a mesh axis runs over, the one named last changes fastest.
Arguments:
- block_input: bfloat16 [4, 2048, 1280], P('dp', 'seq', 'mp'), may hold values from -6 to 6
- conv_weight: bfloat16 [5, 1280, 1536], P(None, None, 'mp'), as said below
- norm_gain: float32 [1536], P('mp'), may hold values from 0.1 to 1.9
- qkv_weight: bfloat16 [1536, 2560], P(None, 'mp'), may hold values from -0.15625 to 0.15625
- encoder_grad: bfloat16 [4, 1024, 1536], P('dp', 'seq', 'mp'), may hold values from -6 to 6
Outputs:
- qkv: bfloat16 [4, 1024, 2560], P('dp', 'seq', 'mp')
- conv_grad: float32 [1280, 5, 1536], P('seq', None, 'mp')
Inputs may be any that keep to these rules, and one draw needn't show every extreme that they name: `conv_weight`: output channel o's kernel column carries a scale factor that varies with o; input channels differ in scale.
All inputs are finite; a program needn't handle non-finite values.
Results may differ from a plain program's by a relative error of at most 0.019.
Values may be sent and summed in bfloat16 or wider, within the bound.
No kernel may reach another device: no remote copies, remote signals or barrier semaphores. Data moves between devices by JAX's collectives and lax.ppermute only.
A program may use at most 64 MiB of HBM per device.

v0:
```python
import jax
import jax.numpy as jnp
from jax import lax
from jax.sharding import PartitionSpec as P

KW = 5


def padded_2(value, sides, width):
    for axis, dim in sides:
        peers, length = (lax.axis_size(axis), value.shape[dim])
        up = [(i, (i + 1) % peers) for i in range(peers - 1)]
        down = [(j, i) for i, j in up]
        last = lax.slice_in_dim(value, length - width, length, axis=dim)
        initial = lax.slice_in_dim(value, 0, width, axis=dim)
        before = lax.ppermute(last, axis, up)
        after = lax.ppermute(initial, axis, down)
        value = jnp.concatenate([before, value, after], axis=dim)
    return value


def gelu_value(v):
    u = 0.7978845608 * (v + 0.044715 * v * v * v)
    return 0.5 * v * (1.0 + jnp.tanh(u))


def gelu_slope(v):
    u = 0.7978845608 * (v + 0.044715 * v * v * v)
    th = jnp.tanh(u)
    return 0.5 * (1.0 + th) + 0.5 * v * (1.0 - th * th) * 0.7978845608 * (1.0 + 0.134145 * v * v)


def on_device(block_input, conv_weight, norm_gain, qkv_weight, encoder_grad):
    local_input = block_input[0]
    length = local_input.shape[0]
    whole = lax.all_gather(local_input, "mp", axis=1, tiled=True)
    padded = padded_2(whole, (("seq", 0),), 2)
    pre = jnp.zeros((length, conv_weight.shape[2]), jnp.float32)
    for k in range(KW):
        pre = pre + jnp.dot(
            padded[k : k + length], conv_weight[k], preferred_element_type=jnp.float32
        )
    act = gelu_value(pre)
    encoded = (0.5 * (act[0::2] + act[1::2])).astype(jnp.bfloat16)
    values = encoded.astype(jnp.float32)
    channels = values.shape[1] * lax.axis_size("mp")
    sums, squares = lax.psum((jnp.sum(values, axis=1), jnp.sum(values * values, axis=1)), "mp")
    mean = sums[:, None] / channels
    var = squares[:, None] / channels - mean * mean
    normalized = ((values - mean) * lax.rsqrt(var + 1e-05) * norm_gain).astype(jnp.bfloat16)
    qkv = jnp.dot(
        lax.all_gather(normalized, "mp", axis=1, tiled=True),
        qkv_weight,
        preferred_element_type=jnp.float32,
    ).astype(jnp.bfloat16)
    spread = jnp.repeat(encoder_grad[0].astype(jnp.float32), 2, axis=0)
    pre_grad = (gelu_slope(pre) * 0.5 * spread).astype(jnp.bfloat16)
    terms = [
        lax.dot_general(
            padded[k : k + length],
            pre_grad,
            (((0,), (0,)), ((), ())),
            preferred_element_type=jnp.float32,
        )
        for k in range(KW)
    ]
    share = lax.psum_scatter(
        jnp.stack(terms, axis=1).astype(jnp.bfloat16), "seq", scatter_dimension=0, tiled=True
    )
    conv_grad = lax.psum(share, "dp").astype(jnp.float32)
    return (qkv[None], conv_grad)


def solution(mesh):
    return jax.shard_map(
        on_device,
        mesh=mesh,
        in_specs=(
            P("dp", "seq", "mp"),
            P(None, None, "mp"),
            P("mp"),
            P(None, "mp"),
            P("dp", "seq", "mp"),
        ),
        out_specs=(P("dp", "seq", "mp"), P("seq", None, "mp")),
        check_vma=False,
    )
```

profile of v0, /device:TPU:0, one launch (start us, length us, event | category | flops | bytes accessed | tf_op | source)
XLA Modules:
  0.0 269.9 jit_solution(15245404691919216207)
XLA Ops:
  7.2 0.0 copy-start
  7.2 0.0 all-gather.6.cloned.1.call-start
  7.2 0.7 all-gather.6.cloned.1.call-update
  7.9 0.0 reduce-scatter.2.cloned.1.call-start
  8.0 1.0 bitcast_convert_fusion
  9.0 0.5 broadcast_in_dim.10
  9.6 2.2 reshape.18
  11.8 1.9 copy.9
  13.7 24.2 %all-gather.6.cloned.1.call-done = bf16[1,1024,1280]{1,2,0:T(8,128)(2,1)} async-done(((bf16[1,1024,320]{1,2,0:T(8,128)(2,1)}), bf16[1,1024,1280]{1,2,0:T(8,128)(2,1)}) %all-gather.6.cloned.1.call-update) | async-done | bytes 2621456 | tf_op jit(solution)/shard_map/all_gather | solution.py:36
  37.9 1.2 slice_bitcast_fusion.1
  39.1 3.4 %collective-permute-start = (bf16[2,1280]{0,1:T(8,128)(2,1)S(1)}, bf16[2,1280]{0,1:T(8,128)(2,1)S(1)}, u32[]{:S(2)}, u32[]{:S(2)}) collective-permute-start(bf16[2,1280]{0,1:T(8,128)(2,1)S(1)} %get-tuple-element.7), channel_id=1, source_target_pairs={{0,16},{1,17},{2,18},{3,19},{4,20},{5,21},{6,22},{7,23},{8,24},{9,... | collective-permute-start | bytes 15368 | tf_op jit(solution)/shard_map/ppermute | solution.py:16
  42.5 0.0 copy-start.1
  42.5 1.7 collective-permute-start.1
  44.3 0.0 slice-start
  44.3 3.4 %fusion.26 = f32[1024,384]{0,1:T(8,128)S(1)} fusion(bf16[5,1280,384]{2,1,0:T(8,128)(2,1)} %param.6, bf16[1,1024,1280]{1,2,0:T(8,128)(2,1)} %all-gather.6.cloned.1.call-done), kind=kOutput, calls=%fused_computation.45 | convolution fusion | flops 1006632960 | bytes 5177344 | tf_op jit(solution)/shard_map/dot_general | solution.py:40
  47.6 2.2 collective-permute-done
  49.8 0.0 copy-done.1
  49.8 0.0 slice-start.1
  49.8 2.8 %fusion.29 = f32[1024,384]{0,1:T(8,128)S(1)} fusion(bf16[5,1280,384]{2,1,0:T(8,128)(2,1)} %param.6, bf16[2,1280]{0,1:T(8,128)(2,1)S(1)} %collective-permute-done, bf16[1024,1280]{0,1:T(8,128)(2,1)S(1)} %bitcast.60), kind=kOutput, calls=%fused_computation.48 | convolution fusion | flops 1011875840 | bytes 5182464 | tf_op jit(solution)/shard_map/dot_general | solution.py:40
  52.6 0.0 slice-done
  52.6 0.0 slice-done.1
  52.6 1.5 fusion.20
  54.2 0.1 collective-permute-done.1
  54.2 1.5 fusion.24
  55.8 3.8 %fusion.19 = (bf16[1024,384]{0,1:T(8,128)(2,1)S(1)}, f32[1024,384]{0,1:T(8,128)}) fusion(f32[1024,384]{0,1:T(8,128)S(1)} %copy.9, bf16[5,1280,384]{2,1,0:T(8,128)(2,1)S(1)} %bitcast.69, bf16[2,1280]{0,1:T(8,128)(2,1)S(1)} %collective-permute-done.1, bf16[1024,1280]{0,1:T(8,128)(2,1)S(1)} %bitcast.63, f32[1024,384]{0,1:T(8,128)S(1)} %fusion.24, ...), kind=kOutput, calls=%fused_computation.32 | convolution fusion | flops 1021706240 | bytes 14155776 | tf_op jit(solution)/shard_map/dot_general | solution.py:40
  59.6 2.5 fusion.3
  62.1 2.5 fusion.5
  64.7 2.7 %fusion.7 = bf16[1280,5,384]{2,0,1:T(8,128)(2,1)} fusion(bf16[1280,5,384]{2,0,1:T(8,128)(2,1)} %fusion.5, bf16[1024,384]{0,1:T(8,128)(2,1)S(1)} %get-tuple-element.9, bf16[1,1024,1280]{1,2,0:T(8,128)(2,1)S(1)} %copy-done.1), kind=kOutput, calls=%fused_computation.18 | convolution fusion | flops 1007124480 | bytes 4390912 | tf_op jit(solution)/shard_map/dot_general | solution.py:59
  67.4 2.5 fusion.9
  69.9 2.5 fusion.11
  72.4 0.0 reduce-scatter.2.cloned.1.call-update
  72.5 0.0 copy-start.2
  72.5 0.0 all-gather.4.cloned.1.call-start
  72.5 27.9 %slice.59 = f32[512,384]{0,1:T(8,128)S(1)} slice(f32[1024,384]{0,1:T(8,128)} %get-tuple-element.10), slice={[1:1024:2], [0:384:1]} | slice | bytes 1572864 | tf_op jit(solution)/shard_map/slice | solution.py:44
  100.4 27.9 %slice.58 = f32[512,384]{0,1:T(8,128)S(1)} slice(f32[1024,384]{0,1:T(8,128)} %get-tuple-element.10), slice={[0:1024:2], [0:384:1]} | slice | bytes 1572864 | tf_op jit(solution)/shard_map/slice | solution.py:44
  128.3 0.9 convert_reduce_fusion
  129.2 6.0 %all-reduce = (f32[512]{0:T(512)S(1)}, f32[512]{0:T(512)S(1)}) all-reduce(f32[512]{0:T(512)S(1)} %get-tuple-element.3, f32[512]{0:T(512)S(1)} %get-tuple-element.2), channel_id=1, replica_groups=mesh['seq'=2,'mp'=4,'dp'=4] {'mp'}, use_global_device_ids=true, to_apply=%region_3.0 | all-reduce | flops 1024 | bytes 8192 | tf_op jit(solution)/shard_map/psum | solution.py:47
  135.3 0.0 copy-done.2
  135.3 1.9 fusion.38
  137.2 0.0 all-gather.4.cloned.1.call-update
  137.2 0.0 all-reduce.3.cloned.1.call-start
  137.2 0.0 reduce-scatter.2.cloned.1.call-done
  137.3 0.5 all-reduce.3.cloned.1.call-update
  137.8 20.3 %all-gather.4.cloned.1.call-done = bf16[512,1536]{0,1:T(8,128)(2,1)} async-done(((bf16[512,384]{0,1:T(8,128)(2,1)}), bf16[512,1536]{0,1:T(8,128)(2,1)}) %all-gather.4.cloned.1.call-update) | async-done | bytes 1572880 | tf_op jit(solution)/shard_map/all_gather | solution.py:52
  158.0 0.0 copy-done
  158.0 3.7 %fusion.22 = bf16[1,512,640]{2,1,0:T(8,128)(2,1)} fusion(bf16[512,1536]{0,1:T(8,128)(2,1)} %all-gather.4.cloned.1.call-done, bf16[1536,640]{1,0:T(8,128)(2,1)S(1)} %copy-done), kind=kOutput, calls=%fused_computation.38 | convolution fusion | flops 1006960640 | bytes 4194304 | tf_op jit(solution)/shard_map/dot_general | solution.py:51
  161.7 97.4 %all-reduce.3.cloned.1.call-done = bf16[640,5,384]{2,0,1:T(8,128)(2,1)} async-done(((bf16[640,5,384]{2,0,1:T(8,128)(2,1)}), bf16[640,5,384]{2,0,1:T(8,128)(2,1)}) %all-reduce.3.cloned.1.call-update) | async-done | bytes 2457616 | tf_op jit(solution)/shard_map/psum | solution.py:70
  259.1 4.3 %convert_element_type.32 = f32[640,5,384]{2,0,1:T(8,128)} convert(bf16[640,5,384]{2,0,1:T(8,128)(2,1)} %all-reduce.3.cloned.1.call-done) | non-fusion elementwise | flops 1228800 | bytes 7372800 | tf_op jit(solution)/shard_map/convert_element_type | solution.py:70
  (2 shorter events, 0.0 us)
Async XLA Ops:
  7.2 150.9 %copy-start = (bf16[1536,640]{1,0:T(8,128)(2,1)S(1)}, bf16[1536,640]{1,0:T(8,128)(2,1)}, u32[]{:S(2)}) copy-start(bf16[1536,640]{1,0:T(8,128)(2,1)} %param.8) | copy-start | bytes 5898244
  7.2 30.7 %all-gather.6.cloned.1.call-start = ((), (), s32[]{:S(2)}) async-start(), calls=%async_computation.4 | async-start | bytes 3276800 | tf_op jit(solution)/shard_map/all_gather | solution.py:36
  7.9 129.3 %reduce-scatter.2.cloned.1.call-start = ((), (), s32[]{:S(2)}) async-start(), calls=%async_computation.2 | async-start | bytes 7372800 | tf_op jit(solution)/shard_map/reduce_scatter | solution.py:67
  39.1 10.7 %collective-permute-start = (bf16[2,1280]{0,1:T(8,128)(2,1)S(1)}, bf16[2,1280]{0,1:T(8,128)(2,1)S(1)}, u32[]{:S(2)}, u32[]{:S(2)}) collective-permute-start(bf16[2,1280]{0,1:T(8,128)(2,1)S(1)} %get-tuple-element.7), channel_id=1, source_target_pairs={{0,16},{1,17},{2,18},{3,19},{4,20},{5,21},{6,22},{7,23},{8,24},{9,... | collective-permute-start | bytes 15368 | tf_op jit(solution)/shard_map/ppermute | solution.py:16
  42.5 7.3 %copy-start.1 = (bf16[1,1024,1280]{1,2,0:T(8,128)(2,1)S(1)}, bf16[1,1024,1280]{1,2,0:T(8,128)(2,1)}, u32[]{:S(2)}) copy-start(bf16[1,1024,1280]{1,2,0:T(8,128)(2,1)} %all-gather.6.cloned.1.call-done) | copy-start | bytes 7864324
  42.5 11.7 %collective-permute-start.1 = (bf16[2,1280]{0,1:T(8,128)(2,1)S(1)}, bf16[2,1280]{0,1:T(8,128)(2,1)S(1)}, u32[]{:S(2)}, u32[]{:S(2)}) collective-permute-start(bf16[2,1280]{0,1:T(8,128)(2,1)S(1)} %get-tuple-element.8), channel_id=1, source_target_pairs={{16,0},{17,1},{18,2},{19,3},{20,4},{21,5},{22,6},{23,7},{24,8},{25... | collective-permute-start | bytes 15368 | tf_op jit(solution)/shard_map/ppermute | solution.py:17
  44.3 8.3 %slice-start = ((s8[4915200]{0:T(1024)(128)(4,1)}), s8[4194304]{0:T(1024)(128)(4,1)S(1)}, s32[]{:S(2)}) async-start(s8[4915200]{0:T(1024)(128)(4,1)} %bitcast.68), calls=%async_computation.5 | async-start | bytes 8388608
  49.8 2.8 %slice-start.1 = ((s8[4915200]{0:T(1024)(128)(4,1)}), s8[720896]{0:T(1024)(128)(4,1)S(1)}, s32[]{:S(2)}) async-start(s8[4915200]{0:T(1024)(128)(4,1)} %bitcast.68), calls=%async_computation.6 | async-start | bytes 1441792
  72.5 62.8 %copy-start.2 = (f32[384]{0:T(512)S(1)}, f32[384]{0:T(512)}, u32[]{:S(2)}) copy-start(f32[384]{0:T(512)} %param.7) | copy-start | bytes 4612
  72.5 85.5 %all-gather.4.cloned.1.call-start = ((), (), s32[]{:S(2)}) async-start(), calls=%async_computation.1 | async-start | bytes 1966080 | tf_op jit(solution)/shard_map/all_gather | solution.py:52
  137.2 121.9 %all-reduce.3.cloned.1.call-start = ((), (), s32[]{:S(2)}) async-start(), calls=%async_computation.3 | async-start | bytes 4915200 | tf_op jit(solution)/shard_map/psum | solution.py:70
Sparse Core Ops, SparseCore 0:
  9.6 28.2 all-gather.5
  72.6 63.0 reduce-scatter.1
  137.8 20.1 all-gather.3
  160.3 98.7 all-reduce.2
where the time goes:
time: 270 us
  waiting for transfers between devices  145 us (54%)
  local copies, waits for them, and re-layouts  61.6 us (23%)
  matrix products  29.5 us (11%)
  between operations  13.9 us (5%)
  other arithmetic  8.17 us (3%)
  blocking collectives  6.04 us (2%)
  starting transfers between devices  5.29 us (2%)
    psum x1, waiting for transfers between devices, on_device(): conv_grad = lax.psum(share, 'dp').astype(jnp.float32)  97.4 us
    slice x2, local copies, waits for them, and re-layouts, on_device(): encoded = (0.5 * (act[0::2] + act[1::2])).astype(jnp.bfloat16)  55.7 us
    all_gather x1, waiting for transfers between devices, on_device(): whole = lax.all_gather(local_input, 'mp', axis=1, tiled=True)  24.2 us
    all_gather x1, waiting for transfers between devices, on_device(): lax.all_gather(normalized, 'mp', axis=1, tiled=True)  20.3 us
    dot_general x5, matrix products, on_device(): jnp.dot(padded[k:k + length], conv_weight[k], preferred_element_type=jnp....  12.9 us
    dot_general x5, matrix products, on_device(): lax.dot_general(padded[k:k + length], pre_grad, (((0,), (0,)), ((), ())),...  12.9 us
    psum x1, blocking collectives, on_device(): lax.psum((jnp.sum(values, axis=1), jnp.sum(values * values, axis=1)), 'mp')  6.04 us
  transfers between devices with their start and end apart: 6, of which 5 were waited for; matrix products, arithmetic and copies ran while one was open for 28% of the time, Pallas kernels for 0%

commit v1 on v0

v1 whole, which is shorter than its diff:
```python
import functools

import jax
import jax.numpy as jnp
from jax import lax
from jax.experimental import pallas as pl
from jax.experimental.pallas import tpu as pltpu
from jax.sharding import PartitionSpec as P

EDGE = 8
LANES = 128
VMEM_BYTES = 56 * 1024 * 1024
F32 = jnp.float32
BF16 = jnp.bfloat16


def gelu_parts(v):
    u = 0.7978845608 * (v + 0.044715 * v * v * v)
    th = jnp.tanh(u)
    value = 0.5 * v * (1.0 + th)
    slope = 0.5 * (1.0 + th) + 0.5 * v * (1.0 - th * th) * 0.7978845608 * (1.0 + 0.134145 * v * v)
    return value, slope


def swap(value, axis, bit):
    peers = lax.axis_size(axis)
    return lax.ppermute(value, axis, [(i, i ^ bit) for i in range(peers)])


def conv_rows(offsets, me, x_refs, halo_refs, w_ref, rows_scr, y_scr):
    taps, width = w_ref.shape[0], w_ref.shape[2]
    depth, length = x_refs[0].shape
    x = jnp.concatenate([ref[...] for ref in x_refs], axis=0)
    halo = jnp.concatenate([ref[...] for ref in halo_refs], axis=0)
    rows_scr[0:length, :] = x.T
    rows_scr[length : length + 16, :] = halo.T[0:16]
    starts = [pl.multiple_of((me ^ off) * depth, 16) for off in offsets]
    for first in range(0, taps, 2):
        group = range(first, min(first + 2, taps))
        w = jnp.concatenate(
            [
                jnp.concatenate([w_ref[k, pl.ds(s, depth), :] for s in starts], axis=0)
                for k in group
            ],
            axis=1,
        )
        y = jnp.dot(rows_scr[...], w, preferred_element_type=F32)
        for c in range(w.shape[1] // LANES):
            part = y[:, c * LANES : (c + 1) * LANES]
            at = first * width // LANES + c
            y_scr[at, EDGE : EDGE + length, :] = part[0:length]
            y_scr[at, EDGE - 2 : EDGE, :] = part[length : length + 2]
            y_scr[at, EDGE + length : EDGE + length + 2, :] = part[length + 2 : length + 4]


def tap_sum(y_scr, start, count, phase, taps, c):
    total = None
    for k in range(taps):
        at = k * (y_scr.shape[0] // taps) + c
        part = y_scr[at, pl.ds(EDGE + 2 * start + phase + k - 2, count, stride=2), :]
        total = part if total is None else total + part
    return total


def first_kernel(offsets, idx_ref, *refs):
    n = len(offsets)
    x_refs, halo_refs, (w_ref, even_ref, odd_ref, rows_scr, y_scr) = refs[:n], refs[n : 2 * n], refs[2 * n :]
    conv_rows(offsets, idx_ref[0], x_refs, halo_refs, w_ref, rows_scr, y_scr)
    taps, width = w_ref.shape[0], w_ref.shape[2]
    half = even_ref.shape[0]
    step = min(64, half)
    for start in range(0, half, step):
        rows = slice(start, start + step)
        for c in range(width // LANES):
            lanes = slice(c * LANES, (c + 1) * LANES)
            even_ref[rows, lanes] = tap_sum(y_scr, start, step, 0, taps, c)
            odd_ref[rows, lanes] = tap_sum(y_scr, start, step, 1, taps, c)


def second_kernel(offsets, idx_ref, *refs):
    n = len(offsets)
    x_refs, halo_refs = refs[:n], refs[n : 2 * n]
    w_ref, even_ref, odd_ref, grad_ref, enc_ref, pre_ref, rows_scr, y_scr, p_scr = refs[2 * n :]
    conv_rows(offsets, idx_ref[0], x_refs, halo_refs, w_ref, rows_scr, y_scr)
    taps, width = w_ref.shape[0], w_ref.shape[2]
    half = even_ref.shape[0]
    step = min(64, half)
    length = 2 * half
    zero = jnp.zeros((EDGE, width), F32)
    pre_ref[0:EDGE, :] = zero
    pre_ref[EDGE + length : 2 * EDGE + length, :] = zero
    for start in range(0, half, step):
        rows = slice(start, start + step)
        for c in range(width // LANES):
            lanes = slice(c * LANES, (c + 1) * LANES)
            even = even_ref[rows, lanes] + tap_sum(y_scr, start, step, 0, taps, c)
            odd = odd_ref[rows, lanes] + tap_sum(y_scr, start, step, 1, taps, c)
            act_even, slope_even = gelu_parts(even)
            act_odd, slope_odd = gelu_parts(odd)
            enc_ref[rows, lanes] = (0.5 * (act_even + act_odd)).astype(BF16)
            spread = grad_ref[rows, lanes].astype(F32)
            p_scr[c, pl.ds(2 * start, step, stride=2), :] = slope_even * 0.5 * spread
            p_scr[c, pl.ds(2 * start + 1, step, stride=2), :] = slope_odd * 0.5 * spread
    for c in range(width // LANES):
        lanes = slice(c * LANES, (c + 1) * LANES)
        pre_ref[EDGE : EDGE + length, lanes] = p_scr[c].astype(BF16).astype(F32)


def grad_kernel(offsets, tap, shards, idx_ref, *refs):
    n = len(offsets)
    x_refs, halo_refs, (p_ref, *out_refs, edge_scr) = refs[:n], refs[n : 2 * n], refs[2 * n :]
    depth, length = x_refs[0].shape
    edge_scr[...] = jnp.zeros_like(edge_scr)
    edge_scr[0:2, :] = p_ref[EDGE - tap : EDGE - tap + 2, :]
    edge_scr[2:4, :] = p_ref[EDGE + length + 2 - tap : EDGE + length + 4 - tap, :]
    p = p_ref[EDGE + 2 - tap : EDGE + 2 - tap + length, :].astype(BF16)
    edge = edge_scr[...].astype(BF16)
    me = idx_ref[0]
    x = jnp.concatenate([ref[...] for ref in x_refs], axis=0)
    halo = jnp.concatenate([ref[...] for ref in halo_refs], axis=0)
    res = jnp.dot(x, p, preferred_element_type=F32) + jnp.dot(halo, edge, preferred_element_type=F32)
    res = res.astype(BF16)
    for j, off in enumerate(offsets):
        part = res[j * depth : (j + 1) * depth]
        at = me ^ off
        if len(out_refs) == 1:
            out_refs[0][pl.ds(pl.multiple_of(at * depth, 16), depth), :] = part
            continue
        per = n // shards
        row = pl.multiple_of(lax.rem(at, per) * depth, 16)
        mine = lax.div(at, per) == idx_ref[1]

        @pl.when(mine)
        def _():
            out_refs[0][pl.ds(row, depth), :] = part

        @pl.when(jnp.logical_not(mine))
        def _():
            out_refs[1][pl.ds(row, depth), :] = part


def qkv_kernel(offsets, idx_ref, *refs):
    n = len(offsets)
    enc_refs, gain_refs, (w_ref, out_ref) = refs[:n], refs[n : 2 * n], refs[2 * n :]
    depth = enc_refs[0].shape[1]
    values = [ref[...].astype(F32) for ref in enc_refs]
    channels = n * depth
    sums = sum(jnp.sum(v, axis=1, keepdims=True) for v in values)
    squares = sum(jnp.sum(v * v, axis=1, keepdims=True) for v in values)
    mean = sums / channels
    var = squares / channels - mean * mean
    scale = lax.rsqrt(var + 1e-05)
    total = None
    for off, v, gain_ref in zip(offsets, values, gain_refs):
        normal = ((v - mean) * scale * gain_ref[...]).astype(BF16)
        w = w_ref[pl.ds(pl.multiple_of((idx_ref[0] ^ off) * depth, 16), depth), :]
        part = jnp.dot(normal, w, preferred_element_type=F32)
        total = part if total is None else total + part
    out_ref[...] = total.astype(BF16)


def call(kernel, out, scratch, idx, *arrays):
    vmem = pl.BlockSpec(memory_space=pltpu.VMEM)
    return pl.pallas_call(
        kernel,
        out_shape=out,
        in_specs=[pl.BlockSpec(memory_space=pltpu.SMEM)] + [vmem] * len(arrays),
        out_specs=jax.tree.map(lambda _: vmem, out),
        scratch_shapes=scratch,
        compiler_params=pltpu.CompilerParams(vmem_limit_bytes=VMEM_BYTES),
    )(idx, *arrays)


def edge_columns(x):
    peers = lax.axis_size("seq")
    up = [(i, (i + 1) % peers) for i in range(peers - 1)]
    down = [(j, i) for i, j in up]
    length = x.shape[1]
    before = lax.ppermute(x[:, length - 2 :], "seq", up)
    after = lax.ppermute(x[:, :2], "seq", down)
    return jnp.concatenate([before, after], axis=1)


def gathered(value, axis, bits):
    blocks, offsets = [value], [0]
    for bit in bits:
        blocks = blocks + [swap(b, axis, bit) for b in blocks]
        offsets = offsets + [o ^ bit for o in offsets]
    return blocks, offsets


def chain_sum(part, axis):
    peers = lax.axis_size(axis)
    if peers % 2:
        return lax.psum(part, axis)
    me = lax.axis_index(axis)
    half = peers // 2
    total = part
    for i in range(half - 1):
        got = lax.ppermute(total, axis, [(i, i + 1), (peers - 1 - i, peers - 2 - i)])
        total = (total.astype(F32) + got.astype(F32)).astype(BF16)
    got = lax.ppermute(total, axis, [(half - 1, half), (half, half - 1)])
    total = (total.astype(F32) + got.astype(F32)).astype(BF16)
    for i in reversed(range(half - 1)):
        got = lax.ppermute(total, axis, [(i + 1, i), (peers - 2 - i, peers - 1 - i)])
        total = jnp.where(jnp.logical_or(me == i, me == peers - 1 - i), got, total)
    return total


def on_device(block_input, conv_weight, norm_gain, qkv_weight, encoder_grad):
    x = jnp.swapaxes(block_input[0], 0, 1)
    depth, length = x.shape
    taps, _, width = conv_weight.shape
    peers, shards = lax.axis_size("mp"), lax.axis_size("seq")
    bits = [1 << b for b in reversed(range(peers.bit_length() - 1))]
    idx = jnp.stack([lax.axis_index("mp"), lax.axis_index("seq")]).astype(jnp.int32)

    blocks, offsets = gathered(x, "mp", bits)
    edges, _ = gathered(edge_columns(x), "mp", bits)
    halos = [jnp.pad(e, ((0, 0), (0, LANES - e.shape[1]))) for e in edges]
    gains, _ = gathered(norm_gain.reshape(1, -1), "mp", bits)

    near = [j for j, o in enumerate(offsets) if o < 2]
    far = [j for j, o in enumerate(offsets) if o >= 2]
    half = length // 2
    pick = lambda items, at: [items[j] for j in at]
    scratch = lambda at: [
        pltpu.VMEM((length + 16, len(at) * depth), BF16),
        pltpu.VMEM((taps * width // LANES, length + 2 * EDGE, LANES), F32),
    ]
    part = jax.ShapeDtypeStruct((half, width), F32)
    even, odd = call(
        functools.partial(first_kernel, pick(offsets, near)),
        (part, part),
        scratch(near),
        idx, *pick(blocks, near), *pick(halos, near), conv_weight,
    )
    encoded, pre_grad = call(
        functools.partial(second_kernel, pick(offsets, far)),
        (jax.ShapeDtypeStruct((half, width), BF16), jax.ShapeDtypeStruct((length + 2 * EDGE, width), F32)),
        scratch(far) + [pltpu.VMEM((width // LANES, length, LANES), F32)],
        idx, *pick(blocks, far), *pick(halos, far), conv_weight, even, odd, encoder_grad[0],
    )

    total = peers * depth
    pair = shards == 2 and peers % shards == 0
    rows = total // shards if pair else total
    sums = []
    for k in range(taps):
        outs = call(
            functools.partial(grad_kernel, offsets, k, shards),
            (jax.ShapeDtypeStruct((rows, width), BF16),) * (2 if pair else 1),
            [pltpu.VMEM((LANES, width), F32)],
            idx, *blocks, *halos, pre_grad,
        )
        if pair:
            got = swap(outs[1], "seq", 1)
            share = (outs[0].astype(F32) + got.astype(F32)).astype(BF16)
        else:
            share = lax.psum_scatter(outs[0], "seq", scatter_dimension=0, tiled=True)
        sums.append(chain_sum(share, "dp"))
    conv_grad = jnp.stack([s.astype(F32) for s in sums], axis=1)

    encs, _ = gathered(encoded, "mp", bits)
    qkv = call(
        functools.partial(qkv_kernel, offsets),
        jax.ShapeDtypeStruct((half, qkv_weight.shape[1]), BF16),
        [],
        idx, *encs, *gains, qkv_weight,
    )
    return (qkv[None], conv_grad)


def solution(mesh):
    return jax.shard_map(
        on_device,
        mesh=mesh,
        in_specs=(
            P("dp", "seq", "mp"),
            P(None, None, "mp"),
            P("mp"),
            P(None, "mp"),
            P("dp", "seq", "mp"),
        ),
        out_specs=(P("dp", "seq", "mp"), P("seq", None, "mp")),
        check_vma=False,
    )
```

time: 270 us -> 227 us (0.84)
  local copies, waits for them, and re-layouts: 61.6 us -> 5.59 us
  Pallas kernels: 0 us -> 48.9 us
  starting transfers between devices: 5.29 us -> 36.8 us
  matrix products: 29.5 us -> 0 us
  waiting for transfers between devices: 145 us -> 128 us
  between operations: 13.9 us -> 1.21 us
  blocking collectives: 6.04 us -> 0 us
    ppermute x2 -> x34, waiting for transfers between devices: 2.31 us -> 128 us  [the longest x5 51.3 us: chain_sum(): lax.ppermute(total, axis, [(i + 1, i), (peers - 2 - i, peers - 1 - i)])]
    psum x1 -> x0, waiting for transfers between devices: 97.4 us -> none  [on_device(): conv_grad = lax.psum(share, 'dp').astype(jnp.float32)]
    slice x3 -> x1, local copies, waits for them, and re-layouts: 57 us -> 1.21 us  [edge_columns(): before = lax.ppermute(x[:, length - 2:], 'seq', up)]
    pallas_call x0 -> x8, Pallas kernels: none -> 48.9 us  [call(): pl.pallas_call(kernel, out_shape=out, in_specs=[pl.BlockSpec(memory_space...]
    all_gather x2 -> x0, waiting for transfers between devices: 44.5 us -> none  [the longest x1 24.2 us: on_device(): whole = lax.all_gather(local_input, 'mp', axis=1, tiled=True)]
    ppermute x2 -> x34, starting transfers between devices: 5.13 us -> 36.8 us  [the longest x17 11.1 us: swap(): return lax.ppermute(value, axis, [(i, i ^ bit) for i in range(peers)])]
    dot_general x11 -> x0, matrix products: 29.5 us -> none  [the longest x5 12.9 us: on_device(): jnp.dot(padded[k:k + length], conv_weight[k], preferred_element_type=jnp....]
    psum x1 -> x0, blocking collectives: 6.04 us -> none  [on_device(): lax.psum((jnp.sum(values, axis=1), jnp.sum(values * values, axis=1)), 'mp')]
  transfers between devices with their start and end apart: 6 -> 34, of which waited for: 5 -> 15; matrix products, arithmetic and copies ran while one was open for 28% -> 3% of each run, Pallas kernels for 0% -> 15%
where the time goes in v1:
time: 227 us; the launch traced here: 226 us
  waiting for transfers between devices  128 us (56%)
  Pallas kernels  48.9 us (22%)
  starting transfers between devices  36.8 us (16%)
  other arithmetic  5.85 us (3%)
  local copies, waits for them, and re-layouts  5.59 us (2%)
    ppermute x5, waiting for transfers between devices, chain_sum(): lax.ppermute(total, axis, [(i + 1, i), (peers - 2 - i, peers - 1 - i)])  51.3 us
    pallas_call x8, Pallas kernels, call(): pl.pallas_call(kernel, out_shape=out, in_specs=[pl.BlockSpec(memory_space...  48.9 us
    ppermute x17, waiting for transfers between devices, swap(): return lax.ppermute(value, axis, [(i, i ^ bit) for i in range(peers)])  42.2 us
    ppermute x5, waiting for transfers between devices, chain_sum(): lax.ppermute(total, axis, [(i, i + 1), (peers - 1 - i, peers - 2 - i)])  29.3 us
    ppermute x17, starting transfers between devices, swap(): return lax.ppermute(value, axis, [(i, i ^ bit) for i in range(peers)])  11.1 us
    ppermute x5, starting transfers between devices, chain_sum(): lax.ppermute(total, axis, [(i, i + 1), (peers - 1 - i, peers - 2 - i)])  11 us
    ppermute x5, starting transfers between devices, chain_sum(): lax.ppermute(total, axis, [(i + 1, i), (peers - 2 - i, peers - 1 - i)])  6.46 us
  transfers between devices with their start and end apart: 34, of which 15 were waited for; matrix products, arithmetic and copies ran while one was open for 3% of the time, Pallas kernels for 15%

profile of v1, /device:TPU:0, one launch (start us, length us, event | category | flops | bytes accessed | tf_op | source)
XLA Modules:
  0.0 226.2 jit_solution(16137537709162711183)
XLA Ops:
  0.6 3.0 %collective-permute-start = (bf16[320,1024]{1,0:T(8,128)(2,1)}, bf16[320,1024]{1,0:T(8,128)(2,1)S(1)}, u32[]{:S(2)}, u32[]{:S(2)}) collective-permute-start(bf16[320,1024]{1,0:T(8,128)(2,1)} %bitcast.17), channel_id=1, source_target_pairs={{0,8},{4,12},{8,0},{12,4},{1,9},{5,13},{9,1},{13,5},{2,10},{6,14},... | collective-permute-start | bytes 1966088 | tf_op jit(solution)/shard_map/ppermute | solution.py:27
  3.7 14.9 %collective-permute-done.refs_0_.refs_1_ = bf16[320,1024]{1,0:T(8,128)(2,1)S(1)} collective-permute-done((bf16[320,1024]{1,0:T(8,128)(2,1)}, bf16[320,1024]{1,0:T(8,128)(2,1)S(1)}, u32[]{:S(2)}, u32[]{:S(2)}) %collective-permute-start) | collective-permute-done | bytes 655392 | tf_op jit(solution)/shard_map/ppermute | solution.py:27
  18.6 1.2 fusion
  19.8 3.6 %collective-permute-start.2 = (bf16[320,2]{1,0:T(8,128)(2,1)S(1)}, bf16[320,2]{1,0:T(8,128)(2,1)S(1)}, u32[]{:S(2)}, u32[]{:S(2)}) collective-permute-start(bf16[320,2]{1,0:T(8,128)(2,1)S(1)} %get-tuple-element.30), channel_id=1, source_target_pairs={{0,16},{1,17},{2,18},{3,19},{4,20},{5,21},{6,22},{7,23},{8,24},{9,... | collective-permute-start | bytes 3848 | tf_op jit(solution)/shard_map/ppermute | solution.py:179
  23.5 1.3 collective-permute-start.3
  24.8 0.9 collective-permute-done.2
  25.6 4.2 %collective-permute-done.3 = bf16[320,2]{1,0:T(8,128)(2,1)S(1)} collective-permute-done((bf16[320,2]{1,0:T(8,128)(2,1)S(1)}, bf16[320,2]{1,0:T(8,128)(2,1)S(1)}, u32[]{:S(2)}, u32[]{:S(2)}) %collective-permute-start.3) | collective-permute-done | bytes 1312 | tf_op jit(solution)/shard_map/ppermute | solution.py:180
  29.9 1.6 collective-permute-start.4
  31.5 2.9 %collective-permute-done.4 = bf16[320,4]{1,0:T(8,128)(2,1)S(1)} collective-permute-done((bf16[320,4]{1,0:T(8,128)(2,1)S(1)}, bf16[320,4]{1,0:T(8,128)(2,1)S(1)}, u32[]{:S(2)}, u32[]{:S(2)}) %collective-permute-start.4) | collective-permute-done | bytes 2592 | tf_op jit(solution)/shard_map/ppermute | solution.py:27
  37.6 0.9 copy-done.2
  38.4 7.8 %shard_map.68 = (f32[512,384]{1,0:T(8,128)}, f32[512,384]{1,0:T(8,128)}) custom-call(s32[2]{0:T(128)} %pad_add_fusion.idx_ref, bf16[320,1024]{1,0:T(8,128)(2,1)} %bitcast.20, bf16[320,1024]{1,0:T(8,128)(2,1)} %copy-done.2, bf16[320,128]{1,0:T(8,128)(2,1)} %pad.15.refs_2_.refs_4_, bf16[320,128]{1,0:T(8,128)(2,1)} %pad.16.refs_3_.refs_6_, ...), custom_call_target="tpu_custom_call" | custom-call | tf_op jit(solution)/shard_map/pallas_call | solution.py:164
  46.2 0.8 copy-done.1
  47.1 9.8 %shard_map.69 = (bf16[512,384]{1,0:T(8,128)(2,1)}, f32[1040,384]{1,0:T(8,128)}) custom-call(s32[2]{0:T(128)} %pad_add_fusion.idx_ref, bf16[320,1024]{1,0:T(8,128)(2,1)} %copy-done, bf16[320,1024]{1,0:T(8,128)(2,1)} %copy-done.1, bf16[320,128]{1,0:T(8,128)(2,1)} %pad.13.refs_2_.refs_5_, bf16[320,128]{1,0:T(8,128)(2,1)} %pad.14.refs_3_.refs_7_, ...), custom_call_target="tpu_custom_call" | custom-call | tf_op jit(solution)/shard_map/pallas_call | solution.py:164
  56.8 5.2 %shard_map.75 = (bf16[640,384]{1,0:T(8,128)(2,1)}, bf16[640,384]{1,0:T(8,128)(2,1)}) custom-call(s32[2]{0:T(128)} %pad_add_fusion.idx_ref, bf16[320,1024]{1,0:T(8,128)(2,1)} %bitcast.21, bf16[320,1024]{1,0:T(8,128)(2,1)} %copy-done, bf16[320,1024]{1,0:T(8,128)(2,1)} %copy-done.2, bf16[320,1024]{1,0:T(8,128)(2,1)} %copy-done.1, ...), custom_call_target="tpu_custom_call" | custom-call | tf_op jit(solution)/shard_map/pallas_call | solution.py:164
  62.1 5.4 %shard_map.74 = (bf16[640,384]{1,0:T(8,128)(2,1)}, bf16[640,384]{1,0:T(8,128)(2,1)}) custom-call(s32[2]{0:T(128)} %pad_add_fusion.idx_ref, bf16[320,1024]{1,0:T(8,128)(2,1)} %bitcast.22, bf16[320,1024]{1,0:T(8,128)(2,1)} %copy-done, bf16[320,1024]{1,0:T(8,128)(2,1)} %copy-done.2, bf16[320,1024]{1,0:T(8,128)(2,1)} %copy-done.1, ...), custom_call_target="tpu_custom_call" | custom-call | tf_op jit(solution)/shard_map/pallas_call | solution.py:164
  67.5 2.0 collective-permute-start.26
  69.5 1.5 collective-permute-start.11
  71.0 5.2 %shard_map.73 = (bf16[640,384]{1,0:T(8,128)(2,1)}, bf16[640,384]{1,0:T(8,128)(2,1)}) custom-call(s32[2]{0:T(128)} %pad_add_fusion.idx_ref, bf16[320,1024]{1,0:T(8,128)(2,1)} %bitcast.23, bf16[320,1024]{1,0:T(8,128)(2,1)} %copy-done, bf16[320,1024]{1,0:T(8,128)(2,1)} %copy-done.2, bf16[320,1024]{1,0:T(8,128)(2,1)} %copy-done.1, ...), custom_call_target="tpu_custom_call" | custom-call | tf_op jit(solution)/shard_map/pallas_call | solution.py:164
  76.3 5.2 %shard_map.72 = (bf16[640,384]{1,0:T(8,128)(2,1)}, bf16[640,384]{1,0:T(8,128)(2,1)}) custom-call(s32[2]{0:T(128)} %pad_add_fusion.idx_ref, bf16[320,1024]{1,0:T(8,128)(2,1)} %bitcast.24, bf16[320,1024]{1,0:T(8,128)(2,1)} %copy-done, bf16[320,1024]{1,0:T(8,128)(2,1)} %copy-done.2, bf16[320,1024]{1,0:T(8,128)(2,1)} %copy-done.1, ...), custom_call_target="tpu_custom_call" | custom-call | tf_op jit(solution)/shard_map/pallas_call | solution.py:164
  81.5 5.3 %shard_map.71 = (bf16[640,384]{1,0:T(8,128)(2,1)}, bf16[640,384]{1,0:T(8,128)(2,1)}) custom-call(s32[2]{0:T(128)} %pad_add_fusion.idx_ref, bf16[320,1024]{1,0:T(8,128)(2,1)} %bitcast.25, bf16[320,1024]{1,0:T(8,128)(2,1)} %copy-done, bf16[320,1024]{1,0:T(8,128)(2,1)} %copy-done.2, bf16[320,1024]{1,0:T(8,128)(2,1)} %copy-done.1, ...), custom_call_target="tpu_custom_call" | custom-call | tf_op jit(solution)/shard_map/pallas_call | solution.py:164
  86.8 2.0 collective-permute-start.18
  89.7 7.7 %collective-permute-done.22 = bf16[640,384]{1,0:T(8,128)(2,1)S(1)} collective-permute-done((bf16[640,384]{1,0:T(8,128)(2,1)}, bf16[640,384]{1,0:T(8,128)(2,1)S(1)}, u32[]{:S(2)}, u32[]{:S(2)}) %collective-permute-start.22) | collective-permute-done | bytes 491552 | tf_op jit(solution)/shard_map/ppermute | solution.py:27
  97.7 2.3 %collective-permute-done.8.refs_1_ = bf16[512,384]{1,0:T(8,128)(2,1)S(1)} collective-permute-done((bf16[512,384]{1,0:T(8,128)(2,1)S(1)}, bf16[512,384]{1,0:T(8,128)(2,1)S(1)}, u32[]{:S(2)}, u32[]{:S(2)}) %collective-permute-start.8) | collective-permute-done | bytes 393248 | tf_op jit(solution)/shard_map/ppermute | solution.py:27
  100.0 7.9 %collective-permute-done.18 = bf16[640,384]{1,0:T(8,128)(2,1)S(1)} collective-permute-done((bf16[640,384]{1,0:T(8,128)(2,1)S(1)}, bf16[640,384]{1,0:T(8,128)(2,1)S(1)}, u32[]{:S(2)}, u32[]{:S(2)}) %collective-permute-start.18) | collective-permute-done | bytes 491552 | tf_op jit(solution)/shard_map/ppermute | solution.py:27
  107.9 3.5 %collective-permute-start.31 = (bf16[640,384]{1,0:T(8,128)(2,1)S(1)}, bf16[640,384]{1,0:T(8,128)(2,1)S(1)}, u32[]{:S(2)}, u32[]{:S(2)}) collective-permute-start(bf16[640,384]{1,0:T(8,128)(2,1)S(1)} %add_convert_fusion.2), channel_id=1, source_target_pairs={{0,1},{3,2},{4,5},{7,6},{8,9},{11,10},{12,13},{15,14},{16,17},{19,... | collective-permute-start | bytes 1474568 | tf_op jit(solution)/shard_map/ppermute | solution.py:200
  111.6 6.4 %collective-permute-done.14 = bf16[640,384]{1,0:T(8,128)(2,1)S(1)} collective-permute-done((bf16[640,384]{1,0:T(8,128)(2,1)S(1)}, bf16[640,384]{1,0:T(8,128)(2,1)S(1)}, u32[]{:S(2)}, u32[]{:S(2)}) %collective-permute-start.14) | collective-permute-done | bytes 491552 | tf_op jit(solution)/shard_map/ppermute | solution.py:27
  118.0 3.5 %collective-permute-start.27 = (bf16[640,384]{1,0:T(8,128)(2,1)S(1)}, bf16[640,384]{1,0:T(8,128)(2,1)S(1)}, u32[]{:S(2)}, u32[]{:S(2)}) collective-permute-start(bf16[640,384]{1,0:T(8,128)(2,1)S(1)} %add_convert_fusion.5), channel_id=1, source_target_pairs={{0,1},{3,2},{4,5},{7,6},{8,9},{11,10},{12,13},{15,14},{16,17},{19,... | collective-permute-start | bytes 1474568 | tf_op jit(solution)/shard_map/ppermute | solution.py:200
  121.7 1.3 collective-permute-start.23
  123.1 1.3 collective-permute-start.19
  124.4 1.3 collective-permute-start.15
  125.8 5.1 %shard_map.70 = bf16[512,640]{1,0:T(8,128)(2,1)} custom-call(s32[2]{0:T(128)} %pad_add_fusion.idx_ref, bf16[512,384]{1,0:T(8,128)(2,1)} %get-tuple-element.18.refs_0_, bf16[512,384]{1,0:T(8,128)(2,1)} %copy-done.9, bf16[512,384]{1,0:T(8,128)(2,1)} %copy-done.10, bf16[512,384]{1,0:T(8,128)(2,1)} %copy-done.11, f32[1,384]{1,0:T(1,128)} %copy-done.12, ...), custom_call_target="tpu_custom_call" | custom-call | tf_op jit(solution)/shard_map/pallas_call | solution.py:164
  131.0 0.7 collective-permute-start.32
  131.7 1.5 collective-permute-done.27
  133.3 0.7 collective-permute-start.28
  134.0 9.7 %collective-permute-done.23 = bf16[640,384]{1,0:T(8,128)(2,1)S(1)} collective-permute-done((bf16[640,384]{1,0:T(8,128)(2,1)S(1)}, bf16[640,384]{1,0:T(8,128)(2,1)S(1)}, u32[]{:S(2)}, u32[]{:S(2)}) %collective-permute-start.23) | collective-permute-done | bytes 491552 | tf_op jit(solution)/shard_map/ppermute | solution.py:200
  143.8 0.7 collective-permute-start.24
  144.5 9.7 %collective-permute-done.19 = bf16[640,384]{1,0:T(8,128)(2,1)S(1)} collective-permute-done((bf16[640,384]{1,0:T(8,128)(2,1)S(1)}, bf16[640,384]{1,0:T(8,128)(2,1)S(1)}, u32[]{:S(2)}, u32[]{:S(2)}) %collective-permute-start.19) | collective-permute-done | bytes 491552 | tf_op jit(solution)/shard_map/ppermute | solution.py:200
  154.3 0.7 collective-permute-start.20
  155.0 8.4 %collective-permute-done.15 = bf16[640,384]{1,0:T(8,128)(2,1)S(1)} collective-permute-done((bf16[640,384]{1,0:T(8,128)(2,1)S(1)}, bf16[640,384]{1,0:T(8,128)(2,1)S(1)}, u32[]{:S(2)}, u32[]{:S(2)}) %collective-permute-start.15) | collective-permute-done | bytes 491552 | tf_op jit(solution)/shard_map/ppermute | solution.py:200
  164.5 1.3 collective-permute-start.33
  165.9 1.3 collective-permute-start.29
  167.3 1.3 collective-permute-start.17
  168.8 1.3 collective-permute-start.21
  170.2 1.3 collective-permute-start.25
  171.5 32.7 %collective-permute-done.17 = bf16[640,384]{1,0:T(8,128)(2,1)S(1)} collective-permute-done((bf16[640,384]{1,0:T(8,128)(2,1)S(1)}, bf16[640,384]{1,0:T(8,128)(2,1)S(1)}, u32[]{:S(2)}, u32[]{:S(2)}) %collective-permute-start.17) | collective-permute-done | bytes 491552 | tf_op jit(solution)/shard_map/ppermute | solution.py:205
  204.3 10.4 %collective-permute-done.21 = bf16[640,384]{1,0:T(8,128)(2,1)S(1)} collective-permute-done((bf16[640,384]{1,0:T(8,128)(2,1)S(1)}, bf16[640,384]{1,0:T(8,128)(2,1)S(1)}, u32[]{:S(2)}, u32[]{:S(2)}) %collective-permute-start.21) | collective-permute-done | bytes 491552 | tf_op jit(solution)/shard_map/ppermute | solution.py:205
  214.9 8.2 %collective-permute-done.25 = bf16[640,384]{1,0:T(8,128)(2,1)S(1)} collective-permute-done((bf16[640,384]{1,0:T(8,128)(2,1)S(1)}, bf16[640,384]{1,0:T(8,128)(2,1)S(1)}, u32[]{:S(2)}, u32[]{:S(2)}) %collective-permute-start.25) | collective-permute-done | bytes 491552 | tf_op jit(solution)/shard_map/ppermute | solution.py:205
  223.6 2.6 %stack.44 = f32[640,5,384]{2,0,1:T(8,128)} convert(bf16[640,5,384]{2,0,1:T(8,128)(2,1)S(1)} %bitcast_dynamic-update-slice_fusion) | non-fusion elementwise | flops 1228800 | bytes 7372800 | tf_op jit(solution)/shard_map/stack | solution.py:262
  (95 shorter events, 7.6 us)
Async XLA Ops:
  0.6 18.0 %collective-permute-start = (bf16[320,1024]{1,0:T(8,128)(2,1)}, bf16[320,1024]{1,0:T(8,128)(2,1)S(1)}, u32[]{:S(2)}, u32[]{:S(2)}) collective-permute-start(bf16[320,1024]{1,0:T(8,128)(2,1)} %bitcast.17), channel_id=1, source_target_pairs={{0,8},{4,12},{8,0},{12,4},{1,9},{5,13},{9,1},{13,5},{2,10},{6,14},... | collective-permute-start | bytes 1966088 | tf_op jit(solution)/shard_map/ppermute | solution.py:27
  3.7 33.9 %collective-permute-start.6 = (bf16[320,1024]{1,0:T(8,128)(2,1)}, bf16[320,1024]{1,0:T(8,128)(2,1)S(1)}, u32[]{:S(2)}, u32[]{:S(2)}) collective-permute-start(bf16[320,1024]{1,0:T(8,128)(2,1)} %bitcast.18), channel_id=1, source_target_pairs={{0,4},{4,0},{8,12},{12,8},{1,5},{5,1},{9,13},{13,9},{2,6},{6,2},{1... | collective-permute-start | bytes 1966088 | tf_op jit(solution)/shard_map/ppermute | solution.py:27
  18.6 27.6 %copy-start = (bf16[320,1024]{1,0:T(8,128)(2,1)}, bf16[320,1024]{1,0:T(8,128)(2,1)S(1)}, u32[]{:S(2)}) copy-start(bf16[320,1024]{1,0:T(8,128)(2,1)S(1)} %collective-permute-done.refs_0_.refs_1_) | copy-start | bytes 1966084
  18.6 27.6 %collective-permute-start.1 = (bf16[320,1024]{1,0:T(8,128)(2,1)S(1)}, bf16[320,1024]{1,0:T(8,128)(2,1)S(1)}, u32[]{:S(2)}, u32[]{:S(2)}) collective-permute-start(bf16[320,1024]{1,0:T(8,128)(2,1)S(1)} %collective-permute-done.refs_0_.refs_1_), channel_id=1, source_target_pairs={{0,4},{4,0},{8,12},{12,8},{1,5},{5,1},{9,13},{13,9},{2,6},{6,2},{1... | collective-permute-start | bytes 1966088 | tf_op jit(solution)/shard_map/ppermute | solution.py:27
  19.8 5.8 %collective-permute-start.2 = (bf16[320,2]{1,0:T(8,128)(2,1)S(1)}, bf16[320,2]{1,0:T(8,128)(2,1)S(1)}, u32[]{:S(2)}, u32[]{:S(2)}) collective-permute-start(bf16[320,2]{1,0:T(8,128)(2,1)S(1)} %get-tuple-element.30), channel_id=1, source_target_pairs={{0,16},{1,17},{2,18},{3,19},{4,20},{5,21},{6,22},{7,23},{8,24},{9,... | collective-permute-start | bytes 3848 | tf_op jit(solution)/shard_map/ppermute | solution.py:179
  23.5 6.3 %collective-permute-start.3 = (bf16[320,2]{1,0:T(8,128)(2,1)S(1)}, bf16[320,2]{1,0:T(8,128)(2,1)S(1)}, u32[]{:S(2)}, u32[]{:S(2)}) collective-permute-start(bf16[320,2]{1,0:T(8,128)(2,1)S(1)} %get-tuple-element.31), channel_id=1, source_target_pairs={{16,0},{17,1},{18,2},{19,3},{20,4},{21,5},{22,6},{23,7},{24,8},{25... | collective-permute-start | bytes 3848 | tf_op jit(solution)/shard_map/ppermute | solution.py:180
  29.9 4.5 %collective-permute-start.4 = (bf16[320,4]{1,0:T(8,128)(2,1)S(1)}, bf16[320,4]{1,0:T(8,128)(2,1)S(1)}, u32[]{:S(2)}, u32[]{:S(2)}) collective-permute-start(bf16[320,4]{1,0:T(8,128)(2,1)S(1)} %pad_maximum_fusion), channel_id=1, source_target_pairs={{0,8},{4,12},{8,0},{12,4},{1,9},{5,13},{9,1},{13,5},{2,10},{6,14},... | collective-permute-start | bytes 7688 | tf_op jit(solution)/shard_map/ppermute | solution.py:27
  31.5 4.8 %collective-permute-start.7 = (bf16[320,4]{1,0:T(8,128)(2,1)S(1)}, bf16[320,4]{1,0:T(8,128)(2,1)S(1)}, u32[]{:S(2)}, u32[]{:S(2)}) collective-permute-start(bf16[320,4]{1,0:T(8,128)(2,1)S(1)} %pad_maximum_fusion), channel_id=1, source_target_pairs={{0,4},{4,0},{8,12},{12,8},{1,5},{5,1},{9,13},{13,9},{2,6},{6,2},{1... | collective-permute-start | bytes 7688 | tf_op jit(solution)/shard_map/ppermute | solution.py:27
  34.4 2.5 %collective-permute-start.5 = (bf16[320,4]{1,0:T(8,128)(2,1)S(1)}, bf16[320,4]{1,0:T(8,128)(2,1)S(1)}, u32[]{:S(2)}, u32[]{:S(2)}) collective-permute-start(bf16[320,4]{1,0:T(8,128)(2,1)S(1)} %collective-permute-done.4), channel_id=1, source_target_pairs={{0,4},{4,0},{8,12},{12,8},{1,5},{5,1},{9,13},{13,9},{2,6},{6,2},{1... | collective-permute-start | bytes 7688 | tf_op jit(solution)/shard_map/ppermute | solution.py:27
  62.1 7.4 %copy-start.13 = (f32[384]{0:T(512)S(1)}, f32[384]{0:T(512)}, u32[]{:S(2)}) copy-start(f32[384]{0:T(512)} %param.7) | copy-start | bytes 4612
  62.1 24.7 %collective-permute-start.30 = (bf16[640,384]{1,0:T(8,128)(2,1)}, bf16[640,384]{1,0:T(8,128)(2,1)S(1)}, u32[]{:S(2)}, u32[]{:S(2)}) collective-permute-start(bf16[640,384]{1,0:T(8,128)(2,1)} %get-tuple-element.29), channel_id=1, source_target_pairs={{0,16},{16,0},{1,17},{17,1},{2,18},{18,2},{3,19},{19,3},{4,20},{20... | collective-permute-start | bytes 1474568 | tf_op jit(solution)/shard_map/ppermute | solution.py:27
  67.5 21.5 %collective-permute-start.26 = (bf16[640,384]{1,0:T(8,128)(2,1)}, bf16[640,384]{1,0:T(8,128)(2,1)S(1)}, u32[]{:S(2)}, u32[]{:S(2)}) collective-permute-start(bf16[640,384]{1,0:T(8,128)(2,1)} %get-tuple-element.27), channel_id=1, source_target_pairs={{0,16},{16,0},{1,17},{17,1},{2,18},{18,2},{3,19},{19,3},{4,20},{20... | collective-permute-start | bytes 1474568 | tf_op jit(solution)/shard_map/ppermute | solution.py:27
  69.5 11.9 %copy-start.12 = (f32[1,384]{1,0:T(1,128)}, f32[1,384]{1,0:T(1,128)S(1)}, u32[]{:S(2)}) copy-start(f32[1,384]{1,0:T(1,128)S(1)} %reshape.7.refs_4_) | copy-start | bytes 4612
  69.5 28.1 %collective-permute-start.11 = (f32[1,384]{1,0:T(1,128)S(1)}, f32[1,384]{1,0:T(1,128)S(1)}, u32[]{:S(2)}, u32[]{:S(2)}) collective-permute-start(f32[1,384]{1,0:T(1,128)S(1)} %reshape.7.refs_4_), channel_id=1, source_target_pairs={{0,8},{4,12},{8,0},{12,4},{1,9},{5,13},{9,1},{13,5},{2,10},{6,14},... | collective-permute-start | bytes 4616 | tf_op jit(solution)/shard_map/ppermute | solution.py:27
  71.0 40.5 %collective-permute-start.12 = (f32[1,384]{1,0:T(1,128)S(1)}, f32[1,384]{1,0:T(1,128)S(1)}, u32[]{:S(2)}, u32[]{:S(2)}) collective-permute-start(f32[1,384]{1,0:T(1,128)S(1)} %reshape.7.refs_4_), channel_id=1, source_target_pairs={{0,4},{4,0},{8,12},{12,8},{1,5},{5,1},{9,13},{13,9},{2,6},{6,2},{1... | collective-permute-start | bytes 4616 | tf_op jit(solution)/shard_map/ppermute | solution.py:27
  76.2 21.2 %collective-permute-start.22 = (bf16[640,384]{1,0:T(8,128)(2,1)}, bf16[640,384]{1,0:T(8,128)(2,1)S(1)}, u32[]{:S(2)}, u32[]{:S(2)}) collective-permute-start(bf16[640,384]{1,0:T(8,128)(2,1)} %get-tuple-element.25), channel_id=1, source_target_pairs={{0,16},{16,0},{1,17},{17,1},{2,18},{18,2},{3,19},{19,3},{4,20},{20... | collective-permute-start | bytes 1474568 | tf_op jit(solution)/shard_map/ppermute | solution.py:27
  81.4 5.4 %copy-start.18 = (bf16[640,384]{1,0:T(8,128)(2,1)S(1)}, bf16[640,384]{1,0:T(8,128)(2,1)}, u32[]{:S(2)}) copy-start(bf16[640,384]{1,0:T(8,128)(2,1)} %get-tuple-element.23) | copy-start | bytes 1474564
  81.4 7.4 %copy-start.6 = (bf16[640,384]{1,0:T(8,128)(2,1)S(1)}, bf16[640,384]{1,0:T(8,128)(2,1)}, u32[]{:S(2)}) copy-start(bf16[640,384]{1,0:T(8,128)(2,1)} %get-tuple-element.28) | copy-start | bytes 1474564
  81.5 7.5 %copy-start.8 = (bf16[512,384]{1,0:T(8,128)(2,1)S(1)}, bf16[512,384]{1,0:T(8,128)(2,1)}, u32[]{:S(2)}) copy-start(bf16[512,384]{1,0:T(8,128)(2,1)} %get-tuple-element.18.refs_0_) | copy-start | bytes 1179652
  81.5 8.1 %copy-start.5 = (bf16[640,384]{1,0:T(8,128)(2,1)S(1)}, bf16[640,384]{1,0:T(8,128)(2,1)}, u32[]{:S(2)}) copy-start(bf16[640,384]{1,0:T(8,128)(2,1)} %get-tuple-element.26) | copy-start | bytes 1474564
  86.8 10.6 %copy-start.17 = (bf16[640,384]{1,0:T(8,128)(2,1)S(1)}, bf16[640,384]{1,0:T(8,128)(2,1)}, u32[]{:S(2)}) copy-start(bf16[640,384]{1,0:T(8,128)(2,1)} %get-tuple-element.21) | copy-start | bytes 1474564
  86.8 10.7 %copy-start.7 = (bf16[640,384]{1,0:T(8,128)(2,1)S(1)}, bf16[640,384]{1,0:T(8,128)(2,1)}, u32[]{:S(2)}) copy-start(bf16[640,384]{1,0:T(8,128)(2,1)} %get-tuple-element.24) | copy-start | bytes 1474564
  86.8 24.6 %copy-start.4 = (bf16[640,384]{1,0:T(8,128)(2,1)S(1)}, bf16[640,384]{1,0:T(8,128)(2,1)}, u32[]{:S(2)}) copy-start(bf16[640,384]{1,0:T(8,128)(2,1)} %get-tuple-element.22) | copy-start | bytes 1474564
  86.8 21.1 %collective-permute-start.18 = (bf16[640,384]{1,0:T(8,128)(2,1)S(1)}, bf16[640,384]{1,0:T(8,128)(2,1)S(1)}, u32[]{:S(2)}, u32[]{:S(2)}) collective-permute-start(bf16[640,384]{1,0:T(8,128)(2,1)S(1)} %copy-done.18), channel_id=1, source_target_pairs={{0,16},{16,0},{1,17},{17,1},{2,18},{18,2},{3,19},{19,3},{4,20},{20... | collective-permute-start | bytes 1474568 | tf_op jit(solution)/shard_map/ppermute | solution.py:27
  88.9 32.6 %copy-start.3 = (bf16[640,384]{1,0:T(8,128)(2,1)S(1)}, bf16[640,384]{1,0:T(8,128)(2,1)}, u32[]{:S(2)}) copy-start(bf16[640,384]{1,0:T(8,128)(2,1)} %get-tuple-element.20) | copy-start | bytes 1474564
  89.0 11.0 %collective-permute-start.8 = (bf16[512,384]{1,0:T(8,128)(2,1)S(1)}, bf16[512,384]{1,0:T(8,128)(2,1)S(1)}, u32[]{:S(2)}, u32[]{:S(2)}) collective-permute-start(bf16[512,384]{1,0:T(8,128)(2,1)S(1)} %copy-done.8), channel_id=1, source_target_pairs={{0,8},{4,12},{8,0},{12,4},{1,9},{5,13},{9,1},{13,5},{2,10},{6,14},... | collective-permute-start | bytes 1179656 | tf_op jit(solution)/shard_map/ppermute | solution.py:27
  97.4 20.7 %collective-permute-start.14 = (bf16[640,384]{1,0:T(8,128)(2,1)S(1)}, bf16[640,384]{1,0:T(8,128)(2,1)S(1)}, u32[]{:S(2)}, u32[]{:S(2)}) collective-permute-start(bf16[640,384]{1,0:T(8,128)(2,1)S(1)} %copy-done.17), channel_id=1, source_target_pairs={{0,16},{16,0},{1,17},{17,1},{2,18},{18,2},{3,19},{19,3},{4,20},{20... | collective-permute-start | bytes 1474568 | tf_op jit(solution)/shard_map/ppermute | solution.py:27
  97.6 28.2 %copy-start.14 = (f32[1,384]{1,0:T(1,128)}, f32[1,384]{1,0:T(1,128)S(1)}, u32[]{:S(2)}) copy-start(f32[1,384]{1,0:T(1,128)S(1)} %collective-permute-done.11.refs_5_) | copy-start | bytes 4612
  97.6 25.5 %collective-permute-start.9 = (bf16[512,384]{1,0:T(8,128)(2,1)S(1)}, bf16[512,384]{1,0:T(8,128)(2,1)S(1)}, u32[]{:S(2)}, u32[]{:S(2)}) collective-permute-start(bf16[512,384]{1,0:T(8,128)(2,1)S(1)} %copy-done.8), channel_id=1, source_target_pairs={{0,4},{4,0},{8,12},{12,8},{1,5},{5,1},{9,13},{13,9},{2,6},{6,2},{1... | collective-permute-start | bytes 1179656 | tf_op jit(solution)/shard_map/ppermute | solution.py:27
  100.0 25.7 %copy-start.9 = (bf16[512,384]{1,0:T(8,128)(2,1)}, bf16[512,384]{1,0:T(8,128)(2,1)S(1)}, u32[]{:S(2)}) copy-start(bf16[512,384]{1,0:T(8,128)(2,1)S(1)} %collective-permute-done.8.refs_1_) | copy-start | bytes 1179652
  100.0 24.4 %collective-permute-start.10 = (bf16[512,384]{1,0:T(8,128)(2,1)S(1)}, bf16[512,384]{1,0:T(8,128)(2,1)S(1)}, u32[]{:S(2)}, u32[]{:S(2)}) collective-permute-start(bf16[512,384]{1,0:T(8,128)(2,1)S(1)} %collective-permute-done.8.refs_1_), channel_id=1, source_target_pairs={{0,4},{4,0},{8,12},{12,8},{1,5},{5,1},{9,13},{13,9},{2,6},{6,2},{1... | collective-permute-start | bytes 1179656 | tf_op jit(solution)/shard_map/ppermute | solution.py:27
  107.9 23.0 %collective-permute-start.31 = (bf16[640,384]{1,0:T(8,128)(2,1)S(1)}, bf16[640,384]{1,0:T(8,128)(2,1)S(1)}, u32[]{:S(2)}, u32[]{:S(2)}) collective-permute-start(bf16[640,384]{1,0:T(8,128)(2,1)S(1)} %add_convert_fusion.2), channel_id=1, source_target_pairs={{0,1},{3,2},{4,5},{7,6},{8,9},{11,10},{12,13},{15,14},{16,17},{19,... | collective-permute-start | bytes 1474568 | tf_op jit(solution)/shard_map/ppermute | solution.py:200
  111.6 14.2 %copy-start.15 = (f32[1,384]{1,0:T(1,128)}, f32[1,384]{1,0:T(1,128)S(1)}, u32[]{:S(2)}) copy-start(f32[1,384]{1,0:T(1,128)S(1)} %collective-permute-done.12.refs_6_) | copy-start | bytes 4612
  111.6 10.1 %collective-permute-start.13 = (f32[1,384]{1,0:T(1,128)S(1)}, f32[1,384]{1,0:T(1,128)S(1)}, u32[]{:S(2)}, u32[]{:S(2)}) collective-permute-start(f32[1,384]{1,0:T(1,128)S(1)} %collective-permute-done.11.refs_5_), channel_id=1, source_target_pairs={{0,4},{4,0},{8,12},{12,8},{1,5},{5,1},{9,13},{13,9},{2,6},{6,2},{1... | collective-permute-start | bytes 4616 | tf_op jit(solution)/shard_map/ppermute | solution.py:27
  118.0 15.1 %collective-permute-start.27 = (bf16[640,384]{1,0:T(8,128)(2,1)S(1)}, bf16[640,384]{1,0:T(8,128)(2,1)S(1)}, u32[]{:S(2)}, u32[]{:S(2)}) collective-permute-start(bf16[640,384]{1,0:T(8,128)(2,1)S(1)} %add_convert_fusion.5), channel_id=1, source_target_pairs={{0,1},{3,2},{4,5},{7,6},{8,9},{11,10},{12,13},{15,14},{16,17},{19,... | collective-permute-start | bytes 1474568 | tf_op jit(solution)/shard_map/ppermute | solution.py:200
  121.7 22.0 %collective-permute-start.23 = (bf16[640,384]{1,0:T(8,128)(2,1)S(1)}, bf16[640,384]{1,0:T(8,128)(2,1)S(1)}, u32[]{:S(2)}, u32[]{:S(2)}) collective-permute-start(bf16[640,384]{1,0:T(8,128)(2,1)S(1)} %add_convert_fusion.8), channel_id=1, source_target_pairs={{0,1},{3,2},{4,5},{7,6},{8,9},{11,10},{12,13},{15,14},{16,17},{19,... | collective-permute-start | bytes 1474568 | tf_op jit(solution)/shard_map/ppermute | solution.py:200
  123.1 31.1 %collective-permute-start.19 = (bf16[640,384]{1,0:T(8,128)(2,1)S(1)}, bf16[640,384]{1,0:T(8,128)(2,1)S(1)}, u32[]{:S(2)}, u32[]{:S(2)}) collective-permute-start(bf16[640,384]{1,0:T(8,128)(2,1)S(1)} %add_convert_fusion.11), channel_id=1, source_target_pairs={{0,1},{3,2},{4,5},{7,6},{8,9},{11,10},{12,13},{15,14},{16,17},{19,... | collective-permute-start | bytes 1474568 | tf_op jit(solution)/shard_map/ppermute | solution.py:200
  124.4 39.1 %collective-permute-start.15 = (bf16[640,384]{1,0:T(8,128)(2,1)S(1)}, bf16[640,384]{1,0:T(8,128)(2,1)S(1)}, u32[]{:S(2)}, u32[]{:S(2)}) collective-permute-start(bf16[640,384]{1,0:T(8,128)(2,1)S(1)} %add_convert_fusion.14), channel_id=1, source_target_pairs={{0,1},{3,2},{4,5},{7,6},{8,9},{11,10},{12,13},{15,14},{16,17},{19,... | collective-permute-start | bytes 1474568 | tf_op jit(solution)/shard_map/ppermute | solution.py:200
  131.0 33.3 %collective-permute-start.32 = (bf16[640,384]{1,0:T(8,128)(2,1)S(1)}, bf16[640,384]{1,0:T(8,128)(2,1)S(1)}, u32[]{:S(2)}, u32[]{:S(2)}) collective-permute-start(bf16[640,384]{1,0:T(8,128)(2,1)S(1)} %add_convert_fusion.1), channel_id=1, source_target_pairs={{1,2},{2,1},{5,6},{6,5},{9,10},{10,9},{13,14},{14,13},{17,18},{18,... | collective-permute-start | bytes 1474568 | tf_op jit(solution)/shard_map/ppermute | solution.py:202
  133.3 32.5 %collective-permute-start.28 = (bf16[640,384]{1,0:T(8,128)(2,1)S(1)}, bf16[640,384]{1,0:T(8,128)(2,1)S(1)}, u32[]{:S(2)}, u32[]{:S(2)}) collective-permute-start(bf16[640,384]{1,0:T(8,128)(2,1)S(1)} %add_convert_fusion.4), channel_id=1, source_target_pairs={{1,2},{2,1},{5,6},{6,5},{9,10},{10,9},{13,14},{14,13},{17,18},{18,... | collective-permute-start | bytes 1474568 | tf_op jit(solution)/shard_map/ppermute | solution.py:202
  143.8 26.3 %collective-permute-start.24 = (bf16[640,384]{1,0:T(8,128)(2,1)S(1)}, bf16[640,384]{1,0:T(8,128)(2,1)S(1)}, u32[]{:S(2)}, u32[]{:S(2)}) collective-permute-start(bf16[640,384]{1,0:T(8,128)(2,1)S(1)} %add_convert_fusion.7), channel_id=1, source_target_pairs={{1,2},{2,1},{5,6},{6,5},{9,10},{10,9},{13,14},{14,13},{17,18},{18,... | collective-permute-start | bytes 1474568 | tf_op jit(solution)/shard_map/ppermute | solution.py:202
  154.3 14.3 %collective-permute-start.20 = (bf16[640,384]{1,0:T(8,128)(2,1)S(1)}, bf16[640,384]{1,0:T(8,128)(2,1)S(1)}, u32[]{:S(2)}, u32[]{:S(2)}) collective-permute-start(bf16[640,384]{1,0:T(8,128)(2,1)S(1)} %add_convert_fusion.10), channel_id=1, source_target_pairs={{1,2},{2,1},{5,6},{6,5},{9,10},{10,9},{13,14},{14,13},{17,18},{18,... | collective-permute-start | bytes 1474568 | tf_op jit(solution)/shard_map/ppermute | solution.py:202
  163.6 3.6 %collective-permute-start.16 = (bf16[640,384]{1,0:T(8,128)(2,1)S(1)}, bf16[640,384]{1,0:T(8,128)(2,1)S(1)}, u32[]{:S(2)}, u32[]{:S(2)}) collective-permute-start(bf16[640,384]{1,0:T(8,128)(2,1)S(1)} %add_convert_fusion.13), channel_id=1, source_target_pairs={{1,2},{2,1},{5,6},{6,5},{9,10},{10,9},{13,14},{14,13},{17,18},{18,... | collective-permute-start | bytes 1474568 | tf_op jit(solution)/shard_map/ppermute | solution.py:202
  164.5 58.9 %collective-permute-start.33 = (bf16[640,384]{1,0:T(8,128)(2,1)S(1)}, bf16[640,384]{1,0:T(8,128)(2,1)S(1)}, u32[]{:S(2)}, u32[]{:S(2)}) collective-permute-start(bf16[640,384]{1,0:T(8,128)(2,1)S(1)} %add_convert_fusion), channel_id=1, source_target_pairs={{1,0},{2,3},{5,4},{6,7},{9,8},{10,11},{13,12},{14,15},{17,16},{18,... | collective-permute-start | bytes 1474568 | tf_op jit(solution)/shard_map/ppermute | solution.py:205
  165.9 57.3 %collective-permute-start.29 = (bf16[640,384]{1,0:T(8,128)(2,1)S(1)}, bf16[640,384]{1,0:T(8,128)(2,1)S(1)}, u32[]{:S(2)}, u32[]{:S(2)}) collective-permute-start(bf16[640,384]{1,0:T(8,128)(2,1)S(1)} %add_convert_fusion.3), channel_id=1, source_target_pairs={{1,0},{2,3},{5,4},{6,7},{9,8},{10,11},{13,12},{14,15},{17,16},{18,... | collective-permute-start | bytes 1474568 | tf_op jit(solution)/shard_map/ppermute | solution.py:205
  167.3 36.9 %collective-permute-start.17 = (bf16[640,384]{1,0:T(8,128)(2,1)S(1)}, bf16[640,384]{1,0:T(8,128)(2,1)S(1)}, u32[]{:S(2)}, u32[]{:S(2)}) collective-permute-start(bf16[640,384]{1,0:T(8,128)(2,1)S(1)} %add_convert_fusion.12), channel_id=1, source_target_pairs={{1,0},{2,3},{5,4},{6,7},{9,8},{10,11},{13,12},{14,15},{17,16},{18,... | collective-permute-start | bytes 1474568 | tf_op jit(solution)/shard_map/ppermute | solution.py:205
  168.8 45.9 %collective-permute-start.21 = (bf16[640,384]{1,0:T(8,128)(2,1)S(1)}, bf16[640,384]{1,0:T(8,128)(2,1)S(1)}, u32[]{:S(2)}, u32[]{:S(2)}) collective-permute-start(bf16[640,384]{1,0:T(8,128)(2,1)S(1)} %add_convert_fusion.9), channel_id=1, source_target_pairs={{1,0},{2,3},{5,4},{6,7},{9,8},{10,11},{13,12},{14,15},{17,16},{18,... | collective-permute-start | bytes 1474568 | tf_op jit(solution)/shard_map/ppermute | solution.py:205
  170.2 52.8 %collective-permute-start.25 = (bf16[640,384]{1,0:T(8,128)(2,1)S(1)}, bf16[640,384]{1,0:T(8,128)(2,1)S(1)}, u32[]{:S(2)}, u32[]{:S(2)}) collective-permute-start(bf16[640,384]{1,0:T(8,128)(2,1)S(1)} %add_convert_fusion.6), channel_id=1, source_target_pairs={{1,0},{2,3},{5,4},{6,7},{9,8},{10,11},{13,12},{14,15},{17,16},{18,... | collective-permute-start | bytes 1474568 | tf_op jit(solution)/shard_map/ppermute | solution.py:205
  (5 other events, 9.9 us)

commit v2 on v1

--- a/solution.py
+++ b/solution.py
@@ -9,7 +9,6 @@
 
 EDGE = 8
 LANES = 128
-VMEM_BYTES = 56 * 1024 * 1024
 F32 = jnp.float32
 BF16 = jnp.bfloat16
 
@@ -106,37 +105,42 @@
         pre_ref[EDGE : EDGE + length, lanes] = p_scr[c].astype(BF16).astype(F32)
 
 
-def grad_kernel(offsets, tap, shards, idx_ref, *refs):
+def grad_kernel(offsets, group, shards, idx_ref, *refs):
     n = len(offsets)
     x_refs, halo_refs, (p_ref, *out_refs, edge_scr) = refs[:n], refs[n : 2 * n], refs[2 * n :]
     depth, length = x_refs[0].shape
+    width = p_ref.shape[1]
     edge_scr[...] = jnp.zeros_like(edge_scr)
-    edge_scr[0:2, :] = p_ref[EDGE - tap : EDGE - tap + 2, :]
-    edge_scr[2:4, :] = p_ref[EDGE + length + 2 - tap : EDGE + length + 4 - tap, :]
-    p = p_ref[EDGE + 2 - tap : EDGE + 2 - tap + length, :].astype(BF16)
+    shifted = []
+    for i, tap in enumerate(group):
+        cols = slice(i * width, (i + 1) * width)
+        edge_scr[0:2, cols] = p_ref[EDGE - tap : EDGE - tap + 2, :]
+        edge_scr[2:4, cols] = p_ref[EDGE + length + 2 - tap : EDGE + length + 4 - tap, :]
+        shifted.append(p_ref[EDGE + 2 - tap : EDGE + 2 - tap + length, :].astype(BF16))
+    p = jnp.concatenate(shifted, axis=1)
     edge = edge_scr[...].astype(BF16)
     me = idx_ref[0]
     x = jnp.concatenate([ref[...] for ref in x_refs], axis=0)
     halo = jnp.concatenate([ref[...] for ref in halo_refs], axis=0)
     res = jnp.dot(x, p, preferred_element_type=F32) + jnp.dot(halo, edge, preferred_element_type=F32)
     res = res.astype(BF16)
-    for j, off in enumerate(offsets):
-        part = res[j * depth : (j + 1) * depth]
-        at = me ^ off
-        if len(out_refs) == 1:
-            out_refs[0][pl.ds(pl.multiple_of(at * depth, 16), depth), :] = part
-            continue
-        per = n // shards
-        row = pl.multiple_of(lax.rem(at, per) * depth, 16)
-        mine = lax.div(at, per) == idx_ref[1]
-
-        @pl.when(mine)
-        def _():
-            out_refs[0][pl.ds(row, depth), :] = part
-
-        @pl.when(jnp.logical_not(mine))
-        def _():
-            out_refs[1][pl.ds(row, depth), :] = part
+    per = n // shards
+    for i in range(len(group)):
+        for j, off in enumerate(offsets):
+            part = res[j * depth : (j + 1) * depth, i * width : (i + 1) * width]
+            at = me ^ off
+            if per == 0:
+                out_refs[i][pl.ds(pl.multiple_of(at * depth, 16), depth), :] = part
+                continue
+            shard = lax.div(at, per)
+            for d in range(shards):
+                for r in range(per):
+                    hit = jnp.logical_and(shard == lax.rem(idx_ref[1] + d, shards), lax.rem(at, per) == r)
+                    ref = out_refs[(i * shards + d) * per + r]
+
+                    @pl.when(hit)
+                    def _(ref=ref, part=part):
+                        ref[...] = part
 
 
 def qkv_kernel(offsets, idx_ref, *refs):
@@ -159,7 +163,7 @@
     out_ref[...] = total.astype(BF16)
 
 
-def call(kernel, out, scratch, idx, *arrays):
+def call(kernel, out, scratch, mib, idx, *arrays):
     vmem = pl.BlockSpec(memory_space=pltpu.VMEM)
     return pl.pallas_call(
         kernel,
@@ -167,8 +171,12 @@
         in_specs=[pl.BlockSpec(memory_space=pltpu.SMEM)] + [vmem] * len(arrays),
         out_specs=jax.tree.map(lambda _: vmem, out),
         scratch_shapes=scratch,
-        compiler_params=pltpu.CompilerParams(vmem_limit_bytes=VMEM_BYTES),
+        compiler_params=pltpu.CompilerParams(vmem_limit_bytes=mib * 1024 * 1024),
     )(idx, *arrays)
+
+
+def after(value, *others):
+    return lax.optimization_barrier((value, *others))[0]
 
 
 def edge_columns(x):
@@ -182,29 +190,56 @@
 
 
 def gathered(value, axis, bits):
-    blocks, offsets = [value], [0]
+    blocks = [value]
     for bit in bits:
         blocks = blocks + [swap(b, axis, bit) for b in blocks]
-        offsets = offsets + [o ^ bit for o in offsets]
-    return blocks, offsets
-
-
-def chain_sum(part, axis):
+    return blocks
+
+
+def added(a, b):
+    return (a.astype(F32) + b.astype(F32)).astype(BF16)
+
+
+def chain_stages(axis):
     peers = lax.axis_size(axis)
-    if peers % 2:
-        return lax.psum(part, axis)
     me = lax.axis_index(axis)
     half = peers // 2
-    total = part
+    stages = []
     for i in range(half - 1):
-        got = lax.ppermute(total, axis, [(i, i + 1), (peers - 1 - i, peers - 2 - i)])
-        total = (total.astype(F32) + got.astype(F32)).astype(BF16)
-    got = lax.ppermute(total, axis, [(half - 1, half), (half, half - 1)])
-    total = (total.astype(F32) + got.astype(F32)).astype(BF16)
+        stages.append((axis, [(i, i + 1), (peers - 1 - i, peers - 2 - i)], added))
+    stages.append((axis, [(half - 1, half), (half, half - 1)], added))
     for i in reversed(range(half - 1)):
-        got = lax.ppermute(total, axis, [(i + 1, i), (peers - 2 - i, peers - 1 - i)])
-        total = jnp.where(jnp.logical_or(me == i, me == peers - 1 - i), got, total)
-    return total
+        outer = jnp.logical_or(me == i, me == peers - 1 - i)
+        choose = lambda a, b, outer=outer: jnp.where(outer, b, a)
+        stages.append((axis, [(i + 1, i), (peers - 2 - i, peers - 1 - i)], choose))
+    return stages
+
+
+def pipelined(parts, stages, sent=None):
+    n, depth = len(parts), len(stages)
+    state, flying, last = list(parts), [None] * n, None
+    late = None
+
+    def launch(c, i, value):
+        axis, pairs, _ = stages[i]
+        flying[c] = lax.ppermute(value, axis, pairs)
+
+    first = list(parts if sent is None else sent)
+    launch(0, 0, first[0])
+    for step in range(n + depth - 1):
+        if step + 1 < n:
+            launch(step + 1, 0, first[step + 1] if last is None else after(first[step + 1], last))
+        for i in range(depth):
+            c = step - i
+            if not 0 <= c < n:
+                continue
+            got = flying[c] if last is None else after(flying[c], last)
+            state[c] = stages[i][2](state[c], got)
+            last = state[c]
+            if i + 1 < depth:
+                launch(c, i + 1, state[c])
+                late = last
+    return state, late
 
 
 def on_device(block_input, conv_weight, norm_gain, qkv_weight, encoder_grad):
@@ -215,11 +250,9 @@
     bits = [1 << b for b in reversed(range(peers.bit_length() - 1))]
     idx = jnp.stack([lax.axis_index("mp"), lax.axis_index("seq")]).astype(jnp.int32)
 
-    blocks, offsets = gathered(x, "mp", bits)
-    edges, _ = gathered(edge_columns(x), "mp", bits)
-    halos = [jnp.pad(e, ((0, 0), (0, LANES - e.shape[1]))) for e in edges]
-    gains, _ = gathered(norm_gain.reshape(1, -1), "mp", bits)
-
+    offsets = [0]
+    for bit in bits:
+        offsets = offsets + [o ^ bit for o in offsets]
     near = [j for j, o in enumerate(offsets) if o < 2]
     far = [j for j, o in enumerate(offsets) if o >= 2]
     half = length // 2
@@ -228,45 +261,74 @@
         pltpu.VMEM((length + 16, len(at) * depth), BF16),
         pltpu.VMEM((taps * width // LANES, length + 2 * EDGE, LANES), F32),
     ]
+
+    blocks = [x]
+    for bit in bits[:-1]:
+        blocks = blocks + [swap(b, "mp", bit) for b in blocks]
+    own = swap(x, "mp", bits[-1])
+    edges = gathered(edge_columns(x), "mp", bits)
+    gains = gathered(norm_gain.reshape(1, -1), "mp", bits)
+    halos = [jnp.pad(e, ((0, 0), (0, LANES - e.shape[1]))) for e in edges]
     part = jax.ShapeDtypeStruct((half, width), F32)
     even, odd = call(
         functools.partial(first_kernel, pick(offsets, near)),
         (part, part),
         scratch(near),
-        idx, *pick(blocks, near), *pick(halos, near), conv_weight,
+        40,
+        after(idx, *gains), x, own, *pick(halos, near), conv_weight,
     )
+    blocks = blocks + [own] + [swap(after(b, even), "mp", bits[-1]) for b in blocks[1:]]
     encoded, pre_grad = call(
         functools.partial(second_kernel, pick(offsets, far)),
         (jax.ShapeDtypeStruct((half, width), BF16), jax.ShapeDtypeStruct((length + 2 * EDGE, width), F32)),
         scratch(far) + [pltpu.VMEM((width // LANES, length, LANES), F32)],
+        40,
         idx, *pick(blocks, far), *pick(halos, far), conv_weight, even, odd, encoder_grad[0],
     )
 
-    total = peers * depth
     pair = shards == 2 and peers % shards == 0
-    rows = total // shards if pair else total
-    sums = []
-    for k in range(taps):
+    per = peers // shards if pair else 0
+    out = (depth, width) if pair else (peers * depth, width)
+    count = shards * per if pair else 1
+    keep, send = [], []
+    done = idx
+    encs = [encoded]
+    for bit in bits[:-1]:
+        encs = encs + [swap(e, "mp", bit) for e in encs]
+    encs_own = swap(encoded, "mp", bits[-1])
+    for group in [(0,)] + [tuple(range(k, min(k + 2, taps))) for k in range(1, taps, 2)]:
         outs = call(
-            functools.partial(grad_kernel, offsets, k, shards),
-            (jax.ShapeDtypeStruct((rows, width), BF16),) * (2 if pair else 1),
-            [pltpu.VMEM((LANES, width), F32)],
-            idx, *blocks, *halos, pre_grad,
+            functools.partial(grad_kernel, offsets, group, shards if pair else peers + 1),
+            (jax.ShapeDtypeStruct(out, BF16),) * (count * len(group)),
+            [pltpu.VMEM((LANES, width * len(group)), F32)],
+            28,
+            done, *blocks, *halos, pre_grad,
         )
-        if pair:
-            got = swap(outs[1], "seq", 1)
-            share = (outs[0].astype(F32) + got.astype(F32)).astype(BF16)
-        else:
-            share = lax.psum_scatter(outs[0], "seq", scatter_dimension=0, tiled=True)
-        sums.append(chain_sum(share, "dp"))
+        done = after(idx, outs[0], *(encs[1:] if group[0] else ()))
+        if not pair:
+            keep += [lax.psum_scatter(o, "seq", scatter_dimension=0, tiled=True) for o in outs]
+            continue
+        for i in range(len(group)):
+            keep += outs[i * count : i * count + per]
+            send += outs[i * count + per : (i + 1) * count]
+    encs = encs + [encs_own] + [swap(e, "mp", bits[-1]) for e in encs[1:]]
+    keep[1] = after(keep[1], *encs)
+    stages = chain_stages("dp") if lax.axis_size("dp") % 2 == 0 else []
+    if pair:
+        stages = [("seq", [(0, 1), (1, 0)], added)] + stages
+    sums, late = pipelined(keep, stages, send if pair else None)
+    if lax.axis_size("dp") % 2:
+        sums = [lax.psum(s, "dp") for s in sums]
+    lines = max(per, 1)
+    sums = [jnp.concatenate(sums[k * lines : (k + 1) * lines], axis=0) for k in range(taps)]
     conv_grad = jnp.stack([s.astype(F32) for s in sums], axis=1)
 
-    encs, _ = gathered(encoded, "mp", bits)
     qkv = call(
         functools.partial(qkv_kernel, offsets),
         jax.ShapeDtypeStruct((half, qkv_weight.shape[1]), BF16),
         [],
-        idx, *encs, *gains, qkv_weight,
+        20,
+        idx if late is None else after(idx, late), *encs, *gains, qkv_weight,
     )
     return (qkv[None], conv_grad)
 

time: 227 us -> 168 us (0.74)
  waiting for transfers between devices: 128 us -> 44.6 us
  starting transfers between devices: 36.8 us -> 79.2 us
  Pallas kernels: 48.9 us -> 26.1 us
  other arithmetic: 5.85 us -> 8.16 us
    ppermute x15 -> x40, waiting for transfers between devices: 80.6 us -> 26 us  [launch(): flying[c] = lax.ppermute(value, axis, pairs)]
    ppermute x15 -> x40, starting transfers between devices: 20.9 us -> 67 us  [launch(): flying[c] = lax.ppermute(value, axis, pairs)]
    ppermute x17 -> x12, waiting for transfers between devices: 42.2 us -> 14.8 us  [swap(): return lax.ppermute(value, axis, [(i, i ^ bit) for i in range(peers)])]
    pallas_call x8 -> x6, Pallas kernels: 48.9 us -> 26.1 us  [call(): pl.pallas_call(kernel, out_shape=out, in_specs=[pl.BlockSpec(memory_space...]
    unnamed x38 -> x22, local copies, waits for them, and re-layouts: 1.78 us -> 5.68 us
    ppermute x17 -> x12, starting transfers between devices: 11.1 us -> 7.43 us  [swap(): return lax.ppermute(value, axis, [(i, i ^ bit) for i in range(peers)])]
    convert_element_type x15 -> x30, other arithmetic: 1.84 us -> 4.7 us  [added(): return (a.astype(F32) + b.astype(F32)).astype(BF16)]
    pad x4, local copies, waits for them, and re-layouts: 2.6 us -> 0.08 us  [on_device(): halos = [jnp.pad(e, ((0, 0), (0, LANES - e.shape[1]))) for e in edges]]
  transfers between devices with their start and end apart: 34 -> 54, of which waited for: 15 -> 17; matrix products, arithmetic and copies ran while one was open for 3% -> 4% of each run, Pallas kernels for 15% -> 12%
where the time goes in v2:
time: 168 us; the launch traced here: 167 us
  starting transfers between devices  79.2 us (47%)
  waiting for transfers between devices  44.6 us (27%)
  Pallas kernels  26.1 us (16%)
  other arithmetic  8.16 us (5%)
  local copies, waits for them, and re-layouts  7.49 us (4%)
    ppermute x40, starting transfers between devices, launch(): flying[c] = lax.ppermute(value, axis, pairs)  67 us
    pallas_call x6, Pallas kernels, call(): pl.pallas_call(kernel, out_shape=out, in_specs=[pl.BlockSpec(memory_space...  26.1 us
    ppermute x40, waiting for transfers between devices, launch(): flying[c] = lax.ppermute(value, axis, pairs)  26 us
    ppermute x12, waiting for transfers between devices, swap(): return lax.ppermute(value, axis, [(i, i ^ bit) for i in range(peers)])  14.8 us
    ppermute x12, starting transfers between devices, swap(): return lax.ppermute(value, axis, [(i, i ^ bit) for i in range(peers)])  7.43 us
    unnamed x22, local copies, waits for them, and re-layouts  5.68 us
    convert_element_type x30, other arithmetic, added(): return (a.astype(F32) + b.astype(F32)).astype(BF16)  4.7 us
    ppermute x1, waiting for transfers between devices, edge_columns(): after = lax.ppermute(x[:, :2], 'seq', down)  3.84 us
  transfers between devices with their start and end apart: 54, of which 17 were waited for; matrix products, arithmetic and copies ran while one was open for 4% of the time, Pallas kernels for 12%

profile of v2, /device:TPU:0, one launch (start us, length us, event | category | flops | bytes accessed | tf_op | source)
XLA Modules:
  0.0 167.0 jit_solution(5615313876297084300)
XLA Ops:
  1.1 2.6 %collective-permute-start = (bf16[320,1024]{1,0:T(8,128)(2,1)}, bf16[320,1024]{1,0:T(8,128)(2,1)S(1)}, u32[]{:S(2)}, u32[]{:S(2)}) collective-permute-start(bf16[320,1024]{1,0:T(8,128)(2,1)} %bitcast.19), channel_id=1, source_target_pairs={{0,8},{4,12},{8,0},{12,4},{1,9},{5,13},{9,1},{13,5},{2,10},{6,14},... | collective-permute-start | bytes 1966088 | tf_op jit(solution)/shard_map/ppermute | solution.py:26
  4.8 3.4 %collective-permute-start.5 = (bf16[320,2]{1,0:T(8,128)(2,1)S(1)}, bf16[320,2]{1,0:T(8,128)(2,1)S(1)}, u32[]{:S(2)}, u32[]{:S(2)}) collective-permute-start(bf16[320,2]{1,0:T(8,128)(2,1)S(1)} %get-tuple-element.156), channel_id=1, source_target_pairs={{0,16},{1,17},{2,18},{3,19},{4,20},{5,21},{6,22},{7,23},{8,24},{9,... | collective-permute-start | bytes 3848 | tf_op jit(solution)/shard_map/ppermute | solution.py:187
  8.2 1.3 collective-permute-start.6
  10.7 3.8 %collective-permute-done.6 = bf16[320,2]{1,0:T(8,128)(2,1)S(1)} collective-permute-done((bf16[320,2]{1,0:T(8,128)(2,1)S(1)}, bf16[320,2]{1,0:T(8,128)(2,1)S(1)}, u32[]{:S(2)}, u32[]{:S(2)}) %collective-permute-start.6) | collective-permute-done | bytes 1312 | tf_op jit(solution)/shard_map/ppermute | solution.py:188
  14.7 4.6 %collective-permute-done.2.refs_5_ = f32[1,384]{1,0:T(1,128)S(1)} collective-permute-done((f32[1,384]{1,0:T(1,128)S(1)}, f32[1,384]{1,0:T(1,128)S(1)}, u32[]{:S(2)}, u32[]{:S(2)}) %collective-permute-start.2) | collective-permute-done | bytes 1568 | tf_op jit(solution)/shard_map/ppermute | solution.py:26
  20.5 2.4 %copy-done = bf16[5,1280,384]{2,1,0:T(8,128)(2,1)S(1)} copy-done((bf16[5,1280,384]{2,1,0:T(8,128)(2,1)S(1)}, bf16[5,1280,384]{2,1,0:T(8,128)(2,1)}, u32[]{:S(2)}) %copy-start) | copy-done | bytes 4915224
  24.0 4.3 %shard_map.68 = (f32[512,384]{1,0:T(8,128)S(1)}, f32[512,384]{1,0:T(8,128)S(1)}) custom-call(s32[2]{0:T(128)S(1)} %pad_add_fusion.idx_ref, bf16[320,1024]{1,0:T(8,128)(2,1)S(1)} %bitcast.21, bf16[320,1024]{1,0:T(8,128)(2,1)S(1)} %collective-permute-done.1.refs_1_.refs_2_, bf16[320,128]{1,0:T(8,128)(2,1)S(1)} %pad.13.refs_2_.refs_4_, ...), custom_call_target="tpu_custom_call" | custom-call | tf_op jit(solution)/shard_map/pallas_call | solution.py:168
  28.6 1.8 %collective-permute-start.9 = (bf16[320,4]{1,0:T(8,128)(2,1)S(1)}, bf16[320,4]{1,0:T(8,128)(2,1)S(1)}, u32[]{:S(2)}, u32[]{:S(2)}) collective-permute-start(bf16[320,4]{1,0:T(8,128)(2,1)S(1)} %pad_maximum_fusion), channel_id=1, source_target_pairs={{0,8},{4,12},{8,0},{12,4},{1,9},{5,13},{9,1},{13,5},{2,10},{6,14},... | collective-permute-start | bytes 7688 | tf_op jit(solution)/shard_map/ppermute | solution.py:26
  30.3 2.9 %collective-permute-done.9 = bf16[320,4]{1,0:T(8,128)(2,1)S(1)} collective-permute-done((bf16[320,4]{1,0:T(8,128)(2,1)S(1)}, bf16[320,4]{1,0:T(8,128)(2,1)S(1)}, u32[]{:S(2)}, u32[]{:S(2)}) %collective-permute-start.9) | collective-permute-done | bytes 2592 | tf_op jit(solution)/shard_map/ppermute | solution.py:26
  33.3 1.3 collective-permute-done.10
  34.6 6.5 %shard_map.69 = (bf16[512,384]{1,0:T(8,128)(2,1)}, f32[1040,384]{1,0:T(8,128)S(1)}) custom-call(s32[2]{0:T(128)S(1)} %pad_add_fusion.idx_ref, bf16[320,1024]{1,0:T(8,128)(2,1)S(1)} %collective-permute-done.refs_0_.refs_1_, bf16[320,1024]{1,0:T(8,128)(2,1)S(1)} %collective-permute-done.8.refs_1_.refs_3_, bf16[320,128]{1,0:T(8,128)(2,1)S(1)} %pad.15.refs_2_.refs_5_, ...), custom_call_target="tpu_custom_call" | custom-call | tf_op jit(solution)/shard_map/pallas_call | solution.py:168
  41.1 1.7 %collective-permute-start.11 = (bf16[512,384]{1,0:T(8,128)(2,1)}, bf16[512,384]{1,0:T(8,128)(2,1)}, u32[]{:S(2)}, u32[]{:S(2)}) collective-permute-start(bf16[512,384]{1,0:T(8,128)(2,1)} %get-tuple-element.87.refs_0_), channel_id=1, source_target_pairs={{0,8},{4,12},{8,0},{12,4},{1,9},{5,13},{9,1},{13,5},{2,10},{6,14},... | collective-permute-start | bytes 1179656 | tf_op jit(solution)/shard_map/ppermute | solution.py:26
  42.9 3.3 %shard_map.70 = (bf16[320,384]{1,0:T(8,128)(2,1)S(1)}, bf16[320,384]{1,0:T(8,128)(2,1)S(1)}, bf16[320,384]{1,0:T(8,128)(2,1)S(1)}, bf16[320,384]{1,0:T(8,128)(2,1)}) custom-call(s32[2]{0:T(128)S(1)} %pad_add_fusion.idx_ref, bf16[320,1024]{1,0:T(8,128)(2,1)S(1)} %bitcast.22, bf16[320,1024]{1,0:T(8,128)(2,1)S(1)} %collective-permute-done.refs_0_.refs_1_, ...), custom_call_target="tpu_custom_call" | custom-call | tf_op jit(solution)/shard_map/pallas_call | solution.py:168
  46.1 1.5 collective-permute-start.12
  47.6 5.0 %collective-permute-done.11.refs_1_ = bf16[512,384]{1,0:T(8,128)(2,1)} collective-permute-done((bf16[512,384]{1,0:T(8,128)(2,1)}, bf16[512,384]{1,0:T(8,128)(2,1)}, u32[]{:S(2)}, u32[]{:S(2)}) %collective-permute-start.11) | collective-permute-done | bytes 393248 | tf_op jit(solution)/shard_map/ppermute | solution.py:26
  52.6 1.7 %collective-permute-start.16 = (bf16[320,384]{1,0:T(8,128)(2,1)}, bf16[320,384]{1,0:T(8,128)(2,1)}, u32[]{:S(2)}, u32[]{:S(2)}) collective-permute-start(bf16[320,384]{1,0:T(8,128)(2,1)} %get-tuple-element.96), channel_id=1, source_target_pairs={{0,16},{16,0},{1,17},{17,1},{2,18},{18,2},{3,19},{19,3},{4,20},{20... | collective-permute-start | bytes 737288 | tf_op jit(solution)/shard_map/ppermute | solution.py:225
  55.0 4.2 %collective-permute-start.13 = (bf16[320,384]{1,0:T(8,128)(2,1)}, bf16[320,384]{1,0:T(8,128)(2,1)}, u32[]{:S(2)}, u32[]{:S(2)}) collective-permute-start(bf16[320,384]{1,0:T(8,128)(2,1)} %add_convert_fusion.29), channel_id=1, source_target_pairs={{0,1},{3,2},{4,5},{7,6},{8,9},{11,10},{12,13},{15,14},{16,17},{19,... | collective-permute-start | bytes 737288 | tf_op jit(solution)/shard_map/ppermute | solution.py:225
  61.4 3.8 %shard_map.71 = (bf16[320,384]{1,0:T(8,128)(2,1)S(1)}, bf16[320,384]{1,0:T(8,128)(2,1)S(1)}, bf16[320,384]{1,0:T(8,128)(2,1)S(1)}, bf16[320,384]{1,0:T(8,128)(2,...) custom-call(s32[2]{0:T(128)S(1)} %pad_add_fusion.idx_ref, ...), custom_call_target="tpu_custom_call" | custom-call | tf_op jit(solution)/shard_map/pallas_call | solution.py:168
  66.4 3.8 %shard_map.72 = (bf16[320,384]{1,0:T(8,128)(2,1)S(1)}, bf16[320,384]{1,0:T(8,128)(2,1)S(1)}, bf16[320,384]{1,0:T(8,128)(2,1)S(1)}, bf16[320,384]{1,0:T(8,128)(2,...) custom-call(s32[2]{0:T(128)S(1)} %pad_add_fusion.idx_ref, ...), custom_call_target="tpu_custom_call" | custom-call | tf_op jit(solution)/shard_map/pallas_call | solution.py:168
  71.2 1.3 collective-permute-start.18
  75.5 3.6 %collective-permute-start.23 = (bf16[320,384]{1,0:T(8,128)(2,1)S(1)}, bf16[320,384]{1,0:T(8,128)(2,1)S(1)}, u32[]{:S(2)}, u32[]{:S(2)}) collective-permute-start(bf16[320,384]{1,0:T(8,128)(2,1)S(1)} %add_convert_fusion.26), channel_id=1, source_target_pairs={{0,1},{3,2},{4,5},{7,6},{8,9},{11,10},{12,13},{15,14},{16,17},{19,... | collective-permute-start | bytes 737288 | tf_op jit(solution)/shard_map/ppermute | solution.py:225
  79.9 1.3 collective-permute-start.21
  81.5 5.3 %collective-permute-start.29 = (bf16[320,384]{1,0:T(8,128)(2,1)S(1)}, bf16[320,384]{1,0:T(8,128)(2,1)S(1)}, u32[]{:S(2)}, u32[]{:S(2)}) collective-permute-start(bf16[320,384]{1,0:T(8,128)(2,1)S(1)} %add_convert_fusion.23), channel_id=1, source_target_pairs={{0,1},{3,2},{4,5},{7,6},{8,9},{11,10},{12,13},{15,14},{16,17},{19,... | collective-permute-start | bytes 737288 | tf_op jit(solution)/shard_map/ppermute | solution.py:225
  86.9 2.3 %collective-permute-start.20 = (bf16[320,384]{1,0:T(8,128)(2,1)S(1)}, bf16[320,384]{1,0:T(8,128)(2,1)S(1)}, u32[]{:S(2)}, u32[]{:S(2)}) collective-permute-start(bf16[320,384]{1,0:T(8,128)(2,1)S(1)} %get-tuple-element.104), channel_id=1, source_target_pairs={{0,16},{16,0},{1,17},{17,1},{2,18},{18,2},{3,19},{19,3},{4,20},{20... | collective-permute-start | bytes 737288 | tf_op jit(solution)/shard_map/ppermute | solution.py:225
  89.9 1.3 collective-permute-start.27
  91.3 2.1 %collective-permute-done.20 = bf16[320,384]{1,0:T(8,128)(2,1)S(1)} collective-permute-done((bf16[320,384]{1,0:T(8,128)(2,1)S(1)}, bf16[320,384]{1,0:T(8,128)(2,1)S(1)}, u32[]{:S(2)}, u32[]{:S(2)}) %collective-permute-start.20) | collective-permute-done | bytes 245792 | tf_op jit(solution)/shard_map/ppermute | solution.py:225
  93.4 2.5 %collective-permute-start.25 = (bf16[320,384]{1,0:T(8,128)(2,1)S(1)}, bf16[320,384]{1,0:T(8,128)(2,1)S(1)}, u32[]{:S(2)}, u32[]{:S(2)}) collective-permute-start(bf16[320,384]{1,0:T(8,128)(2,1)S(1)} %add_convert_fusion.20), channel_id=1, source_target_pairs={{0,1},{3,2},{4,5},{7,6},{8,9},{11,10},{12,13},{15,14},{16,17},{19,... | collective-permute-start | bytes 737288 | tf_op jit(solution)/shard_map/ppermute | solution.py:225
  97.7 1.3 collective-permute-start.33
  99.0 4.0 %collective-permute-done.26 = bf16[320,384]{1,0:T(8,128)(2,1)S(1)} collective-permute-done((bf16[320,384]{1,0:T(8,128)(2,1)S(1)}, bf16[320,384]{1,0:T(8,128)(2,1)S(1)}, u32[]{:S(2)}, u32[]{:S(2)}) %collective-permute-start.26) | collective-permute-done | bytes 245792 | tf_op jit(solution)/shard_map/ppermute | solution.py:225
  103.1 2.5 %collective-permute-start.31 = (bf16[320,384]{1,0:T(8,128)(2,1)S(1)}, bf16[320,384]{1,0:T(8,128)(2,1)S(1)}, u32[]{:S(2)}, u32[]{:S(2)}) collective-permute-start(bf16[320,384]{1,0:T(8,128)(2,1)S(1)} %add_convert_fusion.17), channel_id=1, source_target_pairs={{0,1},{3,2},{4,5},{7,6},{8,9},{11,10},{12,13},{15,14},{16,17},{19,... | collective-permute-start | bytes 737288 | tf_op jit(solution)/shard_map/ppermute | solution.py:225
  106.4 1.3 collective-permute-start.39
  110.0 4.5 %collective-permute-done.32 = bf16[320,384]{1,0:T(8,128)(2,1)S(1)} collective-permute-done((bf16[320,384]{1,0:T(8,128)(2,1)S(1)}, bf16[320,384]{1,0:T(8,128)(2,1)S(1)}, u32[]{:S(2)}, u32[]{:S(2)}) %collective-permute-start.32) | collective-permute-done | bytes 245792 | tf_op jit(solution)/shard_map/ppermute | solution.py:225
  114.6 4.3 %collective-permute-start.37 = (bf16[320,384]{1,0:T(8,128)(2,1)S(1)}, bf16[320,384]{1,0:T(8,128)(2,1)S(1)}, u32[]{:S(2)}, u32[]{:S(2)}) collective-permute-start(bf16[320,384]{1,0:T(8,128)(2,1)S(1)} %add_convert_fusion.14), channel_id=1, source_target_pairs={{0,1},{3,2},{4,5},{7,6},{8,9},{11,10},{12,13},{15,14},{16,17},{19,... | collective-permute-start | bytes 737288 | tf_op jit(solution)/shard_map/ppermute | solution.py:225
  119.7 1.3 collective-permute-start.35
  122.2 4.6 %collective-permute-start.43 = (bf16[320,384]{1,0:T(8,128)(2,1)S(1)}, bf16[320,384]{1,0:T(8,128)(2,1)S(1)}, u32[]{:S(2)}, u32[]{:S(2)}) collective-permute-start(bf16[320,384]{1,0:T(8,128)(2,1)S(1)} %add_convert_fusion.11), channel_id=1, source_target_pairs={{0,1},{3,2},{4,5},{7,6},{8,9},{11,10},{12,13},{15,14},{16,17},{19,... | collective-permute-start | bytes 737288 | tf_op jit(solution)/shard_map/ppermute | solution.py:225
  127.7 1.3 collective-permute-start.41
  129.9 4.8 %collective-permute-start.48 = (bf16[320,384]{1,0:T(8,128)(2,1)S(1)}, bf16[320,384]{1,0:T(8,128)(2,1)S(1)}, u32[]{:S(2)}, u32[]{:S(2)}) collective-permute-start(bf16[320,384]{1,0:T(8,128)(2,1)S(1)} %add_convert_fusion.8), channel_id=1, source_target_pairs={{0,1},{3,2},{4,5},{7,6},{8,9},{11,10},{12,13},{15,14},{16,17},{19,... | collective-permute-start | bytes 737288 | tf_op jit(solution)/shard_map/ppermute | solution.py:225
  135.7 1.5 collective-permute-start.46
  137.2 2.1 %collective-permute-done.41 = bf16[320,384]{1,0:T(8,128)(2,1)S(1)} collective-permute-done((bf16[320,384]{1,0:T(8,128)(2,1)S(1)}, bf16[320,384]{1,0:T(8,128)(2,1)S(1)}, u32[]{:S(2)}, u32[]{:S(2)}) %collective-permute-start.41) | collective-permute-done | bytes 245792 | tf_op jit(solution)/shard_map/ppermute | solution.py:225
  139.4 1.6 collective-permute-done.40
  141.1 2.3 %collective-permute-start.45 = (bf16[320,384]{1,0:T(8,128)(2,1)S(1)}, bf16[320,384]{1,0:T(8,128)(2,1)S(1)}, u32[]{:S(2)}, u32[]{:S(2)}) collective-permute-start(bf16[320,384]{1,0:T(8,128)(2,1)S(1)} %add_convert_fusion.5), channel_id=1, source_target_pairs={{0,1},{3,2},{4,5},{7,6},{8,9},{11,10},{12,13},{15,14},{16,17},{19,... | collective-permute-start | bytes 737288 | tf_op jit(solution)/shard_map/ppermute | solution.py:225
  144.2 1.3 collective-permute-start.50
  147.9 1.3 collective-permute-start.52
  149.2 4.3 %collective-permute-done.50 = bf16[320,384]{1,0:T(8,128)(2,1)S(1)} collective-permute-done((bf16[320,384]{1,0:T(8,128)(2,1)S(1)}, bf16[320,384]{1,0:T(8,128)(2,1)S(1)}, u32[]{:S(2)}, u32[]{:S(2)}) %collective-permute-start.50) | collective-permute-done | bytes 245792 | tf_op jit(solution)/shard_map/ppermute | solution.py:225
  153.6 1.3 collective-permute-start.53
  155.0 4.9 %collective-permute-done.52 = bf16[320,384]{1,0:T(8,128)(2,1)S(1)} collective-permute-done((bf16[320,384]{1,0:T(8,128)(2,1)S(1)}, bf16[320,384]{1,0:T(8,128)(2,1)S(1)}, u32[]{:S(2)}, u32[]{:S(2)}) %collective-permute-start.52) | collective-permute-done | bytes 245792 | tf_op jit(solution)/shard_map/ppermute | solution.py:225
  159.8 4.4 %shard_map.73 = bf16[512,640]{1,0:T(8,128)(2,1)} custom-call(s32[2]{0:T(128)S(1)} %pad_add_fusion.idx_ref, bf16[512,384]{1,0:T(8,128)(2,1)} %get-tuple-element.87.refs_0_, bf16[512,384]{1,0:T(8,128)(2,1)} %collective-permute-done.11.refs_1_, bf16[512,384]{1,0:T(8,128)(2,1)} %collective-permute-done.14.refs_2_, ...), custom_call_target="tpu_custom_call" | custom-call | tf_op jit(solution)/shard_map/pallas_call | solution.py:168
  164.4 2.6 %stack.24 = f32[640,5,384]{2,0,1:T(8,128)} convert(bf16[640,5,384]{2,0,1:T(8,128)(2,1)S(1)} %maximum_dynamic-update-slice_fusion) | non-fusion elementwise | flops 1228800 | bytes 7372800 | tf_op jit(solution)/shard_map/stack | solution.py:324
  (142 shorter events, 28.7 us)
Async XLA Ops:
  0.6 19.9 %collective-permute-start.1 = (bf16[320,1024]{1,0:T(8,128)(2,1)}, bf16[320,1024]{1,0:T(8,128)(2,1)S(1)}, u32[]{:S(2)}, u32[]{:S(2)}) collective-permute-start(bf16[320,1024]{1,0:T(8,128)(2,1)} %bitcast.18), channel_id=1, source_target_pairs={{0,4},{4,0},{8,12},{12,8},{1,5},{5,1},{9,13},{13,9},{2,6},{6,2},{1... | collective-permute-start | bytes 1966088 | tf_op jit(solution)/shard_map/ppermute | solution.py:26
  1.1 27.2 %collective-permute-start = (bf16[320,1024]{1,0:T(8,128)(2,1)}, bf16[320,1024]{1,0:T(8,128)(2,1)S(1)}, u32[]{:S(2)}, u32[]{:S(2)}) collective-permute-start(bf16[320,1024]{1,0:T(8,128)(2,1)} %bitcast.19), channel_id=1, source_target_pairs={{0,8},{4,12},{8,0},{12,4},{1,9},{5,13},{9,1},{13,5},{2,10},{6,14},... | collective-permute-start | bytes 1966088 | tf_op jit(solution)/shard_map/ppermute | solution.py:26
  8.2 6.3 %collective-permute-start.6 = (bf16[320,2]{1,0:T(8,128)(2,1)S(1)}, bf16[320,2]{1,0:T(8,128)(2,1)S(1)}, u32[]{:S(2)}, u32[]{:S(2)}) collective-permute-start(bf16[320,2]{1,0:T(8,128)(2,1)S(1)} %get-tuple-element.157), channel_id=1, source_target_pairs={{16,0},{17,1},{18,2},{19,3},{20,4},{21,5},{22,6},{23,7},{24,8},{25... | collective-permute-start | bytes 3848 | tf_op jit(solution)/shard_map/ppermute | solution.py:188
  10.2 9.1 %collective-permute-start.2 = (f32[1,384]{1,0:T(1,128)S(1)}, f32[1,384]{1,0:T(1,128)S(1)}, u32[]{:S(2)}, u32[]{:S(2)}) collective-permute-start(f32[1,384]{1,0:T(1,128)S(1)} %reshape.152.refs_4_), channel_id=1, source_target_pairs={{0,8},{4,12},{8,0},{12,4},{1,9},{5,13},{9,1},{13,5},{2,10},{6,14},... | collective-permute-start | bytes 4616 | tf_op jit(solution)/shard_map/ppermute | solution.py:26
  10.7 8.7 %collective-permute-start.3 = (f32[1,384]{1,0:T(1,128)S(1)}, f32[1,384]{1,0:T(1,128)S(1)}, u32[]{:S(2)}, u32[]{:S(2)}) collective-permute-start(f32[1,384]{1,0:T(1,128)S(1)} %reshape.152.refs_4_), channel_id=1, source_target_pairs={{0,4},{4,0},{8,12},{12,8},{1,5},{5,1},{9,13},{13,9},{2,6},{6,2},{1... | collective-permute-start | bytes 4616 | tf_op jit(solution)/shard_map/ppermute | solution.py:26
  28.3 6.2 %collective-permute-start.8 = (bf16[320,1024]{1,0:T(8,128)(2,1)S(1)}, bf16[320,1024]{1,0:T(8,128)(2,1)S(1)}, u32[]{:S(2)}, u32[]{:S(2)}) collective-permute-start(bf16[320,1024]{1,0:T(8,128)(2,1)S(1)} %collective-permute-done.refs_0_.refs_1_), channel_id=1, source_target_pairs={{0,4},{4,0},{8,12},{12,8},{1,5},{5,1},{9,13},{13,9},{2,6},{6,2},{1... | collective-permute-start | bytes 1966088 | tf_op jit(solution)/shard_map/ppermute | solution.py:26
  41.1 11.5 %collective-permute-start.11 = (bf16[512,384]{1,0:T(8,128)(2,1)}, bf16[512,384]{1,0:T(8,128)(2,1)}, u32[]{:S(2)}, u32[]{:S(2)}) collective-permute-start(bf16[512,384]{1,0:T(8,128)(2,1)} %get-tuple-element.87.refs_0_), channel_id=1, source_target_pairs={{0,8},{4,12},{8,0},{12,4},{1,9},{5,13},{9,1},{13,5},{2,10},{6,14},... | collective-permute-start | bytes 1179656 | tf_op jit(solution)/shard_map/ppermute | solution.py:26
  46.1 8.2 %collective-permute-start.12 = (bf16[320,384]{1,0:T(8,128)(2,1)S(1)}, bf16[320,384]{1,0:T(8,128)(2,1)S(1)}, u32[]{:S(2)}, u32[]{:S(2)}) collective-permute-start(bf16[320,384]{1,0:T(8,128)(2,1)S(1)} %get-tuple-element.93), channel_id=1, source_target_pairs={{0,16},{16,0},{1,17},{17,1},{2,18},{18,2},{3,19},{19,3},{4,20},{20... | collective-permute-start | bytes 737288 | tf_op jit(solution)/shard_map/ppermute | solution.py:225
  47.6 22.6 %collective-permute-start.14 = (bf16[512,384]{1,0:T(8,128)(2,1)}, bf16[512,384]{1,0:T(8,128)(2,1)}, u32[]{:S(2)}, u32[]{:S(2)}) collective-permute-start(bf16[512,384]{1,0:T(8,128)(2,1)} %get-tuple-element.87.refs_0_), channel_id=1, source_target_pairs={{0,4},{4,0},{8,12},{12,8},{1,5},{5,1},{9,13},{13,9},{2,6},{6,2},{1... | collective-permute-start | bytes 1179656 | tf_op jit(solution)/shard_map/ppermute | solution.py:26
  52.6 17.6 %collective-permute-start.15 = (bf16[512,384]{1,0:T(8,128)(2,1)}, bf16[512,384]{1,0:T(8,128)(2,1)}, u32[]{:S(2)}, u32[]{:S(2)}) collective-permute-start(bf16[512,384]{1,0:T(8,128)(2,1)} %collective-permute-done.11.refs_1_), channel_id=1, source_target_pairs={{0,4},{4,0},{8,12},{12,8},{1,5},{5,1},{9,13},{13,9},{2,6},{6,2},{1... | collective-permute-start | bytes 1179656 | tf_op jit(solution)/shard_map/ppermute | solution.py:26
  52.6 12.7 %collective-permute-start.16 = (bf16[320,384]{1,0:T(8,128)(2,1)}, bf16[320,384]{1,0:T(8,128)(2,1)}, u32[]{:S(2)}, u32[]{:S(2)}) collective-permute-start(bf16[320,384]{1,0:T(8,128)(2,1)} %get-tuple-element.96), channel_id=1, source_target_pairs={{0,16},{16,0},{1,17},{17,1},{2,18},{18,2},{3,19},{19,3},{4,20},{20... | collective-permute-start | bytes 737288 | tf_op jit(solution)/shard_map/ppermute | solution.py:225
  55.0 17.5 %collective-permute-start.13 = (bf16[320,384]{1,0:T(8,128)(2,1)}, bf16[320,384]{1,0:T(8,128)(2,1)}, u32[]{:S(2)}, u32[]{:S(2)}) collective-permute-start(bf16[320,384]{1,0:T(8,128)(2,1)} %add_convert_fusion.29), channel_id=1, source_target_pairs={{0,1},{3,2},{4,5},{7,6},{8,9},{11,10},{12,13},{15,14},{16,17},{19,... | collective-permute-start | bytes 737288 | tf_op jit(solution)/shard_map/ppermute | solution.py:225
  65.2 10.2 %collective-permute-start.19 = (bf16[320,384]{1,0:T(8,128)(2,1)S(1)}, bf16[320,384]{1,0:T(8,128)(2,1)S(1)}, u32[]{:S(2)}, u32[]{:S(2)}) collective-permute-start(bf16[320,384]{1,0:T(8,128)(2,1)S(1)} %get-tuple-element.100), channel_id=1, source_target_pairs={{0,16},{16,0},{1,17},{17,1},{2,18},{18,2},{3,19},{19,3},{4,20},{20... | collective-permute-start | bytes 737288 | tf_op jit(solution)/shard_map/ppermute | solution.py:225
  71.2 7.9 %collective-permute-start.18 = (bf16[320,384]{1,0:T(8,128)(2,1)S(1)}, bf16[320,384]{1,0:T(8,128)(2,1)S(1)}, u32[]{:S(2)}, u32[]{:S(2)}) collective-permute-start(bf16[320,384]{1,0:T(8,128)(2,1)S(1)} %add_convert_fusion.28), channel_id=1, source_target_pairs={{0,1},{3,2},{4,5},{7,6},{8,9},{11,10},{12,13},{15,14},{16,17},{19,... | collective-permute-start | bytes 737288 | tf_op jit(solution)/shard_map/ppermute | solution.py:225
  73.7 6.2 %collective-permute-start.17 = (bf16[320,384]{1,0:T(8,128)(2,1)S(1)}, bf16[320,384]{1,0:T(8,128)(2,1)S(1)}, u32[]{:S(2)}, u32[]{:S(2)}) collective-permute-start(bf16[320,384]{1,0:T(8,128)(2,1)S(1)} %add_convert_fusion.27), channel_id=1, source_target_pairs={{1,2},{2,1},{5,6},{6,5},{9,10},{10,9},{13,14},{14,13},{17,18},{18,... | collective-permute-start | bytes 737288 | tf_op jit(solution)/shard_map/ppermute | solution.py:225
  74.4 7.1 %collective-permute-start.24 = (bf16[320,384]{1,0:T(8,128)(2,1)S(1)}, bf16[320,384]{1,0:T(8,128)(2,1)S(1)}, u32[]{:S(2)}, u32[]{:S(2)}) collective-permute-start(bf16[320,384]{1,0:T(8,128)(2,1)S(1)} %get-tuple-element.107), channel_id=1, source_target_pairs={{0,16},{16,0},{1,17},{17,1},{2,18},{18,2},{3,19},{19,3},{4,20},{20... | collective-permute-start | bytes 737288 | tf_op jit(solution)/shard_map/ppermute | solution.py:225
  75.5 11.3 %collective-permute-start.23 = (bf16[320,384]{1,0:T(8,128)(2,1)S(1)}, bf16[320,384]{1,0:T(8,128)(2,1)S(1)}, u32[]{:S(2)}, u32[]{:S(2)}) collective-permute-start(bf16[320,384]{1,0:T(8,128)(2,1)S(1)} %add_convert_fusion.26), channel_id=1, source_target_pairs={{0,1},{3,2},{4,5},{7,6},{8,9},{11,10},{12,13},{15,14},{16,17},{19,... | collective-permute-start | bytes 737288 | tf_op jit(solution)/shard_map/ppermute | solution.py:225
  79.2 10.7 %collective-permute-start.22 = (bf16[320,384]{1,0:T(8,128)(2,1)S(1)}, bf16[320,384]{1,0:T(8,128)(2,1)S(1)}, u32[]{:S(2)}, u32[]{:S(2)}) collective-permute-start(bf16[320,384]{1,0:T(8,128)(2,1)S(1)} %add_convert_fusion.25), channel_id=1, source_target_pairs={{1,2},{2,1},{5,6},{6,5},{9,10},{10,9},{13,14},{14,13},{17,18},{18,... | collective-permute-start | bytes 737288 | tf_op jit(solution)/shard_map/ppermute | solution.py:225
  79.9 11.3 %collective-permute-start.21 = (bf16[320,384]{1,0:T(8,128)(2,1)S(1)}, bf16[320,384]{1,0:T(8,128)(2,1)S(1)}, u32[]{:S(2)}, u32[]{:S(2)}) collective-permute-start(bf16[320,384]{1,0:T(8,128)(2,1)S(1)} %add_convert_fusion.24), channel_id=1, source_target_pairs={{1,0},{2,3},{5,4},{6,7},{9,8},{10,11},{13,12},{14,15},{17,16},{18,... | collective-permute-start | bytes 737288 | tf_op jit(solution)/shard_map/ppermute | solution.py:225
  81.5 14.4 %collective-permute-start.29 = (bf16[320,384]{1,0:T(8,128)(2,1)S(1)}, bf16[320,384]{1,0:T(8,128)(2,1)S(1)}, u32[]{:S(2)}, u32[]{:S(2)}) collective-permute-start(bf16[320,384]{1,0:T(8,128)(2,1)S(1)} %add_convert_fusion.23), channel_id=1, source_target_pairs={{0,1},{3,2},{4,5},{7,6},{8,9},{11,10},{12,13},{15,14},{16,17},{19,... | collective-permute-start | bytes 737288 | tf_op jit(solution)/shard_map/ppermute | solution.py:225
  86.9 6.5 %collective-permute-start.20 = (bf16[320,384]{1,0:T(8,128)(2,1)S(1)}, bf16[320,384]{1,0:T(8,128)(2,1)S(1)}, u32[]{:S(2)}, u32[]{:S(2)}) collective-permute-start(bf16[320,384]{1,0:T(8,128)(2,1)S(1)} %get-tuple-element.104), channel_id=1, source_target_pairs={{0,16},{16,0},{1,17},{17,1},{2,18},{18,2},{3,19},{19,3},{4,20},{20... | collective-permute-start | bytes 737288 | tf_op jit(solution)/shard_map/ppermute | solution.py:225
  89.2 7.5 %collective-permute-start.28 = (bf16[320,384]{1,0:T(8,128)(2,1)S(1)}, bf16[320,384]{1,0:T(8,128)(2,1)S(1)}, u32[]{:S(2)}, u32[]{:S(2)}) collective-permute-start(bf16[320,384]{1,0:T(8,128)(2,1)S(1)} %add_convert_fusion.22), channel_id=1, source_target_pairs={{1,2},{2,1},{5,6},{6,5},{9,10},{10,9},{13,14},{14,13},{17,18},{18,... | collective-permute-start | bytes 737288 | tf_op jit(solution)/shard_map/ppermute | solution.py:225
  89.9 9.0 %collective-permute-start.27 = (bf16[320,384]{1,0:T(8,128)(2,1)S(1)}, bf16[320,384]{1,0:T(8,128)(2,1)S(1)}, u32[]{:S(2)}, u32[]{:S(2)}) collective-permute-start(bf16[320,384]{1,0:T(8,128)(2,1)S(1)} %add_convert_fusion.21), channel_id=1, source_target_pairs={{1,0},{2,3},{5,4},{6,7},{9,8},{10,11},{13,12},{14,15},{17,16},{18,... | collective-permute-start | bytes 737288 | tf_op jit(solution)/shard_map/ppermute | solution.py:225
  93.4 12.2 %collective-permute-start.25 = (bf16[320,384]{1,0:T(8,128)(2,1)S(1)}, bf16[320,384]{1,0:T(8,128)(2,1)S(1)}, u32[]{:S(2)}, u32[]{:S(2)}) collective-permute-start(bf16[320,384]{1,0:T(8,128)(2,1)S(1)} %add_convert_fusion.20), channel_id=1, source_target_pairs={{0,1},{3,2},{4,5},{7,6},{8,9},{11,10},{12,13},{15,14},{16,17},{19,... | collective-permute-start | bytes 737288 | tf_op jit(solution)/shard_map/ppermute | solution.py:225
  96.0 10.3 %collective-permute-start.34 = (bf16[320,384]{1,0:T(8,128)(2,1)S(1)}, bf16[320,384]{1,0:T(8,128)(2,1)S(1)}, u32[]{:S(2)}, u32[]{:S(2)}) collective-permute-start(bf16[320,384]{1,0:T(8,128)(2,1)S(1)} %add_convert_fusion.19), channel_id=1, source_target_pairs={{1,2},{2,1},{5,6},{6,5},{9,10},{10,9},{13,14},{14,13},{17,18},{18,... | collective-permute-start | bytes 737288 | tf_op jit(solution)/shard_map/ppermute | solution.py:225
  96.7 6.3 %collective-permute-start.26 = (bf16[320,384]{1,0:T(8,128)(2,1)S(1)}, bf16[320,384]{1,0:T(8,128)(2,1)S(1)}, u32[]{:S(2)}, u32[]{:S(2)}) collective-permute-start(bf16[320,384]{1,0:T(8,128)(2,1)S(1)} %get-tuple-element.115), channel_id=1, source_target_pairs={{0,16},{16,0},{1,17},{17,1},{2,18},{18,2},{3,19},{19,3},{4,20},{20... | collective-permute-start | bytes 737288 | tf_op jit(solution)/shard_map/ppermute | solution.py:225
  97.7 10.1 %collective-permute-start.33 = (bf16[320,384]{1,0:T(8,128)(2,1)S(1)}, bf16[320,384]{1,0:T(8,128)(2,1)S(1)}, u32[]{:S(2)}, u32[]{:S(2)}) collective-permute-start(bf16[320,384]{1,0:T(8,128)(2,1)S(1)} %add_convert_fusion.18), channel_id=1, source_target_pairs={{1,0},{2,3},{5,4},{6,7},{9,8},{10,11},{13,12},{14,15},{17,16},{18,... | collective-permute-start | bytes 737288 | tf_op jit(solution)/shard_map/ppermute | solution.py:225
  103.1 15.8 %collective-permute-start.31 = (bf16[320,384]{1,0:T(8,128)(2,1)S(1)}, bf16[320,384]{1,0:T(8,128)(2,1)S(1)}, u32[]{:S(2)}, u32[]{:S(2)}) collective-permute-start(bf16[320,384]{1,0:T(8,128)(2,1)S(1)} %add_convert_fusion.17), channel_id=1, source_target_pairs={{0,1},{3,2},{4,5},{7,6},{8,9},{11,10},{12,13},{15,14},{16,17},{19,... | collective-permute-start | bytes 737288 | tf_op jit(solution)/shard_map/ppermute | solution.py:225
  105.7 14.0 %collective-permute-start.30 = (bf16[320,384]{1,0:T(8,128)(2,1)S(1)}, bf16[320,384]{1,0:T(8,128)(2,1)S(1)}, u32[]{:S(2)}, u32[]{:S(2)}) collective-permute-start(bf16[320,384]{1,0:T(8,128)(2,1)S(1)} %add_convert_fusion.16), channel_id=1, source_target_pairs={{1,2},{2,1},{5,6},{6,5},{9,10},{10,9},{13,14},{14,13},{17,18},{18,... | collective-permute-start | bytes 737288 | tf_op jit(solution)/shard_map/ppermute | solution.py:225
  106.4 14.6 %collective-permute-start.39 = (bf16[320,384]{1,0:T(8,128)(2,1)S(1)}, bf16[320,384]{1,0:T(8,128)(2,1)S(1)}, u32[]{:S(2)}, u32[]{:S(2)}) collective-permute-start(bf16[320,384]{1,0:T(8,128)(2,1)S(1)} %add_convert_fusion.15), channel_id=1, source_target_pairs={{1,0},{2,3},{5,4},{6,7},{9,8},{10,11},{13,12},{14,15},{17,16},{18,... | collective-permute-start | bytes 737288 | tf_op jit(solution)/shard_map/ppermute | solution.py:225
  107.8 6.8 %collective-permute-start.32 = (bf16[320,384]{1,0:T(8,128)(2,1)S(1)}, bf16[320,384]{1,0:T(8,128)(2,1)S(1)}, u32[]{:S(2)}, u32[]{:S(2)}) collective-permute-start(bf16[320,384]{1,0:T(8,128)(2,1)S(1)} %get-tuple-element.123), channel_id=1, source_target_pairs={{0,16},{16,0},{1,17},{17,1},{2,18},{18,2},{3,19},{19,3},{4,20},{20... | collective-permute-start | bytes 737288 | tf_op jit(solution)/shard_map/ppermute | solution.py:225
  108.8 13.3 %collective-permute-start.38 = (bf16[320,384]{1,0:T(8,128)(2,1)S(1)}, bf16[320,384]{1,0:T(8,128)(2,1)S(1)}, u32[]{:S(2)}, u32[]{:S(2)}) collective-permute-start(bf16[320,384]{1,0:T(8,128)(2,1)S(1)} %get-tuple-element.131), channel_id=1, source_target_pairs={{0,16},{16,0},{1,17},{17,1},{2,18},{18,2},{3,19},{19,3},{4,20},{20... | collective-permute-start | bytes 737288 | tf_op jit(solution)/shard_map/ppermute | solution.py:225
  114.6 12.2 %collective-permute-start.37 = (bf16[320,384]{1,0:T(8,128)(2,1)S(1)}, bf16[320,384]{1,0:T(8,128)(2,1)S(1)}, u32[]{:S(2)}, u32[]{:S(2)}) collective-permute-start(bf16[320,384]{1,0:T(8,128)(2,1)S(1)} %add_convert_fusion.14), channel_id=1, source_target_pairs={{0,1},{3,2},{4,5},{7,6},{8,9},{11,10},{12,13},{15,14},{16,17},{19,... | collective-permute-start | bytes 737288 | tf_op jit(solution)/shard_map/ppermute | solution.py:225
  119.0 8.6 %collective-permute-start.36 = (bf16[320,384]{1,0:T(8,128)(2,1)S(1)}, bf16[320,384]{1,0:T(8,128)(2,1)S(1)}, u32[]{:S(2)}, u32[]{:S(2)}) collective-permute-start(bf16[320,384]{1,0:T(8,128)(2,1)S(1)} %add_convert_fusion.13), channel_id=1, source_target_pairs={{1,2},{2,1},{5,6},{6,5},{9,10},{10,9},{13,14},{14,13},{17,18},{18,... | collective-permute-start | bytes 737288 | tf_op jit(solution)/shard_map/ppermute | solution.py:225
  119.7 10.1 %collective-permute-start.35 = (bf16[320,384]{1,0:T(8,128)(2,1)S(1)}, bf16[320,384]{1,0:T(8,128)(2,1)S(1)}, u32[]{:S(2)}, u32[]{:S(2)}) collective-permute-start(bf16[320,384]{1,0:T(8,128)(2,1)S(1)} %add_convert_fusion.12), channel_id=1, source_target_pairs={{1,0},{2,3},{5,4},{6,7},{9,8},{10,11},{13,12},{14,15},{17,16},{18,... | collective-permute-start | bytes 737288 | tf_op jit(solution)/shard_map/ppermute | solution.py:225
  121.1 8.7 %collective-permute-start.44 = (bf16[320,384]{1,0:T(8,128)(2,1)S(1)}, bf16[320,384]{1,0:T(8,128)(2,1)S(1)}, u32[]{:S(2)}, u32[]{:S(2)}) collective-permute-start(bf16[320,384]{1,0:T(8,128)(2,1)S(1)} %get-tuple-element.140), channel_id=1, source_target_pairs={{0,16},{16,0},{1,17},{17,1},{2,18},{18,2},{3,19},{19,3},{4,20},{20... | collective-permute-start | bytes 737288 | tf_op jit(solution)/shard_map/ppermute | solution.py:225
  122.2 12.5 %collective-permute-start.43 = (bf16[320,384]{1,0:T(8,128)(2,1)S(1)}, bf16[320,384]{1,0:T(8,128)(2,1)S(1)}, u32[]{:S(2)}, u32[]{:S(2)}) collective-permute-start(bf16[320,384]{1,0:T(8,128)(2,1)S(1)} %add_convert_fusion.11), channel_id=1, source_target_pairs={{0,1},{3,2},{4,5},{7,6},{8,9},{11,10},{12,13},{15,14},{16,17},{19,... | collective-permute-start | bytes 737288 | tf_op jit(solution)/shard_map/ppermute | solution.py:225
  126.9 8.7 %collective-permute-start.42 = (bf16[320,384]{1,0:T(8,128)(2,1)S(1)}, bf16[320,384]{1,0:T(8,128)(2,1)S(1)}, u32[]{:S(2)}, u32[]{:S(2)}) collective-permute-start(bf16[320,384]{1,0:T(8,128)(2,1)S(1)} %add_convert_fusion.10), channel_id=1, source_target_pairs={{1,2},{2,1},{5,6},{6,5},{9,10},{10,9},{13,14},{14,13},{17,18},{18,... | collective-permute-start | bytes 737288 | tf_op jit(solution)/shard_map/ppermute | solution.py:225
  127.7 11.7 %collective-permute-start.41 = (bf16[320,384]{1,0:T(8,128)(2,1)S(1)}, bf16[320,384]{1,0:T(8,128)(2,1)S(1)}, u32[]{:S(2)}, u32[]{:S(2)}) collective-permute-start(bf16[320,384]{1,0:T(8,128)(2,1)S(1)} %add_convert_fusion.9), channel_id=1, source_target_pairs={{1,0},{2,3},{5,4},{6,7},{9,8},{10,11},{13,12},{14,15},{17,16},{18,... | collective-permute-start | bytes 737288 | tf_op jit(solution)/shard_map/ppermute | solution.py:225
  129.9 13.4 %collective-permute-start.48 = (bf16[320,384]{1,0:T(8,128)(2,1)S(1)}, bf16[320,384]{1,0:T(8,128)(2,1)S(1)}, u32[]{:S(2)}, u32[]{:S(2)}) collective-permute-start(bf16[320,384]{1,0:T(8,128)(2,1)S(1)} %add_convert_fusion.8), channel_id=1, source_target_pairs={{0,1},{3,2},{4,5},{7,6},{8,9},{11,10},{12,13},{15,14},{16,17},{19,... | collective-permute-start | bytes 737288 | tf_op jit(solution)/shard_map/ppermute | solution.py:225
  134.8 6.3 %collective-permute-start.40 = (bf16[320,384]{1,0:T(8,128)(2,1)S(1)}, bf16[320,384]{1,0:T(8,128)(2,1)S(1)}, u32[]{:S(2)}, u32[]{:S(2)}) collective-permute-start(bf16[320,384]{1,0:T(8,128)(2,1)S(1)} %get-tuple-element.137), channel_id=1, source_target_pairs={{0,16},{16,0},{1,17},{17,1},{2,18},{18,2},{3,19},{19,3},{4,20},{20... | collective-permute-start | bytes 737288 | tf_op jit(solution)/shard_map/ppermute | solution.py:225
  134.9 9.2 %collective-permute-start.47 = (bf16[320,384]{1,0:T(8,128)(2,1)S(1)}, bf16[320,384]{1,0:T(8,128)(2,1)S(1)}, u32[]{:S(2)}, u32[]{:S(2)}) collective-permute-start(bf16[320,384]{1,0:T(8,128)(2,1)S(1)} %add_convert_fusion.7), channel_id=1, source_target_pairs={{1,2},{2,1},{5,6},{6,5},{9,10},{10,9},{13,14},{14,13},{17,18},{18,... | collective-permute-start | bytes 737288 | tf_op jit(solution)/shard_map/ppermute | solution.py:225
  135.7 10.2 %collective-permute-start.46 = (bf16[320,384]{1,0:T(8,128)(2,1)S(1)}, bf16[320,384]{1,0:T(8,128)(2,1)S(1)}, u32[]{:S(2)}, u32[]{:S(2)}) collective-permute-start(bf16[320,384]{1,0:T(8,128)(2,1)S(1)} %add_convert_fusion.6), channel_id=1, source_target_pairs={{1,0},{2,3},{5,4},{6,7},{9,8},{10,11},{13,12},{14,15},{17,16},{18,... | collective-permute-start | bytes 737288 | tf_op jit(solution)/shard_map/ppermute | solution.py:225
  141.1 5.9 %collective-permute-start.45 = (bf16[320,384]{1,0:T(8,128)(2,1)S(1)}, bf16[320,384]{1,0:T(8,128)(2,1)S(1)}, u32[]{:S(2)}, u32[]{:S(2)}) collective-permute-start(bf16[320,384]{1,0:T(8,128)(2,1)S(1)} %add_convert_fusion.5), channel_id=1, source_target_pairs={{0,1},{3,2},{4,5},{7,6},{8,9},{11,10},{12,13},{15,14},{16,17},{19,... | collective-permute-start | bytes 737288 | tf_op jit(solution)/shard_map/ppermute | solution.py:225
  144.2 9.2 %collective-permute-start.50 = (bf16[320,384]{1,0:T(8,128)(2,1)S(1)}, bf16[320,384]{1,0:T(8,128)(2,1)S(1)}, u32[]{:S(2)}, u32[]{:S(2)}) collective-permute-start(bf16[320,384]{1,0:T(8,128)(2,1)S(1)} %add_convert_fusion.3), channel_id=1, source_target_pairs={{1,0},{2,3},{5,4},{6,7},{9,8},{10,11},{13,12},{14,15},{17,16},{18,... | collective-permute-start | bytes 737288 | tf_op jit(solution)/shard_map/ppermute | solution.py:225
  147.1 6.4 %collective-permute-start.49 = (bf16[320,384]{1,0:T(8,128)(2,1)S(1)}, bf16[320,384]{1,0:T(8,128)(2,1)S(1)}, u32[]{:S(2)}, u32[]{:S(2)}) collective-permute-start(bf16[320,384]{1,0:T(8,128)(2,1)S(1)} %add_convert_fusion.2), channel_id=1, source_target_pairs={{1,2},{2,1},{5,6},{6,5},{9,10},{10,9},{13,14},{14,13},{17,18},{18,... | collective-permute-start | bytes 737288 | tf_op jit(solution)/shard_map/ppermute | solution.py:225
  147.9 12.0 %collective-permute-start.52 = (bf16[320,384]{1,0:T(8,128)(2,1)S(1)}, bf16[320,384]{1,0:T(8,128)(2,1)S(1)}, u32[]{:S(2)}, u32[]{:S(2)}) collective-permute-start(bf16[320,384]{1,0:T(8,128)(2,1)S(1)} %add_convert_fusion.1), channel_id=1, source_target_pairs={{1,0},{2,3},{5,4},{6,7},{9,8},{10,11},{13,12},{14,15},{17,16},{18,... | collective-permute-start | bytes 737288 | tf_op jit(solution)/shard_map/ppermute | solution.py:225
  153.6 10.7 %collective-permute-start.53 = (bf16[320,384]{1,0:T(8,128)(2,1)S(1)}, bf16[320,384]{1,0:T(8,128)(2,1)S(1)}, u32[]{:S(2)}, u32[]{:S(2)}) collective-permute-start(bf16[320,384]{1,0:T(8,128)(2,1)S(1)} %add_convert_fusion), channel_id=1, source_target_pairs={{1,0},{2,3},{5,4},{6,7},{9,8},{10,11},{13,12},{14,15},{17,16},{18,... | collective-permute-start | bytes 737288 | tf_op jit(solution)/shard_map/ppermute | solution.py:225
  (17 other events, 101.5 us)

commit v3 on v2

--- a/solution.py
+++ b/solution.py
@@ -26,11 +26,18 @@
     return lax.ppermute(value, axis, [(i, i ^ bit) for i in range(peers)])
 
 
+def edge_block(ref, depth):
+    rows = jnp.concatenate([ref[0:8, :], jnp.zeros((LANES - 8, ref.shape[1]), F32)], axis=0)
+    keep = lax.broadcasted_iota(jnp.int32, rows.shape, 0) < 4
+    return jnp.where(keep, rows, 0.0).T[0:depth, :].astype(BF16)
+
+
 def conv_rows(offsets, me, x_refs, halo_refs, w_ref, rows_scr, y_scr):
     taps, width = w_ref.shape[0], w_ref.shape[2]
-    depth, length = x_refs[0].shape
+    length = x_refs[0].shape[1]
     x = jnp.concatenate([ref[...] for ref in x_refs], axis=0)
-    halo = jnp.concatenate([ref[...] for ref in halo_refs], axis=0)
+    depth = x.shape[0] // len(offsets)
+    halo = jnp.concatenate([edge_block(ref, depth) for ref in halo_refs], axis=0)
     rows_scr[0:length, :] = x.T
     rows_scr[length : length + 16, :] = halo.T[0:16]
     starts = [pl.multiple_of((me ^ off) * depth, 16) for off in offsets]
@@ -63,7 +70,8 @@
 
 def first_kernel(offsets, idx_ref, *refs):
     n = len(offsets)
-    x_refs, halo_refs, (w_ref, even_ref, odd_ref, rows_scr, y_scr) = refs[:n], refs[n : 2 * n], refs[2 * n :]
+    *x_refs, w_ref, even_ref, odd_ref, rows_scr, y_scr = refs
+    x_refs, halo_refs = x_refs[:-n], x_refs[-n:]
     conv_rows(offsets, idx_ref[0], x_refs, halo_refs, w_ref, rows_scr, y_scr)
     taps, width = w_ref.shape[0], w_ref.shape[2]
     half = even_ref.shape[0]
@@ -78,8 +86,8 @@
 
 def second_kernel(offsets, idx_ref, *refs):
     n = len(offsets)
-    x_refs, halo_refs = refs[:n], refs[n : 2 * n]
-    w_ref, even_ref, odd_ref, grad_ref, enc_ref, pre_ref, rows_scr, y_scr, p_scr = refs[2 * n :]
+    *x_refs, w_ref, even_ref, odd_ref, grad_ref, enc_ref, pre_ref, rows_scr, y_scr, p_scr = refs
+    x_refs, halo_refs = x_refs[:-n], x_refs[-n:]
     conv_rows(offsets, idx_ref[0], x_refs, halo_refs, w_ref, rows_scr, y_scr)
     taps, width = w_ref.shape[0], w_ref.shape[2]
     half = even_ref.shape[0]
@@ -105,10 +113,12 @@
         pre_ref[EDGE : EDGE + length, lanes] = p_scr[c].astype(BF16).astype(F32)
 
 
-def grad_kernel(offsets, group, shards, idx_ref, *refs):
+def grad_kernel(offsets, group, shards, split, idx_ref, *refs):
     n = len(offsets)
-    x_refs, halo_refs, (p_ref, *out_refs, edge_scr) = refs[:n], refs[n : 2 * n], refs[2 * n :]
-    depth, length = x_refs[0].shape
+    *x_refs, p_ref = refs[: -1 - len(group) * split[1]]
+    out_refs, edge_scr = refs[len(x_refs) + 1 : -1], refs[-1]
+    x_refs, halo_refs = x_refs[:-n], x_refs[-n:]
+    length = x_refs[0].shape[1]
     width = p_ref.shape[1]
     edge_scr[...] = jnp.zeros_like(edge_scr)
     shifted = []
@@ -121,26 +131,38 @@
     edge = edge_scr[...].astype(BF16)
     me = idx_ref[0]
     x = jnp.concatenate([ref[...] for ref in x_refs], axis=0)
-    halo = jnp.concatenate([ref[...] for ref in halo_refs], axis=0)
+    depth = x.shape[0] // n
+    halo = jnp.concatenate([edge_block(ref, depth) for ref in halo_refs], axis=0)
     res = jnp.dot(x, p, preferred_element_type=F32) + jnp.dot(halo, edge, preferred_element_type=F32)
     res = res.astype(BF16)
-    per = n // shards
+    per, each = split
     for i in range(len(group)):
+        outs = out_refs[i * each : (i + 1) * each]
         for j, off in enumerate(offsets):
             part = res[j * depth : (j + 1) * depth, i * width : (i + 1) * width]
             at = me ^ off
-            if per == 0:
-                out_refs[i][pl.ds(pl.multiple_of(at * depth, 16), depth), :] = part
+            if not per:
+                outs[0][pl.ds(pl.multiple_of(at * depth, 16), depth), :] = part
                 continue
-            shard = lax.div(at, per)
-            for d in range(shards):
-                for r in range(per):
-                    hit = jnp.logical_and(shard == lax.rem(idx_ref[1] + d, shards), lax.rem(at, per) == r)
-                    ref = out_refs[(i * shards + d) * per + r]
-
-                    @pl.when(hit)
-                    def _(ref=ref, part=part):
+            mine = lax.div(at, per) == idx_ref[1]
+            row = lax.rem(at, per)
+            for r in range(per):
+
+                @pl.when(jnp.logical_and(mine, row == r))
+                def _(ref=outs[r], part=part):
+                    ref[...] = part
+
+                if each == 2 * per:
+
+                    @pl.when(jnp.logical_and(jnp.logical_not(mine), row == r))
+                    def _(ref=outs[per + r], part=part):
                         ref[...] = part
+
+            if each == per + 1:
+
+                @pl.when(jnp.logical_not(mine))
+                def _(ref=outs[per], part=part):
+                    ref[pl.ds(pl.multiple_of(row * depth, 16), depth), :] = part
 
 
 def qkv_kernel(offsets, idx_ref, *refs):
@@ -156,7 +178,7 @@
     scale = lax.rsqrt(var + 1e-05)
     total = None
     for off, v, gain_ref in zip(offsets, values, gain_refs):
-        normal = ((v - mean) * scale * gain_ref[...]).astype(BF16)
+        normal = ((v - mean) * scale * gain_ref[4:5, 0:depth]).astype(BF16)
         w = w_ref[pl.ds(pl.multiple_of((idx_ref[0] ^ off) * depth, 16), depth), :]
         part = jnp.dot(normal, w, preferred_element_type=F32)
         total = part if total is None else total + part
@@ -179,67 +201,71 @@
     return lax.optimization_barrier((value, *others))[0]
 
 
-def edge_columns(x):
+def edge_rows(x):
     peers = lax.axis_size("seq")
-    up = [(i, (i + 1) % peers) for i in range(peers - 1)]
-    down = [(j, i) for i, j in up]
+    me = lax.axis_index("seq")
     length = x.shape[1]
-    before = lax.ppermute(x[:, length - 2 :], "seq", up)
-    after = lax.ppermute(x[:, :2], "seq", down)
-    return jnp.concatenate([before, after], axis=1)
-
-
-def gathered(value, axis, bits):
-    blocks = [value]
-    for bit in bits:
-        blocks = blocks + [swap(b, axis, bit) for b in blocks]
-    return blocks
+    head, tail = x[:, :2], x[:, length - 2 :]
+    if peers == 2:
+        got = swap(jnp.where(me == 0, tail, head), "seq", 1)
+        zero = jnp.zeros_like(got)
+        before, behind = jnp.where(me == 0, zero, got), jnp.where(me == 0, got, zero)
+    else:
+        up = [(i, (i + 1) % peers) for i in range(peers - 1)]
+        down = [(j, i) for i, j in up]
+        before, behind = lax.ppermute(tail, "seq", up), lax.ppermute(head, "seq", down)
+    return lax.optimization_barrier(jnp.concatenate([before, behind], axis=1)).T
 
 
 def added(a, b):
     return (a.astype(F32) + b.astype(F32)).astype(BF16)
 
 
-def chain_stages(axis):
-    peers = lax.axis_size(axis)
-    me = lax.axis_index(axis)
-    half = peers // 2
-    stages = []
-    for i in range(half - 1):
-        stages.append((axis, [(i, i + 1), (peers - 1 - i, peers - 2 - i)], added))
-    stages.append((axis, [(half - 1, half), (half, half - 1)], added))
-    for i in reversed(range(half - 1)):
-        outer = jnp.logical_or(me == i, me == peers - 1 - i)
-        choose = lambda a, b, outer=outer: jnp.where(outer, b, a)
-        stages.append((axis, [(i + 1, i), (peers - 2 - i, peers - 1 - i)], choose))
-    return stages
-
-
-def pipelined(parts, stages, sent=None):
-    n, depth = len(parts), len(stages)
-    state, flying, last = list(parts), [None] * n, None
-    late = None
-
-    def launch(c, i, value):
-        axis, pairs, _ = stages[i]
-        flying[c] = lax.ppermute(value, axis, pairs)
-
-    first = list(parts if sent is None else sent)
-    launch(0, 0, first[0])
-    for step in range(n + depth - 1):
-        if step + 1 < n:
-            launch(step + 1, 0, first[step + 1] if last is None else after(first[step + 1], last))
-        for i in range(depth):
-            c = step - i
-            if not 0 <= c < n:
+def chain_sums(count, part, sent):
+    me = lax.axis_index("dp")
+    last, late = None, None
+    h, sums = {}, {}
+    ways = [
+        dict(order=(0, 1, 2, 3), step=1, got=None, p={}, s={}, out={}),
+        dict(order=(3, 2, 1, 0), step=-1, got=None, p={}, s={}, out={}),
+    ]
+    for r in range(count + 3):
+        if r < count:
+            h[r] = part(r, last)
+            last = h[r]
+            sent(r, last)
+        for way, other in (ways, ways[::-1]):
+            first, second, third, _ = way["order"]
+            if way["got"] is not None:
+                got = after(way["got"], last)
+                if r - 1 < count:
+                    way["p"][r - 1] = added(h[r - 1], got)
+                if 0 <= r - 2 < count:
+                    way["s"][r - 2] = added(other["p"][r - 2], got)
+                if 0 <= r - 3 < count:
+                    way["out"][r - 3] = got
+                last = got
+            options = [(first, h.get(r)), (second, way["p"].get(r - 1)), (third, way["s"].get(r - 2))]
+            options = [o for o in options if o[1] is not None]
+            way["got"] = None
+            if not options:
                 continue
-            got = flying[c] if last is None else after(flying[c], last)
-            state[c] = stages[i][2](state[c], got)
-            last = state[c]
-            if i + 1 < depth:
-                launch(c, i + 1, state[c])
-                late = last
-    return state, late
+            value = options[-1][1]
+            for peer, choice in options[:-1]:
+                value = jnp.where(me == peer, choice, value)
+            if r - 1 in way["p"] and way is ways[1]:
+                value, way["p"][r - 1] = lax.optimization_barrier((value, way["p"][r - 1]))
+                late = value
+            else:
+                value = lax.optimization_barrier(value)
+            last = value
+            way["got"] = lax.ppermute(value, "dp", [(peer, peer + way["step"]) for peer, _ in options])
+        c = r - 3
+        if c >= 0:
+            lower = jnp.where(me == 0, ways[1]["out"][c], ways[1]["s"][c])
+            upper = jnp.where(me == 3, ways[0]["out"][c], ways[0]["s"][c])
+            sums[c] = jnp.where(me < 2, lower, upper).astype(F32)
+    return [sums[c] for c in range(count)], late
 
 
 def on_device(block_input, conv_weight, norm_gain, qkv_weight, encoder_grad):
@@ -266,30 +292,35 @@
     for bit in bits[:-1]:
         blocks = blocks + [swap(b, "mp", bit) for b in blocks]
     own = swap(x, "mp", bits[-1])
-    edges = gathered(edge_columns(x), "mp", bits)
-    gains = gathered(norm_gain.reshape(1, -1), "mp", bits)
-    halos = [jnp.pad(e, ((0, 0), (0, LANES - e.shape[1]))) for e in edges]
+    edges = edge_rows(x).astype(F32)
+    edges = jnp.pad(edges, ((0, 0), (0, width - depth)))
+    payload = jnp.concatenate([edges, norm_gain.reshape(1, -1), jnp.zeros((3, width), F32)], axis=0)
+    pay_blocks = [payload]
+    for bit in bits[:-1]:
+        pay_blocks = pay_blocks + [swap(b, "mp", bit) for b in pay_blocks]
+    pay_own = swap(payload, "mp", bits[-1])
     part = jax.ShapeDtypeStruct((half, width), F32)
     even, odd = call(
         functools.partial(first_kernel, pick(offsets, near)),
         (part, part),
         scratch(near),
         40,
-        after(idx, *gains), x, own, *pick(halos, near), conv_weight,
+        idx, x, own, payload, pay_own, conv_weight,
     )
-    blocks = blocks + [own] + [swap(after(b, even), "mp", bits[-1]) for b in blocks[1:]]
+    relay = lambda blocks: [swap(after(b, even), "mp", bits[-1]) for b in blocks[1:]]
+    payloads = pay_blocks + [pay_own] + relay(pay_blocks)
+    blocks = blocks + [own] + relay(blocks)
     encoded, pre_grad = call(
         functools.partial(second_kernel, pick(offsets, far)),
         (jax.ShapeDtypeStruct((half, width), BF16), jax.ShapeDtypeStruct((length + 2 * EDGE, width), F32)),
         scratch(far) + [pltpu.VMEM((width // LANES, length, LANES), F32)],
         40,
-        idx, *pick(blocks, far), *pick(halos, far), conv_weight, even, odd, encoder_grad[0],
+        idx, *pick(blocks, far), *pick(payloads, far), conv_weight, even, odd, encoder_grad[0],
     )
 
-    pair = shards == 2 and peers % shards == 0
+    pair = shards == 2 and peers % shards == 0 and lax.axis_size("dp") == 4
     per = peers // shards if pair else 0
-    out = (depth, width) if pair else (peers * depth, width)
-    count = shards * per if pair else 1
+    piece = jax.ShapeDtypeStruct((depth, width), BF16)
     keep, send = [], []
     done = idx
     encs = [encoded]
@@ -297,38 +328,59 @@
         encs = encs + [swap(e, "mp", bit) for e in encs]
     encs_own = swap(encoded, "mp", bits[-1])
     for group in [(0,)] + [tuple(range(k, min(k + 2, taps))) for k in range(1, taps, 2)]:
+        if not pair:
+            outs = (jax.ShapeDtypeStruct((peers * depth, width), BF16),)
+        elif group[0] == 0:
+            outs = (piece,) * (2 * per)
+        else:
+            outs = (piece,) * per + (jax.ShapeDtypeStruct((per * depth, width), BF16),)
+        each = len(outs)
         outs = call(
-            functools.partial(grad_kernel, offsets, group, shards if pair else peers + 1),
-            (jax.ShapeDtypeStruct(out, BF16),) * (count * len(group)),
+            functools.partial(grad_kernel, offsets, group, shards, (per, each)),
+            outs * len(group),
             [pltpu.VMEM((LANES, width * len(group)), F32)],
             28,
-            done, *blocks, *halos, pre_grad,
+            done, *blocks, *payloads, pre_grad,
         )
         done = after(idx, outs[0], *(encs[1:] if group[0] else ()))
-        if not pair:
-            keep += [lax.psum_scatter(o, "seq", scatter_dimension=0, tiled=True) for o in outs]
-            continue
         for i in range(len(group)):
-            keep += outs[i * count : i * count + per]
-            send += outs[i * count + per : (i + 1) * count]
+            mine = outs[i * each : (i + 1) * each]
+            keep += mine[: max(per, 1)]
+            send.append(mine[per:])
     encs = encs + [encs_own] + [swap(e, "mp", bits[-1]) for e in encs[1:]]
-    keep[1] = after(keep[1], *encs)
-    stages = chain_stages("dp") if lax.axis_size("dp") % 2 == 0 else []
+
+    late = encs[-1]
     if pair:
-        stages = [("seq", [(0, 1), (1, 0)], added)] + stages
-    sums, late = pipelined(keep, stages, send if pair else None)
-    if lax.axis_size("dp") % 2:
-        sums = [lax.psum(s, "dp") for s in sums]
-    lines = max(per, 1)
-    sums = [jnp.concatenate(sums[k * lines : (k + 1) * lines], axis=0) for k in range(taps)]
-    conv_grad = jnp.stack([s.astype(F32) for s in sums], axis=1)
+        got = {0: [swap(v, "seq", 1) for v in send[0]]}
+
+        def share(c, last):
+            tap, row = c // per, c % per
+            value = got[tap][row] if tap == 0 else got[tap][0][row * depth : (row + 1) * depth]
+            hold = [] if last is None else [last]
+            if c == 1:
+                hold = hold + encs
+            if hold:
+                value = after(value, *hold)
+            return added(keep[c], value)
+
+        def sent(c, last):
+            tap = c // per + 1
+            if c % per == 0 and tap < taps:
+                got[tap] = [swap(after(v, last), "seq", 1) for v in send[tap]]
+
+        sums, late = chain_sums(taps * per, share, sent)
+        sums = [jnp.concatenate(sums[k * per : (k + 1) * per], axis=0) for k in range(taps)]
+    else:
+        sums = [lax.psum_scatter(v, "seq", scatter_dimension=0, tiled=True) for v in keep]
+        sums = [lax.psum(v, "dp").astype(F32) for v in sums]
+    conv_grad = jnp.stack(sums, axis=1)
 
     qkv = call(
         functools.partial(qkv_kernel, offsets),
         jax.ShapeDtypeStruct((half, qkv_weight.shape[1]), BF16),
         [],
         20,
-        idx if late is None else after(idx, late), *encs, *gains, qkv_weight,
+        after(idx, late), *encs, *payloads, qkv_weight,
     )
     return (qkv[None], conv_grad)
 

time: 168 us -> 173 us (1.030)
  local copies, waits for them, and re-layouts: 7.49 us -> 12.5 us
  starting transfers between devices: 79.2 us -> 74.6 us
  waiting for transfers between devices: 44.6 us -> 47.3 us
  other arithmetic: 8.16 us -> 10.7 us
    ppermute x42 -> x24, starting transfers between devices: 71.7 us -> 58.5 us  [chain_sums(): lax.ppermute(value, 'dp', [(peer, peer + way['step']) for peer, _ in opti...]
    ppermute x12 -> x16, starting transfers between devices: 7.43 us -> 16.1 us  [swap(): return lax.ppermute(value, axis, [(i, i ^ bit) for i in range(peers)])]
    unnamed x22 -> x49, local copies, waits for them, and re-layouts: 5.68 us -> 10.4 us
    select_n x9 -> x25, other arithmetic: 0.29 us -> 4.98 us  [the longest x19 3.18 us: chain_sums(): value = jnp.where(me == peer, choice, value)]
    ppermute x42 -> x24, waiting for transfers between devices: 29.8 us -> 33.1 us  [chain_sums(): lax.ppermute(value, 'dp', [(peer, peer + way['step']) for peer, _ in opti...]
    convert_element_type x30 -> x12, other arithmetic: 4.7 us -> 2.61 us  [added(): return (a.astype(F32) + b.astype(F32)).astype(BF16)]
    ppermute x12 -> x16, waiting for transfers between devices: 14.8 us -> 14.3 us  [swap(): return lax.ppermute(value, axis, [(i, i ^ bit) for i in range(peers)])]
  transfers between devices with their start and end apart: 54 -> 40, of which waited for: 17 -> 25; matrix products, arithmetic and copies ran while one was open for 4% -> 6% of each run, Pallas kernels for 12% -> 10%
where the time goes in v3:
time: 173 us; the launch traced here: 172 us
  starting transfers between devices  74.6 us (43%)
  waiting for transfers between devices  47.3 us (27%)
  Pallas kernels  25.9 us (15%)
  local copies, waits for them, and re-layouts  12.5 us (7%)
  other arithmetic  10.7 us (6%)
    ppermute x24, starting transfers between devices, chain_sums(): lax.ppermute(value, 'dp', [(peer, peer + way['step']) for peer, _ in opti...  58.5 us
    ppermute x24, waiting for transfers between devices, chain_sums(): lax.ppermute(value, 'dp', [(peer, peer + way['step']) for peer, _ in opti...  33.1 us
    pallas_call x6, Pallas kernels, call(): pl.pallas_call(kernel, out_shape=out, in_specs=[pl.BlockSpec(memory_space...  25.9 us
    ppermute x16, starting transfers between devices, swap(): return lax.ppermute(value, axis, [(i, i ^ bit) for i in range(peers)])  16.1 us
    ppermute x16, waiting for transfers between devices, swap(): return lax.ppermute(value, axis, [(i, i ^ bit) for i in range(peers)])  14.3 us
    unnamed x49, local copies, waits for them, and re-layouts  10.4 us
  transfers between devices with their start and end apart: 40, of which 25 were waited for; matrix products, arithmetic and copies ran while one was open for 6% of the time, Pallas kernels for 10%

profile of v3, /device:TPU:0, one launch (start us, length us, event | category | flops | bytes accessed | tf_op | source)
XLA Modules:
  0.0 172.3 jit_solution(7269532687711008030)
XLA Ops:
  0.6 1.4 copy.24
  2.1 3.0 %collective-permute-start.2 = (bf16[320,2]{0,1:T(2,128)(2,1)S(1)}, bf16[320,2]{0,1:T(2,128)(2,1)S(1)}, u32[]{:S(2)}, u32[]{:S(2)}) collective-permute-start(bf16[320,2]{0,1:T(2,128)(2,1)S(1)} %broadcast_select_fusion.6), channel_id=1, source_target_pairs={{0,16},{16,0},{1,17},{17,1},{2,18},{18,2},{3,19},{19,3},{4,20},{20... | collective-permute-start | bytes 3848 | tf_op jit(solution)/shard_map/ppermute | solution.py:26
  5.1 1.5 collective-permute-start
  8.7 2.4 %copy-done = bf16[5,1280,384]{2,1,0:T(8,128)(2,1)S(1)} copy-done((bf16[5,1280,384]{2,1,0:T(8,128)(2,1)S(1)}, bf16[5,1280,384]{2,1,0:T(8,128)(2,1)}, u32[]{:S(2)}) %copy-start) | copy-done | bytes 4915224
  12.2 4.3 %shard_map.68 = (f32[512,384]{1,0:T(8,128)S(1)}, f32[512,384]{1,0:T(8,128)S(1)}) custom-call(s32[2]{0:T(128)S(1)} %pad_add_fusion.idx_ref, bf16[320,1024]{1,0:T(8,128)(2,1)S(1)} %bitcast.31, bf16[320,1024]{1,0:T(8,128)(2,1)S(1)} %collective-permute-done.1.refs_1_.refs_2_, f32[8,384]{1,0:T(8,128)S(1)} %maximum_maximum_fusion.refs_2_.refs_4_, ...), custom_call_target="tpu_custom_call" | custom-call | tf_op jit(solution)/shard_map/pallas_call | solution.py:190
  16.5 6.0 %collective-permute-done.refs_0_.refs_1_ = bf16[320,1024]{1,0:T(8,128)(2,1)S(1)} collective-permute-done((bf16[320,1024]{1,0:T(8,128)(2,1)}, bf16[320,1024]{1,0:T(8,128)(2,1)S(1)}, u32[]{:S(2)}, u32[]{:S(2)}) %collective-permute-start) | collective-permute-done | bytes 655392 | tf_op jit(solution)/shard_map/ppermute | solution.py:26
  22.5 1.5 collective-permute-start.5
  24.0 2.2 %collective-permute-done.5.refs_2_.refs_5_ = f32[8,384]{1,0:T(8,128)S(1)} collective-permute-done((f32[8,384]{1,0:T(8,128)S(1)}, f32[8,384]{1,0:T(8,128)S(1)}, u32[]{:S(2)}, u32[]{:S(2)}) %collective-permute-start.5) | collective-permute-done | bytes 12320 | tf_op jit(solution)/shard_map/ppermute | solution.py:26
  27.4 5.7 %shard_map.69 = (bf16[512,384]{1,0:T(8,128)(2,1)S(1)}, f32[1040,384]{1,0:T(8,128)S(1)}) custom-call(s32[2]{0:T(128)S(1)} %pad_add_fusion.idx_ref, bf16[320,1024]{1,0:T(8,128)(2,1)S(1)} %collective-permute-done.refs_0_.refs_1_, bf16[320,1024]{1,0:T(8,128)(2,1)S(1)} %collective-permute-done.4.refs_1_.refs_3_, ...), custom_call_target="tpu_custom_call" | custom-call | tf_op jit(solution)/shard_map/pallas_call | solution.py:190
  33.1 3.5 %shard_map.70 = (bf16[320,384]{1,0:T(8,128)(2,1)S(1)}, bf16[320,384]{1,0:T(8,128)(2,1)S(1)}, bf16[320,384]{1,0:T(8,128)(2,1)S(1)}, bf16[320,384]{1,0:T(8,128)(2,1)}) custom-call(s32[2]{0:T(128)S(1)} %pad_add_fusion.idx_ref, bf16[320,1024]{1,0:T(8,128)(2,1)S(1)} %bitcast.32, bf16[320,1024]{1,0:T(8,128)(2,1)S(1)} %collective-permute-done.refs_0_.refs_1_, ...), custom_call_target="tpu_custom_call" | custom-call | tf_op jit(solution)/shard_map/pallas_call | solution.py:190
  37.6 1.7 %collective-permute-start.7 = (bf16[512,384]{1,0:T(8,128)(2,1)S(1)}, bf16[512,384]{1,0:T(8,128)(2,1)}, u32[]{:S(2)}, u32[]{:S(2)}) collective-permute-start(bf16[512,384]{1,0:T(8,128)(2,1)S(1)} %get-tuple-element.92.refs_0_), channel_id=1, source_target_pairs={{0,8},{4,12},{8,0},{12,4},{1,9},{5,13},{9,1},{13,5},{2,10},{6,14},... | collective-permute-start | bytes 1179656 | tf_op jit(solution)/shard_map/ppermute | solution.py:26
  40.4 4.5 %shard_map.71 = (bf16[320,384]{1,0:T(8,128)(2,1)S(1)}, bf16[320,384]{1,0:T(8,128)(2,1)S(1)}, bf16[640,384]{1,0:T(8,128)(2,1)}, bf16[320,384]{1,0:T(8,128)(2,1)S(...) custom-call(s32[2]{0:T(128)S(1)} %pad_add_fusion.idx_ref, bf16[320,1024]{1,0:T(8,128)(2,1)S(1)} %bitcast.33, ...), custom_call_target="tpu_custom_call" | custom-call | tf_op jit(solution)/shard_map/pallas_call | solution.py:190
  47.3 1.5 collective-permute-start.9
  50.4 3.5 %collective-permute-start.14 = (bf16[320,384]{1,0:T(8,128)(2,1)}, bf16[320,384]{1,0:T(8,128)(2,1)S(1)}, u32[]{:S(2)}, u32[]{:S(2)}) collective-permute-start(bf16[320,384]{1,0:T(8,128)(2,1)} %add_convert_fusion.11), channel_id=1, source_target_pairs={{0,1},{4,5},{8,9},{12,13},{16,17},{20,21},{24,25},{28,29}} | collective-permute-start | bytes 737288 | tf_op jit(solution)/shard_map/ppermute | solution.py:262
  56.1 3.7 %shard_map.72 = (bf16[320,384]{1,0:T(8,128)(2,1)S(1)}, bf16[320,384]{1,0:T(8,128)(2,1)S(1)}, bf16[640,384]{1,0:T(8,128)(2,1)S(1)}, bf16[320,384]{1,0:T(8,128)(2,...) custom-call(s32[2]{0:T(128)S(1)} %pad_add_fusion.idx_ref, bf16[320,1024]{1,0:T(8,128)(2,1)S(1)} %bitcast.34, ...), custom_call_target="tpu_custom_call" | custom-call | tf_op jit(solution)/shard_map/pallas_call | solution.py:190
  59.8 2.0 %collective-permute-done.9 = bf16[640,384]{1,0:T(8,128)(2,1)} collective-permute-done((bf16[640,384]{1,0:T(8,128)(2,1)}, bf16[640,384]{1,0:T(8,128)(2,1)}, u32[]{:S(2)}, u32[]{:S(2)}) %collective-permute-start.9) | collective-permute-done | bytes 491552 | tf_op jit(solution)/shard_map/ppermute | solution.py:26
  63.5 2.1 %collective-permute-done.10 = bf16[320,384]{1,0:T(8,128)(2,1)} collective-permute-done((bf16[320,384]{1,0:T(8,128)(2,1)}, bf16[320,384]{1,0:T(8,128)(2,1)}, u32[]{:S(2)}, u32[]{:S(2)}) %collective-permute-start.10) | collective-permute-done | bytes 245792 | tf_op jit(solution)/shard_map/ppermute | solution.py:26
  66.7 3.6 %collective-permute-start.17 = (bf16[320,384]{1,0:T(8,128)(2,1)S(1)}, bf16[320,384]{1,0:T(8,128)(2,1)S(1)}, u32[]{:S(2)}, u32[]{:S(2)}) collective-permute-start(bf16[320,384]{1,0:T(8,128)(2,1)S(1)} %broadcast_select_fusion.1), channel_id=1, source_target_pairs={{0,1},{1,2},{4,5},{5,6},{8,9},{9,10},{12,13},{13,14},{16,17},{17,1... | collective-permute-start | bytes 737288 | tf_op jit(solution)/shard_map/ppermute | solution.py:262
  71.3 1.6 collective-permute-start.15
  72.8 1.6 collective-permute-done.17
  74.6 4.4 %collective-permute-start.19 = (bf16[320,384]{1,0:T(8,128)(2,1)S(1)}, bf16[320,384]{1,0:T(8,128)(2,1)S(1)}, u32[]{:S(2)}, u32[]{:S(2)}) collective-permute-start(bf16[320,384]{1,0:T(8,128)(2,1)S(1)} %select_select_fusion.25), channel_id=1, source_target_pairs={{0,1},{1,2},{2,3},{4,5},{5,6},{6,7},{8,9},{9,10},{10,11},{12,13},{... | collective-permute-start | bytes 737288 | tf_op jit(solution)/shard_map/ppermute | solution.py:262
  79.2 1.4 collective-permute-start.18
  80.7 2.0 %collective-permute-done.19 = bf16[320,384]{1,0:T(8,128)(2,1)S(1)} collective-permute-done((bf16[320,384]{1,0:T(8,128)(2,1)S(1)}, bf16[320,384]{1,0:T(8,128)(2,1)S(1)}, u32[]{:S(2)}, u32[]{:S(2)}) %collective-permute-start.19) | collective-permute-done | bytes 245792 | tf_op jit(solution)/shard_map/ppermute | solution.py:262
  82.8 4.4 %collective-permute-start.22 = (bf16[320,384]{1,0:T(8,128)(2,1)S(1)}, bf16[320,384]{1,0:T(8,128)(2,1)S(1)}, u32[]{:S(2)}, u32[]{:S(2)}) collective-permute-start(bf16[320,384]{1,0:T(8,128)(2,1)S(1)} %select_select_fusion.23), channel_id=1, source_target_pairs={{0,1},{1,2},{2,3},{4,5},{5,6},{6,7},{8,9},{9,10},{10,11},{12,13},{... | collective-permute-start | bytes 737288 | tf_op jit(solution)/shard_map/ppermute | solution.py:262
  87.6 1.3 collective-permute-start.21
  89.0 1.6 collective-permute-start.20
  91.0 4.5 %collective-permute-start.24 = (bf16[320,384]{1,0:T(8,128)(2,1)S(1)}, bf16[320,384]{1,0:T(8,128)(2,1)S(1)}, u32[]{:S(2)}, u32[]{:S(2)}) collective-permute-start(bf16[320,384]{1,0:T(8,128)(2,1)S(1)} %select_select_fusion.21), channel_id=1, source_target_pairs={{0,1},{1,2},{2,3},{4,5},{5,6},{6,7},{8,9},{9,10},{10,11},{12,13},{... | collective-permute-start | bytes 737288 | tf_op jit(solution)/shard_map/ppermute | solution.py:262
  96.2 1.3 collective-permute-start.23
  97.7 1.9 %collective-permute-done.24 = bf16[320,384]{1,0:T(8,128)(2,1)S(1)} collective-permute-done((bf16[320,384]{1,0:T(8,128)(2,1)S(1)}, bf16[320,384]{1,0:T(8,128)(2,1)S(1)}, u32[]{:S(2)}, u32[]{:S(2)}) %collective-permute-start.24) | collective-permute-done | bytes 245792 | tf_op jit(solution)/shard_map/ppermute | solution.py:262
  99.8 4.4 %collective-permute-start.27 = (bf16[320,384]{1,0:T(8,128)(2,1)S(1)}, bf16[320,384]{1,0:T(8,128)(2,1)S(1)}, u32[]{:S(2)}, u32[]{:S(2)}) collective-permute-start(bf16[320,384]{1,0:T(8,128)(2,1)S(1)} %select_select_fusion.19), channel_id=1, source_target_pairs={{0,1},{1,2},{2,3},{4,5},{5,6},{6,7},{8,9},{9,10},{10,11},{12,13},{... | collective-permute-start | bytes 737288 | tf_op jit(solution)/shard_map/ppermute | solution.py:262
  105.3 1.3 collective-permute-start.26
  106.7 1.5 collective-permute-start.25
  109.2 4.4 %collective-permute-start.29 = (bf16[320,384]{1,0:T(8,128)(2,1)S(1)}, bf16[320,384]{1,0:T(8,128)(2,1)S(1)}, u32[]{:S(2)}, u32[]{:S(2)}) collective-permute-start(bf16[320,384]{1,0:T(8,128)(2,1)S(1)} %select_select_fusion.17), channel_id=1, source_target_pairs={{0,1},{1,2},{2,3},{4,5},{5,6},{6,7},{8,9},{9,10},{10,11},{12,13},{... | collective-permute-start | bytes 737288 | tf_op jit(solution)/shard_map/ppermute | solution.py:262
  113.6 1.6 collective-permute-done.26
  116.7 2.6 %collective-permute-done.29 = bf16[320,384]{1,0:T(8,128)(2,1)S(1)} collective-permute-done((bf16[320,384]{1,0:T(8,128)(2,1)S(1)}, bf16[320,384]{1,0:T(8,128)(2,1)S(1)}, u32[]{:S(2)}, u32[]{:S(2)}) %collective-permute-start.29) | collective-permute-done | bytes 245792 | tf_op jit(solution)/shard_map/ppermute | solution.py:262
  119.4 4.6 %collective-permute-start.31 = (bf16[320,384]{1,0:T(8,128)(2,1)S(1)}, bf16[320,384]{1,0:T(8,128)(2,1)S(1)}, u32[]{:S(2)}, u32[]{:S(2)}) collective-permute-start(bf16[320,384]{1,0:T(8,128)(2,1)S(1)} %select_select_fusion.15), channel_id=1, source_target_pairs={{0,1},{1,2},{2,3},{4,5},{5,6},{6,7},{8,9},{9,10},{10,11},{12,13},{... | collective-permute-start | bytes 737288 | tf_op jit(solution)/shard_map/ppermute | solution.py:262
  124.1 1.7 collective-permute-done.28
  125.9 1.3 collective-permute-start.30
  128.1 1.8 %collective-permute-done.31 = bf16[320,384]{1,0:T(8,128)(2,1)S(1)} collective-permute-done((bf16[320,384]{1,0:T(8,128)(2,1)S(1)}, bf16[320,384]{1,0:T(8,128)(2,1)S(1)}, u32[]{:S(2)}, u32[]{:S(2)}) %collective-permute-start.31) | collective-permute-done | bytes 245792 | tf_op jit(solution)/shard_map/ppermute | solution.py:262
  130.0 4.4 %collective-permute-start.33 = (bf16[320,384]{1,0:T(8,128)(2,1)S(1)}, bf16[320,384]{1,0:T(8,128)(2,1)S(1)}, u32[]{:S(2)}, u32[]{:S(2)}) collective-permute-start(bf16[320,384]{1,0:T(8,128)(2,1)S(1)} %select_select_fusion.13), channel_id=1, source_target_pairs={{0,1},{1,2},{2,3},{4,5},{5,6},{6,7},{8,9},{9,10},{10,11},{12,13},{... | collective-permute-start | bytes 737288 | tf_op jit(solution)/shard_map/ppermute | solution.py:262
  137.5 2.3 %collective-permute-done.33 = bf16[320,384]{1,0:T(8,128)(2,1)S(1)} collective-permute-done((bf16[320,384]{1,0:T(8,128)(2,1)S(1)}, bf16[320,384]{1,0:T(8,128)(2,1)S(1)}, u32[]{:S(2)}, u32[]{:S(2)}) %collective-permute-start.33) | collective-permute-done | bytes 245792 | tf_op jit(solution)/shard_map/ppermute | solution.py:262
  139.9 4.5 %collective-permute-start.35 = (bf16[320,384]{1,0:T(8,128)(2,1)S(1)}, bf16[320,384]{1,0:T(8,128)(2,1)S(1)}, u32[]{:S(2)}, u32[]{:S(2)}) collective-permute-start(bf16[320,384]{1,0:T(8,128)(2,1)S(1)} %select_select_fusion.11), channel_id=1, source_target_pairs={{0,1},{1,2},{2,3},{4,5},{5,6},{6,7},{8,9},{9,10},{10,11},{12,13},{... | collective-permute-start | bytes 737288 | tf_op jit(solution)/shard_map/ppermute | solution.py:262
  146.3 1.8 %collective-permute-done.35 = bf16[320,384]{1,0:T(8,128)(2,1)S(1)} collective-permute-done((bf16[320,384]{1,0:T(8,128)(2,1)S(1)}, bf16[320,384]{1,0:T(8,128)(2,1)S(1)}, u32[]{:S(2)}, u32[]{:S(2)}) %collective-permute-start.35) | collective-permute-done | bytes 245792 | tf_op jit(solution)/shard_map/ppermute | solution.py:262
  148.9 4.2 %collective-permute-done.34 = bf16[320,384]{1,0:T(8,128)(2,1)S(1)} collective-permute-done((bf16[320,384]{1,0:T(8,128)(2,1)S(1)}, bf16[320,384]{1,0:T(8,128)(2,1)S(1)}, u32[]{:S(2)}, u32[]{:S(2)}) %collective-permute-start.34) | collective-permute-done | bytes 245792 | tf_op jit(solution)/shard_map/ppermute | solution.py:262
  154.7 4.3 %shard_map.73 = bf16[512,640]{1,0:T(8,128)(2,1)} custom-call(s32[2]{0:T(128)S(1)} %pad_add_fusion.idx_ref, bf16[512,384]{1,0:T(8,128)(2,1)S(1)} %get-tuple-element.92.refs_0_, bf16[512,384]{1,0:T(8,128)(2,1)} %collective-permute-done.7.refs_1_, bf16[512,384]{1,0:T(8,128)(2,1)} %collective-permute-done.11.refs_2_, ...), custom_call_target="tpu_custom_call" | custom-call | tf_op jit(solution)/shard_map/pallas_call | solution.py:190
  159.7 1.7 collective-permute-done.36
  163.4 6.1 %collective-permute-done.38 = bf16[320,384]{1,0:T(8,128)(2,1)S(1)} collective-permute-done((bf16[320,384]{1,0:T(8,128)(2,1)S(1)}, bf16[320,384]{1,0:T(8,128)(2,1)S(1)}, u32[]{:S(2)}, u32[]{:S(2)}) %collective-permute-start.38) | collective-permute-done | bytes 245792 | tf_op jit(solution)/shard_map/ppermute | solution.py:262
  169.7 2.6 %stack.44 = f32[640,5,384]{2,0,1:T(8,128)} convert(bf16[640,5,384]{2,0,1:T(8,128)(2,1)S(1)} %fusion.42) | non-fusion elementwise | flops 1228800 | bytes 7372800 | tf_op jit(solution)/shard_map/stack | solution.py:376
  (141 shorter events, 34.0 us)
Async XLA Ops:
  2.1 5.3 %collective-permute-start.2 = (bf16[320,2]{0,1:T(2,128)(2,1)S(1)}, bf16[320,2]{0,1:T(2,128)(2,1)S(1)}, u32[]{:S(2)}, u32[]{:S(2)}) collective-permute-start(bf16[320,2]{0,1:T(2,128)(2,1)S(1)} %broadcast_select_fusion.6), channel_id=1, source_target_pairs={{0,16},{16,0},{1,17},{17,1},{2,18},{18,2},{3,19},{19,3},{4,20},{20... | collective-permute-start | bytes 3848 | tf_op jit(solution)/shard_map/ppermute | solution.py:26
  5.1 3.6 %collective-permute-start.1 = (bf16[320,1024]{1,0:T(8,128)(2,1)}, bf16[320,1024]{1,0:T(8,128)(2,1)S(1)}, u32[]{:S(2)}, u32[]{:S(2)}) collective-permute-start(bf16[320,1024]{1,0:T(8,128)(2,1)} %bitcast.29), channel_id=1, source_target_pairs={{0,4},{4,0},{8,12},{12,8},{1,5},{5,1},{9,13},{13,9},{2,6},{6,2},{1... | collective-permute-start | bytes 1966088 | tf_op jit(solution)/shard_map/ppermute | solution.py:26
  5.1 17.4 %collective-permute-start = (bf16[320,1024]{1,0:T(8,128)(2,1)}, bf16[320,1024]{1,0:T(8,128)(2,1)S(1)}, u32[]{:S(2)}, u32[]{:S(2)}) collective-permute-start(bf16[320,1024]{1,0:T(8,128)(2,1)} %bitcast.30), channel_id=1, source_target_pairs={{0,8},{4,12},{8,0},{12,4},{1,9},{5,13},{9,1},{13,5},{2,10},{6,14},... | collective-permute-start | bytes 1966088 | tf_op jit(solution)/shard_map/ppermute | solution.py:26
  7.5 1.2 collective-permute-start.3
  12.2 20.9 %copy-start.6 = (bf16[320,1024]{1,0:T(8,128)(2,1)}, bf16[320,1024]{1,0:T(8,128)(2,1)S(1)}, u32[]{:S(2)}) copy-start(bf16[320,1024]{1,0:T(8,128)(2,1)S(1)} %collective-permute-done.1.refs_1_.refs_2_) | copy-start | bytes 1966084
  12.2 15.2 %copy-start.1 = (bf16[5,1280,384]{2,1,0:T(8,128)(2,1)S(1)}, bf16[5,1280,384]{2,1,0:T(8,128)(2,1)}, u32[]{:S(2)}) copy-start(bf16[5,1280,384]{2,1,0:T(8,128)(2,1)} %refs_4_.3) | copy-start | bytes 14745604
  12.2 15.2 %copy-start.10 = (bf16[1,512,384]{2,1,0:T(8,128)(2,1)S(1)}, bf16[1,512,384]{2,1,0:T(8,128)(2,1)}, u32[]{:S(2)}) copy-start(bf16[1,512,384]{2,1,0:T(8,128)(2,1)} %param.9) | copy-start | bytes 1179652
  22.5 4.9 %collective-permute-start.4 = (bf16[320,1024]{1,0:T(8,128)(2,1)S(1)}, bf16[320,1024]{1,0:T(8,128)(2,1)S(1)}, u32[]{:S(2)}, u32[]{:S(2)}) collective-permute-start(bf16[320,1024]{1,0:T(8,128)(2,1)S(1)} %collective-permute-done.refs_0_.refs_1_), channel_id=1, source_target_pairs={{0,4},{4,0},{8,12},{12,8},{1,5},{5,1},{9,13},{13,9},{2,6},{6,2},{1... | collective-permute-start | bytes 1966088 | tf_op jit(solution)/shard_map/ppermute | solution.py:26
  22.5 3.7 %collective-permute-start.5 = (f32[8,384]{1,0:T(8,128)S(1)}, f32[8,384]{1,0:T(8,128)S(1)}, u32[]{:S(2)}, u32[]{:S(2)}) collective-permute-start(f32[8,384]{1,0:T(8,128)S(1)} %maximum_maximum_fusion.refs_2_.refs_4_), channel_id=1, source_target_pairs={{0,8},{4,12},{8,0},{12,4},{1,9},{5,13},{9,1},{13,5},{2,10},{6,14},... | collective-permute-start | bytes 36872 | tf_op jit(solution)/shard_map/ppermute | solution.py:26
  26.2 1.2 collective-permute-start.6
  27.3 12.0 %copy-start.4 = (bf16[320,1024]{1,0:T(8,128)(2,1)}, bf16[320,1024]{1,0:T(8,128)(2,1)S(1)}, u32[]{:S(2)}) copy-start(bf16[320,1024]{1,0:T(8,128)(2,1)S(1)} %collective-permute-done.4.refs_1_.refs_3_) | copy-start | bytes 1966084
  37.3 9.1 %collective-permute-start.8 = (bf16[320,384]{1,0:T(8,128)(2,1)S(1)}, bf16[320,384]{1,0:T(8,128)(2,1)S(1)}, u32[]{:S(2)}, u32[]{:S(2)}) collective-permute-start(bf16[320,384]{1,0:T(8,128)(2,1)S(1)} %get-tuple-element.101), channel_id=1, source_target_pairs={{0,16},{16,0},{1,17},{17,1},{2,18},{18,2},{3,19},{19,3},{4,20},{20... | collective-permute-start | bytes 737288 | tf_op jit(solution)/shard_map/ppermute | solution.py:26
  37.6 11.2 %collective-permute-start.7 = (bf16[512,384]{1,0:T(8,128)(2,1)S(1)}, bf16[512,384]{1,0:T(8,128)(2,1)}, u32[]{:S(2)}, u32[]{:S(2)}) collective-permute-start(bf16[512,384]{1,0:T(8,128)(2,1)S(1)} %get-tuple-element.92.refs_0_), channel_id=1, source_target_pairs={{0,8},{4,12},{8,0},{12,4},{1,9},{5,13},{9,1},{13,5},{2,10},{6,14},... | collective-permute-start | bytes 1179656 | tf_op jit(solution)/shard_map/ppermute | solution.py:26
  40.4 13.5 %copy-start.3 = (bf16[1,1024,320]{1,2,0:T(8,128)(2,1)S(1)}, bf16[1,1024,320]{1,2,0:T(8,128)(2,1)}, u32[]{:S(2)}) copy-start(bf16[1,1024,320]{1,2,0:T(8,128)(2,1)} %param.5) | copy-start | bytes 1966084
  47.3 14.5 %collective-permute-start.9 = (bf16[640,384]{1,0:T(8,128)(2,1)}, bf16[640,384]{1,0:T(8,128)(2,1)}, u32[]{:S(2)}, u32[]{:S(2)}) collective-permute-start(bf16[640,384]{1,0:T(8,128)(2,1)} %get-tuple-element.102), channel_id=1, source_target_pairs={{0,16},{16,0},{1,17},{17,1},{2,18},{18,2},{3,19},{19,3},{4,20},{20... | collective-permute-start | bytes 1474568 | tf_op jit(solution)/shard_map/ppermute | solution.py:26
  48.8 16.8 %collective-permute-start.11 = (bf16[512,384]{1,0:T(8,128)(2,1)S(1)}, bf16[512,384]{1,0:T(8,128)(2,1)}, u32[]{:S(2)}, u32[]{:S(2)}) collective-permute-start(bf16[512,384]{1,0:T(8,128)(2,1)S(1)} %get-tuple-element.92.refs_0_), channel_id=1, source_target_pairs={{0,4},{4,0},{8,12},{12,8},{1,5},{5,1},{9,13},{13,9},{2,6},{6,2},{1... | collective-permute-start | bytes 1179656 | tf_op jit(solution)/shard_map/ppermute | solution.py:26
  48.8 16.8 %collective-permute-start.12 = (bf16[512,384]{1,0:T(8,128)(2,1)}, bf16[512,384]{1,0:T(8,128)(2,1)}, u32[]{:S(2)}, u32[]{:S(2)}) collective-permute-start(bf16[512,384]{1,0:T(8,128)(2,1)} %collective-permute-done.7.refs_1_), channel_id=1, source_target_pairs={{0,4},{4,0},{8,12},{12,8},{1,5},{5,1},{9,13},{13,9},{2,6},{6,2},{1... | collective-permute-start | bytes 1179656 | tf_op jit(solution)/shard_map/ppermute | solution.py:26
  49.3 16.3 %collective-permute-start.10 = (bf16[320,384]{1,0:T(8,128)(2,1)}, bf16[320,384]{1,0:T(8,128)(2,1)}, u32[]{:S(2)}, u32[]{:S(2)}) collective-permute-start(bf16[320,384]{1,0:T(8,128)(2,1)} %get-tuple-element.104), channel_id=1, source_target_pairs={{0,16},{16,0},{1,17},{17,1},{2,18},{18,2},{3,19},{19,3},{4,20},{20... | collective-permute-start | bytes 737288 | tf_op jit(solution)/shard_map/ppermute | solution.py:26
  50.4 16.2 %collective-permute-start.14 = (bf16[320,384]{1,0:T(8,128)(2,1)}, bf16[320,384]{1,0:T(8,128)(2,1)S(1)}, u32[]{:S(2)}, u32[]{:S(2)}) collective-permute-start(bf16[320,384]{1,0:T(8,128)(2,1)} %add_convert_fusion.11), channel_id=1, source_target_pairs={{0,1},{4,5},{8,9},{12,13},{16,17},{20,21},{24,25},{28,29}} | collective-permute-start | bytes 737288 | tf_op jit(solution)/shard_map/ppermute | solution.py:262
  59.7 11.5 %copy-start.22 = (bf16[640,384]{1,0:T(8,128)(2,1)S(1)}, bf16[640,384]{1,0:T(8,128)(2,1)}, u32[]{:S(2)}) copy-start(bf16[640,384]{1,0:T(8,128)(2,1)} %copy-done.21) | copy-start | bytes 1474564
  61.7 8.7 %collective-permute-start.13 = (bf16[320,384]{1,0:T(8,128)(2,1)S(1)}, bf16[320,384]{1,0:T(8,128)(2,1)S(1)}, u32[]{:S(2)}, u32[]{:S(2)}) collective-permute-start(bf16[320,384]{1,0:T(8,128)(2,1)S(1)} %copy-done.23), channel_id=1, source_target_pairs={{3,2},{7,6},{11,10},{15,14},{19,18},{23,22},{27,26},{31,30}} | collective-permute-start | bytes 737288 | tf_op jit(solution)/shard_map/ppermute | solution.py:262
  66.7 13.9 %copy-start.16 = (bf16[320,384]{1,0:T(8,128)(2,1)S(1)}, bf16[320,384]{1,0:T(8,128)(2,1)}, u32[]{:S(2)}) copy-start(bf16[320,384]{1,0:T(8,128)(2,1)} %copy-done.15) | copy-start | bytes 737284
  66.7 7.7 %collective-permute-start.17 = (bf16[320,384]{1,0:T(8,128)(2,1)S(1)}, bf16[320,384]{1,0:T(8,128)(2,1)S(1)}, u32[]{:S(2)}, u32[]{:S(2)}) collective-permute-start(bf16[320,384]{1,0:T(8,128)(2,1)S(1)} %broadcast_select_fusion.1), channel_id=1, source_target_pairs={{0,1},{1,2},{4,5},{5,6},{8,9},{9,10},{12,13},{13,14},{16,17},{17,1... | collective-permute-start | bytes 737288 | tf_op jit(solution)/shard_map/ppermute | solution.py:262
  70.5 8.5 %collective-permute-start.16 = (bf16[320,384]{1,0:T(8,128)(2,1)S(1)}, bf16[320,384]{1,0:T(8,128)(2,1)S(1)}, u32[]{:S(2)}, u32[]{:S(2)}) collective-permute-start(bf16[320,384]{1,0:T(8,128)(2,1)S(1)} %get-tuple-element.108), channel_id=1, source_target_pairs={{3,2},{2,1},{7,6},{6,5},{11,10},{10,9},{15,14},{14,13},{19,18},{18... | collective-permute-start | bytes 737288 | tf_op jit(solution)/shard_map/ppermute | solution.py:262
  71.3 17.6 %collective-permute-start.15 = (bf16[640,384]{1,0:T(8,128)(2,1)S(1)}, bf16[640,384]{1,0:T(8,128)(2,1)S(1)}, u32[]{:S(2)}, u32[]{:S(2)}) collective-permute-start(bf16[640,384]{1,0:T(8,128)(2,1)S(1)} %copy-done.22), channel_id=1, source_target_pairs={{0,16},{16,0},{1,17},{17,1},{2,18},{18,2},{3,19},{19,3},{4,20},{20... | collective-permute-start | bytes 1474568 | tf_op jit(solution)/shard_map/ppermute | solution.py:26
  74.6 8.1 %collective-permute-start.19 = (bf16[320,384]{1,0:T(8,128)(2,1)S(1)}, bf16[320,384]{1,0:T(8,128)(2,1)S(1)}, u32[]{:S(2)}, u32[]{:S(2)}) collective-permute-start(bf16[320,384]{1,0:T(8,128)(2,1)S(1)} %select_select_fusion.25), channel_id=1, source_target_pairs={{0,1},{1,2},{2,3},{4,5},{5,6},{6,7},{8,9},{9,10},{10,11},{12,13},{... | collective-permute-start | bytes 737288 | tf_op jit(solution)/shard_map/ppermute | solution.py:262
  79.2 8.2 %collective-permute-start.18 = (bf16[320,384]{1,0:T(8,128)(2,1)S(1)}, bf16[320,384]{1,0:T(8,128)(2,1)S(1)}, u32[]{:S(2)}, u32[]{:S(2)}) collective-permute-start(bf16[320,384]{1,0:T(8,128)(2,1)S(1)} %get-tuple-element.114), channel_id=1, source_target_pairs={{3,2},{2,1},{1,0},{7,6},{6,5},{5,4},{11,10},{10,9},{9,8},{15,14},{... | collective-permute-start | bytes 737288 | tf_op jit(solution)/shard_map/ppermute | solution.py:262
  82.8 8.1 %collective-permute-start.22 = (bf16[320,384]{1,0:T(8,128)(2,1)S(1)}, bf16[320,384]{1,0:T(8,128)(2,1)S(1)}, u32[]{:S(2)}, u32[]{:S(2)}) collective-permute-start(bf16[320,384]{1,0:T(8,128)(2,1)S(1)} %select_select_fusion.23), channel_id=1, source_target_pairs={{0,1},{1,2},{2,3},{4,5},{5,6},{6,7},{8,9},{9,10},{10,11},{12,13},{... | collective-permute-start | bytes 737288 | tf_op jit(solution)/shard_map/ppermute | solution.py:262
  87.6 8.1 %collective-permute-start.21 = (bf16[320,384]{1,0:T(8,128)(2,1)S(1)}, bf16[320,384]{1,0:T(8,128)(2,1)S(1)}, u32[]{:S(2)}, u32[]{:S(2)}) collective-permute-start(bf16[320,384]{1,0:T(8,128)(2,1)S(1)} %get-tuple-element.120), channel_id=1, source_target_pairs={{3,2},{2,1},{1,0},{7,6},{6,5},{5,4},{11,10},{10,9},{9,8},{15,14},{... | collective-permute-start | bytes 737288 | tf_op jit(solution)/shard_map/ppermute | solution.py:262
  89.0 17.5 %collective-permute-start.20 = (bf16[640,384]{1,0:T(8,128)(2,1)S(1)}, bf16[640,384]{1,0:T(8,128)(2,1)S(1)}, u32[]{:S(2)}, u32[]{:S(2)}) collective-permute-start(bf16[640,384]{1,0:T(8,128)(2,1)S(1)} %get-tuple-element.122), channel_id=1, source_target_pairs={{0,16},{16,0},{1,17},{17,1},{2,18},{18,2},{3,19},{19,3},{4,20},{20... | collective-permute-start | bytes 1474568 | tf_op jit(solution)/shard_map/ppermute | solution.py:26
  91.0 8.6 %collective-permute-start.24 = (bf16[320,384]{1,0:T(8,128)(2,1)S(1)}, bf16[320,384]{1,0:T(8,128)(2,1)S(1)}, u32[]{:S(2)}, u32[]{:S(2)}) collective-permute-start(bf16[320,384]{1,0:T(8,128)(2,1)S(1)} %select_select_fusion.21), channel_id=1, source_target_pairs={{0,1},{1,2},{2,3},{4,5},{5,6},{6,7},{8,9},{9,10},{10,11},{12,13},{... | collective-permute-start | bytes 737288 | tf_op jit(solution)/shard_map/ppermute | solution.py:262
  96.2 8.8 %collective-permute-start.23 = (bf16[320,384]{1,0:T(8,128)(2,1)S(1)}, bf16[320,384]{1,0:T(8,128)(2,1)S(1)}, u32[]{:S(2)}, u32[]{:S(2)}) collective-permute-start(bf16[320,384]{1,0:T(8,128)(2,1)S(1)} %get-tuple-element.126), channel_id=1, source_target_pairs={{3,2},{2,1},{1,0},{7,6},{6,5},{5,4},{11,10},{10,9},{9,8},{15,14},{... | collective-permute-start | bytes 737288 | tf_op jit(solution)/shard_map/ppermute | solution.py:262
  99.8 9.2 %collective-permute-start.27 = (bf16[320,384]{1,0:T(8,128)(2,1)S(1)}, bf16[320,384]{1,0:T(8,128)(2,1)S(1)}, u32[]{:S(2)}, u32[]{:S(2)}) collective-permute-start(bf16[320,384]{1,0:T(8,128)(2,1)S(1)} %select_select_fusion.19), channel_id=1, source_target_pairs={{0,1},{1,2},{2,3},{4,5},{5,6},{6,7},{8,9},{9,10},{10,11},{12,13},{... | collective-permute-start | bytes 737288 | tf_op jit(solution)/shard_map/ppermute | solution.py:262
  105.3 9.9 %collective-permute-start.26 = (bf16[320,384]{1,0:T(8,128)(2,1)S(1)}, bf16[320,384]{1,0:T(8,128)(2,1)S(1)}, u32[]{:S(2)}, u32[]{:S(2)}) collective-permute-start(bf16[320,384]{1,0:T(8,128)(2,1)S(1)} %get-tuple-element.132), channel_id=1, source_target_pairs={{3,2},{2,1},{1,0},{7,6},{6,5},{5,4},{11,10},{10,9},{9,8},{15,14},{... | collective-permute-start | bytes 737288 | tf_op jit(solution)/shard_map/ppermute | solution.py:262
  106.7 21.2 %collective-permute-start.25 = (bf16[640,384]{1,0:T(8,128)(2,1)S(1)}, bf16[640,384]{1,0:T(8,128)(2,1)S(1)}, u32[]{:S(2)}, u32[]{:S(2)}) collective-permute-start(bf16[640,384]{1,0:T(8,128)(2,1)S(1)} %get-tuple-element.134), channel_id=1, source_target_pairs={{0,16},{16,0},{1,17},{17,1},{2,18},{18,2},{3,19},{19,3},{4,20},{20... | collective-permute-start | bytes 1474568 | tf_op jit(solution)/shard_map/ppermute | solution.py:26
  109.2 10.1 %collective-permute-start.29 = (bf16[320,384]{1,0:T(8,128)(2,1)S(1)}, bf16[320,384]{1,0:T(8,128)(2,1)S(1)}, u32[]{:S(2)}, u32[]{:S(2)}) collective-permute-start(bf16[320,384]{1,0:T(8,128)(2,1)S(1)} %select_select_fusion.17), channel_id=1, source_target_pairs={{0,1},{1,2},{2,3},{4,5},{5,6},{6,7},{8,9},{9,10},{10,11},{12,13},{... | collective-permute-start | bytes 737288 | tf_op jit(solution)/shard_map/ppermute | solution.py:262
  115.3 10.4 %collective-permute-start.28 = (bf16[320,384]{1,0:T(8,128)(2,1)S(1)}, bf16[320,384]{1,0:T(8,128)(2,1)S(1)}, u32[]{:S(2)}, u32[]{:S(2)}) collective-permute-start(bf16[320,384]{1,0:T(8,128)(2,1)S(1)} %get-tuple-element.139), channel_id=1, source_target_pairs={{3,2},{2,1},{1,0},{7,6},{6,5},{5,4},{11,10},{10,9},{9,8},{15,14},{... | collective-permute-start | bytes 737288 | tf_op jit(solution)/shard_map/ppermute | solution.py:262
  119.4 10.4 %collective-permute-start.31 = (bf16[320,384]{1,0:T(8,128)(2,1)S(1)}, bf16[320,384]{1,0:T(8,128)(2,1)S(1)}, u32[]{:S(2)}, u32[]{:S(2)}) collective-permute-start(bf16[320,384]{1,0:T(8,128)(2,1)S(1)} %select_select_fusion.15), channel_id=1, source_target_pairs={{0,1},{1,2},{2,3},{4,5},{5,6},{6,7},{8,9},{9,10},{10,11},{12,13},{... | collective-permute-start | bytes 737288 | tf_op jit(solution)/shard_map/ppermute | solution.py:262
  125.9 9.8 %collective-permute-start.30 = (bf16[320,384]{1,0:T(8,128)(2,1)S(1)}, bf16[320,384]{1,0:T(8,128)(2,1)S(1)}, u32[]{:S(2)}, u32[]{:S(2)}) collective-permute-start(bf16[320,384]{1,0:T(8,128)(2,1)S(1)} %get-tuple-element.144), channel_id=1, source_target_pairs={{3,2},{2,1},{1,0},{7,6},{6,5},{5,4},{11,10},{10,9},{9,8},{15,14},{... | collective-permute-start | bytes 737288 | tf_op jit(solution)/shard_map/ppermute | solution.py:262
  130.0 9.7 %collective-permute-start.33 = (bf16[320,384]{1,0:T(8,128)(2,1)S(1)}, bf16[320,384]{1,0:T(8,128)(2,1)S(1)}, u32[]{:S(2)}, u32[]{:S(2)}) collective-permute-start(bf16[320,384]{1,0:T(8,128)(2,1)S(1)} %select_select_fusion.13), channel_id=1, source_target_pairs={{0,1},{1,2},{2,3},{4,5},{5,6},{6,7},{8,9},{9,10},{10,11},{12,13},{... | collective-permute-start | bytes 737288 | tf_op jit(solution)/shard_map/ppermute | solution.py:262
  136.1 8.7 %collective-permute-start.32 = (bf16[320,384]{1,0:T(8,128)(2,1)S(1)}, bf16[320,384]{1,0:T(8,128)(2,1)S(1)}, u32[]{:S(2)}, u32[]{:S(2)}) collective-permute-start(bf16[320,384]{1,0:T(8,128)(2,1)S(1)} %get-tuple-element.150), channel_id=1, source_target_pairs={{3,2},{2,1},{1,0},{7,6},{6,5},{5,4},{11,10},{10,9},{9,8},{15,14},{... | collective-permute-start | bytes 737288 | tf_op jit(solution)/shard_map/ppermute | solution.py:262
  139.9 14.7 %copy-start.9 = (bf16[1536,640]{1,0:T(8,128)(2,1)S(1)}, bf16[1536,640]{1,0:T(8,128)(2,1)}, u32[]{:S(2)}) copy-start(bf16[1536,640]{1,0:T(8,128)(2,1)} %refs_8_.1) | copy-start | bytes 5898244
  139.9 8.2 %collective-permute-start.35 = (bf16[320,384]{1,0:T(8,128)(2,1)S(1)}, bf16[320,384]{1,0:T(8,128)(2,1)S(1)}, u32[]{:S(2)}, u32[]{:S(2)}) collective-permute-start(bf16[320,384]{1,0:T(8,128)(2,1)S(1)} %select_select_fusion.11), channel_id=1, source_target_pairs={{0,1},{1,2},{2,3},{4,5},{5,6},{6,7},{8,9},{9,10},{10,11},{12,13},{... | collective-permute-start | bytes 737288 | tf_op jit(solution)/shard_map/ppermute | solution.py:262
  145.0 8.1 %collective-permute-start.34 = (bf16[320,384]{1,0:T(8,128)(2,1)S(1)}, bf16[320,384]{1,0:T(8,128)(2,1)S(1)}, u32[]{:S(2)}, u32[]{:S(2)}) collective-permute-start(bf16[320,384]{1,0:T(8,128)(2,1)S(1)} %get-tuple-element.155), channel_id=1, source_target_pairs={{3,2},{2,1},{1,0},{7,6},{6,5},{5,4},{11,10},{10,9},{9,8},{15,14},{... | collective-permute-start | bytes 737288 | tf_op jit(solution)/shard_map/ppermute | solution.py:262
  148.3 10.7 %collective-permute-start.37 = (bf16[320,384]{1,0:T(8,128)(2,1)S(1)}, bf16[320,384]{1,0:T(8,128)(2,1)S(1)}, u32[]{:S(2)}, u32[]{:S(2)}) collective-permute-start(bf16[320,384]{1,0:T(8,128)(2,1)S(1)} %broadcast_select_fusion), channel_id=1, source_target_pairs={{1,2},{2,3},{5,6},{6,7},{9,10},{10,11},{13,14},{14,15},{17,18},{18... | collective-permute-start | bytes 737288 | tf_op jit(solution)/shard_map/ppermute | solution.py:262
  153.3 8.1 %collective-permute-start.36 = (bf16[320,384]{1,0:T(8,128)(2,1)S(1)}, bf16[320,384]{1,0:T(8,128)(2,1)S(1)}, u32[]{:S(2)}, u32[]{:S(2)}) collective-permute-start(bf16[320,384]{1,0:T(8,128)(2,1)S(1)} %get-tuple-element.159), channel_id=1, source_target_pairs={{2,1},{1,0},{6,5},{5,4},{10,9},{9,8},{14,13},{13,12},{18,17},{17,1... | collective-permute-start | bytes 737288 | tf_op jit(solution)/shard_map/ppermute | solution.py:262
  159.0 4.4 %collective-permute-start.39 = (bf16[320,384]{1,0:T(8,128)(2,1)S(1)}, bf16[320,384]{1,0:T(8,128)(2,1)S(1)}, u32[]{:S(2)}, u32[]{:S(2)}) collective-permute-start(bf16[320,384]{1,0:T(8,128)(2,1)S(1)} %add_convert_fusion.1), channel_id=1, source_target_pairs={{2,3},{6,7},{10,11},{14,15},{18,19},{22,23},{26,27},{30,31}} | collective-permute-start | bytes 737288 | tf_op jit(solution)/shard_map/ppermute | solution.py:262
  161.5 8.1 %collective-permute-start.38 = (bf16[320,384]{1,0:T(8,128)(2,1)S(1)}, bf16[320,384]{1,0:T(8,128)(2,1)S(1)}, u32[]{:S(2)}, u32[]{:S(2)}) collective-permute-start(bf16[320,384]{1,0:T(8,128)(2,1)S(1)} %add_convert_fusion), channel_id=1, source_target_pairs={{1,0},{5,4},{9,8},{13,12},{17,16},{21,20},{25,24},{29,28}} | collective-permute-start | bytes 737288 | tf_op jit(solution)/shard_map/ppermute | solution.py:262
  (16 other events, 60.2 us)

commit v4 on v3

--- a/solution.py
+++ b/solution.py
@@ -201,20 +201,39 @@
     return lax.optimization_barrier((value, *others))[0]
 
 
-def edge_rows(x):
+def edge_kernel(head_ref, tail_ref, out_ref):
+    depth = head_ref.shape[0]
+    extra = jnp.zeros((out_ref.shape[1] - depth, LANES), F32)
+    head = jnp.concatenate([head_ref[...].astype(F32), extra], axis=0).T
+    tail = jnp.concatenate([tail_ref[...].astype(F32), extra], axis=0).T
+    out_ref[...] = jnp.zeros_like(out_ref)
+    out_ref[0:2, :] = head[0:2]
+    out_ref[2:4, :] = tail[LANES - 2 : LANES]
+
+
+def edge_rows(x, width):
     peers = lax.axis_size("seq")
     me = lax.axis_index("seq")
-    length = x.shape[1]
-    head, tail = x[:, :2], x[:, length - 2 :]
+    depth, length = x.shape
+    ends = pl.pallas_call(
+        edge_kernel,
+        out_shape=jax.ShapeDtypeStruct((8, width), F32),
+        grid=(1,),
+        in_specs=[
+            pl.BlockSpec((depth, LANES), lambda i: (0, 0)),
+            pl.BlockSpec((depth, LANES), lambda i: (0, length // LANES - 1)),
+        ],
+        out_specs=pl.BlockSpec((8, width), lambda i: (0, 0)),
+    )(x, x)
     if peers == 2:
-        got = swap(jnp.where(me == 0, tail, head), "seq", 1)
-        zero = jnp.zeros_like(got)
-        before, behind = jnp.where(me == 0, zero, got), jnp.where(me == 0, got, zero)
+        before = behind = swap(ends, "seq", 1)
     else:
         up = [(i, (i + 1) % peers) for i in range(peers - 1)]
         down = [(j, i) for i, j in up]
-        before, behind = lax.ppermute(tail, "seq", up), lax.ppermute(head, "seq", down)
-    return lax.optimization_barrier(jnp.concatenate([before, behind], axis=1)).T
+        before, behind = lax.ppermute(ends, "seq", up), lax.ppermute(ends, "seq", down)
+    before = jnp.where(me == 0, 0.0, before[2:4])
+    behind = jnp.where(me == peers - 1, 0.0, behind[0:2])
+    return jnp.concatenate([before, behind], axis=0)
 
 
 def added(a, b):
@@ -223,49 +242,36 @@
 
 def chain_sums(count, part, sent):
     me = lax.axis_index("dp")
+    end = jnp.logical_or(me == 0, me == 3)
+    outer_pairs = [(0, 1), (1, 0), (2, 3), (3, 2)]
+    middle_pairs = [(0, 0), (1, 2), (2, 1), (3, 3)]
     last, late = None, None
-    h, sums = {}, {}
-    ways = [
-        dict(order=(0, 1, 2, 3), step=1, got=None, p={}, s={}, out={}),
-        dict(order=(3, 2, 1, 0), step=-1, got=None, p={}, s={}, out={}),
-    ]
-    for r in range(count + 3):
+    h, p, s, outer, middle, sums = {}, {}, {}, {}, {}, {}
+    for r in range(count + 5):
         if r < count:
             h[r] = part(r, last)
             last = h[r]
             sent(r, last)
-        for way, other in (ways, ways[::-1]):
-            first, second, third, _ = way["order"]
-            if way["got"] is not None:
-                got = after(way["got"], last)
-                if r - 1 < count:
-                    way["p"][r - 1] = added(h[r - 1], got)
-                if 0 <= r - 2 < count:
-                    way["s"][r - 2] = added(other["p"][r - 2], got)
-                if 0 <= r - 3 < count:
-                    way["out"][r - 3] = got
-                last = got
-            options = [(first, h.get(r)), (second, way["p"].get(r - 1)), (third, way["s"].get(r - 2))]
-            options = [o for o in options if o[1] is not None]
-            way["got"] = None
-            if not options:
-                continue
-            value = options[-1][1]
-            for peer, choice in options[:-1]:
-                value = jnp.where(me == peer, choice, value)
-            if r - 1 in way["p"] and way is ways[1]:
-                value, way["p"][r - 1] = lax.optimization_barrier((value, way["p"][r - 1]))
-                late = value
-            else:
-                value = lax.optimization_barrier(value)
-            last = value
-            way["got"] = lax.ppermute(value, "dp", [(peer, peer + way["step"]) for peer, _ in options])
-        c = r - 3
-        if c >= 0:
-            lower = jnp.where(me == 0, ways[1]["out"][c], ways[1]["s"][c])
-            upper = jnp.where(me == 3, ways[0]["out"][c], ways[0]["s"][c])
-            sums[c] = jnp.where(me < 2, lower, upper).astype(F32)
-    return [sums[c] for c in range(count)], late
+        if r < count + 3:
+            value = h.get(r, s.get(r - 3))
+            if r in h and r - 3 in s:
+                value = jnp.where(end, h[r], s[r - 3])
+            last = value = lax.optimization_barrier(value)
+            outer[r] = lax.ppermute(value, "dp", outer_pairs)
+        if r - 1 in outer:
+            got = after(outer.pop(r - 1), last)
+            if r - 1 < count:
+                last = p[r - 1] = lax.optimization_barrier(added(h[r - 1], got))
+                late = last
+                middle[r - 1] = lax.ppermute(last, "dp", middle_pairs)
+            if r - 4 >= 0:
+                sums[r - 4] = lax.optimization_barrier(jnp.where(end, got, s[r - 4]))
+                if r - 1 >= count:
+                    last = sums[r - 4]
+        if r - 2 in middle:
+            got = after(middle.pop(r - 2), last)
+            last = s[r - 2] = lax.optimization_barrier(added(p[r - 2], got))
+    return [sums[c].astype(F32) for c in range(count)], late
 
 
 def on_device(block_input, conv_weight, norm_gain, qkv_weight, encoder_grad):
@@ -292,29 +298,25 @@
     for bit in bits[:-1]:
         blocks = blocks + [swap(b, "mp", bit) for b in blocks]
     own = swap(x, "mp", bits[-1])
-    edges = edge_rows(x).astype(F32)
-    edges = jnp.pad(edges, ((0, 0), (0, width - depth)))
+    edges = edge_rows(x, width)
     payload = jnp.concatenate([edges, norm_gain.reshape(1, -1), jnp.zeros((3, width), F32)], axis=0)
-    pay_blocks = [payload]
-    for bit in bits[:-1]:
-        pay_blocks = pay_blocks + [swap(b, "mp", bit) for b in pay_blocks]
-    pay_own = swap(payload, "mp", bits[-1])
+    payloads = [payload] + [swap(payload, "mp", o) for o in offsets[1:]]
+
     part = jax.ShapeDtypeStruct((half, width), F32)
     even, odd = call(
         functools.partial(first_kernel, pick(offsets, near)),
         (part, part),
         scratch(near),
-        40,
-        idx, x, own, payload, pay_own, conv_weight,
+        24,
+        idx, x, own, *pick(payloads, near), conv_weight,
     )
-    relay = lambda blocks: [swap(after(b, even), "mp", bits[-1]) for b in blocks[1:]]
-    payloads = pay_blocks + [pay_own] + relay(pay_blocks)
-    blocks = blocks + [own] + relay(blocks)
+    hold = [even] + pick(payloads, far)
+    blocks = blocks + [own] + [swap(after(b, *hold), "mp", bits[-1]) for b in blocks[1:]]
     encoded, pre_grad = call(
         functools.partial(second_kernel, pick(offsets, far)),
         (jax.ShapeDtypeStruct((half, width), BF16), jax.ShapeDtypeStruct((length + 2 * EDGE, width), F32)),
         scratch(far) + [pltpu.VMEM((width // LANES, length, LANES), F32)],
-        40,
+        24,
         idx, *pick(blocks, far), *pick(payloads, far), conv_weight, even, odd, encoder_grad[0],
     )
 
@@ -339,7 +341,7 @@
             functools.partial(grad_kernel, offsets, group, shards, (per, each)),
             outs * len(group),
             [pltpu.VMEM((LANES, width * len(group)), F32)],
-            28,
+            14,
             done, *blocks, *payloads, pre_grad,
         )
         done = after(idx, outs[0], *(encs[1:] if group[0] else ()))
@@ -379,7 +381,7 @@
         functools.partial(qkv_kernel, offsets),
         jax.ShapeDtypeStruct((half, qkv_weight.shape[1]), BF16),
         [],
-        20,
+        8,
         after(idx, late), *encs, *payloads, qkv_weight,
     )
     return (qkv[None], conv_grad)

time: 173 us -> 137 us (0.79)
  waiting for transfers between devices: 47.3 us -> 19.2 us
  starting transfers between devices: 74.6 us -> 70.5 us
  other arithmetic: 10.7 us -> 7.63 us
  local copies, waits for them, and re-layouts: 12.5 us -> 9.85 us
  Pallas kernels: 25.9 us -> 28.3 us
    ppermute x24 -> x23, waiting for transfers between devices: 33.1 us -> 6.42 us  [the longest x13 6.39 us: chain_sums(): outer[r] = lax.ppermute(value, 'dp', outer_pairs)]
    select_n x25 -> x17, other arithmetic: 4.98 us -> 1.09 us  [the longest x7 0.73 us: chain_sums(): value = jnp.where(end, h[r], s[r - 3])]
    ppermute x24 -> x23, starting transfers between devices: 58.5 us -> 55.2 us  [the longest x13 48.3 us: chain_sums(): outer[r] = lax.ppermute(value, 'dp', outer_pairs)]
    unnamed x49 -> x40, local copies, waits for them, and re-layouts: 10.4 us -> 7.82 us
  transfers between devices with their start and end apart: 40 -> 39, of which waited for: 25 -> 10; matrix products, arithmetic and copies ran while one was open for 6% -> 5% of each run, Pallas kernels for 10% -> 13%
where the time goes in v4:
time: 137 us
  starting transfers between devices  70.5 us (51%)
  Pallas kernels  28.3 us (21%)
  waiting for transfers between devices  19.2 us (14%)
  local copies, waits for them, and re-layouts  9.85 us (7%)
  other arithmetic  7.63 us (6%)
    ppermute x13, starting transfers between devices, chain_sums(): outer[r] = lax.ppermute(value, 'dp', outer_pairs)  48.3 us
    pallas_call x6, Pallas kernels, call(): pl.pallas_call(kernel, out_shape=out, in_specs=[pl.BlockSpec(memory_space...  26.6 us
    ppermute x16, starting transfers between devices, swap(): return lax.ppermute(value, axis, [(i, i ^ bit) for i in range(peers)])  15.3 us
    ppermute x16, waiting for transfers between devices, swap(): return lax.ppermute(value, axis, [(i, i ^ bit) for i in range(peers)])  12.8 us
    unnamed x40, local copies, waits for them, and re-layouts  7.82 us
    ppermute x10, starting transfers between devices, chain_sums(): middle[r - 1] = lax.ppermute(last, 'dp', middle_pairs)  6.98 us
    ppermute x13, waiting for transfers between devices, chain_sums(): outer[r] = lax.ppermute(value, 'dp', outer_pairs)  6.39 us
    convert_element_type x23, other arithmetic, added(): return (a.astype(F32) + b.astype(F32)).astype(BF16)  3.43 us
  transfers between devices with their start and end apart: 39, of which 10 were waited for; matrix products, arithmetic and copies ran while one was open for 5% of the time, Pallas kernels for 13%

profile of v4, /device:TPU:0, one launch (start us, length us, event | category | flops | bytes accessed | tf_op | source)
XLA Modules:
  0.0 136.7 jit_solution(12778394875230166084)
XLA Ops:
  1.1 2.6 %collective-permute-start = (bf16[320,1024]{1,0:T(8,128)(2,1)}, bf16[320,1024]{1,0:T(8,128)(2,1)S(1)}, u32[]{:S(2)}, u32[]{:S(2)}) collective-permute-start(bf16[320,1024]{1,0:T(8,128)(2,1)} %bitcast.28), channel_id=1, source_target_pairs={{0,8},{4,12},{8,0},{12,4},{1,9},{5,13},{9,1},{13,5},{2,10},{6,14},... | collective-permute-start | bytes 1966088 | tf_op jit(solution)/shard_map/ppermute | solution.py:26
  3.7 1.7 %shard_map.68 = f32[8,384]{1,0:T(8,128)} custom-call(bf16[320,1024]{1,0:T(8,128)(2,1)} %bitcast.29, bf16[320,1024]{1,0:T(8,128)(2,1)} %bitcast.30), custom_call_target="tpu_custom_call" | custom-call | tf_op jit(solution)/shard_map/pallas_call | solution.py:218
  5.4 1.5 %collective-permute-start.2 = (f32[8,384]{1,0:T(8,128)}, f32[8,384]{1,0:T(8,128)S(1)}, u32[]{:S(2)}, u32[]{:S(2)}) collective-permute-start(f32[8,384]{1,0:T(8,128)} %shard_map.68), channel_id=1, source_target_pairs={{0,16},{16,0},{1,17},{17,1},{2,18},{18,2},{3,19},{19,3},{4,20},{20... | collective-permute-start | bytes 36872 | tf_op jit(solution)/shard_map/ppermute | solution.py:26
  6.9 0.7 reshape.7
  7.7 1.7 %collective-permute-done.2 = f32[8,384]{1,0:T(8,128)S(1)} collective-permute-done((f32[8,384]{1,0:T(8,128)}, f32[8,384]{1,0:T(8,128)S(1)}, u32[]{:S(2)}, u32[]{:S(2)}) %collective-permute-start.2) | collective-permute-done | bytes 12320 | tf_op jit(solution)/shard_map/ppermute | solution.py:26
  9.5 1.8 %collective-permute-start.5 = (f32[8,384]{1,0:T(8,128)S(1)}, f32[8,384]{1,0:T(8,128)S(1)}, u32[]{:S(2)}, u32[]{:S(2)}) collective-permute-start(f32[8,384]{1,0:T(8,128)S(1)} %maximum_maximum_fusion.refs_2_.refs_4_), channel_id=1, source_target_pairs={{0,12},{4,8},{8,4},{12,0},{1,13},{5,9},{9,5},{13,1},{2,14},{6,10},... | collective-permute-start | bytes 36872 | tf_op jit(solution)/shard_map/ppermute | solution.py:26
  11.4 1.1 copy-done
  12.5 2.4 %copy-done.2 = bf16[5,1280,384]{2,1,0:T(8,128)(2,1)S(1)} copy-done((bf16[5,1280,384]{2,1,0:T(8,128)(2,1)S(1)}, bf16[5,1280,384]{2,1,0:T(8,128)(2,1)}, u32[]{:S(2)}) %copy-start.2) | copy-done | bytes 4915224
  14.9 4.3 %shard_map.69 = (f32[512,384]{1,0:T(8,128)S(1)}, f32[512,384]{1,0:T(8,128)S(1)}) custom-call(s32[2]{0:T(128)S(1)} %pad_add_fusion.idx_ref, bf16[320,1024]{1,0:T(8,128)(2,1)S(1)} %bitcast.31, bf16[320,1024]{1,0:T(8,128)(2,1)S(1)} %collective-permute-done.1.refs_1_.refs_2_, f32[8,384]{1,0:T(8,128)S(1)} %maximum_maximum_fusion.refs_2_.refs_4_, ...), custom_call_target="tpu_custom_call" | custom-call | tf_op jit(solution)/shard_map/pallas_call | solution.py:190
  19.8 2.0 %collective-permute-done.6.refs_1_.refs_3_ = bf16[320,1024]{1,0:T(8,128)(2,1)S(1)} collective-permute-done((bf16[320,1024]{1,0:T(8,128)(2,1)S(1)}, bf16[320,1024]{1,0:T(8,128)(2,1)S(1)}, u32[]{:S(2)}, u32[]{:S(2)}) %collective-permute-start.6) | collective-permute-done | bytes 655392 | tf_op jit(solution)/shard_map/ppermute | solution.py:26
  21.8 6.5 %shard_map.70 = (bf16[512,384]{1,0:T(8,128)(2,1)}, f32[1040,384]{1,0:T(8,128)S(1)}) custom-call(s32[2]{0:T(128)S(1)} %pad_add_fusion.idx_ref, bf16[320,1024]{1,0:T(8,128)(2,1)S(1)} %collective-permute-done.refs_0_.refs_1_, bf16[320,1024]{1,0:T(8,128)(2,1)S(1)} %collective-permute-done.6.refs_1_.refs_3_, f32[8,384]{1,0:T(8,128)S(1)} %collective-permute-done.4.refs_2_.refs_5_, ...), custom_call_target="tpu_custom_call" | custom-call | tf_op jit(solution)/shard_map/pallas_call | solution.py:190
  28.3 3.4 %shard_map.71 = (bf16[320,384]{1,0:T(8,128)(2,1)S(1)}, bf16[320,384]{1,0:T(8,128)(2,1)S(1)}, bf16[320,384]{1,0:T(8,128)(2,1)S(1)}, bf16[320,384]{1,0:T(8,128)(2,1)}) custom-call(s32[2]{0:T(128)S(1)} %pad_add_fusion.idx_ref, bf16[320,1024]{1,0:T(8,128)(2,1)S(1)} %bitcast.32, bf16[320,1024]{1,0:T(8,128)(2,1)S(1)} %collective-permute-done.refs_0_.refs_1_, ...), custom_call_target="tpu_custom_call" | custom-call | tf_op jit(solution)/shard_map/pallas_call | solution.py:190
  31.7 0.7 copy-done.15
  32.4 1.7 %collective-permute-start.8 = (bf16[320,384]{1,0:T(8,128)(2,1)S(1)}, bf16[320,384]{1,0:T(8,128)(2,1)S(1)}, u32[]{:S(2)}, u32[]{:S(2)}) collective-permute-start(bf16[320,384]{1,0:T(8,128)(2,1)S(1)} %get-tuple-element.78), channel_id=1, source_target_pairs={{0,16},{16,0},{1,17},{17,1},{2,18},{18,2},{3,19},{19,3},{4,20},{20... | collective-permute-start | bytes 737288 | tf_op jit(solution)/shard_map/ppermute | solution.py:26
  34.2 1.5 %collective-permute-start.7 = (bf16[512,384]{1,0:T(8,128)(2,1)}, bf16[512,384]{1,0:T(8,128)(2,1)}, u32[]{:S(2)}, u32[]{:S(2)}) collective-permute-start(bf16[512,384]{1,0:T(8,128)(2,1)} %get-tuple-element.69.refs_0_), channel_id=1, source_target_pairs={{0,8},{4,12},{8,0},{12,4},{1,9},{5,13},{9,1},{13,5},{2,10},{6,14},... | collective-permute-start | bytes 1179656 | tf_op jit(solution)/shard_map/ppermute | solution.py:26
  35.7 4.4 %shard_map.72 = (bf16[320,384]{1,0:T(8,128)(2,1)S(1)}, bf16[320,384]{1,0:T(8,128)(2,1)S(1)}, bf16[640,384]{1,0:T(8,128)(2,1)}, bf16[320,384]{1,0:T(8,128)(2,1)S(...) custom-call(s32[2]{0:T(128)S(1)} %pad_add_fusion.idx_ref, bf16[320,1024]{1,0:T(8,128)(2,1)S(1)} %bitcast.33, ...), custom_call_target="tpu_custom_call" | custom-call | tf_op jit(solution)/shard_map/pallas_call | solution.py:190
  40.1 0.7 copy-done.11
  40.8 0.7 copy-done.13
  41.5 0.9 add_convert_fusion.29
  42.9 2.4 %collective-permute-done.7.refs_1_ = bf16[512,384]{1,0:T(8,128)(2,1)} collective-permute-done((bf16[512,384]{1,0:T(8,128)(2,1)}, bf16[512,384]{1,0:T(8,128)(2,1)}, u32[]{:S(2)}, u32[]{:S(2)}) %collective-permute-start.7) | collective-permute-done | bytes 393248 | tf_op jit(solution)/shard_map/ppermute | solution.py:26
  45.7 1.8 %collective-permute-start.10 = (bf16[320,384]{1,0:T(8,128)(2,1)}, bf16[320,384]{1,0:T(8,128)(2,1)S(1)}, u32[]{:S(2)}, u32[]{:S(2)}) collective-permute-start(bf16[320,384]{1,0:T(8,128)(2,1)} %add_convert_fusion.29), channel_id=1, source_target_pairs={{0,1},{1,0},{2,3},{3,2},{4,5},{5,4},{6,7},{7,6},{8,9},{9,8},{10,11... | collective-permute-start | bytes 737288 | tf_op jit(solution)/shard_map/ppermute | solution.py:260
  47.5 1.1 copy-done.5
  48.6 1.1 copy-done.8
  49.6 3.6 %shard_map.73 = (bf16[320,384]{1,0:T(8,128)(2,1)S(1)}, bf16[320,384]{1,0:T(8,128)(2,1)S(1)}, bf16[640,384]{1,0:T(8,128)(2,1)S(1)}, bf16[320,384]{1,0:T(8,128)(2,...) custom-call(s32[2]{0:T(128)S(1)} %pad_add_fusion.idx_ref, bf16[320,1024]{1,0:T(8,128)(2,1)S(1)} %bitcast.34, ...), custom_call_target="tpu_custom_call" | custom-call | tf_op jit(solution)/shard_map/pallas_call | solution.py:190
  53.3 3.5 %collective-permute-done.9 = bf16[640,384]{1,0:T(8,128)(2,1)} collective-permute-done((bf16[640,384]{1,0:T(8,128)(2,1)}, bf16[640,384]{1,0:T(8,128)(2,1)}, u32[]{:S(2)}, u32[]{:S(2)}) %collective-permute-start.9) | collective-permute-done | bytes 491552 | tf_op jit(solution)/shard_map/ppermute | solution.py:26
  56.8 1.1 fusion.8
  58.0 2.7 %collective-permute-done.11 = bf16[320,384]{1,0:T(8,128)(2,1)} collective-permute-done((bf16[320,384]{1,0:T(8,128)(2,1)}, bf16[320,384]{1,0:T(8,128)(2,1)}, u32[]{:S(2)}, u32[]{:S(2)}) %collective-permute-start.11) | collective-permute-done | bytes 245792 | tf_op jit(solution)/shard_map/ppermute | solution.py:26
  60.7 1.0 add_convert_fusion.28
  61.7 1.6 %collective-permute-start.15 = (bf16[320,384]{1,0:T(8,128)(2,1)S(1)}, bf16[320,384]{1,0:T(8,128)(2,1)S(1)}, u32[]{:S(2)}, u32[]{:S(2)}) collective-permute-start(bf16[320,384]{1,0:T(8,128)(2,1)S(1)} %add_convert_fusion.28), channel_id=1, source_target_pairs={{0,1},{1,0},{2,3},{3,2},{4,5},{5,4},{6,7},{7,6},{8,9},{9,8},{10,11... | collective-permute-start | bytes 737288 | tf_op jit(solution)/shard_map/ppermute | solution.py:260
  63.4 0.7 collective-permute-start.18
  64.8 4.4 %collective-permute-start.17 = (bf16[320,384]{1,0:T(8,128)(2,1)S(1)}, bf16[320,384]{1,0:T(8,128)(2,1)S(1)}, u32[]{:S(2)}, u32[]{:S(2)}) collective-permute-start(bf16[320,384]{1,0:T(8,128)(2,1)S(1)} %add_convert_fusion.26), channel_id=1, source_target_pairs={{0,1},{1,0},{2,3},{3,2},{4,5},{5,4},{6,7},{7,6},{8,9},{9,8},{10,11... | collective-permute-start | bytes 737288 | tf_op jit(solution)/shard_map/ppermute | solution.py:260
  69.3 0.7 collective-permute-start.16
  70.1 5.0 %collective-permute-start.20 = (bf16[320,384]{1,0:T(8,128)(2,1)S(1)}, bf16[320,384]{1,0:T(8,128)(2,1)S(1)}, u32[]{:S(2)}, u32[]{:S(2)}) collective-permute-start(bf16[320,384]{1,0:T(8,128)(2,1)S(1)} %broadcast_select_fusion.16), channel_id=1, source_target_pairs={{0,1},{1,0},{2,3},{3,2},{4,5},{5,4},{6,7},{7,6},{8,9},{9,8},{10,11... | collective-permute-start | bytes 737288 | tf_op jit(solution)/shard_map/ppermute | solution.py:260
  76.2 2.1 %collective-permute-start.19 = (bf16[640,384]{1,0:T(8,128)(2,1)S(1)}, bf16[640,384]{1,0:T(8,128)(2,1)S(1)}, u32[]{:S(2)}, u32[]{:S(2)}) collective-permute-start(bf16[640,384]{1,0:T(8,128)(2,1)S(1)} %get-tuple-element.93), channel_id=1, source_target_pairs={{0,16},{16,0},{1,17},{17,1},{2,18},{18,2},{3,19},{19,3},{4,20},{20... | collective-permute-start | bytes 1474568 | tf_op jit(solution)/shard_map/ppermute | solution.py:26
  78.3 3.5 %collective-permute-start.22 = (bf16[320,384]{1,0:T(8,128)(2,1)S(1)}, bf16[320,384]{1,0:T(8,128)(2,1)S(1)}, u32[]{:S(2)}, u32[]{:S(2)}) collective-permute-start(bf16[320,384]{1,0:T(8,128)(2,1)S(1)} %get-tuple-element.124), channel_id=1, source_target_pairs={{0,1},{1,0},{2,3},{3,2},{4,5},{5,4},{6,7},{7,6},{8,9},{9,8},{10,11... | collective-permute-start | bytes 737288 | tf_op jit(solution)/shard_map/ppermute | solution.py:260
  82.8 5.1 %collective-permute-start.27 = (bf16[320,384]{1,0:T(8,128)(2,1)S(1)}, bf16[320,384]{1,0:T(8,128)(2,1)S(1)}, u32[]{:S(2)}, u32[]{:S(2)}) collective-permute-start(bf16[320,384]{1,0:T(8,128)(2,1)S(1)} %broadcast_select_fusion.14), channel_id=1, source_target_pairs={{0,1},{1,0},{2,3},{3,2},{4,5},{5,4},{6,7},{7,6},{8,9},{9,8},{10,11... | collective-permute-start | bytes 737288 | tf_op jit(solution)/shard_map/ppermute | solution.py:260
  89.3 1.9 %collective-permute-start.24 = (bf16[640,384]{1,0:T(8,128)(2,1)S(1)}, bf16[640,384]{1,0:T(8,128)(2,1)S(1)}, u32[]{:S(2)}, u32[]{:S(2)}) collective-permute-start(bf16[640,384]{1,0:T(8,128)(2,1)S(1)} %get-tuple-element.101), channel_id=1, source_target_pairs={{0,16},{16,0},{1,17},{17,1},{2,18},{18,2},{3,19},{19,3},{4,20},{20... | collective-permute-start | bytes 1474568 | tf_op jit(solution)/shard_map/ppermute | solution.py:26
  91.2 4.0 %collective-permute-start.25 = (bf16[320,384]{1,0:T(8,128)(2,1)S(1)}, bf16[320,384]{1,0:T(8,128)(2,1)S(1)}, u32[]{:S(2)}, u32[]{:S(2)}) collective-permute-start(bf16[320,384]{1,0:T(8,128)(2,1)S(1)} %get-tuple-element.122), channel_id=1, source_target_pairs={{0,1},{1,0},{2,3},{3,2},{4,5},{5,4},{6,7},{7,6},{8,9},{9,8},{10,11... | collective-permute-start | bytes 737288 | tf_op jit(solution)/shard_map/ppermute | solution.py:260
  96.2 3.7 %collective-permute-start.29 = (bf16[320,384]{1,0:T(8,128)(2,1)S(1)}, bf16[320,384]{1,0:T(8,128)(2,1)S(1)}, u32[]{:S(2)}, u32[]{:S(2)}) collective-permute-start(bf16[320,384]{1,0:T(8,128)(2,1)S(1)} %broadcast_select_fusion.12), channel_id=1, source_target_pairs={{0,1},{1,0},{2,3},{3,2},{4,5},{5,4},{6,7},{7,6},{8,9},{9,8},{10,11... | collective-permute-start | bytes 737288 | tf_op jit(solution)/shard_map/ppermute | solution.py:260
  101.1 6.7 %collective-permute-start.33 = (bf16[320,384]{1,0:T(8,128)(2,1)S(1)}, bf16[320,384]{1,0:T(8,128)(2,1)S(1)}, u32[]{:S(2)}, u32[]{:S(2)}) collective-permute-start(bf16[320,384]{1,0:T(8,128)(2,1)S(1)} %broadcast_select_fusion.11), channel_id=1, source_target_pairs={{0,1},{1,0},{2,3},{3,2},{4,5},{5,4},{6,7},{7,6},{8,9},{9,8},{10,11... | collective-permute-start | bytes 737288 | tf_op jit(solution)/shard_map/ppermute | solution.py:260
  108.8 4.0 %collective-permute-start.31 = (bf16[320,384]{1,0:T(8,128)(2,1)S(1)}, bf16[320,384]{1,0:T(8,128)(2,1)S(1)}, u32[]{:S(2)}, u32[]{:S(2)}) collective-permute-start(bf16[320,384]{1,0:T(8,128)(2,1)S(1)} %broadcast_select_fusion.10), channel_id=1, source_target_pairs={{0,1},{1,0},{2,3},{3,2},{4,5},{5,4},{6,7},{7,6},{8,9},{9,8},{10,11... | collective-permute-start | bytes 737288 | tf_op jit(solution)/shard_map/ppermute | solution.py:260
  113.7 4.4 %collective-permute-start.34 = (bf16[320,384]{1,0:T(8,128)(2,1)S(1)}, bf16[320,384]{1,0:T(8,128)(2,1)S(1)}, u32[]{:S(2)}, u32[]{:S(2)}) collective-permute-start(bf16[320,384]{1,0:T(8,128)(2,1)S(1)} %add_convert_fusion.3), channel_id=1, source_target_pairs={{0,1},{1,0},{2,3},{3,2},{4,5},{5,4},{6,7},{7,6},{8,9},{9,8},{10,11... | collective-permute-start | bytes 737288 | tf_op jit(solution)/shard_map/ppermute | solution.py:260
  118.3 0.9 collective-permute-start.37
  119.3 4.3 %shard_map.74 = bf16[512,640]{1,0:T(8,128)(2,1)} custom-call(s32[2]{0:T(128)S(1)} %pad_add_fusion.idx_ref, bf16[512,384]{1,0:T(8,128)(2,1)} %get-tuple-element.69.refs_0_, bf16[512,384]{1,0:T(8,128)(2,1)} %collective-permute-done.7.refs_1_, bf16[512,384]{1,0:T(8,128)(2,1)} %collective-permute-done.12.refs_2_, ...), custom_call_target="tpu_custom_call" | custom-call | tf_op jit(solution)/shard_map/pallas_call | solution.py:190
  123.7 3.5 %collective-permute-start.36 = (bf16[320,384]{1,0:T(8,128)(2,1)S(1)}, bf16[320,384]{1,0:T(8,128)(2,1)S(1)}, u32[]{:S(2)}, u32[]{:S(2)}) collective-permute-start(bf16[320,384]{1,0:T(8,128)(2,1)S(1)} %add_convert_fusion.1), channel_id=1, source_target_pairs={{0,1},{1,0},{2,3},{3,2},{4,5},{5,4},{6,7},{7,6},{8,9},{9,8},{10,11... | collective-permute-start | bytes 737288 | tf_op jit(solution)/shard_map/ppermute | solution.py:260
  127.9 3.5 %collective-permute-done.36 = bf16[320,384]{1,0:T(8,128)(2,1)S(1)} collective-permute-done((bf16[320,384]{1,0:T(8,128)(2,1)S(1)}, bf16[320,384]{1,0:T(8,128)(2,1)S(1)}, u32[]{:S(2)}, u32[]{:S(2)}) %collective-permute-start.36) | collective-permute-done | bytes 245792 | tf_op jit(solution)/shard_map/ppermute | solution.py:260
  131.4 2.6 %collective-permute-done.38 = bf16[320,384]{1,0:T(8,128)(2,1)S(1)} collective-permute-done((bf16[320,384]{1,0:T(8,128)(2,1)S(1)}, bf16[320,384]{1,0:T(8,128)(2,1)S(1)}, u32[]{:S(2)}, u32[]{:S(2)}) %collective-permute-start.38) | collective-permute-done | bytes 245792 | tf_op jit(solution)/shard_map/ppermute | solution.py:260
  134.1 2.6 %stack.44 = f32[640,5,384]{2,0,1:T(8,128)} convert(bf16[640,5,384]{2,0,1:T(8,128)(2,1)S(1)} %fusion.4) | non-fusion elementwise | flops 1228800 | bytes 7372800 | tf_op jit(solution)/shard_map/stack | solution.py:378
  (132 shorter events, 11.7 us)
Async XLA Ops:
  0.6 10.8 %collective-permute-start.1 = (bf16[320,1024]{1,0:T(8,128)(2,1)}, bf16[320,1024]{1,0:T(8,128)(2,1)S(1)}, u32[]{:S(2)}, u32[]{:S(2)}) collective-permute-start(bf16[320,1024]{1,0:T(8,128)(2,1)} %bitcast.27), channel_id=1, source_target_pairs={{0,4},{4,0},{8,12},{12,8},{1,5},{5,1},{9,13},{13,9},{2,6},{6,2},{1... | collective-permute-start | bytes 1966088 | tf_op jit(solution)/shard_map/ppermute | solution.py:26
  1.1 18.5 %collective-permute-start = (bf16[320,1024]{1,0:T(8,128)(2,1)}, bf16[320,1024]{1,0:T(8,128)(2,1)S(1)}, u32[]{:S(2)}, u32[]{:S(2)}) collective-permute-start(bf16[320,1024]{1,0:T(8,128)(2,1)} %bitcast.28), channel_id=1, source_target_pairs={{0,8},{4,12},{8,0},{12,4},{1,9},{5,13},{9,1},{13,5},{2,10},{6,14},... | collective-permute-start | bytes 1966088 | tf_op jit(solution)/shard_map/ppermute | solution.py:26
  5.4 3.9 %collective-permute-start.2 = (f32[8,384]{1,0:T(8,128)}, f32[8,384]{1,0:T(8,128)S(1)}, u32[]{:S(2)}, u32[]{:S(2)}) collective-permute-start(f32[8,384]{1,0:T(8,128)} %shard_map.68), channel_id=1, source_target_pairs={{0,16},{16,0},{1,17},{17,1},{2,18},{18,2},{3,19},{19,3},{4,20},{20... | collective-permute-start | bytes 36872 | tf_op jit(solution)/shard_map/ppermute | solution.py:26
  9.4 2.0 %collective-permute-start.3 = (f32[8,384]{1,0:T(8,128)S(1)}, f32[8,384]{1,0:T(8,128)S(1)}, u32[]{:S(2)}, u32[]{:S(2)}) collective-permute-start(f32[8,384]{1,0:T(8,128)S(1)} %maximum_maximum_fusion.refs_2_.refs_4_), channel_id=1, source_target_pairs={{0,4},{4,0},{8,12},{12,8},{1,5},{5,1},{9,13},{13,9},{2,6},{6,2},{1... | collective-permute-start | bytes 36872 | tf_op jit(solution)/shard_map/ppermute | solution.py:26
  9.4 10.2 %collective-permute-start.4 = (f32[8,384]{1,0:T(8,128)S(1)}, f32[8,384]{1,0:T(8,128)S(1)}, u32[]{:S(2)}, u32[]{:S(2)}) collective-permute-start(f32[8,384]{1,0:T(8,128)S(1)} %maximum_maximum_fusion.refs_2_.refs_4_), channel_id=1, source_target_pairs={{0,8},{4,12},{8,0},{12,4},{1,9},{5,13},{9,1},{13,5},{2,10},{6,14},... | collective-permute-start | bytes 36872 | tf_op jit(solution)/shard_map/ppermute | solution.py:26
  9.5 10.2 %collective-permute-start.5 = (f32[8,384]{1,0:T(8,128)S(1)}, f32[8,384]{1,0:T(8,128)S(1)}, u32[]{:S(2)}, u32[]{:S(2)}) collective-permute-start(f32[8,384]{1,0:T(8,128)S(1)} %maximum_maximum_fusion.refs_2_.refs_4_), channel_id=1, source_target_pairs={{0,12},{4,8},{8,4},{12,0},{1,13},{5,9},{9,5},{13,1},{2,14},{6,10},... | collective-permute-start | bytes 36872 | tf_op jit(solution)/shard_map/ppermute | solution.py:26
  14.9 6.9 %copy-start.3 = (bf16[5,1280,384]{2,1,0:T(8,128)(2,1)S(1)}, bf16[5,1280,384]{2,1,0:T(8,128)(2,1)}, u32[]{:S(2)}) copy-start(bf16[5,1280,384]{2,1,0:T(8,128)(2,1)} %refs_4_.3) | copy-start | bytes 14745604
  14.9 6.9 %copy-start.10 = (bf16[1,512,384]{2,1,0:T(8,128)(2,1)S(1)}, bf16[1,512,384]{2,1,0:T(8,128)(2,1)}, u32[]{:S(2)}) copy-start(bf16[1,512,384]{2,1,0:T(8,128)(2,1)} %param.9) | copy-start | bytes 1179652
  19.7 2.1 %collective-permute-start.6 = (bf16[320,1024]{1,0:T(8,128)(2,1)S(1)}, bf16[320,1024]{1,0:T(8,128)(2,1)S(1)}, u32[]{:S(2)}, u32[]{:S(2)}) collective-permute-start(bf16[320,1024]{1,0:T(8,128)(2,1)S(1)} %collective-permute-done.refs_0_.refs_1_), channel_id=1, source_target_pairs={{0,4},{4,0},{8,12},{12,8},{1,5},{5,1},{9,13},{13,9},{2,6},{6,2},{1... | collective-permute-start | bytes 1966088 | tf_op jit(solution)/shard_map/ppermute | solution.py:26
  21.8 13.9 %copy-start.4 = (bf16[320,1024]{1,0:T(8,128)(2,1)}, bf16[320,1024]{1,0:T(8,128)(2,1)S(1)}, u32[]{:S(2)}) copy-start(bf16[320,1024]{1,0:T(8,128)(2,1)S(1)} %collective-permute-done.6.refs_1_.refs_3_) | copy-start | bytes 1966084
  32.4 9.1 %collective-permute-start.8 = (bf16[320,384]{1,0:T(8,128)(2,1)S(1)}, bf16[320,384]{1,0:T(8,128)(2,1)S(1)}, u32[]{:S(2)}, u32[]{:S(2)}) collective-permute-start(bf16[320,384]{1,0:T(8,128)(2,1)S(1)} %get-tuple-element.78), channel_id=1, source_target_pairs={{0,16},{16,0},{1,17},{17,1},{2,18},{18,2},{3,19},{19,3},{4,20},{20... | collective-permute-start | bytes 737288 | tf_op jit(solution)/shard_map/ppermute | solution.py:26
  34.2 11.2 %collective-permute-start.7 = (bf16[512,384]{1,0:T(8,128)(2,1)}, bf16[512,384]{1,0:T(8,128)(2,1)}, u32[]{:S(2)}, u32[]{:S(2)}) collective-permute-start(bf16[512,384]{1,0:T(8,128)(2,1)} %get-tuple-element.69.refs_0_), channel_id=1, source_target_pairs={{0,8},{4,12},{8,0},{12,4},{1,9},{5,13},{9,1},{13,5},{2,10},{6,14},... | collective-permute-start | bytes 1179656 | tf_op jit(solution)/shard_map/ppermute | solution.py:26
  42.4 14.5 %collective-permute-start.9 = (bf16[640,384]{1,0:T(8,128)(2,1)}, bf16[640,384]{1,0:T(8,128)(2,1)}, u32[]{:S(2)}, u32[]{:S(2)}) collective-permute-start(bf16[640,384]{1,0:T(8,128)(2,1)} %get-tuple-element.79), channel_id=1, source_target_pairs={{0,16},{16,0},{1,17},{17,1},{2,18},{18,2},{3,19},{19,3},{4,20},{20... | collective-permute-start | bytes 1474568 | tf_op jit(solution)/shard_map/ppermute | solution.py:26
  42.9 17.7 %collective-permute-start.12 = (bf16[512,384]{1,0:T(8,128)(2,1)}, bf16[512,384]{1,0:T(8,128)(2,1)}, u32[]{:S(2)}, u32[]{:S(2)}) collective-permute-start(bf16[512,384]{1,0:T(8,128)(2,1)} %get-tuple-element.69.refs_0_), channel_id=1, source_target_pairs={{0,4},{4,0},{8,12},{12,8},{1,5},{5,1},{9,13},{13,9},{2,6},{6,2},{1... | collective-permute-start | bytes 1179656 | tf_op jit(solution)/shard_map/ppermute | solution.py:26
  45.3 15.3 %collective-permute-start.13 = (bf16[512,384]{1,0:T(8,128)(2,1)}, bf16[512,384]{1,0:T(8,128)(2,1)}, u32[]{:S(2)}, u32[]{:S(2)}) collective-permute-start(bf16[512,384]{1,0:T(8,128)(2,1)} %collective-permute-done.7.refs_1_), channel_id=1, source_target_pairs={{0,4},{4,0},{8,12},{12,8},{1,5},{5,1},{9,13},{13,9},{2,6},{6,2},{1... | collective-permute-start | bytes 1179656 | tf_op jit(solution)/shard_map/ppermute | solution.py:26
  45.4 15.3 %collective-permute-start.11 = (bf16[320,384]{1,0:T(8,128)(2,1)}, bf16[320,384]{1,0:T(8,128)(2,1)}, u32[]{:S(2)}, u32[]{:S(2)}) collective-permute-start(bf16[320,384]{1,0:T(8,128)(2,1)} %get-tuple-element.81), channel_id=1, source_target_pairs={{0,16},{16,0},{1,17},{17,1},{2,18},{18,2},{3,19},{19,3},{4,20},{20... | collective-permute-start | bytes 737288 | tf_op jit(solution)/shard_map/ppermute | solution.py:26
  45.7 17.7 %collective-permute-start.10 = (bf16[320,384]{1,0:T(8,128)(2,1)}, bf16[320,384]{1,0:T(8,128)(2,1)S(1)}, u32[]{:S(2)}, u32[]{:S(2)}) collective-permute-start(bf16[320,384]{1,0:T(8,128)(2,1)} %add_convert_fusion.29), channel_id=1, source_target_pairs={{0,1},{1,0},{2,3},{3,2},{4,5},{5,4},{6,7},{7,6},{8,9},{9,8},{10,11... | collective-permute-start | bytes 737288 | tf_op jit(solution)/shard_map/ppermute | solution.py:260
  49.6 11.0 %copy-start.16 = (bf16[320,384]{1,0:T(8,128)(2,1)S(1)}, bf16[320,384]{1,0:T(8,128)(2,1)}, u32[]{:S(2)}) copy-start(bf16[320,384]{1,0:T(8,128)(2,1)} %copy-done.15) | copy-start | bytes 737284
  49.6 13.7 %copy-start.19 = (bf16[320,384]{1,0:T(8,128)(2,1)S(1)}, bf16[320,384]{1,0:T(8,128)(2,1)}, u32[]{:S(2)}) copy-start(bf16[320,384]{1,0:T(8,128)(2,1)} %add_convert_fusion.29) | copy-start | bytes 737284
  49.6 14.4 %copy-start.14 = (bf16[320,384]{1,0:T(8,128)(2,1)S(1)}, bf16[320,384]{1,0:T(8,128)(2,1)}, u32[]{:S(2)}) copy-start(bf16[320,384]{1,0:T(8,128)(2,1)} %copy-done.13) | copy-start | bytes 737284
  53.3 10.9 %copy-start.18 = (bf16[640,384]{1,0:T(8,128)(2,1)S(1)}, bf16[640,384]{1,0:T(8,128)(2,1)}, u32[]{:S(2)}) copy-start(bf16[640,384]{1,0:T(8,128)(2,1)} %copy-done.17) | copy-start | bytes 1474564
  61.7 7.5 %collective-permute-start.15 = (bf16[320,384]{1,0:T(8,128)(2,1)S(1)}, bf16[320,384]{1,0:T(8,128)(2,1)S(1)}, u32[]{:S(2)}, u32[]{:S(2)}) collective-permute-start(bf16[320,384]{1,0:T(8,128)(2,1)S(1)} %add_convert_fusion.28), channel_id=1, source_target_pairs={{0,1},{1,0},{2,3},{3,2},{4,5},{5,4},{6,7},{7,6},{8,9},{9,8},{10,11... | collective-permute-start | bytes 737288 | tf_op jit(solution)/shard_map/ppermute | solution.py:260
  63.4 6.5 %collective-permute-start.18 = (bf16[320,384]{1,0:T(8,128)(2,1)S(1)}, bf16[320,384]{1,0:T(8,128)(2,1)S(1)}, u32[]{:S(2)}, u32[]{:S(2)}) collective-permute-start(bf16[320,384]{1,0:T(8,128)(2,1)S(1)} %add_convert_fusion.27), channel_id=1, source_target_pairs={{0,0},{1,2},{2,1},{3,3},{4,4},{5,6},{6,5},{7,7},{8,8},{9,10},{10,9... | collective-permute-start | bytes 737288 | tf_op jit(solution)/shard_map/ppermute | solution.py:266
  64.2 11.9 %copy-start.12 = (bf16[320,384]{1,0:T(8,128)(2,1)S(1)}, bf16[320,384]{1,0:T(8,128)(2,1)}, u32[]{:S(2)}) copy-start(bf16[320,384]{1,0:T(8,128)(2,1)} %copy-done.11) | copy-start | bytes 737284
  64.2 11.8 %collective-permute-start.14 = (bf16[640,384]{1,0:T(8,128)(2,1)S(1)}, bf16[640,384]{1,0:T(8,128)(2,1)S(1)}, u32[]{:S(2)}, u32[]{:S(2)}) collective-permute-start(bf16[640,384]{1,0:T(8,128)(2,1)S(1)} %copy-done.18), channel_id=1, source_target_pairs={{0,16},{16,0},{1,17},{17,1},{2,18},{18,2},{3,19},{19,3},{4,20},{20... | collective-permute-start | bytes 1474568 | tf_op jit(solution)/shard_map/ppermute | solution.py:26
  64.8 10.4 %collective-permute-start.17 = (bf16[320,384]{1,0:T(8,128)(2,1)S(1)}, bf16[320,384]{1,0:T(8,128)(2,1)S(1)}, u32[]{:S(2)}, u32[]{:S(2)}) collective-permute-start(bf16[320,384]{1,0:T(8,128)(2,1)S(1)} %add_convert_fusion.26), channel_id=1, source_target_pairs={{0,1},{1,0},{2,3},{3,2},{4,5},{5,4},{6,7},{7,6},{8,9},{9,8},{10,11... | collective-permute-start | bytes 737288 | tf_op jit(solution)/shard_map/ppermute | solution.py:260
  69.3 6.7 %collective-permute-start.16 = (bf16[320,384]{1,0:T(8,128)(2,1)S(1)}, bf16[320,384]{1,0:T(8,128)(2,1)S(1)}, u32[]{:S(2)}, u32[]{:S(2)}) collective-permute-start(bf16[320,384]{1,0:T(8,128)(2,1)S(1)} %add_convert_fusion.25), channel_id=1, source_target_pairs={{0,0},{1,2},{2,1},{3,3},{4,4},{5,6},{6,5},{7,7},{8,8},{9,10},{10,9... | collective-permute-start | bytes 737288 | tf_op jit(solution)/shard_map/ppermute | solution.py:266
  70.1 11.7 %collective-permute-start.20 = (bf16[320,384]{1,0:T(8,128)(2,1)S(1)}, bf16[320,384]{1,0:T(8,128)(2,1)S(1)}, u32[]{:S(2)}, u32[]{:S(2)}) collective-permute-start(bf16[320,384]{1,0:T(8,128)(2,1)S(1)} %broadcast_select_fusion.16), channel_id=1, source_target_pairs={{0,1},{1,0},{2,3},{3,2},{4,5},{5,4},{6,7},{7,6},{8,9},{9,8},{10,11... | collective-permute-start | bytes 737288 | tf_op jit(solution)/shard_map/ppermute | solution.py:260
  75.2 7.4 %collective-permute-start.23 = (bf16[320,384]{1,0:T(8,128)(2,1)S(1)}, bf16[320,384]{1,0:T(8,128)(2,1)S(1)}, u32[]{:S(2)}, u32[]{:S(2)}) collective-permute-start(bf16[320,384]{1,0:T(8,128)(2,1)S(1)} %add_convert_fusion.22), channel_id=1, source_target_pairs={{0,0},{1,2},{2,1},{3,3},{4,4},{5,6},{6,5},{7,7},{8,8},{9,10},{10,9... | collective-permute-start | bytes 737288 | tf_op jit(solution)/shard_map/ppermute | solution.py:266
  76.2 12.9 %collective-permute-start.19 = (bf16[640,384]{1,0:T(8,128)(2,1)S(1)}, bf16[640,384]{1,0:T(8,128)(2,1)S(1)}, u32[]{:S(2)}, u32[]{:S(2)}) collective-permute-start(bf16[640,384]{1,0:T(8,128)(2,1)S(1)} %get-tuple-element.93), channel_id=1, source_target_pairs={{0,16},{16,0},{1,17},{17,1},{2,18},{18,2},{3,19},{19,3},{4,20},{20... | collective-permute-start | bytes 1474568 | tf_op jit(solution)/shard_map/ppermute | solution.py:26
  78.3 9.9 %collective-permute-start.22 = (bf16[320,384]{1,0:T(8,128)(2,1)S(1)}, bf16[320,384]{1,0:T(8,128)(2,1)S(1)}, u32[]{:S(2)}, u32[]{:S(2)}) collective-permute-start(bf16[320,384]{1,0:T(8,128)(2,1)S(1)} %get-tuple-element.124), channel_id=1, source_target_pairs={{0,1},{1,0},{2,3},{3,2},{4,5},{5,4},{6,7},{7,6},{8,9},{9,8},{10,11... | collective-permute-start | bytes 737288 | tf_op jit(solution)/shard_map/ppermute | solution.py:260
  81.9 7.0 %collective-permute-start.21 = (bf16[320,384]{1,0:T(8,128)(2,1)S(1)}, bf16[320,384]{1,0:T(8,128)(2,1)S(1)}, u32[]{:S(2)}, u32[]{:S(2)}) collective-permute-start(bf16[320,384]{1,0:T(8,128)(2,1)S(1)} %add_convert_fusion.19), channel_id=1, source_target_pairs={{0,0},{1,2},{2,1},{3,3},{4,4},{5,6},{6,5},{7,7},{8,8},{9,10},{10,9... | collective-permute-start | bytes 737288 | tf_op jit(solution)/shard_map/ppermute | solution.py:266
  82.8 12.4 %collective-permute-start.27 = (bf16[320,384]{1,0:T(8,128)(2,1)S(1)}, bf16[320,384]{1,0:T(8,128)(2,1)S(1)}, u32[]{:S(2)}, u32[]{:S(2)}) collective-permute-start(bf16[320,384]{1,0:T(8,128)(2,1)S(1)} %broadcast_select_fusion.14), channel_id=1, source_target_pairs={{0,1},{1,0},{2,3},{3,2},{4,5},{5,4},{6,7},{7,6},{8,9},{9,8},{10,11... | collective-permute-start | bytes 737288 | tf_op jit(solution)/shard_map/ppermute | solution.py:260
  88.2 7.8 %collective-permute-start.26 = (bf16[320,384]{1,0:T(8,128)(2,1)S(1)}, bf16[320,384]{1,0:T(8,128)(2,1)S(1)}, u32[]{:S(2)}, u32[]{:S(2)}) collective-permute-start(bf16[320,384]{1,0:T(8,128)(2,1)S(1)} %add_convert_fusion.16), channel_id=1, source_target_pairs={{0,0},{1,2},{2,1},{3,3},{4,4},{5,6},{6,5},{7,7},{8,8},{9,10},{10,9... | collective-permute-start | bytes 737288 | tf_op jit(solution)/shard_map/ppermute | solution.py:266
  89.3 11.7 %collective-permute-start.24 = (bf16[640,384]{1,0:T(8,128)(2,1)S(1)}, bf16[640,384]{1,0:T(8,128)(2,1)S(1)}, u32[]{:S(2)}, u32[]{:S(2)}) collective-permute-start(bf16[640,384]{1,0:T(8,128)(2,1)S(1)} %get-tuple-element.101), channel_id=1, source_target_pairs={{0,16},{16,0},{1,17},{17,1},{2,18},{18,2},{3,19},{19,3},{4,20},{20... | collective-permute-start | bytes 1474568 | tf_op jit(solution)/shard_map/ppermute | solution.py:26
  91.2 8.8 %collective-permute-start.25 = (bf16[320,384]{1,0:T(8,128)(2,1)S(1)}, bf16[320,384]{1,0:T(8,128)(2,1)S(1)}, u32[]{:S(2)}, u32[]{:S(2)}) collective-permute-start(bf16[320,384]{1,0:T(8,128)(2,1)S(1)} %get-tuple-element.122), channel_id=1, source_target_pairs={{0,1},{1,0},{2,3},{3,2},{4,5},{5,4},{6,7},{7,6},{8,9},{9,8},{10,11... | collective-permute-start | bytes 737288 | tf_op jit(solution)/shard_map/ppermute | solution.py:260
  95.3 5.5 %collective-permute-start.30 = (bf16[320,384]{1,0:T(8,128)(2,1)S(1)}, bf16[320,384]{1,0:T(8,128)(2,1)S(1)}, u32[]{:S(2)}, u32[]{:S(2)}) collective-permute-start(bf16[320,384]{1,0:T(8,128)(2,1)S(1)} %add_convert_fusion.13), channel_id=1, source_target_pairs={{0,0},{1,2},{2,1},{3,3},{4,4},{5,6},{6,5},{7,7},{8,8},{9,10},{10,9... | collective-permute-start | bytes 737288 | tf_op jit(solution)/shard_map/ppermute | solution.py:266
  96.2 11.6 %collective-permute-start.29 = (bf16[320,384]{1,0:T(8,128)(2,1)S(1)}, bf16[320,384]{1,0:T(8,128)(2,1)S(1)}, u32[]{:S(2)}, u32[]{:S(2)}) collective-permute-start(bf16[320,384]{1,0:T(8,128)(2,1)S(1)} %broadcast_select_fusion.12), channel_id=1, source_target_pairs={{0,1},{1,0},{2,3},{3,2},{4,5},{5,4},{6,7},{7,6},{8,9},{9,8},{10,11... | collective-permute-start | bytes 737288 | tf_op jit(solution)/shard_map/ppermute | solution.py:260
  100.1 8.6 %collective-permute-start.28 = (bf16[320,384]{1,0:T(8,128)(2,1)S(1)}, bf16[320,384]{1,0:T(8,128)(2,1)S(1)}, u32[]{:S(2)}, u32[]{:S(2)}) collective-permute-start(bf16[320,384]{1,0:T(8,128)(2,1)S(1)} %add_convert_fusion.10), channel_id=1, source_target_pairs={{0,0},{1,2},{2,1},{3,3},{4,4},{5,6},{6,5},{7,7},{8,8},{9,10},{10,9... | collective-permute-start | bytes 737288 | tf_op jit(solution)/shard_map/ppermute | solution.py:266
  101.1 11.7 %collective-permute-start.33 = (bf16[320,384]{1,0:T(8,128)(2,1)S(1)}, bf16[320,384]{1,0:T(8,128)(2,1)S(1)}, u32[]{:S(2)}, u32[]{:S(2)}) collective-permute-start(bf16[320,384]{1,0:T(8,128)(2,1)S(1)} %broadcast_select_fusion.11), channel_id=1, source_target_pairs={{0,1},{1,0},{2,3},{3,2},{4,5},{5,4},{6,7},{7,6},{8,9},{9,8},{10,11... | collective-permute-start | bytes 737288 | tf_op jit(solution)/shard_map/ppermute | solution.py:260
  107.9 5.7 %collective-permute-start.32 = (bf16[320,384]{1,0:T(8,128)(2,1)S(1)}, bf16[320,384]{1,0:T(8,128)(2,1)S(1)}, u32[]{:S(2)}, u32[]{:S(2)}) collective-permute-start(bf16[320,384]{1,0:T(8,128)(2,1)S(1)} %add_convert_fusion.7), channel_id=1, source_target_pairs={{0,0},{1,2},{2,1},{3,3},{4,4},{5,6},{6,5},{7,7},{8,8},{9,10},{10,9... | collective-permute-start | bytes 737288 | tf_op jit(solution)/shard_map/ppermute | solution.py:266
  108.8 10.4 %copy-start.9 = (bf16[1536,640]{1,0:T(8,128)(2,1)S(1)}, bf16[1536,640]{1,0:T(8,128)(2,1)}, u32[]{:S(2)}) copy-start(bf16[1536,640]{1,0:T(8,128)(2,1)} %refs_8_.1) | copy-start | bytes 5898244
  108.8 9.3 %collective-permute-start.31 = (bf16[320,384]{1,0:T(8,128)(2,1)S(1)}, bf16[320,384]{1,0:T(8,128)(2,1)S(1)}, u32[]{:S(2)}, u32[]{:S(2)}) collective-permute-start(bf16[320,384]{1,0:T(8,128)(2,1)S(1)} %broadcast_select_fusion.10), channel_id=1, source_target_pairs={{0,1},{1,0},{2,3},{3,2},{4,5},{5,4},{6,7},{7,6},{8,9},{9,8},{10,11... | collective-permute-start | bytes 737288 | tf_op jit(solution)/shard_map/ppermute | solution.py:260
  113.0 10.6 %collective-permute-start.35 = (bf16[320,384]{1,0:T(8,128)(2,1)S(1)}, bf16[320,384]{1,0:T(8,128)(2,1)S(1)}, u32[]{:S(2)}, u32[]{:S(2)}) collective-permute-start(bf16[320,384]{1,0:T(8,128)(2,1)S(1)} %add_convert_fusion.4), channel_id=1, source_target_pairs={{0,0},{1,2},{2,1},{3,3},{4,4},{5,6},{6,5},{7,7},{8,8},{9,10},{10,9... | collective-permute-start | bytes 737288 | tf_op jit(solution)/shard_map/ppermute | solution.py:266
  113.7 13.5 %collective-permute-start.34 = (bf16[320,384]{1,0:T(8,128)(2,1)S(1)}, bf16[320,384]{1,0:T(8,128)(2,1)S(1)}, u32[]{:S(2)}, u32[]{:S(2)}) collective-permute-start(bf16[320,384]{1,0:T(8,128)(2,1)S(1)} %add_convert_fusion.3), channel_id=1, source_target_pairs={{0,1},{1,0},{2,3},{3,2},{4,5},{5,4},{6,7},{7,6},{8,9},{9,8},{10,11... | collective-permute-start | bytes 737288 | tf_op jit(solution)/shard_map/ppermute | solution.py:260
  118.3 9.0 %collective-permute-start.37 = (bf16[320,384]{1,0:T(8,128)(2,1)S(1)}, bf16[320,384]{1,0:T(8,128)(2,1)S(1)}, u32[]{:S(2)}, u32[]{:S(2)}) collective-permute-start(bf16[320,384]{1,0:T(8,128)(2,1)S(1)} %add_convert_fusion.2), channel_id=1, source_target_pairs={{0,0},{1,2},{2,1},{3,3},{4,4},{5,6},{6,5},{7,7},{8,8},{9,10},{10,9... | collective-permute-start | bytes 737288 | tf_op jit(solution)/shard_map/ppermute | solution.py:266
  123.7 7.7 %collective-permute-start.36 = (bf16[320,384]{1,0:T(8,128)(2,1)S(1)}, bf16[320,384]{1,0:T(8,128)(2,1)S(1)}, u32[]{:S(2)}, u32[]{:S(2)}) collective-permute-start(bf16[320,384]{1,0:T(8,128)(2,1)S(1)} %add_convert_fusion.1), channel_id=1, source_target_pairs={{0,1},{1,0},{2,3},{3,2},{4,5},{5,4},{6,7},{7,6},{8,9},{9,8},{10,11... | collective-permute-start | bytes 737288 | tf_op jit(solution)/shard_map/ppermute | solution.py:260
  127.4 6.7 %collective-permute-start.38 = (bf16[320,384]{1,0:T(8,128)(2,1)S(1)}, bf16[320,384]{1,0:T(8,128)(2,1)S(1)}, u32[]{:S(2)}, u32[]{:S(2)}) collective-permute-start(bf16[320,384]{1,0:T(8,128)(2,1)S(1)} %add_convert_fusion), channel_id=1, source_target_pairs={{0,1},{1,0},{2,3},{3,2},{4,5},{5,4},{6,7},{7,6},{8,9},{9,8},{10,11... | collective-permute-start | bytes 737288 | tf_op jit(solution)/shard_map/ppermute | solution.py:260
  (11 other events, 25.9 us)

commit v5 on v4

--- a/solution.py
+++ b/solution.py
@@ -84,11 +84,13 @@
             odd_ref[rows, lanes] = tap_sum(y_scr, start, step, 1, taps, c)
 
 
-def second_kernel(offsets, idx_ref, *refs):
+def second_kernel(offsets, far, per, idx_ref, *refs):
     n = len(offsets)
-    *x_refs, w_ref, even_ref, odd_ref, grad_ref, enc_ref, pre_ref, rows_scr, y_scr, p_scr = refs
-    x_refs, halo_refs = x_refs[:-n], x_refs[-n:]
-    conv_rows(offsets, idx_ref[0], x_refs, halo_refs, w_ref, rows_scr, y_scr)
+    blocks, pays, refs = refs[:n], refs[n : 2 * n], refs[2 * n :]
+    w_ref, even_ref, odd_ref, grad_ref, enc_ref, pre_ref, *sent_refs, rows_scr, y_scr, p_scr, x_scr, edge_scr = refs
+    me = idx_ref[0]
+    pick = lambda items: [items[j] for j in far]
+    conv_rows(pick(offsets), me, pick(blocks), pick(pays), w_ref, rows_scr, y_scr)
     taps, width = w_ref.shape[0], w_ref.shape[2]
     half = even_ref.shape[0]
     step = min(64, half)
@@ -111,15 +113,25 @@
     for c in range(width // LANES):
         lanes = slice(c * LANES, (c + 1) * LANES)
         pre_ref[EDGE : EDGE + length, lanes] = p_scr[c].astype(BF16).astype(F32)
-
-
-def grad_kernel(offsets, group, shards, split, idx_ref, *refs):
-    n = len(offsets)
-    *x_refs, p_ref = refs[: -1 - len(group) * split[1]]
-    out_refs, edge_scr = refs[len(x_refs) + 1 : -1], refs[-1]
-    x_refs, halo_refs = x_refs[:-n], x_refs[-n:]
-    length = x_refs[0].shape[1]
-    width = p_ref.shape[1]
+    if not sent_refs:
+        return
+    wanted = (1 - idx_ref[1]) * per
+    depth = blocks[0].shape[0]
+    for off, block, pay in zip(offsets, blocks, pays):
+
+        @pl.when(me ^ off == wanted)
+        def _(block=block, pay=pay):
+            x_scr[:, 0:length] = block[...]
+            x_scr[:, length : length + LANES] = edge_block(pay, depth)
+
+    p, edge = shifted_rows(pre_ref, edge_scr, (0,))
+    res = jnp.dot(x_scr[:, 0:length], p, preferred_element_type=F32)
+    res = res + jnp.dot(x_scr[:, length : length + LANES], edge, preferred_element_type=F32)
+    sent_refs[0][...] = res.astype(BF16)
+
+
+def shifted_rows(p_ref, edge_scr, group):
+    length, width = p_ref.shape[0] - 2 * EDGE, p_ref.shape[1]
     edge_scr[...] = jnp.zeros_like(edge_scr)
     shifted = []
     for i, tap in enumerate(group):
@@ -127,15 +139,22 @@
         edge_scr[0:2, cols] = p_ref[EDGE - tap : EDGE - tap + 2, :]
         edge_scr[2:4, cols] = p_ref[EDGE + length + 2 - tap : EDGE + length + 4 - tap, :]
         shifted.append(p_ref[EDGE + 2 - tap : EDGE + 2 - tap + length, :].astype(BF16))
-    p = jnp.concatenate(shifted, axis=1)
-    edge = edge_scr[...].astype(BF16)
+    return jnp.concatenate(shifted, axis=1), edge_scr[...].astype(BF16)
+
+
+def grad_kernel(offsets, group, per, pieces, idx_ref, *refs):
+    n = len(offsets)
+    blocks, pays, p_ref = refs[:n], refs[n : 2 * n], refs[2 * n]
+    out_refs, edge_scr = refs[2 * n + 1 : -1], refs[-1]
+    width = p_ref.shape[1]
+    p, edge = shifted_rows(p_ref, edge_scr, group)
     me = idx_ref[0]
-    x = jnp.concatenate([ref[...] for ref in x_refs], axis=0)
+    x = jnp.concatenate([ref[...] for ref in blocks], axis=0)
     depth = x.shape[0] // n
-    halo = jnp.concatenate([edge_block(ref, depth) for ref in halo_refs], axis=0)
+    halo = jnp.concatenate([edge_block(ref, depth) for ref in pays], axis=0)
     res = jnp.dot(x, p, preferred_element_type=F32) + jnp.dot(halo, edge, preferred_element_type=F32)
     res = res.astype(BF16)
-    per, each = split
+    each = len(out_refs) // len(group)
     for i in range(len(group)):
         outs = out_refs[i * each : (i + 1) * each]
         for j, off in enumerate(offsets):
@@ -145,23 +164,20 @@
                 outs[0][pl.ds(pl.multiple_of(at * depth, 16), depth), :] = part
                 continue
             mine = lax.div(at, per) == idx_ref[1]
+            other = jnp.logical_not(mine)
             row = lax.rem(at, per)
-            for r in range(per):
-
-                @pl.when(jnp.logical_and(mine, row == r))
-                def _(ref=outs[r], part=part):
+            hits = [(outs[r], jnp.logical_and(mine, row == r)) for r in range(per)]
+            hits += [(outs[per + k], jnp.logical_and(other, row == r)) for k, r in enumerate(pieces)]
+            for ref, hit in hits:
+
+                @pl.when(hit)
+                def _(ref=ref, part=part):
                     ref[...] = part
 
-                if each == 2 * per:
-
-                    @pl.when(jnp.logical_and(jnp.logical_not(mine), row == r))
-                    def _(ref=outs[per + r], part=part):
-                        ref[...] = part
-
-            if each == per + 1:
-
-                @pl.when(jnp.logical_not(mine))
-                def _(ref=outs[per], part=part):
+            if not pieces:
+
+                @pl.when(other)
+                def _(ref=outs[per], part=part, row=row):
                     ref[pl.ds(pl.multiple_of(row * depth, 16), depth), :] = part
 
 
@@ -224,6 +240,7 @@
             pl.BlockSpec((depth, LANES), lambda i: (0, length // LANES - 1)),
         ],
         out_specs=pl.BlockSpec((8, width), lambda i: (0, 0)),
+        compiler_params=pltpu.CompilerParams(vmem_limit_bytes=2 * 1024 * 1024),
     )(x, x)
     if peers == 2:
         before = behind = swap(ends, "seq", 1)
@@ -312,69 +329,100 @@
     )
     hold = [even] + pick(payloads, far)
     blocks = blocks + [own] + [swap(after(b, *hold), "mp", bits[-1]) for b in blocks[1:]]
-    encoded, pre_grad = call(
-        functools.partial(second_kernel, pick(offsets, far)),
-        (jax.ShapeDtypeStruct((half, width), BF16), jax.ShapeDtypeStruct((length + 2 * EDGE, width), F32)),
-        scratch(far) + [pltpu.VMEM((width // LANES, length, LANES), F32)],
-        24,
-        idx, *pick(blocks, far), *pick(payloads, far), conv_weight, even, odd, encoder_grad[0],
-    )
-
     pair = shards == 2 and peers % shards == 0 and lax.axis_size("dp") == 4
     per = peers // shards if pair else 0
     piece = jax.ShapeDtypeStruct((depth, width), BF16)
-    keep, send = [], []
-    done = idx
+    encoded, pre_grad, *first = call(
+        functools.partial(second_kernel, offsets, far, per),
+        (
+            jax.ShapeDtypeStruct((half, width), BF16),
+            jax.ShapeDtypeStruct((length + 2 * EDGE, width), F32),
+            *([piece] if pair else []),
+        ),
+        scratch(far)
+        + [
+            pltpu.VMEM((width // LANES, length, LANES), F32),
+            pltpu.VMEM((depth, length + LANES), BF16),
+            pltpu.VMEM((LANES, width), F32),
+        ],
+        26,
+        idx, *blocks, *payloads, conv_weight, even, odd, encoder_grad[0],
+    )
     encs = [encoded]
     for bit in bits[:-1]:
         encs = encs + [swap(e, "mp", bit) for e in encs]
-    encs_own = swap(encoded, "mp", bits[-1])
-    for group in [(0,)] + [tuple(range(k, min(k + 2, taps))) for k in range(1, taps, 2)]:
+
+    everything = tuple(range(per))
+    pieces_of = lambda k: everything[1:] if k == 0 else (everything if k == taps - 1 else ())
+
+    def gradient(group, hold):
+        pieces = pieces_of(group[0])
         if not pair:
             outs = (jax.ShapeDtypeStruct((peers * depth, width), BF16),)
-        elif group[0] == 0:
-            outs = (piece,) * (2 * per)
         else:
-            outs = (piece,) * per + (jax.ShapeDtypeStruct((per * depth, width), BF16),)
+            whole = (jax.ShapeDtypeStruct((per * depth, width), BF16),)
+            outs = (piece,) * per + ((piece,) * len(pieces) if pieces else whole)
         each = len(outs)
         outs = call(
-            functools.partial(grad_kernel, offsets, group, shards, (per, each)),
+            functools.partial(grad_kernel, offsets, group, per, pieces),
             outs * len(group),
             [pltpu.VMEM((LANES, width * len(group)), F32)],
             14,
-            done, *blocks, *payloads, pre_grad,
+            after(idx, *hold) if hold else idx, *blocks, *payloads, pre_grad,
         )
-        done = after(idx, outs[0], *(encs[1:] if group[0] else ()))
-        for i in range(len(group)):
-            mine = outs[i * each : (i + 1) * each]
-            keep += mine[: max(per, 1)]
-            send.append(mine[per:])
-    encs = encs + [encs_own] + [swap(e, "mp", bits[-1]) for e in encs[1:]]
-
-    late = encs[-1]
+        outs = [outs[i * each : (i + 1) * each] for i in range(len(group))]
+        return [list(o[:per]) for o in outs], [list(o[per:]) for o in outs]
+
     if pair:
-        got = {0: [swap(v, "seq", 1) for v in send[0]]}
+        groups = [(0,)] + [tuple(range(k, min(k + 2, taps - 1))) for k in range(1, taps - 1, 2)] + [(taps - 1,)]
+        keep, send, got = [], [], {}
+        relays = []
+
+        def work(hold):
+            if not groups:
+                return
+            mine, other = gradient(groups.pop(0), hold)
+            for m, o in zip(mine, other):
+                keep.append(m)
+                send.append((list(first) + o) if len(send) == 0 else o)
+
+        def launch(tap, hold):
+            while len(send) <= tap:
+                work(hold)
+            got[tap] = [swap(after(v, *hold) if hold else v, "seq", 1) for v in send[tap]]
+
+        work([])
+        launch(0, [])
+        launch(1, [])
 
         def share(c, last):
             tap, row = c // per, c % per
-            value = got[tap][row] if tap == 0 else got[tap][0][row * depth : (row + 1) * depth]
+            value = got[tap][row] if len(got[tap]) > 1 else got[tap][0][row * depth : (row + 1) * depth]
             hold = [] if last is None else [last]
-            if c == 1:
-                hold = hold + encs
+            if c == per:
+                relays.extend([swap(after(e, last), "mp", bits[-1]) for e in encs])
+            if c == 2 * per:
+                hold = hold + relays
             if hold:
                 value = after(value, *hold)
-            return added(keep[c], value)
+            return added(keep[tap][row], value)
 
         def sent(c, last):
-            tap = c // per + 1
-            if c % per == 0 and tap < taps:
-                got[tap] = [swap(after(v, last), "seq", 1) for v in send[tap]]
+            if c == per - 1:
+                work([last] + encs[1:])
+                work([last])
+            if c % per == per - 1 and c // per + 2 < taps:
+                launch(c // per + 2, [last])
 
         sums, late = chain_sums(taps * per, share, sent)
+        encs = encs + relays
         sums = [jnp.concatenate(sums[k * per : (k + 1) * per], axis=0) for k in range(taps)]
     else:
-        sums = [lax.psum_scatter(v, "seq", scatter_dimension=0, tiled=True) for v in keep]
+        sums = [gradient((k,), [])[1][0][0] for k in range(taps)]
+        sums = [lax.psum_scatter(v, "seq", scatter_dimension=0, tiled=True) for v in sums]
         sums = [lax.psum(v, "dp").astype(F32) for v in sums]
+        encs = encs + [swap(e, "mp", bits[-1]) for e in encs]
+        late = encs[-1]
     conv_grad = jnp.stack(sums, axis=1)
 
     qkv = call(

time: 137 us -> 139 us (1.015)
  starting transfers between devices: 70.5 us -> 66.9 us
  local copies, waits for them, and re-layouts: 9.85 us -> 12.7 us
  waiting for transfers between devices: 19.2 us -> 20.6 us
    ppermute x13, waiting for transfers between devices: 6.39 us -> 16.8 us  [chain_sums(): outer[r] = lax.ppermute(value, 'dp', outer_pairs)]
    ppermute x16 -> x17, waiting for transfers between devices: 12.8 us -> 3.7 us  [swap(): return lax.ppermute(value, axis, [(i, i ^ bit) for i in range(peers)])]
    ppermute x13, starting transfers between devices: 48.3 us -> 43.6 us  [chain_sums(): outer[r] = lax.ppermute(value, 'dp', outer_pairs)]
    unnamed x40 -> x36, local copies, waits for them, and re-layouts: 7.82 us -> 10.7 us
    pallas_call x1, Pallas kernels: 1.69 us -> 0.14 us  [edge_rows(): pl.pallas_call(edge_kernel, out_shape=jax.ShapeDtypeStruct((8, width), F3...]
    pallas_call x6 -> x7, Pallas kernels: 26.6 us -> 27.9 us  [call(): pl.pallas_call(kernel, out_shape=out, in_specs=[pl.BlockSpec(memory_space...]
    ppermute x16 -> x17, starting transfers between devices: 15.3 us -> 16.3 us  [swap(): return lax.ppermute(value, axis, [(i, i ^ bit) for i in range(peers)])]
  transfers between devices with their start and end apart: 39 -> 40, of which waited for: 10 -> 9; matrix products, arithmetic and copies ran while one was open for 5% -> 6% of each run, Pallas kernels for 13% -> 15%
where the time goes in v5:
time: 139 us; the launch traced here: 138 us
  starting transfers between devices  66.9 us (48%)
  Pallas kernels  28 us (20%)
  waiting for transfers between devices  20.6 us (15%)
  local copies, waits for them, and re-layouts  12.7 us (9%)
  other arithmetic  8.69 us (6%)
    ppermute x13, starting transfers between devices, chain_sums(): outer[r] = lax.ppermute(value, 'dp', outer_pairs)  43.6 us
    pallas_call x7, Pallas kernels, call(): pl.pallas_call(kernel, out_shape=out, in_specs=[pl.BlockSpec(memory_space...  27.9 us
    ppermute x13, waiting for transfers between devices, chain_sums(): outer[r] = lax.ppermute(value, 'dp', outer_pairs)  16.8 us
    ppermute x17, starting transfers between devices, swap(): return lax.ppermute(value, axis, [(i, i ^ bit) for i in range(peers)])  16.3 us
    unnamed x36, local copies, waits for them, and re-layouts  10.7 us
    ppermute x10, starting transfers between devices, chain_sums(): middle[r - 1] = lax.ppermute(last, 'dp', middle_pairs)  6.98 us
    convert_element_type x23, other arithmetic, added(): return (a.astype(F32) + b.astype(F32)).astype(BF16)  4.52 us
    ppermute x17, waiting for transfers between devices, swap(): return lax.ppermute(value, axis, [(i, i ^ bit) for i in range(peers)])  3.7 us
  transfers between devices with their start and end apart: 40, of which 9 were waited for; matrix products, arithmetic and copies ran while one was open for 6% of the time, Pallas kernels for 15%

profile of v5, /device:TPU:0, one launch (start us, length us, event | category | flops | bytes accessed | tf_op | source)
XLA Modules:
  0.0 138.2 jit_solution(7671843773380370285)
XLA Ops:
  1.1 2.6 %collective-permute-start = (bf16[320,1024]{1,0:T(8,128)(2,1)}, bf16[320,1024]{1,0:T(8,128)(2,1)S(1)}, u32[]{:S(2)}, u32[]{:S(2)}) collective-permute-start(bf16[320,1024]{1,0:T(8,128)(2,1)} %bitcast.28), channel_id=1, source_target_pairs={{0,8},{4,12},{8,0},{12,4},{1,9},{5,13},{9,1},{13,5},{2,10},{6,14},... | collective-permute-start | bytes 1966088 | tf_op jit(solution)/shard_map/ppermute | solution.py:26
  3.7 1.1 copy-done
  5.0 1.6 %collective-permute-start.2 = (f32[8,384]{1,0:T(8,128)S(1)}, f32[8,384]{1,0:T(8,128)S(1)}, u32[]{:S(2)}, u32[]{:S(2)}) collective-permute-start(f32[8,384]{1,0:T(8,128)S(1)} %shard_map.68), channel_id=1, source_target_pairs={{0,16},{16,0},{1,17},{17,1},{2,18},{18,2},{3,19},{19,3},{4,20},{20... | collective-permute-start | bytes 36872 | tf_op jit(solution)/shard_map/ppermute | solution.py:26
  7.3 1.4 %collective-permute-done.2 = f32[8,384]{1,0:T(8,128)S(1)} collective-permute-done((f32[8,384]{1,0:T(8,128)S(1)}, f32[8,384]{1,0:T(8,128)S(1)}, u32[]{:S(2)}, u32[]{:S(2)}) %collective-permute-start.2) | collective-permute-done | bytes 12320 | tf_op jit(solution)/shard_map/ppermute | solution.py:26
  9.0 1.8 %collective-permute-start.5 = (f32[8,384]{1,0:T(8,128)S(1)}, f32[8,384]{1,0:T(8,128)S(1)}, u32[]{:S(2)}, u32[]{:S(2)}) collective-permute-start(f32[8,384]{1,0:T(8,128)S(1)} %maximum_maximum_fusion.refs_2_.refs_4_), channel_id=1, source_target_pairs={{0,12},{4,8},{8,4},{12,0},{1,13},{5,9},{9,5},{13,1},{2,14},{6,10},... | collective-permute-start | bytes 36872 | tf_op jit(solution)/shard_map/ppermute | solution.py:26
  10.8 1.1 copy-done.1
  11.9 2.4 %copy-done.3 = bf16[5,1280,384]{2,1,0:T(8,128)(2,1)S(1)} copy-done((bf16[5,1280,384]{2,1,0:T(8,128)(2,1)S(1)}, bf16[5,1280,384]{2,1,0:T(8,128)(2,1)}, u32[]{:S(2)}) %copy-start.3) | copy-done | bytes 4915224
  14.3 4.3 %shard_map.69 = (f32[512,384]{1,0:T(8,128)S(1)}, f32[512,384]{1,0:T(8,128)S(1)}) custom-call(s32[2]{0:T(128)S(1)} %pad_add_fusion.idx_ref, bf16[320,1024]{1,0:T(8,128)(2,1)S(1)} %bitcast.31, bf16[320,1024]{1,0:T(8,128)(2,1)S(1)} %collective-permute-done.1.refs_1_.refs_2_, f32[8,384]{1,0:T(8,128)S(1)} %maximum_maximum_fusion.refs_2_.refs_4_, ...), custom_call_target="tpu_custom_call" | custom-call | tf_op jit(solution)/shard_map/pallas_call | solution.py:206
  18.6 1.1 collective-permute-done.4.refs_5_
  20.6 1.1 collective-permute-done.6.refs_3_
  21.8 1.3 copy-done.6
  23.1 6.6 %shard_map.70 = (bf16[512,384]{1,0:T(8,128)(2,1)}, f32[1040,384]{1,0:T(8,128)S(1)}, bf16[320,384]{1,0:T(8,128)(2,1)S(1)}) custom-call(s32[2]{0:T(128)S(1)} %pad_add_fusion.idx_ref, bf16[320,1024]{1,0:T(8,128)(2,1)S(1)} %bitcast.32, bf16[320,1024]{1,0:T(8,128)(2,1)S(1)} %copy-done.6, bf16[320,1024]{1,0:T(8,128)(2,1)S(1)} %collective-permute-done.1.refs_1_.refs_2_, ...), custom_call_target="tpu_custom_call" | custom-call | tf_op jit(solution)/shard_map/pallas_call | solution.py:206
  29.7 1.7 %collective-permute-start.8 = (bf16[320,384]{1,0:T(8,128)(2,1)S(1)}, bf16[320,384]{1,0:T(8,128)(2,1)S(1)}, u32[]{:S(2)}, u32[]{:S(2)}) collective-permute-start(bf16[320,384]{1,0:T(8,128)(2,1)S(1)} %get-tuple-element.72), channel_id=1, source_target_pairs={{0,16},{16,0},{1,17},{17,1},{2,18},{18,2},{3,19},{19,3},{4,20},{20... | collective-permute-start | bytes 737288 | tf_op jit(solution)/shard_map/ppermute | solution.py:26
  31.5 3.4 %shard_map.71 = (bf16[320,384]{1,0:T(8,128)(2,1)S(1)}, bf16[320,384]{1,0:T(8,128)(2,1)S(1)}, bf16[320,384]{1,0:T(8,128)(2,1)}) custom-call(s32[2]{0:T(128)S(1)} %pad_add_fusion.idx_ref, bf16[320,1024]{1,0:T(8,128)(2,1)S(1)} %bitcast.33, bf16[320,1024]{1,0:T(8,128)(2,1)S(1)} %copy-done.6, bf16[320,1024]{1,0:T(8,128)(2,1)S(1)} %collective-permute-done.1.refs_1_.refs_2_, ...), custom_call_target="tpu_custom_call" | custom-call | tf_op jit(solution)/shard_map/pallas_call | solution.py:206
  35.6 1.5 %collective-permute-start.19 = (bf16[512,384]{1,0:T(8,128)(2,1)}, bf16[512,384]{1,0:T(8,128)(2,1)}, u32[]{:S(2)}, u32[]{:S(2)}) collective-permute-start(bf16[512,384]{1,0:T(8,128)(2,1)} %get-tuple-element.92.refs_0_), channel_id=1, source_target_pairs={{0,8},{4,12},{8,0},{12,4},{1,9},{5,13},{9,1},{13,5},{2,10},{6,14},... | collective-permute-start | bytes 1179656 | tf_op jit(solution)/shard_map/ppermute | solution.py:26
  37.1 4.4 %shard_map.73 = (bf16[320,384]{1,0:T(8,128)(2,1)S(1)}, bf16[320,384]{1,0:T(8,128)(2,1)S(1)}, bf16[640,384]{1,0:T(8,128)(2,1)}, bf16[320,384]{1,0:T(8,128)(2,1)S(...) custom-call(s32[2]{0:T(128)S(1)} %pad_add_fusion.idx_ref, bf16[320,1024]{1,0:T(8,128)(2,1)S(1)} %bitcast.34, ...), custom_call_target="tpu_custom_call" | custom-call | tf_op jit(solution)/shard_map/pallas_call | solution.py:206
  42.9 1.3 collective-permute-start.10
  45.0 1.6 %collective-permute-start.11 = (bf16[320,384]{1,0:T(8,128)(2,1)}, bf16[320,384]{1,0:T(8,128)(2,1)}, u32[]{:S(2)}, u32[]{:S(2)}) collective-permute-start(bf16[320,384]{1,0:T(8,128)(2,1)} %add_convert_fusion.29), channel_id=1, source_target_pairs={{0,1},{1,0},{2,3},{3,2},{4,5},{5,4},{6,7},{7,6},{8,9},{9,8},{10,11... | collective-permute-start | bytes 737288 | tf_op jit(solution)/shard_map/ppermute | solution.py:277
  46.6 1.1 add_convert_fusion.28
  48.9 1.1 copy-done.7
  50.0 1.1 copy-done.9
  51.1 2.5 %shard_map.72 = (bf16[320,384]{1,0:T(8,128)(2,1)S(1)}, bf16[320,384]{1,0:T(8,128)(2,1)S(1)}, bf16[320,384]{1,0:T(8,128)(2,1)S(1)}, bf16[320,384]{1,0:T(8,128)(2,1)S(1)}) custom-call(s32[2]{0:T(128)S(1)} %pad_add_fusion.idx_ref, bf16[320,1024]{1,0:T(8,128)(2,1)S(1)} %bitcast.35, bf16[320,1024]{1,0:T(8,128)(2,1)S(1)} %copy-done.7, ...), custom_call_target="tpu_custom_call" | custom-call | tf_op jit(solution)/shard_map/pallas_call | solution.py:206
  53.7 2.5 %shard_map.74 = (bf16[320,384]{1,0:T(8,128)(2,1)S(1)}, bf16[320,384]{1,0:T(8,128)(2,1)S(1)}, bf16[640,384]{1,0:T(8,128)(2,1)S(1)}) custom-call(s32[2]{0:T(128)S(1)} %pad_add_fusion.idx_ref, bf16[320,1024]{1,0:T(8,128)(2,1)S(1)} %bitcast.36, bf16[320,1024]{1,0:T(8,128)(2,1)S(1)} %copy-done.7, bf16[320,1024]{1,0:T(8,128)(2,1)S(1)} %collective-permute-done.1.refs_1_.refs_2_, ...), custom_call_target="tpu_custom_call" | custom-call | tf_op jit(solution)/shard_map/pallas_call | solution.py:206
  56.2 1.2 add_convert_fusion.27
  58.7 1.1 fusion.7
  59.9 4.4 %collective-permute-start.12 = (bf16[320,384]{1,0:T(8,128)(2,1)S(1)}, bf16[320,384]{1,0:T(8,128)(2,1)S(1)}, u32[]{:S(2)}, u32[]{:S(2)}) collective-permute-start(bf16[320,384]{1,0:T(8,128)(2,1)S(1)} %add_convert_fusion.26), channel_id=1, source_target_pairs={{0,1},{1,0},{2,3},{3,2},{4,5},{5,4},{6,7},{7,6},{8,9},{9,8},{10,11... | collective-permute-start | bytes 737288 | tf_op jit(solution)/shard_map/ppermute | solution.py:277
  65.3 5.2 %collective-permute-done.12 = bf16[320,384]{1,0:T(8,128)(2,1)S(1)} collective-permute-done((bf16[320,384]{1,0:T(8,128)(2,1)S(1)}, bf16[320,384]{1,0:T(8,128)(2,1)S(1)}, u32[]{:S(2)}, u32[]{:S(2)}) %collective-permute-start.12) | collective-permute-done | bytes 245792 | tf_op jit(solution)/shard_map/ppermute | solution.py:277
  70.5 1.7 %collective-permute-start.16 = (bf16[320,384]{1,0:T(8,128)(2,1)S(1)}, bf16[320,384]{1,0:T(8,128)(2,1)S(1)}, u32[]{:S(2)}, u32[]{:S(2)}) collective-permute-start(bf16[320,384]{1,0:T(8,128)(2,1)S(1)} %get-tuple-element.130), channel_id=1, source_target_pairs={{0,1},{1,0},{2,3},{3,2},{4,5},{5,4},{6,7},{7,6},{8,9},{9,8},{10,11... | collective-permute-start | bytes 737288 | tf_op jit(solution)/shard_map/ppermute | solution.py:277
  73.1 1.4 %collective-permute-start.22 = (bf16[640,384]{1,0:T(8,128)(2,1)S(1)}, bf16[640,384]{1,0:T(8,128)(2,1)S(1)}, u32[]{:S(2)}, u32[]{:S(2)}) collective-permute-start(bf16[640,384]{1,0:T(8,128)(2,1)S(1)} %get-tuple-element.102), channel_id=1, source_target_pairs={{0,16},{16,0},{1,17},{17,1},{2,18},{18,2},{3,19},{19,3},{4,20},{20... | collective-permute-start | bytes 1474568 | tf_op jit(solution)/shard_map/ppermute | solution.py:26
  74.7 5.7 %collective-permute-start.24 = (bf16[320,384]{1,0:T(8,128)(2,1)S(1)}, bf16[320,384]{1,0:T(8,128)(2,1)S(1)}, u32[]{:S(2)}, u32[]{:S(2)}) collective-permute-start(bf16[320,384]{1,0:T(8,128)(2,1)S(1)} %broadcast_select_fusion.15), channel_id=1, source_target_pairs={{0,1},{1,0},{2,3},{3,2},{4,5},{5,4},{6,7},{7,6},{8,9},{9,8},{10,11... | collective-permute-start | bytes 737288 | tf_op jit(solution)/shard_map/ppermute | solution.py:277
  81.3 0.9 collective-permute-start.21
  82.2 1.2 collective-permute-start.30
  83.4 2.5 %collective-permute-done.24 = bf16[320,384]{1,0:T(8,128)(2,1)S(1)} collective-permute-done((bf16[320,384]{1,0:T(8,128)(2,1)S(1)}, bf16[320,384]{1,0:T(8,128)(2,1)S(1)}, u32[]{:S(2)}, u32[]{:S(2)}) %collective-permute-start.24) | collective-permute-done | bytes 245792 | tf_op jit(solution)/shard_map/ppermute | solution.py:277
  85.9 2.5 %collective-permute-start.27 = (bf16[320,384]{1,0:T(8,128)(2,1)S(1)}, bf16[320,384]{1,0:T(8,128)(2,1)S(1)}, u32[]{:S(2)}, u32[]{:S(2)}) collective-permute-start(bf16[320,384]{1,0:T(8,128)(2,1)S(1)} %get-tuple-element.128), channel_id=1, source_target_pairs={{0,1},{1,0},{2,3},{3,2},{4,5},{5,4},{6,7},{7,6},{8,9},{9,8},{10,11... | collective-permute-start | bytes 737288 | tf_op jit(solution)/shard_map/ppermute | solution.py:277
  89.5 3.7 %collective-permute-start.25 = (bf16[320,384]{1,0:T(8,128)(2,1)S(1)}, bf16[320,384]{1,0:T(8,128)(2,1)S(1)}, u32[]{:S(2)}, u32[]{:S(2)}) collective-permute-start(bf16[320,384]{1,0:T(8,128)(2,1)S(1)} %broadcast_select_fusion.13), channel_id=1, source_target_pairs={{0,1},{1,0},{2,3},{3,2},{4,5},{5,4},{6,7},{7,6},{8,9},{9,8},{10,11... | collective-permute-start | bytes 737288 | tf_op jit(solution)/shard_map/ppermute | solution.py:277
  93.3 1.1 collective-permute-done.27
  95.4 5.0 %collective-permute-start.29 = (bf16[320,384]{1,0:T(8,128)(2,1)S(1)}, bf16[320,384]{1,0:T(8,128)(2,1)S(1)}, u32[]{:S(2)}, u32[]{:S(2)}) collective-permute-start(bf16[320,384]{1,0:T(8,128)(2,1)S(1)} %broadcast_select_fusion.12), channel_id=1, source_target_pairs={{0,1},{1,0},{2,3},{3,2},{4,5},{5,4},{6,7},{7,6},{8,9},{9,8},{10,11... | collective-permute-start | bytes 737288 | tf_op jit(solution)/shard_map/ppermute | solution.py:277
  101.4 6.4 %collective-permute-start.34 = (bf16[320,384]{1,0:T(8,128)(2,1)S(1)}, bf16[320,384]{1,0:T(8,128)(2,1)S(1)}, u32[]{:S(2)}, u32[]{:S(2)}) collective-permute-start(bf16[320,384]{1,0:T(8,128)(2,1)S(1)} %broadcast_select_fusion.11), channel_id=1, source_target_pairs={{0,1},{1,0},{2,3},{3,2},{4,5},{5,4},{6,7},{7,6},{8,9},{9,8},{10,11... | collective-permute-start | bytes 737288 | tf_op jit(solution)/shard_map/ppermute | solution.py:277
  108.1 0.9 collective-permute-start.33
  109.2 3.9 %collective-permute-start.32 = (bf16[320,384]{1,0:T(8,128)(2,1)S(1)}, bf16[320,384]{1,0:T(8,128)(2,1)S(1)}, u32[]{:S(2)}, u32[]{:S(2)}) collective-permute-start(bf16[320,384]{1,0:T(8,128)(2,1)S(1)} %broadcast_select_fusion.10), channel_id=1, source_target_pairs={{0,1},{1,0},{2,3},{3,2},{4,5},{5,4},{6,7},{7,6},{8,9},{9,8},{10,11... | collective-permute-start | bytes 737288 | tf_op jit(solution)/shard_map/ppermute | solution.py:277
  113.1 1.2 collective-permute-done.34
  115.3 3.0 %collective-permute-start.35 = (bf16[320,384]{1,0:T(8,128)(2,1)S(1)}, bf16[320,384]{1,0:T(8,128)(2,1)S(1)}, u32[]{:S(2)}, u32[]{:S(2)}) collective-permute-start(bf16[320,384]{1,0:T(8,128)(2,1)S(1)} %add_convert_fusion.3), channel_id=1, source_target_pairs={{0,1},{1,0},{2,3},{3,2},{4,5},{5,4},{6,7},{7,6},{8,9},{9,8},{10,11... | collective-permute-start | bytes 737288 | tf_op jit(solution)/shard_map/ppermute | solution.py:277
  118.4 1.5 %collective-permute-done.32 = bf16[320,384]{1,0:T(8,128)(2,1)S(1)} collective-permute-done((bf16[320,384]{1,0:T(8,128)(2,1)S(1)}, bf16[320,384]{1,0:T(8,128)(2,1)S(1)}, u32[]{:S(2)}, u32[]{:S(2)}) %collective-permute-start.32) | collective-permute-done | bytes 245792 | tf_op jit(solution)/shard_map/ppermute | solution.py:277
  120.8 4.2 %collective-permute-start.37 = (bf16[320,384]{1,0:T(8,128)(2,1)S(1)}, bf16[320,384]{1,0:T(8,128)(2,1)S(1)}, u32[]{:S(2)}, u32[]{:S(2)}) collective-permute-start(bf16[320,384]{1,0:T(8,128)(2,1)S(1)} %add_convert_fusion.1), channel_id=1, source_target_pairs={{0,1},{1,0},{2,3},{3,2},{4,5},{5,4},{6,7},{7,6},{8,9},{9,8},{10,11... | collective-permute-start | bytes 737288 | tf_op jit(solution)/shard_map/ppermute | solution.py:277
  124.9 4.1 %shard_map.75 = bf16[512,640]{1,0:T(8,128)(2,1)} custom-call(s32[2]{0:T(128)S(1)} %pad_add_fusion.idx_ref, bf16[512,384]{1,0:T(8,128)(2,1)} %get-tuple-element.92.refs_0_, bf16[512,384]{1,0:T(8,128)(2,1)} %collective-permute-done.19.refs_1_, bf16[512,384]{1,0:T(8,128)(2,1)S(1)} %collective-permute-done.18.refs_2_, ...), custom_call_target="tpu_custom_call" | custom-call | tf_op jit(solution)/shard_map/pallas_call | solution.py:206
  129.2 0.9 collective-permute-start.39
  130.2 5.2 %collective-permute-done.39 = bf16[320,384]{1,0:T(8,128)(2,1)S(1)} collective-permute-done((bf16[320,384]{1,0:T(8,128)(2,1)S(1)}, bf16[320,384]{1,0:T(8,128)(2,1)S(1)}, u32[]{:S(2)}, u32[]{:S(2)}) %collective-permute-start.39) | collective-permute-done | bytes 245792 | tf_op jit(solution)/shard_map/ppermute | solution.py:277
  135.6 2.6 %stack.44 = f32[640,5,384]{2,0,1:T(8,128)} convert(bf16[640,5,384]{2,0,1:T(8,128)(2,1)S(1)} %fusion.4) | non-fusion elementwise | flops 1228800 | bytes 7372800 | tf_op jit(solution)/shard_map/stack | solution.py:426
  (130 shorter events, 16.4 us)
Async XLA Ops:
  0.6 10.2 %collective-permute-start.1 = (bf16[320,1024]{1,0:T(8,128)(2,1)}, bf16[320,1024]{1,0:T(8,128)(2,1)S(1)}, u32[]{:S(2)}, u32[]{:S(2)}) collective-permute-start(bf16[320,1024]{1,0:T(8,128)(2,1)} %bitcast.27), channel_id=1, source_target_pairs={{0,4},{4,0},{8,12},{12,8},{1,5},{5,1},{9,13},{13,9},{2,6},{6,2},{1... | collective-permute-start | bytes 1966088 | tf_op jit(solution)/shard_map/ppermute | solution.py:26
  1.1 18.5 %collective-permute-start = (bf16[320,1024]{1,0:T(8,128)(2,1)}, bf16[320,1024]{1,0:T(8,128)(2,1)S(1)}, u32[]{:S(2)}, u32[]{:S(2)}) collective-permute-start(bf16[320,1024]{1,0:T(8,128)(2,1)} %bitcast.28), channel_id=1, source_target_pairs={{0,8},{4,12},{8,0},{12,4},{1,9},{5,13},{9,1},{13,5},{2,10},{6,14},... | collective-permute-start | bytes 1966088 | tf_op jit(solution)/shard_map/ppermute | solution.py:26
  5.0 3.8 %collective-permute-start.2 = (f32[8,384]{1,0:T(8,128)S(1)}, f32[8,384]{1,0:T(8,128)S(1)}, u32[]{:S(2)}, u32[]{:S(2)}) collective-permute-start(f32[8,384]{1,0:T(8,128)S(1)} %shard_map.68), channel_id=1, source_target_pairs={{0,16},{16,0},{1,17},{17,1},{2,18},{18,2},{3,19},{19,3},{4,20},{20... | collective-permute-start | bytes 36872 | tf_op jit(solution)/shard_map/ppermute | solution.py:26
  8.9 2.0 %collective-permute-start.3 = (f32[8,384]{1,0:T(8,128)S(1)}, f32[8,384]{1,0:T(8,128)S(1)}, u32[]{:S(2)}, u32[]{:S(2)}) collective-permute-start(f32[8,384]{1,0:T(8,128)S(1)} %maximum_maximum_fusion.refs_2_.refs_4_), channel_id=1, source_target_pairs={{0,4},{4,0},{8,12},{12,8},{1,5},{5,1},{9,13},{13,9},{2,6},{6,2},{1... | collective-permute-start | bytes 36872 | tf_op jit(solution)/shard_map/ppermute | solution.py:26
  8.9 10.8 %collective-permute-start.4 = (f32[8,384]{1,0:T(8,128)S(1)}, f32[8,384]{1,0:T(8,128)S(1)}, u32[]{:S(2)}, u32[]{:S(2)}) collective-permute-start(f32[8,384]{1,0:T(8,128)S(1)} %maximum_maximum_fusion.refs_2_.refs_4_), channel_id=1, source_target_pairs={{0,8},{4,12},{8,0},{12,4},{1,9},{5,13},{9,1},{13,5},{2,10},{6,14},... | collective-permute-start | bytes 36872 | tf_op jit(solution)/shard_map/ppermute | solution.py:26
  9.0 10.7 %collective-permute-start.5 = (f32[8,384]{1,0:T(8,128)S(1)}, f32[8,384]{1,0:T(8,128)S(1)}, u32[]{:S(2)}, u32[]{:S(2)}) collective-permute-start(f32[8,384]{1,0:T(8,128)S(1)} %maximum_maximum_fusion.refs_2_.refs_4_), channel_id=1, source_target_pairs={{0,12},{4,8},{8,4},{12,0},{1,13},{5,9},{9,5},{13,1},{2,14},{6,10},... | collective-permute-start | bytes 36872 | tf_op jit(solution)/shard_map/ppermute | solution.py:26
  11.9 2.4 %copy-start.3 = (bf16[5,1280,384]{2,1,0:T(8,128)(2,1)S(1)}, bf16[5,1280,384]{2,1,0:T(8,128)(2,1)}, u32[]{:S(2)}) copy-start(bf16[5,1280,384]{2,1,0:T(8,128)(2,1)} %refs_8_.2) | copy-start | bytes 14745604
  14.3 7.5 %copy-start.2 = (bf16[1,1024,320]{1,2,0:T(8,128)(2,1)S(1)}, bf16[1,1024,320]{1,2,0:T(8,128)(2,1)}, u32[]{:S(2)}) copy-start(bf16[1,1024,320]{1,2,0:T(8,128)(2,1)} %param.5) | copy-start | bytes 1966084
  14.3 7.5 %copy-start.4 = (bf16[5,1280,384]{2,1,0:T(8,128)(2,1)S(1)}, bf16[5,1280,384]{2,1,0:T(8,128)(2,1)}, u32[]{:S(2)}) copy-start(bf16[5,1280,384]{2,1,0:T(8,128)(2,1)} %refs_8_.2) | copy-start | bytes 14745604
  14.3 7.5 %copy-start.11 = (bf16[1,512,384]{2,1,0:T(8,128)(2,1)S(1)}, bf16[1,512,384]{2,1,0:T(8,128)(2,1)}, u32[]{:S(2)}) copy-start(bf16[1,512,384]{2,1,0:T(8,128)(2,1)} %param.9) | copy-start | bytes 1179652
  19.7 2.1 %collective-permute-start.6 = (bf16[320,1024]{1,0:T(8,128)(2,1)S(1)}, bf16[320,1024]{1,0:T(8,128)(2,1)S(1)}, u32[]{:S(2)}, u32[]{:S(2)}) collective-permute-start(bf16[320,1024]{1,0:T(8,128)(2,1)S(1)} %collective-permute-done.refs_1_), channel_id=1, source_target_pairs={{0,4},{4,0},{8,12},{12,8},{1,5},{5,1},{9,13},{13,9},{2,6},{6,2},{1... | collective-permute-start | bytes 1966088 | tf_op jit(solution)/shard_map/ppermute | solution.py:26
  21.8 15.3 %copy-start.8 = (bf16[320,1024]{1,0:T(8,128)(2,1)}, bf16[320,1024]{1,0:T(8,128)(2,1)S(1)}, u32[]{:S(2)}) copy-start(bf16[320,1024]{1,0:T(8,128)(2,1)S(1)} %collective-permute-done.6.refs_3_) | copy-start | bytes 1966084
  29.7 14.5 %collective-permute-start.8 = (bf16[320,384]{1,0:T(8,128)(2,1)S(1)}, bf16[320,384]{1,0:T(8,128)(2,1)S(1)}, u32[]{:S(2)}, u32[]{:S(2)}) collective-permute-start(bf16[320,384]{1,0:T(8,128)(2,1)S(1)} %get-tuple-element.72), channel_id=1, source_target_pairs={{0,16},{16,0},{1,17},{17,1},{2,18},{18,2},{3,19},{19,3},{4,20},{20... | collective-permute-start | bytes 737288 | tf_op jit(solution)/shard_map/ppermute | solution.py:26
  34.9 11.7 %collective-permute-start.7 = (bf16[320,384]{1,0:T(8,128)(2,1)}, bf16[320,384]{1,0:T(8,128)(2,1)}, u32[]{:S(2)}, u32[]{:S(2)}) collective-permute-start(bf16[320,384]{1,0:T(8,128)(2,1)} %get-tuple-element.70), channel_id=1, source_target_pairs={{0,16},{16,0},{1,17},{17,1},{2,18},{18,2},{3,19},{19,3},{4,20},{20... | collective-permute-start | bytes 737288 | tf_op jit(solution)/shard_map/ppermute | solution.py:26
  35.6 18.1 %collective-permute-start.19 = (bf16[512,384]{1,0:T(8,128)(2,1)}, bf16[512,384]{1,0:T(8,128)(2,1)}, u32[]{:S(2)}, u32[]{:S(2)}) collective-permute-start(bf16[512,384]{1,0:T(8,128)(2,1)} %get-tuple-element.92.refs_0_), channel_id=1, source_target_pairs={{0,8},{4,12},{8,0},{12,4},{1,9},{5,13},{9,1},{13,5},{2,10},{6,14},... | collective-permute-start | bytes 1179656 | tf_op jit(solution)/shard_map/ppermute | solution.py:26
  42.9 15.3 %collective-permute-start.10 = (bf16[640,384]{1,0:T(8,128)(2,1)}, bf16[640,384]{1,0:T(8,128)(2,1)}, u32[]{:S(2)}, u32[]{:S(2)}) collective-permute-start(bf16[640,384]{1,0:T(8,128)(2,1)} %get-tuple-element.81), channel_id=1, source_target_pairs={{0,16},{16,0},{1,17},{17,1},{2,18},{18,2},{3,19},{19,3},{4,20},{20... | collective-permute-start | bytes 1474568 | tf_op jit(solution)/shard_map/ppermute | solution.py:26
  45.0 11.2 %collective-permute-start.11 = (bf16[320,384]{1,0:T(8,128)(2,1)}, bf16[320,384]{1,0:T(8,128)(2,1)}, u32[]{:S(2)}, u32[]{:S(2)}) collective-permute-start(bf16[320,384]{1,0:T(8,128)(2,1)} %add_convert_fusion.29), channel_id=1, source_target_pairs={{0,1},{1,0},{2,3},{3,2},{4,5},{5,4},{6,7},{7,6},{8,9},{9,8},{10,11... | collective-permute-start | bytes 737288 | tf_op jit(solution)/shard_map/ppermute | solution.py:277
  47.7 25.4 %collective-permute-start.9 = (bf16[640,384]{1,0:T(8,128)(2,1)}, bf16[640,384]{1,0:T(8,128)(2,1)S(1)}, u32[]{:S(2)}, u32[]{:S(2)}) collective-permute-start(bf16[640,384]{1,0:T(8,128)(2,1)} %copy-done.17), channel_id=1, source_target_pairs={{0,16},{16,0},{1,17},{17,1},{2,18},{18,2},{3,19},{19,3},{4,20},{20... | collective-permute-start | bytes 1474568 | tf_op jit(solution)/shard_map/ppermute | solution.py:26
  48.5 11.4 %collective-permute-start.14 = (bf16[320,384]{1,0:T(8,128)(2,1)S(1)}, bf16[320,384]{1,0:T(8,128)(2,1)S(1)}, u32[]{:S(2)}, u32[]{:S(2)}) collective-permute-start(bf16[320,384]{1,0:T(8,128)(2,1)S(1)} %add_convert_fusion.28), channel_id=1, source_target_pairs={{0,1},{1,0},{2,3},{3,2},{4,5},{5,4},{6,7},{7,6},{8,9},{9,8},{10,11... | collective-permute-start | bytes 737288 | tf_op jit(solution)/shard_map/ppermute | solution.py:277
  53.7 6.1 %copy-start.15 = (bf16[320,384]{1,0:T(8,128)(2,1)S(1)}, bf16[320,384]{1,0:T(8,128)(2,1)}, u32[]{:S(2)}) copy-start(bf16[320,384]{1,0:T(8,128)(2,1)} %copy-done.14) | copy-start | bytes 737284
  56.2 8.9 %copy-start.13 = (bf16[320,384]{1,0:T(8,128)(2,1)S(1)}, bf16[320,384]{1,0:T(8,128)(2,1)}, u32[]{:S(2)}) copy-start(bf16[320,384]{1,0:T(8,128)(2,1)} %copy-done.12) | copy-start | bytes 737284
  57.4 7.0 %collective-permute-start.13 = (bf16[320,384]{1,0:T(8,128)(2,1)S(1)}, bf16[320,384]{1,0:T(8,128)(2,1)S(1)}, u32[]{:S(2)}, u32[]{:S(2)}) collective-permute-start(bf16[320,384]{1,0:T(8,128)(2,1)S(1)} %add_convert_fusion.27), channel_id=1, source_target_pairs={{0,0},{1,2},{2,1},{3,3},{4,4},{5,6},{6,5},{7,7},{8,8},{9,10},{10,9... | collective-permute-start | bytes 737288 | tf_op jit(solution)/shard_map/ppermute | solution.py:283
  58.1 16.5 %collective-permute-start.20 = (bf16[512,384]{1,0:T(8,128)(2,1)}, bf16[512,384]{1,0:T(8,128)(2,1)S(1)}, u32[]{:S(2)}, u32[]{:S(2)}) collective-permute-start(bf16[512,384]{1,0:T(8,128)(2,1)} %collective-permute-done.19.refs_1_), channel_id=1, source_target_pairs={{0,4},{4,0},{8,12},{12,8},{1,5},{5,1},{9,13},{13,9},{2,6},{6,2},{1... | collective-permute-start | bytes 1179656 | tf_op jit(solution)/shard_map/ppermute | solution.py:26
  58.2 16.4 %collective-permute-start.18 = (bf16[512,384]{1,0:T(8,128)(2,1)}, bf16[512,384]{1,0:T(8,128)(2,1)S(1)}, u32[]{:S(2)}, u32[]{:S(2)}) collective-permute-start(bf16[512,384]{1,0:T(8,128)(2,1)} %get-tuple-element.92.refs_0_), channel_id=1, source_target_pairs={{0,4},{4,0},{8,12},{12,8},{1,5},{5,1},{9,13},{13,9},{2,6},{6,2},{1... | collective-permute-start | bytes 1179656 | tf_op jit(solution)/shard_map/ppermute | solution.py:26
  59.9 10.6 %collective-permute-start.12 = (bf16[320,384]{1,0:T(8,128)(2,1)S(1)}, bf16[320,384]{1,0:T(8,128)(2,1)S(1)}, u32[]{:S(2)}, u32[]{:S(2)}) collective-permute-start(bf16[320,384]{1,0:T(8,128)(2,1)S(1)} %add_convert_fusion.26), channel_id=1, source_target_pairs={{0,1},{1,0},{2,3},{3,2},{4,5},{5,4},{6,7},{7,6},{8,9},{9,8},{10,11... | collective-permute-start | bytes 737288 | tf_op jit(solution)/shard_map/ppermute | solution.py:277
  64.4 7.9 %collective-permute-start.17 = (bf16[320,384]{1,0:T(8,128)(2,1)S(1)}, bf16[320,384]{1,0:T(8,128)(2,1)S(1)}, u32[]{:S(2)}, u32[]{:S(2)}) collective-permute-start(bf16[320,384]{1,0:T(8,128)(2,1)S(1)} %add_convert_fusion.25), channel_id=1, source_target_pairs={{0,0},{1,2},{2,1},{3,3},{4,4},{5,6},{6,5},{7,7},{8,8},{9,10},{10,9... | collective-permute-start | bytes 737288 | tf_op jit(solution)/shard_map/ppermute | solution.py:283
  70.5 9.8 %collective-permute-start.16 = (bf16[320,384]{1,0:T(8,128)(2,1)S(1)}, bf16[320,384]{1,0:T(8,128)(2,1)S(1)}, u32[]{:S(2)}, u32[]{:S(2)}) collective-permute-start(bf16[320,384]{1,0:T(8,128)(2,1)S(1)} %get-tuple-element.130), channel_id=1, source_target_pairs={{0,1},{1,0},{2,3},{3,2},{4,5},{5,4},{6,7},{7,6},{8,9},{9,8},{10,11... | collective-permute-start | bytes 737288 | tf_op jit(solution)/shard_map/ppermute | solution.py:277
  72.4 8.8 %collective-permute-start.15 = (bf16[320,384]{1,0:T(8,128)(2,1)S(1)}, bf16[320,384]{1,0:T(8,128)(2,1)S(1)}, u32[]{:S(2)}, u32[]{:S(2)}) collective-permute-start(bf16[320,384]{1,0:T(8,128)(2,1)S(1)} %add_convert_fusion.22), channel_id=1, source_target_pairs={{0,0},{1,2},{2,1},{3,3},{4,4},{5,6},{6,5},{7,7},{8,8},{9,10},{10,9... | collective-permute-start | bytes 737288 | tf_op jit(solution)/shard_map/ppermute | solution.py:283
  73.1 16.3 %collective-permute-start.22 = (bf16[640,384]{1,0:T(8,128)(2,1)S(1)}, bf16[640,384]{1,0:T(8,128)(2,1)S(1)}, u32[]{:S(2)}, u32[]{:S(2)}) collective-permute-start(bf16[640,384]{1,0:T(8,128)(2,1)S(1)} %get-tuple-element.102), channel_id=1, source_target_pairs={{0,16},{16,0},{1,17},{17,1},{2,18},{18,2},{3,19},{19,3},{4,20},{20... | collective-permute-start | bytes 1474568 | tf_op jit(solution)/shard_map/ppermute | solution.py:26
  74.7 11.2 %collective-permute-start.24 = (bf16[320,384]{1,0:T(8,128)(2,1)S(1)}, bf16[320,384]{1,0:T(8,128)(2,1)S(1)}, u32[]{:S(2)}, u32[]{:S(2)}) collective-permute-start(bf16[320,384]{1,0:T(8,128)(2,1)S(1)} %broadcast_select_fusion.15), channel_id=1, source_target_pairs={{0,1},{1,0},{2,3},{3,2},{4,5},{5,4},{6,7},{7,6},{8,9},{9,8},{10,11... | collective-permute-start | bytes 737288 | tf_op jit(solution)/shard_map/ppermute | solution.py:277
  80.4 8.2 %collective-permute-start.23 = (bf16[320,384]{1,0:T(8,128)(2,1)S(1)}, bf16[320,384]{1,0:T(8,128)(2,1)S(1)}, u32[]{:S(2)}, u32[]{:S(2)}) collective-permute-start(bf16[320,384]{1,0:T(8,128)(2,1)S(1)} %add_convert_fusion.19), channel_id=1, source_target_pairs={{0,0},{1,2},{2,1},{3,3},{4,4},{5,6},{6,5},{7,7},{8,8},{9,10},{10,9... | collective-permute-start | bytes 737288 | tf_op jit(solution)/shard_map/ppermute | solution.py:283
  81.3 27.7 %collective-permute-start.21 = (bf16[320,384]{1,0:T(8,128)(2,1)S(1)}, bf16[320,384]{1,0:T(8,128)(2,1)S(1)}, u32[]{:S(2)}, u32[]{:S(2)}) collective-permute-start(bf16[320,384]{1,0:T(8,128)(2,1)S(1)} %get-tuple-element.98), channel_id=1, source_target_pairs={{0,16},{16,0},{1,17},{17,1},{2,18},{18,2},{3,19},{19,3},{4,20},{20... | collective-permute-start | bytes 737288 | tf_op jit(solution)/shard_map/ppermute | solution.py:26
  82.2 19.0 %collective-permute-start.30 = (bf16[320,384]{1,0:T(8,128)(2,1)S(1)}, bf16[320,384]{1,0:T(8,128)(2,1)S(1)}, u32[]{:S(2)}, u32[]{:S(2)}) collective-permute-start(bf16[320,384]{1,0:T(8,128)(2,1)S(1)} %get-tuple-element.113), channel_id=1, source_target_pairs={{0,16},{16,0},{1,17},{17,1},{2,18},{18,2},{3,19},{19,3},{4,20},{20... | collective-permute-start | bytes 737288 | tf_op jit(solution)/shard_map/ppermute | solution.py:26
  85.9 8.5 %collective-permute-start.27 = (bf16[320,384]{1,0:T(8,128)(2,1)S(1)}, bf16[320,384]{1,0:T(8,128)(2,1)S(1)}, u32[]{:S(2)}, u32[]{:S(2)}) collective-permute-start(bf16[320,384]{1,0:T(8,128)(2,1)S(1)} %get-tuple-element.128), channel_id=1, source_target_pairs={{0,1},{1,0},{2,3},{3,2},{4,5},{5,4},{6,7},{7,6},{8,9},{9,8},{10,11... | collective-permute-start | bytes 737288 | tf_op jit(solution)/shard_map/ppermute | solution.py:277
  88.6 6.6 %collective-permute-start.26 = (bf16[320,384]{1,0:T(8,128)(2,1)S(1)}, bf16[320,384]{1,0:T(8,128)(2,1)S(1)}, u32[]{:S(2)}, u32[]{:S(2)}) collective-permute-start(bf16[320,384]{1,0:T(8,128)(2,1)S(1)} %add_convert_fusion.16), channel_id=1, source_target_pairs={{0,0},{1,2},{2,1},{3,3},{4,4},{5,6},{6,5},{7,7},{8,8},{9,10},{10,9... | collective-permute-start | bytes 737288 | tf_op jit(solution)/shard_map/ppermute | solution.py:283
  89.5 10.8 %collective-permute-start.25 = (bf16[320,384]{1,0:T(8,128)(2,1)S(1)}, bf16[320,384]{1,0:T(8,128)(2,1)S(1)}, u32[]{:S(2)}, u32[]{:S(2)}) collective-permute-start(bf16[320,384]{1,0:T(8,128)(2,1)S(1)} %broadcast_select_fusion.13), channel_id=1, source_target_pairs={{0,1},{1,0},{2,3},{3,2},{4,5},{5,4},{6,7},{7,6},{8,9},{9,8},{10,11... | collective-permute-start | bytes 737288 | tf_op jit(solution)/shard_map/ppermute | solution.py:277
  94.5 6.7 %collective-permute-start.31 = (bf16[320,384]{1,0:T(8,128)(2,1)S(1)}, bf16[320,384]{1,0:T(8,128)(2,1)S(1)}, u32[]{:S(2)}, u32[]{:S(2)}) collective-permute-start(bf16[320,384]{1,0:T(8,128)(2,1)S(1)} %add_convert_fusion.13), channel_id=1, source_target_pairs={{0,0},{1,2},{2,1},{3,3},{4,4},{5,6},{6,5},{7,7},{8,8},{9,10},{10,9... | collective-permute-start | bytes 737288 | tf_op jit(solution)/shard_map/ppermute | solution.py:283
  95.4 12.5 %collective-permute-start.29 = (bf16[320,384]{1,0:T(8,128)(2,1)S(1)}, bf16[320,384]{1,0:T(8,128)(2,1)S(1)}, u32[]{:S(2)}, u32[]{:S(2)}) collective-permute-start(bf16[320,384]{1,0:T(8,128)(2,1)S(1)} %broadcast_select_fusion.12), channel_id=1, source_target_pairs={{0,1},{1,0},{2,3},{3,2},{4,5},{5,4},{6,7},{7,6},{8,9},{9,8},{10,11... | collective-permute-start | bytes 737288 | tf_op jit(solution)/shard_map/ppermute | solution.py:277
  100.5 8.5 %collective-permute-start.28 = (bf16[320,384]{1,0:T(8,128)(2,1)S(1)}, bf16[320,384]{1,0:T(8,128)(2,1)S(1)}, u32[]{:S(2)}, u32[]{:S(2)}) collective-permute-start(bf16[320,384]{1,0:T(8,128)(2,1)S(1)} %add_convert_fusion.10), channel_id=1, source_target_pairs={{0,0},{1,2},{2,1},{3,3},{4,4},{5,6},{6,5},{7,7},{8,8},{9,10},{10,9... | collective-permute-start | bytes 737288 | tf_op jit(solution)/shard_map/ppermute | solution.py:283
  101.4 12.9 %collective-permute-start.34 = (bf16[320,384]{1,0:T(8,128)(2,1)S(1)}, bf16[320,384]{1,0:T(8,128)(2,1)S(1)}, u32[]{:S(2)}, u32[]{:S(2)}) collective-permute-start(bf16[320,384]{1,0:T(8,128)(2,1)S(1)} %broadcast_select_fusion.11), channel_id=1, source_target_pairs={{0,1},{1,0},{2,3},{3,2},{4,5},{5,4},{6,7},{7,6},{8,9},{9,8},{10,11... | collective-permute-start | bytes 737288 | tf_op jit(solution)/shard_map/ppermute | solution.py:277
  108.1 7.2 %collective-permute-start.33 = (bf16[320,384]{1,0:T(8,128)(2,1)S(1)}, bf16[320,384]{1,0:T(8,128)(2,1)S(1)}, u32[]{:S(2)}, u32[]{:S(2)}) collective-permute-start(bf16[320,384]{1,0:T(8,128)(2,1)S(1)} %add_convert_fusion.7), channel_id=1, source_target_pairs={{0,0},{1,2},{2,1},{3,3},{4,4},{5,6},{6,5},{7,7},{8,8},{9,10},{10,9... | collective-permute-start | bytes 737288 | tf_op jit(solution)/shard_map/ppermute | solution.py:283
  109.2 15.8 %copy-start.10 = (bf16[1536,640]{1,0:T(8,128)(2,1)S(1)}, bf16[1536,640]{1,0:T(8,128)(2,1)}, u32[]{:S(2)}) copy-start(bf16[1536,640]{1,0:T(8,128)(2,1)} %refs_8_.3) | copy-start | bytes 5898244
  109.2 10.7 %collective-permute-start.32 = (bf16[320,384]{1,0:T(8,128)(2,1)S(1)}, bf16[320,384]{1,0:T(8,128)(2,1)S(1)}, u32[]{:S(2)}, u32[]{:S(2)}) collective-permute-start(bf16[320,384]{1,0:T(8,128)(2,1)S(1)} %broadcast_select_fusion.10), channel_id=1, source_target_pairs={{0,1},{1,0},{2,3},{3,2},{4,5},{5,4},{6,7},{7,6},{8,9},{9,8},{10,11... | collective-permute-start | bytes 737288 | tf_op jit(solution)/shard_map/ppermute | solution.py:277
  114.5 6.2 %collective-permute-start.36 = (bf16[320,384]{1,0:T(8,128)(2,1)S(1)}, bf16[320,384]{1,0:T(8,128)(2,1)S(1)}, u32[]{:S(2)}, u32[]{:S(2)}) collective-permute-start(bf16[320,384]{1,0:T(8,128)(2,1)S(1)} %add_convert_fusion.4), channel_id=1, source_target_pairs={{0,0},{1,2},{2,1},{3,3},{4,4},{5,6},{6,5},{7,7},{8,8},{9,10},{10,9... | collective-permute-start | bytes 737288 | tf_op jit(solution)/shard_map/ppermute | solution.py:283
  115.3 13.7 %collective-permute-start.35 = (bf16[320,384]{1,0:T(8,128)(2,1)S(1)}, bf16[320,384]{1,0:T(8,128)(2,1)S(1)}, u32[]{:S(2)}, u32[]{:S(2)}) collective-permute-start(bf16[320,384]{1,0:T(8,128)(2,1)S(1)} %add_convert_fusion.3), channel_id=1, source_target_pairs={{0,1},{1,0},{2,3},{3,2},{4,5},{5,4},{6,7},{7,6},{8,9},{9,8},{10,11... | collective-permute-start | bytes 737288 | tf_op jit(solution)/shard_map/ppermute | solution.py:277
  120.0 9.1 %collective-permute-start.38 = (bf16[320,384]{1,0:T(8,128)(2,1)S(1)}, bf16[320,384]{1,0:T(8,128)(2,1)S(1)}, u32[]{:S(2)}, u32[]{:S(2)}) collective-permute-start(bf16[320,384]{1,0:T(8,128)(2,1)S(1)} %add_convert_fusion.2), channel_id=1, source_target_pairs={{0,0},{1,2},{2,1},{3,3},{4,4},{5,6},{6,5},{7,7},{8,8},{9,10},{10,9... | collective-permute-start | bytes 737288 | tf_op jit(solution)/shard_map/ppermute | solution.py:283
  120.8 9.4 %collective-permute-start.37 = (bf16[320,384]{1,0:T(8,128)(2,1)S(1)}, bf16[320,384]{1,0:T(8,128)(2,1)S(1)}, u32[]{:S(2)}, u32[]{:S(2)}) collective-permute-start(bf16[320,384]{1,0:T(8,128)(2,1)S(1)} %add_convert_fusion.1), channel_id=1, source_target_pairs={{0,1},{1,0},{2,3},{3,2},{4,5},{5,4},{6,7},{7,6},{8,9},{9,8},{10,11... | collective-permute-start | bytes 737288 | tf_op jit(solution)/shard_map/ppermute | solution.py:277
  129.2 6.3 %collective-permute-start.39 = (bf16[320,384]{1,0:T(8,128)(2,1)S(1)}, bf16[320,384]{1,0:T(8,128)(2,1)S(1)}, u32[]{:S(2)}, u32[]{:S(2)}) collective-permute-start(bf16[320,384]{1,0:T(8,128)(2,1)S(1)} %add_convert_fusion), channel_id=1, source_target_pairs={{0,1},{1,0},{2,3},{3,2},{4,5},{5,4},{6,7},{7,6},{8,9},{9,8},{10,11... | collective-permute-start | bytes 737288 | tf_op jit(solution)/shard_map/ppermute | solution.py:277
  (10 other events, 10.7 us)

commit v6 on v5

--- a/solution.py
+++ b/solution.py
@@ -32,24 +32,34 @@
     return jnp.where(keep, rows, 0.0).T[0:depth, :].astype(BF16)
 
 
-def conv_rows(offsets, me, x_refs, halo_refs, w_ref, rows_scr, y_scr):
+def conv_rows(offsets, me, x_refs, halo_refs, w_ref, rows_scr, y_scr, w_scr, sems):
     taps, width = w_ref.shape[0], w_ref.shape[2]
     length = x_refs[0].shape[1]
+    depth = w_scr.shape[1] // len(offsets)
+
+    def copies(k):
+        return [
+            pltpu.make_async_copy(
+                w_ref.at[k, pl.ds(pl.multiple_of((me ^ off) * depth, 16), depth), :],
+                w_scr.at[k, j * depth : (j + 1) * depth, :],
+                sems.at[k, j],
+            )
+            for j, off in enumerate(offsets)
+        ]
+
+    for k in range(taps):
+        for copy in copies(k):
+            copy.start()
     x = jnp.concatenate([ref[...] for ref in x_refs], axis=0)
-    depth = x.shape[0] // len(offsets)
     halo = jnp.concatenate([edge_block(ref, depth) for ref in halo_refs], axis=0)
     rows_scr[0:length, :] = x.T
     rows_scr[length : length + 16, :] = halo.T[0:16]
-    starts = [pl.multiple_of((me ^ off) * depth, 16) for off in offsets]
     for first in range(0, taps, 2):
         group = range(first, min(first + 2, taps))
-        w = jnp.concatenate(
-            [
-                jnp.concatenate([w_ref[k, pl.ds(s, depth), :] for s in starts], axis=0)
-                for k in group
-            ],
-            axis=1,
-        )
+        for k in group:
+            for copy in copies(k):
+                copy.wait()
+        w = jnp.concatenate([w_scr[k] for k in group], axis=1)
         y = jnp.dot(rows_scr[...], w, preferred_element_type=F32)
         for c in range(w.shape[1] // LANES):
             part = y[:, c * LANES : (c + 1) * LANES]
@@ -70,9 +80,9 @@
 
 def first_kernel(offsets, idx_ref, *refs):
     n = len(offsets)
-    *x_refs, w_ref, even_ref, odd_ref, rows_scr, y_scr = refs
+    *x_refs, w_ref, even_ref, odd_ref, rows_scr, y_scr, w_scr, sems = refs
     x_refs, halo_refs = x_refs[:-n], x_refs[-n:]
-    conv_rows(offsets, idx_ref[0], x_refs, halo_refs, w_ref, rows_scr, y_scr)
+    conv_rows(offsets, idx_ref[0], x_refs, halo_refs, w_ref, rows_scr, y_scr, w_scr, sems)
     taps, width = w_ref.shape[0], w_ref.shape[2]
     half = even_ref.shape[0]
     step = min(64, half)
@@ -87,10 +97,11 @@
 def second_kernel(offsets, far, per, idx_ref, *refs):
     n = len(offsets)
     blocks, pays, refs = refs[:n], refs[n : 2 * n], refs[2 * n :]
-    w_ref, even_ref, odd_ref, grad_ref, enc_ref, pre_ref, *sent_refs, rows_scr, y_scr, p_scr, x_scr, edge_scr = refs
+    w_ref, even_ref, odd_ref, grad_ref, enc_ref, pre_ref, *sent_refs = refs[:-7]
+    rows_scr, y_scr, w_scr, sems, p_scr, x_scr, edge_scr = refs[-7:]
     me = idx_ref[0]
     pick = lambda items: [items[j] for j in far]
-    conv_rows(pick(offsets), me, pick(blocks), pick(pays), w_ref, rows_scr, y_scr)
+    conv_rows(pick(offsets), me, pick(blocks), pick(pays), w_ref, rows_scr, y_scr, w_scr, sems)
     taps, width = w_ref.shape[0], w_ref.shape[2]
     half = even_ref.shape[0]
     step = min(64, half)
@@ -145,7 +156,7 @@
 def grad_kernel(offsets, group, per, pieces, idx_ref, *refs):
     n = len(offsets)
     blocks, pays, p_ref = refs[:n], refs[n : 2 * n], refs[2 * n]
-    out_refs, edge_scr = refs[2 * n + 1 : -1], refs[-1]
+    out_refs, edge_scr = list(refs[2 * n + 1 : -1]), refs[-1]
     width = p_ref.shape[1]
     p, edge = shifted_rows(p_ref, edge_scr, group)
     me = idx_ref[0]
@@ -154,31 +165,32 @@
     halo = jnp.concatenate([edge_block(ref, depth) for ref in pays], axis=0)
     res = jnp.dot(x, p, preferred_element_type=F32) + jnp.dot(halo, edge, preferred_element_type=F32)
     res = res.astype(BF16)
-    each = len(out_refs) // len(group)
     for i in range(len(group)):
-        outs = out_refs[i * each : (i + 1) * each]
+        own_ref = out_refs.pop(0)
+        other_refs = [out_refs.pop(0) for _ in range(len(pieces[i]) or min(per, 1))]
         for j, off in enumerate(offsets):
             part = res[j * depth : (j + 1) * depth, i * width : (i + 1) * width]
             at = me ^ off
             if not per:
-                outs[0][pl.ds(pl.multiple_of(at * depth, 16), depth), :] = part
+                own_ref[pl.ds(pl.multiple_of(at * depth, 16), depth), :] = part
                 continue
             mine = lax.div(at, per) == idx_ref[1]
             other = jnp.logical_not(mine)
             row = lax.rem(at, per)
-            hits = [(outs[r], jnp.logical_and(mine, row == r)) for r in range(per)]
-            hits += [(outs[per + k], jnp.logical_and(other, row == r)) for k, r in enumerate(pieces)]
+            hits = [(own_ref, mine)]
+            if not pieces[i]:
+                hits.append((other_refs[0], other))
             for ref, hit in hits:
 
                 @pl.when(hit)
+                def _(ref=ref, part=part, row=row):
+                    ref[pl.ds(pl.multiple_of(row * depth, 16), depth), :] = part
+
+            for r, ref in zip(pieces[i], other_refs):
+
+                @pl.when(jnp.logical_and(other, row == r))
                 def _(ref=ref, part=part):
                     ref[...] = part
-
-            if not pieces:
-
-                @pl.when(other)
-                def _(ref=outs[per], part=part, row=row):
-                    ref[pl.ds(pl.multiple_of(row * depth, 16), depth), :] = part
 
 
 def qkv_kernel(offsets, idx_ref, *refs):
@@ -201,12 +213,15 @@
     out_ref[...] = total.astype(BF16)
 
 
-def call(kernel, out, scratch, mib, idx, *arrays):
+def call(kernel, out, scratch, mib, idx, *arrays, far_off=()):
     vmem = pl.BlockSpec(memory_space=pltpu.VMEM)
+    held = [j for j, a in enumerate(arrays) if any(v is a for v in far_off)]
+    arrays = [pltpu.with_memory_space_constraint(a, pltpu.HBM) if j in held else a for j, a in enumerate(arrays)]
+    specs = [pl.BlockSpec(memory_space=pltpu.HBM) if j in held else vmem for j in range(len(arrays))]
     return pl.pallas_call(
         kernel,
         out_shape=out,
-        in_specs=[pl.BlockSpec(memory_space=pltpu.SMEM)] + [vmem] * len(arrays),
+        in_specs=[pl.BlockSpec(memory_space=pltpu.SMEM)] + specs,
         out_specs=jax.tree.map(lambda _: vmem, out),
         scratch_shapes=scratch,
         compiler_params=pltpu.CompilerParams(vmem_limit_bytes=mib * 1024 * 1024),
@@ -215,6 +230,31 @@
 
 def after(value, *others):
     return lax.optimization_barrier((value, *others))[0]
+
+
+def write_kernel(*refs):
+    *part_refs, out_ref = refs
+    pieces = len(part_refs) // out_ref.shape[0]
+    rows = part_refs[0].shape[0]
+    for i, ref in enumerate(part_refs):
+        tap, r = i // pieces, i % pieces
+        out_ref[tap, r * rows : (r + 1) * rows, :] = ref[...].astype(F32)
+
+
+def written(parts, taps, at, buffer, shape):
+    rows, width = parts[0].shape
+    extra = [] if buffer is None else [buffer]
+    kernel = write_kernel if buffer is None else lambda b, *refs: write_kernel(*refs)
+    return pl.pallas_call(
+        kernel,
+        out_shape=jax.ShapeDtypeStruct(shape, F32),
+        grid=(1,),
+        in_specs=[pl.BlockSpec(memory_space=pl.ANY)] * len(extra)
+        + [pl.BlockSpec((rows, width), lambda i: (0, 0))] * len(parts),
+        out_specs=pl.BlockSpec((taps, shape[1], width), lambda i: (at // taps, 0, 0)),
+        input_output_aliases={0: 0} if extra else {},
+        compiler_params=pltpu.CompilerParams(vmem_limit_bytes=16 * 1024 * 1024),
+    )(*extra, *parts)
 
 
 def edge_kernel(head_ref, tail_ref, out_ref):
@@ -257,38 +297,36 @@
     return (a.astype(F32) + b.astype(F32)).astype(BF16)
 
 
-def chain_sums(count, part, sent):
+def chain_sums(count, part, sent, idle):
     me = lax.axis_index("dp")
     end = jnp.logical_or(me == 0, me == 3)
     outer_pairs = [(0, 1), (1, 0), (2, 3), (3, 2)]
     middle_pairs = [(0, 0), (1, 2), (2, 1), (3, 3)]
-    last, late = None, None
+    last = None
     h, p, s, outer, middle, sums = {}, {}, {}, {}, {}, {}
-    for r in range(count + 5):
+    for r in range(count + 3):
+        if r - 2 in middle:
+            got = after(middle.pop(r - 2), last)
+            last = s[r - 2] = lax.optimization_barrier(added(p[r - 2], got))
         if r < count:
-            h[r] = part(r, last)
-            last = h[r]
-            sent(r, last)
-        if r < count + 3:
-            value = h.get(r, s.get(r - 3))
-            if r in h and r - 3 in s:
-                value = jnp.where(end, h[r], s[r - 3])
+            last = h[r] = part(r, last)
+        if r < count + 2:
+            value = h.get(r, s.get(r - 2))
+            if r in h and r - 2 in s:
+                value = jnp.where(end, h[r], s[r - 2])
             last = value = lax.optimization_barrier(value)
             outer[r] = lax.ppermute(value, "dp", outer_pairs)
+            last = sent(r, last)
         if r - 1 in outer:
             got = after(outer.pop(r - 1), last)
             if r - 1 < count:
                 last = p[r - 1] = lax.optimization_barrier(added(h[r - 1], got))
-                late = last
                 middle[r - 1] = lax.ppermute(last, "dp", middle_pairs)
-            if r - 4 >= 0:
-                sums[r - 4] = lax.optimization_barrier(jnp.where(end, got, s[r - 4]))
-                if r - 1 >= count:
-                    last = sums[r - 4]
-        if r - 2 in middle:
-            got = after(middle.pop(r - 2), last)
-            last = s[r - 2] = lax.optimization_barrier(added(p[r - 2], got))
-    return [sums[c].astype(F32) for c in range(count)], late
+            if r >= 3:
+                sums[r - 3] = jnp.where(end, got, s[r - 3])
+            if r - 1 < count:
+                last = idle(r - 1, last, sums)
+    return [sums[c] for c in range(count)]
 
 
 def on_device(block_input, conv_weight, norm_gain, qkv_weight, encoder_grad):
@@ -309,6 +347,8 @@
     scratch = lambda at: [
         pltpu.VMEM((length + 16, len(at) * depth), BF16),
         pltpu.VMEM((taps * width // LANES, length + 2 * EDGE, LANES), F32),
+        pltpu.VMEM((taps, len(at) * depth, width), BF16),
+        pltpu.SemaphoreType.DMA((taps, len(at))),
     ]
 
     blocks = [x]
@@ -326,6 +366,7 @@
         scratch(near),
         24,
         idx, x, own, *pick(payloads, near), conv_weight,
+        far_off=(conv_weight,),
     )
     hold = [even] + pick(payloads, far)
     blocks = blocks + [own] + [swap(after(b, *hold), "mp", bits[-1]) for b in blocks[1:]]
@@ -347,92 +388,104 @@
         ],
         26,
         idx, *blocks, *payloads, conv_weight, even, odd, encoder_grad[0],
+        far_off=(conv_weight,),
     )
     encs = [encoded]
     for bit in bits[:-1]:
         encs = encs + [swap(e, "mp", bit) for e in encs]
 
     everything = tuple(range(per))
-    pieces_of = lambda k: everything[1:] if k == 0 else (everything if k == taps - 1 else ())
+    pieces_of = lambda k: (everything[1:], everything)[k] if k < 2 else ()
 
     def gradient(group, hold):
-        pieces = pieces_of(group[0])
-        if not pair:
-            outs = (jax.ShapeDtypeStruct((peers * depth, width), BF16),)
-        else:
-            whole = (jax.ShapeDtypeStruct((per * depth, width), BF16),)
-            outs = (piece,) * per + ((piece,) * len(pieces) if pieces else whole)
-        each = len(outs)
-        outs = call(
+        pieces = [pieces_of(k) for k in group]
+        outs = []
+        for q in pieces:
+            if not pair:
+                outs.append([jax.ShapeDtypeStruct((peers * depth, width), BF16)])
+                continue
+            whole = jax.ShapeDtypeStruct((per * depth, width), BF16)
+            outs.append([whole] + ([piece] * len(q) if q else [whole]))
+        flat = call(
             functools.partial(grad_kernel, offsets, group, per, pieces),
-            outs * len(group),
+            tuple(o for tap in outs for o in tap),
             [pltpu.VMEM((LANES, width * len(group)), F32)],
-            14,
+            16,
             after(idx, *hold) if hold else idx, *blocks, *payloads, pre_grad,
         )
-        outs = [outs[i * each : (i + 1) * each] for i in range(len(group))]
-        return [list(o[:per]) for o in outs], [list(o[per:]) for o in outs]
-
-    if pair:
-        groups = [(0,)] + [tuple(range(k, min(k + 2, taps - 1))) for k in range(1, taps - 1, 2)] + [(taps - 1,)]
-        keep, send, got = [], [], {}
-        relays = []
-
-        def work(hold):
-            if not groups:
-                return
-            mine, other = gradient(groups.pop(0), hold)
-            for m, o in zip(mine, other):
-                keep.append(m)
-                send.append((list(first) + o) if len(send) == 0 else o)
-
-        def launch(tap, hold):
-            while len(send) <= tap:
-                work(hold)
-            got[tap] = [swap(after(v, *hold) if hold else v, "seq", 1) for v in send[tap]]
-
-        work([])
-        launch(0, [])
-        launch(1, [])
-
-        def share(c, last):
-            tap, row = c // per, c % per
-            value = got[tap][row] if len(got[tap]) > 1 else got[tap][0][row * depth : (row + 1) * depth]
-            hold = [] if last is None else [last]
-            if c == per:
-                relays.extend([swap(after(e, last), "mp", bits[-1]) for e in encs])
-            if c == 2 * per:
-                hold = hold + relays
-            if hold:
-                value = after(value, *hold)
-            return added(keep[tap][row], value)
-
-        def sent(c, last):
-            if c == per - 1:
-                work([last] + encs[1:])
-                work([last])
-            if c % per == per - 1 and c // per + 2 < taps:
-                launch(c // per + 2, [last])
-
-        sums, late = chain_sums(taps * per, share, sent)
-        encs = encs + relays
-        sums = [jnp.concatenate(sums[k * per : (k + 1) * per], axis=0) for k in range(taps)]
-    else:
-        sums = [gradient((k,), [])[1][0][0] for k in range(taps)]
-        sums = [lax.psum_scatter(v, "seq", scatter_dimension=0, tiled=True) for v in sums]
-        sums = [lax.psum(v, "dp").astype(F32) for v in sums]
-        encs = encs + [swap(e, "mp", bits[-1]) for e in encs]
-        late = encs[-1]
-    conv_grad = jnp.stack(sums, axis=1)
-
-    qkv = call(
+        flat = list(flat)
+        taken = [[flat.pop(0) for _ in tap] for tap in outs]
+        return [t[0] for t in taken], [t[1:] for t in taken]
+
+    qkv_call = lambda idx, encs: call(
         functools.partial(qkv_kernel, offsets),
         jax.ShapeDtypeStruct((half, qkv_weight.shape[1]), BF16),
         [],
         8,
-        after(idx, late), *encs, *payloads, qkv_weight,
+        idx, *encs, *payloads, qkv_weight,
     )
-    return (qkv[None], conv_grad)
+    if not pair:
+        sums = [gradient((k,), [])[0][0] for k in range(taps)]
+        sums = [lax.psum_scatter(v, "seq", scatter_dimension=0, tiled=True) for v in sums]
+        sums = [lax.psum(v, "dp").astype(F32) for v in sums]
+        encs = encs + [swap(e, "mp", bits[-1]) for e in encs]
+        return (qkv_call(idx, encs)[None], jnp.stack(sums, axis=1))
+
+    chunks = taps * per
+    keep, send, got, relays, done = [], [], {}, [], {}
+
+    def work(group, hold):
+        if not group:
+            return
+        mine, other = gradient(group, hold)
+        keep.extend(mine)
+        send.extend(other if send else [list(first) + other[0]] + other[1:])
+
+    def launch(tap, hold):
+        if tap < taps:
+            got[tap] = [swap(after(v, *hold) if hold else v, "seq", 1) for v in send[tap]]
+
+    work((0,), [])
+    launch(0, [])
+
+    def share(c, last):
+        tap, row = c // per, c % per
+        rows = slice(row * depth, (row + 1) * depth)
+        value = got[tap][row] if len(got[tap]) > 1 else got[tap][0][rows]
+        return added(keep[tap][rows], value if last is None else after(value, last))
+
+    def sent(r, last):
+        if r == 0:
+            work(tuple(range(1, min(3, taps))), [last])
+            launch(1, [])
+            last = keep[-1]
+        return last
+
+    def idle(c, last, sums):
+        if c == 0:
+            work(tuple(range(3, taps)), [last] + encs[1:])
+            last = keep[-1]
+        if c == 1:
+            relays.extend([swap(after(e, last), "mp", bits[-1]) for e in encs])
+        if c % per == 0 and c // per + 2 < taps:
+            launch(c // per + 2, [last])
+        if c == chunks - 4:
+            last = done["qkv"] = qkv_call(after(idx, last, *relays), encs + relays)
+        if c == chunks - 1:
+            early = (len(sums) // per) if len(sums) >= per * (taps - 1) else 0
+            if early:
+                parts = [sums[i] for i in range(early * per)]
+                parts[0] = after(parts[0], last)
+                last = done["early"] = written(parts, early, 0, None, (taps, per * depth, width))
+        return last
+
+    sums = chain_sums(chunks, share, sent, idle)
+    shape = (taps, per * depth, width)
+    if "early" in done:
+        conv_grad = written(sums[(taps - 1) * per :], 1, taps - 1, done["early"], shape)
+    else:
+        conv_grad = written(sums, taps, 0, None, shape)
+    return (done["qkv"][None], jnp.swapaxes(conv_grad, 0, 1))
 
 
 def solution(mesh):

time: 139 us -> 167 us (1.20)
  waiting for transfers between devices: 20.6 us -> 43.7 us
  Pallas kernels: 28 us -> 34.3 us
  starting transfers between devices: 66.9 us -> 71.5 us
  local copies, waits for them, and re-layouts: 12.7 us -> 8.41 us
    ppermute x13 -> x12, waiting for transfers between devices: 16.8 us -> 33 us  [chain_sums(): outer[r] = lax.ppermute(value, 'dp', outer_pairs)]
    ppermute x17, waiting for transfers between devices: 3.7 us -> 10.7 us  [swap(): return lax.ppermute(value, axis, [(i, i ^ bit) for i in range(peers)])]
    unnamed x36 -> x34, local copies, waits for them, and re-layouts: 10.7 us -> 7.5 us
    pallas_call x0 -> x2, Pallas kernels: none -> 3.19 us  [written(): pl.pallas_call(kernel, out_shape=jax.ShapeDtypeStruct(shape, F32), grid=(...]
    pallas_call x7 -> x6, Pallas kernels: 27.9 us -> 31 us  [call(): pl.pallas_call(kernel, out_shape=out, in_specs=[pl.BlockSpec(memory_space...]
    ppermute x10, starting transfers between devices: 6.98 us -> 9.85 us  [chain_sums(): middle[r - 1] = lax.ppermute(last, 'dp', middle_pairs)]
    another operation x2 -> x0, other arithmetic: 2.68 us -> none  [on_device(): conv_grad = jnp.stack(sums, axis=1)]
    ppermute x13 -> x12, starting transfers between devices: 43.6 us -> 44.7 us  [chain_sums(): outer[r] = lax.ppermute(value, 'dp', outer_pairs)]
  transfers between devices with their start and end apart: 40 -> 39, of which waited for: 9 -> 15; matrix products, arithmetic and copies ran while one was open for 6% -> 5% of each run, Pallas kernels for 15% -> 15%
where the time goes in v6:
time: 167 us; the launch traced here: 166 us
  starting transfers between devices  71.5 us (43%)
  waiting for transfers between devices  43.7 us (26%)
  Pallas kernels  34.3 us (21%)
  local copies, waits for them, and re-layouts  8.41 us (5%)
  other arithmetic  7.33 us (4%)
    ppermute x12, starting transfers between devices, chain_sums(): outer[r] = lax.ppermute(value, 'dp', outer_pairs)  44.7 us
    ppermute x12, waiting for transfers between devices, chain_sums(): outer[r] = lax.ppermute(value, 'dp', outer_pairs)  33 us
    pallas_call x6, Pallas kernels, call(): pl.pallas_call(kernel, out_shape=out, in_specs=[pl.BlockSpec(memory_space...  31 us
    ppermute x17, starting transfers between devices, swap(): return lax.ppermute(value, axis, [(i, i ^ bit) for i in range(peers)])  17 us
    ppermute x17, waiting for transfers between devices, swap(): return lax.ppermute(value, axis, [(i, i ^ bit) for i in range(peers)])  10.7 us
    ppermute x10, starting transfers between devices, chain_sums(): middle[r - 1] = lax.ppermute(last, 'dp', middle_pairs)  9.85 us
    unnamed x34, local copies, waits for them, and re-layouts  7.5 us
    convert_element_type x22, other arithmetic, added(): return (a.astype(F32) + b.astype(F32)).astype(BF16)  5.14 us
  transfers between devices with their start and end apart: 39, of which 15 were waited for; matrix products, arithmetic and copies ran while one was open for 5% of the time, Pallas kernels for 15%

profile of v6, /device:TPU:0, one launch (start us, length us, event | category | flops | bytes accessed | tf_op | source)
XLA Modules:
  0.0 166.4 jit_solution(10136292211821314824)
XLA Ops:
  1.1 2.6 %collective-permute-start = (bf16[320,1024]{1,0:T(8,128)(2,1)}, bf16[320,1024]{1,0:T(8,128)(2,1)S(1)}, u32[]{:S(2)}, u32[]{:S(2)}) collective-permute-start(bf16[320,1024]{1,0:T(8,128)(2,1)} %bitcast.9), channel_id=1, source_target_pairs={{0,8},{4,12},{8,0},{12,4},{1,9},{5,13},{9,1},{13,5},{2,10},{6,14},... | collective-permute-start | bytes 1966088 | tf_op jit(solution)/shard_map/ppermute | solution.py:26
  3.7 1.1 copy-done
  5.0 1.6 collective-permute-start.2
  7.3 1.4 collective-permute-done.2
  8.9 0.9 collective-permute-start.4
  9.8 0.9 collective-permute-start.3
  11.6 1.1 copy-done.1
  12.7 7.2 %shard_map.69 = (f32[512,384]{1,0:T(8,128)S(1)}, f32[512,384]{1,0:T(8,128)S(1)}) custom-call(s32[2]{0:T(128)S(1)} %pad_add_fusion.idx_ref, bf16[320,1024]{1,0:T(8,128)(2,1)S(1)} %bitcast.12, bf16[320,1024]{1,0:T(8,128)(2,1)S(1)} %collective-permute-done.1.refs_1_.refs_2_, f32[8,384]{1,0:T(8,128)S(1)} %maximum_maximum_fusion.refs_2_.refs_4_, ...), custom_call_target="tpu_custom_call" | custom-call | tf_op jit(solution)/shard_map/pallas_call | solution.py:221
  22.1 1.3 copy-done.4
  23.4 9.1 %shard_map.70 = (bf16[512,384]{1,0:T(8,128)(2,1)}, f32[1040,384]{1,0:T(8,128)S(1)}, bf16[320,384]{1,0:T(8,128)(2,1)S(1)}) custom-call(s32[2]{0:T(128)S(1)} %pad_add_fusion.idx_ref, bf16[320,1024]{1,0:T(8,128)(2,1)S(1)} %bitcast.13, bf16[320,1024]{1,0:T(8,128)(2,1)S(1)} %copy-done.4, bf16[320,1024]{1,0:T(8,128)(2,1)S(1)} %collective-permute-done.1.refs_1_.refs_2_, ...), custom_call_target="tpu_custom_call" | custom-call | tf_op jit(solution)/shard_map/pallas_call | solution.py:221
  32.4 1.6 collective-permute-start.7
  34.1 2.7 %shard_map.71 = (bf16[640,384]{1,0:T(8,128)(2,1)S(1)}, bf16[320,384]{1,0:T(8,128)(2,1)S(1)}) custom-call(s32[2]{0:T(128)S(1)} %pad_add_fusion.idx_ref, bf16[320,1024]{1,0:T(8,128)(2,1)S(1)} %bitcast.14, bf16[320,1024]{1,0:T(8,128)(2,1)S(1)} %copy-done.4, bf16[320,1024]{1,0:T(8,128)(2,1)S(1)} %collective-permute-done.1.refs_1_.refs_2_, ...), custom_call_target="tpu_custom_call" | custom-call | tf_op jit(solution)/shard_map/pallas_call | solution.py:221
  37.3 4.0 %collective-permute-done.7 = bf16[320,384]{1,0:T(8,128)(2,1)S(1)} collective-permute-done((bf16[320,384]{1,0:T(8,128)(2,1)S(1)}, bf16[320,384]{1,0:T(8,128)(2,1)S(1)}, u32[]{:S(2)}, u32[]{:S(2)}) %collective-permute-start.7) | collective-permute-done | bytes 245792 | tf_op jit(solution)/shard_map/ppermute | solution.py:26
  41.4 1.7 %collective-permute-start.8 = (bf16[320,384]{1,0:T(8,128)(2,1)S(1)}, bf16[320,384]{1,0:T(8,128)(2,1)S(1)}, u32[]{:S(2)}, u32[]{:S(2)}) collective-permute-start(bf16[320,384]{1,0:T(8,128)(2,1)S(1)} %add_convert_fusion.29), channel_id=1, source_target_pairs={{0,1},{1,0},{2,3},{3,2},{4,5},{5,4},{6,7},{7,6},{8,9},{9,8},{10,11... | collective-permute-start | bytes 737288 | tf_op jit(solution)/shard_map/ppermute | solution.py:318
  43.1 1.5 collective-permute-start.10
  44.6 4.3 %shard_map.72 = (bf16[640,384]{1,0:T(8,128)(2,1)S(1)}, bf16[320,384]{1,0:T(8,128)(2,1)}, bf16[320,384]{1,0:T(8,128)(2,1)S(1)}, bf16[640,384]{1,0:T(8,128)(2,1)S(1)}, bf16[640,384]{1,0:T(8,128)(2,1)S(1)}) custom-call(s32[2]{0:T(128)S(1)} %pad_add_fusion.idx_ref, bf16[320,1024]{1,0:T(8,128)(2,1)S(1)} %bitcast.15, bf16[320,1024]{1,0:T(8,128)(2,1)S(1)} %copy-done.4, ...), custom_call_target="tpu_custom_call" | custom-call | tf_op jit(solution)/shard_map/pallas_call | solution.py:221
  51.5 3.5 %collective-permute-start.12 = (bf16[320,384]{1,0:T(8,128)(2,1)}, bf16[320,384]{1,0:T(8,128)(2,1)}, u32[]{:S(2)}, u32[]{:S(2)}) collective-permute-start(bf16[320,384]{1,0:T(8,128)(2,1)} %add_convert_fusion.27), channel_id=1, source_target_pairs={{0,0},{1,2},{2,1},{3,3},{4,4},{5,6},{6,5},{7,7},{8,8},{9,10},{10,9... | collective-permute-start | bytes 737288 | tf_op jit(solution)/shard_map/ppermute | solution.py:324
  55.0 1.5 collective-permute-start.11
  56.5 1.6 collective-permute-start.15
  58.1 1.1 copy-done.5
  59.2 1.1 copy-done.7
  60.3 3.6 %shard_map.73 = (bf16[640,384]{1,0:T(8,128)(2,1)S(1)}, bf16[640,384]{1,0:T(8,128)(2,1)S(1)}, bf16[640,384]{1,0:T(8,128)(2,1)S(1)}, bf16[640,384]{1,0:T(8,128)(2,1)S(1)}) custom-call(s32[2]{0:T(128)S(1)} %pad_add_fusion.idx_ref, bf16[320,1024]{1,0:T(8,128)(2,1)S(1)} %bitcast.16, bf16[320,1024]{1,0:T(8,128)(2,1)S(1)} %copy-done.5, ...), custom_call_target="tpu_custom_call" | custom-call | tf_op jit(solution)/shard_map/pallas_call | solution.py:221
  63.9 1.1 add_convert_fusion.26
  65.1 1.0 broadcast_select_fusion.17
  67.5 1.5 collective-permute-start.18
  69.0 3.3 %collective-permute-start.13 = (bf16[320,384]{1,0:T(8,128)(2,1)S(1)}, bf16[320,384]{1,0:T(8,128)(2,1)S(1)}, u32[]{:S(2)}, u32[]{:S(2)}) collective-permute-start(bf16[320,384]{1,0:T(8,128)(2,1)S(1)} %broadcast_select_fusion.17), channel_id=1, source_target_pairs={{0,1},{1,0},{2,3},{3,2},{4,5},{5,4},{6,7},{7,6},{8,9},{9,8},{10,11... | collective-permute-start | bytes 737288 | tf_op jit(solution)/shard_map/ppermute | solution.py:318
  72.3 3.5 %collective-permute-done.14 = bf16[320,384]{1,0:T(8,128)(2,1)S(1)} collective-permute-done((bf16[320,384]{1,0:T(8,128)(2,1)S(1)}, bf16[320,384]{1,0:T(8,128)(2,1)S(1)}, u32[]{:S(2)}, u32[]{:S(2)}) %collective-permute-start.14) | collective-permute-done | bytes 245792 | tf_op jit(solution)/shard_map/ppermute | solution.py:26
  76.4 1.0 add_convert_fusion.21
  78.2 4.5 %collective-permute-start.21 = (bf16[320,384]{1,0:T(8,128)(2,1)S(1)}, bf16[320,384]{1,0:T(8,128)(2,1)S(1)}, u32[]{:S(2)}, u32[]{:S(2)}) collective-permute-start(bf16[320,384]{1,0:T(8,128)(2,1)S(1)} %broadcast_select_fusion.16), channel_id=1, source_target_pairs={{0,1},{1,0},{2,3},{3,2},{4,5},{5,4},{6,7},{7,6},{8,9},{9,8},{10,11... | collective-permute-start | bytes 737288 | tf_op jit(solution)/shard_map/ppermute | solution.py:318
  82.9 3.9 %collective-permute-done.21 = bf16[320,384]{1,0:T(8,128)(2,1)S(1)} collective-permute-done((bf16[320,384]{1,0:T(8,128)(2,1)S(1)}, bf16[320,384]{1,0:T(8,128)(2,1)S(1)}, u32[]{:S(2)}, u32[]{:S(2)}) %collective-permute-start.21) | collective-permute-done | bytes 245792 | tf_op jit(solution)/shard_map/ppermute | solution.py:318
  88.3 5.4 %collective-permute-start.20 = (bf16[320,384]{1,0:T(8,128)(2,1)S(1)}, bf16[320,384]{1,0:T(8,128)(2,1)S(1)}, u32[]{:S(2)}, u32[]{:S(2)}) collective-permute-start(bf16[320,384]{1,0:T(8,128)(2,1)S(1)} %broadcast_select_fusion.15), channel_id=1, source_target_pairs={{0,1},{1,0},{2,3},{3,2},{4,5},{5,4},{6,7},{7,6},{8,9},{9,8},{10,11... | collective-permute-start | bytes 737288 | tf_op jit(solution)/shard_map/ppermute | solution.py:318
  93.9 6.3 %collective-permute-done.20 = bf16[320,384]{1,0:T(8,128)(2,1)S(1)} collective-permute-done((bf16[320,384]{1,0:T(8,128)(2,1)S(1)}, bf16[320,384]{1,0:T(8,128)(2,1)S(1)}, u32[]{:S(2)}, u32[]{:S(2)}) %collective-permute-start.20) | collective-permute-done | bytes 245792 | tf_op jit(solution)/shard_map/ppermute | solution.py:318
  101.0 4.1 %collective-permute-start.25 = (bf16[320,384]{1,0:T(8,128)(2,1)S(1)}, bf16[320,384]{1,0:T(8,128)(2,1)S(1)}, u32[]{:S(2)}, u32[]{:S(2)}) collective-permute-start(bf16[320,384]{1,0:T(8,128)(2,1)S(1)} %broadcast_select_fusion.14), channel_id=1, source_target_pairs={{0,1},{1,0},{2,3},{3,2},{4,5},{5,4},{6,7},{7,6},{8,9},{9,8},{10,11... | collective-permute-start | bytes 737288 | tf_op jit(solution)/shard_map/ppermute | solution.py:318
  105.3 3.9 %collective-permute-done.25 = bf16[320,384]{1,0:T(8,128)(2,1)S(1)} collective-permute-done((bf16[320,384]{1,0:T(8,128)(2,1)S(1)}, bf16[320,384]{1,0:T(8,128)(2,1)S(1)}, u32[]{:S(2)}, u32[]{:S(2)}) %collective-permute-start.25) | collective-permute-done | bytes 245792 | tf_op jit(solution)/shard_map/ppermute | solution.py:318
  110.7 1.6 collective-permute-start.29
  112.3 5.1 %collective-permute-start.24 = (bf16[320,384]{1,0:T(8,128)(2,1)S(1)}, bf16[320,384]{1,0:T(8,128)(2,1)S(1)}, u32[]{:S(2)}, u32[]{:S(2)}) collective-permute-start(bf16[320,384]{1,0:T(8,128)(2,1)S(1)} %broadcast_select_fusion.13), channel_id=1, source_target_pairs={{0,1},{1,0},{2,3},{3,2},{4,5},{5,4},{6,7},{7,6},{8,9},{9,8},{10,11... | collective-permute-start | bytes 737288 | tf_op jit(solution)/shard_map/ppermute | solution.py:318
  117.6 5.7 %collective-permute-done.24 = bf16[320,384]{1,0:T(8,128)(2,1)S(1)} collective-permute-done((bf16[320,384]{1,0:T(8,128)(2,1)S(1)}, bf16[320,384]{1,0:T(8,128)(2,1)S(1)}, u32[]{:S(2)}, u32[]{:S(2)}) %collective-permute-start.24) | collective-permute-done | bytes 245792 | tf_op jit(solution)/shard_map/ppermute | solution.py:318
  124.3 3.3 %collective-permute-start.30 = (bf16[320,384]{1,0:T(8,128)(2,1)S(1)}, bf16[320,384]{1,0:T(8,128)(2,1)S(1)}, u32[]{:S(2)}, u32[]{:S(2)}) collective-permute-start(bf16[320,384]{1,0:T(8,128)(2,1)S(1)} %broadcast_select_fusion.12), channel_id=1, source_target_pairs={{0,1},{1,0},{2,3},{3,2},{4,5},{5,4},{6,7},{7,6},{8,9},{9,8},{10,11... | collective-permute-start | bytes 737288 | tf_op jit(solution)/shard_map/ppermute | solution.py:318
  127.7 4.1 %shard_map.74 = bf16[512,640]{1,0:T(8,128)(2,1)} custom-call(s32[2]{0:T(128)S(1)} %pad_add_fusion.idx_ref, bf16[512,384]{1,0:T(8,128)(2,1)} %get-tuple-element.99.refs_0_, bf16[512,384]{1,0:T(8,128)(2,1)} %collective-permute-done.10.refs_1_, bf16[512,384]{1,0:T(8,128)(2,1)S(1)} %collective-permute-done.27.refs_2_, ...), custom_call_target="tpu_custom_call" | custom-call | tf_op jit(solution)/shard_map/pallas_call | solution.py:221
  133.3 4.8 %collective-permute-start.34 = (bf16[320,384]{1,0:T(8,128)(2,1)S(1)}, bf16[320,384]{1,0:T(8,128)(2,1)S(1)}, u32[]{:S(2)}, u32[]{:S(2)}) collective-permute-start(bf16[320,384]{1,0:T(8,128)(2,1)S(1)} %broadcast_select_fusion.10), channel_id=1, source_target_pairs={{0,1},{1,0},{2,3},{3,2},{4,5},{5,4},{6,7},{7,6},{8,9},{9,8},{10,11... | collective-permute-start | bytes 737288 | tf_op jit(solution)/shard_map/ppermute | solution.py:318
  138.2 4.0 %collective-permute-done.34 = bf16[320,384]{1,0:T(8,128)(2,1)S(1)} collective-permute-done((bf16[320,384]{1,0:T(8,128)(2,1)S(1)}, bf16[320,384]{1,0:T(8,128)(2,1)S(1)}, u32[]{:S(2)}, u32[]{:S(2)}) %collective-permute-start.34) | collective-permute-done | bytes 245792 | tf_op jit(solution)/shard_map/ppermute | solution.py:318
  143.1 3.6 %collective-permute-start.33 = (bf16[320,384]{1,0:T(8,128)(2,1)S(1)}, bf16[320,384]{1,0:T(8,128)(2,1)S(1)}, u32[]{:S(2)}, u32[]{:S(2)}) collective-permute-start(bf16[320,384]{1,0:T(8,128)(2,1)S(1)} %broadcast_select_fusion.9), channel_id=1, source_target_pairs={{0,1},{1,0},{2,3},{3,2},{4,5},{5,4},{6,7},{7,6},{8,9},{9,8},{10,11... | collective-permute-start | bytes 737288 | tf_op jit(solution)/shard_map/ppermute | solution.py:318
  146.8 4.1 %collective-permute-done.33 = bf16[320,384]{1,0:T(8,128)(2,1)S(1)} collective-permute-done((bf16[320,384]{1,0:T(8,128)(2,1)S(1)}, bf16[320,384]{1,0:T(8,128)(2,1)S(1)}, u32[]{:S(2)}, u32[]{:S(2)}) %collective-permute-start.33) | collective-permute-done | bytes 245792 | tf_op jit(solution)/shard_map/ppermute | solution.py:318
  151.7 5.1 %collective-permute-start.36 = (bf16[320,384]{1,0:T(8,128)(2,1)S(1)}, bf16[320,384]{1,0:T(8,128)(2,1)S(1)}, u32[]{:S(2)}, u32[]{:S(2)}) collective-permute-start(bf16[320,384]{1,0:T(8,128)(2,1)S(1)} %add_convert_fusion.2), channel_id=1, source_target_pairs={{0,1},{1,0},{2,3},{3,2},{4,5},{5,4},{6,7},{7,6},{8,9},{9,8},{10,11... | collective-permute-start | bytes 737288 | tf_op jit(solution)/shard_map/ppermute | solution.py:318
  156.8 2.2 %shard_map.75.b = f32[5,640,384]{2,1,0:T(8,128)} custom-call(bf16[320,384]{1,0:T(8,128)(2,1)S(1)} %broadcast_select_fusion.11.refs_0_, bf16[320,384]{1,0:T(8,128)(2,1)S(1)} %broadcast_select_fusion.8.refs_1_, bf16[320,384]{1,0:T(8,128)(2,1)S(1)} %broadcast_select_fusion.7.refs_2_, bf16[320,384]{1,0:T(8,128)(2,1)S(1)} %broadcast_select_fusion.6.refs_3_, ...), custom_call_target="tpu_custom_call" | custom-call | tf_op jit(solution)/shard_map/pallas_call | solution.py:248
  159.1 2.1 %collective-permute-start.38 = (bf16[320,384]{1,0:T(8,128)(2,1)S(1)}, bf16[320,384]{1,0:T(8,128)(2,1)S(1)}, u32[]{:S(2)}, u32[]{:S(2)}) collective-permute-start(bf16[320,384]{1,0:T(8,128)(2,1)S(1)} %add_convert_fusion), channel_id=1, source_target_pairs={{0,1},{1,0},{2,3},{3,2},{4,5},{5,4},{6,7},{7,6},{8,9},{9,8},{10,11... | collective-permute-start | bytes 737288 | tf_op jit(solution)/shard_map/ppermute | solution.py:318
  161.5 3.8 %collective-permute-done.38 = bf16[320,384]{1,0:T(8,128)(2,1)S(1)} collective-permute-done((bf16[320,384]{1,0:T(8,128)(2,1)S(1)}, bf16[320,384]{1,0:T(8,128)(2,1)S(1)}, u32[]{:S(2)}, u32[]{:S(2)}) %collective-permute-start.38) | collective-permute-done | bytes 245792 | tf_op jit(solution)/shard_map/ppermute | solution.py:318
  165.4 1.0 shard_map.76
  (121 shorter events, 19.4 us)
Async XLA Ops:
  0.6 10.9 %collective-permute-start.1 = (bf16[320,1024]{1,0:T(8,128)(2,1)}, bf16[320,1024]{1,0:T(8,128)(2,1)S(1)}, u32[]{:S(2)}, u32[]{:S(2)}) collective-permute-start(bf16[320,1024]{1,0:T(8,128)(2,1)} %bitcast.8), channel_id=1, source_target_pairs={{0,4},{4,0},{8,12},{12,8},{1,5},{5,1},{9,13},{13,9},{2,6},{6,2},{1... | collective-permute-start | bytes 1966088 | tf_op jit(solution)/shard_map/ppermute | solution.py:26
  1.1 18.7 %collective-permute-start = (bf16[320,1024]{1,0:T(8,128)(2,1)}, bf16[320,1024]{1,0:T(8,128)(2,1)S(1)}, u32[]{:S(2)}, u32[]{:S(2)}) collective-permute-start(bf16[320,1024]{1,0:T(8,128)(2,1)} %bitcast.9), channel_id=1, source_target_pairs={{0,8},{4,12},{8,0},{12,4},{1,9},{5,13},{9,1},{13,5},{2,10},{6,14},... | collective-permute-start | bytes 1966088 | tf_op jit(solution)/shard_map/ppermute | solution.py:26
  4.9 17.2 %copy-start.2 = (bf16[1,1024,320]{1,2,0:T(8,128)(2,1)S(1)}, bf16[1,1024,320]{1,2,0:T(8,128)(2,1)}, u32[]{:S(2)}) copy-start(bf16[1,1024,320]{1,2,0:T(8,128)(2,1)} %param.5) | copy-start | bytes 1966084
  4.9 17.2 %copy-start.11 = (bf16[1,512,384]{2,1,0:T(8,128)(2,1)S(1)}, bf16[1,512,384]{2,1,0:T(8,128)(2,1)}, u32[]{:S(2)}) copy-start(bf16[1,512,384]{2,1,0:T(8,128)(2,1)} %param.9) | copy-start | bytes 1179652
  5.0 3.8 %collective-permute-start.2 = (f32[8,384]{1,0:T(8,128)S(1)}, f32[8,384]{1,0:T(8,128)S(1)}, u32[]{:S(2)}, u32[]{:S(2)}) collective-permute-start(f32[8,384]{1,0:T(8,128)S(1)} %shard_map.68), channel_id=1, source_target_pairs={{0,16},{16,0},{1,17},{17,1},{2,18},{18,2},{3,19},{19,3},{4,20},{20... | collective-permute-start | bytes 36872 | tf_op jit(solution)/shard_map/ppermute | solution.py:26
  8.9 11.0 %collective-permute-start.5 = (f32[8,384]{1,0:T(8,128)S(1)}, f32[8,384]{1,0:T(8,128)S(1)}, u32[]{:S(2)}, u32[]{:S(2)}) collective-permute-start(f32[8,384]{1,0:T(8,128)S(1)} %maximum_maximum_fusion.refs_2_.refs_4_), channel_id=1, source_target_pairs={{0,12},{4,8},{8,4},{12,0},{1,13},{5,9},{9,5},{13,1},{2,14},{6,10},... | collective-permute-start | bytes 36872 | tf_op jit(solution)/shard_map/ppermute | solution.py:26
  8.9 11.0 %collective-permute-start.4 = (f32[8,384]{1,0:T(8,128)S(1)}, f32[8,384]{1,0:T(8,128)S(1)}, u32[]{:S(2)}, u32[]{:S(2)}) collective-permute-start(f32[8,384]{1,0:T(8,128)S(1)} %maximum_maximum_fusion.refs_2_.refs_4_), channel_id=1, source_target_pairs={{0,8},{4,12},{8,0},{12,4},{1,9},{5,13},{9,1},{13,5},{2,10},{6,14},... | collective-permute-start | bytes 36872 | tf_op jit(solution)/shard_map/ppermute | solution.py:26
  9.8 1.8 %collective-permute-start.3 = (f32[8,384]{1,0:T(8,128)S(1)}, f32[8,384]{1,0:T(8,128)S(1)}, u32[]{:S(2)}, u32[]{:S(2)}) collective-permute-start(f32[8,384]{1,0:T(8,128)S(1)} %maximum_maximum_fusion.refs_2_.refs_4_), channel_id=1, source_target_pairs={{0,4},{4,0},{8,12},{12,8},{1,5},{5,1},{9,13},{13,9},{2,6},{6,2},{1... | collective-permute-start | bytes 36872 | tf_op jit(solution)/shard_map/ppermute | solution.py:26
  19.9 2.2 %collective-permute-start.6 = (bf16[320,1024]{1,0:T(8,128)(2,1)S(1)}, bf16[320,1024]{1,0:T(8,128)(2,1)S(1)}, u32[]{:S(2)}, u32[]{:S(2)}) collective-permute-start(bf16[320,1024]{1,0:T(8,128)(2,1)S(1)} %collective-permute-done.refs_1_), channel_id=1, source_target_pairs={{0,4},{4,0},{8,12},{12,8},{1,5},{5,1},{9,13},{13,9},{2,6},{6,2},{1... | collective-permute-start | bytes 1966088 | tf_op jit(solution)/shard_map/ppermute | solution.py:26
  22.1 22.6 %copy-start.6 = (bf16[320,1024]{1,0:T(8,128)(2,1)}, bf16[320,1024]{1,0:T(8,128)(2,1)S(1)}, u32[]{:S(2)}) copy-start(bf16[320,1024]{1,0:T(8,128)(2,1)S(1)} %collective-permute-done.6.refs_3_) | copy-start | bytes 1966084
  22.1 1.3 copy-start.4
  32.4 8.8 %collective-permute-start.7 = (bf16[320,384]{1,0:T(8,128)(2,1)S(1)}, bf16[320,384]{1,0:T(8,128)(2,1)S(1)}, u32[]{:S(2)}, u32[]{:S(2)}) collective-permute-start(bf16[320,384]{1,0:T(8,128)(2,1)S(1)} %get-tuple-element.64), channel_id=1, source_target_pairs={{0,16},{16,0},{1,17},{17,1},{2,18},{18,2},{3,19},{19,3},{4,20},{20... | collective-permute-start | bytes 737288 | tf_op jit(solution)/shard_map/ppermute | solution.py:26
  36.8 13.0 %collective-permute-start.9 = (bf16[320,384]{1,0:T(8,128)(2,1)S(1)}, bf16[320,384]{1,0:T(8,128)(2,1)S(1)}, u32[]{:S(2)}, u32[]{:S(2)}) collective-permute-start(bf16[320,384]{1,0:T(8,128)(2,1)S(1)} %get-tuple-element.65), channel_id=1, source_target_pairs={{0,16},{16,0},{1,17},{17,1},{2,18},{18,2},{3,19},{19,3},{4,20},{20... | collective-permute-start | bytes 737288 | tf_op jit(solution)/shard_map/ppermute | solution.py:26
  41.4 9.3 %collective-permute-start.8 = (bf16[320,384]{1,0:T(8,128)(2,1)S(1)}, bf16[320,384]{1,0:T(8,128)(2,1)S(1)}, u32[]{:S(2)}, u32[]{:S(2)}) collective-permute-start(bf16[320,384]{1,0:T(8,128)(2,1)S(1)} %add_convert_fusion.29), channel_id=1, source_target_pairs={{0,1},{1,0},{2,3},{3,2},{4,5},{5,4},{6,7},{7,6},{8,9},{9,8},{10,11... | collective-permute-start | bytes 737288 | tf_op jit(solution)/shard_map/ppermute | solution.py:318
  43.1 15.0 %collective-permute-start.10 = (bf16[512,384]{1,0:T(8,128)(2,1)}, bf16[512,384]{1,0:T(8,128)(2,1)}, u32[]{:S(2)}, u32[]{:S(2)}) collective-permute-start(bf16[512,384]{1,0:T(8,128)(2,1)} %get-tuple-element.99.refs_0_), channel_id=1, source_target_pairs={{0,8},{4,12},{8,0},{12,4},{1,9},{5,13},{9,1},{13,5},{2,10},{6,14},... | collective-permute-start | bytes 1179656 | tf_op jit(solution)/shard_map/ppermute | solution.py:26
  51.5 12.4 %collective-permute-start.12 = (bf16[320,384]{1,0:T(8,128)(2,1)}, bf16[320,384]{1,0:T(8,128)(2,1)}, u32[]{:S(2)}, u32[]{:S(2)}) collective-permute-start(bf16[320,384]{1,0:T(8,128)(2,1)} %add_convert_fusion.27), channel_id=1, source_target_pairs={{0,0},{1,2},{2,1},{3,3},{4,4},{5,6},{6,5},{7,7},{8,8},{9,10},{10,9... | collective-permute-start | bytes 737288 | tf_op jit(solution)/shard_map/ppermute | solution.py:324
  55.0 10.0 %collective-permute-start.11 = (bf16[320,384]{1,0:T(8,128)(2,1)}, bf16[320,384]{1,0:T(8,128)(2,1)}, u32[]{:S(2)}, u32[]{:S(2)}) collective-permute-start(bf16[320,384]{1,0:T(8,128)(2,1)} %get-tuple-element.75), channel_id=1, source_target_pairs={{0,16},{16,0},{1,17},{17,1},{2,18},{18,2},{3,19},{19,3},{4,20},{20... | collective-permute-start | bytes 737288 | tf_op jit(solution)/shard_map/ppermute | solution.py:26
  56.5 9.6 %collective-permute-start.15 = (bf16[320,384]{1,0:T(8,128)(2,1)}, bf16[320,384]{1,0:T(8,128)(2,1)S(1)}, u32[]{:S(2)}, u32[]{:S(2)}) collective-permute-start(bf16[320,384]{1,0:T(8,128)(2,1)} %add_convert_fusion.28), channel_id=1, source_target_pairs={{0,1},{1,0},{2,3},{3,2},{4,5},{5,4},{6,7},{7,6},{8,9},{9,8},{10,11... | collective-permute-start | bytes 737288 | tf_op jit(solution)/shard_map/ppermute | solution.py:318
  60.3 4.8 %copy-start.10 = (bf16[640,384]{1,0:T(8,128)(2,1)S(1)}, bf16[640,384]{1,0:T(8,128)(2,1)}, u32[]{:S(2)}) copy-start(bf16[640,384]{1,0:T(8,128)(2,1)} %copy-done.9) | copy-start | bytes 1474564
  60.3 5.9 %copy-start.16 = (bf16[320,384]{1,0:T(8,128)(2,1)S(1)}, bf16[320,384]{1,0:T(8,128)(2,1)}, u32[]{:S(2)}) copy-start(bf16[320,384]{1,0:T(8,128)(2,1)} %add_convert_fusion.28) | copy-start | bytes 737284
  60.3 6.6 %copy-start.15 = (bf16[320,384]{1,0:T(8,128)(2,1)S(1)}, bf16[320,384]{1,0:T(8,128)(2,1)}, u32[]{:S(2)}) copy-start(bf16[320,384]{1,0:T(8,128)(2,1)} %copy-done.14) | copy-start | bytes 737284
  60.3 7.2 %copy-start.13 = (bf16[640,384]{1,0:T(8,128)(2,1)S(1)}, bf16[640,384]{1,0:T(8,128)(2,1)}, u32[]{:S(2)}) copy-start(bf16[640,384]{1,0:T(8,128)(2,1)} %copy-done.12) | copy-start | bytes 1474564
  66.2 6.0 %collective-permute-start.16 = (bf16[320,384]{1,0:T(8,128)(2,1)S(1)}, bf16[320,384]{1,0:T(8,128)(2,1)S(1)}, u32[]{:S(2)}, u32[]{:S(2)}) collective-permute-start(bf16[320,384]{1,0:T(8,128)(2,1)S(1)} %add_convert_fusion.24), channel_id=1, source_target_pairs={{0,0},{1,2},{2,1},{3,3},{4,4},{5,6},{6,5},{7,7},{8,8},{9,10},{10,9... | collective-permute-start | bytes 737288 | tf_op jit(solution)/shard_map/ppermute | solution.py:324
  66.9 9.0 %collective-permute-start.14 = (bf16[320,384]{1,0:T(8,128)(2,1)S(1)}, bf16[320,384]{1,0:T(8,128)(2,1)S(1)}, u32[]{:S(2)}, u32[]{:S(2)}) collective-permute-start(bf16[320,384]{1,0:T(8,128)(2,1)S(1)} %copy-done.15), channel_id=1, source_target_pairs={{0,16},{16,0},{1,17},{17,1},{2,18},{18,2},{3,19},{19,3},{4,20},{20... | collective-permute-start | bytes 737288 | tf_op jit(solution)/shard_map/ppermute | solution.py:26
  67.5 15.2 %collective-permute-start.18 = (bf16[640,384]{1,0:T(8,128)(2,1)S(1)}, bf16[640,384]{1,0:T(8,128)(2,1)S(1)}, u32[]{:S(2)}, u32[]{:S(2)}) collective-permute-start(bf16[640,384]{1,0:T(8,128)(2,1)S(1)} %copy-done.13), channel_id=1, source_target_pairs={{0,16},{16,0},{1,17},{17,1},{2,18},{18,2},{3,19},{19,3},{4,20},{20... | collective-permute-start | bytes 1474568 | tf_op jit(solution)/shard_map/ppermute | solution.py:26
  69.0 7.4 %collective-permute-start.13 = (bf16[320,384]{1,0:T(8,128)(2,1)S(1)}, bf16[320,384]{1,0:T(8,128)(2,1)S(1)}, u32[]{:S(2)}, u32[]{:S(2)}) collective-permute-start(bf16[320,384]{1,0:T(8,128)(2,1)S(1)} %broadcast_select_fusion.17), channel_id=1, source_target_pairs={{0,1},{1,0},{2,3},{3,2},{4,5},{5,4},{6,7},{7,6},{8,9},{9,8},{10,11... | collective-permute-start | bytes 737288 | tf_op jit(solution)/shard_map/ppermute | solution.py:318
  77.5 5.3 %collective-permute-start.19 = (bf16[320,384]{1,0:T(8,128)(2,1)S(1)}, bf16[320,384]{1,0:T(8,128)(2,1)S(1)}, u32[]{:S(2)}, u32[]{:S(2)}) collective-permute-start(bf16[320,384]{1,0:T(8,128)(2,1)S(1)} %add_convert_fusion.21), channel_id=1, source_target_pairs={{0,0},{1,2},{2,1},{3,3},{4,4},{5,6},{6,5},{7,7},{8,8},{9,10},{10,9... | collective-permute-start | bytes 737288 | tf_op jit(solution)/shard_map/ppermute | solution.py:324
  78.2 8.7 %collective-permute-start.21 = (bf16[320,384]{1,0:T(8,128)(2,1)S(1)}, bf16[320,384]{1,0:T(8,128)(2,1)S(1)}, u32[]{:S(2)}, u32[]{:S(2)}) collective-permute-start(bf16[320,384]{1,0:T(8,128)(2,1)S(1)} %broadcast_select_fusion.16), channel_id=1, source_target_pairs={{0,1},{1,0},{2,3},{3,2},{4,5},{5,4},{6,7},{7,6},{8,9},{9,8},{10,11... | collective-permute-start | bytes 737288 | tf_op jit(solution)/shard_map/ppermute | solution.py:318
  87.0 6.7 %collective-permute-start.22 = (bf16[320,384]{1,0:T(8,128)(2,1)S(1)}, bf16[320,384]{1,0:T(8,128)(2,1)S(1)}, u32[]{:S(2)}, u32[]{:S(2)}) collective-permute-start(bf16[320,384]{1,0:T(8,128)(2,1)S(1)} %add_convert_fusion.18), channel_id=1, source_target_pairs={{0,0},{1,2},{2,1},{3,3},{4,4},{5,6},{6,5},{7,7},{8,8},{9,10},{10,9... | collective-permute-start | bytes 737288 | tf_op jit(solution)/shard_map/ppermute | solution.py:324
  87.7 17.4 %collective-permute-start.17 = (bf16[640,384]{1,0:T(8,128)(2,1)S(1)}, bf16[640,384]{1,0:T(8,128)(2,1)S(1)}, u32[]{:S(2)}, u32[]{:S(2)}) collective-permute-start(bf16[640,384]{1,0:T(8,128)(2,1)S(1)} %get-tuple-element.84), channel_id=1, source_target_pairs={{0,16},{16,0},{1,17},{17,1},{2,18},{18,2},{3,19},{19,3},{4,20},{20... | collective-permute-start | bytes 1474568 | tf_op jit(solution)/shard_map/ppermute | solution.py:26
  88.3 11.9 %collective-permute-start.20 = (bf16[320,384]{1,0:T(8,128)(2,1)S(1)}, bf16[320,384]{1,0:T(8,128)(2,1)S(1)}, u32[]{:S(2)}, u32[]{:S(2)}) collective-permute-start(bf16[320,384]{1,0:T(8,128)(2,1)S(1)} %broadcast_select_fusion.15), channel_id=1, source_target_pairs={{0,1},{1,0},{2,3},{3,2},{4,5},{5,4},{6,7},{7,6},{8,9},{9,8},{10,11... | collective-permute-start | bytes 737288 | tf_op jit(solution)/shard_map/ppermute | solution.py:318
  93.7 33.9 %copy-start.8 = (bf16[1536,640]{1,0:T(8,128)(2,1)S(1)}, bf16[1536,640]{1,0:T(8,128)(2,1)}, u32[]{:S(2)}) copy-start(bf16[1536,640]{1,0:T(8,128)(2,1)} %refs_8_.3) | copy-start | bytes 5898244
  100.3 4.9 %collective-permute-start.23 = (bf16[320,384]{1,0:T(8,128)(2,1)S(1)}, bf16[320,384]{1,0:T(8,128)(2,1)S(1)}, u32[]{:S(2)}, u32[]{:S(2)}) collective-permute-start(bf16[320,384]{1,0:T(8,128)(2,1)S(1)} %add_convert_fusion.15), channel_id=1, source_target_pairs={{0,0},{1,2},{2,1},{3,3},{4,4},{5,6},{6,5},{7,7},{8,8},{9,10},{10,9... | collective-permute-start | bytes 737288 | tf_op jit(solution)/shard_map/ppermute | solution.py:324
  101.0 8.3 %collective-permute-start.25 = (bf16[320,384]{1,0:T(8,128)(2,1)S(1)}, bf16[320,384]{1,0:T(8,128)(2,1)S(1)}, u32[]{:S(2)}, u32[]{:S(2)}) collective-permute-start(bf16[320,384]{1,0:T(8,128)(2,1)S(1)} %broadcast_select_fusion.14), channel_id=1, source_target_pairs={{0,1},{1,0},{2,3},{3,2},{4,5},{5,4},{6,7},{7,6},{8,9},{9,8},{10,11... | collective-permute-start | bytes 737288 | tf_op jit(solution)/shard_map/ppermute | solution.py:318
  109.4 8.0 %collective-permute-start.26 = (bf16[320,384]{1,0:T(8,128)(2,1)S(1)}, bf16[320,384]{1,0:T(8,128)(2,1)S(1)}, u32[]{:S(2)}, u32[]{:S(2)}) collective-permute-start(bf16[320,384]{1,0:T(8,128)(2,1)S(1)} %add_convert_fusion.12), channel_id=1, source_target_pairs={{0,0},{1,2},{2,1},{3,3},{4,4},{5,6},{6,5},{7,7},{8,8},{9,10},{10,9... | collective-permute-start | bytes 737288 | tf_op jit(solution)/shard_map/ppermute | solution.py:324
  110.0 17.6 %collective-permute-start.27 = (bf16[512,384]{1,0:T(8,128)(2,1)}, bf16[512,384]{1,0:T(8,128)(2,1)S(1)}, u32[]{:S(2)}, u32[]{:S(2)}) collective-permute-start(bf16[512,384]{1,0:T(8,128)(2,1)} %get-tuple-element.99.refs_0_), channel_id=1, source_target_pairs={{0,4},{4,0},{8,12},{12,8},{1,5},{5,1},{9,13},{13,9},{2,6},{6,2},{1... | collective-permute-start | bytes 1179656 | tf_op jit(solution)/shard_map/ppermute | solution.py:26
  110.1 17.5 %collective-permute-start.28 = (bf16[512,384]{1,0:T(8,128)(2,1)}, bf16[512,384]{1,0:T(8,128)(2,1)S(1)}, u32[]{:S(2)}, u32[]{:S(2)}) collective-permute-start(bf16[512,384]{1,0:T(8,128)(2,1)} %collective-permute-done.10.refs_1_), channel_id=1, source_target_pairs={{0,4},{4,0},{8,12},{12,8},{1,5},{5,1},{9,13},{13,9},{2,6},{6,2},{1... | collective-permute-start | bytes 1179656 | tf_op jit(solution)/shard_map/ppermute | solution.py:26
  110.7 21.2 %collective-permute-start.29 = (bf16[640,384]{1,0:T(8,128)(2,1)S(1)}, bf16[640,384]{1,0:T(8,128)(2,1)S(1)}, u32[]{:S(2)}, u32[]{:S(2)}) collective-permute-start(bf16[640,384]{1,0:T(8,128)(2,1)S(1)} %get-tuple-element.103), channel_id=1, source_target_pairs={{0,16},{16,0},{1,17},{17,1},{2,18},{18,2},{3,19},{19,3},{4,20},{20... | collective-permute-start | bytes 1474568 | tf_op jit(solution)/shard_map/ppermute | solution.py:26
  112.3 11.0 %collective-permute-start.24 = (bf16[320,384]{1,0:T(8,128)(2,1)S(1)}, bf16[320,384]{1,0:T(8,128)(2,1)S(1)}, u32[]{:S(2)}, u32[]{:S(2)}) collective-permute-start(bf16[320,384]{1,0:T(8,128)(2,1)S(1)} %broadcast_select_fusion.13), channel_id=1, source_target_pairs={{0,1},{1,0},{2,3},{3,2},{4,5},{5,4},{6,7},{7,6},{8,9},{9,8},{10,11... | collective-permute-start | bytes 737288 | tf_op jit(solution)/shard_map/ppermute | solution.py:318
  123.4 8.5 %collective-permute-start.31 = (bf16[320,384]{1,0:T(8,128)(2,1)S(1)}, bf16[320,384]{1,0:T(8,128)(2,1)S(1)}, u32[]{:S(2)}, u32[]{:S(2)}) collective-permute-start(bf16[320,384]{1,0:T(8,128)(2,1)S(1)} %add_convert_fusion.9), channel_id=1, source_target_pairs={{0,0},{1,2},{2,1},{3,3},{4,4},{5,6},{6,5},{7,7},{8,8},{9,10},{10,9... | collective-permute-start | bytes 737288 | tf_op jit(solution)/shard_map/ppermute | solution.py:324
  124.3 8.1 %collective-permute-start.30 = (bf16[320,384]{1,0:T(8,128)(2,1)S(1)}, bf16[320,384]{1,0:T(8,128)(2,1)S(1)}, u32[]{:S(2)}, u32[]{:S(2)}) collective-permute-start(bf16[320,384]{1,0:T(8,128)(2,1)S(1)} %broadcast_select_fusion.12), channel_id=1, source_target_pairs={{0,1},{1,0},{2,3},{3,2},{4,5},{5,4},{6,7},{7,6},{8,9},{9,8},{10,11... | collective-permute-start | bytes 737288 | tf_op jit(solution)/shard_map/ppermute | solution.py:318
  132.5 5.5 %collective-permute-start.32 = (bf16[320,384]{1,0:T(8,128)(2,1)S(1)}, bf16[320,384]{1,0:T(8,128)(2,1)S(1)}, u32[]{:S(2)}, u32[]{:S(2)}) collective-permute-start(bf16[320,384]{1,0:T(8,128)(2,1)S(1)} %add_convert_fusion.6), channel_id=1, source_target_pairs={{0,0},{1,2},{2,1},{3,3},{4,4},{5,6},{6,5},{7,7},{8,8},{9,10},{10,9... | collective-permute-start | bytes 737288 | tf_op jit(solution)/shard_map/ppermute | solution.py:324
  133.3 8.9 %collective-permute-start.34 = (bf16[320,384]{1,0:T(8,128)(2,1)S(1)}, bf16[320,384]{1,0:T(8,128)(2,1)S(1)}, u32[]{:S(2)}, u32[]{:S(2)}) collective-permute-start(bf16[320,384]{1,0:T(8,128)(2,1)S(1)} %broadcast_select_fusion.10), channel_id=1, source_target_pairs={{0,1},{1,0},{2,3},{3,2},{4,5},{5,4},{6,7},{7,6},{8,9},{9,8},{10,11... | collective-permute-start | bytes 737288 | tf_op jit(solution)/shard_map/ppermute | solution.py:318
  142.3 4.4 %collective-permute-start.35 = (bf16[320,384]{1,0:T(8,128)(2,1)S(1)}, bf16[320,384]{1,0:T(8,128)(2,1)S(1)}, u32[]{:S(2)}, u32[]{:S(2)}) collective-permute-start(bf16[320,384]{1,0:T(8,128)(2,1)S(1)} %add_convert_fusion.3), channel_id=1, source_target_pairs={{0,0},{1,2},{2,1},{3,3},{4,4},{5,6},{6,5},{7,7},{8,8},{9,10},{10,9... | collective-permute-start | bytes 737288 | tf_op jit(solution)/shard_map/ppermute | solution.py:324
  143.1 7.8 %collective-permute-start.33 = (bf16[320,384]{1,0:T(8,128)(2,1)S(1)}, bf16[320,384]{1,0:T(8,128)(2,1)S(1)}, u32[]{:S(2)}, u32[]{:S(2)}) collective-permute-start(bf16[320,384]{1,0:T(8,128)(2,1)S(1)} %broadcast_select_fusion.9), channel_id=1, source_target_pairs={{0,1},{1,0},{2,3},{3,2},{4,5},{5,4},{6,7},{7,6},{8,9},{9,8},{10,11... | collective-permute-start | bytes 737288 | tf_op jit(solution)/shard_map/ppermute | solution.py:318
  150.9 8.0 %collective-permute-start.37 = (bf16[320,384]{1,0:T(8,128)(2,1)S(1)}, bf16[320,384]{1,0:T(8,128)(2,1)S(1)}, u32[]{:S(2)}, u32[]{:S(2)}) collective-permute-start(bf16[320,384]{1,0:T(8,128)(2,1)S(1)} %add_convert_fusion.1), channel_id=1, source_target_pairs={{0,0},{1,2},{2,1},{3,3},{4,4},{5,6},{6,5},{7,7},{8,8},{9,10},{10,9... | collective-permute-start | bytes 737288 | tf_op jit(solution)/shard_map/ppermute | solution.py:324
  151.7 9.9 %collective-permute-start.36 = (bf16[320,384]{1,0:T(8,128)(2,1)S(1)}, bf16[320,384]{1,0:T(8,128)(2,1)S(1)}, u32[]{:S(2)}, u32[]{:S(2)}) collective-permute-start(bf16[320,384]{1,0:T(8,128)(2,1)S(1)} %add_convert_fusion.2), channel_id=1, source_target_pairs={{0,1},{1,0},{2,3},{3,2},{4,5},{5,4},{6,7},{7,6},{8,9},{9,8},{10,11... | collective-permute-start | bytes 737288 | tf_op jit(solution)/shard_map/ppermute | solution.py:318
  159.1 6.3 %collective-permute-start.38 = (bf16[320,384]{1,0:T(8,128)(2,1)S(1)}, bf16[320,384]{1,0:T(8,128)(2,1)S(1)}, u32[]{:S(2)}, u32[]{:S(2)}) collective-permute-start(bf16[320,384]{1,0:T(8,128)(2,1)S(1)} %add_convert_fusion), channel_id=1, source_target_pairs={{0,1},{1,0},{2,3},{3,2},{4,5},{5,4},{6,7},{7,6},{8,9},{9,8},{10,11... | collective-permute-start | bytes 737288 | tf_op jit(solution)/shard_map/ppermute | solution.py:318
  (8 other events, 7.9 us)

commit v7 on v6

--- a/solution.py
+++ b/solution.py
@@ -32,34 +32,24 @@
     return jnp.where(keep, rows, 0.0).T[0:depth, :].astype(BF16)
 
 
-def conv_rows(offsets, me, x_refs, halo_refs, w_ref, rows_scr, y_scr, w_scr, sems):
+def conv_rows(offsets, me, x_refs, halo_refs, w_ref, rows_scr, y_scr):
     taps, width = w_ref.shape[0], w_ref.shape[2]
     length = x_refs[0].shape[1]
-    depth = w_scr.shape[1] // len(offsets)
-
-    def copies(k):
-        return [
-            pltpu.make_async_copy(
-                w_ref.at[k, pl.ds(pl.multiple_of((me ^ off) * depth, 16), depth), :],
-                w_scr.at[k, j * depth : (j + 1) * depth, :],
-                sems.at[k, j],
-            )
-            for j, off in enumerate(offsets)
-        ]
-
-    for k in range(taps):
-        for copy in copies(k):
-            copy.start()
     x = jnp.concatenate([ref[...] for ref in x_refs], axis=0)
+    depth = x.shape[0] // len(offsets)
     halo = jnp.concatenate([edge_block(ref, depth) for ref in halo_refs], axis=0)
     rows_scr[0:length, :] = x.T
     rows_scr[length : length + 16, :] = halo.T[0:16]
+    starts = [pl.multiple_of((me ^ off) * depth, 16) for off in offsets]
     for first in range(0, taps, 2):
         group = range(first, min(first + 2, taps))
-        for k in group:
-            for copy in copies(k):
-                copy.wait()
-        w = jnp.concatenate([w_scr[k] for k in group], axis=1)
+        w = jnp.concatenate(
+            [
+                jnp.concatenate([w_ref[k, pl.ds(s, depth), :] for s in starts], axis=0)
+                for k in group
+            ],
+            axis=1,
+        )
         y = jnp.dot(rows_scr[...], w, preferred_element_type=F32)
         for c in range(w.shape[1] // LANES):
             part = y[:, c * LANES : (c + 1) * LANES]
@@ -80,9 +70,9 @@
 
 def first_kernel(offsets, idx_ref, *refs):
     n = len(offsets)
-    *x_refs, w_ref, even_ref, odd_ref, rows_scr, y_scr, w_scr, sems = refs
+    *x_refs, w_ref, even_ref, odd_ref, rows_scr, y_scr = refs
     x_refs, halo_refs = x_refs[:-n], x_refs[-n:]
-    conv_rows(offsets, idx_ref[0], x_refs, halo_refs, w_ref, rows_scr, y_scr, w_scr, sems)
+    conv_rows(offsets, idx_ref[0], x_refs, halo_refs, w_ref, rows_scr, y_scr)
     taps, width = w_ref.shape[0], w_ref.shape[2]
     half = even_ref.shape[0]
     step = min(64, half)
@@ -97,11 +87,11 @@
 def second_kernel(offsets, far, per, idx_ref, *refs):
     n = len(offsets)
     blocks, pays, refs = refs[:n], refs[n : 2 * n], refs[2 * n :]
-    w_ref, even_ref, odd_ref, grad_ref, enc_ref, pre_ref, *sent_refs = refs[:-7]
-    rows_scr, y_scr, w_scr, sems, p_scr, x_scr, edge_scr = refs[-7:]
+    w_ref, even_ref, odd_ref, grad_ref, enc_ref, pre_ref, *sent_refs = refs[:-5]
+    rows_scr, y_scr, p_scr, x_scr, edge_scr = refs[-5:]
     me = idx_ref[0]
     pick = lambda items: [items[j] for j in far]
-    conv_rows(pick(offsets), me, pick(blocks), pick(pays), w_ref, rows_scr, y_scr, w_scr, sems)
+    conv_rows(pick(offsets), me, pick(blocks), pick(pays), w_ref, rows_scr, y_scr)
     taps, width = w_ref.shape[0], w_ref.shape[2]
     half = even_ref.shape[0]
     step = min(64, half)
@@ -213,19 +203,20 @@
     out_ref[...] = total.astype(BF16)
 
 
-def call(kernel, out, scratch, mib, idx, *arrays, far_off=()):
+def call(kernel, out, scratch, mib, idx, *arrays):
     vmem = pl.BlockSpec(memory_space=pltpu.VMEM)
-    held = [j for j, a in enumerate(arrays) if any(v is a for v in far_off)]
-    arrays = [pltpu.with_memory_space_constraint(a, pltpu.HBM) if j in held else a for j, a in enumerate(arrays)]
-    specs = [pl.BlockSpec(memory_space=pltpu.HBM) if j in held else vmem for j in range(len(arrays))]
     return pl.pallas_call(
         kernel,
         out_shape=out,
-        in_specs=[pl.BlockSpec(memory_space=pltpu.SMEM)] + specs,
+        in_specs=[pl.BlockSpec(memory_space=pltpu.SMEM)] + [vmem] * len(arrays),
         out_specs=jax.tree.map(lambda _: vmem, out),
         scratch_shapes=scratch,
         compiler_params=pltpu.CompilerParams(vmem_limit_bytes=mib * 1024 * 1024),
     )(idx, *arrays)
+
+
+def pinned(value):
+    return pltpu.with_memory_space_constraint(value, pltpu.VMEM)
 
 
 def after(value, *others):
@@ -304,16 +295,13 @@
     middle_pairs = [(0, 0), (1, 2), (2, 1), (3, 3)]
     last = None
     h, p, s, outer, middle, sums = {}, {}, {}, {}, {}, {}
-    for r in range(count + 3):
-        if r - 2 in middle:
-            got = after(middle.pop(r - 2), last)
-            last = s[r - 2] = lax.optimization_barrier(added(p[r - 2], got))
+    for r in range(count + 5):
         if r < count:
             last = h[r] = part(r, last)
-        if r < count + 2:
-            value = h.get(r, s.get(r - 2))
-            if r in h and r - 2 in s:
-                value = jnp.where(end, h[r], s[r - 2])
+        if r < count + 3:
+            value = h.get(r, s.get(r - 3))
+            if r in h and r - 3 in s:
+                value = jnp.where(end, h[r], s[r - 3])
             last = value = lax.optimization_barrier(value)
             outer[r] = lax.ppermute(value, "dp", outer_pairs)
             last = sent(r, last)
@@ -322,10 +310,14 @@
             if r - 1 < count:
                 last = p[r - 1] = lax.optimization_barrier(added(h[r - 1], got))
                 middle[r - 1] = lax.ppermute(last, "dp", middle_pairs)
-            if r >= 3:
-                sums[r - 3] = jnp.where(end, got, s[r - 3])
-            if r - 1 < count:
-                last = idle(r - 1, last, sums)
+            if r >= 4:
+                sums[r - 4] = lax.optimization_barrier(jnp.where(end, got, s[r - 4]))
+                if r - 1 >= count:
+                    last = sums[r - 4]
+            last = idle(r - 1, last, sums)
+        if r - 2 in middle:
+            got = after(middle.pop(r - 2), last)
+            last = s[r - 2] = lax.optimization_barrier(added(p[r - 2], got))
     return [sums[c] for c in range(count)]
 
 
@@ -347,14 +339,14 @@
     scratch = lambda at: [
         pltpu.VMEM((length + 16, len(at) * depth), BF16),
         pltpu.VMEM((taps * width // LANES, length + 2 * EDGE, LANES), F32),
-        pltpu.VMEM((taps, len(at) * depth, width), BF16),
-        pltpu.SemaphoreType.DMA((taps, len(at))),
     ]
 
     blocks = [x]
     for bit in bits[:-1]:
-        blocks = blocks + [swap(b, "mp", bit) for b in blocks]
-    own = swap(x, "mp", bits[-1])
+        blocks = blocks + [pinned(swap(b, "mp", bit)) for b in blocks]
+    own = pinned(swap(x, "mp", bits[-1]))
+    weight = pinned(conv_weight)
+    near_x = pinned(x)
     edges = edge_rows(x, width)
     payload = jnp.concatenate([edges, norm_gain.reshape(1, -1), jnp.zeros((3, width), F32)], axis=0)
     payloads = [payload] + [swap(payload, "mp", o) for o in offsets[1:]]
@@ -365,11 +357,11 @@
         (part, part),
         scratch(near),
         24,
-        idx, x, own, *pick(payloads, near), conv_weight,
-        far_off=(conv_weight,),
+        idx, near_x, own, *pick(payloads, near), weight,
     )
     hold = [even] + pick(payloads, far)
-    blocks = blocks + [own] + [swap(after(b, *hold), "mp", bits[-1]) for b in blocks[1:]]
+    blocks = blocks + [own] + [pinned(swap(after(b, *hold), "mp", bits[-1])) for b in blocks[1:]]
+    blocks[0] = near_x
     pair = shards == 2 and peers % shards == 0 and lax.axis_size("dp") == 4
     per = peers // shards if pair else 0
     piece = jax.ShapeDtypeStruct((depth, width), BF16)
@@ -387,8 +379,7 @@
             pltpu.VMEM((LANES, width), F32),
         ],
         26,
-        idx, *blocks, *payloads, conv_weight, even, odd, encoder_grad[0],
-        far_off=(conv_weight,),
+        idx, *blocks, *payloads, weight, even, odd, encoder_grad[0],
     )
     encs = [encoded]
     for bit in bits[:-1]:
@@ -447,6 +438,8 @@
 
     work((0,), [])
     launch(0, [])
+    work((1,), [keep[-1]])
+    launch(1, [])
 
     def share(c, last):
         tap, row = c // per, c % per
@@ -455,36 +448,31 @@
         return added(keep[tap][rows], value if last is None else after(value, last))
 
     def sent(r, last):
-        if r == 0:
-            work(tuple(range(1, min(3, taps))), [last])
-            launch(1, [])
+        return last
+
+    def idle(c, last, sums):
+        if c % per == 0 and c // per + 2 < taps:
+            tap = c // per + 2
+            work((tap,), [last] + (encs[1:] if tap == 2 else []))
+            launch(tap, [])
             last = keep[-1]
-        return last
-
-    def idle(c, last, sums):
-        if c == 0:
-            work(tuple(range(3, taps)), [last] + encs[1:])
-            last = keep[-1]
-        if c == 1:
+        if c == per - 1:
             relays.extend([swap(after(e, last), "mp", bits[-1]) for e in encs])
-        if c % per == 0 and c // per + 2 < taps:
-            launch(c // per + 2, [last])
-        if c == chunks - 4:
+        if c == chunks - 2:
             last = done["qkv"] = qkv_call(after(idx, last, *relays), encs + relays)
-        if c == chunks - 1:
-            early = (len(sums) // per) if len(sums) >= per * (taps - 1) else 0
-            if early:
-                parts = [sums[i] for i in range(early * per)]
-                parts[0] = after(parts[0], last)
-                last = done["early"] = written(parts, early, 0, None, (taps, per * depth, width))
+        if c == chunks:
+            early = len(sums) // per
+            parts = [sums[i] for i in range(early * per)]
+            parts[0] = after(parts[0], last)
+            last = done["early"] = written(parts, early, 0, None, (taps, per * depth, width))
+            done["at"] = early
         return last
 
     sums = chain_sums(chunks, share, sent, idle)
     shape = (taps, per * depth, width)
-    if "early" in done:
-        conv_grad = written(sums[(taps - 1) * per :], 1, taps - 1, done["early"], shape)
-    else:
-        conv_grad = written(sums, taps, 0, None, shape)
+    conv_grad, early = done["early"], done["at"]
+    for k in range(early, taps):
+        conv_grad = written(sums[k * per : (k + 1) * per], 1, k, conv_grad, shape)
     return (done["qkv"][None], jnp.swapaxes(conv_grad, 0, 1))
 
 

time: 167 us -> 141 us (0.84)
  waiting for transfers between devices: 43.7 us -> 31.7 us
  starting transfers between devices: 71.5 us -> 60.8 us
  Pallas kernels: 34.3 us -> 31 us
  other arithmetic: 7.33 us -> 5.56 us
    ppermute x12 -> x13, waiting for transfers between devices: 33 us -> 11 us  [chain_sums(): outer[r] = lax.ppermute(value, 'dp', outer_pairs)]
    ppermute x17, waiting for transfers between devices: 10.7 us -> 20.7 us  [swap(): return lax.ppermute(value, axis, [(i, i ^ bit) for i in range(peers)])]
    ppermute x12 -> x13, starting transfers between devices: 44.7 us -> 35.7 us  [chain_sums(): outer[r] = lax.ppermute(value, 'dp', outer_pairs)]
    pallas_call x6 -> x8, Pallas kernels: 31 us -> 27.7 us  [call(): pl.pallas_call(kernel, out_shape=out, in_specs=[pl.BlockSpec(memory_space...]
    ppermute x10, starting transfers between devices: 9.85 us -> 6.98 us  [chain_sums(): middle[r - 1] = lax.ppermute(last, 'dp', middle_pairs)]
    unnamed x34 -> x28, local copies, waits for them, and re-layouts: 7.5 us -> 8.96 us
    convert_element_type x22 -> x23, other arithmetic: 5.14 us -> 4.4 us  [added(): return (a.astype(F32) + b.astype(F32)).astype(BF16)]
  transfers between devices with their start and end apart: 39 -> 40, of which waited for: 15 -> 14; matrix products, arithmetic and copies ran while one was open for 5% -> 5% of each run, Pallas kernels for 15% -> 17%
where the time goes in v7:
time: 141 us; the launch traced here: 140 us
  starting transfers between devices  60.8 us (43%)
  waiting for transfers between devices  31.7 us (22%)
  Pallas kernels  31 us (22%)
  local copies, waits for them, and re-layouts  9.87 us (7%)
  other arithmetic  5.56 us (4%)
    ppermute x13, starting transfers between devices, chain_sums(): outer[r] = lax.ppermute(value, 'dp', outer_pairs)  35.7 us
    pallas_call x8, Pallas kernels, call(): pl.pallas_call(kernel, out_shape=out, in_specs=[pl.BlockSpec(memory_space...  27.7 us
    ppermute x17, waiting for transfers between devices, swap(): return lax.ppermute(value, axis, [(i, i ^ bit) for i in range(peers)])  20.7 us
    ppermute x17, starting transfers between devices, swap(): return lax.ppermute(value, axis, [(i, i ^ bit) for i in range(peers)])  18 us
    ppermute x13, waiting for transfers between devices, chain_sums(): outer[r] = lax.ppermute(value, 'dp', outer_pairs)  11 us
    unnamed x28, local copies, waits for them, and re-layouts  8.96 us
    ppermute x10, starting transfers between devices, chain_sums(): middle[r - 1] = lax.ppermute(last, 'dp', middle_pairs)  6.98 us
    convert_element_type x23, other arithmetic, added(): return (a.astype(F32) + b.astype(F32)).astype(BF16)  4.4 us
  transfers between devices with their start and end apart: 40, of which 14 were waited for; matrix products, arithmetic and copies ran while one was open for 5% of the time, Pallas kernels for 17%

profile of v7, /device:TPU:0, one launch (start us, length us, event | category | flops | bytes accessed | tf_op | source)
XLA Modules:
  0.0 140.1 jit_solution(13779478504096877545)
XLA Ops:
  1.1 2.6 %collective-permute-start = (bf16[320,1024]{1,0:T(8,128)(2,1)}, bf16[320,1024]{1,0:T(8,128)(2,1)S(1)}, u32[]{:S(2)}, u32[]{:S(2)}) collective-permute-start(bf16[320,1024]{1,0:T(8,128)(2,1)} %bitcast.9), channel_id=1, source_target_pairs={{0,8},{4,12},{8,0},{12,4},{1,9},{5,13},{9,1},{13,5},{2,10},{6,14},... | collective-permute-start | bytes 1966088 | tf_op jit(solution)/shard_map/ppermute | solution.py:26
  3.7 1.1 copy-done
  5.0 1.6 %collective-permute-start.2 = (f32[8,384]{1,0:T(8,128)S(1)}, f32[8,384]{1,0:T(8,128)S(1)}, u32[]{:S(2)}, u32[]{:S(2)}) collective-permute-start(f32[8,384]{1,0:T(8,128)S(1)} %shard_map.68), channel_id=1, source_target_pairs={{0,16},{16,0},{1,17},{17,1},{2,18},{18,2},{3,19},{19,3},{4,20},{20... | collective-permute-start | bytes 36872 | tf_op jit(solution)/shard_map/ppermute | solution.py:26
  7.3 1.4 %collective-permute-done.2 = f32[8,384]{1,0:T(8,128)S(1)} collective-permute-done((f32[8,384]{1,0:T(8,128)S(1)}, f32[8,384]{1,0:T(8,128)S(1)}, u32[]{:S(2)}, u32[]{:S(2)}) %collective-permute-start.2) | collective-permute-done | bytes 12320 | tf_op jit(solution)/shard_map/ppermute | solution.py:26
  8.9 0.9 collective-permute-start.4
  9.8 0.9 collective-permute-start.3
  11.6 1.1 copy-done.1
  12.7 2.4 %copy-done.8 = bf16[5,1280,384]{2,1,0:T(8,128)(2,1)S(1)} copy-done((bf16[5,1280,384]{2,1,0:T(8,128)(2,1)S(1)}, bf16[5,1280,384]{2,1,0:T(8,128)(2,1)}, u32[]{:S(2)}) %copy-start.8) | copy-done | bytes 4915224
  15.1 4.3 %shard_map.69 = (f32[512,384]{1,0:T(8,128)S(1)}, f32[512,384]{1,0:T(8,128)S(1)}) custom-call(s32[2]{0:T(128)S(1)} %pad_add_fusion.idx_ref, bf16[320,1024]{1,0:T(8,128)(2,1)S(1)} %bitcast.12, bf16[320,1024]{1,0:T(8,128)(2,1)S(1)} %collective-permute-done.1.refs_1_.refs_2_, f32[8,384]{1,0:T(8,128)S(1)} %maximum_maximum_fusion.refs_2_.refs_4_, ...), custom_call_target="tpu_custom_call" | custom-call | tf_op jit(solution)/shard_map/pallas_call | solution.py:208
  20.6 1.3 collective-permute-done.6.refs_3_
  21.9 1.3 copy-done.4
  23.2 6.4 %shard_map.70 = (bf16[512,384]{1,0:T(8,128)(2,1)S(1)}, f32[1040,384]{1,0:T(8,128)S(1)}, bf16[320,384]{1,0:T(8,128)(2,1)S(1)}) custom-call(s32[2]{0:T(128)S(1)} %pad_add_fusion.idx_ref, bf16[320,1024]{1,0:T(8,128)(2,1)S(1)} %bitcast.13, bf16[320,1024]{1,0:T(8,128)(2,1)S(1)} %copy-done.4, bf16[320,1024]{1,0:T(8,128)(2,1)S(1)} %collective-permute-done.1.refs_1_.refs_2_, ...), custom_call_target="tpu_custom_call" | custom-call | tf_op jit(solution)/shard_map/pallas_call | solution.py:208
  29.7 1.8 %collective-permute-start.7 = (bf16[320,384]{1,0:T(8,128)(2,1)S(1)}, bf16[320,384]{1,0:T(8,128)(2,1)S(1)}, u32[]{:S(2)}, u32[]{:S(2)}) collective-permute-start(bf16[320,384]{1,0:T(8,128)(2,1)S(1)} %get-tuple-element.64), channel_id=1, source_target_pairs={{0,16},{16,0},{1,17},{17,1},{2,18},{18,2},{3,19},{19,3},{4,20},{20... | collective-permute-start | bytes 737288 | tf_op jit(solution)/shard_map/ppermute | solution.py:26
  31.4 3.4 %shard_map.71 = (bf16[640,384]{1,0:T(8,128)(2,1)S(1)}, bf16[320,384]{1,0:T(8,128)(2,1)}) custom-call(s32[2]{0:T(128)S(1)} %pad_add_fusion.idx_ref, bf16[320,1024]{1,0:T(8,128)(2,1)S(1)} %bitcast.14, bf16[320,1024]{1,0:T(8,128)(2,1)S(1)} %copy-done.4, bf16[320,1024]{1,0:T(8,128)(2,1)S(1)} %collective-permute-done.1.refs_1_.refs_2_, ...), custom_call_target="tpu_custom_call" | custom-call | tf_op jit(solution)/shard_map/pallas_call | solution.py:208
  35.1 2.8 %collective-permute-done.7 = bf16[320,384]{1,0:T(8,128)(2,1)S(1)} collective-permute-done((bf16[320,384]{1,0:T(8,128)(2,1)S(1)}, bf16[320,384]{1,0:T(8,128)(2,1)S(1)}, u32[]{:S(2)}, u32[]{:S(2)}) %collective-permute-start.7) | collective-permute-done | bytes 245792 | tf_op jit(solution)/shard_map/ppermute | solution.py:26
  38.7 2.1 %collective-permute-start.8 = (bf16[320,384]{1,0:T(8,128)(2,1)}, bf16[320,384]{1,0:T(8,128)(2,1)}, u32[]{:S(2)}, u32[]{:S(2)}) collective-permute-start(bf16[320,384]{1,0:T(8,128)(2,1)} %add_convert_fusion.29), channel_id=1, source_target_pairs={{0,1},{1,0},{2,3},{3,2},{4,5},{5,4},{6,7},{7,6},{8,9},{9,8},{10,11... | collective-permute-start | bytes 737288 | tf_op jit(solution)/shard_map/ppermute | solution.py:306
  40.7 1.5 %collective-permute-start.10 = (bf16[512,384]{1,0:T(8,128)(2,1)}, bf16[512,384]{1,0:T(8,128)(2,1)S(1)}, u32[]{:S(2)}, u32[]{:S(2)}) collective-permute-start(bf16[512,384]{1,0:T(8,128)(2,1)} %copy-done.12), channel_id=1, source_target_pairs={{0,8},{4,12},{8,0},{12,4},{1,9},{5,13},{9,1},{13,5},{2,10},{6,14},... | collective-permute-start | bytes 1179656 | tf_op jit(solution)/shard_map/ppermute | solution.py:26
  42.2 1.1 copy-done.5
  43.3 1.1 copy-done.7
  44.4 2.5 %shard_map.73 = (bf16[640,384]{1,0:T(8,128)(2,1)S(1)}, bf16[320,384]{1,0:T(8,128)(2,1)S(1)}, bf16[320,384]{1,0:T(8,128)(2,1)S(1)}) custom-call(s32[2]{0:T(128)S(1)} %pad_add_fusion.idx_ref, bf16[320,1024]{1,0:T(8,128)(2,1)S(1)} %bitcast.15, bf16[320,1024]{1,0:T(8,128)(2,1)S(1)} %copy-done.5, bf16[320,1024]{1,0:T(8,128)(2,1)S(1)} %collective-permute-done.1.refs_1_.refs_2_, ...), custom_call_target="tpu_custom_call" | custom-call | tf_op jit(solution)/shard_map/pallas_call | solution.py:208
  46.9 2.0 %collective-permute-start.13 = (bf16[320,384]{1,0:T(8,128)(2,1)S(1)}, bf16[320,384]{1,0:T(8,128)(2,1)S(1)}, u32[]{:S(2)}, u32[]{:S(2)}) collective-permute-start(bf16[320,384]{1,0:T(8,128)(2,1)S(1)} %get-tuple-element.74), channel_id=1, source_target_pairs={{0,16},{16,0},{1,17},{17,1},{2,18},{18,2},{3,19},{19,3},{4,20},{20... | collective-permute-start | bytes 737288 | tf_op jit(solution)/shard_map/ppermute | solution.py:26
  49.0 1.0 add_convert_fusion.28
  50.6 1.1 add_convert_fusion.27
  52.4 2.5 %shard_map.72 = (bf16[640,384]{1,0:T(8,128)(2,1)S(1)}, bf16[640,384]{1,0:T(8,128)(2,1)S(1)}) custom-call(s32[2]{0:T(128)S(1)} %pad_add_fusion.idx_ref, bf16[320,1024]{1,0:T(8,128)(2,1)S(1)} %bitcast.16, bf16[320,1024]{1,0:T(8,128)(2,1)S(1)} %copy-done.5, bf16[320,1024]{1,0:T(8,128)(2,1)S(1)} %collective-permute-done.1.refs_1_.refs_2_, ...), custom_call_target="tpu_custom_call" | custom-call | tf_op jit(solution)/shard_map/pallas_call | solution.py:208
  54.9 0.9 collective-permute-done.13
  57.1 4.8 %collective-permute-start.15 = (bf16[320,384]{1,0:T(8,128)(2,1)S(1)}, bf16[320,384]{1,0:T(8,128)(2,1)S(1)}, u32[]{:S(2)}, u32[]{:S(2)}) collective-permute-start(bf16[320,384]{1,0:T(8,128)(2,1)S(1)} %add_convert_fusion.26), channel_id=1, source_target_pairs={{0,1},{1,0},{2,3},{3,2},{4,5},{5,4},{6,7},{7,6},{8,9},{9,8},{10,11... | collective-permute-start | bytes 737288 | tf_op jit(solution)/shard_map/ppermute | solution.py:306
  62.5 2.0 %collective-permute-start.11 = (bf16[640,384]{1,0:T(8,128)(2,1)S(1)}, bf16[640,384]{1,0:T(8,128)(2,1)S(1)}, u32[]{:S(2)}, u32[]{:S(2)}) collective-permute-start(bf16[640,384]{1,0:T(8,128)(2,1)S(1)} %get-tuple-element.71), channel_id=1, source_target_pairs={{0,16},{16,0},{1,17},{17,1},{2,18},{18,2},{3,19},{19,3},{4,20},{20... | collective-permute-start | bytes 1474568 | tf_op jit(solution)/shard_map/ppermute | solution.py:26
  64.5 1.8 %collective-permute-done.15 = bf16[320,384]{1,0:T(8,128)(2,1)S(1)} collective-permute-done((bf16[320,384]{1,0:T(8,128)(2,1)S(1)}, bf16[320,384]{1,0:T(8,128)(2,1)S(1)}, u32[]{:S(2)}, u32[]{:S(2)}) %collective-permute-start.15) | collective-permute-done | bytes 245792 | tf_op jit(solution)/shard_map/ppermute | solution.py:306
  66.3 2.5 %collective-permute-start.20 = (bf16[320,384]{1,0:T(8,128)(2,1)S(1)}, bf16[320,384]{1,0:T(8,128)(2,1)S(1)}, u32[]{:S(2)}, u32[]{:S(2)}) collective-permute-start(bf16[320,384]{1,0:T(8,128)(2,1)S(1)} %broadcast_select_fusion.16), channel_id=1, source_target_pairs={{0,1},{1,0},{2,3},{3,2},{4,5},{5,4},{6,7},{7,6},{8,9},{9,8},{10,11... | collective-permute-start | bytes 737288 | tf_op jit(solution)/shard_map/ppermute | solution.py:306
  68.9 2.5 %shard_map.74 = (bf16[640,384]{1,0:T(8,128)(2,1)S(1)}, bf16[640,384]{1,0:T(8,128)(2,1)S(1)}) custom-call(s32[2]{0:T(128)S(1)} %pad_add_fusion.idx_ref, bf16[320,1024]{1,0:T(8,128)(2,1)S(1)} %bitcast.17, bf16[320,1024]{1,0:T(8,128)(2,1)S(1)} %copy-done.5, bf16[320,1024]{1,0:T(8,128)(2,1)S(1)} %collective-permute-done.1.refs_1_.refs_2_, ...), custom_call_target="tpu_custom_call" | custom-call | tf_op jit(solution)/shard_map/pallas_call | solution.py:208
  72.2 3.7 %collective-permute-done.11 = bf16[640,384]{1,0:T(8,128)(2,1)S(1)} collective-permute-done((bf16[640,384]{1,0:T(8,128)(2,1)S(1)}, bf16[640,384]{1,0:T(8,128)(2,1)S(1)}, u32[]{:S(2)}, u32[]{:S(2)}) %collective-permute-start.11) | collective-permute-done | bytes 491552 | tf_op jit(solution)/shard_map/ppermute | solution.py:26
  75.9 1.7 %collective-permute-start.23 = (bf16[640,384]{1,0:T(8,128)(2,1)S(1)}, bf16[640,384]{1,0:T(8,128)(2,1)S(1)}, u32[]{:S(2)}, u32[]{:S(2)}) collective-permute-start(bf16[640,384]{1,0:T(8,128)(2,1)S(1)} %get-tuple-element.92), channel_id=1, source_target_pairs={{0,16},{16,0},{1,17},{17,1},{2,18},{18,2},{3,19},{19,3},{4,20},{20... | collective-permute-start | bytes 1474568 | tf_op jit(solution)/shard_map/ppermute | solution.py:26
  79.1 9.3 %collective-permute-done.23 = bf16[640,384]{1,0:T(8,128)(2,1)S(1)} collective-permute-done((bf16[640,384]{1,0:T(8,128)(2,1)S(1)}, bf16[640,384]{1,0:T(8,128)(2,1)S(1)}, u32[]{:S(2)}, u32[]{:S(2)}) %collective-permute-start.23) | collective-permute-done | bytes 491552 | tf_op jit(solution)/shard_map/ppermute | solution.py:26
  89.7 2.5 %shard_map.75 = (bf16[640,384]{1,0:T(8,128)(2,1)S(1)}, bf16[640,384]{1,0:T(8,128)(2,1)S(1)}) custom-call(s32[2]{0:T(128)S(1)} %pad_add_fusion.idx_ref, bf16[320,1024]{1,0:T(8,128)(2,1)S(1)} %bitcast.18, bf16[320,1024]{1,0:T(8,128)(2,1)S(1)} %copy-done.5, bf16[320,1024]{1,0:T(8,128)(2,1)S(1)} %collective-permute-done.1.refs_1_.refs_2_, ...), custom_call_target="tpu_custom_call" | custom-call | tf_op jit(solution)/shard_map/pallas_call | solution.py:208
  92.3 1.6 %collective-permute-start.21 = (bf16[640,384]{1,0:T(8,128)(2,1)S(1)}, bf16[640,384]{1,0:T(8,128)(2,1)S(1)}, u32[]{:S(2)}, u32[]{:S(2)}) collective-permute-start(bf16[640,384]{1,0:T(8,128)(2,1)S(1)} %get-tuple-element.91), channel_id=1, source_target_pairs={{0,16},{16,0},{1,17},{17,1},{2,18},{18,2},{3,19},{19,3},{4,20},{20... | collective-permute-start | bytes 1474568 | tf_op jit(solution)/shard_map/ppermute | solution.py:26
  94.8 3.8 %collective-permute-start.26 = (bf16[320,384]{1,0:T(8,128)(2,1)S(1)}, bf16[320,384]{1,0:T(8,128)(2,1)S(1)}, u32[]{:S(2)}, u32[]{:S(2)}) collective-permute-start(bf16[320,384]{1,0:T(8,128)(2,1)S(1)} %broadcast_select_fusion.13), channel_id=1, source_target_pairs={{0,1},{1,0},{2,3},{3,2},{4,5},{5,4},{6,7},{7,6},{8,9},{9,8},{10,11... | collective-permute-start | bytes 737288 | tf_op jit(solution)/shard_map/ppermute | solution.py:306
  99.6 3.2 %collective-permute-done.26 = bf16[320,384]{1,0:T(8,128)(2,1)S(1)} collective-permute-done((bf16[320,384]{1,0:T(8,128)(2,1)S(1)}, bf16[320,384]{1,0:T(8,128)(2,1)S(1)}, u32[]{:S(2)}, u32[]{:S(2)}) %collective-permute-start.26) | collective-permute-done | bytes 245792 | tf_op jit(solution)/shard_map/ppermute | solution.py:306
  102.8 2.3 %collective-permute-start.30 = (bf16[320,384]{1,0:T(8,128)(2,1)S(1)}, bf16[320,384]{1,0:T(8,128)(2,1)S(1)}, u32[]{:S(2)}, u32[]{:S(2)}) collective-permute-start(bf16[320,384]{1,0:T(8,128)(2,1)S(1)} %broadcast_select_fusion.12), channel_id=1, source_target_pairs={{0,1},{1,0},{2,3},{3,2},{4,5},{5,4},{6,7},{7,6},{8,9},{9,8},{10,11... | collective-permute-start | bytes 737288 | tf_op jit(solution)/shard_map/ppermute | solution.py:306
  106.2 4.8 %collective-permute-start.28 = (bf16[320,384]{1,0:T(8,128)(2,1)S(1)}, bf16[320,384]{1,0:T(8,128)(2,1)S(1)}, u32[]{:S(2)}, u32[]{:S(2)}) collective-permute-start(bf16[320,384]{1,0:T(8,128)(2,1)S(1)} %broadcast_select_fusion.11), channel_id=1, source_target_pairs={{0,1},{1,0},{2,3},{3,2},{4,5},{5,4},{6,7},{7,6},{8,9},{9,8},{10,11... | collective-permute-start | bytes 737288 | tf_op jit(solution)/shard_map/ppermute | solution.py:306
  112.2 5.6 %collective-permute-start.36 = (bf16[320,384]{1,0:T(8,128)(2,1)S(1)}, bf16[320,384]{1,0:T(8,128)(2,1)S(1)}, u32[]{:S(2)}, u32[]{:S(2)}) collective-permute-start(bf16[320,384]{1,0:T(8,128)(2,1)S(1)} %broadcast_select_fusion.10), channel_id=1, source_target_pairs={{0,1},{1,0},{2,3},{3,2},{4,5},{5,4},{6,7},{7,6},{8,9},{9,8},{10,11... | collective-permute-start | bytes 737288 | tf_op jit(solution)/shard_map/ppermute | solution.py:306
  118.5 3.5 %shard_map.76 = bf16[512,640]{1,0:T(8,128)(2,1)} custom-call(s32[2]{0:T(128)S(1)} %pad_add_fusion.idx_ref, bf16[512,384]{1,0:T(8,128)(2,1)S(1)} %copy-done.13, bf16[512,384]{1,0:T(8,128)(2,1)S(1)} %collective-permute-done.10.refs_1_, bf16[512,384]{1,0:T(8,128)(2,1)S(1)} %collective-permute-done.31.refs_2_, ...), custom_call_target="tpu_custom_call" | custom-call | tf_op jit(solution)/shard_map/pallas_call | solution.py:208
  122.2 2.8 %collective-permute-start.34 = (bf16[320,384]{1,0:T(8,128)(2,1)S(1)}, bf16[320,384]{1,0:T(8,128)(2,1)S(1)}, u32[]{:S(2)}, u32[]{:S(2)}) collective-permute-start(bf16[320,384]{1,0:T(8,128)(2,1)S(1)} %add_convert_fusion.3), channel_id=1, source_target_pairs={{0,1},{1,0},{2,3},{3,2},{4,5},{5,4},{6,7},{7,6},{8,9},{9,8},{10,11... | collective-permute-start | bytes 737288 | tf_op jit(solution)/shard_map/ppermute | solution.py:306
  125.9 4.2 %collective-permute-start.37 = (bf16[320,384]{1,0:T(8,128)(2,1)S(1)}, bf16[320,384]{1,0:T(8,128)(2,1)S(1)}, u32[]{:S(2)}, u32[]{:S(2)}) collective-permute-start(bf16[320,384]{1,0:T(8,128)(2,1)S(1)} %add_convert_fusion.1), channel_id=1, source_target_pairs={{0,1},{1,0},{2,3},{3,2},{4,5},{5,4},{6,7},{7,6},{8,9},{9,8},{10,11... | collective-permute-start | bytes 737288 | tf_op jit(solution)/shard_map/ppermute | solution.py:306
  130.2 2.2 %shard_map.77.b = f32[5,640,384]{2,1,0:T(8,128)} custom-call(bf16[320,384]{1,0:T(8,128)(2,1)S(1)} %broadcast_select_fusion.9.refs_0_, bf16[320,384]{1,0:T(8,128)(2,1)S(1)} %broadcast_select_fusion.7.refs_1_, bf16[320,384]{1,0:T(8,128)(2,1)S(1)} %broadcast_select_fusion.6.refs_2_, bf16[320,384]{1,0:T(8,128)(2,1)S(1)} %broadcast_select_fusion.5.refs_3_, ...), custom_call_target="tpu_custom_call" | custom-call | tf_op jit(solution)/shard_map/pallas_call | solution.py:239
  132.5 1.7 %collective-permute-start.39 = (bf16[320,384]{1,0:T(8,128)(2,1)S(1)}, bf16[320,384]{1,0:T(8,128)(2,1)S(1)}, u32[]{:S(2)}, u32[]{:S(2)}) collective-permute-start(bf16[320,384]{1,0:T(8,128)(2,1)S(1)} %add_convert_fusion), channel_id=1, source_target_pairs={{0,1},{1,0},{2,3},{3,2},{4,5},{5,4},{6,7},{7,6},{8,9},{9,8},{10,11... | collective-permute-start | bytes 737288 | tf_op jit(solution)/shard_map/ppermute | solution.py:306
  134.2 2.2 %collective-permute-done.37 = bf16[320,384]{1,0:T(8,128)(2,1)S(1)} collective-permute-done((bf16[320,384]{1,0:T(8,128)(2,1)S(1)}, bf16[320,384]{1,0:T(8,128)(2,1)S(1)}, u32[]{:S(2)}, u32[]{:S(2)}) %collective-permute-start.37) | collective-permute-done | bytes 245792 | tf_op jit(solution)/shard_map/ppermute | solution.py:306
  136.4 2.6 %collective-permute-done.39 = bf16[320,384]{1,0:T(8,128)(2,1)S(1)} collective-permute-done((bf16[320,384]{1,0:T(8,128)(2,1)S(1)}, bf16[320,384]{1,0:T(8,128)(2,1)S(1)}, u32[]{:S(2)}, u32[]{:S(2)}) %collective-permute-start.39) | collective-permute-done | bytes 245792 | tf_op jit(solution)/shard_map/ppermute | solution.py:306
  139.1 1.0 shard_map.78
  (120 shorter events, 17.4 us)
Async XLA Ops:
  0.6 10.9 %collective-permute-start.1 = (bf16[320,1024]{1,0:T(8,128)(2,1)}, bf16[320,1024]{1,0:T(8,128)(2,1)S(1)}, u32[]{:S(2)}, u32[]{:S(2)}) collective-permute-start(bf16[320,1024]{1,0:T(8,128)(2,1)} %bitcast.8), channel_id=1, source_target_pairs={{0,4},{4,0},{8,12},{12,8},{1,5},{5,1},{9,13},{13,9},{2,6},{6,2},{1... | collective-permute-start | bytes 1966088 | tf_op jit(solution)/shard_map/ppermute | solution.py:26
  1.1 18.7 %collective-permute-start = (bf16[320,1024]{1,0:T(8,128)(2,1)}, bf16[320,1024]{1,0:T(8,128)(2,1)S(1)}, u32[]{:S(2)}, u32[]{:S(2)}) collective-permute-start(bf16[320,1024]{1,0:T(8,128)(2,1)} %bitcast.9), channel_id=1, source_target_pairs={{0,8},{4,12},{8,0},{12,4},{1,9},{5,13},{9,1},{13,5},{2,10},{6,14},... | collective-permute-start | bytes 1966088 | tf_op jit(solution)/shard_map/ppermute | solution.py:26
  4.9 17.0 %copy-start.2 = (bf16[1,1024,320]{1,2,0:T(8,128)(2,1)S(1)}, bf16[1,1024,320]{1,2,0:T(8,128)(2,1)}, u32[]{:S(2)}) copy-start(bf16[1,1024,320]{1,2,0:T(8,128)(2,1)} %param.5) | copy-start | bytes 1966084
  4.9 17.0 %copy-start.11 = (bf16[1,512,384]{2,1,0:T(8,128)(2,1)S(1)}, bf16[1,512,384]{2,1,0:T(8,128)(2,1)}, u32[]{:S(2)}) copy-start(bf16[1,512,384]{2,1,0:T(8,128)(2,1)} %param.9) | copy-start | bytes 1179652
  5.0 3.8 %collective-permute-start.2 = (f32[8,384]{1,0:T(8,128)S(1)}, f32[8,384]{1,0:T(8,128)S(1)}, u32[]{:S(2)}, u32[]{:S(2)}) collective-permute-start(f32[8,384]{1,0:T(8,128)S(1)} %shard_map.68), channel_id=1, source_target_pairs={{0,16},{16,0},{1,17},{17,1},{2,18},{18,2},{3,19},{19,3},{4,20},{20... | collective-permute-start | bytes 36872 | tf_op jit(solution)/shard_map/ppermute | solution.py:26
  8.9 10.5 %collective-permute-start.5 = (f32[8,384]{1,0:T(8,128)S(1)}, f32[8,384]{1,0:T(8,128)S(1)}, u32[]{:S(2)}, u32[]{:S(2)}) collective-permute-start(f32[8,384]{1,0:T(8,128)S(1)} %maximum_maximum_fusion.refs_2_.refs_4_), channel_id=1, source_target_pairs={{0,12},{4,8},{8,4},{12,0},{1,13},{5,9},{9,5},{13,1},{2,14},{6,10},... | collective-permute-start | bytes 36872 | tf_op jit(solution)/shard_map/ppermute | solution.py:26
  8.9 10.9 %collective-permute-start.4 = (f32[8,384]{1,0:T(8,128)S(1)}, f32[8,384]{1,0:T(8,128)S(1)}, u32[]{:S(2)}, u32[]{:S(2)}) collective-permute-start(f32[8,384]{1,0:T(8,128)S(1)} %maximum_maximum_fusion.refs_2_.refs_4_), channel_id=1, source_target_pairs={{0,8},{4,12},{8,0},{12,4},{1,9},{5,13},{9,1},{13,5},{2,10},{6,14},... | collective-permute-start | bytes 36872 | tf_op jit(solution)/shard_map/ppermute | solution.py:26
  9.8 1.8 %collective-permute-start.3 = (f32[8,384]{1,0:T(8,128)S(1)}, f32[8,384]{1,0:T(8,128)S(1)}, u32[]{:S(2)}, u32[]{:S(2)}) collective-permute-start(f32[8,384]{1,0:T(8,128)S(1)} %maximum_maximum_fusion.refs_2_.refs_4_), channel_id=1, source_target_pairs={{0,4},{4,0},{8,12},{12,8},{1,5},{5,1},{9,13},{13,9},{2,6},{6,2},{1... | collective-permute-start | bytes 36872 | tf_op jit(solution)/shard_map/ppermute | solution.py:26
  12.7 2.4 %copy-start.8 = (bf16[5,1280,384]{2,1,0:T(8,128)(2,1)S(1)}, bf16[5,1280,384]{2,1,0:T(8,128)(2,1)}, u32[]{:S(2)}) copy-start(bf16[5,1280,384]{2,1,0:T(8,128)(2,1)} %refs_8_.2) | copy-start | bytes 14745604
  15.1 6.9 %copy-start.9 = (bf16[5,1280,384]{2,1,0:T(8,128)(2,1)S(1)}, bf16[5,1280,384]{2,1,0:T(8,128)(2,1)}, u32[]{:S(2)}) copy-start(bf16[5,1280,384]{2,1,0:T(8,128)(2,1)} %refs_8_.2) | copy-start | bytes 14745604
  19.8 2.1 %collective-permute-start.6 = (bf16[320,1024]{1,0:T(8,128)(2,1)S(1)}, bf16[320,1024]{1,0:T(8,128)(2,1)S(1)}, u32[]{:S(2)}, u32[]{:S(2)}) collective-permute-start(bf16[320,1024]{1,0:T(8,128)(2,1)S(1)} %collective-permute-done.refs_1_), channel_id=1, source_target_pairs={{0,4},{4,0},{8,12},{12,8},{1,5},{5,1},{9,13},{13,9},{2,6},{6,2},{1... | collective-permute-start | bytes 1966088 | tf_op jit(solution)/shard_map/ppermute | solution.py:26
  21.9 12.9 %copy-start.6 = (bf16[320,1024]{1,0:T(8,128)(2,1)}, bf16[320,1024]{1,0:T(8,128)(2,1)S(1)}, u32[]{:S(2)}) copy-start(bf16[320,1024]{1,0:T(8,128)(2,1)S(1)} %collective-permute-done.6.refs_3_) | copy-start | bytes 1966084
  29.7 5.1 %copy-start.12 = (bf16[512,384]{1,0:T(8,128)(2,1)}, bf16[512,384]{1,0:T(8,128)(2,1)S(1)}, u32[]{:S(2)}) copy-start(bf16[512,384]{1,0:T(8,128)(2,1)S(1)} %get-tuple-element.105.refs_0_) | copy-start | bytes 1179652
  29.7 8.2 %collective-permute-start.7 = (bf16[320,384]{1,0:T(8,128)(2,1)S(1)}, bf16[320,384]{1,0:T(8,128)(2,1)S(1)}, u32[]{:S(2)}, u32[]{:S(2)}) collective-permute-start(bf16[320,384]{1,0:T(8,128)(2,1)S(1)} %get-tuple-element.64), channel_id=1, source_target_pairs={{0,16},{16,0},{1,17},{17,1},{2,18},{18,2},{3,19},{19,3},{4,20},{20... | collective-permute-start | bytes 737288 | tf_op jit(solution)/shard_map/ppermute | solution.py:26
  34.8 14.2 %collective-permute-start.9 = (bf16[320,384]{1,0:T(8,128)(2,1)}, bf16[320,384]{1,0:T(8,128)(2,1)}, u32[]{:S(2)}, u32[]{:S(2)}) collective-permute-start(bf16[320,384]{1,0:T(8,128)(2,1)} %get-tuple-element.65), channel_id=1, source_target_pairs={{0,16},{16,0},{1,17},{17,1},{2,18},{18,2},{3,19},{19,3},{4,20},{20... | collective-permute-start | bytes 737288 | tf_op jit(solution)/shard_map/ppermute | solution.py:26
  38.7 11.9 %collective-permute-start.8 = (bf16[320,384]{1,0:T(8,128)(2,1)}, bf16[320,384]{1,0:T(8,128)(2,1)}, u32[]{:S(2)}, u32[]{:S(2)}) collective-permute-start(bf16[320,384]{1,0:T(8,128)(2,1)} %add_convert_fusion.29), channel_id=1, source_target_pairs={{0,1},{1,0},{2,3},{3,2},{4,5},{5,4},{6,7},{7,6},{8,9},{9,8},{10,11... | collective-permute-start | bytes 737288 | tf_op jit(solution)/shard_map/ppermute | solution.py:306
  40.7 11.7 %collective-permute-start.10 = (bf16[512,384]{1,0:T(8,128)(2,1)}, bf16[512,384]{1,0:T(8,128)(2,1)S(1)}, u32[]{:S(2)}, u32[]{:S(2)}) collective-permute-start(bf16[512,384]{1,0:T(8,128)(2,1)} %copy-done.12), channel_id=1, source_target_pairs={{0,8},{4,12},{8,0},{12,4},{1,9},{5,13},{9,1},{13,5},{2,10},{6,14},... | collective-permute-start | bytes 1179656 | tf_op jit(solution)/shard_map/ppermute | solution.py:26
  44.4 17.5 %copy-start.13 = (bf16[512,384]{1,0:T(8,128)(2,1)S(1)}, bf16[512,384]{1,0:T(8,128)(2,1)}, u32[]{:S(2)}) copy-start(bf16[512,384]{1,0:T(8,128)(2,1)} %copy-done.12) | copy-start | bytes 1179652
  46.9 8.9 %collective-permute-start.13 = (bf16[320,384]{1,0:T(8,128)(2,1)S(1)}, bf16[320,384]{1,0:T(8,128)(2,1)S(1)}, u32[]{:S(2)}, u32[]{:S(2)}) collective-permute-start(bf16[320,384]{1,0:T(8,128)(2,1)S(1)} %get-tuple-element.74), channel_id=1, source_target_pairs={{0,16},{16,0},{1,17},{17,1},{2,18},{18,2},{3,19},{19,3},{4,20},{20... | collective-permute-start | bytes 737288 | tf_op jit(solution)/shard_map/ppermute | solution.py:26
  48.9 13.6 %collective-permute-start.16 = (bf16[320,384]{1,0:T(8,128)(2,1)S(1)}, bf16[320,384]{1,0:T(8,128)(2,1)S(1)}, u32[]{:S(2)}, u32[]{:S(2)}) collective-permute-start(bf16[320,384]{1,0:T(8,128)(2,1)S(1)} %get-tuple-element.77), channel_id=1, source_target_pairs={{0,16},{16,0},{1,17},{17,1},{2,18},{18,2},{3,19},{19,3},{4,20},{20... | collective-permute-start | bytes 737288 | tf_op jit(solution)/shard_map/ppermute | solution.py:26
  50.0 6.3 %collective-permute-start.12 = (bf16[320,384]{1,0:T(8,128)(2,1)S(1)}, bf16[320,384]{1,0:T(8,128)(2,1)S(1)}, u32[]{:S(2)}, u32[]{:S(2)}) collective-permute-start(bf16[320,384]{1,0:T(8,128)(2,1)S(1)} %add_convert_fusion.28), channel_id=1, source_target_pairs={{0,1},{1,0},{2,3},{3,2},{4,5},{5,4},{6,7},{7,6},{8,9},{9,8},{10,11... | collective-permute-start | bytes 737288 | tf_op jit(solution)/shard_map/ppermute | solution.py:306
  51.7 10.2 %collective-permute-start.17 = (bf16[320,384]{1,0:T(8,128)(2,1)S(1)}, bf16[320,384]{1,0:T(8,128)(2,1)S(1)}, u32[]{:S(2)}, u32[]{:S(2)}) collective-permute-start(bf16[320,384]{1,0:T(8,128)(2,1)S(1)} %add_convert_fusion.27), channel_id=1, source_target_pairs={{0,0},{1,2},{2,1},{3,3},{4,4},{5,6},{6,5},{7,7},{8,8},{9,10},{10,9... | collective-permute-start | bytes 737288 | tf_op jit(solution)/shard_map/ppermute | solution.py:312
  56.4 15.0 %collective-permute-start.14 = (bf16[320,384]{1,0:T(8,128)(2,1)S(1)}, bf16[320,384]{1,0:T(8,128)(2,1)S(1)}, u32[]{:S(2)}, u32[]{:S(2)}) collective-permute-start(bf16[320,384]{1,0:T(8,128)(2,1)S(1)} %add_convert_fusion.25), channel_id=1, source_target_pairs={{0,0},{1,2},{2,1},{3,3},{4,4},{5,6},{6,5},{7,7},{8,8},{9,10},{10,9... | collective-permute-start | bytes 737288 | tf_op jit(solution)/shard_map/ppermute | solution.py:312
  57.1 9.3 %collective-permute-start.15 = (bf16[320,384]{1,0:T(8,128)(2,1)S(1)}, bf16[320,384]{1,0:T(8,128)(2,1)S(1)}, u32[]{:S(2)}, u32[]{:S(2)}) collective-permute-start(bf16[320,384]{1,0:T(8,128)(2,1)S(1)} %add_convert_fusion.26), channel_id=1, source_target_pairs={{0,1},{1,0},{2,3},{3,2},{4,5},{5,4},{6,7},{7,6},{8,9},{9,8},{10,11... | collective-permute-start | bytes 737288 | tf_op jit(solution)/shard_map/ppermute | solution.py:306
  61.9 56.6 %collective-permute-start.31 = (bf16[512,384]{1,0:T(8,128)(2,1)S(1)}, bf16[512,384]{1,0:T(8,128)(2,1)S(1)}, u32[]{:S(2)}, u32[]{:S(2)}) collective-permute-start(bf16[512,384]{1,0:T(8,128)(2,1)S(1)} %copy-done.13), channel_id=1, source_target_pairs={{0,4},{4,0},{8,12},{12,8},{1,5},{5,1},{9,13},{13,9},{2,6},{6,2},{1... | collective-permute-start | bytes 1179656 | tf_op jit(solution)/shard_map/ppermute | solution.py:26
  61.9 56.6 %collective-permute-start.32 = (bf16[512,384]{1,0:T(8,128)(2,1)S(1)}, bf16[512,384]{1,0:T(8,128)(2,1)S(1)}, u32[]{:S(2)}, u32[]{:S(2)}) collective-permute-start(bf16[512,384]{1,0:T(8,128)(2,1)S(1)} %collective-permute-done.10.refs_1_), channel_id=1, source_target_pairs={{0,4},{4,0},{8,12},{12,8},{1,5},{5,1},{9,13},{13,9},{2,6},{6,2},{1... | collective-permute-start | bytes 1179656 | tf_op jit(solution)/shard_map/ppermute | solution.py:26
  62.5 13.4 %collective-permute-start.11 = (bf16[640,384]{1,0:T(8,128)(2,1)S(1)}, bf16[640,384]{1,0:T(8,128)(2,1)S(1)}, u32[]{:S(2)}, u32[]{:S(2)}) collective-permute-start(bf16[640,384]{1,0:T(8,128)(2,1)S(1)} %get-tuple-element.71), channel_id=1, source_target_pairs={{0,16},{16,0},{1,17},{17,1},{2,18},{18,2},{3,19},{19,3},{4,20},{20... | collective-permute-start | bytes 1474568 | tf_op jit(solution)/shard_map/ppermute | solution.py:26
  66.3 11.4 %collective-permute-start.20 = (bf16[320,384]{1,0:T(8,128)(2,1)S(1)}, bf16[320,384]{1,0:T(8,128)(2,1)S(1)}, u32[]{:S(2)}, u32[]{:S(2)}) collective-permute-start(bf16[320,384]{1,0:T(8,128)(2,1)S(1)} %broadcast_select_fusion.16), channel_id=1, source_target_pairs={{0,1},{1,0},{2,3},{3,2},{4,5},{5,4},{6,7},{7,6},{8,9},{9,8},{10,11... | collective-permute-start | bytes 737288 | tf_op jit(solution)/shard_map/ppermute | solution.py:306
  71.4 6.7 %collective-permute-start.19 = (bf16[320,384]{1,0:T(8,128)(2,1)S(1)}, bf16[320,384]{1,0:T(8,128)(2,1)S(1)}, u32[]{:S(2)}, u32[]{:S(2)}) collective-permute-start(bf16[320,384]{1,0:T(8,128)(2,1)S(1)} %add_convert_fusion.22), channel_id=1, source_target_pairs={{0,0},{1,2},{2,1},{3,3},{4,4},{5,6},{6,5},{7,7},{8,8},{9,10},{10,9... | collective-permute-start | bytes 737288 | tf_op jit(solution)/shard_map/ppermute | solution.py:312
  75.9 12.5 %collective-permute-start.23 = (bf16[640,384]{1,0:T(8,128)(2,1)S(1)}, bf16[640,384]{1,0:T(8,128)(2,1)S(1)}, u32[]{:S(2)}, u32[]{:S(2)}) collective-permute-start(bf16[640,384]{1,0:T(8,128)(2,1)S(1)} %get-tuple-element.92), channel_id=1, source_target_pairs={{0,16},{16,0},{1,17},{17,1},{2,18},{18,2},{3,19},{19,3},{4,20},{20... | collective-permute-start | bytes 1474568 | tf_op jit(solution)/shard_map/ppermute | solution.py:26
  77.8 11.0 %collective-permute-start.18 = (bf16[320,384]{1,0:T(8,128)(2,1)S(1)}, bf16[320,384]{1,0:T(8,128)(2,1)S(1)}, u32[]{:S(2)}, u32[]{:S(2)}) collective-permute-start(bf16[320,384]{1,0:T(8,128)(2,1)S(1)} %broadcast_select_fusion.15), channel_id=1, source_target_pairs={{0,1},{1,0},{2,3},{3,2},{4,5},{5,4},{6,7},{7,6},{8,9},{9,8},{10,11... | collective-permute-start | bytes 737288 | tf_op jit(solution)/shard_map/ppermute | solution.py:306
  78.2 14.0 %collective-permute-start.24 = (bf16[320,384]{1,0:T(8,128)(2,1)S(1)}, bf16[320,384]{1,0:T(8,128)(2,1)S(1)}, u32[]{:S(2)}, u32[]{:S(2)}) collective-permute-start(bf16[320,384]{1,0:T(8,128)(2,1)S(1)} %add_convert_fusion.19), channel_id=1, source_target_pairs={{0,0},{1,2},{2,1},{3,3},{4,4},{5,6},{6,5},{7,7},{8,8},{9,10},{10,9... | collective-permute-start | bytes 737288 | tf_op jit(solution)/shard_map/ppermute | solution.py:312
  88.4 6.3 %collective-permute-start.22 = (bf16[320,384]{1,0:T(8,128)(2,1)S(1)}, bf16[320,384]{1,0:T(8,128)(2,1)S(1)}, u32[]{:S(2)}, u32[]{:S(2)}) collective-permute-start(bf16[320,384]{1,0:T(8,128)(2,1)S(1)} %broadcast_select_fusion.14), channel_id=1, source_target_pairs={{0,1},{1,0},{2,3},{3,2},{4,5},{5,4},{6,7},{7,6},{8,9},{9,8},{10,11... | collective-permute-start | bytes 737288 | tf_op jit(solution)/shard_map/ppermute | solution.py:306
  88.9 9.8 %collective-permute-start.27 = (bf16[320,384]{1,0:T(8,128)(2,1)S(1)}, bf16[320,384]{1,0:T(8,128)(2,1)S(1)}, u32[]{:S(2)}, u32[]{:S(2)}) collective-permute-start(bf16[320,384]{1,0:T(8,128)(2,1)S(1)} %add_convert_fusion.16), channel_id=1, source_target_pairs={{0,0},{1,2},{2,1},{3,3},{4,4},{5,6},{6,5},{7,7},{8,8},{9,10},{10,9... | collective-permute-start | bytes 737288 | tf_op jit(solution)/shard_map/ppermute | solution.py:312
  92.3 13.7 %collective-permute-start.21 = (bf16[640,384]{1,0:T(8,128)(2,1)S(1)}, bf16[640,384]{1,0:T(8,128)(2,1)S(1)}, u32[]{:S(2)}, u32[]{:S(2)}) collective-permute-start(bf16[640,384]{1,0:T(8,128)(2,1)S(1)} %get-tuple-element.91), channel_id=1, source_target_pairs={{0,16},{16,0},{1,17},{17,1},{2,18},{18,2},{3,19},{19,3},{4,20},{20... | collective-permute-start | bytes 1474568 | tf_op jit(solution)/shard_map/ppermute | solution.py:26
  94.8 8.0 %collective-permute-start.26 = (bf16[320,384]{1,0:T(8,128)(2,1)S(1)}, bf16[320,384]{1,0:T(8,128)(2,1)S(1)}, u32[]{:S(2)}, u32[]{:S(2)}) collective-permute-start(bf16[320,384]{1,0:T(8,128)(2,1)S(1)} %broadcast_select_fusion.13), channel_id=1, source_target_pairs={{0,1},{1,0},{2,3},{3,2},{4,5},{5,4},{6,7},{7,6},{8,9},{9,8},{10,11... | collective-permute-start | bytes 737288 | tf_op jit(solution)/shard_map/ppermute | solution.py:306
  98.7 6.5 %collective-permute-start.25 = (bf16[320,384]{1,0:T(8,128)(2,1)S(1)}, bf16[320,384]{1,0:T(8,128)(2,1)S(1)}, u32[]{:S(2)}, u32[]{:S(2)}) collective-permute-start(bf16[320,384]{1,0:T(8,128)(2,1)S(1)} %add_convert_fusion.13), channel_id=1, source_target_pairs={{0,0},{1,2},{2,1},{3,3},{4,4},{5,6},{6,5},{7,7},{8,8},{9,10},{10,9... | collective-permute-start | bytes 737288 | tf_op jit(solution)/shard_map/ppermute | solution.py:312
  99.5 19.1 %copy-start.10 = (bf16[1536,640]{1,0:T(8,128)(2,1)S(1)}, bf16[1536,640]{1,0:T(8,128)(2,1)}, u32[]{:S(2)}) copy-start(bf16[1536,640]{1,0:T(8,128)(2,1)} %refs_8_.3) | copy-start | bytes 5898244
  102.8 8.1 %collective-permute-start.30 = (bf16[320,384]{1,0:T(8,128)(2,1)S(1)}, bf16[320,384]{1,0:T(8,128)(2,1)S(1)}, u32[]{:S(2)}, u32[]{:S(2)}) collective-permute-start(bf16[320,384]{1,0:T(8,128)(2,1)S(1)} %broadcast_select_fusion.12), channel_id=1, source_target_pairs={{0,1},{1,0},{2,3},{3,2},{4,5},{5,4},{6,7},{7,6},{8,9},{9,8},{10,11... | collective-permute-start | bytes 737288 | tf_op jit(solution)/shard_map/ppermute | solution.py:306
  105.2 6.7 %collective-permute-start.29 = (bf16[320,384]{1,0:T(8,128)(2,1)S(1)}, bf16[320,384]{1,0:T(8,128)(2,1)S(1)}, u32[]{:S(2)}, u32[]{:S(2)}) collective-permute-start(bf16[320,384]{1,0:T(8,128)(2,1)S(1)} %add_convert_fusion.10), channel_id=1, source_target_pairs={{0,0},{1,2},{2,1},{3,3},{4,4},{5,6},{6,5},{7,7},{8,8},{9,10},{10,9... | collective-permute-start | bytes 737288 | tf_op jit(solution)/shard_map/ppermute | solution.py:312
  106.2 11.6 %collective-permute-start.28 = (bf16[320,384]{1,0:T(8,128)(2,1)S(1)}, bf16[320,384]{1,0:T(8,128)(2,1)S(1)}, u32[]{:S(2)}, u32[]{:S(2)}) collective-permute-start(bf16[320,384]{1,0:T(8,128)(2,1)S(1)} %broadcast_select_fusion.11), channel_id=1, source_target_pairs={{0,1},{1,0},{2,3},{3,2},{4,5},{5,4},{6,7},{7,6},{8,9},{9,8},{10,11... | collective-permute-start | bytes 737288 | tf_op jit(solution)/shard_map/ppermute | solution.py:306
  111.1 11.0 %collective-permute-start.33 = (bf16[320,384]{1,0:T(8,128)(2,1)S(1)}, bf16[320,384]{1,0:T(8,128)(2,1)S(1)}, u32[]{:S(2)}, u32[]{:S(2)}) collective-permute-start(bf16[320,384]{1,0:T(8,128)(2,1)S(1)} %add_convert_fusion.7), channel_id=1, source_target_pairs={{0,0},{1,2},{2,1},{3,3},{4,4},{5,6},{6,5},{7,7},{8,8},{9,10},{10,9... | collective-permute-start | bytes 737288 | tf_op jit(solution)/shard_map/ppermute | solution.py:312
  112.2 12.8 %collective-permute-start.36 = (bf16[320,384]{1,0:T(8,128)(2,1)S(1)}, bf16[320,384]{1,0:T(8,128)(2,1)S(1)}, u32[]{:S(2)}, u32[]{:S(2)}) collective-permute-start(bf16[320,384]{1,0:T(8,128)(2,1)S(1)} %broadcast_select_fusion.10), channel_id=1, source_target_pairs={{0,1},{1,0},{2,3},{3,2},{4,5},{5,4},{6,7},{7,6},{8,9},{9,8},{10,11... | collective-permute-start | bytes 737288 | tf_op jit(solution)/shard_map/ppermute | solution.py:306
  117.8 8.0 %collective-permute-start.35 = (bf16[320,384]{1,0:T(8,128)(2,1)S(1)}, bf16[320,384]{1,0:T(8,128)(2,1)S(1)}, u32[]{:S(2)}, u32[]{:S(2)}) collective-permute-start(bf16[320,384]{1,0:T(8,128)(2,1)S(1)} %add_convert_fusion.4), channel_id=1, source_target_pairs={{0,0},{1,2},{2,1},{3,3},{4,4},{5,6},{6,5},{7,7},{8,8},{9,10},{10,9... | collective-permute-start | bytes 737288 | tf_op jit(solution)/shard_map/ppermute | solution.py:312
  122.2 8.0 %collective-permute-start.34 = (bf16[320,384]{1,0:T(8,128)(2,1)S(1)}, bf16[320,384]{1,0:T(8,128)(2,1)S(1)}, u32[]{:S(2)}, u32[]{:S(2)}) collective-permute-start(bf16[320,384]{1,0:T(8,128)(2,1)S(1)} %add_convert_fusion.3), channel_id=1, source_target_pairs={{0,1},{1,0},{2,3},{3,2},{4,5},{5,4},{6,7},{7,6},{8,9},{9,8},{10,11... | collective-permute-start | bytes 737288 | tf_op jit(solution)/shard_map/ppermute | solution.py:306
  125.2 7.2 %collective-permute-start.38 = (bf16[320,384]{1,0:T(8,128)(2,1)S(1)}, bf16[320,384]{1,0:T(8,128)(2,1)S(1)}, u32[]{:S(2)}, u32[]{:S(2)}) collective-permute-start(bf16[320,384]{1,0:T(8,128)(2,1)S(1)} %add_convert_fusion.2), channel_id=1, source_target_pairs={{0,0},{1,2},{2,1},{3,3},{4,4},{5,6},{6,5},{7,7},{8,8},{9,10},{10,9... | collective-permute-start | bytes 737288 | tf_op jit(solution)/shard_map/ppermute | solution.py:312
  125.9 10.5 %collective-permute-start.37 = (bf16[320,384]{1,0:T(8,128)(2,1)S(1)}, bf16[320,384]{1,0:T(8,128)(2,1)S(1)}, u32[]{:S(2)}, u32[]{:S(2)}) collective-permute-start(bf16[320,384]{1,0:T(8,128)(2,1)S(1)} %add_convert_fusion.1), channel_id=1, source_target_pairs={{0,1},{1,0},{2,3},{3,2},{4,5},{5,4},{6,7},{7,6},{8,9},{9,8},{10,11... | collective-permute-start | bytes 737288 | tf_op jit(solution)/shard_map/ppermute | solution.py:306
  132.5 6.6 %collective-permute-start.39 = (bf16[320,384]{1,0:T(8,128)(2,1)S(1)}, bf16[320,384]{1,0:T(8,128)(2,1)S(1)}, u32[]{:S(2)}, u32[]{:S(2)}) collective-permute-start(bf16[320,384]{1,0:T(8,128)(2,1)S(1)} %add_convert_fusion), channel_id=1, source_target_pairs={{0,1},{1,0},{2,3},{3,2},{4,5},{5,4},{6,7},{7,6},{8,9},{9,8},{10,11... | collective-permute-start | bytes 737288 | tf_op jit(solution)/shard_map/ppermute | solution.py:306
  (6 other events, 6.5 us)

commit v8 on v7

--- a/solution.py
+++ b/solution.py
@@ -140,7 +140,7 @@
         edge_scr[0:2, cols] = p_ref[EDGE - tap : EDGE - tap + 2, :]
         edge_scr[2:4, cols] = p_ref[EDGE + length + 2 - tap : EDGE + length + 4 - tap, :]
         shifted.append(p_ref[EDGE + 2 - tap : EDGE + 2 - tap + length, :].astype(BF16))
-    return jnp.concatenate(shifted, axis=1), edge_scr[...].astype(BF16)
+    return jnp.concatenate(shifted, axis=1), edge_scr[:, 0 : len(group) * width].astype(BF16)
 
 
 def grad_kernel(offsets, group, per, pieces, idx_ref, *refs):
@@ -148,39 +148,42 @@
     blocks, pays, p_ref = refs[:n], refs[n : 2 * n], refs[2 * n]
     out_refs, edge_scr = list(refs[2 * n + 1 : -1]), refs[-1]
     width = p_ref.shape[1]
-    p, edge = shifted_rows(p_ref, edge_scr, group)
     me = idx_ref[0]
     x = jnp.concatenate([ref[...] for ref in blocks], axis=0)
     depth = x.shape[0] // n
     halo = jnp.concatenate([edge_block(ref, depth) for ref in pays], axis=0)
-    res = jnp.dot(x, p, preferred_element_type=F32) + jnp.dot(halo, edge, preferred_element_type=F32)
-    res = res.astype(BF16)
-    for i in range(len(group)):
-        own_ref = out_refs.pop(0)
-        other_refs = [out_refs.pop(0) for _ in range(len(pieces[i]) or min(per, 1))]
-        for j, off in enumerate(offsets):
-            part = res[j * depth : (j + 1) * depth, i * width : (i + 1) * width]
-            at = me ^ off
-            if not per:
-                own_ref[pl.ds(pl.multiple_of(at * depth, 16), depth), :] = part
-                continue
-            mine = lax.div(at, per) == idx_ref[1]
-            other = jnp.logical_not(mine)
-            row = lax.rem(at, per)
-            hits = [(own_ref, mine)]
-            if not pieces[i]:
-                hits.append((other_refs[0], other))
-            for ref, hit in hits:
-
-                @pl.when(hit)
-                def _(ref=ref, part=part, row=row):
-                    ref[pl.ds(pl.multiple_of(row * depth, 16), depth), :] = part
-
-            for r, ref in zip(pieces[i], other_refs):
-
-                @pl.when(jnp.logical_and(other, row == r))
-                def _(ref=ref, part=part):
-                    ref[...] = part
+    for first in range(0, len(group), 2):
+        some = group[first : first + 2]
+        p, edge = shifted_rows(p_ref, edge_scr, some)
+        res = jnp.dot(x, p, preferred_element_type=F32) + jnp.dot(halo, edge, preferred_element_type=F32)
+        res = res.astype(BF16)
+        for i in range(len(some)):
+            own_ref = out_refs.pop(0)
+            named = pieces[first + i]
+            other_refs = [out_refs.pop(0) for _ in range(len(named) or min(per, 1))]
+            for j, off in enumerate(offsets):
+                part = res[j * depth : (j + 1) * depth, i * width : (i + 1) * width]
+                at = me ^ off
+                if not per:
+                    own_ref[pl.ds(pl.multiple_of(at * depth, 16), depth), :] = part
+                    continue
+                mine = lax.div(at, per) == idx_ref[1]
+                other = jnp.logical_not(mine)
+                row = lax.rem(at, per)
+                hits = [(own_ref, mine)]
+                if not named:
+                    hits.append((other_refs[0], other))
+                for ref, hit in hits:
+
+                    @pl.when(hit)
+                    def _(ref=ref, part=part, row=row):
+                        ref[pl.ds(pl.multiple_of(row * depth, 16), depth), :] = part
+
+                for r, ref in zip(named, other_refs):
+
+                    @pl.when(jnp.logical_and(other, row == r))
+                    def _(ref=ref, part=part):
+                        ref[...] = part
 
 
 def qkv_kernel(offsets, idx_ref, *refs):
@@ -213,10 +216,6 @@
         scratch_shapes=scratch,
         compiler_params=pltpu.CompilerParams(vmem_limit_bytes=mib * 1024 * 1024),
     )(idx, *arrays)
-
-
-def pinned(value):
-    return pltpu.with_memory_space_constraint(value, pltpu.VMEM)
 
 
 def after(value, *others):
@@ -292,7 +291,7 @@
     me = lax.axis_index("dp")
     end = jnp.logical_or(me == 0, me == 3)
     outer_pairs = [(0, 1), (1, 0), (2, 3), (3, 2)]
-    middle_pairs = [(0, 0), (1, 2), (2, 1), (3, 3)]
+    middle_pairs = [(1, 2), (2, 1)]
     last = None
     h, p, s, outer, middle, sums = {}, {}, {}, {}, {}, {}
     for r in range(count + 5):
@@ -304,7 +303,7 @@
                 value = jnp.where(end, h[r], s[r - 3])
             last = value = lax.optimization_barrier(value)
             outer[r] = lax.ppermute(value, "dp", outer_pairs)
-            last = sent(r, last)
+            last = sent(r, last, sums)
         if r - 1 in outer:
             got = after(outer.pop(r - 1), last)
             if r - 1 < count:
@@ -343,10 +342,8 @@
 
     blocks = [x]
     for bit in bits[:-1]:
-        blocks = blocks + [pinned(swap(b, "mp", bit)) for b in blocks]
-    own = pinned(swap(x, "mp", bits[-1]))
-    weight = pinned(conv_weight)
-    near_x = pinned(x)
+        blocks = blocks + [swap(b, "mp", bit) for b in blocks]
+    own = swap(x, "mp", bits[-1])
     edges = edge_rows(x, width)
     payload = jnp.concatenate([edges, norm_gain.reshape(1, -1), jnp.zeros((3, width), F32)], axis=0)
     payloads = [payload] + [swap(payload, "mp", o) for o in offsets[1:]]
@@ -357,11 +354,10 @@
         (part, part),
         scratch(near),
         24,
-        idx, near_x, own, *pick(payloads, near), weight,
+        idx, x, own, *pick(payloads, near), conv_weight,
     )
     hold = [even] + pick(payloads, far)
-    blocks = blocks + [own] + [pinned(swap(after(b, *hold), "mp", bits[-1])) for b in blocks[1:]]
-    blocks[0] = near_x
+    blocks = blocks + [own] + [swap(after(b, *hold), "mp", bits[-1]) for b in blocks[1:]]
     pair = shards == 2 and peers % shards == 0 and lax.axis_size("dp") == 4
     per = peers // shards if pair else 0
     piece = jax.ShapeDtypeStruct((depth, width), BF16)
@@ -379,7 +375,7 @@
             pltpu.VMEM((LANES, width), F32),
         ],
         26,
-        idx, *blocks, *payloads, weight, even, odd, encoder_grad[0],
+        idx, *blocks, *payloads, conv_weight, even, odd, encoder_grad[0],
     )
     encs = [encoded]
     for bit in bits[:-1]:
@@ -400,8 +396,8 @@
         flat = call(
             functools.partial(grad_kernel, offsets, group, per, pieces),
             tuple(o for tap in outs for o in tap),
-            [pltpu.VMEM((LANES, width * len(group)), F32)],
-            16,
+            [pltpu.VMEM((LANES, width * min(len(group), 2)), F32)],
+            24 if len(group) > 2 else 16,
             after(idx, *hold) if hold else idx, *blocks, *payloads, pre_grad,
         )
         flat = list(flat)
@@ -438,7 +434,7 @@
 
     work((0,), [])
     launch(0, [])
-    work((1,), [keep[-1]])
+    work(tuple(range(1, taps)), [keep[-1]])
     launch(1, [])
 
     def share(c, last):
@@ -447,19 +443,17 @@
         value = got[tap][row] if len(got[tap]) > 1 else got[tap][0][rows]
         return added(keep[tap][rows], value if last is None else after(value, last))
 
-    def sent(r, last):
+    def sent(r, last, sums):
+        if r % per == per - 1 and r // per + 2 < taps and r < chunks:
+            launch(r // per + 2, [last])
+        if r == chunks + 2:
+            last = done["qkv"] = qkv_call(after(idx, last, *relays), encs + relays)
         return last
 
     def idle(c, last, sums):
-        if c % per == 0 and c // per + 2 < taps:
-            tap = c // per + 2
-            work((tap,), [last] + (encs[1:] if tap == 2 else []))
-            launch(tap, [])
-            last = keep[-1]
-        if c == per - 1:
-            relays.extend([swap(after(e, last), "mp", bits[-1]) for e in encs])
-        if c == chunks - 2:
-            last = done["qkv"] = qkv_call(after(idx, last, *relays), encs + relays)
+        if c == per:
+            held = encs[1:]
+            relays.extend([swap(after(e, last, *held), "mp", bits[-1]) for e in encs])
         if c == chunks:
             early = len(sums) // per
             parts = [sums[i] for i in range(early * per)]

time: 141 us -> 147 us (1.043)
  starting transfers between devices: 60.8 us -> 69.4 us
  waiting for transfers between devices: 31.7 us -> 27.8 us
  Pallas kernels: 31 us -> 32.6 us
    ppermute x13, starting transfers between devices: 35.7 us -> 44.2 us  [chain_sums(): outer[r] = lax.ppermute(value, 'dp', outer_pairs)]
    ppermute x17, waiting for transfers between devices: 20.7 us -> 14.3 us  [swap(): return lax.ppermute(value, axis, [(i, i ^ bit) for i in range(peers)])]
    ppermute x13, waiting for transfers between devices: 11 us -> 13.5 us  [chain_sums(): outer[r] = lax.ppermute(value, 'dp', outer_pairs)]
    pallas_call x8 -> x5, Pallas kernels: 27.7 us -> 29.3 us  [call(): pl.pallas_call(kernel, out_shape=out, in_specs=[pl.BlockSpec(memory_space...]
  transfers between devices with their start and end apart: 40 -> 40, of which waited for: 14 -> 13; matrix products, arithmetic and copies ran while one was open for 5% -> 4% of each run, Pallas kernels for 17% -> 17%
where the time goes in v8:
time: 147 us; the launch traced here: 146 us
  starting transfers between devices  69.4 us (47%)
  Pallas kernels  32.6 us (22%)
  waiting for transfers between devices  27.8 us (19%)
  local copies, waits for them, and re-layouts  9.87 us (7%)
  other arithmetic  5.62 us (4%)
    ppermute x13, starting transfers between devices, chain_sums(): outer[r] = lax.ppermute(value, 'dp', outer_pairs)  44.2 us
    pallas_call x5, Pallas kernels, call(): pl.pallas_call(kernel, out_shape=out, in_specs=[pl.BlockSpec(memory_space...  29.3 us
    ppermute x17, starting transfers between devices, swap(): return lax.ppermute(value, axis, [(i, i ^ bit) for i in range(peers)])  18.1 us
    ppermute x17, waiting for transfers between devices, swap(): return lax.ppermute(value, axis, [(i, i ^ bit) for i in range(peers)])  14.3 us
    ppermute x13, waiting for transfers between devices, chain_sums(): outer[r] = lax.ppermute(value, 'dp', outer_pairs)  13.5 us
    unnamed x28, local copies, waits for them, and re-layouts  8.96 us
    ppermute x10, starting transfers between devices, chain_sums(): middle[r - 1] = lax.ppermute(last, 'dp', middle_pairs)  7.1 us
    convert_element_type x23, other arithmetic, added(): return (a.astype(F32) + b.astype(F32)).astype(BF16)  4.44 us
  transfers between devices with their start and end apart: 40, of which 13 were waited for; matrix products, arithmetic and copies ran while one was open for 4% of the time, Pallas kernels for 17%

profile of v8, /device:TPU:0, one launch (start us, length us, event | category | flops | bytes accessed | tf_op | source)
XLA Modules:
  0.0 146.5 jit_solution(5347448348663471346)
XLA Ops:
  1.1 2.6 %collective-permute-start = (bf16[320,1024]{1,0:T(8,128)(2,1)}, bf16[320,1024]{1,0:T(8,128)(2,1)S(1)}, u32[]{:S(2)}, u32[]{:S(2)}) collective-permute-start(bf16[320,1024]{1,0:T(8,128)(2,1)} %bitcast.9), channel_id=1, source_target_pairs={{0,8},{4,12},{8,0},{12,4},{1,9},{5,13},{9,1},{13,5},{2,10},{6,14},... | collective-permute-start | bytes 1966088 | tf_op jit(solution)/shard_map/ppermute | solution.py:26
  3.7 1.1 copy-done
  5.0 1.6 %collective-permute-start.2 = (f32[8,384]{1,0:T(8,128)S(1)}, f32[8,384]{1,0:T(8,128)S(1)}, u32[]{:S(2)}, u32[]{:S(2)}) collective-permute-start(f32[8,384]{1,0:T(8,128)S(1)} %shard_map.68), channel_id=1, source_target_pairs={{0,16},{16,0},{1,17},{17,1},{2,18},{18,2},{3,19},{19,3},{4,20},{20... | collective-permute-start | bytes 36872 | tf_op jit(solution)/shard_map/ppermute | solution.py:26
  7.3 1.4 collective-permute-done.2
  8.9 0.9 collective-permute-start.4
  9.8 0.9 collective-permute-start.3
  11.6 1.1 copy-done.1
  12.7 2.4 %copy-done.3 = bf16[5,1280,384]{2,1,0:T(8,128)(2,1)S(1)} copy-done((bf16[5,1280,384]{2,1,0:T(8,128)(2,1)S(1)}, bf16[5,1280,384]{2,1,0:T(8,128)(2,1)}, u32[]{:S(2)}) %copy-start.3) | copy-done | bytes 4915224
  15.1 4.3 %shard_map.69 = (f32[512,384]{1,0:T(8,128)S(1)}, f32[512,384]{1,0:T(8,128)S(1)}) custom-call(s32[2]{0:T(128)S(1)} %pad_add_fusion.idx_ref, bf16[320,1024]{1,0:T(8,128)(2,1)S(1)} %bitcast.12, bf16[320,1024]{1,0:T(8,128)(2,1)S(1)} %collective-permute-done.1.refs_1_.refs_2_, f32[8,384]{1,0:T(8,128)S(1)} %maximum_maximum_fusion.refs_2_.refs_4_, ...), custom_call_target="tpu_custom_call" | custom-call | tf_op jit(solution)/shard_map/pallas_call | solution.py:211
  19.8 0.8 copy-done.5
  20.6 1.3 collective-permute-done.6.refs_3_
  21.9 1.3 copy-done.6
  23.2 6.4 %shard_map.70 = (bf16[512,384]{1,0:T(8,128)(2,1)S(1)}, f32[1040,384]{1,0:T(8,128)S(1)}, bf16[320,384]{1,0:T(8,128)(2,1)S(1)}) custom-call(s32[2]{0:T(128)S(1)} %pad_add_fusion.idx_ref, bf16[320,1024]{1,0:T(8,128)(2,1)S(1)} %bitcast.13, bf16[320,1024]{1,0:T(8,128)(2,1)S(1)} %copy-done.6, bf16[320,1024]{1,0:T(8,128)(2,1)S(1)} %collective-permute-done.1.refs_1_.refs_2_, ...), custom_call_target="tpu_custom_call" | custom-call | tf_op jit(solution)/shard_map/pallas_call | solution.py:211
  29.7 1.8 %collective-permute-start.8 = (bf16[320,384]{1,0:T(8,128)(2,1)S(1)}, bf16[320,384]{1,0:T(8,128)(2,1)S(1)}, u32[]{:S(2)}, u32[]{:S(2)}) collective-permute-start(bf16[320,384]{1,0:T(8,128)(2,1)S(1)} %get-tuple-element.70), channel_id=1, source_target_pairs={{0,16},{16,0},{1,17},{17,1},{2,18},{18,2},{3,19},{19,3},{4,20},{20... | collective-permute-start | bytes 737288 | tf_op jit(solution)/shard_map/ppermute | solution.py:26
  31.5 3.4 %shard_map.71 = (bf16[640,384]{1,0:T(8,128)(2,1)S(1)}, bf16[320,384]{1,0:T(8,128)(2,1)}) custom-call(s32[2]{0:T(128)S(1)} %pad_add_fusion.idx_ref, bf16[320,1024]{1,0:T(8,128)(2,1)S(1)} %bitcast.14, bf16[320,1024]{1,0:T(8,128)(2,1)S(1)} %copy-done.6, bf16[320,1024]{1,0:T(8,128)(2,1)S(1)} %collective-permute-done.1.refs_1_.refs_2_, ...), custom_call_target="tpu_custom_call" | custom-call | tf_op jit(solution)/shard_map/pallas_call | solution.py:211
  35.2 2.8 %collective-permute-done.8 = bf16[320,384]{1,0:T(8,128)(2,1)S(1)} collective-permute-done((bf16[320,384]{1,0:T(8,128)(2,1)S(1)}, bf16[320,384]{1,0:T(8,128)(2,1)S(1)}, u32[]{:S(2)}, u32[]{:S(2)}) %collective-permute-start.8) | collective-permute-done | bytes 245792 | tf_op jit(solution)/shard_map/ppermute | solution.py:26
  38.7 2.0 %collective-permute-start.11 = (bf16[320,384]{1,0:T(8,128)(2,1)}, bf16[320,384]{1,0:T(8,128)(2,1)}, u32[]{:S(2)}, u32[]{:S(2)}) collective-permute-start(bf16[320,384]{1,0:T(8,128)(2,1)} %add_convert_fusion.29), channel_id=1, source_target_pairs={{0,1},{1,0},{2,3},{3,2},{4,5},{5,4},{6,7},{7,6},{8,9},{9,8},{10,11... | collective-permute-start | bytes 737288 | tf_op jit(solution)/shard_map/ppermute | solution.py:305
  40.7 1.5 %collective-permute-start.35 = (bf16[512,384]{1,0:T(8,128)(2,1)}, bf16[512,384]{1,0:T(8,128)(2,1)S(1)}, u32[]{:S(2)}, u32[]{:S(2)}) collective-permute-start(bf16[512,384]{1,0:T(8,128)(2,1)} %copy-done.12), channel_id=1, source_target_pairs={{0,8},{4,12},{8,0},{12,4},{1,9},{5,13},{9,1},{13,5},{2,10},{6,14},... | collective-permute-start | bytes 1179656 | tf_op jit(solution)/shard_map/ppermute | solution.py:26
  42.3 1.1 copy-done.7
  43.4 1.1 copy-done.9
  44.4 11.7 %shard_map.72 = (bf16[640,384]{1,0:T(8,128)(2,1)S(1)}, bf16[320,384]{1,0:T(8,128)(2,1)S(1)}, bf16[320,384]{1,0:T(8,128)(2,1)S(1)}, bf16[640,384]{1,0:T(8,128)(2,...) custom-call(s32[2]{0:T(128)S(1)} %pad_add_fusion.idx_ref, ...), custom_call_target="tpu_custom_call" | custom-call | tf_op jit(solution)/shard_map/pallas_call | solution.py:211
  56.1 2.0 %collective-permute-start.10 = (bf16[320,384]{1,0:T(8,128)(2,1)S(1)}, bf16[320,384]{1,0:T(8,128)(2,1)S(1)}, u32[]{:S(2)}, u32[]{:S(2)}) collective-permute-start(bf16[320,384]{1,0:T(8,128)(2,1)S(1)} %get-tuple-element.74), channel_id=1, source_target_pairs={{0,16},{16,0},{1,17},{17,1},{2,18},{18,2},{3,19},{19,3},{4,20},{20... | collective-permute-start | bytes 737288 | tf_op jit(solution)/shard_map/ppermute | solution.py:26
  58.2 1.0 add_convert_fusion.28
  59.7 1.9 %collective-permute-start.9 = (bf16[640,384]{1,0:T(8,128)(2,1)S(1)}, bf16[640,384]{1,0:T(8,128)(2,1)S(1)}, u32[]{:S(2)}, u32[]{:S(2)}) collective-permute-start(bf16[640,384]{1,0:T(8,128)(2,1)S(1)} %get-tuple-element.72), channel_id=1, source_target_pairs={{0,16},{16,0},{1,17},{17,1},{2,18},{18,2},{3,19},{19,3},{4,20},{20... | collective-permute-start | bytes 1474568 | tf_op jit(solution)/shard_map/ppermute | solution.py:26
  61.6 1.1 add_convert_fusion.27
  62.8 2.3 %collective-permute-done.10 = bf16[320,384]{1,0:T(8,128)(2,1)S(1)} collective-permute-done((bf16[320,384]{1,0:T(8,128)(2,1)S(1)}, bf16[320,384]{1,0:T(8,128)(2,1)S(1)}, u32[]{:S(2)}, u32[]{:S(2)}) %collective-permute-start.10) | collective-permute-done | bytes 245792 | tf_op jit(solution)/shard_map/ppermute | solution.py:26
  65.8 4.4 %collective-permute-start.12 = (bf16[320,384]{1,0:T(8,128)(2,1)S(1)}, bf16[320,384]{1,0:T(8,128)(2,1)S(1)}, u32[]{:S(2)}, u32[]{:S(2)}) collective-permute-start(bf16[320,384]{1,0:T(8,128)(2,1)S(1)} %add_convert_fusion.26), channel_id=1, source_target_pairs={{0,1},{1,0},{2,3},{3,2},{4,5},{5,4},{6,7},{7,6},{8,9},{9,8},{10,11... | collective-permute-start | bytes 737288 | tf_op jit(solution)/shard_map/ppermute | solution.py:305
  71.2 9.1 %collective-permute-start.17 = (bf16[320,384]{1,0:T(8,128)(2,1)S(1)}, bf16[320,384]{1,0:T(8,128)(2,1)S(1)}, u32[]{:S(2)}, u32[]{:S(2)}) collective-permute-start(bf16[320,384]{1,0:T(8,128)(2,1)S(1)} %broadcast_select_fusion.16), channel_id=1, source_target_pairs={{0,1},{1,0},{2,3},{3,2},{4,5},{5,4},{6,7},{7,6},{8,9},{9,8},{10,11... | collective-permute-start | bytes 737288 | tf_op jit(solution)/shard_map/ppermute | solution.py:305
  81.7 2.4 %collective-permute-start.20 = (bf16[640,384]{1,0:T(8,128)(2,1)S(1)}, bf16[640,384]{1,0:T(8,128)(2,1)S(1)}, u32[]{:S(2)}, u32[]{:S(2)}) collective-permute-start(bf16[640,384]{1,0:T(8,128)(2,1)S(1)} %get-tuple-element.90), channel_id=1, source_target_pairs={{0,16},{16,0},{1,17},{17,1},{2,18},{18,2},{3,19},{19,3},{4,20},{20... | collective-permute-start | bytes 1474568 | tf_op jit(solution)/shard_map/ppermute | solution.py:26
  84.5 3.0 %collective-permute-start.22 = (bf16[320,384]{1,0:T(8,128)(2,1)S(1)}, bf16[320,384]{1,0:T(8,128)(2,1)S(1)}, u32[]{:S(2)}, u32[]{:S(2)}) collective-permute-start(bf16[320,384]{1,0:T(8,128)(2,1)S(1)} %broadcast_select_fusion.15), channel_id=1, source_target_pairs={{0,1},{1,0},{2,3},{3,2},{4,5},{5,4},{6,7},{7,6},{8,9},{9,8},{10,11... | collective-permute-start | bytes 737288 | tf_op jit(solution)/shard_map/ppermute | solution.py:305
  88.5 5.0 %collective-permute-done.22 = bf16[320,384]{1,0:T(8,128)(2,1)S(1)} collective-permute-done((bf16[320,384]{1,0:T(8,128)(2,1)S(1)}, bf16[320,384]{1,0:T(8,128)(2,1)S(1)}, u32[]{:S(2)}, u32[]{:S(2)}) %collective-permute-start.22) | collective-permute-done | bytes 245792 | tf_op jit(solution)/shard_map/ppermute | solution.py:305
  93.4 1.7 %collective-permute-start.25 = (bf16[320,384]{1,0:T(8,128)(2,1)S(1)}, bf16[320,384]{1,0:T(8,128)(2,1)S(1)}, u32[]{:S(2)}, u32[]{:S(2)}) collective-permute-start(bf16[320,384]{1,0:T(8,128)(2,1)S(1)} %broadcast_select_fusion.14), channel_id=1, source_target_pairs={{0,1},{1,0},{2,3},{3,2},{4,5},{5,4},{6,7},{7,6},{8,9},{9,8},{10,11... | collective-permute-start | bytes 737288 | tf_op jit(solution)/shard_map/ppermute | solution.py:305
  95.3 0.9 collective-permute-start.24
  96.3 1.0 collective-permute-start.19
  97.5 3.0 %collective-permute-done.25 = bf16[320,384]{1,0:T(8,128)(2,1)S(1)} collective-permute-done((bf16[320,384]{1,0:T(8,128)(2,1)S(1)}, bf16[320,384]{1,0:T(8,128)(2,1)S(1)}, u32[]{:S(2)}, u32[]{:S(2)}) %collective-permute-start.25) | collective-permute-done | bytes 245792 | tf_op jit(solution)/shard_map/ppermute | solution.py:305
  100.5 1.5 %collective-permute-start.23 = (bf16[320,384]{1,0:T(8,128)(2,1)S(1)}, bf16[320,384]{1,0:T(8,128)(2,1)S(1)}, u32[]{:S(2)}, u32[]{:S(2)}) collective-permute-start(bf16[320,384]{1,0:T(8,128)(2,1)S(1)} %broadcast_select_fusion.13), channel_id=1, source_target_pairs={{0,1},{1,0},{2,3},{3,2},{4,5},{5,4},{6,7},{7,6},{8,9},{9,8},{10,11... | collective-permute-start | bytes 737288 | tf_op jit(solution)/shard_map/ppermute | solution.py:305
  103.0 5.3 %collective-permute-done.19 = bf16[640,384]{1,0:T(8,128)(2,1)S(1)} collective-permute-done((bf16[640,384]{1,0:T(8,128)(2,1)S(1)}, bf16[640,384]{1,0:T(8,128)(2,1)S(1)}, u32[]{:S(2)}, u32[]{:S(2)}) %collective-permute-start.19) | collective-permute-done | bytes 491552 | tf_op jit(solution)/shard_map/ppermute | solution.py:26
  108.3 4.9 %collective-permute-start.27 = (bf16[320,384]{1,0:T(8,128)(2,1)S(1)}, bf16[320,384]{1,0:T(8,128)(2,1)S(1)}, u32[]{:S(2)}, u32[]{:S(2)}) collective-permute-start(bf16[320,384]{1,0:T(8,128)(2,1)S(1)} %broadcast_select_fusion.12), channel_id=1, source_target_pairs={{0,1},{1,0},{2,3},{3,2},{4,5},{5,4},{6,7},{7,6},{8,9},{9,8},{10,11... | collective-permute-start | bytes 737288 | tf_op jit(solution)/shard_map/ppermute | solution.py:305
  114.3 1.6 %collective-permute-start.31 = (bf16[320,384]{1,0:T(8,128)(2,1)S(1)}, bf16[320,384]{1,0:T(8,128)(2,1)S(1)}, u32[]{:S(2)}, u32[]{:S(2)}) collective-permute-start(bf16[320,384]{1,0:T(8,128)(2,1)S(1)} %broadcast_select_fusion.11), channel_id=1, source_target_pairs={{0,1},{1,0},{2,3},{3,2},{4,5},{5,4},{6,7},{7,6},{8,9},{9,8},{10,11... | collective-permute-start | bytes 737288 | tf_op jit(solution)/shard_map/ppermute | solution.py:305
  115.9 4.0 %collective-permute-done.27 = bf16[320,384]{1,0:T(8,128)(2,1)S(1)} collective-permute-done((bf16[320,384]{1,0:T(8,128)(2,1)S(1)}, bf16[320,384]{1,0:T(8,128)(2,1)S(1)}, u32[]{:S(2)}, u32[]{:S(2)}) %collective-permute-start.27) | collective-permute-done | bytes 245792 | tf_op jit(solution)/shard_map/ppermute | solution.py:305
  120.9 3.3 %collective-permute-start.29 = (bf16[320,384]{1,0:T(8,128)(2,1)S(1)}, bf16[320,384]{1,0:T(8,128)(2,1)S(1)}, u32[]{:S(2)}, u32[]{:S(2)}) collective-permute-start(bf16[320,384]{1,0:T(8,128)(2,1)S(1)} %broadcast_select_fusion.10), channel_id=1, source_target_pairs={{0,1},{1,0},{2,3},{3,2},{4,5},{5,4},{6,7},{7,6},{8,9},{9,8},{10,11... | collective-permute-start | bytes 737288 | tf_op jit(solution)/shard_map/ppermute | solution.py:305
  125.9 5.4 %collective-permute-start.33 = (bf16[320,384]{1,0:T(8,128)(2,1)S(1)}, bf16[320,384]{1,0:T(8,128)(2,1)S(1)}, u32[]{:S(2)}, u32[]{:S(2)}) collective-permute-start(bf16[320,384]{1,0:T(8,128)(2,1)S(1)} %add_convert_fusion.3), channel_id=1, source_target_pairs={{0,1},{1,0},{2,3},{3,2},{4,5},{5,4},{6,7},{7,6},{8,9},{9,8},{10,11... | collective-permute-start | bytes 737288 | tf_op jit(solution)/shard_map/ppermute | solution.py:305
  131.4 0.8 collective-permute-start.32
  132.3 4.5 %collective-permute-start.38 = (bf16[320,384]{1,0:T(8,128)(2,1)S(1)}, bf16[320,384]{1,0:T(8,128)(2,1)S(1)}, u32[]{:S(2)}, u32[]{:S(2)}) collective-permute-start(bf16[320,384]{1,0:T(8,128)(2,1)S(1)} %add_convert_fusion.1), channel_id=1, source_target_pairs={{0,1},{1,0},{2,3},{3,2},{4,5},{5,4},{6,7},{7,6},{8,9},{9,8},{10,11... | collective-permute-start | bytes 737288 | tf_op jit(solution)/shard_map/ppermute | solution.py:305
  136.8 2.2 %shard_map.73.b = f32[5,640,384]{2,1,0:T(8,128)} custom-call(bf16[320,384]{1,0:T(8,128)(2,1)S(1)} %broadcast_select_fusion.9.refs_0_, bf16[320,384]{1,0:T(8,128)(2,1)S(1)} %broadcast_select_fusion.7.refs_1_, bf16[320,384]{1,0:T(8,128)(2,1)S(1)} %broadcast_select_fusion.6.refs_2_, bf16[320,384]{1,0:T(8,128)(2,1)S(1)} %broadcast_select_fusion.5.refs_3_, ...), custom_call_target="tpu_custom_call" | custom-call | tf_op jit(solution)/shard_map/pallas_call | solution.py:238
  139.1 2.1 %collective-permute-start.39 = (bf16[320,384]{1,0:T(8,128)(2,1)S(1)}, bf16[320,384]{1,0:T(8,128)(2,1)S(1)}, u32[]{:S(2)}, u32[]{:S(2)}) collective-permute-start(bf16[320,384]{1,0:T(8,128)(2,1)S(1)} %add_convert_fusion), channel_id=1, source_target_pairs={{0,1},{1,0},{2,3},{3,2},{4,5},{5,4},{6,7},{7,6},{8,9},{9,8},{10,11... | collective-permute-start | bytes 737288 | tf_op jit(solution)/shard_map/ppermute | solution.py:305
  141.3 3.5 %shard_map.74 = bf16[512,640]{1,0:T(8,128)(2,1)} custom-call(s32[2]{0:T(128)S(1)} %pad_add_fusion.idx_ref, bf16[512,384]{1,0:T(8,128)(2,1)S(1)} %copy-done.13, bf16[512,384]{1,0:T(8,128)(2,1)S(1)} %collective-permute-done.35.refs_1_, bf16[512,384]{1,0:T(8,128)(2,1)S(1)} %collective-permute-done.36.refs_2_, ...), custom_call_target="tpu_custom_call" | custom-call | tf_op jit(solution)/shard_map/pallas_call | solution.py:211
  145.5 1.0 shard_map.75
  (117 shorter events, 14.8 us)
Async XLA Ops:
  0.6 10.9 %collective-permute-start.1 = (bf16[320,1024]{1,0:T(8,128)(2,1)}, bf16[320,1024]{1,0:T(8,128)(2,1)S(1)}, u32[]{:S(2)}, u32[]{:S(2)}) collective-permute-start(bf16[320,1024]{1,0:T(8,128)(2,1)} %bitcast.8), channel_id=1, source_target_pairs={{0,4},{4,0},{8,12},{12,8},{1,5},{5,1},{9,13},{13,9},{2,6},{6,2},{1... | collective-permute-start | bytes 1966088 | tf_op jit(solution)/shard_map/ppermute | solution.py:26
  1.1 18.7 %collective-permute-start = (bf16[320,1024]{1,0:T(8,128)(2,1)}, bf16[320,1024]{1,0:T(8,128)(2,1)S(1)}, u32[]{:S(2)}, u32[]{:S(2)}) collective-permute-start(bf16[320,1024]{1,0:T(8,128)(2,1)} %bitcast.9), channel_id=1, source_target_pairs={{0,8},{4,12},{8,0},{12,4},{1,9},{5,13},{9,1},{13,5},{2,10},{6,14},... | collective-permute-start | bytes 1966088 | tf_op jit(solution)/shard_map/ppermute | solution.py:26
  4.9 17.0 %copy-start.2 = (bf16[1,1024,320]{1,2,0:T(8,128)(2,1)S(1)}, bf16[1,1024,320]{1,2,0:T(8,128)(2,1)}, u32[]{:S(2)}) copy-start(bf16[1,1024,320]{1,2,0:T(8,128)(2,1)} %param.5) | copy-start | bytes 1966084
  4.9 17.0 %copy-start.11 = (bf16[1,512,384]{2,1,0:T(8,128)(2,1)S(1)}, bf16[1,512,384]{2,1,0:T(8,128)(2,1)}, u32[]{:S(2)}) copy-start(bf16[1,512,384]{2,1,0:T(8,128)(2,1)} %param.9) | copy-start | bytes 1179652
  5.0 3.8 %collective-permute-start.2 = (f32[8,384]{1,0:T(8,128)S(1)}, f32[8,384]{1,0:T(8,128)S(1)}, u32[]{:S(2)}, u32[]{:S(2)}) collective-permute-start(f32[8,384]{1,0:T(8,128)S(1)} %shard_map.68), channel_id=1, source_target_pairs={{0,16},{16,0},{1,17},{17,1},{2,18},{18,2},{3,19},{19,3},{4,20},{20... | collective-permute-start | bytes 36872 | tf_op jit(solution)/shard_map/ppermute | solution.py:26
  8.9 10.5 %collective-permute-start.5 = (f32[8,384]{1,0:T(8,128)S(1)}, f32[8,384]{1,0:T(8,128)S(1)}, u32[]{:S(2)}, u32[]{:S(2)}) collective-permute-start(f32[8,384]{1,0:T(8,128)S(1)} %maximum_maximum_fusion.refs_2_.refs_4_), channel_id=1, source_target_pairs={{0,12},{4,8},{8,4},{12,0},{1,13},{5,9},{9,5},{13,1},{2,14},{6,10},... | collective-permute-start | bytes 36872 | tf_op jit(solution)/shard_map/ppermute | solution.py:26
  8.9 10.9 %collective-permute-start.4 = (f32[8,384]{1,0:T(8,128)S(1)}, f32[8,384]{1,0:T(8,128)S(1)}, u32[]{:S(2)}, u32[]{:S(2)}) collective-permute-start(f32[8,384]{1,0:T(8,128)S(1)} %maximum_maximum_fusion.refs_2_.refs_4_), channel_id=1, source_target_pairs={{0,8},{4,12},{8,0},{12,4},{1,9},{5,13},{9,1},{13,5},{2,10},{6,14},... | collective-permute-start | bytes 36872 | tf_op jit(solution)/shard_map/ppermute | solution.py:26
  9.8 1.8 %collective-permute-start.3 = (f32[8,384]{1,0:T(8,128)S(1)}, f32[8,384]{1,0:T(8,128)S(1)}, u32[]{:S(2)}, u32[]{:S(2)}) collective-permute-start(f32[8,384]{1,0:T(8,128)S(1)} %maximum_maximum_fusion.refs_2_.refs_4_), channel_id=1, source_target_pairs={{0,4},{4,0},{8,12},{12,8},{1,5},{5,1},{9,13},{13,9},{2,6},{6,2},{1... | collective-permute-start | bytes 36872 | tf_op jit(solution)/shard_map/ppermute | solution.py:26
  12.7 2.4 %copy-start.3 = (bf16[5,1280,384]{2,1,0:T(8,128)(2,1)S(1)}, bf16[5,1280,384]{2,1,0:T(8,128)(2,1)}, u32[]{:S(2)}) copy-start(bf16[5,1280,384]{2,1,0:T(8,128)(2,1)} %refs_8_.2) | copy-start | bytes 14745604
  15.1 6.9 %copy-start.4 = (bf16[5,1280,384]{2,1,0:T(8,128)(2,1)S(1)}, bf16[5,1280,384]{2,1,0:T(8,128)(2,1)}, u32[]{:S(2)}) copy-start(bf16[5,1280,384]{2,1,0:T(8,128)(2,1)} %refs_8_.2) | copy-start | bytes 14745604
  19.8 2.1 %collective-permute-start.6 = (bf16[320,1024]{1,0:T(8,128)(2,1)S(1)}, bf16[320,1024]{1,0:T(8,128)(2,1)S(1)}, u32[]{:S(2)}, u32[]{:S(2)}) collective-permute-start(bf16[320,1024]{1,0:T(8,128)(2,1)S(1)} %collective-permute-done.refs_1_), channel_id=1, source_target_pairs={{0,4},{4,0},{8,12},{12,8},{1,5},{5,1},{9,13},{13,9},{2,6},{6,2},{1... | collective-permute-start | bytes 1966088 | tf_op jit(solution)/shard_map/ppermute | solution.py:26
  21.9 13.0 %copy-start.8 = (bf16[320,1024]{1,0:T(8,128)(2,1)}, bf16[320,1024]{1,0:T(8,128)(2,1)S(1)}, u32[]{:S(2)}) copy-start(bf16[320,1024]{1,0:T(8,128)(2,1)S(1)} %collective-permute-done.6.refs_3_) | copy-start | bytes 1966084
  29.7 5.2 %copy-start.12 = (bf16[512,384]{1,0:T(8,128)(2,1)}, bf16[512,384]{1,0:T(8,128)(2,1)S(1)}, u32[]{:S(2)}) copy-start(bf16[512,384]{1,0:T(8,128)(2,1)S(1)} %get-tuple-element.111.refs_0_) | copy-start | bytes 1179652
  29.7 8.2 %collective-permute-start.8 = (bf16[320,384]{1,0:T(8,128)(2,1)S(1)}, bf16[320,384]{1,0:T(8,128)(2,1)S(1)}, u32[]{:S(2)}, u32[]{:S(2)}) collective-permute-start(bf16[320,384]{1,0:T(8,128)(2,1)S(1)} %get-tuple-element.70), channel_id=1, source_target_pairs={{0,16},{16,0},{1,17},{17,1},{2,18},{18,2},{3,19},{19,3},{4,20},{20... | collective-permute-start | bytes 737288 | tf_op jit(solution)/shard_map/ppermute | solution.py:26
  34.9 23.3 %collective-permute-start.7 = (bf16[320,384]{1,0:T(8,128)(2,1)}, bf16[320,384]{1,0:T(8,128)(2,1)}, u32[]{:S(2)}, u32[]{:S(2)}) collective-permute-start(bf16[320,384]{1,0:T(8,128)(2,1)} %get-tuple-element.69), channel_id=1, source_target_pairs={{0,16},{16,0},{1,17},{17,1},{2,18},{18,2},{3,19},{19,3},{4,20},{20... | collective-permute-start | bytes 737288 | tf_op jit(solution)/shard_map/ppermute | solution.py:26
  38.7 21.1 %collective-permute-start.11 = (bf16[320,384]{1,0:T(8,128)(2,1)}, bf16[320,384]{1,0:T(8,128)(2,1)}, u32[]{:S(2)}, u32[]{:S(2)}) collective-permute-start(bf16[320,384]{1,0:T(8,128)(2,1)} %add_convert_fusion.29), channel_id=1, source_target_pairs={{0,1},{1,0},{2,3},{3,2},{4,5},{5,4},{6,7},{7,6},{8,9},{9,8},{10,11... | collective-permute-start | bytes 737288 | tf_op jit(solution)/shard_map/ppermute | solution.py:305
  40.7 40.3 %collective-permute-start.35 = (bf16[512,384]{1,0:T(8,128)(2,1)}, bf16[512,384]{1,0:T(8,128)(2,1)S(1)}, u32[]{:S(2)}, u32[]{:S(2)}) collective-permute-start(bf16[512,384]{1,0:T(8,128)(2,1)} %copy-done.12), channel_id=1, source_target_pairs={{0,8},{4,12},{8,0},{12,4},{1,9},{5,13},{9,1},{13,5},{2,10},{6,14},... | collective-permute-start | bytes 1179656 | tf_op jit(solution)/shard_map/ppermute | solution.py:26
  44.4 36.7 %copy-start.13 = (bf16[512,384]{1,0:T(8,128)(2,1)S(1)}, bf16[512,384]{1,0:T(8,128)(2,1)}, u32[]{:S(2)}) copy-start(bf16[512,384]{1,0:T(8,128)(2,1)} %copy-done.12) | copy-start | bytes 1179652
  56.1 9.0 %collective-permute-start.10 = (bf16[320,384]{1,0:T(8,128)(2,1)S(1)}, bf16[320,384]{1,0:T(8,128)(2,1)S(1)}, u32[]{:S(2)}, u32[]{:S(2)}) collective-permute-start(bf16[320,384]{1,0:T(8,128)(2,1)S(1)} %get-tuple-element.74), channel_id=1, source_target_pairs={{0,16},{16,0},{1,17},{17,1},{2,18},{18,2},{3,19},{19,3},{4,20},{20... | collective-permute-start | bytes 737288 | tf_op jit(solution)/shard_map/ppermute | solution.py:26
  58.1 13.0 %collective-permute-start.13 = (bf16[320,384]{1,0:T(8,128)(2,1)S(1)}, bf16[320,384]{1,0:T(8,128)(2,1)S(1)}, u32[]{:S(2)}, u32[]{:S(2)}) collective-permute-start(bf16[320,384]{1,0:T(8,128)(2,1)S(1)} %get-tuple-element.77), channel_id=1, source_target_pairs={{0,16},{16,0},{1,17},{17,1},{2,18},{18,2},{3,19},{19,3},{4,20},{20... | collective-permute-start | bytes 737288 | tf_op jit(solution)/shard_map/ppermute | solution.py:26
  59.2 6.6 %collective-permute-start.15 = (bf16[320,384]{1,0:T(8,128)(2,1)S(1)}, bf16[320,384]{1,0:T(8,128)(2,1)S(1)}, u32[]{:S(2)}, u32[]{:S(2)}) collective-permute-start(bf16[320,384]{1,0:T(8,128)(2,1)S(1)} %add_convert_fusion.28), channel_id=1, source_target_pairs={{0,1},{1,0},{2,3},{3,2},{4,5},{5,4},{6,7},{7,6},{8,9},{9,8},{10,11... | collective-permute-start | bytes 737288 | tf_op jit(solution)/shard_map/ppermute | solution.py:305
  59.7 22.0 %collective-permute-start.9 = (bf16[640,384]{1,0:T(8,128)(2,1)S(1)}, bf16[640,384]{1,0:T(8,128)(2,1)S(1)}, u32[]{:S(2)}, u32[]{:S(2)}) collective-permute-start(bf16[640,384]{1,0:T(8,128)(2,1)S(1)} %get-tuple-element.72), channel_id=1, source_target_pairs={{0,16},{16,0},{1,17},{17,1},{2,18},{18,2},{3,19},{19,3},{4,20},{20... | collective-permute-start | bytes 1474568 | tf_op jit(solution)/shard_map/ppermute | solution.py:26
  65.1 5.3 %collective-permute-start.14 = (bf16[320,384]{1,0:T(8,128)(2,1)S(1)}, bf16[320,384]{1,0:T(8,128)(2,1)S(1)}, u32[]{:S(2)}, u32[]{:S(2)}) collective-permute-start(bf16[320,384]{1,0:T(8,128)(2,1)S(1)} %add_convert_fusion.27), channel_id=1, source_target_pairs={{1,2},{2,1},{5,6},{6,5},{9,10},{10,9},{13,14},{14,13},{17,18},{18,... | collective-permute-start | bytes 737288 | tf_op jit(solution)/shard_map/ppermute | solution.py:311
  65.8 14.4 %collective-permute-start.12 = (bf16[320,384]{1,0:T(8,128)(2,1)S(1)}, bf16[320,384]{1,0:T(8,128)(2,1)S(1)}, u32[]{:S(2)}, u32[]{:S(2)}) collective-permute-start(bf16[320,384]{1,0:T(8,128)(2,1)S(1)} %add_convert_fusion.26), channel_id=1, source_target_pairs={{0,1},{1,0},{2,3},{3,2},{4,5},{5,4},{6,7},{7,6},{8,9},{9,8},{10,11... | collective-permute-start | bytes 737288 | tf_op jit(solution)/shard_map/ppermute | solution.py:305
  70.3 10.7 %collective-permute-start.18 = (bf16[320,384]{1,0:T(8,128)(2,1)S(1)}, bf16[320,384]{1,0:T(8,128)(2,1)S(1)}, u32[]{:S(2)}, u32[]{:S(2)}) collective-permute-start(bf16[320,384]{1,0:T(8,128)(2,1)S(1)} %add_convert_fusion.25), channel_id=1, source_target_pairs={{1,2},{2,1},{5,6},{6,5},{9,10},{10,9},{13,14},{14,13},{17,18},{18,... | collective-permute-start | bytes 737288 | tf_op jit(solution)/shard_map/ppermute | solution.py:311
  71.2 13.2 %collective-permute-start.17 = (bf16[320,384]{1,0:T(8,128)(2,1)S(1)}, bf16[320,384]{1,0:T(8,128)(2,1)S(1)}, u32[]{:S(2)}, u32[]{:S(2)}) collective-permute-start(bf16[320,384]{1,0:T(8,128)(2,1)S(1)} %broadcast_select_fusion.16), channel_id=1, source_target_pairs={{0,1},{1,0},{2,3},{3,2},{4,5},{5,4},{6,7},{7,6},{8,9},{9,8},{10,11... | collective-permute-start | bytes 737288 | tf_op jit(solution)/shard_map/ppermute | solution.py:305
  80.3 7.3 %collective-permute-start.16 = (bf16[320,384]{1,0:T(8,128)(2,1)S(1)}, bf16[320,384]{1,0:T(8,128)(2,1)S(1)}, u32[]{:S(2)}, u32[]{:S(2)}) collective-permute-start(bf16[320,384]{1,0:T(8,128)(2,1)S(1)} %add_convert_fusion.22), channel_id=1, source_target_pairs={{1,2},{2,1},{5,6},{6,5},{9,10},{10,9},{13,14},{14,13},{17,18},{18,... | collective-permute-start | bytes 737288 | tf_op jit(solution)/shard_map/ppermute | solution.py:311
  81.1 60.1 %collective-permute-start.36 = (bf16[512,384]{1,0:T(8,128)(2,1)S(1)}, bf16[512,384]{1,0:T(8,128)(2,1)S(1)}, u32[]{:S(2)}, u32[]{:S(2)}) collective-permute-start(bf16[512,384]{1,0:T(8,128)(2,1)S(1)} %copy-done.13), channel_id=1, source_target_pairs={{0,4},{4,0},{8,12},{12,8},{1,5},{5,1},{9,13},{13,9},{2,6},{6,2},{1... | collective-permute-start | bytes 1179656 | tf_op jit(solution)/shard_map/ppermute | solution.py:26
  81.2 60.0 %collective-permute-start.37 = (bf16[512,384]{1,0:T(8,128)(2,1)S(1)}, bf16[512,384]{1,0:T(8,128)(2,1)S(1)}, u32[]{:S(2)}, u32[]{:S(2)}) collective-permute-start(bf16[512,384]{1,0:T(8,128)(2,1)S(1)} %collective-permute-done.35.refs_1_), channel_id=1, source_target_pairs={{0,4},{4,0},{8,12},{12,8},{1,5},{5,1},{9,13},{13,9},{2,6},{6,2},{1... | collective-permute-start | bytes 1179656 | tf_op jit(solution)/shard_map/ppermute | solution.py:26
  81.7 14.6 %collective-permute-start.20 = (bf16[640,384]{1,0:T(8,128)(2,1)S(1)}, bf16[640,384]{1,0:T(8,128)(2,1)S(1)}, u32[]{:S(2)}, u32[]{:S(2)}) collective-permute-start(bf16[640,384]{1,0:T(8,128)(2,1)S(1)} %get-tuple-element.90), channel_id=1, source_target_pairs={{0,16},{16,0},{1,17},{17,1},{2,18},{18,2},{3,19},{19,3},{4,20},{20... | collective-permute-start | bytes 1474568 | tf_op jit(solution)/shard_map/ppermute | solution.py:26
  84.5 9.0 %collective-permute-start.22 = (bf16[320,384]{1,0:T(8,128)(2,1)S(1)}, bf16[320,384]{1,0:T(8,128)(2,1)S(1)}, u32[]{:S(2)}, u32[]{:S(2)}) collective-permute-start(bf16[320,384]{1,0:T(8,128)(2,1)S(1)} %broadcast_select_fusion.15), channel_id=1, source_target_pairs={{0,1},{1,0},{2,3},{3,2},{4,5},{5,4},{6,7},{7,6},{8,9},{9,8},{10,11... | collective-permute-start | bytes 737288 | tf_op jit(solution)/shard_map/ppermute | solution.py:305
  87.6 7.7 %collective-permute-start.21 = (bf16[320,384]{1,0:T(8,128)(2,1)S(1)}, bf16[320,384]{1,0:T(8,128)(2,1)S(1)}, u32[]{:S(2)}, u32[]{:S(2)}) collective-permute-start(bf16[320,384]{1,0:T(8,128)(2,1)S(1)} %add_convert_fusion.19), channel_id=1, source_target_pairs={{1,2},{2,1},{5,6},{6,5},{9,10},{10,9},{13,14},{14,13},{17,18},{18,... | collective-permute-start | bytes 737288 | tf_op jit(solution)/shard_map/ppermute | solution.py:311
  93.4 7.1 %collective-permute-start.25 = (bf16[320,384]{1,0:T(8,128)(2,1)S(1)}, bf16[320,384]{1,0:T(8,128)(2,1)S(1)}, u32[]{:S(2)}, u32[]{:S(2)}) collective-permute-start(bf16[320,384]{1,0:T(8,128)(2,1)S(1)} %broadcast_select_fusion.14), channel_id=1, source_target_pairs={{0,1},{1,0},{2,3},{3,2},{4,5},{5,4},{6,7},{7,6},{8,9},{9,8},{10,11... | collective-permute-start | bytes 737288 | tf_op jit(solution)/shard_map/ppermute | solution.py:305
  95.3 6.7 %collective-permute-start.24 = (bf16[320,384]{1,0:T(8,128)(2,1)S(1)}, bf16[320,384]{1,0:T(8,128)(2,1)S(1)}, u32[]{:S(2)}, u32[]{:S(2)}) collective-permute-start(bf16[320,384]{1,0:T(8,128)(2,1)S(1)} %add_convert_fusion.16), channel_id=1, source_target_pairs={{1,2},{2,1},{5,6},{6,5},{9,10},{10,9},{13,14},{14,13},{17,18},{18,... | collective-permute-start | bytes 737288 | tf_op jit(solution)/shard_map/ppermute | solution.py:311
  96.3 11.9 %collective-permute-start.19 = (bf16[640,384]{1,0:T(8,128)(2,1)S(1)}, bf16[640,384]{1,0:T(8,128)(2,1)S(1)}, u32[]{:S(2)}, u32[]{:S(2)}) collective-permute-start(bf16[640,384]{1,0:T(8,128)(2,1)S(1)} %get-tuple-element.87), channel_id=1, source_target_pairs={{0,16},{16,0},{1,17},{17,1},{2,18},{18,2},{3,19},{19,3},{4,20},{20... | collective-permute-start | bytes 1474568 | tf_op jit(solution)/shard_map/ppermute | solution.py:26
  100.5 12.8 %collective-permute-start.23 = (bf16[320,384]{1,0:T(8,128)(2,1)S(1)}, bf16[320,384]{1,0:T(8,128)(2,1)S(1)}, u32[]{:S(2)}, u32[]{:S(2)}) collective-permute-start(bf16[320,384]{1,0:T(8,128)(2,1)S(1)} %broadcast_select_fusion.13), channel_id=1, source_target_pairs={{0,1},{1,0},{2,3},{3,2},{4,5},{5,4},{6,7},{7,6},{8,9},{9,8},{10,11... | collective-permute-start | bytes 737288 | tf_op jit(solution)/shard_map/ppermute | solution.py:305
  102.1 12.0 %collective-permute-start.28 = (bf16[320,384]{1,0:T(8,128)(2,1)S(1)}, bf16[320,384]{1,0:T(8,128)(2,1)S(1)}, u32[]{:S(2)}, u32[]{:S(2)}) collective-permute-start(bf16[320,384]{1,0:T(8,128)(2,1)S(1)} %add_convert_fusion.13), channel_id=1, source_target_pairs={{1,2},{2,1},{5,6},{6,5},{9,10},{10,9},{13,14},{14,13},{17,18},{18,... | collective-permute-start | bytes 737288 | tf_op jit(solution)/shard_map/ppermute | solution.py:311
  108.3 11.6 %collective-permute-start.27 = (bf16[320,384]{1,0:T(8,128)(2,1)S(1)}, bf16[320,384]{1,0:T(8,128)(2,1)S(1)}, u32[]{:S(2)}, u32[]{:S(2)}) collective-permute-start(bf16[320,384]{1,0:T(8,128)(2,1)S(1)} %broadcast_select_fusion.12), channel_id=1, source_target_pairs={{0,1},{1,0},{2,3},{3,2},{4,5},{5,4},{6,7},{7,6},{8,9},{9,8},{10,11... | collective-permute-start | bytes 737288 | tf_op jit(solution)/shard_map/ppermute | solution.py:305
  113.4 7.3 %collective-permute-start.26 = (bf16[320,384]{1,0:T(8,128)(2,1)S(1)}, bf16[320,384]{1,0:T(8,128)(2,1)S(1)}, u32[]{:S(2)}, u32[]{:S(2)}) collective-permute-start(bf16[320,384]{1,0:T(8,128)(2,1)S(1)} %add_convert_fusion.10), channel_id=1, source_target_pairs={{1,2},{2,1},{5,6},{6,5},{9,10},{10,9},{13,14},{14,13},{17,18},{18,... | collective-permute-start | bytes 737288 | tf_op jit(solution)/shard_map/ppermute | solution.py:311
  114.3 10.7 %collective-permute-start.31 = (bf16[320,384]{1,0:T(8,128)(2,1)S(1)}, bf16[320,384]{1,0:T(8,128)(2,1)S(1)}, u32[]{:S(2)}, u32[]{:S(2)}) collective-permute-start(bf16[320,384]{1,0:T(8,128)(2,1)S(1)} %broadcast_select_fusion.11), channel_id=1, source_target_pairs={{0,1},{1,0},{2,3},{3,2},{4,5},{5,4},{6,7},{7,6},{8,9},{9,8},{10,11... | collective-permute-start | bytes 737288 | tf_op jit(solution)/shard_map/ppermute | solution.py:305
  120.1 5.7 %collective-permute-start.30 = (bf16[320,384]{1,0:T(8,128)(2,1)S(1)}, bf16[320,384]{1,0:T(8,128)(2,1)S(1)}, u32[]{:S(2)}, u32[]{:S(2)}) collective-permute-start(bf16[320,384]{1,0:T(8,128)(2,1)S(1)} %add_convert_fusion.7), channel_id=1, source_target_pairs={{1,2},{2,1},{5,6},{6,5},{9,10},{10,9},{13,14},{14,13},{17,18},{18,... | collective-permute-start | bytes 737288 | tf_op jit(solution)/shard_map/ppermute | solution.py:311
  120.9 10.3 %collective-permute-start.29 = (bf16[320,384]{1,0:T(8,128)(2,1)S(1)}, bf16[320,384]{1,0:T(8,128)(2,1)S(1)}, u32[]{:S(2)}, u32[]{:S(2)}) collective-permute-start(bf16[320,384]{1,0:T(8,128)(2,1)S(1)} %broadcast_select_fusion.10), channel_id=1, source_target_pairs={{0,1},{1,0},{2,3},{3,2},{4,5},{5,4},{6,7},{7,6},{8,9},{9,8},{10,11... | collective-permute-start | bytes 737288 | tf_op jit(solution)/shard_map/ppermute | solution.py:305
  125.1 7.1 %collective-permute-start.34 = (bf16[320,384]{1,0:T(8,128)(2,1)S(1)}, bf16[320,384]{1,0:T(8,128)(2,1)S(1)}, u32[]{:S(2)}, u32[]{:S(2)}) collective-permute-start(bf16[320,384]{1,0:T(8,128)(2,1)S(1)} %add_convert_fusion.4), channel_id=1, source_target_pairs={{1,2},{2,1},{5,6},{6,5},{9,10},{10,9},{13,14},{14,13},{17,18},{18,... | collective-permute-start | bytes 737288 | tf_op jit(solution)/shard_map/ppermute | solution.py:311
  125.9 10.9 %collective-permute-start.33 = (bf16[320,384]{1,0:T(8,128)(2,1)S(1)}, bf16[320,384]{1,0:T(8,128)(2,1)S(1)}, u32[]{:S(2)}, u32[]{:S(2)}) collective-permute-start(bf16[320,384]{1,0:T(8,128)(2,1)S(1)} %add_convert_fusion.3), channel_id=1, source_target_pairs={{0,1},{1,0},{2,3},{3,2},{4,5},{5,4},{6,7},{7,6},{8,9},{9,8},{10,11... | collective-permute-start | bytes 737288 | tf_op jit(solution)/shard_map/ppermute | solution.py:305
  131.3 9.9 %copy-start.10 = (bf16[1536,640]{1,0:T(8,128)(2,1)S(1)}, bf16[1536,640]{1,0:T(8,128)(2,1)}, u32[]{:S(2)}) copy-start(bf16[1536,640]{1,0:T(8,128)(2,1)} %refs_8_.3) | copy-start | bytes 5898244
  131.4 7.6 %collective-permute-start.32 = (bf16[320,384]{1,0:T(8,128)(2,1)S(1)}, bf16[320,384]{1,0:T(8,128)(2,1)S(1)}, u32[]{:S(2)}, u32[]{:S(2)}) collective-permute-start(bf16[320,384]{1,0:T(8,128)(2,1)S(1)} %add_convert_fusion.2), channel_id=1, source_target_pairs={{1,2},{2,1},{5,6},{6,5},{9,10},{10,9},{13,14},{14,13},{17,18},{18,... | collective-permute-start | bytes 737288 | tf_op jit(solution)/shard_map/ppermute | solution.py:311
  132.3 12.5 %collective-permute-start.38 = (bf16[320,384]{1,0:T(8,128)(2,1)S(1)}, bf16[320,384]{1,0:T(8,128)(2,1)S(1)}, u32[]{:S(2)}, u32[]{:S(2)}) collective-permute-start(bf16[320,384]{1,0:T(8,128)(2,1)S(1)} %add_convert_fusion.1), channel_id=1, source_target_pairs={{0,1},{1,0},{2,3},{3,2},{4,5},{5,4},{6,7},{7,6},{8,9},{9,8},{10,11... | collective-permute-start | bytes 737288 | tf_op jit(solution)/shard_map/ppermute | solution.py:305
  139.1 6.3 %collective-permute-start.39 = (bf16[320,384]{1,0:T(8,128)(2,1)S(1)}, bf16[320,384]{1,0:T(8,128)(2,1)S(1)}, u32[]{:S(2)}, u32[]{:S(2)}) collective-permute-start(bf16[320,384]{1,0:T(8,128)(2,1)S(1)} %add_convert_fusion), channel_id=1, source_target_pairs={{0,1},{1,0},{2,3},{3,2},{4,5},{5,4},{6,7},{7,6},{8,9},{9,8},{10,11... | collective-permute-start | bytes 737288 | tf_op jit(solution)/shard_map/ppermute | solution.py:305
  (6 other events, 6.5 us)

commit v9 on v8

--- a/solution.py
+++ b/solution.py
@@ -222,29 +222,38 @@
     return lax.optimization_barrier((value, *others))[0]
 
 
-def write_kernel(*refs):
+def write_kernel(end_ref, *refs):
     *part_refs, out_ref = refs
-    pieces = len(part_refs) // out_ref.shape[0]
+    count = len(part_refs) // 2
+    pieces = count // out_ref.shape[0]
     rows = part_refs[0].shape[0]
-    for i, ref in enumerate(part_refs):
+    for i in range(count):
         tap, r = i // pieces, i % pieces
-        out_ref[tap, r * rows : (r + 1) * rows, :] = ref[...].astype(F32)
+        for ref, here in ((part_refs[2 * i], end_ref[0] > 0), (part_refs[2 * i + 1], end_ref[0] == 0)):
+
+            @pl.when(here)
+            def _(ref=ref, tap=tap, r=r):
+                out_ref[tap, r * rows : (r + 1) * rows, :] = ref[...].astype(F32)
 
 
 def written(parts, taps, at, buffer, shape):
+    me = lax.axis_index("dp")
+    end = jnp.logical_or(me == 0, me == lax.axis_size("dp") - 1).astype(jnp.int32).reshape(1)
+    parts = [v for pair in parts for v in pair]
     rows, width = parts[0].shape
     extra = [] if buffer is None else [buffer]
-    kernel = write_kernel if buffer is None else lambda b, *refs: write_kernel(*refs)
+    kernel = write_kernel if buffer is None else lambda end, b, *refs: write_kernel(end, *refs)
     return pl.pallas_call(
         kernel,
         out_shape=jax.ShapeDtypeStruct(shape, F32),
         grid=(1,),
-        in_specs=[pl.BlockSpec(memory_space=pl.ANY)] * len(extra)
+        in_specs=[pl.BlockSpec(memory_space=pltpu.SMEM)]
+        + [pl.BlockSpec(memory_space=pl.ANY)] * len(extra)
         + [pl.BlockSpec((rows, width), lambda i: (0, 0))] * len(parts),
         out_specs=pl.BlockSpec((taps, shape[1], width), lambda i: (at // taps, 0, 0)),
-        input_output_aliases={0: 0} if extra else {},
+        input_output_aliases={1: 0} if extra else {},
         compiler_params=pltpu.CompilerParams(vmem_limit_bytes=16 * 1024 * 1024),
-    )(*extra, *parts)
+    )(end, *extra, *parts)
 
 
 def edge_kernel(head_ref, tail_ref, out_ref):
@@ -296,7 +305,7 @@
     h, p, s, outer, middle, sums = {}, {}, {}, {}, {}, {}
     for r in range(count + 5):
         if r < count:
-            last = h[r] = part(r, last)
+            h[r] = part(r, last)
         if r < count + 3:
             value = h.get(r, s.get(r - 3))
             if r in h and r - 3 in s:
@@ -310,9 +319,9 @@
                 last = p[r - 1] = lax.optimization_barrier(added(h[r - 1], got))
                 middle[r - 1] = lax.ppermute(last, "dp", middle_pairs)
             if r >= 4:
-                sums[r - 4] = lax.optimization_barrier(jnp.where(end, got, s[r - 4]))
+                sums[r - 4] = (got, s[r - 4])
                 if r - 1 >= count:
-                    last = sums[r - 4]
+                    last = got
             last = idle(r - 1, last, sums)
         if r - 2 in middle:
             got = after(middle.pop(r - 2), last)
@@ -382,7 +391,7 @@
         encs = encs + [swap(e, "mp", bit) for e in encs]
 
     everything = tuple(range(per))
-    pieces_of = lambda k: (everything[1:], everything)[k] if k < 2 else ()
+    pieces_of = lambda k: everything[1:] if k == 0 else (everything if k in (1, taps - 1) else ())
 
     def gradient(group, hold):
         pieces = [pieces_of(k) for k in group]
@@ -434,7 +443,7 @@
 
     work((0,), [])
     launch(0, [])
-    work(tuple(range(1, taps)), [keep[-1]])
+    work(tuple(range(1, min(3, taps))), [keep[-1]])
     launch(1, [])
 
     def share(c, last):
@@ -444,6 +453,9 @@
         return added(keep[tap][rows], value if last is None else after(value, last))
 
     def sent(r, last, sums):
+        if r == per - 1:
+            work(tuple(range(3, taps)), [last] + encs[1:])
+            last = keep[-1]
         if r % per == per - 1 and r // per + 2 < taps and r < chunks:
             launch(r // per + 2, [last])
         if r == chunks + 2:
@@ -457,7 +469,7 @@
         if c == chunks:
             early = len(sums) // per
             parts = [sums[i] for i in range(early * per)]
-            parts[0] = after(parts[0], last)
+            parts[0] = (after(parts[0][0], last), parts[0][1])
             last = done["early"] = written(parts, early, 0, None, (taps, per * depth, width))
             done["at"] = early
         return last

time: 147 us -> 134 us (0.912)
  waiting for transfers between devices: 27.8 us -> 10.7 us
  other arithmetic: 5.62 us -> 8.77 us
  Pallas kernels: 32.6 us -> 30.3 us
  starting transfers between devices: 69.4 us -> 71.6 us
    ppermute x13, waiting for transfers between devices: 13.5 us -> 4.89 us  [chain_sums(): outer[r] = lax.ppermute(value, 'dp', outer_pairs)]
    ppermute x17 -> x18, waiting for transfers between devices: 14.3 us -> 5.77 us  [swap(): return lax.ppermute(value, axis, [(i, i ^ bit) for i in range(peers)])]
    pallas_call x5 -> x6, Pallas kernels: 29.3 us -> 25.7 us  [call(): pl.pallas_call(kernel, out_shape=out, in_specs=[pl.BlockSpec(memory_space...]
    convert_element_type x23, other arithmetic: 4.44 us -> 7.91 us  [added(): return (a.astype(F32) + b.astype(F32)).astype(BF16)]
    ppermute x13, starting transfers between devices: 44.2 us -> 46 us  [chain_sums(): outer[r] = lax.ppermute(value, 'dp', outer_pairs)]
    ppermute x17 -> x18, starting transfers between devices: 18.1 us -> 17.5 us  [swap(): return lax.ppermute(value, axis, [(i, i ^ bit) for i in range(peers)])]
  transfers between devices with their start and end apart: 40 -> 41, of which waited for: 13 -> 10; matrix products, arithmetic and copies ran while one was open for 4% -> 7% of each run, Pallas kernels for 17% -> 17%
where the time goes in v9:
time: 134 us; the launch traced here: 133 us
  starting transfers between devices  71.6 us (53%)
  Pallas kernels  30.3 us (23%)
  local copies, waits for them, and re-layouts  10.8 us (8%)
  waiting for transfers between devices  10.7 us (8%)
  other arithmetic  8.77 us (7%)
    ppermute x13, starting transfers between devices, chain_sums(): outer[r] = lax.ppermute(value, 'dp', outer_pairs)  46 us
    pallas_call x6, Pallas kernels, call(): pl.pallas_call(kernel, out_shape=out, in_specs=[pl.BlockSpec(memory_space...  25.7 us
    ppermute x18, starting transfers between devices, swap(): return lax.ppermute(value, axis, [(i, i ^ bit) for i in range(peers)])  17.5 us
    unnamed x28, local copies, waits for them, and re-layouts  9.9 us
    ppermute x10, starting transfers between devices, chain_sums(): middle[r - 1] = lax.ppermute(last, 'dp', middle_pairs)  8.14 us
    convert_element_type x23, other arithmetic, added(): return (a.astype(F32) + b.astype(F32)).astype(BF16)  7.91 us
    ppermute x18, waiting for transfers between devices, swap(): return lax.ppermute(value, axis, [(i, i ^ bit) for i in range(peers)])  5.77 us
    ppermute x13, waiting for transfers between devices, chain_sums(): outer[r] = lax.ppermute(value, 'dp', outer_pairs)  4.89 us
  transfers between devices with their start and end apart: 41, of which 10 were waited for; matrix products, arithmetic and copies ran while one was open for 7% of the time, Pallas kernels for 17%

profile of v9, /device:TPU:0, one launch (start us, length us, event | category | flops | bytes accessed | tf_op | source)
XLA Modules:
  0.0 133.2 jit_solution(15219185984193915592)
XLA Ops:
  1.1 2.6 %collective-permute-start = (bf16[320,1024]{1,0:T(8,128)(2,1)}, bf16[320,1024]{1,0:T(8,128)(2,1)S(1)}, u32[]{:S(2)}, u32[]{:S(2)}) collective-permute-start(bf16[320,1024]{1,0:T(8,128)(2,1)} %bitcast.10), channel_id=1, source_target_pairs={{0,8},{4,12},{8,0},{12,4},{1,9},{5,13},{9,1},{13,5},{2,10},{6,14},... | collective-permute-start | bytes 1966088 | tf_op jit(solution)/shard_map/ppermute | solution.py:26
  3.7 1.1 copy-done
  5.0 1.6 %collective-permute-start.2 = (f32[8,384]{1,0:T(8,128)S(1)}, f32[8,384]{1,0:T(8,128)S(1)}, u32[]{:S(2)}, u32[]{:S(2)}) collective-permute-start(f32[8,384]{1,0:T(8,128)S(1)} %shard_map.68), channel_id=1, source_target_pairs={{0,16},{16,0},{1,17},{17,1},{2,18},{18,2},{3,19},{19,3},{4,20},{20... | collective-permute-start | bytes 36872 | tf_op jit(solution)/shard_map/ppermute | solution.py:26
  7.3 1.4 %collective-permute-done.2 = f32[8,384]{1,0:T(8,128)S(1)} collective-permute-done((f32[8,384]{1,0:T(8,128)S(1)}, f32[8,384]{1,0:T(8,128)S(1)}, u32[]{:S(2)}, u32[]{:S(2)}) %collective-permute-start.2) | collective-permute-done | bytes 12320 | tf_op jit(solution)/shard_map/ppermute | solution.py:26
  8.9 0.9 collective-permute-start.4
  9.8 0.9 collective-permute-start.3
  11.6 1.1 copy-done.1
  12.7 2.4 %copy-done.3 = bf16[5,1280,384]{2,1,0:T(8,128)(2,1)S(1)} copy-done((bf16[5,1280,384]{2,1,0:T(8,128)(2,1)S(1)}, bf16[5,1280,384]{2,1,0:T(8,128)(2,1)}, u32[]{:S(2)}) %copy-start.3) | copy-done | bytes 4915224
  15.1 4.3 %shard_map.69 = (f32[512,384]{1,0:T(8,128)S(1)}, f32[512,384]{1,0:T(8,128)S(1)}) custom-call(s32[2]{0:T(128)S(1)} %pad_add_fusion.idx_ref, bf16[320,1024]{1,0:T(8,128)(2,1)S(1)} %bitcast.13, bf16[320,1024]{1,0:T(8,128)(2,1)S(1)} %collective-permute-done.1.refs_1_.refs_2_, f32[8,384]{1,0:T(8,128)S(1)} %maximum_maximum_fusion.refs_2_.refs_4_, ...), custom_call_target="tpu_custom_call" | custom-call | tf_op jit(solution)/shard_map/pallas_call | solution.py:211
  19.8 0.8 copy-done.5
  20.6 1.3 collective-permute-done.6.refs_3_
  21.9 1.3 copy-done.6
  23.2 6.6 %shard_map.70 = (bf16[512,384]{1,0:T(8,128)(2,1)}, f32[1040,384]{1,0:T(8,128)S(1)}, bf16[320,384]{1,0:T(8,128)(2,1)S(1)}) custom-call(s32[2]{0:T(128)S(1)} %pad_add_fusion.idx_ref, bf16[320,1024]{1,0:T(8,128)(2,1)S(1)} %bitcast.14, bf16[320,1024]{1,0:T(8,128)(2,1)S(1)} %copy-done.6, bf16[320,1024]{1,0:T(8,128)(2,1)S(1)} %collective-permute-done.1.refs_1_.refs_2_, ...), custom_call_target="tpu_custom_call" | custom-call | tf_op jit(solution)/shard_map/pallas_call | solution.py:211
  29.9 1.7 %collective-permute-start.8 = (bf16[320,384]{1,0:T(8,128)(2,1)S(1)}, bf16[320,384]{1,0:T(8,128)(2,1)S(1)}, u32[]{:S(2)}, u32[]{:S(2)}) collective-permute-start(bf16[320,384]{1,0:T(8,128)(2,1)S(1)} %get-tuple-element.68), channel_id=1, source_target_pairs={{0,16},{16,0},{1,17},{17,1},{2,18},{18,2},{3,19},{19,3},{4,20},{20... | collective-permute-start | bytes 737288 | tf_op jit(solution)/shard_map/ppermute | solution.py:26
  31.6 3.4 %shard_map.71 = (bf16[640,384]{1,0:T(8,128)(2,1)S(1)}, bf16[320,384]{1,0:T(8,128)(2,1)}) custom-call(s32[2]{0:T(128)S(1)} %pad_add_fusion.idx_ref, bf16[320,1024]{1,0:T(8,128)(2,1)S(1)} %bitcast.15, bf16[320,1024]{1,0:T(8,128)(2,1)S(1)} %copy-done.6, bf16[320,1024]{1,0:T(8,128)(2,1)S(1)} %collective-permute-done.1.refs_1_.refs_2_, ...), custom_call_target="tpu_custom_call" | custom-call | tf_op jit(solution)/shard_map/pallas_call | solution.py:211
  35.3 1.7 %collective-permute-start.9 = (bf16[512,384]{1,0:T(8,128)(2,1)}, bf16[512,384]{1,0:T(8,128)(2,1)}, u32[]{:S(2)}, u32[]{:S(2)}) collective-permute-start(bf16[512,384]{1,0:T(8,128)(2,1)} %get-tuple-element.117.refs_0_), channel_id=1, source_target_pairs={{0,8},{4,12},{8,0},{12,4},{1,9},{5,13},{9,1},{13,5},{2,10},{6,14},... | collective-permute-start | bytes 1179656 | tf_op jit(solution)/shard_map/ppermute | solution.py:26
  37.0 1.0 collective-permute-done.8
  38.8 2.0 %collective-permute-start.12 = (bf16[320,384]{1,0:T(8,128)(2,1)}, bf16[320,384]{1,0:T(8,128)(2,1)}, u32[]{:S(2)}, u32[]{:S(2)}) collective-permute-start(bf16[320,384]{1,0:T(8,128)(2,1)} %add_convert_fusion.29), channel_id=1, source_target_pairs={{0,1},{1,0},{2,3},{3,2},{4,5},{5,4},{6,7},{7,6},{8,9},{9,8},{10,11... | collective-permute-start | bytes 737288 | tf_op jit(solution)/shard_map/ppermute | solution.py:314
  40.8 1.1 copy-done.7
  41.9 1.1 copy-done.9
  43.0 3.6 %shard_map.73 = (bf16[640,384]{1,0:T(8,128)(2,1)S(1)}, bf16[320,384]{1,0:T(8,128)(2,1)S(1)}, bf16[320,384]{1,0:T(8,128)(2,1)S(1)}, bf16[640,384]{1,0:T(8,128)(2,1)S(1)}, bf16[640,384]{1,0:T(8,128)(2,1)S(1)}) custom-call(s32[2]{0:T(128)S(1)} %pad_add_fusion.idx_ref, bf16[320,1024]{1,0:T(8,128)(2,1)S(1)} %bitcast.16, bf16[320,1024]{1,0:T(8,128)(2,1)S(1)} %copy-done.7, ...), custom_call_target="tpu_custom_call" | custom-call | tf_op jit(solution)/shard_map/pallas_call | solution.py:211
  46.6 1.9 %collective-permute-start.11 = (bf16[320,384]{1,0:T(8,128)(2,1)S(1)}, bf16[320,384]{1,0:T(8,128)(2,1)S(1)}, u32[]{:S(2)}, u32[]{:S(2)}) collective-permute-start(bf16[320,384]{1,0:T(8,128)(2,1)S(1)} %get-tuple-element.79), channel_id=1, source_target_pairs={{0,16},{16,0},{1,17},{17,1},{2,18},{18,2},{3,19},{19,3},{4,20},{20... | collective-permute-start | bytes 737288 | tf_op jit(solution)/shard_map/ppermute | solution.py:26
  48.7 1.0 add_convert_fusion.28
  50.2 3.6 %shard_map.72 = (bf16[640,384]{1,0:T(8,128)(2,1)S(1)}, bf16[640,384]{1,0:T(8,128)(2,1)S(1)}, bf16[640,384]{1,0:T(8,128)(2,1)S(1)}, bf16[320,384]{1,0:T(8,128)(2,1)S(1)}, bf16[320,384]{1,0:T(8,128)(2,1)S(1)}) custom-call(s32[2]{0:T(128)S(1)} %pad_add_fusion.idx_ref, bf16[320,1024]{1,0:T(8,128)(2,1)S(1)} %bitcast.17, bf16[320,1024]{1,0:T(8,128)(2,1)S(1)} %copy-done.7, ...), custom_call_target="tpu_custom_call" | custom-call | tf_op jit(solution)/shard_map/pallas_call | solution.py:211
  53.9 2.0 %collective-permute-start.10 = (bf16[640,384]{1,0:T(8,128)(2,1)S(1)}, bf16[640,384]{1,0:T(8,128)(2,1)S(1)}, u32[]{:S(2)}, u32[]{:S(2)}) collective-permute-start(bf16[640,384]{1,0:T(8,128)(2,1)S(1)} %get-tuple-element.77), channel_id=1, source_target_pairs={{0,16},{16,0},{1,17},{17,1},{2,18},{18,2},{3,19},{19,3},{4,20},{20... | collective-permute-start | bytes 1474568 | tf_op jit(solution)/shard_map/ppermute | solution.py:26
  55.9 1.1 add_convert_fusion.27
  57.8 4.4 %collective-permute-start.13 = (bf16[320,384]{1,0:T(8,128)(2,1)S(1)}, bf16[320,384]{1,0:T(8,128)(2,1)S(1)}, u32[]{:S(2)}, u32[]{:S(2)}) collective-permute-start(bf16[320,384]{1,0:T(8,128)(2,1)S(1)} %add_convert_fusion.26), channel_id=1, source_target_pairs={{0,1},{1,0},{2,3},{3,2},{4,5},{5,4},{6,7},{7,6},{8,9},{9,8},{10,11... | collective-permute-start | bytes 737288 | tf_op jit(solution)/shard_map/ppermute | solution.py:314
  63.2 6.0 %collective-permute-start.18 = (bf16[320,384]{1,0:T(8,128)(2,1)S(1)}, bf16[320,384]{1,0:T(8,128)(2,1)S(1)}, u32[]{:S(2)}, u32[]{:S(2)}) collective-permute-start(bf16[320,384]{1,0:T(8,128)(2,1)S(1)} %broadcast_select_fusion.6), channel_id=1, source_target_pairs={{0,1},{1,0},{2,3},{3,2},{4,5},{5,4},{6,7},{7,6},{8,9},{9,8},{10,11... | collective-permute-start | bytes 737288 | tf_op jit(solution)/shard_map/ppermute | solution.py:314
  71.6 3.4 %collective-permute-start.23 = (bf16[320,384]{1,0:T(8,128)(2,1)S(1)}, bf16[320,384]{1,0:T(8,128)(2,1)S(1)}, u32[]{:S(2)}, u32[]{:S(2)}) collective-permute-start(bf16[320,384]{1,0:T(8,128)(2,1)S(1)} %broadcast_select_fusion.5), channel_id=1, source_target_pairs={{0,1},{1,0},{2,3},{3,2},{4,5},{5,4},{6,7},{7,6},{8,9},{9,8},{10,11... | collective-permute-start | bytes 737288 | tf_op jit(solution)/shard_map/ppermute | solution.py:314
  74.9 1.0 collective-permute-done.18.refs_0_
  76.9 4.3 %collective-permute-start.26 = (bf16[320,384]{1,0:T(8,128)(2,1)S(1)}, bf16[320,384]{1,0:T(8,128)(2,1)S(1)}, u32[]{:S(2)}, u32[]{:S(2)}) collective-permute-start(bf16[320,384]{1,0:T(8,128)(2,1)S(1)} %broadcast_select_fusion.4), channel_id=1, source_target_pairs={{0,1},{1,0},{2,3},{3,2},{4,5},{5,4},{6,7},{7,6},{8,9},{9,8},{10,11... | collective-permute-start | bytes 737288 | tf_op jit(solution)/shard_map/ppermute | solution.py:314
  81.6 1.7 %collective-permute-start.29 = (bf16[320,384]{1,0:T(8,128)(2,1)S(1)}, bf16[320,384]{1,0:T(8,128)(2,1)S(1)}, u32[]{:S(2)}, u32[]{:S(2)}) collective-permute-start(bf16[320,384]{1,0:T(8,128)(2,1)S(1)} %get-tuple-element.104), channel_id=1, source_target_pairs={{0,16},{16,0},{1,17},{17,1},{2,18},{18,2},{3,19},{19,3},{4,20},{20... | collective-permute-start | bytes 737288 | tf_op jit(solution)/shard_map/ppermute | solution.py:26
  84.3 4.9 %collective-permute-start.24 = (bf16[320,384]{1,0:T(8,128)(2,1)S(1)}, bf16[320,384]{1,0:T(8,128)(2,1)S(1)}, u32[]{:S(2)}, u32[]{:S(2)}) collective-permute-start(bf16[320,384]{1,0:T(8,128)(2,1)S(1)} %broadcast_select_fusion.3), channel_id=1, source_target_pairs={{0,1},{1,0},{2,3},{3,2},{4,5},{5,4},{6,7},{7,6},{8,9},{9,8},{10,11... | collective-permute-start | bytes 737288 | tf_op jit(solution)/shard_map/ppermute | solution.py:314
  90.2 5.3 %collective-permute-start.28 = (bf16[320,384]{1,0:T(8,128)(2,1)S(1)}, bf16[320,384]{1,0:T(8,128)(2,1)S(1)}, u32[]{:S(2)}, u32[]{:S(2)}) collective-permute-start(bf16[320,384]{1,0:T(8,128)(2,1)S(1)} %broadcast_select_fusion.2), channel_id=1, source_target_pairs={{0,1},{1,0},{2,3},{3,2},{4,5},{5,4},{6,7},{7,6},{8,9},{9,8},{10,11... | collective-permute-start | bytes 737288 | tf_op jit(solution)/shard_map/ppermute | solution.py:314
  97.0 3.7 %collective-permute-start.33 = (bf16[320,384]{1,0:T(8,128)(2,1)S(1)}, bf16[320,384]{1,0:T(8,128)(2,1)S(1)}, u32[]{:S(2)}, u32[]{:S(2)}) collective-permute-start(bf16[320,384]{1,0:T(8,128)(2,1)S(1)} %broadcast_select_fusion.1), channel_id=1, source_target_pairs={{0,1},{1,0},{2,3},{3,2},{4,5},{5,4},{6,7},{7,6},{8,9},{9,8},{10,11... | collective-permute-start | bytes 737288 | tf_op jit(solution)/shard_map/ppermute | solution.py:314
  101.7 4.8 %collective-permute-start.31 = (bf16[320,384]{1,0:T(8,128)(2,1)S(1)}, bf16[320,384]{1,0:T(8,128)(2,1)S(1)}, u32[]{:S(2)}, u32[]{:S(2)}) collective-permute-start(bf16[320,384]{1,0:T(8,128)(2,1)S(1)} %broadcast_select_fusion), channel_id=1, source_target_pairs={{0,1},{1,0},{2,3},{3,2},{4,5},{5,4},{6,7},{7,6},{8,9},{9,8},{10,11... | collective-permute-start | bytes 737288 | tf_op jit(solution)/shard_map/ppermute | solution.py:314
  106.4 1.0 collective-permute-done.33.refs_10_
  108.3 1.4 %collective-permute-start.36 = (bf16[320,384]{1,0:T(8,128)(2,1)}, bf16[320,384]{1,0:T(8,128)(2,1)}, u32[]{:S(2)}, u32[]{:S(2)}) collective-permute-start(bf16[320,384]{1,0:T(8,128)(2,1)} %add_convert_fusion.4), channel_id=1, source_target_pairs={{1,2},{2,1},{5,6},{6,5},{9,10},{10,9},{13,14},{14,13},{17,18},{18,... | collective-permute-start | bytes 737288 | tf_op jit(solution)/shard_map/ppermute | solution.py:320
  109.7 2.7 %collective-permute-start.35 = (bf16[320,384]{1,0:T(8,128)(2,1)S(1)}, bf16[320,384]{1,0:T(8,128)(2,1)}, u32[]{:S(2)}, u32[]{:S(2)}) collective-permute-start(bf16[320,384]{1,0:T(8,128)(2,1)S(1)} %add_convert_fusion.3.refs_15_), channel_id=1, source_target_pairs={{0,1},{1,0},{2,3},{3,2},{4,5},{5,4},{6,7},{7,6},{8,9},{9,8},{10,11... | collective-permute-start | bytes 737288 | tf_op jit(solution)/shard_map/ppermute | solution.py:314
  113.2 1.3 %collective-permute-start.34 = (bf16[320,384]{1,0:T(8,128)(2,1)}, bf16[320,384]{1,0:T(8,128)(2,1)}, u32[]{:S(2)}, u32[]{:S(2)}) collective-permute-start(bf16[320,384]{1,0:T(8,128)(2,1)} %add_convert_fusion.2), channel_id=1, source_target_pairs={{1,2},{2,1},{5,6},{6,5},{9,10},{10,9},{13,14},{14,13},{17,18},{18,... | collective-permute-start | bytes 737288 | tf_op jit(solution)/shard_map/ppermute | solution.py:320
  115.0 1.1 add_convert_fusion.1.refs_1_
  116.2 3.7 %collective-permute-start.39 = (bf16[320,384]{1,0:T(8,128)(2,1)S(1)}, bf16[320,384]{1,0:T(8,128)(2,1)S(1)}, u32[]{:S(2)}, u32[]{:S(2)}) collective-permute-start(bf16[320,384]{1,0:T(8,128)(2,1)S(1)} %add_convert_fusion.1.refs_1_), channel_id=1, source_target_pairs={{0,1},{1,0},{2,3},{3,2},{4,5},{5,4},{6,7},{7,6},{8,9},{9,8},{10,11... | collective-permute-start | bytes 737288 | tf_op jit(solution)/shard_map/ppermute | solution.py:314
  119.9 0.9 copy-done.12
  120.9 3.4 %shard_map.74.b = f32[5,640,384]{2,1,0:T(8,128)} custom-call(s32[1]{0:T(128)} %bitcast.6.end_ref.end, bf16[320,384]{1,0:T(8,128)(2,1)S(1)} %collective-permute-done.18.refs_0_, bf16[320,384]{1,0:T(8,128)(2,1)S(1)} %add_convert_fusion.24.refs_1_, bf16[320,384]{1,0:T(8,128)(2,1)S(1)} %collective-permute-done.23.refs_2_, ...), custom_call_target="tpu_custom_call" | custom-call | tf_op jit(solution)/shard_map/pallas_call | solution.py:246
  124.3 1.1 add_convert_fusion.refs_3_
  125.6 4.1 %shard_map.75 = bf16[512,640]{1,0:T(8,128)(2,1)} custom-call(s32[2]{0:T(128)S(1)} %pad_add_fusion.idx_ref, bf16[512,384]{1,0:T(8,128)(2,1)} %get-tuple-element.117.refs_0_, bf16[512,384]{1,0:T(8,128)(2,1)} %collective-permute-done.9.refs_1_, bf16[512,384]{1,0:T(8,128)(2,1)S(1)} %collective-permute-done.37.refs_2_, ...), custom_call_target="tpu_custom_call" | custom-call | tf_op jit(solution)/shard_map/pallas_call | solution.py:211
  129.8 2.3 %collective-permute-done.40.refs_2_ = bf16[320,384]{1,0:T(8,128)(2,1)S(1)} collective-permute-done((bf16[320,384]{1,0:T(8,128)(2,1)S(1)}, bf16[320,384]{1,0:T(8,128)(2,1)S(1)}, u32[]{:S(2)}, u32[]{:S(2)}) %collective-permute-start.40) | collective-permute-done | bytes 245792 | tf_op jit(solution)/shard_map/ppermute | solution.py:314
  132.1 1.0 shard_map.76
  (109 shorter events, 16.5 us)
Async XLA Ops:
  0.6 10.9 %collective-permute-start.1 = (bf16[320,1024]{1,0:T(8,128)(2,1)}, bf16[320,1024]{1,0:T(8,128)(2,1)S(1)}, u32[]{:S(2)}, u32[]{:S(2)}) collective-permute-start(bf16[320,1024]{1,0:T(8,128)(2,1)} %bitcast.9), channel_id=1, source_target_pairs={{0,4},{4,0},{8,12},{12,8},{1,5},{5,1},{9,13},{13,9},{2,6},{6,2},{1... | collective-permute-start | bytes 1966088 | tf_op jit(solution)/shard_map/ppermute | solution.py:26
  1.1 18.7 %collective-permute-start = (bf16[320,1024]{1,0:T(8,128)(2,1)}, bf16[320,1024]{1,0:T(8,128)(2,1)S(1)}, u32[]{:S(2)}, u32[]{:S(2)}) collective-permute-start(bf16[320,1024]{1,0:T(8,128)(2,1)} %bitcast.10), channel_id=1, source_target_pairs={{0,8},{4,12},{8,0},{12,4},{1,9},{5,13},{9,1},{13,5},{2,10},{6,14},... | collective-permute-start | bytes 1966088 | tf_op jit(solution)/shard_map/ppermute | solution.py:26
  4.9 17.0 %copy-start.2 = (bf16[1,1024,320]{1,2,0:T(8,128)(2,1)S(1)}, bf16[1,1024,320]{1,2,0:T(8,128)(2,1)}, u32[]{:S(2)}) copy-start(bf16[1,1024,320]{1,2,0:T(8,128)(2,1)} %param.5) | copy-start | bytes 1966084
  4.9 17.0 %copy-start.13 = (bf16[1,512,384]{2,1,0:T(8,128)(2,1)S(1)}, bf16[1,512,384]{2,1,0:T(8,128)(2,1)}, u32[]{:S(2)}) copy-start(bf16[1,512,384]{2,1,0:T(8,128)(2,1)} %param.9) | copy-start | bytes 1179652
  5.0 3.8 %collective-permute-start.2 = (f32[8,384]{1,0:T(8,128)S(1)}, f32[8,384]{1,0:T(8,128)S(1)}, u32[]{:S(2)}, u32[]{:S(2)}) collective-permute-start(f32[8,384]{1,0:T(8,128)S(1)} %shard_map.68), channel_id=1, source_target_pairs={{0,16},{16,0},{1,17},{17,1},{2,18},{18,2},{3,19},{19,3},{4,20},{20... | collective-permute-start | bytes 36872 | tf_op jit(solution)/shard_map/ppermute | solution.py:26
  8.9 10.5 %collective-permute-start.5 = (f32[8,384]{1,0:T(8,128)S(1)}, f32[8,384]{1,0:T(8,128)S(1)}, u32[]{:S(2)}, u32[]{:S(2)}) collective-permute-start(f32[8,384]{1,0:T(8,128)S(1)} %maximum_maximum_fusion.refs_2_.refs_4_), channel_id=1, source_target_pairs={{0,12},{4,8},{8,4},{12,0},{1,13},{5,9},{9,5},{13,1},{2,14},{6,10},... | collective-permute-start | bytes 36872 | tf_op jit(solution)/shard_map/ppermute | solution.py:26
  8.9 10.9 %collective-permute-start.4 = (f32[8,384]{1,0:T(8,128)S(1)}, f32[8,384]{1,0:T(8,128)S(1)}, u32[]{:S(2)}, u32[]{:S(2)}) collective-permute-start(f32[8,384]{1,0:T(8,128)S(1)} %maximum_maximum_fusion.refs_2_.refs_4_), channel_id=1, source_target_pairs={{0,8},{4,12},{8,0},{12,4},{1,9},{5,13},{9,1},{13,5},{2,10},{6,14},... | collective-permute-start | bytes 36872 | tf_op jit(solution)/shard_map/ppermute | solution.py:26
  9.8 1.8 %collective-permute-start.3 = (f32[8,384]{1,0:T(8,128)S(1)}, f32[8,384]{1,0:T(8,128)S(1)}, u32[]{:S(2)}, u32[]{:S(2)}) collective-permute-start(f32[8,384]{1,0:T(8,128)S(1)} %maximum_maximum_fusion.refs_2_.refs_4_), channel_id=1, source_target_pairs={{0,4},{4,0},{8,12},{12,8},{1,5},{5,1},{9,13},{13,9},{2,6},{6,2},{1... | collective-permute-start | bytes 36872 | tf_op jit(solution)/shard_map/ppermute | solution.py:26
  12.7 2.4 %copy-start.3 = (bf16[5,1280,384]{2,1,0:T(8,128)(2,1)S(1)}, bf16[5,1280,384]{2,1,0:T(8,128)(2,1)}, u32[]{:S(2)}) copy-start(bf16[5,1280,384]{2,1,0:T(8,128)(2,1)} %refs_8_.2) | copy-start | bytes 14745604
  15.1 6.9 %copy-start.4 = (bf16[5,1280,384]{2,1,0:T(8,128)(2,1)S(1)}, bf16[5,1280,384]{2,1,0:T(8,128)(2,1)}, u32[]{:S(2)}) copy-start(bf16[5,1280,384]{2,1,0:T(8,128)(2,1)} %refs_8_.2) | copy-start | bytes 14745604
  19.8 2.1 %collective-permute-start.6 = (bf16[320,1024]{1,0:T(8,128)(2,1)S(1)}, bf16[320,1024]{1,0:T(8,128)(2,1)S(1)}, u32[]{:S(2)}, u32[]{:S(2)}) collective-permute-start(bf16[320,1024]{1,0:T(8,128)(2,1)S(1)} %collective-permute-done.refs_1_), channel_id=1, source_target_pairs={{0,4},{4,0},{8,12},{12,8},{1,5},{5,1},{9,13},{13,9},{2,6},{6,2},{1... | collective-permute-start | bytes 1966088 | tf_op jit(solution)/shard_map/ppermute | solution.py:26
  21.9 13.1 %copy-start.8 = (bf16[320,1024]{1,0:T(8,128)(2,1)}, bf16[320,1024]{1,0:T(8,128)(2,1)S(1)}, u32[]{:S(2)}) copy-start(bf16[320,1024]{1,0:T(8,128)(2,1)S(1)} %collective-permute-done.6.refs_3_) | copy-start | bytes 1966084
  21.9 1.3 copy-start.6
  29.9 8.2 %collective-permute-start.8 = (bf16[320,384]{1,0:T(8,128)(2,1)S(1)}, bf16[320,384]{1,0:T(8,128)(2,1)S(1)}, u32[]{:S(2)}, u32[]{:S(2)}) collective-permute-start(bf16[320,384]{1,0:T(8,128)(2,1)S(1)} %get-tuple-element.68), channel_id=1, source_target_pairs={{0,16},{16,0},{1,17},{17,1},{2,18},{18,2},{3,19},{19,3},{4,20},{20... | collective-permute-start | bytes 737288 | tf_op jit(solution)/shard_map/ppermute | solution.py:26
  35.0 13.8 %collective-permute-start.7 = (bf16[320,384]{1,0:T(8,128)(2,1)}, bf16[320,384]{1,0:T(8,128)(2,1)}, u32[]{:S(2)}, u32[]{:S(2)}) collective-permute-start(bf16[320,384]{1,0:T(8,128)(2,1)} %get-tuple-element.67), channel_id=1, source_target_pairs={{0,16},{16,0},{1,17},{17,1},{2,18},{18,2},{3,19},{19,3},{4,20},{20... | collective-permute-start | bytes 737288 | tf_op jit(solution)/shard_map/ppermute | solution.py:26
  35.3 14.9 %collective-permute-start.9 = (bf16[512,384]{1,0:T(8,128)(2,1)}, bf16[512,384]{1,0:T(8,128)(2,1)}, u32[]{:S(2)}, u32[]{:S(2)}) collective-permute-start(bf16[512,384]{1,0:T(8,128)(2,1)} %get-tuple-element.117.refs_0_), channel_id=1, source_target_pairs={{0,8},{4,12},{8,0},{12,4},{1,9},{5,13},{9,1},{13,5},{2,10},{6,14},... | collective-permute-start | bytes 1179656 | tf_op jit(solution)/shard_map/ppermute | solution.py:26
  38.8 17.1 %collective-permute-start.12 = (bf16[320,384]{1,0:T(8,128)(2,1)}, bf16[320,384]{1,0:T(8,128)(2,1)}, u32[]{:S(2)}, u32[]{:S(2)}) collective-permute-start(bf16[320,384]{1,0:T(8,128)(2,1)} %add_convert_fusion.29), channel_id=1, source_target_pairs={{0,1},{1,0},{2,3},{3,2},{4,5},{5,4},{6,7},{7,6},{8,9},{9,8},{10,11... | collective-permute-start | bytes 737288 | tf_op jit(solution)/shard_map/ppermute | solution.py:314
  46.6 11.0 %collective-permute-start.11 = (bf16[320,384]{1,0:T(8,128)(2,1)S(1)}, bf16[320,384]{1,0:T(8,128)(2,1)S(1)}, u32[]{:S(2)}, u32[]{:S(2)}) collective-permute-start(bf16[320,384]{1,0:T(8,128)(2,1)S(1)} %get-tuple-element.79), channel_id=1, source_target_pairs={{0,16},{16,0},{1,17},{17,1},{2,18},{18,2},{3,19},{19,3},{4,20},{20... | collective-permute-start | bytes 737288 | tf_op jit(solution)/shard_map/ppermute | solution.py:26
  48.6 14.5 %collective-permute-start.14 = (bf16[320,384]{1,0:T(8,128)(2,1)S(1)}, bf16[320,384]{1,0:T(8,128)(2,1)S(1)}, u32[]{:S(2)}, u32[]{:S(2)}) collective-permute-start(bf16[320,384]{1,0:T(8,128)(2,1)S(1)} %get-tuple-element.82), channel_id=1, source_target_pairs={{0,16},{16,0},{1,17},{17,1},{2,18},{18,2},{3,19},{19,3},{4,20},{20... | collective-permute-start | bytes 737288 | tf_op jit(solution)/shard_map/ppermute | solution.py:26
  49.8 12.5 %collective-permute-start.16 = (bf16[320,384]{1,0:T(8,128)(2,1)S(1)}, bf16[320,384]{1,0:T(8,128)(2,1)S(1)}, u32[]{:S(2)}, u32[]{:S(2)}) collective-permute-start(bf16[320,384]{1,0:T(8,128)(2,1)S(1)} %add_convert_fusion.28), channel_id=1, source_target_pairs={{0,1},{1,0},{2,3},{3,2},{4,5},{5,4},{6,7},{7,6},{8,9},{9,8},{10,11... | collective-permute-start | bytes 737288 | tf_op jit(solution)/shard_map/ppermute | solution.py:314
  53.9 17.5 %collective-permute-start.10 = (bf16[640,384]{1,0:T(8,128)(2,1)S(1)}, bf16[640,384]{1,0:T(8,128)(2,1)S(1)}, u32[]{:S(2)}, u32[]{:S(2)}) collective-permute-start(bf16[640,384]{1,0:T(8,128)(2,1)S(1)} %get-tuple-element.77), channel_id=1, source_target_pairs={{0,16},{16,0},{1,17},{17,1},{2,18},{18,2},{3,19},{19,3},{4,20},{20... | collective-permute-start | bytes 1474568 | tf_op jit(solution)/shard_map/ppermute | solution.py:26
  57.0 6.0 %collective-permute-start.15 = (bf16[320,384]{1,0:T(8,128)(2,1)S(1)}, bf16[320,384]{1,0:T(8,128)(2,1)S(1)}, u32[]{:S(2)}, u32[]{:S(2)}) collective-permute-start(bf16[320,384]{1,0:T(8,128)(2,1)S(1)} %add_convert_fusion.27), channel_id=1, source_target_pairs={{1,2},{2,1},{5,6},{6,5},{9,10},{10,9},{13,14},{14,13},{17,18},{18,... | collective-permute-start | bytes 737288 | tf_op jit(solution)/shard_map/ppermute | solution.py:320
  57.8 11.4 %collective-permute-start.13 = (bf16[320,384]{1,0:T(8,128)(2,1)S(1)}, bf16[320,384]{1,0:T(8,128)(2,1)S(1)}, u32[]{:S(2)}, u32[]{:S(2)}) collective-permute-start(bf16[320,384]{1,0:T(8,128)(2,1)S(1)} %add_convert_fusion.26), channel_id=1, source_target_pairs={{0,1},{1,0},{2,3},{3,2},{4,5},{5,4},{6,7},{7,6},{8,9},{9,8},{10,11... | collective-permute-start | bytes 737288 | tf_op jit(solution)/shard_map/ppermute | solution.py:314
  62.3 7.6 %collective-permute-start.19 = (bf16[320,384]{1,0:T(8,128)(2,1)S(1)}, bf16[320,384]{1,0:T(8,128)(2,1)S(1)}, u32[]{:S(2)}, u32[]{:S(2)}) collective-permute-start(bf16[320,384]{1,0:T(8,128)(2,1)S(1)} %add_convert_fusion.25), channel_id=1, source_target_pairs={{1,2},{2,1},{5,6},{6,5},{9,10},{10,9},{13,14},{14,13},{17,18},{18,... | collective-permute-start | bytes 737288 | tf_op jit(solution)/shard_map/ppermute | solution.py:320
  63.2 12.8 %collective-permute-start.18 = (bf16[320,384]{1,0:T(8,128)(2,1)S(1)}, bf16[320,384]{1,0:T(8,128)(2,1)S(1)}, u32[]{:S(2)}, u32[]{:S(2)}) collective-permute-start(bf16[320,384]{1,0:T(8,128)(2,1)S(1)} %broadcast_select_fusion.6), channel_id=1, source_target_pairs={{0,1},{1,0},{2,3},{3,2},{4,5},{5,4},{6,7},{7,6},{8,9},{9,8},{10,11... | collective-permute-start | bytes 737288 | tf_op jit(solution)/shard_map/ppermute | solution.py:314
  69.2 7.5 %collective-permute-start.17 = (bf16[320,384]{1,0:T(8,128)(2,1)S(1)}, bf16[320,384]{1,0:T(8,128)(2,1)S(1)}, u32[]{:S(2)}, u32[]{:S(2)}) collective-permute-start(bf16[320,384]{1,0:T(8,128)(2,1)S(1)} %add_convert_fusion.22), channel_id=1, source_target_pairs={{1,2},{2,1},{5,6},{6,5},{9,10},{10,9},{13,14},{14,13},{17,18},{18,... | collective-permute-start | bytes 737288 | tf_op jit(solution)/shard_map/ppermute | solution.py:320
  70.0 14.2 %collective-permute-start.21 = (bf16[640,384]{1,0:T(8,128)(2,1)S(1)}, bf16[640,384]{1,0:T(8,128)(2,1)S(1)}, u32[]{:S(2)}, u32[]{:S(2)}) collective-permute-start(bf16[640,384]{1,0:T(8,128)(2,1)S(1)} %get-tuple-element.95), channel_id=1, source_target_pairs={{0,16},{16,0},{1,17},{17,1},{2,18},{18,2},{3,19},{19,3},{4,20},{20... | collective-permute-start | bytes 1474568 | tf_op jit(solution)/shard_map/ppermute | solution.py:26
  71.6 10.1 %collective-permute-start.23 = (bf16[320,384]{1,0:T(8,128)(2,1)S(1)}, bf16[320,384]{1,0:T(8,128)(2,1)S(1)}, u32[]{:S(2)}, u32[]{:S(2)}) collective-permute-start(bf16[320,384]{1,0:T(8,128)(2,1)S(1)} %broadcast_select_fusion.5), channel_id=1, source_target_pairs={{0,1},{1,0},{2,3},{3,2},{4,5},{5,4},{6,7},{7,6},{8,9},{9,8},{10,11... | collective-permute-start | bytes 737288 | tf_op jit(solution)/shard_map/ppermute | solution.py:314
  76.1 7.3 %collective-permute-start.22 = (bf16[320,384]{1,0:T(8,128)(2,1)S(1)}, bf16[320,384]{1,0:T(8,128)(2,1)S(1)}, u32[]{:S(2)}, u32[]{:S(2)}) collective-permute-start(bf16[320,384]{1,0:T(8,128)(2,1)S(1)} %add_convert_fusion.19), channel_id=1, source_target_pairs={{1,2},{2,1},{5,6},{6,5},{9,10},{10,9},{13,14},{14,13},{17,18},{18,... | collective-permute-start | bytes 737288 | tf_op jit(solution)/shard_map/ppermute | solution.py:320
  76.9 12.3 %collective-permute-start.26 = (bf16[320,384]{1,0:T(8,128)(2,1)S(1)}, bf16[320,384]{1,0:T(8,128)(2,1)S(1)}, u32[]{:S(2)}, u32[]{:S(2)}) collective-permute-start(bf16[320,384]{1,0:T(8,128)(2,1)S(1)} %broadcast_select_fusion.4), channel_id=1, source_target_pairs={{0,1},{1,0},{2,3},{3,2},{4,5},{5,4},{6,7},{7,6},{8,9},{9,8},{10,11... | collective-permute-start | bytes 737288 | tf_op jit(solution)/shard_map/ppermute | solution.py:314
  81.3 20.3 %collective-permute-start.20 = (bf16[320,384]{1,0:T(8,128)(2,1)S(1)}, bf16[320,384]{1,0:T(8,128)(2,1)S(1)}, u32[]{:S(2)}, u32[]{:S(2)}) collective-permute-start(bf16[320,384]{1,0:T(8,128)(2,1)S(1)} %get-tuple-element.92), channel_id=1, source_target_pairs={{0,16},{16,0},{1,17},{17,1},{2,18},{18,2},{3,19},{19,3},{4,20},{20... | collective-permute-start | bytes 737288 | tf_op jit(solution)/shard_map/ppermute | solution.py:26
  81.6 15.3 %collective-permute-start.29 = (bf16[320,384]{1,0:T(8,128)(2,1)S(1)}, bf16[320,384]{1,0:T(8,128)(2,1)S(1)}, u32[]{:S(2)}, u32[]{:S(2)}) collective-permute-start(bf16[320,384]{1,0:T(8,128)(2,1)S(1)} %get-tuple-element.104), channel_id=1, source_target_pairs={{0,16},{16,0},{1,17},{17,1},{2,18},{18,2},{3,19},{19,3},{4,20},{20... | collective-permute-start | bytes 737288 | tf_op jit(solution)/shard_map/ppermute | solution.py:26
  83.4 6.6 %collective-permute-start.25 = (bf16[320,384]{1,0:T(8,128)(2,1)S(1)}, bf16[320,384]{1,0:T(8,128)(2,1)S(1)}, u32[]{:S(2)}, u32[]{:S(2)}) collective-permute-start(bf16[320,384]{1,0:T(8,128)(2,1)S(1)} %add_convert_fusion.16), channel_id=1, source_target_pairs={{1,2},{2,1},{5,6},{6,5},{9,10},{10,9},{13,14},{14,13},{17,18},{18,... | collective-permute-start | bytes 737288 | tf_op jit(solution)/shard_map/ppermute | solution.py:320
  84.3 11.7 %collective-permute-start.24 = (bf16[320,384]{1,0:T(8,128)(2,1)S(1)}, bf16[320,384]{1,0:T(8,128)(2,1)S(1)}, u32[]{:S(2)}, u32[]{:S(2)}) collective-permute-start(bf16[320,384]{1,0:T(8,128)(2,1)S(1)} %broadcast_select_fusion.3), channel_id=1, source_target_pairs={{0,1},{1,0},{2,3},{3,2},{4,5},{5,4},{6,7},{7,6},{8,9},{9,8},{10,11... | collective-permute-start | bytes 737288 | tf_op jit(solution)/shard_map/ppermute | solution.py:314
  89.3 7.5 %collective-permute-start.30 = (bf16[320,384]{1,0:T(8,128)(2,1)S(1)}, bf16[320,384]{1,0:T(8,128)(2,1)S(1)}, u32[]{:S(2)}, u32[]{:S(2)}) collective-permute-start(bf16[320,384]{1,0:T(8,128)(2,1)S(1)} %add_convert_fusion.13), channel_id=1, source_target_pairs={{1,2},{2,1},{5,6},{6,5},{9,10},{10,9},{13,14},{14,13},{17,18},{18,... | collective-permute-start | bytes 737288 | tf_op jit(solution)/shard_map/ppermute | solution.py:320
  90.2 10.5 %collective-permute-start.28 = (bf16[320,384]{1,0:T(8,128)(2,1)S(1)}, bf16[320,384]{1,0:T(8,128)(2,1)S(1)}, u32[]{:S(2)}, u32[]{:S(2)}) collective-permute-start(bf16[320,384]{1,0:T(8,128)(2,1)S(1)} %broadcast_select_fusion.2), channel_id=1, source_target_pairs={{0,1},{1,0},{2,3},{3,2},{4,5},{5,4},{6,7},{7,6},{8,9},{9,8},{10,11... | collective-permute-start | bytes 737288 | tf_op jit(solution)/shard_map/ppermute | solution.py:314
  96.1 5.4 %collective-permute-start.27 = (bf16[320,384]{1,0:T(8,128)(2,1)S(1)}, bf16[320,384]{1,0:T(8,128)(2,1)S(1)}, u32[]{:S(2)}, u32[]{:S(2)}) collective-permute-start(bf16[320,384]{1,0:T(8,128)(2,1)S(1)} %add_convert_fusion.10), channel_id=1, source_target_pairs={{1,2},{2,1},{5,6},{6,5},{9,10},{10,9},{13,14},{14,13},{17,18},{18,... | collective-permute-start | bytes 737288 | tf_op jit(solution)/shard_map/ppermute | solution.py:320
  97.0 10.5 %collective-permute-start.33 = (bf16[320,384]{1,0:T(8,128)(2,1)S(1)}, bf16[320,384]{1,0:T(8,128)(2,1)S(1)}, u32[]{:S(2)}, u32[]{:S(2)}) collective-permute-start(bf16[320,384]{1,0:T(8,128)(2,1)S(1)} %broadcast_select_fusion.1), channel_id=1, source_target_pairs={{0,1},{1,0},{2,3},{3,2},{4,5},{5,4},{6,7},{7,6},{8,9},{9,8},{10,11... | collective-permute-start | bytes 737288 | tf_op jit(solution)/shard_map/ppermute | solution.py:314
  100.8 8.9 %collective-permute-start.32 = (bf16[320,384]{1,0:T(8,128)(2,1)S(1)}, bf16[320,384]{1,0:T(8,128)(2,1)S(1)}, u32[]{:S(2)}, u32[]{:S(2)}) collective-permute-start(bf16[320,384]{1,0:T(8,128)(2,1)S(1)} %add_convert_fusion.7), channel_id=1, source_target_pairs={{1,2},{2,1},{5,6},{6,5},{9,10},{10,9},{13,14},{14,13},{17,18},{18,... | collective-permute-start | bytes 737288 | tf_op jit(solution)/shard_map/ppermute | solution.py:320
  101.7 10.7 %collective-permute-start.31 = (bf16[320,384]{1,0:T(8,128)(2,1)S(1)}, bf16[320,384]{1,0:T(8,128)(2,1)S(1)}, u32[]{:S(2)}, u32[]{:S(2)}) collective-permute-start(bf16[320,384]{1,0:T(8,128)(2,1)S(1)} %broadcast_select_fusion), channel_id=1, source_target_pairs={{0,1},{1,0},{2,3},{3,2},{4,5},{5,4},{6,7},{7,6},{8,9},{9,8},{10,11... | collective-permute-start | bytes 737288 | tf_op jit(solution)/shard_map/ppermute | solution.py:314
  108.3 6.8 %collective-permute-start.36 = (bf16[320,384]{1,0:T(8,128)(2,1)}, bf16[320,384]{1,0:T(8,128)(2,1)}, u32[]{:S(2)}, u32[]{:S(2)}) collective-permute-start(bf16[320,384]{1,0:T(8,128)(2,1)} %add_convert_fusion.4), channel_id=1, source_target_pairs={{1,2},{2,1},{5,6},{6,5},{9,10},{10,9},{13,14},{14,13},{17,18},{18,... | collective-permute-start | bytes 737288 | tf_op jit(solution)/shard_map/ppermute | solution.py:320
  109.7 10.2 %collective-permute-start.35 = (bf16[320,384]{1,0:T(8,128)(2,1)S(1)}, bf16[320,384]{1,0:T(8,128)(2,1)}, u32[]{:S(2)}, u32[]{:S(2)}) collective-permute-start(bf16[320,384]{1,0:T(8,128)(2,1)S(1)} %add_convert_fusion.3.refs_15_), channel_id=1, source_target_pairs={{0,1},{1,0},{2,3},{3,2},{4,5},{5,4},{6,7},{7,6},{8,9},{9,8},{10,11... | collective-permute-start | bytes 737288 | tf_op jit(solution)/shard_map/ppermute | solution.py:314
  113.2 11.1 %collective-permute-start.34 = (bf16[320,384]{1,0:T(8,128)(2,1)}, bf16[320,384]{1,0:T(8,128)(2,1)}, u32[]{:S(2)}, u32[]{:S(2)}) collective-permute-start(bf16[320,384]{1,0:T(8,128)(2,1)} %add_convert_fusion.2), channel_id=1, source_target_pairs={{1,2},{2,1},{5,6},{6,5},{9,10},{10,9},{13,14},{14,13},{17,18},{18,... | collective-permute-start | bytes 737288 | tf_op jit(solution)/shard_map/ppermute | solution.py:320
  114.5 11.1 %collective-permute-start.37 = (bf16[512,384]{1,0:T(8,128)(2,1)}, bf16[512,384]{1,0:T(8,128)(2,1)S(1)}, u32[]{:S(2)}, u32[]{:S(2)}) collective-permute-start(bf16[512,384]{1,0:T(8,128)(2,1)} %get-tuple-element.117.refs_0_), channel_id=1, source_target_pairs={{0,4},{4,0},{8,12},{12,8},{1,5},{5,1},{9,13},{13,9},{2,6},{6,2},{1... | collective-permute-start | bytes 1179656 | tf_op jit(solution)/shard_map/ppermute | solution.py:26
  114.5 11.1 %collective-permute-start.38 = (bf16[512,384]{1,0:T(8,128)(2,1)}, bf16[512,384]{1,0:T(8,128)(2,1)S(1)}, u32[]{:S(2)}, u32[]{:S(2)}) collective-permute-start(bf16[512,384]{1,0:T(8,128)(2,1)} %collective-permute-done.9.refs_1_), channel_id=1, source_target_pairs={{0,4},{4,0},{8,12},{12,8},{1,5},{5,1},{9,13},{13,9},{2,6},{6,2},{1... | collective-permute-start | bytes 1179656 | tf_op jit(solution)/shard_map/ppermute | solution.py:26
  116.2 9.5 %copy-start.10 = (bf16[1536,640]{1,0:T(8,128)(2,1)S(1)}, bf16[1536,640]{1,0:T(8,128)(2,1)}, u32[]{:S(2)}) copy-start(bf16[1536,640]{1,0:T(8,128)(2,1)} %refs_8_.3) | copy-start | bytes 5898244
  116.2 13.6 %collective-permute-start.39 = (bf16[320,384]{1,0:T(8,128)(2,1)S(1)}, bf16[320,384]{1,0:T(8,128)(2,1)S(1)}, u32[]{:S(2)}, u32[]{:S(2)}) collective-permute-start(bf16[320,384]{1,0:T(8,128)(2,1)S(1)} %add_convert_fusion.1.refs_1_), channel_id=1, source_target_pairs={{0,1},{1,0},{2,3},{3,2},{4,5},{5,4},{6,7},{7,6},{8,9},{9,8},{10,11... | collective-permute-start | bytes 737288 | tf_op jit(solution)/shard_map/ppermute | solution.py:314
  125.4 6.7 %collective-permute-start.40 = (bf16[320,384]{1,0:T(8,128)(2,1)S(1)}, bf16[320,384]{1,0:T(8,128)(2,1)S(1)}, u32[]{:S(2)}, u32[]{:S(2)}) collective-permute-start(bf16[320,384]{1,0:T(8,128)(2,1)S(1)} %add_convert_fusion.refs_3_), channel_id=1, source_target_pairs={{0,1},{1,0},{2,3},{3,2},{4,5},{5,4},{6,7},{7,6},{8,9},{9,8},{10,11... | collective-permute-start | bytes 737288 | tf_op jit(solution)/shard_map/ppermute | solution.py:314
  (7 other events, 7.0 us)

commit v10 on v9

--- a/solution.py
+++ b/solution.py
@@ -87,8 +87,8 @@
 def second_kernel(offsets, far, per, idx_ref, *refs):
     n = len(offsets)
     blocks, pays, refs = refs[:n], refs[n : 2 * n], refs[2 * n :]
-    w_ref, even_ref, odd_ref, grad_ref, enc_ref, pre_ref, *sent_refs = refs[:-5]
-    rows_scr, y_scr, p_scr, x_scr, edge_scr = refs[-5:]
+    w_ref, even_ref, odd_ref, grad_ref, enc_ref, pre_ref, all_ref, *sent_refs = refs[:-4]
+    rows_scr, y_scr, p_scr, edge_scr = refs[-4:]
     me = idx_ref[0]
     pick = lambda items: [items[j] for j in far]
     conv_rows(pick(offsets), me, pick(blocks), pick(pays), w_ref, rows_scr, y_scr)
@@ -114,21 +114,15 @@
     for c in range(width // LANES):
         lanes = slice(c * LANES, (c + 1) * LANES)
         pre_ref[EDGE : EDGE + length, lanes] = p_scr[c].astype(BF16).astype(F32)
-    if not sent_refs:
-        return
-    wanted = (1 - idx_ref[1]) * per
     depth = blocks[0].shape[0]
     for off, block, pay in zip(offsets, blocks, pays):
-
-        @pl.when(me ^ off == wanted)
-        def _(block=block, pay=pay):
-            x_scr[:, 0:length] = block[...]
-            x_scr[:, length : length + LANES] = edge_block(pay, depth)
-
-    p, edge = shifted_rows(pre_ref, edge_scr, (0,))
-    res = jnp.dot(x_scr[:, 0:length], p, preferred_element_type=F32)
-    res = res + jnp.dot(x_scr[:, length : length + LANES], edge, preferred_element_type=F32)
-    sent_refs[0][...] = res.astype(BF16)
+        rows = pl.ds(pl.multiple_of((me ^ off) * depth, 16), depth)
+        all_ref[rows, 0:length] = block[...]
+        all_ref[rows, length : length + LANES] = edge_block(pay, depth)
+    if sent_refs:
+        wanted = pl.ds(pl.multiple_of((1 - idx_ref[1]) * per * depth, 16), depth)
+        rows = shifted_rows(pre_ref, edge_scr, (0,))
+        sent_refs[0][...] = jnp.dot(all_ref[wanted, :], rows, preferred_element_type=F32).astype(BF16)
 
 
 def shifted_rows(p_ref, edge_scr, group):
@@ -140,50 +134,32 @@
         edge_scr[0:2, cols] = p_ref[EDGE - tap : EDGE - tap + 2, :]
         edge_scr[2:4, cols] = p_ref[EDGE + length + 2 - tap : EDGE + length + 4 - tap, :]
         shifted.append(p_ref[EDGE + 2 - tap : EDGE + 2 - tap + length, :].astype(BF16))
-    return jnp.concatenate(shifted, axis=1), edge_scr[:, 0 : len(group) * width].astype(BF16)
-
-
-def grad_kernel(offsets, group, per, pieces, idx_ref, *refs):
-    n = len(offsets)
-    blocks, pays, p_ref = refs[:n], refs[n : 2 * n], refs[2 * n]
-    out_refs, edge_scr = list(refs[2 * n + 1 : -1]), refs[-1]
+    edge = edge_scr[:, 0 : len(group) * width].astype(BF16)
+    return jnp.concatenate([jnp.concatenate(shifted, axis=1), edge], axis=0)
+
+
+def grad_kernel(group, depth, per, pieces, idx_ref, all_ref, p_ref, *refs):
+    out_refs, edge_scr = list(refs[:-1]), refs[-1]
     width = p_ref.shape[1]
-    me = idx_ref[0]
-    x = jnp.concatenate([ref[...] for ref in blocks], axis=0)
-    depth = x.shape[0] // n
-    halo = jnp.concatenate([edge_block(ref, depth) for ref in pays], axis=0)
+    half = per * depth
     for first in range(0, len(group), 2):
         some = group[first : first + 2]
-        p, edge = shifted_rows(p_ref, edge_scr, some)
-        res = jnp.dot(x, p, preferred_element_type=F32) + jnp.dot(halo, edge, preferred_element_type=F32)
-        res = res.astype(BF16)
+        rows = shifted_rows(p_ref, edge_scr, some)
+        res = jnp.dot(all_ref[...], rows, preferred_element_type=F32).astype(BF16)
         for i in range(len(some)):
+            part = res[:, i * width : (i + 1) * width]
             own_ref = out_refs.pop(0)
+            if not per:
+                own_ref[...] = part
+                continue
+            lower = idx_ref[1] == 0
+            own_ref[...] = jnp.where(lower, part[0:half], part[half : 2 * half])
+            other = jnp.where(lower, part[half : 2 * half], part[0:half])
             named = pieces[first + i]
-            other_refs = [out_refs.pop(0) for _ in range(len(named) or min(per, 1))]
-            for j, off in enumerate(offsets):
-                part = res[j * depth : (j + 1) * depth, i * width : (i + 1) * width]
-                at = me ^ off
-                if not per:
-                    own_ref[pl.ds(pl.multiple_of(at * depth, 16), depth), :] = part
-                    continue
-                mine = lax.div(at, per) == idx_ref[1]
-                other = jnp.logical_not(mine)
-                row = lax.rem(at, per)
-                hits = [(own_ref, mine)]
-                if not named:
-                    hits.append((other_refs[0], other))
-                for ref, hit in hits:
-
-                    @pl.when(hit)
-                    def _(ref=ref, part=part, row=row):
-                        ref[pl.ds(pl.multiple_of(row * depth, 16), depth), :] = part
-
-                for r, ref in zip(named, other_refs):
-
-                    @pl.when(jnp.logical_and(other, row == r))
-                    def _(ref=ref, part=part):
-                        ref[...] = part
+            if not named:
+                out_refs.pop(0)[...] = other
+            for r in named:
+                out_refs.pop(0)[...] = other[r * depth : (r + 1) * depth]
 
 
 def qkv_kernel(offsets, idx_ref, *refs):
@@ -370,17 +346,17 @@
     pair = shards == 2 and peers % shards == 0 and lax.axis_size("dp") == 4
     per = peers // shards if pair else 0
     piece = jax.ShapeDtypeStruct((depth, width), BF16)
-    encoded, pre_grad, *first = call(
+    encoded, pre_grad, joined, *first = call(
         functools.partial(second_kernel, offsets, far, per),
         (
             jax.ShapeDtypeStruct((half, width), BF16),
             jax.ShapeDtypeStruct((length + 2 * EDGE, width), F32),
+            jax.ShapeDtypeStruct((peers * depth, length + LANES), BF16),
             *([piece] if pair else []),
         ),
         scratch(far)
         + [
             pltpu.VMEM((width // LANES, length, LANES), F32),
-            pltpu.VMEM((depth, length + LANES), BF16),
             pltpu.VMEM((LANES, width), F32),
         ],
         26,
@@ -391,7 +367,7 @@
         encs = encs + [swap(e, "mp", bit) for e in encs]
 
     everything = tuple(range(per))
-    pieces_of = lambda k: everything[1:] if k == 0 else (everything if k in (1, taps - 1) else ())
+    pieces_of = lambda k: everything[1:] if k == 0 else (everything if k == 1 else ())
 
     def gradient(group, hold):
         pieces = [pieces_of(k) for k in group]
@@ -403,11 +379,11 @@
             whole = jax.ShapeDtypeStruct((per * depth, width), BF16)
             outs.append([whole] + ([piece] * len(q) if q else [whole]))
         flat = call(
-            functools.partial(grad_kernel, offsets, group, per, pieces),
+            functools.partial(grad_kernel, group, depth, per, pieces),
             tuple(o for tap in outs for o in tap),
             [pltpu.VMEM((LANES, width * min(len(group), 2)), F32)],
             24 if len(group) > 2 else 16,
-            after(idx, *hold) if hold else idx, *blocks, *payloads, pre_grad,
+            after(idx, *hold) if hold else idx, joined, pre_grad,
         )
         flat = list(flat)
         taken = [[flat.pop(0) for _ in tap] for tap in outs]
@@ -452,26 +428,28 @@
         value = got[tap][row] if len(got[tap]) > 1 else got[tap][0][rows]
         return added(keep[tap][rows], value if last is None else after(value, last))
 
+    starts = {(k - 1) * per - 1 - (k == 3): k for k in range(2, taps)}
+
     def sent(r, last, sums):
-        if r == per - 1:
-            work(tuple(range(3, taps)), [last] + encs[1:])
-            last = keep[-1]
-        if r % per == per - 1 and r // per + 2 < taps and r < chunks:
-            launch(r // per + 2, [last])
+        if r < chunks and r in starts:
+            launch(starts[r], [last])
         if r == chunks + 2:
-            last = done["qkv"] = qkv_call(after(idx, last, *relays), encs + relays)
-        return last
-
-    def idle(c, last, sums):
-        if c == per:
-            held = encs[1:]
-            relays.extend([swap(after(e, last, *held), "mp", bits[-1]) for e in encs])
-        if c == chunks:
             early = len(sums) // per
             parts = [sums[i] for i in range(early * per)]
             parts[0] = (after(parts[0][0], last), parts[0][1])
             last = done["early"] = written(parts, early, 0, None, (taps, per * depth, width))
             done["at"] = early
+        return last
+
+    def idle(c, last, sums):
+        if c == per + 4:
+            held = encs[1:]
+            relays.extend([swap(after(e, last, *held), "mp", bits[-1]) for e in encs])
+        if c == 0:
+            work(tuple(range(3, taps)), [last] + encs[1:])
+            last = keep[-1]
+        if c == chunks:
+            last = done["qkv"] = qkv_call(after(idx, last, *relays), encs + relays)
         return last
 
     sums = chain_sums(chunks, share, sent, idle)

time: 134 us -> 130 us (0.970)
  starting transfers between devices: 71.6 us -> 64.4 us
  local copies, waits for them, and re-layouts: 10.8 us -> 14.9 us
  waiting for transfers between devices: 10.7 us -> 14.7 us
  other arithmetic: 8.77 us -> 5.25 us
  Pallas kernels: 30.3 us -> 28.4 us
    ppermute x13, starting transfers between devices: 46 us -> 40.5 us  [chain_sums(): outer[r] = lax.ppermute(value, 'dp', outer_pairs)]
    unnamed x28 -> x46, local copies, waits for them, and re-layouts: 9.9 us -> 14 us
    convert_element_type x23, other arithmetic: 7.91 us -> 4.42 us  [added(): return (a.astype(F32) + b.astype(F32)).astype(BF16)]
    ppermute x18 -> x17, waiting for transfers between devices: 5.77 us -> 8.64 us  [swap(): return lax.ppermute(value, axis, [(i, i ^ bit) for i in range(peers)])]
    pallas_call x6, Pallas kernels: 25.7 us -> 23.9 us  [call(): pl.pallas_call(kernel, out_shape=out, in_specs=[pl.BlockSpec(memory_space...]
    ppermute x18 -> x17, starting transfers between devices: 17.5 us -> 17 us  [swap(): return lax.ppermute(value, axis, [(i, i ^ bit) for i in range(peers)])]
  transfers between devices with their start and end apart: 41 -> 40, of which waited for: 10 -> 9; matrix products, arithmetic and copies ran while one was open for 7% -> 5% of each run, Pallas kernels for 17% -> 16%
where the time goes in v10:
time: 130 us; the launch traced here: 129 us
  starting transfers between devices  64.4 us (50%)
  Pallas kernels  28.4 us (22%)
  local copies, waits for them, and re-layouts  14.9 us (11%)
  waiting for transfers between devices  14.7 us (11%)
  other arithmetic  5.25 us (4%)
    ppermute x13, starting transfers between devices, chain_sums(): outer[r] = lax.ppermute(value, 'dp', outer_pairs)  40.5 us
    pallas_call x6, Pallas kernels, call(): pl.pallas_call(kernel, out_shape=out, in_specs=[pl.BlockSpec(memory_space...  23.9 us
    ppermute x17, starting transfers between devices, swap(): return lax.ppermute(value, axis, [(i, i ^ bit) for i in range(peers)])  17 us
    unnamed x46, local copies, waits for them, and re-layouts  14 us
    ppermute x17, waiting for transfers between devices, swap(): return lax.ppermute(value, axis, [(i, i ^ bit) for i in range(peers)])  8.64 us
    ppermute x10, starting transfers between devices, chain_sums(): middle[r - 1] = lax.ppermute(last, 'dp', middle_pairs)  6.89 us
    ppermute x13, waiting for transfers between devices, chain_sums(): outer[r] = lax.ppermute(value, 'dp', outer_pairs)  6.02 us
    convert_element_type x23, other arithmetic, added(): return (a.astype(F32) + b.astype(F32)).astype(BF16)  4.42 us
  transfers between devices with their start and end apart: 40, of which 9 were waited for; matrix products, arithmetic and copies ran while one was open for 5% of the time, Pallas kernels for 16%

profile of v10, /device:TPU:0, one launch (start us, length us, event | category | flops | bytes accessed | tf_op | source)
XLA Modules:
  0.0 128.8 jit_solution(15927684849455954026)
XLA Ops:
  1.1 2.6 %collective-permute-start = (bf16[320,1024]{1,0:T(8,128)(2,1)}, bf16[320,1024]{1,0:T(8,128)(2,1)S(1)}, u32[]{:S(2)}, u32[]{:S(2)}) collective-permute-start(bf16[320,1024]{1,0:T(8,128)(2,1)} %bitcast.10), channel_id=1, source_target_pairs={{0,8},{4,12},{8,0},{12,4},{1,9},{5,13},{9,1},{13,5},{2,10},{6,14},... | collective-permute-start | bytes 1966088 | tf_op jit(solution)/shard_map/ppermute | solution.py:26
  3.7 1.1 copy-done.4
  5.0 1.6 %collective-permute-start.2 = (f32[8,384]{1,0:T(8,128)S(1)}, f32[8,384]{1,0:T(8,128)S(1)}, u32[]{:S(2)}, u32[]{:S(2)}) collective-permute-start(f32[8,384]{1,0:T(8,128)S(1)} %shard_map.68), channel_id=1, source_target_pairs={{0,16},{16,0},{1,17},{17,1},{2,18},{18,2},{3,19},{19,3},{4,20},{20... | collective-permute-start | bytes 36872 | tf_op jit(solution)/shard_map/ppermute | solution.py:26
  7.3 1.4 %collective-permute-done.2 = f32[8,384]{1,0:T(8,128)S(1)} collective-permute-done((f32[8,384]{1,0:T(8,128)S(1)}, f32[8,384]{1,0:T(8,128)S(1)}, u32[]{:S(2)}, u32[]{:S(2)}) %collective-permute-start.2) | collective-permute-done | bytes 12320 | tf_op jit(solution)/shard_map/ppermute | solution.py:26
  8.9 0.9 collective-permute-start.4
  9.8 0.9 collective-permute-start.3
  11.6 2.4 %copy-done = bf16[5,1280,384]{2,1,0:T(8,128)(2,1)S(1)} copy-done((bf16[5,1280,384]{2,1,0:T(8,128)(2,1)S(1)}, bf16[5,1280,384]{2,1,0:T(8,128)(2,1)}, u32[]{:S(2)}) %copy-start) | copy-done | bytes 4915224
  14.0 1.1 copy-done.5
  15.1 4.3 %shard_map.69 = (f32[512,384]{1,0:T(8,128)S(1)}, f32[512,384]{1,0:T(8,128)S(1)}) custom-call(s32[2]{0:T(128)S(1)} %pad_add_fusion.idx_ref, bf16[320,1024]{1,0:T(8,128)(2,1)S(1)} %bitcast.13, bf16[320,1024]{1,0:T(8,128)(2,1)S(1)} %collective-permute-done.1.refs_1_.refs_2_, f32[8,384]{1,0:T(8,128)S(1)} %maximum_maximum_fusion.refs_2_.refs_4_, ...), custom_call_target="tpu_custom_call" | custom-call | tf_op jit(solution)/shard_map/pallas_call | solution.py:187
  20.6 1.3 collective-permute-done.6.refs_3_
  21.9 1.1 copy-done.8
  23.0 1.1 copy-done.17
  24.1 6.2 %shard_map.70 = (bf16[512,384]{1,0:T(8,128)(2,1)S(1)}, f32[1040,384]{1,0:T(8,128)S(1)}, bf16[1280,1152]{1,0:T(8,128)(2,1)S(1)}, bf16[320,384]{1,0:T(8,128)(2,1)S(1)}) custom-call(s32[2]{0:T(128)S(1)} %pad_add_fusion.idx_ref, bf16[320,1024]{1,0:T(8,128)(2,1)S(1)} %bitcast.14, bf16[320,1024]{1,0:T(8,128)(2,1)S(1)} %copy-done.17, ...), custom_call_target="tpu_custom_call" | custom-call | tf_op jit(solution)/shard_map/pallas_call | solution.py:187
  30.3 1.8 %collective-permute-start.7 = (bf16[320,384]{1,0:T(8,128)(2,1)S(1)}, bf16[320,384]{1,0:T(8,128)(2,1)S(1)}, u32[]{:S(2)}, u32[]{:S(2)}) collective-permute-start(bf16[320,384]{1,0:T(8,128)(2,1)S(1)} %get-tuple-element.67), channel_id=1, source_target_pairs={{0,16},{16,0},{1,17},{17,1},{2,18},{18,2},{3,19},{19,3},{4,20},{20... | collective-permute-start | bytes 737288 | tf_op jit(solution)/shard_map/ppermute | solution.py:26
  32.1 3.0 %shard_map.71 = (bf16[640,384]{1,0:T(8,128)(2,1)S(1)}, bf16[320,384]{1,0:T(8,128)(2,1)}) custom-call(s32[2]{0:T(128)S(1)} %pad_add_fusion.idx_ref, bf16[1280,1152]{1,0:T(8,128)(2,1)S(1)} %get-tuple-element.64.all_ref, f32[1040,384]{1,0:T(8,128)S(1)} %get-tuple-element.65.p_ref), custom_call_target="tpu_custom_call" | custom-call | tf_op jit(solution)/shard_map/pallas_call | solution.py:187
  35.1 1.1 copy-done.2
  36.6 1.8 %collective-permute-done.7 = bf16[320,384]{1,0:T(8,128)(2,1)S(1)} collective-permute-done((bf16[320,384]{1,0:T(8,128)(2,1)S(1)}, bf16[320,384]{1,0:T(8,128)(2,1)S(1)}, u32[]{:S(2)}, u32[]{:S(2)}) %collective-permute-start.7) | collective-permute-done | bytes 245792 | tf_op jit(solution)/shard_map/ppermute | solution.py:26
  39.2 1.8 %collective-permute-start.8 = (bf16[320,384]{1,0:T(8,128)(2,1)}, bf16[320,384]{1,0:T(8,128)(2,1)}, u32[]{:S(2)}, u32[]{:S(2)}) collective-permute-start(bf16[320,384]{1,0:T(8,128)(2,1)} %add_convert_fusion.29), channel_id=1, source_target_pairs={{0,1},{1,0},{2,3},{3,2},{4,5},{5,4},{6,7},{7,6},{8,9},{9,8},{10,11... | collective-permute-start | bytes 737288 | tf_op jit(solution)/shard_map/ppermute | solution.py:290
  40.9 1.5 %collective-permute-start.10 = (bf16[512,384]{1,0:T(8,128)(2,1)}, bf16[512,384]{1,0:T(8,128)(2,1)S(1)}, u32[]{:S(2)}, u32[]{:S(2)}) collective-permute-start(bf16[512,384]{1,0:T(8,128)(2,1)} %copy-done.19), channel_id=1, source_target_pairs={{0,8},{4,12},{8,0},{12,4},{1,9},{5,13},{9,1},{13,5},{2,10},{6,14},... | collective-permute-start | bytes 1179656 | tf_op jit(solution)/shard_map/ppermute | solution.py:26
  42.5 1.4 %copy-done.3 = f32[1040,384]{1,0:T(8,128)S(1)} copy-done((f32[1040,384]{1,0:T(8,128)S(1)}, f32[1040,384]{1,0:T(8,128)}, u32[]{:S(2)}) %copy-start.3) | copy-done | bytes 1597464
  43.9 3.5 %shard_map.73 = (bf16[640,384]{1,0:T(8,128)(2,1)S(1)}, bf16[320,384]{1,0:T(8,128)(2,1)S(1)}, bf16[320,384]{1,0:T(8,128)(2,1)S(1)}, bf16[640,384]{1,0:T(8,128)(2,1)S(1)}, bf16[640,384]{1,0:T(8,128)(2,1)S(1)}) custom-call(s32[2]{0:T(128)S(1)} %pad_add_fusion.idx_ref, bf16[1280,1152]{1,0:T(8,128)(2,1)S(1)} %get-tuple-element.64.all_ref, f32[1040,384]{1,0:T(8,128)S(1)} %copy-done.3), custom_call_target="tpu_custom_call" | custom-call | tf_op jit(solution)/shard_map/pallas_call | solution.py:187
  47.4 2.1 %collective-permute-start.11 = (bf16[320,384]{1,0:T(8,128)(2,1)S(1)}, bf16[320,384]{1,0:T(8,128)(2,1)S(1)}, u32[]{:S(2)}, u32[]{:S(2)}) collective-permute-start(bf16[320,384]{1,0:T(8,128)(2,1)S(1)} %get-tuple-element.77), channel_id=1, source_target_pairs={{0,16},{16,0},{1,17},{17,1},{2,18},{18,2},{3,19},{19,3},{4,20},{20... | collective-permute-start | bytes 737288 | tf_op jit(solution)/shard_map/ppermute | solution.py:26
  49.6 1.0 add_convert_fusion.28
  51.1 1.9 %collective-permute-start.13 = (bf16[640,384]{1,0:T(8,128)(2,1)S(1)}, bf16[640,384]{1,0:T(8,128)(2,1)S(1)}, u32[]{:S(2)}, u32[]{:S(2)}) collective-permute-start(bf16[640,384]{1,0:T(8,128)(2,1)S(1)} %get-tuple-element.83), channel_id=1, source_target_pairs={{0,16},{16,0},{1,17},{17,1},{2,18},{18,2},{3,19},{19,3},{4,20},{20... | collective-permute-start | bytes 1474568 | tf_op jit(solution)/shard_map/ppermute | solution.py:26
  53.1 1.1 add_convert_fusion.27
  54.9 3.3 %shard_map.72 = (bf16[640,384]{1,0:T(8,128)(2,1)S(1)}, bf16[640,384]{1,0:T(8,128)(2,1)S(1)}, bf16[640,384]{1,0:T(8,128)(2,1)S(1)}, bf16[640,384]{1,0:T(8,128)(2,1)S(1)}) custom-call(s32[2]{0:T(128)S(1)} %pad_add_fusion.idx_ref, bf16[1280,1152]{1,0:T(8,128)(2,1)S(1)} %get-tuple-element.64.all_ref, f32[1040,384]{1,0:T(8,128)S(1)} %copy-done.3), custom_call_target="tpu_custom_call" | custom-call | tf_op jit(solution)/shard_map/pallas_call | solution.py:187
  58.3 4.5 %collective-permute-start.16 = (bf16[320,384]{1,0:T(8,128)(2,1)S(1)}, bf16[320,384]{1,0:T(8,128)(2,1)S(1)}, u32[]{:S(2)}, u32[]{:S(2)}) collective-permute-start(bf16[320,384]{1,0:T(8,128)(2,1)S(1)} %add_convert_fusion.26), channel_id=1, source_target_pairs={{0,1},{1,0},{2,3},{3,2},{4,5},{5,4},{6,7},{7,6},{8,9},{9,8},{10,11... | collective-permute-start | bytes 737288 | tf_op jit(solution)/shard_map/ppermute | solution.py:290
  63.9 1.8 %collective-permute-start.21 = (bf16[320,384]{1,0:T(8,128)(2,1)S(1)}, bf16[320,384]{1,0:T(8,128)(2,1)S(1)}, u32[]{:S(2)}, u32[]{:S(2)}) collective-permute-start(bf16[320,384]{1,0:T(8,128)(2,1)S(1)} %broadcast_select_fusion.6), channel_id=1, source_target_pairs={{0,1},{1,0},{2,3},{3,2},{4,5},{5,4},{6,7},{7,6},{8,9},{9,8},{10,11... | collective-permute-start | bytes 737288 | tf_op jit(solution)/shard_map/ppermute | solution.py:290
  65.6 2.8 %collective-permute-done.16 = bf16[320,384]{1,0:T(8,128)(2,1)S(1)} collective-permute-done((bf16[320,384]{1,0:T(8,128)(2,1)S(1)}, bf16[320,384]{1,0:T(8,128)(2,1)S(1)}, u32[]{:S(2)}, u32[]{:S(2)}) %collective-permute-start.16) | collective-permute-done | bytes 245792 | tf_op jit(solution)/shard_map/ppermute | solution.py:290
  69.3 2.9 %collective-permute-done.13 = bf16[640,384]{1,0:T(8,128)(2,1)S(1)} collective-permute-done((bf16[640,384]{1,0:T(8,128)(2,1)S(1)}, bf16[640,384]{1,0:T(8,128)(2,1)S(1)}, u32[]{:S(2)}, u32[]{:S(2)}) %collective-permute-start.13) | collective-permute-done | bytes 491552 | tf_op jit(solution)/shard_map/ppermute | solution.py:26
  72.3 1.7 %collective-permute-start.19 = (bf16[320,384]{1,0:T(8,128)(2,1)S(1)}, bf16[320,384]{1,0:T(8,128)(2,1)S(1)}, u32[]{:S(2)}, u32[]{:S(2)}) collective-permute-start(bf16[320,384]{1,0:T(8,128)(2,1)S(1)} %broadcast_select_fusion.5), channel_id=1, source_target_pairs={{0,1},{1,0},{2,3},{3,2},{4,5},{5,4},{6,7},{7,6},{8,9},{9,8},{10,11... | collective-permute-start | bytes 737288 | tf_op jit(solution)/shard_map/ppermute | solution.py:290
  75.2 4.9 %collective-permute-start.23 = (bf16[320,384]{1,0:T(8,128)(2,1)S(1)}, bf16[320,384]{1,0:T(8,128)(2,1)S(1)}, u32[]{:S(2)}, u32[]{:S(2)}) collective-permute-start(bf16[320,384]{1,0:T(8,128)(2,1)S(1)} %broadcast_select_fusion.4), channel_id=1, source_target_pairs={{0,1},{1,0},{2,3},{3,2},{4,5},{5,4},{6,7},{7,6},{8,9},{9,8},{10,11... | collective-permute-start | bytes 737288 | tf_op jit(solution)/shard_map/ppermute | solution.py:290
  80.9 2.0 %collective-permute-start.26 = (bf16[640,384]{1,0:T(8,128)(2,1)S(1)}, bf16[640,384]{1,0:T(8,128)(2,1)S(1)}, u32[]{:S(2)}, u32[]{:S(2)}) collective-permute-start(bf16[640,384]{1,0:T(8,128)(2,1)S(1)} %get-tuple-element.101), channel_id=1, source_target_pairs={{0,16},{16,0},{1,17},{17,1},{2,18},{18,2},{3,19},{19,3},{4,20},{20... | collective-permute-start | bytes 1474568 | tf_op jit(solution)/shard_map/ppermute | solution.py:26
  83.2 3.0 %collective-permute-start.28 = (bf16[320,384]{1,0:T(8,128)(2,1)S(1)}, bf16[320,384]{1,0:T(8,128)(2,1)S(1)}, u32[]{:S(2)}, u32[]{:S(2)}) collective-permute-start(bf16[320,384]{1,0:T(8,128)(2,1)S(1)} %broadcast_select_fusion.3), channel_id=1, source_target_pairs={{0,1},{1,0},{2,3},{3,2},{4,5},{5,4},{6,7},{7,6},{8,9},{9,8},{10,11... | collective-permute-start | bytes 737288 | tf_op jit(solution)/shard_map/ppermute | solution.py:290
  87.3 4.4 %collective-permute-start.25 = (bf16[320,384]{1,0:T(8,128)(2,1)S(1)}, bf16[320,384]{1,0:T(8,128)(2,1)S(1)}, u32[]{:S(2)}, u32[]{:S(2)}) collective-permute-start(bf16[320,384]{1,0:T(8,128)(2,1)S(1)} %broadcast_select_fusion.2), channel_id=1, source_target_pairs={{0,1},{1,0},{2,3},{3,2},{4,5},{5,4},{6,7},{7,6},{8,9},{9,8},{10,11... | collective-permute-start | bytes 737288 | tf_op jit(solution)/shard_map/ppermute | solution.py:290
  93.4 4.7 %collective-permute-start.30 = (bf16[320,384]{1,0:T(8,128)(2,1)S(1)}, bf16[320,384]{1,0:T(8,128)(2,1)S(1)}, u32[]{:S(2)}, u32[]{:S(2)}) collective-permute-start(bf16[320,384]{1,0:T(8,128)(2,1)S(1)} %broadcast_select_fusion.1), channel_id=1, source_target_pairs={{0,1},{1,0},{2,3},{3,2},{4,5},{5,4},{6,7},{7,6},{8,9},{9,8},{10,11... | collective-permute-start | bytes 737288 | tf_op jit(solution)/shard_map/ppermute | solution.py:290
  99.1 2.8 %collective-permute-start.34 = (bf16[320,384]{1,0:T(8,128)(2,1)S(1)}, bf16[320,384]{1,0:T(8,128)(2,1)S(1)}, u32[]{:S(2)}, u32[]{:S(2)}) collective-permute-start(bf16[320,384]{1,0:T(8,128)(2,1)S(1)} %broadcast_select_fusion), channel_id=1, source_target_pairs={{0,1},{1,0},{2,3},{3,2},{4,5},{5,4},{6,7},{7,6},{8,9},{9,8},{10,11... | collective-permute-start | bytes 737288 | tf_op jit(solution)/shard_map/ppermute | solution.py:290
  101.9 3.0 %collective-permute-done.30.refs_10_ = bf16[320,384]{1,0:T(8,128)(2,1)S(1)} collective-permute-done((bf16[320,384]{1,0:T(8,128)(2,1)S(1)}, bf16[320,384]{1,0:T(8,128)(2,1)S(1)}, u32[]{:S(2)}, u32[]{:S(2)}) %collective-permute-start.30) | collective-permute-done | bytes 245792 | tf_op jit(solution)/shard_map/ppermute | solution.py:290
  105.7 4.4 %collective-permute-start.32 = (bf16[320,384]{1,0:T(8,128)(2,1)S(1)}, bf16[320,384]{1,0:T(8,128)(2,1)S(1)}, u32[]{:S(2)}, u32[]{:S(2)}) collective-permute-start(bf16[320,384]{1,0:T(8,128)(2,1)S(1)} %add_convert_fusion.3.refs_15_), channel_id=1, source_target_pairs={{0,1},{1,0},{2,3},{3,2},{4,5},{5,4},{6,7},{7,6},{8,9},{9,8},{10,11... | collective-permute-start | bytes 737288 | tf_op jit(solution)/shard_map/ppermute | solution.py:290
  111.1 4.2 %collective-permute-start.38 = (bf16[320,384]{1,0:T(8,128)(2,1)S(1)}, bf16[320,384]{1,0:T(8,128)(2,1)}, u32[]{:S(2)}, u32[]{:S(2)}) collective-permute-start(bf16[320,384]{1,0:T(8,128)(2,1)S(1)} %add_convert_fusion.1.refs_1_), channel_id=1, source_target_pairs={{0,1},{1,0},{2,3},{3,2},{4,5},{5,4},{6,7},{7,6},{8,9},{9,8},{10,11... | collective-permute-start | bytes 737288 | tf_op jit(solution)/shard_map/ppermute | solution.py:290
  115.3 3.6 %shard_map.74 = bf16[512,640]{1,0:T(8,128)(2,1)} custom-call(s32[2]{0:T(128)S(1)} %pad_add_fusion.idx_ref, bf16[512,384]{1,0:T(8,128)(2,1)S(1)} %copy-done.20, bf16[512,384]{1,0:T(8,128)(2,1)S(1)} %collective-permute-done.10.refs_1_, bf16[512,384]{1,0:T(8,128)(2,1)S(1)} %collective-permute-done.35.refs_2_, ...), custom_call_target="tpu_custom_call" | custom-call | tf_op jit(solution)/shard_map/pallas_call | solution.py:187
  118.9 1.7 %collective-permute-start.39 = (bf16[320,384]{1,0:T(8,128)(2,1)S(1)}, bf16[320,384]{1,0:T(8,128)(2,1)}, u32[]{:S(2)}, u32[]{:S(2)}) collective-permute-start(bf16[320,384]{1,0:T(8,128)(2,1)S(1)} %add_convert_fusion.refs_3_), channel_id=1, source_target_pairs={{0,1},{1,0},{2,3},{3,2},{4,5},{5,4},{6,7},{7,6},{8,9},{9,8},{10,11... | collective-permute-start | bytes 737288 | tf_op jit(solution)/shard_map/ppermute | solution.py:290
  120.7 0.9 copy-done.11
  121.6 0.9 copy-done.13
  122.6 0.9 copy-done.15
  123.5 0.9 copy-done.22
  124.5 2.2 %shard_map.75.b = f32[5,640,384]{2,1,0:T(8,128)} custom-call(s32[1]{0:T(128)} %bitcast.7.end_ref.end, bf16[320,384]{1,0:T(8,128)(2,1)S(1)} %collective-permute-done.21.refs_0_, bf16[320,384]{1,0:T(8,128)(2,1)S(1)} %add_convert_fusion.24.refs_1_, bf16[320,384]{1,0:T(8,128)(2,1)S(1)} %collective-permute-done.19.refs_2_, ...), custom_call_target="tpu_custom_call" | custom-call | tf_op jit(solution)/shard_map/pallas_call | solution.py:222
  126.7 2.1 %shard_map.76 = f32[5,640,384]{2,1,0:T(8,128)} custom-call(s32[1]{0:T(128)} %bitcast.7.end_ref.end, f32[5,640,384]{2,1,0:T(8,128)} %shard_map.75.b, bf16[320,384]{1,0:T(8,128)(2,1)} %collective-permute-done.38.refs_0_, bf16[320,384]{1,0:T(8,128)(2,1)S(1)} %add_convert_fusion.1.refs_1_, ...), custom_call_target="tpu_custom_call", output_to_operand_aliasing={{}: (1, {})} | custom-call | tf_op jit(solution)/shard_map/pallas_call | solution.py:222
  (126 shorter events, 15.6 us)
Async XLA Ops:
  0.6 10.9 %collective-permute-start.1 = (bf16[320,1024]{1,0:T(8,128)(2,1)}, bf16[320,1024]{1,0:T(8,128)(2,1)S(1)}, u32[]{:S(2)}, u32[]{:S(2)}) collective-permute-start(bf16[320,1024]{1,0:T(8,128)(2,1)} %bitcast.9), channel_id=1, source_target_pairs={{0,4},{4,0},{8,12},{12,8},{1,5},{5,1},{9,13},{13,9},{2,6},{6,2},{1... | collective-permute-start | bytes 1966088 | tf_op jit(solution)/shard_map/ppermute | solution.py:26
  1.1 18.7 %collective-permute-start = (bf16[320,1024]{1,0:T(8,128)(2,1)}, bf16[320,1024]{1,0:T(8,128)(2,1)S(1)}, u32[]{:S(2)}, u32[]{:S(2)}) collective-permute-start(bf16[320,1024]{1,0:T(8,128)(2,1)} %bitcast.10), channel_id=1, source_target_pairs={{0,8},{4,12},{8,0},{12,4},{1,9},{5,13},{9,1},{13,5},{2,10},{6,14},... | collective-permute-start | bytes 1966088 | tf_op jit(solution)/shard_map/ppermute | solution.py:26
  4.9 17.0 %copy-start.18 = (bf16[1,512,384]{2,1,0:T(8,128)(2,1)S(1)}, bf16[1,512,384]{2,1,0:T(8,128)(2,1)}, u32[]{:S(2)}) copy-start(bf16[1,512,384]{2,1,0:T(8,128)(2,1)} %param.9) | copy-start | bytes 1179652
  5.0 3.8 %collective-permute-start.2 = (f32[8,384]{1,0:T(8,128)S(1)}, f32[8,384]{1,0:T(8,128)S(1)}, u32[]{:S(2)}, u32[]{:S(2)}) collective-permute-start(f32[8,384]{1,0:T(8,128)S(1)} %shard_map.68), channel_id=1, source_target_pairs={{0,16},{16,0},{1,17},{17,1},{2,18},{18,2},{3,19},{19,3},{4,20},{20... | collective-permute-start | bytes 36872 | tf_op jit(solution)/shard_map/ppermute | solution.py:26
  8.9 10.5 %collective-permute-start.5 = (f32[8,384]{1,0:T(8,128)S(1)}, f32[8,384]{1,0:T(8,128)S(1)}, u32[]{:S(2)}, u32[]{:S(2)}) collective-permute-start(f32[8,384]{1,0:T(8,128)S(1)} %maximum_maximum_fusion.refs_2_.refs_4_), channel_id=1, source_target_pairs={{0,12},{4,8},{8,4},{12,0},{1,13},{5,9},{9,5},{13,1},{2,14},{6,10},... | collective-permute-start | bytes 36872 | tf_op jit(solution)/shard_map/ppermute | solution.py:26
  8.9 10.9 %collective-permute-start.4 = (f32[8,384]{1,0:T(8,128)S(1)}, f32[8,384]{1,0:T(8,128)S(1)}, u32[]{:S(2)}, u32[]{:S(2)}) collective-permute-start(f32[8,384]{1,0:T(8,128)S(1)} %maximum_maximum_fusion.refs_2_.refs_4_), channel_id=1, source_target_pairs={{0,8},{4,12},{8,0},{12,4},{1,9},{5,13},{9,1},{13,5},{2,10},{6,14},... | collective-permute-start | bytes 36872 | tf_op jit(solution)/shard_map/ppermute | solution.py:26
  9.8 1.8 %collective-permute-start.3 = (f32[8,384]{1,0:T(8,128)S(1)}, f32[8,384]{1,0:T(8,128)S(1)}, u32[]{:S(2)}, u32[]{:S(2)}) collective-permute-start(f32[8,384]{1,0:T(8,128)S(1)} %maximum_maximum_fusion.refs_2_.refs_4_), channel_id=1, source_target_pairs={{0,4},{4,0},{8,12},{12,8},{1,5},{5,1},{9,13},{13,9},{2,6},{6,2},{1... | collective-permute-start | bytes 36872 | tf_op jit(solution)/shard_map/ppermute | solution.py:26
  15.1 6.9 %copy-start.7 = (bf16[320,1024]{1,0:T(8,128)(2,1)}, bf16[320,1024]{1,0:T(8,128)(2,1)S(1)}, u32[]{:S(2)}) copy-start(bf16[320,1024]{1,0:T(8,128)(2,1)S(1)} %collective-permute-done.1.refs_1_.refs_2_) | copy-start | bytes 1966084
  15.1 6.9 %copy-start.1 = (bf16[5,1280,384]{2,1,0:T(8,128)(2,1)S(1)}, bf16[5,1280,384]{2,1,0:T(8,128)(2,1)}, u32[]{:S(2)}) copy-start(bf16[5,1280,384]{2,1,0:T(8,128)(2,1)} %refs_8_.2) | copy-start | bytes 14745604
  15.1 6.9 %copy-start.6 = (bf16[1,1024,320]{1,2,0:T(8,128)(2,1)S(1)}, bf16[1,1024,320]{1,2,0:T(8,128)(2,1)}, u32[]{:S(2)}) copy-start(bf16[1,1024,320]{1,2,0:T(8,128)(2,1)} %param.5) | copy-start | bytes 1966084
  19.8 2.1 %collective-permute-start.6 = (bf16[320,1024]{1,0:T(8,128)(2,1)S(1)}, bf16[320,1024]{1,0:T(8,128)(2,1)S(1)}, u32[]{:S(2)}, u32[]{:S(2)}) collective-permute-start(bf16[320,1024]{1,0:T(8,128)(2,1)S(1)} %collective-permute-done.refs_1_), channel_id=1, source_target_pairs={{0,4},{4,0},{8,12},{12,8},{1,5},{5,1},{9,13},{13,9},{2,6},{6,2},{1... | collective-permute-start | bytes 1966088 | tf_op jit(solution)/shard_map/ppermute | solution.py:26
  30.3 4.8 %copy-start.19 = (bf16[512,384]{1,0:T(8,128)(2,1)}, bf16[512,384]{1,0:T(8,128)(2,1)S(1)}, u32[]{:S(2)}) copy-start(bf16[512,384]{1,0:T(8,128)(2,1)S(1)} %get-tuple-element.113.refs_0_) | copy-start | bytes 1179652
  30.3 8.1 %collective-permute-start.7 = (bf16[320,384]{1,0:T(8,128)(2,1)S(1)}, bf16[320,384]{1,0:T(8,128)(2,1)S(1)}, u32[]{:S(2)}, u32[]{:S(2)}) collective-permute-start(bf16[320,384]{1,0:T(8,128)(2,1)S(1)} %get-tuple-element.67), channel_id=1, source_target_pairs={{0,16},{16,0},{1,17},{17,1},{2,18},{18,2},{3,19},{19,3},{4,20},{20... | collective-permute-start | bytes 737288 | tf_op jit(solution)/shard_map/ppermute | solution.py:26
  36.3 13.3 %collective-permute-start.9 = (bf16[320,384]{1,0:T(8,128)(2,1)}, bf16[320,384]{1,0:T(8,128)(2,1)}, u32[]{:S(2)}, u32[]{:S(2)}) collective-permute-start(bf16[320,384]{1,0:T(8,128)(2,1)} %get-tuple-element.68), channel_id=1, source_target_pairs={{0,16},{16,0},{1,17},{17,1},{2,18},{18,2},{3,19},{19,3},{4,20},{20... | collective-permute-start | bytes 737288 | tf_op jit(solution)/shard_map/ppermute | solution.py:26
  39.2 11.9 %collective-permute-start.8 = (bf16[320,384]{1,0:T(8,128)(2,1)}, bf16[320,384]{1,0:T(8,128)(2,1)}, u32[]{:S(2)}, u32[]{:S(2)}) collective-permute-start(bf16[320,384]{1,0:T(8,128)(2,1)} %add_convert_fusion.29), channel_id=1, source_target_pairs={{0,1},{1,0},{2,3},{3,2},{4,5},{5,4},{6,7},{7,6},{8,9},{9,8},{10,11... | collective-permute-start | bytes 737288 | tf_op jit(solution)/shard_map/ppermute | solution.py:290
  40.9 13.3 %collective-permute-start.10 = (bf16[512,384]{1,0:T(8,128)(2,1)}, bf16[512,384]{1,0:T(8,128)(2,1)S(1)}, u32[]{:S(2)}, u32[]{:S(2)}) collective-permute-start(bf16[512,384]{1,0:T(8,128)(2,1)} %copy-done.19), channel_id=1, source_target_pairs={{0,8},{4,12},{8,0},{12,4},{1,9},{5,13},{9,1},{13,5},{2,10},{6,14},... | collective-permute-start | bytes 1179656 | tf_op jit(solution)/shard_map/ppermute | solution.py:26
  47.4 10.8 %collective-permute-start.11 = (bf16[320,384]{1,0:T(8,128)(2,1)S(1)}, bf16[320,384]{1,0:T(8,128)(2,1)S(1)}, u32[]{:S(2)}, u32[]{:S(2)}) collective-permute-start(bf16[320,384]{1,0:T(8,128)(2,1)S(1)} %get-tuple-element.77), channel_id=1, source_target_pairs={{0,16},{16,0},{1,17},{17,1},{2,18},{18,2},{3,19},{19,3},{4,20},{20... | collective-permute-start | bytes 737288 | tf_op jit(solution)/shard_map/ppermute | solution.py:26
  49.5 14.3 %collective-permute-start.17 = (bf16[320,384]{1,0:T(8,128)(2,1)S(1)}, bf16[320,384]{1,0:T(8,128)(2,1)S(1)}, u32[]{:S(2)}, u32[]{:S(2)}) collective-permute-start(bf16[320,384]{1,0:T(8,128)(2,1)S(1)} %get-tuple-element.85), channel_id=1, source_target_pairs={{0,16},{16,0},{1,17},{17,1},{2,18},{18,2},{3,19},{19,3},{4,20},{20... | collective-permute-start | bytes 737288 | tf_op jit(solution)/shard_map/ppermute | solution.py:26
  50.6 12.2 %collective-permute-start.14 = (bf16[320,384]{1,0:T(8,128)(2,1)S(1)}, bf16[320,384]{1,0:T(8,128)(2,1)S(1)}, u32[]{:S(2)}, u32[]{:S(2)}) collective-permute-start(bf16[320,384]{1,0:T(8,128)(2,1)S(1)} %add_convert_fusion.28), channel_id=1, source_target_pairs={{0,1},{1,0},{2,3},{3,2},{4,5},{5,4},{6,7},{7,6},{8,9},{9,8},{10,11... | collective-permute-start | bytes 737288 | tf_op jit(solution)/shard_map/ppermute | solution.py:290
  51.1 21.1 %collective-permute-start.13 = (bf16[640,384]{1,0:T(8,128)(2,1)S(1)}, bf16[640,384]{1,0:T(8,128)(2,1)S(1)}, u32[]{:S(2)}, u32[]{:S(2)}) collective-permute-start(bf16[640,384]{1,0:T(8,128)(2,1)S(1)} %get-tuple-element.83), channel_id=1, source_target_pairs={{0,16},{16,0},{1,17},{17,1},{2,18},{18,2},{3,19},{19,3},{4,20},{20... | collective-permute-start | bytes 1474568 | tf_op jit(solution)/shard_map/ppermute | solution.py:26
  54.2 9.3 %collective-permute-start.18 = (bf16[320,384]{1,0:T(8,128)(2,1)S(1)}, bf16[320,384]{1,0:T(8,128)(2,1)S(1)}, u32[]{:S(2)}, u32[]{:S(2)}) collective-permute-start(bf16[320,384]{1,0:T(8,128)(2,1)S(1)} %add_convert_fusion.27), channel_id=1, source_target_pairs={{1,2},{2,1},{5,6},{6,5},{9,10},{10,9},{13,14},{14,13},{17,18},{18,... | collective-permute-start | bytes 737288 | tf_op jit(solution)/shard_map/ppermute | solution.py:296
  58.3 10.2 %collective-permute-start.16 = (bf16[320,384]{1,0:T(8,128)(2,1)S(1)}, bf16[320,384]{1,0:T(8,128)(2,1)S(1)}, u32[]{:S(2)}, u32[]{:S(2)}) collective-permute-start(bf16[320,384]{1,0:T(8,128)(2,1)S(1)} %add_convert_fusion.26), channel_id=1, source_target_pairs={{0,1},{1,0},{2,3},{3,2},{4,5},{5,4},{6,7},{7,6},{8,9},{9,8},{10,11... | collective-permute-start | bytes 737288 | tf_op jit(solution)/shard_map/ppermute | solution.py:290
  62.9 6.4 %collective-permute-start.15 = (bf16[320,384]{1,0:T(8,128)(2,1)S(1)}, bf16[320,384]{1,0:T(8,128)(2,1)S(1)}, u32[]{:S(2)}, u32[]{:S(2)}) collective-permute-start(bf16[320,384]{1,0:T(8,128)(2,1)S(1)} %add_convert_fusion.25), channel_id=1, source_target_pairs={{1,2},{2,1},{5,6},{6,5},{9,10},{10,9},{13,14},{14,13},{17,18},{18,... | collective-permute-start | bytes 737288 | tf_op jit(solution)/shard_map/ppermute | solution.py:296
  63.6 19.4 %collective-permute-start.12 = (bf16[640,384]{1,0:T(8,128)(2,1)S(1)}, bf16[640,384]{1,0:T(8,128)(2,1)S(1)}, u32[]{:S(2)}, u32[]{:S(2)}) collective-permute-start(bf16[640,384]{1,0:T(8,128)(2,1)S(1)} %get-tuple-element.80), channel_id=1, source_target_pairs={{0,16},{16,0},{1,17},{17,1},{2,18},{18,2},{3,19},{19,3},{4,20},{20... | collective-permute-start | bytes 1474568 | tf_op jit(solution)/shard_map/ppermute | solution.py:26
  63.9 10.2 %collective-permute-start.21 = (bf16[320,384]{1,0:T(8,128)(2,1)S(1)}, bf16[320,384]{1,0:T(8,128)(2,1)S(1)}, u32[]{:S(2)}, u32[]{:S(2)}) collective-permute-start(bf16[320,384]{1,0:T(8,128)(2,1)S(1)} %broadcast_select_fusion.6), channel_id=1, source_target_pairs={{0,1},{1,0},{2,3},{3,2},{4,5},{5,4},{6,7},{7,6},{8,9},{9,8},{10,11... | collective-permute-start | bytes 737288 | tf_op jit(solution)/shard_map/ppermute | solution.py:290
  68.5 6.4 %collective-permute-start.20 = (bf16[320,384]{1,0:T(8,128)(2,1)S(1)}, bf16[320,384]{1,0:T(8,128)(2,1)S(1)}, u32[]{:S(2)}, u32[]{:S(2)}) collective-permute-start(bf16[320,384]{1,0:T(8,128)(2,1)S(1)} %add_convert_fusion.22), channel_id=1, source_target_pairs={{1,2},{2,1},{5,6},{6,5},{9,10},{10,9},{13,14},{14,13},{17,18},{18,... | collective-permute-start | bytes 737288 | tf_op jit(solution)/shard_map/ppermute | solution.py:296
  72.3 7.7 %collective-permute-start.19 = (bf16[320,384]{1,0:T(8,128)(2,1)S(1)}, bf16[320,384]{1,0:T(8,128)(2,1)S(1)}, u32[]{:S(2)}, u32[]{:S(2)}) collective-permute-start(bf16[320,384]{1,0:T(8,128)(2,1)S(1)} %broadcast_select_fusion.5), channel_id=1, source_target_pairs={{0,1},{1,0},{2,3},{3,2},{4,5},{5,4},{6,7},{7,6},{8,9},{9,8},{10,11... | collective-permute-start | bytes 737288 | tf_op jit(solution)/shard_map/ppermute | solution.py:290
  74.2 18.5 %copy-start.20 = (bf16[512,384]{1,0:T(8,128)(2,1)S(1)}, bf16[512,384]{1,0:T(8,128)(2,1)}, u32[]{:S(2)}) copy-start(bf16[512,384]{1,0:T(8,128)(2,1)} %copy-done.19) | copy-start | bytes 1179652
  74.2 8.8 %collective-permute-start.24 = (bf16[320,384]{1,0:T(8,128)(2,1)S(1)}, bf16[320,384]{1,0:T(8,128)(2,1)S(1)}, u32[]{:S(2)}, u32[]{:S(2)}) collective-permute-start(bf16[320,384]{1,0:T(8,128)(2,1)S(1)} %add_convert_fusion.19), channel_id=1, source_target_pairs={{1,2},{2,1},{5,6},{6,5},{9,10},{10,9},{13,14},{14,13},{17,18},{18,... | collective-permute-start | bytes 737288 | tf_op jit(solution)/shard_map/ppermute | solution.py:296
  75.2 11.2 %collective-permute-start.23 = (bf16[320,384]{1,0:T(8,128)(2,1)S(1)}, bf16[320,384]{1,0:T(8,128)(2,1)S(1)}, u32[]{:S(2)}, u32[]{:S(2)}) collective-permute-start(bf16[320,384]{1,0:T(8,128)(2,1)S(1)} %broadcast_select_fusion.4), channel_id=1, source_target_pairs={{0,1},{1,0},{2,3},{3,2},{4,5},{5,4},{6,7},{7,6},{8,9},{9,8},{10,11... | collective-permute-start | bytes 737288 | tf_op jit(solution)/shard_map/ppermute | solution.py:290
  80.2 7.0 %collective-permute-start.22 = (bf16[320,384]{1,0:T(8,128)(2,1)S(1)}, bf16[320,384]{1,0:T(8,128)(2,1)S(1)}, u32[]{:S(2)}, u32[]{:S(2)}) collective-permute-start(bf16[320,384]{1,0:T(8,128)(2,1)S(1)} %add_convert_fusion.16), channel_id=1, source_target_pairs={{1,2},{2,1},{5,6},{6,5},{9,10},{10,9},{13,14},{14,13},{17,18},{18,... | collective-permute-start | bytes 737288 | tf_op jit(solution)/shard_map/ppermute | solution.py:296
  80.9 12.4 %collective-permute-start.26 = (bf16[640,384]{1,0:T(8,128)(2,1)S(1)}, bf16[640,384]{1,0:T(8,128)(2,1)S(1)}, u32[]{:S(2)}, u32[]{:S(2)}) collective-permute-start(bf16[640,384]{1,0:T(8,128)(2,1)S(1)} %get-tuple-element.101), channel_id=1, source_target_pairs={{0,16},{16,0},{1,17},{17,1},{2,18},{18,2},{3,19},{19,3},{4,20},{20... | collective-permute-start | bytes 1474568 | tf_op jit(solution)/shard_map/ppermute | solution.py:26
  83.2 8.6 %collective-permute-start.28 = (bf16[320,384]{1,0:T(8,128)(2,1)S(1)}, bf16[320,384]{1,0:T(8,128)(2,1)S(1)}, u32[]{:S(2)}, u32[]{:S(2)}) collective-permute-start(bf16[320,384]{1,0:T(8,128)(2,1)S(1)} %broadcast_select_fusion.3), channel_id=1, source_target_pairs={{0,1},{1,0},{2,3},{3,2},{4,5},{5,4},{6,7},{7,6},{8,9},{9,8},{10,11... | collective-permute-start | bytes 737288 | tf_op jit(solution)/shard_map/ppermute | solution.py:290
  86.5 6.1 %collective-permute-start.27 = (bf16[320,384]{1,0:T(8,128)(2,1)S(1)}, bf16[320,384]{1,0:T(8,128)(2,1)S(1)}, u32[]{:S(2)}, u32[]{:S(2)}) collective-permute-start(bf16[320,384]{1,0:T(8,128)(2,1)S(1)} %add_convert_fusion.13), channel_id=1, source_target_pairs={{1,2},{2,1},{5,6},{6,5},{9,10},{10,9},{13,14},{14,13},{17,18},{18,... | collective-permute-start | bytes 737288 | tf_op jit(solution)/shard_map/ppermute | solution.py:296
  87.3 28.0 %copy-start.9 = (bf16[1536,640]{1,0:T(8,128)(2,1)S(1)}, bf16[1536,640]{1,0:T(8,128)(2,1)}, u32[]{:S(2)}) copy-start(bf16[1536,640]{1,0:T(8,128)(2,1)} %refs_8_.3) | copy-start | bytes 5898244
  87.3 10.8 %collective-permute-start.25 = (bf16[320,384]{1,0:T(8,128)(2,1)S(1)}, bf16[320,384]{1,0:T(8,128)(2,1)S(1)}, u32[]{:S(2)}, u32[]{:S(2)}) collective-permute-start(bf16[320,384]{1,0:T(8,128)(2,1)S(1)} %broadcast_select_fusion.2), channel_id=1, source_target_pairs={{0,1},{1,0},{2,3},{3,2},{4,5},{5,4},{6,7},{7,6},{8,9},{9,8},{10,11... | collective-permute-start | bytes 737288 | tf_op jit(solution)/shard_map/ppermute | solution.py:290
  91.9 7.0 %collective-permute-start.31 = (bf16[320,384]{1,0:T(8,128)(2,1)S(1)}, bf16[320,384]{1,0:T(8,128)(2,1)S(1)}, u32[]{:S(2)}, u32[]{:S(2)}) collective-permute-start(bf16[320,384]{1,0:T(8,128)(2,1)S(1)} %add_convert_fusion.10), channel_id=1, source_target_pairs={{1,2},{2,1},{5,6},{6,5},{9,10},{10,9},{13,14},{14,13},{17,18},{18,... | collective-permute-start | bytes 737288 | tf_op jit(solution)/shard_map/ppermute | solution.py:296
  92.7 22.6 %collective-permute-start.35 = (bf16[512,384]{1,0:T(8,128)(2,1)S(1)}, bf16[512,384]{1,0:T(8,128)(2,1)S(1)}, u32[]{:S(2)}, u32[]{:S(2)}) collective-permute-start(bf16[512,384]{1,0:T(8,128)(2,1)S(1)} %copy-done.20), channel_id=1, source_target_pairs={{0,4},{4,0},{8,12},{12,8},{1,5},{5,1},{9,13},{13,9},{2,6},{6,2},{1... | collective-permute-start | bytes 1179656 | tf_op jit(solution)/shard_map/ppermute | solution.py:26
  92.7 22.6 %collective-permute-start.36 = (bf16[512,384]{1,0:T(8,128)(2,1)S(1)}, bf16[512,384]{1,0:T(8,128)(2,1)S(1)}, u32[]{:S(2)}, u32[]{:S(2)}) collective-permute-start(bf16[512,384]{1,0:T(8,128)(2,1)S(1)} %collective-permute-done.10.refs_1_), channel_id=1, source_target_pairs={{0,4},{4,0},{8,12},{12,8},{1,5},{5,1},{9,13},{13,9},{2,6},{6,2},{1... | collective-permute-start | bytes 1179656 | tf_op jit(solution)/shard_map/ppermute | solution.py:26
  93.4 11.5 %collective-permute-start.30 = (bf16[320,384]{1,0:T(8,128)(2,1)S(1)}, bf16[320,384]{1,0:T(8,128)(2,1)S(1)}, u32[]{:S(2)}, u32[]{:S(2)}) collective-permute-start(bf16[320,384]{1,0:T(8,128)(2,1)S(1)} %broadcast_select_fusion.1), channel_id=1, source_target_pairs={{0,1},{1,0},{2,3},{3,2},{4,5},{5,4},{6,7},{7,6},{8,9},{9,8},{10,11... | collective-permute-start | bytes 737288 | tf_op jit(solution)/shard_map/ppermute | solution.py:290
  98.2 7.4 %collective-permute-start.29 = (bf16[320,384]{1,0:T(8,128)(2,1)S(1)}, bf16[320,384]{1,0:T(8,128)(2,1)S(1)}, u32[]{:S(2)}, u32[]{:S(2)}) collective-permute-start(bf16[320,384]{1,0:T(8,128)(2,1)S(1)} %add_convert_fusion.7), channel_id=1, source_target_pairs={{1,2},{2,1},{5,6},{6,5},{9,10},{10,9},{13,14},{14,13},{17,18},{18,... | collective-permute-start | bytes 737288 | tf_op jit(solution)/shard_map/ppermute | solution.py:296
  99.1 11.1 %collective-permute-start.34 = (bf16[320,384]{1,0:T(8,128)(2,1)S(1)}, bf16[320,384]{1,0:T(8,128)(2,1)S(1)}, u32[]{:S(2)}, u32[]{:S(2)}) collective-permute-start(bf16[320,384]{1,0:T(8,128)(2,1)S(1)} %broadcast_select_fusion), channel_id=1, source_target_pairs={{0,1},{1,0},{2,3},{3,2},{4,5},{5,4},{6,7},{7,6},{8,9},{9,8},{10,11... | collective-permute-start | bytes 737288 | tf_op jit(solution)/shard_map/ppermute | solution.py:290
  105.0 6.0 %collective-permute-start.33 = (bf16[320,384]{1,0:T(8,128)(2,1)S(1)}, bf16[320,384]{1,0:T(8,128)(2,1)S(1)}, u32[]{:S(2)}, u32[]{:S(2)}) collective-permute-start(bf16[320,384]{1,0:T(8,128)(2,1)S(1)} %add_convert_fusion.4), channel_id=1, source_target_pairs={{1,2},{2,1},{5,6},{6,5},{9,10},{10,9},{13,14},{14,13},{17,18},{18,... | collective-permute-start | bytes 737288 | tf_op jit(solution)/shard_map/ppermute | solution.py:296
  105.7 9.5 %collective-permute-start.32 = (bf16[320,384]{1,0:T(8,128)(2,1)S(1)}, bf16[320,384]{1,0:T(8,128)(2,1)S(1)}, u32[]{:S(2)}, u32[]{:S(2)}) collective-permute-start(bf16[320,384]{1,0:T(8,128)(2,1)S(1)} %add_convert_fusion.3.refs_15_), channel_id=1, source_target_pairs={{0,1},{1,0},{2,3},{3,2},{4,5},{5,4},{6,7},{7,6},{8,9},{9,8},{10,11... | collective-permute-start | bytes 737288 | tf_op jit(solution)/shard_map/ppermute | solution.py:290
  110.3 8.6 %collective-permute-start.37 = (bf16[320,384]{1,0:T(8,128)(2,1)S(1)}, bf16[320,384]{1,0:T(8,128)(2,1)S(1)}, u32[]{:S(2)}, u32[]{:S(2)}) collective-permute-start(bf16[320,384]{1,0:T(8,128)(2,1)S(1)} %add_convert_fusion.2), channel_id=1, source_target_pairs={{1,2},{2,1},{5,6},{6,5},{9,10},{10,9},{13,14},{14,13},{17,18},{18,... | collective-permute-start | bytes 737288 | tf_op jit(solution)/shard_map/ppermute | solution.py:296
  111.1 15.7 %collective-permute-start.38 = (bf16[320,384]{1,0:T(8,128)(2,1)S(1)}, bf16[320,384]{1,0:T(8,128)(2,1)}, u32[]{:S(2)}, u32[]{:S(2)}) collective-permute-start(bf16[320,384]{1,0:T(8,128)(2,1)S(1)} %add_convert_fusion.1.refs_1_), channel_id=1, source_target_pairs={{0,1},{1,0},{2,3},{3,2},{4,5},{5,4},{6,7},{7,6},{8,9},{9,8},{10,11... | collective-permute-start | bytes 737288 | tf_op jit(solution)/shard_map/ppermute | solution.py:290
  115.3 3.6 %copy-start.21 = (bf16[320,384]{1,0:T(8,128)(2,1)}, bf16[320,384]{1,0:T(8,128)(2,1)S(1)}, u32[]{:S(2)}) copy-start(bf16[320,384]{1,0:T(8,128)(2,1)S(1)} %collective-permute-done.32.refs_14_) | copy-start | bytes 737284
  118.9 7.8 %collective-permute-start.39 = (bf16[320,384]{1,0:T(8,128)(2,1)S(1)}, bf16[320,384]{1,0:T(8,128)(2,1)}, u32[]{:S(2)}, u32[]{:S(2)}) collective-permute-start(bf16[320,384]{1,0:T(8,128)(2,1)S(1)} %add_convert_fusion.refs_3_), channel_id=1, source_target_pairs={{0,1},{1,0},{2,3},{3,2},{4,5},{5,4},{6,7},{7,6},{8,9},{9,8},{10,11... | collective-permute-start | bytes 737288 | tf_op jit(solution)/shard_map/ppermute | solution.py:290
  (15 other events, 16.3 us)

commit v11 on v10

--- a/solution.py
+++ b/solution.py
@@ -382,7 +382,7 @@
             functools.partial(grad_kernel, group, depth, per, pieces),
             tuple(o for tap in outs for o in tap),
             [pltpu.VMEM((LANES, width * min(len(group), 2)), F32)],
-            24 if len(group) > 2 else 16,
+            18,
             after(idx, *hold) if hold else idx, joined, pre_grad,
         )
         flat = list(flat)
@@ -417,16 +417,16 @@
         if tap < taps:
             got[tap] = [swap(after(v, *hold) if hold else v, "seq", 1) for v in send[tap]]
 
-    work((0,), [])
+    work(tuple(range(min(3, taps))), [])
     launch(0, [])
-    work(tuple(range(1, min(3, taps))), [keep[-1]])
     launch(1, [])
 
     def share(c, last):
         tap, row = c // per, c % per
         rows = slice(row * depth, (row + 1) * depth)
         value = got[tap][row] if len(got[tap]) > 1 else got[tap][0][rows]
-        return added(keep[tap][rows], value if last is None else after(value, last))
+        hold = ([] if last is None else [last]) + (encs[1:] if c == 2 else [])
+        return added(keep[tap][rows], after(value, *hold) if hold else value)
 
     starts = {(k - 1) * per - 1 - (k == 3): k for k in range(2, taps)}
 
@@ -446,7 +446,7 @@
             held = encs[1:]
             relays.extend([swap(after(e, last, *held), "mp", bits[-1]) for e in encs])
         if c == 0:
-            work(tuple(range(3, taps)), [last] + encs[1:])
+            work(tuple(range(3, taps)), [last])
             last = keep[-1]
         if c == chunks:
             last = done["qkv"] = qkv_call(after(idx, last, *relays), encs + relays)

time: 130 us -> 132 us (1.015)
  starting transfers between devices: 64.4 us -> 69.1 us
  waiting for transfers between devices: 14.7 us -> 10.8 us
  local copies, waits for them, and re-layouts: 14.9 us -> 17.1 us
  Pallas kernels: 28.4 us -> 26.8 us
    ppermute x13, starting transfers between devices: 40.5 us -> 45.8 us  [chain_sums(): outer[r] = lax.ppermute(value, 'dp', outer_pairs)]
    ppermute x17, waiting for transfers between devices: 8.64 us -> 5.23 us  [swap(): return lax.ppermute(value, axis, [(i, i ^ bit) for i in range(peers)])]
    unnamed x46 -> x64, local copies, waits for them, and re-layouts: 14 us -> 16.1 us
    pallas_call x6 -> x5, Pallas kernels: 23.9 us -> 22.3 us  [call(): pl.pallas_call(kernel, out_shape=out, in_specs=[pl.BlockSpec(memory_space...]
  transfers between devices with their start and end apart: 40 -> 40, of which waited for: 9 -> 8; matrix products, arithmetic and copies ran while one was open for 5% -> 6% of each run, Pallas kernels for 16% -> 14%
where the time goes in v11:
time: 132 us; the launch traced here: 131 us
  starting transfers between devices  69.1 us (52%)
  Pallas kernels  26.8 us (20%)
  local copies, waits for them, and re-layouts  17.1 us (13%)
  waiting for transfers between devices  10.8 us (8%)
  other arithmetic  6.32 us (5%)
  between operations  1.42 us (1%)
    ppermute x13, starting transfers between devices, chain_sums(): outer[r] = lax.ppermute(value, 'dp', outer_pairs)  45.8 us
    pallas_call x5, Pallas kernels, call(): pl.pallas_call(kernel, out_shape=out, in_specs=[pl.BlockSpec(memory_space...  22.3 us
    ppermute x17, starting transfers between devices, swap(): return lax.ppermute(value, axis, [(i, i ^ bit) for i in range(peers)])  16.3 us
    unnamed x64, local copies, waits for them, and re-layouts  16.1 us
    ppermute x10, starting transfers between devices, chain_sums(): middle[r - 1] = lax.ppermute(last, 'dp', middle_pairs)  7.03 us
    convert_element_type x23, other arithmetic, added(): return (a.astype(F32) + b.astype(F32)).astype(BF16)  5.5 us
    ppermute x13, waiting for transfers between devices, chain_sums(): outer[r] = lax.ppermute(value, 'dp', outer_pairs)  5.49 us
    ppermute x17, waiting for transfers between devices, swap(): return lax.ppermute(value, axis, [(i, i ^ bit) for i in range(peers)])  5.23 us
  transfers between devices with their start and end apart: 40, of which 8 were waited for; matrix products, arithmetic and copies ran while one was open for 6% of the time, Pallas kernels for 14%

profile of v11, /device:TPU:0, one launch (start us, length us, event | category | flops | bytes accessed | tf_op | source)
XLA Modules:
  0.0 131.5 jit_solution(8573014377776467824)
XLA Ops:
  1.1 2.6 %collective-permute-start = (bf16[320,1024]{1,0:T(8,128)(2,1)}, bf16[320,1024]{1,0:T(8,128)(2,1)S(1)}, u32[]{:S(2)}, u32[]{:S(2)}) collective-permute-start(bf16[320,1024]{1,0:T(8,128)(2,1)} %bitcast.10), channel_id=1, source_target_pairs={{0,8},{4,12},{8,0},{12,4},{1,9},{5,13},{9,1},{13,5},{2,10},{6,14},... | collective-permute-start | bytes 1966088 | tf_op jit(solution)/shard_map/ppermute | solution.py:26
  3.7 1.1 copy-done.2
  5.0 1.6 %collective-permute-start.2 = (f32[8,384]{1,0:T(8,128)S(1)}, f32[8,384]{1,0:T(8,128)S(1)}, u32[]{:S(2)}, u32[]{:S(2)}) collective-permute-start(f32[8,384]{1,0:T(8,128)S(1)} %shard_map.68), channel_id=1, source_target_pairs={{0,16},{16,0},{1,17},{17,1},{2,18},{18,2},{3,19},{19,3},{4,20},{20... | collective-permute-start | bytes 36872 | tf_op jit(solution)/shard_map/ppermute | solution.py:26
  7.3 1.4 %collective-permute-done.2 = f32[8,384]{1,0:T(8,128)S(1)} collective-permute-done((f32[8,384]{1,0:T(8,128)S(1)}, f32[8,384]{1,0:T(8,128)S(1)}, u32[]{:S(2)}, u32[]{:S(2)}) %collective-permute-start.2) | collective-permute-done | bytes 12320 | tf_op jit(solution)/shard_map/ppermute | solution.py:26
  8.9 0.9 collective-permute-start.4
  9.8 0.9 collective-permute-start.3
  11.6 2.4 %copy-done = bf16[5,1280,384]{2,1,0:T(8,128)(2,1)S(1)} copy-done((bf16[5,1280,384]{2,1,0:T(8,128)(2,1)S(1)}, bf16[5,1280,384]{2,1,0:T(8,128)(2,1)}, u32[]{:S(2)}) %copy-start) | copy-done | bytes 4915224
  14.0 1.1 copy-done.3
  15.1 4.3 %shard_map.69 = (f32[512,384]{1,0:T(8,128)S(1)}, f32[512,384]{1,0:T(8,128)S(1)}) custom-call(s32[2]{0:T(128)S(1)} %pad_add_fusion.idx_ref, bf16[320,1024]{1,0:T(8,128)(2,1)S(1)} %bitcast.13, bf16[320,1024]{1,0:T(8,128)(2,1)S(1)} %collective-permute-done.1.refs_1_.refs_2_, f32[8,384]{1,0:T(8,128)S(1)} %maximum_maximum_fusion.refs_2_.refs_4_, ...), custom_call_target="tpu_custom_call" | custom-call | tf_op jit(solution)/shard_map/pallas_call | solution.py:187
  20.6 1.3 collective-permute-done.6.refs_3_
  21.9 1.1 copy-done.8
  23.0 1.1 copy-done.23
  24.1 6.2 %shard_map.70 = (bf16[512,384]{1,0:T(8,128)(2,1)S(1)}, f32[1040,384]{1,0:T(8,128)S(1)}, bf16[1280,1152]{1,0:T(8,128)(2,1)S(1)}, bf16[320,384]{1,0:T(8,128)(2,1)S(1)}) custom-call(s32[2]{0:T(128)S(1)} %pad_add_fusion.idx_ref, bf16[320,1024]{1,0:T(8,128)(2,1)S(1)} %bitcast.14, bf16[320,1024]{1,0:T(8,128)(2,1)S(1)} %copy-done.23, ...), custom_call_target="tpu_custom_call" | custom-call | tf_op jit(solution)/shard_map/pallas_call | solution.py:187
  30.3 1.8 %collective-permute-start.7 = (bf16[320,384]{1,0:T(8,128)(2,1)S(1)}, bf16[320,384]{1,0:T(8,128)(2,1)S(1)}, u32[]{:S(2)}, u32[]{:S(2)}) collective-permute-start(bf16[320,384]{1,0:T(8,128)(2,1)S(1)} %get-tuple-element.66), channel_id=1, source_target_pairs={{0,16},{16,0},{1,17},{17,1},{2,18},{18,2},{3,19},{19,3},{4,20},{20... | collective-permute-start | bytes 737288 | tf_op jit(solution)/shard_map/ppermute | solution.py:26
  32.1 4.9 %shard_map.71 = (bf16[640,384]{1,0:T(8,128)(2,1)}, bf16[320,384]{1,0:T(8,128)(2,1)}, bf16[640,384]{1,0:T(8,128)(2,1)S(1)}, bf16[320,384]{1,0:T(8,128)(2,1)S(1)},...) custom-call(s32[2]{0:T(128)S(1)} %pad_add_fusion.idx_ref, ...), custom_call_target="tpu_custom_call" | custom-call | tf_op jit(solution)/shard_map/pallas_call | solution.py:187
  37.3 1.0 copy-done.5
  40.8 1.7 %add_convert_fusion.29 = bf16[320,384]{1,0:T(8,128)(2,1)} fusion(bf16[320,384]{1,0:T(8,128)(2,1)S(1)} %collective-permute-done.7, bf16[640,384]{1,0:T(8,128)(2,1)} %get-tuple-element.65), kind=kLoop, calls=%fused_computation.29 | loop fusion | flops 491520 | bytes 737280 | tf_op jit(solution)/shard_map/convert_element_type | solution.py:272
  42.6 1.8 %collective-permute-start.8 = (bf16[320,384]{1,0:T(8,128)(2,1)}, bf16[320,384]{1,0:T(8,128)(2,1)}, u32[]{:S(2)}, u32[]{:S(2)}) collective-permute-start(bf16[320,384]{1,0:T(8,128)(2,1)} %add_convert_fusion.29), channel_id=1, source_target_pairs={{0,1},{1,0},{2,3},{3,2},{4,5},{5,4},{6,7},{7,6},{8,9},{9,8},{10,11... | collective-permute-start | bytes 737288 | tf_op jit(solution)/shard_map/ppermute | solution.py:290
  44.4 1.5 %collective-permute-start.11 = (bf16[512,384]{1,0:T(8,128)(2,1)}, bf16[512,384]{1,0:T(8,128)(2,1)S(1)}, u32[]{:S(2)}, u32[]{:S(2)}) collective-permute-start(bf16[512,384]{1,0:T(8,128)(2,1)} %copy-done.25), channel_id=1, source_target_pairs={{0,8},{4,12},{8,0},{12,4},{1,9},{5,13},{9,1},{13,5},{2,10},{6,14},... | collective-permute-start | bytes 1179656 | tf_op jit(solution)/shard_map/ppermute | solution.py:26
  45.9 1.5 %collective-permute-start.10 = (bf16[320,384]{1,0:T(8,128)(2,1)}, bf16[320,384]{1,0:T(8,128)(2,1)S(1)}, u32[]{:S(2)}, u32[]{:S(2)}) collective-permute-start(bf16[320,384]{1,0:T(8,128)(2,1)} %copy-done.31), channel_id=1, source_target_pairs={{0,16},{16,0},{1,17},{17,1},{2,18},{18,2},{3,19},{19,3},{4,20},{20... | collective-permute-start | bytes 737288 | tf_op jit(solution)/shard_map/ppermute | solution.py:26
  47.9 1.3 collective-permute-done.9
  49.2 1.1 add_convert_fusion.28
  50.4 2.1 %collective-permute-start.14 = (bf16[320,384]{1,0:T(8,128)(2,1)S(1)}, bf16[320,384]{1,0:T(8,128)(2,1)S(1)}, u32[]{:S(2)}, u32[]{:S(2)}) collective-permute-start(bf16[320,384]{1,0:T(8,128)(2,1)S(1)} %add_convert_fusion.28), channel_id=1, source_target_pairs={{0,1},{1,0},{2,3},{3,2},{4,5},{5,4},{6,7},{7,6},{8,9},{9,8},{10,11... | collective-permute-start | bytes 737288 | tf_op jit(solution)/shard_map/ppermute | solution.py:290
  52.7 1.1 add_convert_fusion.27
  53.9 1.4 %copy-done.6 = f32[1040,384]{1,0:T(8,128)S(1)} copy-done((f32[1040,384]{1,0:T(8,128)S(1)}, f32[1040,384]{1,0:T(8,128)}, u32[]{:S(2)}) %copy-start.6) | copy-done | bytes 1597464
  55.3 3.3 %shard_map.72 = (bf16[640,384]{1,0:T(8,128)(2,1)S(1)}, bf16[640,384]{1,0:T(8,128)(2,1)S(1)}, bf16[640,384]{1,0:T(8,128)(2,1)S(1)}, bf16[640,384]{1,0:T(8,128)(2,1)S(1)}) custom-call(s32[2]{0:T(128)S(1)} %pad_add_fusion.idx_ref, bf16[1280,1152]{1,0:T(8,128)(2,1)S(1)} %get-tuple-element.63.all_ref, f32[1040,384]{1,0:T(8,128)S(1)} %copy-done.6), custom_call_target="tpu_custom_call" | custom-call | tf_op jit(solution)/shard_map/pallas_call | solution.py:187
  59.4 4.5 %collective-permute-start.16 = (bf16[320,384]{1,0:T(8,128)(2,1)S(1)}, bf16[320,384]{1,0:T(8,128)(2,1)S(1)}, u32[]{:S(2)}, u32[]{:S(2)}) collective-permute-start(bf16[320,384]{1,0:T(8,128)(2,1)S(1)} %add_convert_fusion.26), channel_id=1, source_target_pairs={{0,1},{1,0},{2,3},{3,2},{4,5},{5,4},{6,7},{7,6},{8,9},{9,8},{10,11... | collective-permute-start | bytes 737288 | tf_op jit(solution)/shard_map/ppermute | solution.py:290
  64.6 1.8 %collective-permute-start.12 = (bf16[640,384]{1,0:T(8,128)(2,1)S(1)}, bf16[640,384]{1,0:T(8,128)(2,1)S(1)}, u32[]{:S(2)}, u32[]{:S(2)}) collective-permute-start(bf16[640,384]{1,0:T(8,128)(2,1)S(1)} %get-tuple-element.78), channel_id=1, source_target_pairs={{0,16},{16,0},{1,17},{17,1},{2,18},{18,2},{3,19},{19,3},{4,20},{20... | collective-permute-start | bytes 1474568 | tf_op jit(solution)/shard_map/ppermute | solution.py:26
  66.6 5.6 %collective-permute-start.21 = (bf16[320,384]{1,0:T(8,128)(2,1)S(1)}, bf16[320,384]{1,0:T(8,128)(2,1)S(1)}, u32[]{:S(2)}, u32[]{:S(2)}) collective-permute-start(bf16[320,384]{1,0:T(8,128)(2,1)S(1)} %broadcast_select_fusion.6), channel_id=1, source_target_pairs={{0,1},{1,0},{2,3},{3,2},{4,5},{5,4},{6,7},{7,6},{8,9},{9,8},{10,11... | collective-permute-start | bytes 737288 | tf_op jit(solution)/shard_map/ppermute | solution.py:290
  73.3 2.5 %collective-permute-start.19 = (bf16[320,384]{1,0:T(8,128)(2,1)S(1)}, bf16[320,384]{1,0:T(8,128)(2,1)S(1)}, u32[]{:S(2)}, u32[]{:S(2)}) collective-permute-start(bf16[320,384]{1,0:T(8,128)(2,1)S(1)} %broadcast_select_fusion.5), channel_id=1, source_target_pairs={{0,1},{1,0},{2,3},{3,2},{4,5},{5,4},{6,7},{7,6},{8,9},{9,8},{10,11... | collective-permute-start | bytes 737288 | tf_op jit(solution)/shard_map/ppermute | solution.py:290
  75.8 2.4 %collective-permute-done.21.refs_0_ = bf16[320,384]{1,0:T(8,128)(2,1)S(1)} collective-permute-done((bf16[320,384]{1,0:T(8,128)(2,1)S(1)}, bf16[320,384]{1,0:T(8,128)(2,1)S(1)}, u32[]{:S(2)}, u32[]{:S(2)}) %collective-permute-start.21) | collective-permute-done | bytes 245792 | tf_op jit(solution)/shard_map/ppermute | solution.py:290
  79.3 4.1 %collective-permute-start.23 = (bf16[320,384]{1,0:T(8,128)(2,1)S(1)}, bf16[320,384]{1,0:T(8,128)(2,1)S(1)}, u32[]{:S(2)}, u32[]{:S(2)}) collective-permute-start(bf16[320,384]{1,0:T(8,128)(2,1)S(1)} %broadcast_select_fusion.4), channel_id=1, source_target_pairs={{0,1},{1,0},{2,3},{3,2},{4,5},{5,4},{6,7},{7,6},{8,9},{9,8},{10,11... | collective-permute-start | bytes 737288 | tf_op jit(solution)/shard_map/ppermute | solution.py:290
  84.1 1.5 %collective-permute-start.26 = (bf16[640,384]{1,0:T(8,128)(2,1)S(1)}, bf16[640,384]{1,0:T(8,128)(2,1)S(1)}, u32[]{:S(2)}, u32[]{:S(2)}) collective-permute-start(bf16[640,384]{1,0:T(8,128)(2,1)S(1)} %get-tuple-element.99), channel_id=1, source_target_pairs={{0,16},{16,0},{1,17},{17,1},{2,18},{18,2},{3,19},{19,3},{4,20},{20... | collective-permute-start | bytes 1474568 | tf_op jit(solution)/shard_map/ppermute | solution.py:26
  85.9 3.2 %collective-permute-start.28 = (bf16[320,384]{1,0:T(8,128)(2,1)S(1)}, bf16[320,384]{1,0:T(8,128)(2,1)S(1)}, u32[]{:S(2)}, u32[]{:S(2)}) collective-permute-start(bf16[320,384]{1,0:T(8,128)(2,1)S(1)} %broadcast_select_fusion.3), channel_id=1, source_target_pairs={{0,1},{1,0},{2,3},{3,2},{4,5},{5,4},{6,7},{7,6},{8,9},{9,8},{10,11... | collective-permute-start | bytes 737288 | tf_op jit(solution)/shard_map/ppermute | solution.py:290
  90.6 4.8 %collective-permute-start.25 = (bf16[320,384]{1,0:T(8,128)(2,1)S(1)}, bf16[320,384]{1,0:T(8,128)(2,1)S(1)}, u32[]{:S(2)}, u32[]{:S(2)}) collective-permute-start(bf16[320,384]{1,0:T(8,128)(2,1)S(1)} %broadcast_select_fusion.2), channel_id=1, source_target_pairs={{0,1},{1,0},{2,3},{3,2},{4,5},{5,4},{6,7},{7,6},{8,9},{9,8},{10,11... | collective-permute-start | bytes 737288 | tf_op jit(solution)/shard_map/ppermute | solution.py:290
  97.1 3.4 %collective-permute-start.30 = (bf16[320,384]{1,0:T(8,128)(2,1)S(1)}, bf16[320,384]{1,0:T(8,128)(2,1)S(1)}, u32[]{:S(2)}, u32[]{:S(2)}) collective-permute-start(bf16[320,384]{1,0:T(8,128)(2,1)S(1)} %broadcast_select_fusion.1), channel_id=1, source_target_pairs={{0,1},{1,0},{2,3},{3,2},{4,5},{5,4},{6,7},{7,6},{8,9},{9,8},{10,11... | collective-permute-start | bytes 737288 | tf_op jit(solution)/shard_map/ppermute | solution.py:290
  101.7 3.1 %collective-permute-start.34 = (bf16[320,384]{1,0:T(8,128)(2,1)S(1)}, bf16[320,384]{1,0:T(8,128)(2,1)S(1)}, u32[]{:S(2)}, u32[]{:S(2)}) collective-permute-start(bf16[320,384]{1,0:T(8,128)(2,1)S(1)} %broadcast_select_fusion), channel_id=1, source_target_pairs={{0,1},{1,0},{2,3},{3,2},{4,5},{5,4},{6,7},{7,6},{8,9},{9,8},{10,11... | collective-permute-start | bytes 737288 | tf_op jit(solution)/shard_map/ppermute | solution.py:290
  104.7 2.6 %collective-permute-done.30.refs_10_ = bf16[320,384]{1,0:T(8,128)(2,1)S(1)} collective-permute-done((bf16[320,384]{1,0:T(8,128)(2,1)S(1)}, bf16[320,384]{1,0:T(8,128)(2,1)S(1)}, u32[]{:S(2)}, u32[]{:S(2)}) %collective-permute-start.30) | collective-permute-done | bytes 245792 | tf_op jit(solution)/shard_map/ppermute | solution.py:290
  108.2 5.1 %collective-permute-start.32 = (bf16[320,384]{1,0:T(8,128)(2,1)S(1)}, bf16[320,384]{1,0:T(8,128)(2,1)S(1)}, u32[]{:S(2)}, u32[]{:S(2)}) collective-permute-start(bf16[320,384]{1,0:T(8,128)(2,1)S(1)} %add_convert_fusion.3.refs_15_), channel_id=1, source_target_pairs={{0,1},{1,0},{2,3},{3,2},{4,5},{5,4},{6,7},{7,6},{8,9},{9,8},{10,11... | collective-permute-start | bytes 737288 | tf_op jit(solution)/shard_map/ppermute | solution.py:290
  114.1 4.4 %collective-permute-start.38 = (bf16[320,384]{1,0:T(8,128)(2,1)S(1)}, bf16[320,384]{1,0:T(8,128)(2,1)}, u32[]{:S(2)}, u32[]{:S(2)}) collective-permute-start(bf16[320,384]{1,0:T(8,128)(2,1)S(1)} %add_convert_fusion.1.refs_1_), channel_id=1, source_target_pairs={{0,1},{1,0},{2,3},{3,2},{4,5},{5,4},{6,7},{7,6},{8,9},{9,8},{10,11... | collective-permute-start | bytes 737288 | tf_op jit(solution)/shard_map/ppermute | solution.py:290
  118.5 3.6 %shard_map.73 = bf16[512,640]{1,0:T(8,128)(2,1)} custom-call(s32[2]{0:T(128)S(1)} %pad_add_fusion.idx_ref, bf16[512,384]{1,0:T(8,128)(2,1)S(1)} %copy-done.26, bf16[512,384]{1,0:T(8,128)(2,1)S(1)} %collective-permute-done.11.refs_1_, bf16[512,384]{1,0:T(8,128)(2,1)S(1)} %collective-permute-done.35.refs_2_, ...), custom_call_target="tpu_custom_call" | custom-call | tf_op jit(solution)/shard_map/pallas_call | solution.py:187
  122.2 1.2 collective-permute-start.39
  123.4 0.9 copy-done.17
  124.3 0.9 copy-done.19
  125.2 0.9 copy-done.21
  126.2 0.9 copy-done.28
  127.1 2.2 %shard_map.74.b = f32[5,640,384]{2,1,0:T(8,128)} custom-call(s32[1]{0:T(128)} %bitcast.7.end_ref.end, bf16[320,384]{1,0:T(8,128)(2,1)S(1)} %collective-permute-done.21.refs_0_, bf16[320,384]{1,0:T(8,128)(2,1)S(1)} %add_convert_fusion.24.refs_1_, bf16[320,384]{1,0:T(8,128)(2,1)S(1)} %collective-permute-done.19.refs_2_, ...), custom_call_target="tpu_custom_call" | custom-call | tf_op jit(solution)/shard_map/pallas_call | solution.py:222
  129.4 2.1 %shard_map.75 = f32[5,640,384]{2,1,0:T(8,128)} custom-call(s32[1]{0:T(128)} %bitcast.7.end_ref.end, f32[5,640,384]{2,1,0:T(8,128)} %shard_map.74.b, bf16[320,384]{1,0:T(8,128)(2,1)} %collective-permute-done.38.refs_0_, bf16[320,384]{1,0:T(8,128)(2,1)S(1)} %add_convert_fusion.1.refs_1_, ...), custom_call_target="tpu_custom_call", output_to_operand_aliasing={{}: (1, {})} | custom-call | tf_op jit(solution)/shard_map/pallas_call | solution.py:222
  (143 shorter events, 17.7 us)
Async XLA Ops:
  0.6 10.9 %collective-permute-start.1 = (bf16[320,1024]{1,0:T(8,128)(2,1)}, bf16[320,1024]{1,0:T(8,128)(2,1)S(1)}, u32[]{:S(2)}, u32[]{:S(2)}) collective-permute-start(bf16[320,1024]{1,0:T(8,128)(2,1)} %bitcast.9), channel_id=1, source_target_pairs={{0,4},{4,0},{8,12},{12,8},{1,5},{5,1},{9,13},{13,9},{2,6},{6,2},{1... | collective-permute-start | bytes 1966088 | tf_op jit(solution)/shard_map/ppermute | solution.py:26
  1.1 18.7 %collective-permute-start = (bf16[320,1024]{1,0:T(8,128)(2,1)}, bf16[320,1024]{1,0:T(8,128)(2,1)S(1)}, u32[]{:S(2)}, u32[]{:S(2)}) collective-permute-start(bf16[320,1024]{1,0:T(8,128)(2,1)} %bitcast.10), channel_id=1, source_target_pairs={{0,8},{4,12},{8,0},{12,4},{1,9},{5,13},{9,1},{13,5},{2,10},{6,14},... | collective-permute-start | bytes 1966088 | tf_op jit(solution)/shard_map/ppermute | solution.py:26
  4.9 17.0 %copy-start.24 = (bf16[1,512,384]{2,1,0:T(8,128)(2,1)S(1)}, bf16[1,512,384]{2,1,0:T(8,128)(2,1)}, u32[]{:S(2)}) copy-start(bf16[1,512,384]{2,1,0:T(8,128)(2,1)} %param.9) | copy-start | bytes 1179652
  5.0 3.8 %collective-permute-start.2 = (f32[8,384]{1,0:T(8,128)S(1)}, f32[8,384]{1,0:T(8,128)S(1)}, u32[]{:S(2)}, u32[]{:S(2)}) collective-permute-start(f32[8,384]{1,0:T(8,128)S(1)} %shard_map.68), channel_id=1, source_target_pairs={{0,16},{16,0},{1,17},{17,1},{2,18},{18,2},{3,19},{19,3},{4,20},{20... | collective-permute-start | bytes 36872 | tf_op jit(solution)/shard_map/ppermute | solution.py:26
  8.9 10.5 %collective-permute-start.5 = (f32[8,384]{1,0:T(8,128)S(1)}, f32[8,384]{1,0:T(8,128)S(1)}, u32[]{:S(2)}, u32[]{:S(2)}) collective-permute-start(f32[8,384]{1,0:T(8,128)S(1)} %maximum_maximum_fusion.refs_2_.refs_4_), channel_id=1, source_target_pairs={{0,12},{4,8},{8,4},{12,0},{1,13},{5,9},{9,5},{13,1},{2,14},{6,10},... | collective-permute-start | bytes 36872 | tf_op jit(solution)/shard_map/ppermute | solution.py:26
  8.9 10.9 %collective-permute-start.4 = (f32[8,384]{1,0:T(8,128)S(1)}, f32[8,384]{1,0:T(8,128)S(1)}, u32[]{:S(2)}, u32[]{:S(2)}) collective-permute-start(f32[8,384]{1,0:T(8,128)S(1)} %maximum_maximum_fusion.refs_2_.refs_4_), channel_id=1, source_target_pairs={{0,8},{4,12},{8,0},{12,4},{1,9},{5,13},{9,1},{13,5},{2,10},{6,14},... | collective-permute-start | bytes 36872 | tf_op jit(solution)/shard_map/ppermute | solution.py:26
  9.8 1.8 %collective-permute-start.3 = (f32[8,384]{1,0:T(8,128)S(1)}, f32[8,384]{1,0:T(8,128)S(1)}, u32[]{:S(2)}, u32[]{:S(2)}) collective-permute-start(f32[8,384]{1,0:T(8,128)S(1)} %maximum_maximum_fusion.refs_2_.refs_4_), channel_id=1, source_target_pairs={{0,4},{4,0},{8,12},{12,8},{1,5},{5,1},{9,13},{13,9},{2,6},{6,2},{1... | collective-permute-start | bytes 36872 | tf_op jit(solution)/shard_map/ppermute | solution.py:26
  15.1 6.9 %copy-start.1 = (bf16[5,1280,384]{2,1,0:T(8,128)(2,1)S(1)}, bf16[5,1280,384]{2,1,0:T(8,128)(2,1)}, u32[]{:S(2)}) copy-start(bf16[5,1280,384]{2,1,0:T(8,128)(2,1)} %refs_8_.2) | copy-start | bytes 14745604
  15.1 6.9 %copy-start.4 = (bf16[1,1024,320]{1,2,0:T(8,128)(2,1)S(1)}, bf16[1,1024,320]{1,2,0:T(8,128)(2,1)}, u32[]{:S(2)}) copy-start(bf16[1,1024,320]{1,2,0:T(8,128)(2,1)} %param.5) | copy-start | bytes 1966084
  19.8 2.1 %collective-permute-start.6 = (bf16[320,1024]{1,0:T(8,128)(2,1)S(1)}, bf16[320,1024]{1,0:T(8,128)(2,1)S(1)}, u32[]{:S(2)}, u32[]{:S(2)}) collective-permute-start(bf16[320,1024]{1,0:T(8,128)(2,1)S(1)} %collective-permute-done.refs_1_), channel_id=1, source_target_pairs={{0,4},{4,0},{8,12},{12,8},{1,5},{5,1},{9,13},{13,9},{2,6},{6,2},{1... | collective-permute-start | bytes 1966088 | tf_op jit(solution)/shard_map/ppermute | solution.py:26
  30.3 10.5 %collective-permute-start.7 = (bf16[320,384]{1,0:T(8,128)(2,1)S(1)}, bf16[320,384]{1,0:T(8,128)(2,1)S(1)}, u32[]{:S(2)}, u32[]{:S(2)}) collective-permute-start(bf16[320,384]{1,0:T(8,128)(2,1)S(1)} %get-tuple-element.66), channel_id=1, source_target_pairs={{0,16},{16,0},{1,17},{17,1},{2,18},{18,2},{3,19},{19,3},{4,20},{20... | collective-permute-start | bytes 737288 | tf_op jit(solution)/shard_map/ppermute | solution.py:26
  40.5 8.7 %collective-permute-start.9 = (bf16[320,384]{1,0:T(8,128)(2,1)}, bf16[320,384]{1,0:T(8,128)(2,1)}, u32[]{:S(2)}, u32[]{:S(2)}) collective-permute-start(bf16[320,384]{1,0:T(8,128)(2,1)} %get-tuple-element.67), channel_id=1, source_target_pairs={{0,16},{16,0},{1,17},{17,1},{2,18},{18,2},{3,19},{19,3},{4,20},{20... | collective-permute-start | bytes 737288 | tf_op jit(solution)/shard_map/ppermute | solution.py:26
  42.6 9.9 %collective-permute-start.8 = (bf16[320,384]{1,0:T(8,128)(2,1)}, bf16[320,384]{1,0:T(8,128)(2,1)}, u32[]{:S(2)}, u32[]{:S(2)}) collective-permute-start(bf16[320,384]{1,0:T(8,128)(2,1)} %add_convert_fusion.29), channel_id=1, source_target_pairs={{0,1},{1,0},{2,3},{3,2},{4,5},{5,4},{6,7},{7,6},{8,9},{9,8},{10,11... | collective-permute-start | bytes 737288 | tf_op jit(solution)/shard_map/ppermute | solution.py:290
  44.4 14.9 %copy-start.11 = (bf16[640,384]{1,0:T(8,128)(2,1)S(1)}, bf16[640,384]{1,0:T(8,128)(2,1)}, u32[]{:S(2)}) copy-start(bf16[640,384]{1,0:T(8,128)(2,1)} %copy-done.10) | copy-start | bytes 1474564
  44.4 14.9 %collective-permute-start.11 = (bf16[512,384]{1,0:T(8,128)(2,1)}, bf16[512,384]{1,0:T(8,128)(2,1)S(1)}, u32[]{:S(2)}, u32[]{:S(2)}) collective-permute-start(bf16[512,384]{1,0:T(8,128)(2,1)} %copy-done.25), channel_id=1, source_target_pairs={{0,8},{4,12},{8,0},{12,4},{1,9},{5,13},{9,1},{13,5},{2,10},{6,14},... | collective-permute-start | bytes 1179656 | tf_op jit(solution)/shard_map/ppermute | solution.py:26
  45.9 12.7 %collective-permute-start.10 = (bf16[320,384]{1,0:T(8,128)(2,1)}, bf16[320,384]{1,0:T(8,128)(2,1)S(1)}, u32[]{:S(2)}, u32[]{:S(2)}) collective-permute-start(bf16[320,384]{1,0:T(8,128)(2,1)} %copy-done.31), channel_id=1, source_target_pairs={{0,16},{16,0},{1,17},{17,1},{2,18},{18,2},{3,19},{19,3},{4,20},{20... | collective-permute-start | bytes 737288 | tf_op jit(solution)/shard_map/ppermute | solution.py:26
  47.4 19.1 %collective-permute-start.17 = (bf16[320,384]{1,0:T(8,128)(2,1)}, bf16[320,384]{1,0:T(8,128)(2,1)S(1)}, u32[]{:S(2)}, u32[]{:S(2)}) collective-permute-start(bf16[320,384]{1,0:T(8,128)(2,1)} %copy-done.30), channel_id=1, source_target_pairs={{0,16},{16,0},{1,17},{17,1},{2,18},{18,2},{3,19},{19,3},{4,20},{20... | collective-permute-start | bytes 737288 | tf_op jit(solution)/shard_map/ppermute | solution.py:26
  50.4 13.5 %collective-permute-start.14 = (bf16[320,384]{1,0:T(8,128)(2,1)S(1)}, bf16[320,384]{1,0:T(8,128)(2,1)S(1)}, u32[]{:S(2)}, u32[]{:S(2)}) collective-permute-start(bf16[320,384]{1,0:T(8,128)(2,1)S(1)} %add_convert_fusion.28), channel_id=1, source_target_pairs={{0,1},{1,0},{2,3},{3,2},{4,5},{5,4},{6,7},{7,6},{8,9},{9,8},{10,11... | collective-permute-start | bytes 737288 | tf_op jit(solution)/shard_map/ppermute | solution.py:290
  52.5 20.6 %collective-permute-start.13 = (bf16[640,384]{1,0:T(8,128)(2,1)}, bf16[640,384]{1,0:T(8,128)(2,1)S(1)}, u32[]{:S(2)}, u32[]{:S(2)}) collective-permute-start(bf16[640,384]{1,0:T(8,128)(2,1)} %copy-done.29), channel_id=1, source_target_pairs={{0,16},{16,0},{1,17},{17,1},{2,18},{18,2},{3,19},{19,3},{4,20},{20... | collective-permute-start | bytes 1474568 | tf_op jit(solution)/shard_map/ppermute | solution.py:26
  58.6 6.0 %collective-permute-start.18 = (bf16[320,384]{1,0:T(8,128)(2,1)S(1)}, bf16[320,384]{1,0:T(8,128)(2,1)S(1)}, u32[]{:S(2)}, u32[]{:S(2)}) collective-permute-start(bf16[320,384]{1,0:T(8,128)(2,1)S(1)} %add_convert_fusion.27), channel_id=1, source_target_pairs={{1,2},{2,1},{5,6},{6,5},{9,10},{10,9},{13,14},{14,13},{17,18},{18,... | collective-permute-start | bytes 737288 | tf_op jit(solution)/shard_map/ppermute | solution.py:296
  59.4 12.9 %collective-permute-start.16 = (bf16[320,384]{1,0:T(8,128)(2,1)S(1)}, bf16[320,384]{1,0:T(8,128)(2,1)S(1)}, u32[]{:S(2)}, u32[]{:S(2)}) collective-permute-start(bf16[320,384]{1,0:T(8,128)(2,1)S(1)} %add_convert_fusion.26), channel_id=1, source_target_pairs={{0,1},{1,0},{2,3},{3,2},{4,5},{5,4},{6,7},{7,6},{8,9},{9,8},{10,11... | collective-permute-start | bytes 737288 | tf_op jit(solution)/shard_map/ppermute | solution.py:290
  63.9 9.1 %collective-permute-start.15 = (bf16[320,384]{1,0:T(8,128)(2,1)S(1)}, bf16[320,384]{1,0:T(8,128)(2,1)S(1)}, u32[]{:S(2)}, u32[]{:S(2)}) collective-permute-start(bf16[320,384]{1,0:T(8,128)(2,1)S(1)} %add_convert_fusion.25), channel_id=1, source_target_pairs={{1,2},{2,1},{5,6},{6,5},{9,10},{10,9},{13,14},{14,13},{17,18},{18,... | collective-permute-start | bytes 737288 | tf_op jit(solution)/shard_map/ppermute | solution.py:296
  64.6 21.0 %collective-permute-start.12 = (bf16[640,384]{1,0:T(8,128)(2,1)S(1)}, bf16[640,384]{1,0:T(8,128)(2,1)S(1)}, u32[]{:S(2)}, u32[]{:S(2)}) collective-permute-start(bf16[640,384]{1,0:T(8,128)(2,1)S(1)} %get-tuple-element.78), channel_id=1, source_target_pairs={{0,16},{16,0},{1,17},{17,1},{2,18},{18,2},{3,19},{19,3},{4,20},{20... | collective-permute-start | bytes 1474568 | tf_op jit(solution)/shard_map/ppermute | solution.py:26
  66.6 11.5 %collective-permute-start.21 = (bf16[320,384]{1,0:T(8,128)(2,1)S(1)}, bf16[320,384]{1,0:T(8,128)(2,1)S(1)}, u32[]{:S(2)}, u32[]{:S(2)}) collective-permute-start(bf16[320,384]{1,0:T(8,128)(2,1)S(1)} %broadcast_select_fusion.6), channel_id=1, source_target_pairs={{0,1},{1,0},{2,3},{3,2},{4,5},{5,4},{6,7},{7,6},{8,9},{9,8},{10,11... | collective-permute-start | bytes 737288 | tf_op jit(solution)/shard_map/ppermute | solution.py:290
  72.4 6.7 %collective-permute-start.20 = (bf16[320,384]{1,0:T(8,128)(2,1)S(1)}, bf16[320,384]{1,0:T(8,128)(2,1)S(1)}, u32[]{:S(2)}, u32[]{:S(2)}) collective-permute-start(bf16[320,384]{1,0:T(8,128)(2,1)S(1)} %add_convert_fusion.22), channel_id=1, source_target_pairs={{1,2},{2,1},{5,6},{6,5},{9,10},{10,9},{13,14},{14,13},{17,18},{18,... | collective-permute-start | bytes 737288 | tf_op jit(solution)/shard_map/ppermute | solution.py:296
  73.3 10.0 %collective-permute-start.19 = (bf16[320,384]{1,0:T(8,128)(2,1)S(1)}, bf16[320,384]{1,0:T(8,128)(2,1)S(1)}, u32[]{:S(2)}, u32[]{:S(2)}) collective-permute-start(bf16[320,384]{1,0:T(8,128)(2,1)S(1)} %broadcast_select_fusion.5), channel_id=1, source_target_pairs={{0,1},{1,0},{2,3},{3,2},{4,5},{5,4},{6,7},{7,6},{8,9},{9,8},{10,11... | collective-permute-start | bytes 737288 | tf_op jit(solution)/shard_map/ppermute | solution.py:290
  78.3 18.1 %copy-start.26 = (bf16[512,384]{1,0:T(8,128)(2,1)S(1)}, bf16[512,384]{1,0:T(8,128)(2,1)}, u32[]{:S(2)}) copy-start(bf16[512,384]{1,0:T(8,128)(2,1)} %copy-done.25) | copy-start | bytes 1179652
  78.3 7.4 %collective-permute-start.24 = (bf16[320,384]{1,0:T(8,128)(2,1)S(1)}, bf16[320,384]{1,0:T(8,128)(2,1)S(1)}, u32[]{:S(2)}, u32[]{:S(2)}) collective-permute-start(bf16[320,384]{1,0:T(8,128)(2,1)S(1)} %add_convert_fusion.19), channel_id=1, source_target_pairs={{1,2},{2,1},{5,6},{6,5},{9,10},{10,9},{13,14},{14,13},{17,18},{18,... | collective-permute-start | bytes 737288 | tf_op jit(solution)/shard_map/ppermute | solution.py:296
  79.3 10.4 %collective-permute-start.23 = (bf16[320,384]{1,0:T(8,128)(2,1)S(1)}, bf16[320,384]{1,0:T(8,128)(2,1)S(1)}, u32[]{:S(2)}, u32[]{:S(2)}) collective-permute-start(bf16[320,384]{1,0:T(8,128)(2,1)S(1)} %broadcast_select_fusion.4), channel_id=1, source_target_pairs={{0,1},{1,0},{2,3},{3,2},{4,5},{5,4},{6,7},{7,6},{8,9},{9,8},{10,11... | collective-permute-start | bytes 737288 | tf_op jit(solution)/shard_map/ppermute | solution.py:290
  83.4 7.0 %collective-permute-start.22 = (bf16[320,384]{1,0:T(8,128)(2,1)S(1)}, bf16[320,384]{1,0:T(8,128)(2,1)S(1)}, u32[]{:S(2)}, u32[]{:S(2)}) collective-permute-start(bf16[320,384]{1,0:T(8,128)(2,1)S(1)} %add_convert_fusion.16), channel_id=1, source_target_pairs={{1,2},{2,1},{5,6},{6,5},{9,10},{10,9},{13,14},{14,13},{17,18},{18,... | collective-permute-start | bytes 737288 | tf_op jit(solution)/shard_map/ppermute | solution.py:296
  84.1 12.8 %collective-permute-start.26 = (bf16[640,384]{1,0:T(8,128)(2,1)S(1)}, bf16[640,384]{1,0:T(8,128)(2,1)S(1)}, u32[]{:S(2)}, u32[]{:S(2)}) collective-permute-start(bf16[640,384]{1,0:T(8,128)(2,1)S(1)} %get-tuple-element.99), channel_id=1, source_target_pairs={{0,16},{16,0},{1,17},{17,1},{2,18},{18,2},{3,19},{19,3},{4,20},{20... | collective-permute-start | bytes 1474568 | tf_op jit(solution)/shard_map/ppermute | solution.py:26
  85.9 9.6 %collective-permute-start.28 = (bf16[320,384]{1,0:T(8,128)(2,1)S(1)}, bf16[320,384]{1,0:T(8,128)(2,1)S(1)}, u32[]{:S(2)}, u32[]{:S(2)}) collective-permute-start(bf16[320,384]{1,0:T(8,128)(2,1)S(1)} %broadcast_select_fusion.3), channel_id=1, source_target_pairs={{0,1},{1,0},{2,3},{3,2},{4,5},{5,4},{6,7},{7,6},{8,9},{9,8},{10,11... | collective-permute-start | bytes 737288 | tf_op jit(solution)/shard_map/ppermute | solution.py:290
  89.7 6.5 %collective-permute-start.27 = (bf16[320,384]{1,0:T(8,128)(2,1)S(1)}, bf16[320,384]{1,0:T(8,128)(2,1)S(1)}, u32[]{:S(2)}, u32[]{:S(2)}) collective-permute-start(bf16[320,384]{1,0:T(8,128)(2,1)S(1)} %add_convert_fusion.13), channel_id=1, source_target_pairs={{1,2},{2,1},{5,6},{6,5},{9,10},{10,9},{13,14},{14,13},{17,18},{18,... | collective-permute-start | bytes 737288 | tf_op jit(solution)/shard_map/ppermute | solution.py:296
  90.6 27.9 %copy-start.9 = (bf16[1536,640]{1,0:T(8,128)(2,1)S(1)}, bf16[1536,640]{1,0:T(8,128)(2,1)}, u32[]{:S(2)}) copy-start(bf16[1536,640]{1,0:T(8,128)(2,1)} %refs_8_.3) | copy-start | bytes 5898244
  90.6 9.9 %collective-permute-start.25 = (bf16[320,384]{1,0:T(8,128)(2,1)S(1)}, bf16[320,384]{1,0:T(8,128)(2,1)S(1)}, u32[]{:S(2)}, u32[]{:S(2)}) collective-permute-start(bf16[320,384]{1,0:T(8,128)(2,1)S(1)} %broadcast_select_fusion.2), channel_id=1, source_target_pairs={{0,1},{1,0},{2,3},{3,2},{4,5},{5,4},{6,7},{7,6},{8,9},{9,8},{10,11... | collective-permute-start | bytes 737288 | tf_op jit(solution)/shard_map/ppermute | solution.py:290
  95.6 5.9 %collective-permute-start.31 = (bf16[320,384]{1,0:T(8,128)(2,1)S(1)}, bf16[320,384]{1,0:T(8,128)(2,1)S(1)}, u32[]{:S(2)}, u32[]{:S(2)}) collective-permute-start(bf16[320,384]{1,0:T(8,128)(2,1)S(1)} %add_convert_fusion.10), channel_id=1, source_target_pairs={{1,2},{2,1},{5,6},{6,5},{9,10},{10,9},{13,14},{14,13},{17,18},{18,... | collective-permute-start | bytes 737288 | tf_op jit(solution)/shard_map/ppermute | solution.py:296
  96.4 22.2 %collective-permute-start.35 = (bf16[512,384]{1,0:T(8,128)(2,1)S(1)}, bf16[512,384]{1,0:T(8,128)(2,1)S(1)}, u32[]{:S(2)}, u32[]{:S(2)}) collective-permute-start(bf16[512,384]{1,0:T(8,128)(2,1)S(1)} %copy-done.26), channel_id=1, source_target_pairs={{0,4},{4,0},{8,12},{12,8},{1,5},{5,1},{9,13},{13,9},{2,6},{6,2},{1... | collective-permute-start | bytes 1179656 | tf_op jit(solution)/shard_map/ppermute | solution.py:26
  96.4 22.1 %collective-permute-start.36 = (bf16[512,384]{1,0:T(8,128)(2,1)S(1)}, bf16[512,384]{1,0:T(8,128)(2,1)S(1)}, u32[]{:S(2)}, u32[]{:S(2)}) collective-permute-start(bf16[512,384]{1,0:T(8,128)(2,1)S(1)} %collective-permute-done.11.refs_1_), channel_id=1, source_target_pairs={{0,4},{4,0},{8,12},{12,8},{1,5},{5,1},{9,13},{13,9},{2,6},{6,2},{1... | collective-permute-start | bytes 1179656 | tf_op jit(solution)/shard_map/ppermute | solution.py:26
  97.1 10.2 %collective-permute-start.30 = (bf16[320,384]{1,0:T(8,128)(2,1)S(1)}, bf16[320,384]{1,0:T(8,128)(2,1)S(1)}, u32[]{:S(2)}, u32[]{:S(2)}) collective-permute-start(bf16[320,384]{1,0:T(8,128)(2,1)S(1)} %broadcast_select_fusion.1), channel_id=1, source_target_pairs={{0,1},{1,0},{2,3},{3,2},{4,5},{5,4},{6,7},{7,6},{8,9},{9,8},{10,11... | collective-permute-start | bytes 737288 | tf_op jit(solution)/shard_map/ppermute | solution.py:290
  100.6 22.7 %copy-start.13 = (bf16[320,384]{1,0:T(8,128)(2,1)S(1)}, bf16[320,384]{1,0:T(8,128)(2,1)}, u32[]{:S(2)}) copy-start(bf16[320,384]{1,0:T(8,128)(2,1)} %copy-done.12) | copy-start | bytes 737284
  100.6 22.7 %copy-start.15 = (bf16[320,384]{1,0:T(8,128)(2,1)S(1)}, bf16[320,384]{1,0:T(8,128)(2,1)}, u32[]{:S(2)}) copy-start(bf16[320,384]{1,0:T(8,128)(2,1)} %copy-done.14) | copy-start | bytes 737284
  100.7 7.4 %collective-permute-start.29 = (bf16[320,384]{1,0:T(8,128)(2,1)S(1)}, bf16[320,384]{1,0:T(8,128)(2,1)S(1)}, u32[]{:S(2)}, u32[]{:S(2)}) collective-permute-start(bf16[320,384]{1,0:T(8,128)(2,1)S(1)} %add_convert_fusion.7), channel_id=1, source_target_pairs={{1,2},{2,1},{5,6},{6,5},{9,10},{10,9},{13,14},{14,13},{17,18},{18,... | collective-permute-start | bytes 737288 | tf_op jit(solution)/shard_map/ppermute | solution.py:296
  101.7 11.6 %collective-permute-start.34 = (bf16[320,384]{1,0:T(8,128)(2,1)S(1)}, bf16[320,384]{1,0:T(8,128)(2,1)S(1)}, u32[]{:S(2)}, u32[]{:S(2)}) collective-permute-start(bf16[320,384]{1,0:T(8,128)(2,1)S(1)} %broadcast_select_fusion), channel_id=1, source_target_pairs={{0,1},{1,0},{2,3},{3,2},{4,5},{5,4},{6,7},{7,6},{8,9},{9,8},{10,11... | collective-permute-start | bytes 737288 | tf_op jit(solution)/shard_map/ppermute | solution.py:290
  107.4 6.7 %collective-permute-start.33 = (bf16[320,384]{1,0:T(8,128)(2,1)S(1)}, bf16[320,384]{1,0:T(8,128)(2,1)S(1)}, u32[]{:S(2)}, u32[]{:S(2)}) collective-permute-start(bf16[320,384]{1,0:T(8,128)(2,1)S(1)} %add_convert_fusion.4), channel_id=1, source_target_pairs={{1,2},{2,1},{5,6},{6,5},{9,10},{10,9},{13,14},{14,13},{17,18},{18,... | collective-permute-start | bytes 737288 | tf_op jit(solution)/shard_map/ppermute | solution.py:296
  108.2 10.4 %collective-permute-start.32 = (bf16[320,384]{1,0:T(8,128)(2,1)S(1)}, bf16[320,384]{1,0:T(8,128)(2,1)S(1)}, u32[]{:S(2)}, u32[]{:S(2)}) collective-permute-start(bf16[320,384]{1,0:T(8,128)(2,1)S(1)} %add_convert_fusion.3.refs_15_), channel_id=1, source_target_pairs={{0,1},{1,0},{2,3},{3,2},{4,5},{5,4},{6,7},{7,6},{8,9},{9,8},{10,11... | collective-permute-start | bytes 737288 | tf_op jit(solution)/shard_map/ppermute | solution.py:290
  113.4 8.8 %collective-permute-start.37 = (bf16[320,384]{1,0:T(8,128)(2,1)S(1)}, bf16[320,384]{1,0:T(8,128)(2,1)S(1)}, u32[]{:S(2)}, u32[]{:S(2)}) collective-permute-start(bf16[320,384]{1,0:T(8,128)(2,1)S(1)} %add_convert_fusion.2), channel_id=1, source_target_pairs={{1,2},{2,1},{5,6},{6,5},{9,10},{10,9},{13,14},{14,13},{17,18},{18,... | collective-permute-start | bytes 737288 | tf_op jit(solution)/shard_map/ppermute | solution.py:296
  114.1 15.3 %collective-permute-start.38 = (bf16[320,384]{1,0:T(8,128)(2,1)S(1)}, bf16[320,384]{1,0:T(8,128)(2,1)}, u32[]{:S(2)}, u32[]{:S(2)}) collective-permute-start(bf16[320,384]{1,0:T(8,128)(2,1)S(1)} %add_convert_fusion.1.refs_1_), channel_id=1, source_target_pairs={{0,1},{1,0},{2,3},{3,2},{4,5},{5,4},{6,7},{7,6},{8,9},{9,8},{10,11... | collective-permute-start | bytes 737288 | tf_op jit(solution)/shard_map/ppermute | solution.py:290
  122.2 7.2 %collective-permute-start.39 = (bf16[320,384]{1,0:T(8,128)(2,1)S(1)}, bf16[320,384]{1,0:T(8,128)(2,1)}, u32[]{:S(2)}, u32[]{:S(2)}) collective-permute-start(bf16[320,384]{1,0:T(8,128)(2,1)S(1)} %add_convert_fusion.refs_3_), channel_id=1, source_target_pairs={{0,1},{1,0},{2,3},{3,2},{4,5},{5,4},{6,7},{7,6},{8,9},{9,8},{10,11... | collective-permute-start | bytes 737288 | tf_op jit(solution)/shard_map/ppermute | solution.py:290
  (24 other events, 38.7 us)

commit v12 on v10

--- a/solution.py
+++ b/solution.py
@@ -376,7 +376,7 @@
             if not pair:
                 outs.append([jax.ShapeDtypeStruct((peers * depth, width), BF16)])
                 continue
-            whole = jax.ShapeDtypeStruct((per * depth, width), BF16)
+            whole = pltpu.HBM((per * depth, width), BF16)
             outs.append([whole] + ([piece] * len(q) if q else [whole]))
         flat = call(
             functools.partial(grad_kernel, group, depth, per, pieces),

time: 130 us -> 134 us (1.031)
  Pallas kernels: 28.4 us -> 30.9 us
    pallas_call x6, Pallas kernels: 23.9 us -> 26.4 us  [call(): pl.pallas_call(kernel, out_shape=out, in_specs=[pl.BlockSpec(memory_space...]
    ppermute x13, waiting for transfers between devices: 6.02 us -> 7.91 us  [chain_sums(): outer[r] = lax.ppermute(value, 'dp', outer_pairs)]
    ppermute x17, waiting for transfers between devices: 8.64 us -> 7.15 us  [swap(): return lax.ppermute(value, axis, [(i, i ^ bit) for i in range(peers)])]
    unnamed x46 -> x56, local copies, waits for them, and re-layouts: 14 us -> 14 us
  transfers between devices with their start and end apart: 40 -> 40, of which waited for: 9 -> 13; matrix products, arithmetic and copies ran while one was open for 5% -> 5% of each run, Pallas kernels for 16% -> 17%
where the time goes in v12:
time: 134 us; the launch traced here: 133 us
  starting transfers between devices  64.3 us (48%)
  Pallas kernels  30.9 us (23%)
  waiting for transfers between devices  15.1 us (11%)
  local copies, waits for them, and re-layouts  14.9 us (11%)
  other arithmetic  6.36 us (5%)
    ppermute x13, starting transfers between devices, chain_sums(): outer[r] = lax.ppermute(value, 'dp', outer_pairs)  40.4 us
    pallas_call x6, Pallas kernels, call(): pl.pallas_call(kernel, out_shape=out, in_specs=[pl.BlockSpec(memory_space...  26.4 us
    ppermute x17, starting transfers between devices, swap(): return lax.ppermute(value, axis, [(i, i ^ bit) for i in range(peers)])  16.9 us
    unnamed x56, local copies, waits for them, and re-layouts  14 us
    ppermute x13, waiting for transfers between devices, chain_sums(): outer[r] = lax.ppermute(value, 'dp', outer_pairs)  7.91 us
    ppermute x17, waiting for transfers between devices, swap(): return lax.ppermute(value, axis, [(i, i ^ bit) for i in range(peers)])  7.15 us
    ppermute x10, starting transfers between devices, chain_sums(): middle[r - 1] = lax.ppermute(last, 'dp', middle_pairs)  7.03 us
    convert_element_type x23, other arithmetic, added(): return (a.astype(F32) + b.astype(F32)).astype(BF16)  5.49 us
  transfers between devices with their start and end apart: 40, of which 13 were waited for; matrix products, arithmetic and copies ran while one was open for 5% of the time, Pallas kernels for 17%

profile of v12, /device:TPU:0, one launch (start us, length us, event | category | flops | bytes accessed | tf_op | source)
XLA Modules:
  0.0 132.7 jit_solution(17146412651255703735)
XLA Ops:
  1.1 2.6 %collective-permute-start = (bf16[320,1024]{1,0:T(8,128)(2,1)}, bf16[320,1024]{1,0:T(8,128)(2,1)S(1)}, u32[]{:S(2)}, u32[]{:S(2)}) collective-permute-start(bf16[320,1024]{1,0:T(8,128)(2,1)} %bitcast.10), channel_id=1, source_target_pairs={{0,8},{4,12},{8,0},{12,4},{1,9},{5,13},{9,1},{13,5},{2,10},{6,14},... | collective-permute-start | bytes 1966088 | tf_op jit(solution)/shard_map/ppermute | solution.py:26
  3.7 1.1 copy-done.4
  5.0 1.6 %collective-permute-start.2 = (f32[8,384]{1,0:T(8,128)S(1)}, f32[8,384]{1,0:T(8,128)S(1)}, u32[]{:S(2)}, u32[]{:S(2)}) collective-permute-start(f32[8,384]{1,0:T(8,128)S(1)} %shard_map.68), channel_id=1, source_target_pairs={{0,16},{16,0},{1,17},{17,1},{2,18},{18,2},{3,19},{19,3},{4,20},{20... | collective-permute-start | bytes 36872 | tf_op jit(solution)/shard_map/ppermute | solution.py:26
  7.3 1.4 %collective-permute-done.2 = f32[8,384]{1,0:T(8,128)S(1)} collective-permute-done((f32[8,384]{1,0:T(8,128)S(1)}, f32[8,384]{1,0:T(8,128)S(1)}, u32[]{:S(2)}, u32[]{:S(2)}) %collective-permute-start.2) | collective-permute-done | bytes 12320 | tf_op jit(solution)/shard_map/ppermute | solution.py:26
  8.9 0.9 collective-permute-start.4
  11.6 2.4 %copy-done = bf16[5,1280,384]{2,1,0:T(8,128)(2,1)S(1)} copy-done((bf16[5,1280,384]{2,1,0:T(8,128)(2,1)S(1)}, bf16[5,1280,384]{2,1,0:T(8,128)(2,1)}, u32[]{:S(2)}) %copy-start) | copy-done | bytes 4915224
  14.0 1.1 copy-done.5
  15.1 4.3 %shard_map.69 = (f32[512,384]{1,0:T(8,128)S(1)}, f32[512,384]{1,0:T(8,128)S(1)}) custom-call(s32[2]{0:T(128)S(1)} %pad_add_fusion.idx_ref, bf16[320,1024]{1,0:T(8,128)(2,1)S(1)} %bitcast.13, bf16[320,1024]{1,0:T(8,128)(2,1)S(1)} %collective-permute-done.1.refs_1_.refs_2_, f32[8,384]{1,0:T(8,128)S(1)} %maximum_maximum_fusion.refs_2_.refs_4_, ...), custom_call_target="tpu_custom_call" | custom-call | tf_op jit(solution)/shard_map/pallas_call | solution.py:187
  20.6 1.3 collective-permute-done.6.refs_3_
  21.9 1.1 copy-done.8
  23.0 1.1 copy-done.17
  24.1 6.2 %shard_map.70 = (bf16[512,384]{1,0:T(8,128)(2,1)S(1)}, f32[1040,384]{1,0:T(8,128)S(1)}, bf16[1280,1152]{1,0:T(8,128)(2,1)S(1)}, bf16[320,384]{1,0:T(8,128)(2,1)S(1)}) custom-call(s32[2]{0:T(128)S(1)} %pad_add_fusion.idx_ref, bf16[320,1024]{1,0:T(8,128)(2,1)S(1)} %bitcast.14, bf16[320,1024]{1,0:T(8,128)(2,1)S(1)} %copy-done.17, ...), custom_call_target="tpu_custom_call" | custom-call | tf_op jit(solution)/shard_map/pallas_call | solution.py:187
  30.3 1.8 %collective-permute-start.7 = (bf16[320,384]{1,0:T(8,128)(2,1)S(1)}, bf16[320,384]{1,0:T(8,128)(2,1)S(1)}, u32[]{:S(2)}, u32[]{:S(2)}) collective-permute-start(bf16[320,384]{1,0:T(8,128)(2,1)S(1)} %get-tuple-element.67), channel_id=1, source_target_pairs={{0,16},{16,0},{1,17},{17,1},{2,18},{18,2},{3,19},{19,3},{4,20},{20... | collective-permute-start | bytes 737288 | tf_op jit(solution)/shard_map/ppermute | solution.py:26
  32.1 3.1 %shard_map.71 = (bf16[640,384]{1,0:T(8,128)(2,1)}, bf16[320,384]{1,0:T(8,128)(2,1)S(1)}) custom-call(s32[2]{0:T(128)S(1)} %pad_add_fusion.idx_ref, bf16[1280,1152]{1,0:T(8,128)(2,1)S(1)} %get-tuple-element.64.all_ref, f32[1040,384]{1,0:T(8,128)S(1)} %get-tuple-element.65.p_ref), custom_call_target="tpu_custom_call" | custom-call | tf_op jit(solution)/shard_map/pallas_call | solution.py:187
  35.2 1.1 copy-done.2
  36.7 1.8 %collective-permute-done.7 = bf16[320,384]{1,0:T(8,128)(2,1)S(1)} collective-permute-done((bf16[320,384]{1,0:T(8,128)(2,1)S(1)}, bf16[320,384]{1,0:T(8,128)(2,1)S(1)}, u32[]{:S(2)}, u32[]{:S(2)}) %collective-permute-start.7) | collective-permute-done | bytes 245792 | tf_op jit(solution)/shard_map/ppermute | solution.py:26
  38.4 1.7 %add_convert_fusion.29 = bf16[320,384]{1,0:T(8,128)(2,1)} fusion(bf16[320,384]{1,0:T(8,128)(2,1)S(1)} %collective-permute-done.7, bf16[640,384]{1,0:T(8,128)(2,1)} %get-tuple-element.66), kind=kLoop, calls=%fused_computation.29 | loop fusion | flops 491520 | bytes 737280 | tf_op jit(solution)/shard_map/convert_element_type | solution.py:272
  40.1 1.8 %collective-permute-start.8 = (bf16[320,384]{1,0:T(8,128)(2,1)}, bf16[320,384]{1,0:T(8,128)(2,1)}, u32[]{:S(2)}, u32[]{:S(2)}) collective-permute-start(bf16[320,384]{1,0:T(8,128)(2,1)} %add_convert_fusion.29), channel_id=1, source_target_pairs={{0,1},{1,0},{2,3},{3,2},{4,5},{5,4},{6,7},{7,6},{8,9},{9,8},{10,11... | collective-permute-start | bytes 737288 | tf_op jit(solution)/shard_map/ppermute | solution.py:290
  41.9 1.5 %collective-permute-start.10 = (bf16[512,384]{1,0:T(8,128)(2,1)}, bf16[512,384]{1,0:T(8,128)(2,1)S(1)}, u32[]{:S(2)}, u32[]{:S(2)}) collective-permute-start(bf16[512,384]{1,0:T(8,128)(2,1)} %copy-done.19), channel_id=1, source_target_pairs={{0,8},{4,12},{8,0},{12,4},{1,9},{5,13},{9,1},{13,5},{2,10},{6,14},... | collective-permute-start | bytes 1179656 | tf_op jit(solution)/shard_map/ppermute | solution.py:26
  43.4 1.4 %copy-done.3 = f32[1040,384]{1,0:T(8,128)S(1)} copy-done((f32[1040,384]{1,0:T(8,128)S(1)}, f32[1040,384]{1,0:T(8,128)}, u32[]{:S(2)}) %copy-start.3) | copy-done | bytes 1597464
  44.8 4.6 %shard_map.73 = (bf16[640,384]{1,0:T(8,128)(2,1)}, bf16[320,384]{1,0:T(8,128)(2,1)S(1)}, bf16[320,384]{1,0:T(8,128)(2,1)S(1)}, bf16[640,384]{1,0:T(8,128)(2,1)}, bf16[640,384]{1,0:T(8,128)(2,1)}) custom-call(s32[2]{0:T(128)S(1)} %pad_add_fusion.idx_ref, bf16[1280,1152]{1,0:T(8,128)(2,1)S(1)} %get-tuple-element.64.all_ref, f32[1040,384]{1,0:T(8,128)S(1)} %copy-done.3), custom_call_target="tpu_custom_call" | custom-call | tf_op jit(solution)/shard_map/pallas_call | solution.py:187
  49.5 2.2 %collective-permute-start.11 = (bf16[320,384]{1,0:T(8,128)(2,1)S(1)}, bf16[320,384]{1,0:T(8,128)(2,1)S(1)}, u32[]{:S(2)}, u32[]{:S(2)}) collective-permute-start(bf16[320,384]{1,0:T(8,128)(2,1)S(1)} %get-tuple-element.77), channel_id=1, source_target_pairs={{0,16},{16,0},{1,17},{17,1},{2,18},{18,2},{3,19},{19,3},{4,20},{20... | collective-permute-start | bytes 737288 | tf_op jit(solution)/shard_map/ppermute | solution.py:26
  51.7 1.1 add_convert_fusion.28
  53.3 2.0 %collective-permute-start.13 = (bf16[640,384]{1,0:T(8,128)(2,1)}, bf16[640,384]{1,0:T(8,128)(2,1)S(1)}, u32[]{:S(2)}, u32[]{:S(2)}) collective-permute-start(bf16[640,384]{1,0:T(8,128)(2,1)} %get-tuple-element.83), channel_id=1, source_target_pairs={{0,16},{16,0},{1,17},{17,1},{2,18},{18,2},{3,19},{19,3},{4,20},{20... | collective-permute-start | bytes 1474568 | tf_op jit(solution)/shard_map/ppermute | solution.py:26
  55.3 1.1 add_convert_fusion.27
  57.3 4.6 %shard_map.72 = (bf16[640,384]{1,0:T(8,128)(2,1)}, bf16[640,384]{1,0:T(8,128)(2,1)}, bf16[640,384]{1,0:T(8,128)(2,1)}, bf16[640,384]{1,0:T(8,128)(2,1)}) custom-call(s32[2]{0:T(128)S(1)} %pad_add_fusion.idx_ref, bf16[1280,1152]{1,0:T(8,128)(2,1)S(1)} %get-tuple-element.64.all_ref, f32[1040,384]{1,0:T(8,128)S(1)} %copy-done.3), custom_call_target="tpu_custom_call" | custom-call | tf_op jit(solution)/shard_map/pallas_call | solution.py:187
  61.9 4.5 %collective-permute-start.16 = (bf16[320,384]{1,0:T(8,128)(2,1)S(1)}, bf16[320,384]{1,0:T(8,128)(2,1)S(1)}, u32[]{:S(2)}, u32[]{:S(2)}) collective-permute-start(bf16[320,384]{1,0:T(8,128)(2,1)S(1)} %add_convert_fusion.26), channel_id=1, source_target_pairs={{0,1},{1,0},{2,3},{3,2},{4,5},{5,4},{6,7},{7,6},{8,9},{9,8},{10,11... | collective-permute-start | bytes 737288 | tf_op jit(solution)/shard_map/ppermute | solution.py:290
  67.5 1.8 %collective-permute-start.21 = (bf16[320,384]{1,0:T(8,128)(2,1)S(1)}, bf16[320,384]{1,0:T(8,128)(2,1)S(1)}, u32[]{:S(2)}, u32[]{:S(2)}) collective-permute-start(bf16[320,384]{1,0:T(8,128)(2,1)S(1)} %broadcast_select_fusion.6), channel_id=1, source_target_pairs={{0,1},{1,0},{2,3},{3,2},{4,5},{5,4},{6,7},{7,6},{8,9},{9,8},{10,11... | collective-permute-start | bytes 737288 | tf_op jit(solution)/shard_map/ppermute | solution.py:290
  69.2 2.8 %collective-permute-done.16 = bf16[320,384]{1,0:T(8,128)(2,1)S(1)} collective-permute-done((bf16[320,384]{1,0:T(8,128)(2,1)S(1)}, bf16[320,384]{1,0:T(8,128)(2,1)S(1)}, u32[]{:S(2)}, u32[]{:S(2)}) %collective-permute-start.16) | collective-permute-done | bytes 245792 | tf_op jit(solution)/shard_map/ppermute | solution.py:290
  72.8 1.5 %collective-permute-done.13 = bf16[640,384]{1,0:T(8,128)(2,1)S(1)} collective-permute-done((bf16[640,384]{1,0:T(8,128)(2,1)}, bf16[640,384]{1,0:T(8,128)(2,1)S(1)}, u32[]{:S(2)}, u32[]{:S(2)}) %collective-permute-start.13) | collective-permute-done | bytes 491552 | tf_op jit(solution)/shard_map/ppermute | solution.py:26
  74.5 3.1 %collective-permute-start.19 = (bf16[320,384]{1,0:T(8,128)(2,1)S(1)}, bf16[320,384]{1,0:T(8,128)(2,1)S(1)}, u32[]{:S(2)}, u32[]{:S(2)}) collective-permute-start(bf16[320,384]{1,0:T(8,128)(2,1)S(1)} %broadcast_select_fusion.5), channel_id=1, source_target_pairs={{0,1},{1,0},{2,3},{3,2},{4,5},{5,4},{6,7},{7,6},{8,9},{9,8},{10,11... | collective-permute-start | bytes 737288 | tf_op jit(solution)/shard_map/ppermute | solution.py:290
  78.7 4.9 %collective-permute-start.23 = (bf16[320,384]{1,0:T(8,128)(2,1)S(1)}, bf16[320,384]{1,0:T(8,128)(2,1)S(1)}, u32[]{:S(2)}, u32[]{:S(2)}) collective-permute-start(bf16[320,384]{1,0:T(8,128)(2,1)S(1)} %broadcast_select_fusion.4), channel_id=1, source_target_pairs={{0,1},{1,0},{2,3},{3,2},{4,5},{5,4},{6,7},{7,6},{8,9},{9,8},{10,11... | collective-permute-start | bytes 737288 | tf_op jit(solution)/shard_map/ppermute | solution.py:290
  84.5 1.9 %collective-permute-start.26 = (bf16[640,384]{1,0:T(8,128)(2,1)S(1)}, bf16[640,384]{1,0:T(8,128)(2,1)S(1)}, u32[]{:S(2)}, u32[]{:S(2)}) collective-permute-start(bf16[640,384]{1,0:T(8,128)(2,1)S(1)} %copy-done.27), channel_id=1, source_target_pairs={{0,16},{16,0},{1,17},{17,1},{2,18},{18,2},{3,19},{19,3},{4,20},{20... | collective-permute-start | bytes 1474568 | tf_op jit(solution)/shard_map/ppermute | solution.py:26
  86.6 3.0 %collective-permute-start.28 = (bf16[320,384]{1,0:T(8,128)(2,1)S(1)}, bf16[320,384]{1,0:T(8,128)(2,1)S(1)}, u32[]{:S(2)}, u32[]{:S(2)}) collective-permute-start(bf16[320,384]{1,0:T(8,128)(2,1)S(1)} %broadcast_select_fusion.3), channel_id=1, source_target_pairs={{0,1},{1,0},{2,3},{3,2},{4,5},{5,4},{6,7},{7,6},{8,9},{9,8},{10,11... | collective-permute-start | bytes 737288 | tf_op jit(solution)/shard_map/ppermute | solution.py:290
  91.3 3.4 %collective-permute-start.25 = (bf16[320,384]{1,0:T(8,128)(2,1)S(1)}, bf16[320,384]{1,0:T(8,128)(2,1)S(1)}, u32[]{:S(2)}, u32[]{:S(2)}) collective-permute-start(bf16[320,384]{1,0:T(8,128)(2,1)S(1)} %broadcast_select_fusion.2), channel_id=1, source_target_pairs={{0,1},{1,0},{2,3},{3,2},{4,5},{5,4},{6,7},{7,6},{8,9},{9,8},{10,11... | collective-permute-start | bytes 737288 | tf_op jit(solution)/shard_map/ppermute | solution.py:290
  96.6 4.8 %collective-permute-start.30 = (bf16[320,384]{1,0:T(8,128)(2,1)S(1)}, bf16[320,384]{1,0:T(8,128)(2,1)S(1)}, u32[]{:S(2)}, u32[]{:S(2)}) collective-permute-start(bf16[320,384]{1,0:T(8,128)(2,1)S(1)} %broadcast_select_fusion.1), channel_id=1, source_target_pairs={{0,1},{1,0},{2,3},{3,2},{4,5},{5,4},{6,7},{7,6},{8,9},{9,8},{10,11... | collective-permute-start | bytes 737288 | tf_op jit(solution)/shard_map/ppermute | solution.py:290
  102.4 2.8 %collective-permute-start.34 = (bf16[320,384]{1,0:T(8,128)(2,1)S(1)}, bf16[320,384]{1,0:T(8,128)(2,1)S(1)}, u32[]{:S(2)}, u32[]{:S(2)}) collective-permute-start(bf16[320,384]{1,0:T(8,128)(2,1)S(1)} %broadcast_select_fusion), channel_id=1, source_target_pairs={{0,1},{1,0},{2,3},{3,2},{4,5},{5,4},{6,7},{7,6},{8,9},{9,8},{10,11... | collective-permute-start | bytes 737288 | tf_op jit(solution)/shard_map/ppermute | solution.py:290
  105.2 3.0 %collective-permute-done.30.refs_10_ = bf16[320,384]{1,0:T(8,128)(2,1)S(1)} collective-permute-done((bf16[320,384]{1,0:T(8,128)(2,1)S(1)}, bf16[320,384]{1,0:T(8,128)(2,1)S(1)}, u32[]{:S(2)}, u32[]{:S(2)}) %collective-permute-start.30) | collective-permute-done | bytes 245792 | tf_op jit(solution)/shard_map/ppermute | solution.py:290
  109.1 3.9 %collective-permute-start.32 = (bf16[320,384]{1,0:T(8,128)(2,1)S(1)}, bf16[320,384]{1,0:T(8,128)(2,1)S(1)}, u32[]{:S(2)}, u32[]{:S(2)}) collective-permute-start(bf16[320,384]{1,0:T(8,128)(2,1)S(1)} %add_convert_fusion.3.refs_15_), channel_id=1, source_target_pairs={{0,1},{1,0},{2,3},{3,2},{4,5},{5,4},{6,7},{7,6},{8,9},{9,8},{10,11... | collective-permute-start | bytes 737288 | tf_op jit(solution)/shard_map/ppermute | solution.py:290
  114.3 4.3 %collective-permute-start.38 = (bf16[320,384]{1,0:T(8,128)(2,1)S(1)}, bf16[320,384]{1,0:T(8,128)(2,1)}, u32[]{:S(2)}, u32[]{:S(2)}) collective-permute-start(bf16[320,384]{1,0:T(8,128)(2,1)S(1)} %add_convert_fusion.1.refs_1_), channel_id=1, source_target_pairs={{0,1},{1,0},{2,3},{3,2},{4,5},{5,4},{6,7},{7,6},{8,9},{9,8},{10,11... | collective-permute-start | bytes 737288 | tf_op jit(solution)/shard_map/ppermute | solution.py:290
  119.1 3.6 %shard_map.74 = bf16[512,640]{1,0:T(8,128)(2,1)} custom-call(s32[2]{0:T(128)S(1)} %pad_add_fusion.idx_ref, bf16[512,384]{1,0:T(8,128)(2,1)S(1)} %copy-done.20, bf16[512,384]{1,0:T(8,128)(2,1)S(1)} %collective-permute-done.10.refs_1_, bf16[512,384]{1,0:T(8,128)(2,1)S(1)} %collective-permute-done.35.refs_2_, ...), custom_call_target="tpu_custom_call" | custom-call | tf_op jit(solution)/shard_map/pallas_call | solution.py:187
  122.8 1.8 %collective-permute-start.39 = (bf16[320,384]{1,0:T(8,128)(2,1)S(1)}, bf16[320,384]{1,0:T(8,128)(2,1)}, u32[]{:S(2)}, u32[]{:S(2)}) collective-permute-start(bf16[320,384]{1,0:T(8,128)(2,1)S(1)} %add_convert_fusion.refs_3_), channel_id=1, source_target_pairs={{0,1},{1,0},{2,3},{3,2},{4,5},{5,4},{6,7},{7,6},{8,9},{9,8},{10,11... | collective-permute-start | bytes 737288 | tf_op jit(solution)/shard_map/ppermute | solution.py:290
  124.6 0.9 copy-done.11
  125.5 0.9 copy-done.13
  126.5 0.9 copy-done.15
  127.4 0.9 copy-done.22
  128.4 2.2 %shard_map.75.b = f32[5,640,384]{2,1,0:T(8,128)} custom-call(s32[1]{0:T(128)} %bitcast.7.end_ref.end, bf16[320,384]{1,0:T(8,128)(2,1)S(1)} %collective-permute-done.21.refs_0_, bf16[320,384]{1,0:T(8,128)(2,1)S(1)} %add_convert_fusion.24.refs_1_, bf16[320,384]{1,0:T(8,128)(2,1)S(1)} %collective-permute-done.19.refs_2_, ...), custom_call_target="tpu_custom_call" | custom-call | tf_op jit(solution)/shard_map/pallas_call | solution.py:222
  130.6 2.1 %shard_map.76 = f32[5,640,384]{2,1,0:T(8,128)} custom-call(s32[1]{0:T(128)} %bitcast.7.end_ref.end, f32[5,640,384]{2,1,0:T(8,128)} %shard_map.75.b, bf16[320,384]{1,0:T(8,128)(2,1)} %collective-permute-done.38.refs_0_, bf16[320,384]{1,0:T(8,128)(2,1)S(1)} %add_convert_fusion.1.refs_1_, ...), custom_call_target="tpu_custom_call", output_to_operand_aliasing={{}: (1, {})} | custom-call | tf_op jit(solution)/shard_map/pallas_call | solution.py:222
  (136 shorter events, 17.8 us)
Async XLA Ops:
  0.6 10.9 %collective-permute-start.1 = (bf16[320,1024]{1,0:T(8,128)(2,1)}, bf16[320,1024]{1,0:T(8,128)(2,1)S(1)}, u32[]{:S(2)}, u32[]{:S(2)}) collective-permute-start(bf16[320,1024]{1,0:T(8,128)(2,1)} %bitcast.9), channel_id=1, source_target_pairs={{0,4},{4,0},{8,12},{12,8},{1,5},{5,1},{9,13},{13,9},{2,6},{6,2},{1... | collective-permute-start | bytes 1966088 | tf_op jit(solution)/shard_map/ppermute | solution.py:26
  1.1 18.7 %collective-permute-start = (bf16[320,1024]{1,0:T(8,128)(2,1)}, bf16[320,1024]{1,0:T(8,128)(2,1)S(1)}, u32[]{:S(2)}, u32[]{:S(2)}) collective-permute-start(bf16[320,1024]{1,0:T(8,128)(2,1)} %bitcast.10), channel_id=1, source_target_pairs={{0,8},{4,12},{8,0},{12,4},{1,9},{5,13},{9,1},{13,5},{2,10},{6,14},... | collective-permute-start | bytes 1966088 | tf_op jit(solution)/shard_map/ppermute | solution.py:26
  4.9 17.0 %copy-start.18 = (bf16[1,512,384]{2,1,0:T(8,128)(2,1)S(1)}, bf16[1,512,384]{2,1,0:T(8,128)(2,1)}, u32[]{:S(2)}) copy-start(bf16[1,512,384]{2,1,0:T(8,128)(2,1)} %param.9) | copy-start | bytes 1179652
  5.0 3.8 %collective-permute-start.2 = (f32[8,384]{1,0:T(8,128)S(1)}, f32[8,384]{1,0:T(8,128)S(1)}, u32[]{:S(2)}, u32[]{:S(2)}) collective-permute-start(f32[8,384]{1,0:T(8,128)S(1)} %shard_map.68), channel_id=1, source_target_pairs={{0,16},{16,0},{1,17},{17,1},{2,18},{18,2},{3,19},{19,3},{4,20},{20... | collective-permute-start | bytes 36872 | tf_op jit(solution)/shard_map/ppermute | solution.py:26
  8.9 10.5 %collective-permute-start.5 = (f32[8,384]{1,0:T(8,128)S(1)}, f32[8,384]{1,0:T(8,128)S(1)}, u32[]{:S(2)}, u32[]{:S(2)}) collective-permute-start(f32[8,384]{1,0:T(8,128)S(1)} %maximum_maximum_fusion.refs_2_.refs_4_), channel_id=1, source_target_pairs={{0,12},{4,8},{8,4},{12,0},{1,13},{5,9},{9,5},{13,1},{2,14},{6,10},... | collective-permute-start | bytes 36872 | tf_op jit(solution)/shard_map/ppermute | solution.py:26
  8.9 10.9 %collective-permute-start.4 = (f32[8,384]{1,0:T(8,128)S(1)}, f32[8,384]{1,0:T(8,128)S(1)}, u32[]{:S(2)}, u32[]{:S(2)}) collective-permute-start(f32[8,384]{1,0:T(8,128)S(1)} %maximum_maximum_fusion.refs_2_.refs_4_), channel_id=1, source_target_pairs={{0,8},{4,12},{8,0},{12,4},{1,9},{5,13},{9,1},{13,5},{2,10},{6,14},... | collective-permute-start | bytes 36872 | tf_op jit(solution)/shard_map/ppermute | solution.py:26
  9.8 1.8 %collective-permute-start.3 = (f32[8,384]{1,0:T(8,128)S(1)}, f32[8,384]{1,0:T(8,128)S(1)}, u32[]{:S(2)}, u32[]{:S(2)}) collective-permute-start(f32[8,384]{1,0:T(8,128)S(1)} %maximum_maximum_fusion.refs_2_.refs_4_), channel_id=1, source_target_pairs={{0,4},{4,0},{8,12},{12,8},{1,5},{5,1},{9,13},{13,9},{2,6},{6,2},{1... | collective-permute-start | bytes 36872 | tf_op jit(solution)/shard_map/ppermute | solution.py:26
  19.8 2.1 %collective-permute-start.6 = (bf16[320,1024]{1,0:T(8,128)(2,1)S(1)}, bf16[320,1024]{1,0:T(8,128)(2,1)S(1)}, u32[]{:S(2)}, u32[]{:S(2)}) collective-permute-start(bf16[320,1024]{1,0:T(8,128)(2,1)S(1)} %collective-permute-done.refs_1_), channel_id=1, source_target_pairs={{0,4},{4,0},{8,12},{12,8},{1,5},{5,1},{9,13},{13,9},{2,6},{6,2},{1... | collective-permute-start | bytes 1966088 | tf_op jit(solution)/shard_map/ppermute | solution.py:26
  30.3 8.1 %collective-permute-start.7 = (bf16[320,384]{1,0:T(8,128)(2,1)S(1)}, bf16[320,384]{1,0:T(8,128)(2,1)S(1)}, u32[]{:S(2)}, u32[]{:S(2)}) collective-permute-start(bf16[320,384]{1,0:T(8,128)(2,1)S(1)} %get-tuple-element.67), channel_id=1, source_target_pairs={{0,16},{16,0},{1,17},{17,1},{2,18},{18,2},{3,19},{19,3},{4,20},{20... | collective-permute-start | bytes 737288 | tf_op jit(solution)/shard_map/ppermute | solution.py:26
  36.4 15.3 %collective-permute-start.9 = (bf16[320,384]{1,0:T(8,128)(2,1)S(1)}, bf16[320,384]{1,0:T(8,128)(2,1)}, u32[]{:S(2)}, u32[]{:S(2)}) collective-permute-start(bf16[320,384]{1,0:T(8,128)(2,1)S(1)} %get-tuple-element.68), channel_id=1, source_target_pairs={{0,16},{16,0},{1,17},{17,1},{2,18},{18,2},{3,19},{19,3},{4,20},{20... | collective-permute-start | bytes 737288 | tf_op jit(solution)/shard_map/ppermute | solution.py:26
  40.1 13.2 %collective-permute-start.8 = (bf16[320,384]{1,0:T(8,128)(2,1)}, bf16[320,384]{1,0:T(8,128)(2,1)}, u32[]{:S(2)}, u32[]{:S(2)}) collective-permute-start(bf16[320,384]{1,0:T(8,128)(2,1)} %add_convert_fusion.29), channel_id=1, source_target_pairs={{0,1},{1,0},{2,3},{3,2},{4,5},{5,4},{6,7},{7,6},{8,9},{9,8},{10,11... | collective-permute-start | bytes 737288 | tf_op jit(solution)/shard_map/ppermute | solution.py:290
  41.9 14.6 %collective-permute-start.10 = (bf16[512,384]{1,0:T(8,128)(2,1)}, bf16[512,384]{1,0:T(8,128)(2,1)S(1)}, u32[]{:S(2)}, u32[]{:S(2)}) collective-permute-start(bf16[512,384]{1,0:T(8,128)(2,1)} %copy-done.19), channel_id=1, source_target_pairs={{0,8},{4,12},{8,0},{12,4},{1,9},{5,13},{9,1},{13,5},{2,10},{6,14},... | collective-permute-start | bytes 1179656 | tf_op jit(solution)/shard_map/ppermute | solution.py:26
  49.5 12.4 %copy-start.26 = (bf16[640,384]{1,0:T(8,128)(2,1)S(1)}, bf16[640,384]{1,0:T(8,128)(2,1)}, u32[]{:S(2)}) copy-start(bf16[640,384]{1,0:T(8,128)(2,1)} %get-tuple-element.76) | copy-start | bytes 1474564
  49.5 12.4 %collective-permute-start.11 = (bf16[320,384]{1,0:T(8,128)(2,1)S(1)}, bf16[320,384]{1,0:T(8,128)(2,1)S(1)}, u32[]{:S(2)}, u32[]{:S(2)}) collective-permute-start(bf16[320,384]{1,0:T(8,128)(2,1)S(1)} %get-tuple-element.77), channel_id=1, source_target_pairs={{0,16},{16,0},{1,17},{17,1},{2,18},{18,2},{3,19},{19,3},{4,20},{20... | collective-permute-start | bytes 737288 | tf_op jit(solution)/shard_map/ppermute | solution.py:26
  51.6 15.7 %collective-permute-start.17 = (bf16[320,384]{1,0:T(8,128)(2,1)S(1)}, bf16[320,384]{1,0:T(8,128)(2,1)S(1)}, u32[]{:S(2)}, u32[]{:S(2)}) collective-permute-start(bf16[320,384]{1,0:T(8,128)(2,1)S(1)} %get-tuple-element.85), channel_id=1, source_target_pairs={{0,16},{16,0},{1,17},{17,1},{2,18},{18,2},{3,19},{19,3},{4,20},{20... | collective-permute-start | bytes 737288 | tf_op jit(solution)/shard_map/ppermute | solution.py:26
  52.8 13.6 %collective-permute-start.14 = (bf16[320,384]{1,0:T(8,128)(2,1)S(1)}, bf16[320,384]{1,0:T(8,128)(2,1)S(1)}, u32[]{:S(2)}, u32[]{:S(2)}) collective-permute-start(bf16[320,384]{1,0:T(8,128)(2,1)S(1)} %add_convert_fusion.28), channel_id=1, source_target_pairs={{0,1},{1,0},{2,3},{3,2},{4,5},{5,4},{6,7},{7,6},{8,9},{9,8},{10,11... | collective-permute-start | bytes 737288 | tf_op jit(solution)/shard_map/ppermute | solution.py:290
  53.3 21.0 %collective-permute-start.13 = (bf16[640,384]{1,0:T(8,128)(2,1)}, bf16[640,384]{1,0:T(8,128)(2,1)S(1)}, u32[]{:S(2)}, u32[]{:S(2)}) collective-permute-start(bf16[640,384]{1,0:T(8,128)(2,1)} %get-tuple-element.83), channel_id=1, source_target_pairs={{0,16},{16,0},{1,17},{17,1},{2,18},{18,2},{3,19},{19,3},{4,20},{20... | collective-permute-start | bytes 1474568 | tf_op jit(solution)/shard_map/ppermute | solution.py:26
  56.4 17.9 %copy-start.25 = (bf16[640,384]{1,0:T(8,128)(2,1)S(1)}, bf16[640,384]{1,0:T(8,128)(2,1)}, u32[]{:S(2)}) copy-start(bf16[640,384]{1,0:T(8,128)(2,1)} %get-tuple-element.81) | copy-start | bytes 1474564
  56.4 10.7 %collective-permute-start.18 = (bf16[320,384]{1,0:T(8,128)(2,1)S(1)}, bf16[320,384]{1,0:T(8,128)(2,1)S(1)}, u32[]{:S(2)}, u32[]{:S(2)}) collective-permute-start(bf16[320,384]{1,0:T(8,128)(2,1)S(1)} %add_convert_fusion.27), channel_id=1, source_target_pairs={{1,2},{2,1},{5,6},{6,5},{9,10},{10,9},{13,14},{14,13},{17,18},{18,... | collective-permute-start | bytes 737288 | tf_op jit(solution)/shard_map/ppermute | solution.py:296
  61.9 22.6 %copy-start.27 = (bf16[640,384]{1,0:T(8,128)(2,1)S(1)}, bf16[640,384]{1,0:T(8,128)(2,1)}, u32[]{:S(2)}) copy-start(bf16[640,384]{1,0:T(8,128)(2,1)} %get-tuple-element.101) | copy-start | bytes 1474564
  61.9 10.0 %collective-permute-start.16 = (bf16[320,384]{1,0:T(8,128)(2,1)S(1)}, bf16[320,384]{1,0:T(8,128)(2,1)S(1)}, u32[]{:S(2)}, u32[]{:S(2)}) collective-permute-start(bf16[320,384]{1,0:T(8,128)(2,1)S(1)} %add_convert_fusion.26), channel_id=1, source_target_pairs={{0,1},{1,0},{2,3},{3,2},{4,5},{5,4},{6,7},{7,6},{8,9},{9,8},{10,11... | collective-permute-start | bytes 737288 | tf_op jit(solution)/shard_map/ppermute | solution.py:290
  66.5 6.3 %collective-permute-start.15 = (bf16[320,384]{1,0:T(8,128)(2,1)S(1)}, bf16[320,384]{1,0:T(8,128)(2,1)S(1)}, u32[]{:S(2)}, u32[]{:S(2)}) collective-permute-start(bf16[320,384]{1,0:T(8,128)(2,1)S(1)} %add_convert_fusion.25), channel_id=1, source_target_pairs={{1,2},{2,1},{5,6},{6,5},{9,10},{10,9},{13,14},{14,13},{17,18},{18,... | collective-permute-start | bytes 737288 | tf_op jit(solution)/shard_map/ppermute | solution.py:296
  67.2 19.2 %collective-permute-start.12 = (bf16[640,384]{1,0:T(8,128)(2,1)}, bf16[640,384]{1,0:T(8,128)(2,1)S(1)}, u32[]{:S(2)}, u32[]{:S(2)}) collective-permute-start(bf16[640,384]{1,0:T(8,128)(2,1)} %get-tuple-element.80), channel_id=1, source_target_pairs={{0,16},{16,0},{1,17},{17,1},{2,18},{18,2},{3,19},{19,3},{4,20},{20... | collective-permute-start | bytes 1474568 | tf_op jit(solution)/shard_map/ppermute | solution.py:26
  67.4 19.2 %copy-start.24 = (bf16[640,384]{1,0:T(8,128)(2,1)S(1)}, bf16[640,384]{1,0:T(8,128)(2,1)}, u32[]{:S(2)}) copy-start(bf16[640,384]{1,0:T(8,128)(2,1)} %get-tuple-element.73) | copy-start | bytes 1474564
  67.5 10.1 %collective-permute-start.21 = (bf16[320,384]{1,0:T(8,128)(2,1)S(1)}, bf16[320,384]{1,0:T(8,128)(2,1)S(1)}, u32[]{:S(2)}, u32[]{:S(2)}) collective-permute-start(bf16[320,384]{1,0:T(8,128)(2,1)S(1)} %broadcast_select_fusion.6), channel_id=1, source_target_pairs={{0,1},{1,0},{2,3},{3,2},{4,5},{5,4},{6,7},{7,6},{8,9},{9,8},{10,11... | collective-permute-start | bytes 737288 | tf_op jit(solution)/shard_map/ppermute | solution.py:290
  72.1 6.5 %collective-permute-start.20 = (bf16[320,384]{1,0:T(8,128)(2,1)S(1)}, bf16[320,384]{1,0:T(8,128)(2,1)S(1)}, u32[]{:S(2)}, u32[]{:S(2)}) collective-permute-start(bf16[320,384]{1,0:T(8,128)(2,1)S(1)} %add_convert_fusion.22), channel_id=1, source_target_pairs={{1,2},{2,1},{5,6},{6,5},{9,10},{10,9},{13,14},{14,13},{17,18},{18,... | collective-permute-start | bytes 737288 | tf_op jit(solution)/shard_map/ppermute | solution.py:296
  74.5 9.3 %collective-permute-start.19 = (bf16[320,384]{1,0:T(8,128)(2,1)S(1)}, bf16[320,384]{1,0:T(8,128)(2,1)S(1)}, u32[]{:S(2)}, u32[]{:S(2)}) collective-permute-start(bf16[320,384]{1,0:T(8,128)(2,1)S(1)} %broadcast_select_fusion.5), channel_id=1, source_target_pairs={{0,1},{1,0},{2,3},{3,2},{4,5},{5,4},{6,7},{7,6},{8,9},{9,8},{10,11... | collective-permute-start | bytes 737288 | tf_op jit(solution)/shard_map/ppermute | solution.py:290
  77.7 18.2 %copy-start.20 = (bf16[512,384]{1,0:T(8,128)(2,1)S(1)}, bf16[512,384]{1,0:T(8,128)(2,1)}, u32[]{:S(2)}) copy-start(bf16[512,384]{1,0:T(8,128)(2,1)} %copy-done.19) | copy-start | bytes 1179652
  77.7 8.7 %collective-permute-start.24 = (bf16[320,384]{1,0:T(8,128)(2,1)S(1)}, bf16[320,384]{1,0:T(8,128)(2,1)S(1)}, u32[]{:S(2)}, u32[]{:S(2)}) collective-permute-start(bf16[320,384]{1,0:T(8,128)(2,1)S(1)} %add_convert_fusion.19), channel_id=1, source_target_pairs={{1,2},{2,1},{5,6},{6,5},{9,10},{10,9},{13,14},{14,13},{17,18},{18,... | collective-permute-start | bytes 737288 | tf_op jit(solution)/shard_map/ppermute | solution.py:296
  78.6 17.9 %copy-start.23 = (bf16[640,384]{1,0:T(8,128)(2,1)S(1)}, bf16[640,384]{1,0:T(8,128)(2,1)}, u32[]{:S(2)}) copy-start(bf16[640,384]{1,0:T(8,128)(2,1)} %get-tuple-element.78) | copy-start | bytes 1474564
  78.7 11.6 %collective-permute-start.23 = (bf16[320,384]{1,0:T(8,128)(2,1)S(1)}, bf16[320,384]{1,0:T(8,128)(2,1)S(1)}, u32[]{:S(2)}, u32[]{:S(2)}) collective-permute-start(bf16[320,384]{1,0:T(8,128)(2,1)S(1)} %broadcast_select_fusion.4), channel_id=1, source_target_pairs={{0,1},{1,0},{2,3},{3,2},{4,5},{5,4},{6,7},{7,6},{8,9},{9,8},{10,11... | collective-permute-start | bytes 737288 | tf_op jit(solution)/shard_map/ppermute | solution.py:290
  83.8 7.3 %collective-permute-start.22 = (bf16[320,384]{1,0:T(8,128)(2,1)S(1)}, bf16[320,384]{1,0:T(8,128)(2,1)S(1)}, u32[]{:S(2)}, u32[]{:S(2)}) collective-permute-start(bf16[320,384]{1,0:T(8,128)(2,1)S(1)} %add_convert_fusion.16), channel_id=1, source_target_pairs={{1,2},{2,1},{5,6},{6,5},{9,10},{10,9},{13,14},{14,13},{17,18},{18,... | collective-permute-start | bytes 737288 | tf_op jit(solution)/shard_map/ppermute | solution.py:296
  84.5 11.9 %collective-permute-start.26 = (bf16[640,384]{1,0:T(8,128)(2,1)S(1)}, bf16[640,384]{1,0:T(8,128)(2,1)S(1)}, u32[]{:S(2)}, u32[]{:S(2)}) collective-permute-start(bf16[640,384]{1,0:T(8,128)(2,1)S(1)} %copy-done.27), channel_id=1, source_target_pairs={{0,16},{16,0},{1,17},{17,1},{2,18},{18,2},{3,19},{19,3},{4,20},{20... | collective-permute-start | bytes 1474568 | tf_op jit(solution)/shard_map/ppermute | solution.py:26
  86.6 8.4 %collective-permute-start.28 = (bf16[320,384]{1,0:T(8,128)(2,1)S(1)}, bf16[320,384]{1,0:T(8,128)(2,1)S(1)}, u32[]{:S(2)}, u32[]{:S(2)}) collective-permute-start(bf16[320,384]{1,0:T(8,128)(2,1)S(1)} %broadcast_select_fusion.3), channel_id=1, source_target_pairs={{0,1},{1,0},{2,3},{3,2},{4,5},{5,4},{6,7},{7,6},{8,9},{9,8},{10,11... | collective-permute-start | bytes 737288 | tf_op jit(solution)/shard_map/ppermute | solution.py:290
  90.4 5.4 %collective-permute-start.27 = (bf16[320,384]{1,0:T(8,128)(2,1)S(1)}, bf16[320,384]{1,0:T(8,128)(2,1)S(1)}, u32[]{:S(2)}, u32[]{:S(2)}) collective-permute-start(bf16[320,384]{1,0:T(8,128)(2,1)S(1)} %add_convert_fusion.13), channel_id=1, source_target_pairs={{1,2},{2,1},{5,6},{6,5},{9,10},{10,9},{13,14},{14,13},{17,18},{18,... | collective-permute-start | bytes 737288 | tf_op jit(solution)/shard_map/ppermute | solution.py:296
  91.3 27.8 %copy-start.9 = (bf16[1536,640]{1,0:T(8,128)(2,1)S(1)}, bf16[1536,640]{1,0:T(8,128)(2,1)}, u32[]{:S(2)}) copy-start(bf16[1536,640]{1,0:T(8,128)(2,1)} %refs_8_.3) | copy-start | bytes 5898244
  91.3 10.1 %collective-permute-start.25 = (bf16[320,384]{1,0:T(8,128)(2,1)S(1)}, bf16[320,384]{1,0:T(8,128)(2,1)S(1)}, u32[]{:S(2)}, u32[]{:S(2)}) collective-permute-start(bf16[320,384]{1,0:T(8,128)(2,1)S(1)} %broadcast_select_fusion.2), channel_id=1, source_target_pairs={{0,1},{1,0},{2,3},{3,2},{4,5},{5,4},{6,7},{7,6},{8,9},{9,8},{10,11... | collective-permute-start | bytes 737288 | tf_op jit(solution)/shard_map/ppermute | solution.py:290
  95.1 7.1 %collective-permute-start.31 = (bf16[320,384]{1,0:T(8,128)(2,1)S(1)}, bf16[320,384]{1,0:T(8,128)(2,1)S(1)}, u32[]{:S(2)}, u32[]{:S(2)}) collective-permute-start(bf16[320,384]{1,0:T(8,128)(2,1)S(1)} %add_convert_fusion.10), channel_id=1, source_target_pairs={{1,2},{2,1},{5,6},{6,5},{9,10},{10,9},{13,14},{14,13},{17,18},{18,... | collective-permute-start | bytes 737288 | tf_op jit(solution)/shard_map/ppermute | solution.py:296
  95.9 23.2 %collective-permute-start.35 = (bf16[512,384]{1,0:T(8,128)(2,1)S(1)}, bf16[512,384]{1,0:T(8,128)(2,1)S(1)}, u32[]{:S(2)}, u32[]{:S(2)}) collective-permute-start(bf16[512,384]{1,0:T(8,128)(2,1)S(1)} %copy-done.20), channel_id=1, source_target_pairs={{0,4},{4,0},{8,12},{12,8},{1,5},{5,1},{9,13},{13,9},{2,6},{6,2},{1... | collective-permute-start | bytes 1179656 | tf_op jit(solution)/shard_map/ppermute | solution.py:26
  96.0 23.2 %collective-permute-start.36 = (bf16[512,384]{1,0:T(8,128)(2,1)S(1)}, bf16[512,384]{1,0:T(8,128)(2,1)S(1)}, u32[]{:S(2)}, u32[]{:S(2)}) collective-permute-start(bf16[512,384]{1,0:T(8,128)(2,1)S(1)} %collective-permute-done.10.refs_1_), channel_id=1, source_target_pairs={{0,4},{4,0},{8,12},{12,8},{1,5},{5,1},{9,13},{13,9},{2,6},{6,2},{1... | collective-permute-start | bytes 1179656 | tf_op jit(solution)/shard_map/ppermute | solution.py:26
  96.6 11.5 %collective-permute-start.30 = (bf16[320,384]{1,0:T(8,128)(2,1)S(1)}, bf16[320,384]{1,0:T(8,128)(2,1)S(1)}, u32[]{:S(2)}, u32[]{:S(2)}) collective-permute-start(bf16[320,384]{1,0:T(8,128)(2,1)S(1)} %broadcast_select_fusion.1), channel_id=1, source_target_pairs={{0,1},{1,0},{2,3},{3,2},{4,5},{5,4},{6,7},{7,6},{8,9},{9,8},{10,11... | collective-permute-start | bytes 737288 | tf_op jit(solution)/shard_map/ppermute | solution.py:290
  101.5 7.4 %collective-permute-start.29 = (bf16[320,384]{1,0:T(8,128)(2,1)S(1)}, bf16[320,384]{1,0:T(8,128)(2,1)S(1)}, u32[]{:S(2)}, u32[]{:S(2)}) collective-permute-start(bf16[320,384]{1,0:T(8,128)(2,1)S(1)} %add_convert_fusion.7), channel_id=1, source_target_pairs={{1,2},{2,1},{5,6},{6,5},{9,10},{10,9},{13,14},{14,13},{17,18},{18,... | collective-permute-start | bytes 737288 | tf_op jit(solution)/shard_map/ppermute | solution.py:296
  102.4 11.0 %collective-permute-start.34 = (bf16[320,384]{1,0:T(8,128)(2,1)S(1)}, bf16[320,384]{1,0:T(8,128)(2,1)S(1)}, u32[]{:S(2)}, u32[]{:S(2)}) collective-permute-start(bf16[320,384]{1,0:T(8,128)(2,1)S(1)} %broadcast_select_fusion), channel_id=1, source_target_pairs={{0,1},{1,0},{2,3},{3,2},{4,5},{5,4},{6,7},{7,6},{8,9},{9,8},{10,11... | collective-permute-start | bytes 737288 | tf_op jit(solution)/shard_map/ppermute | solution.py:290
  108.3 6.0 %collective-permute-start.33 = (bf16[320,384]{1,0:T(8,128)(2,1)S(1)}, bf16[320,384]{1,0:T(8,128)(2,1)S(1)}, u32[]{:S(2)}, u32[]{:S(2)}) collective-permute-start(bf16[320,384]{1,0:T(8,128)(2,1)S(1)} %add_convert_fusion.4), channel_id=1, source_target_pairs={{1,2},{2,1},{5,6},{6,5},{9,10},{10,9},{13,14},{14,13},{17,18},{18,... | collective-permute-start | bytes 737288 | tf_op jit(solution)/shard_map/ppermute | solution.py:296
  109.1 10.1 %collective-permute-start.32 = (bf16[320,384]{1,0:T(8,128)(2,1)S(1)}, bf16[320,384]{1,0:T(8,128)(2,1)S(1)}, u32[]{:S(2)}, u32[]{:S(2)}) collective-permute-start(bf16[320,384]{1,0:T(8,128)(2,1)S(1)} %add_convert_fusion.3.refs_15_), channel_id=1, source_target_pairs={{0,1},{1,0},{2,3},{3,2},{4,5},{5,4},{6,7},{7,6},{8,9},{9,8},{10,11... | collective-permute-start | bytes 737288 | tf_op jit(solution)/shard_map/ppermute | solution.py:290
  113.5 9.1 %collective-permute-start.37 = (bf16[320,384]{1,0:T(8,128)(2,1)S(1)}, bf16[320,384]{1,0:T(8,128)(2,1)S(1)}, u32[]{:S(2)}, u32[]{:S(2)}) collective-permute-start(bf16[320,384]{1,0:T(8,128)(2,1)S(1)} %add_convert_fusion.2), channel_id=1, source_target_pairs={{1,2},{2,1},{5,6},{6,5},{9,10},{10,9},{13,14},{14,13},{17,18},{18,... | collective-permute-start | bytes 737288 | tf_op jit(solution)/shard_map/ppermute | solution.py:296
  114.3 16.3 %collective-permute-start.38 = (bf16[320,384]{1,0:T(8,128)(2,1)S(1)}, bf16[320,384]{1,0:T(8,128)(2,1)}, u32[]{:S(2)}, u32[]{:S(2)}) collective-permute-start(bf16[320,384]{1,0:T(8,128)(2,1)S(1)} %add_convert_fusion.1.refs_1_), channel_id=1, source_target_pairs={{0,1},{1,0},{2,3},{3,2},{4,5},{5,4},{6,7},{7,6},{8,9},{9,8},{10,11... | collective-permute-start | bytes 737288 | tf_op jit(solution)/shard_map/ppermute | solution.py:290
  122.8 7.8 %collective-permute-start.39 = (bf16[320,384]{1,0:T(8,128)(2,1)S(1)}, bf16[320,384]{1,0:T(8,128)(2,1)}, u32[]{:S(2)}, u32[]{:S(2)}) collective-permute-start(bf16[320,384]{1,0:T(8,128)(2,1)S(1)} %add_convert_fusion.refs_3_), channel_id=1, source_target_pairs={{0,1},{1,0},{2,3},{3,2},{4,5},{5,4},{6,7},{7,6},{8,9},{9,8},{10,11... | collective-permute-start | bytes 737288 | tf_op jit(solution)/shard_map/ppermute | solution.py:290
  (20 other events, 45.4 us)

commit v13 on v10

--- a/solution.py
+++ b/solution.py
@@ -426,7 +426,10 @@
         tap, row = c // per, c % per
         rows = slice(row * depth, (row + 1) * depth)
         value = got[tap][row] if len(got[tap]) > 1 else got[tap][0][rows]
-        return added(keep[tap][rows], value if last is None else after(value, last))
+        hold = [keep[1]] if last is None else [last]
+        if c == -1:
+            hold = hold + encs[1:]
+        return added(keep[tap][rows], after(value, *hold))
 
     starts = {(k - 1) * per - 1 - (k == 3): k for k in range(2, taps)}
 

time: 130 us -> 134 us (1.031)
  starting transfers between devices: 64.4 us -> 66.1 us
  waiting for transfers between devices: 14.7 us -> 16.3 us
    ppermute x13, waiting for transfers between devices: 6.02 us -> 11.1 us  [chain_sums(): outer[r] = lax.ppermute(value, 'dp', outer_pairs)]
    ppermute x17, waiting for transfers between devices: 8.64 us -> 5.22 us  [swap(): return lax.ppermute(value, axis, [(i, i ^ bit) for i in range(peers)])]
    ppermute x13, starting transfers between devices: 40.5 us -> 41.9 us  [chain_sums(): outer[r] = lax.ppermute(value, 'dp', outer_pairs)]
    unnamed x46 -> x66, local copies, waits for them, and re-layouts: 14 us -> 14.4 us
  transfers between devices with their start and end apart: 40 -> 40, of which waited for: 9 -> 13; matrix products, arithmetic and copies ran while one was open for 5% -> 5% of each run, Pallas kernels for 16% -> 15%
where the time goes in v13:
time: 134 us; the launch traced here: 133 us
  starting transfers between devices  66.1 us (49%)
  Pallas kernels  28.4 us (21%)
  waiting for transfers between devices  16.3 us (12%)
  local copies, waits for them, and re-layouts  15.3 us (11%)
  other arithmetic  5.45 us (4%)
    ppermute x13, starting transfers between devices, chain_sums(): outer[r] = lax.ppermute(value, 'dp', outer_pairs)  41.9 us
    pallas_call x6, Pallas kernels, call(): pl.pallas_call(kernel, out_shape=out, in_specs=[pl.BlockSpec(memory_space...  23.9 us
    ppermute x17, starting transfers between devices, swap(): return lax.ppermute(value, axis, [(i, i ^ bit) for i in range(peers)])  17.2 us
    unnamed x66, local copies, waits for them, and re-layouts  14.4 us
    ppermute x13, waiting for transfers between devices, chain_sums(): outer[r] = lax.ppermute(value, 'dp', outer_pairs)  11.1 us
    ppermute x10, starting transfers between devices, chain_sums(): middle[r - 1] = lax.ppermute(last, 'dp', middle_pairs)  7.01 us
    ppermute x17, waiting for transfers between devices, swap(): return lax.ppermute(value, axis, [(i, i ^ bit) for i in range(peers)])  5.22 us
    convert_element_type x23, other arithmetic, added(): return (a.astype(F32) + b.astype(F32)).astype(BF16)  4.62 us
  transfers between devices with their start and end apart: 40, of which 13 were waited for; matrix products, arithmetic and copies ran while one was open for 5% of the time, Pallas kernels for 15%

profile of v13, /device:TPU:0, one launch (start us, length us, event | category | flops | bytes accessed | tf_op | source)
XLA Modules:
  0.0 132.8 jit_solution(10797076369729040419)
XLA Ops:
  1.1 2.6 %collective-permute-start = (bf16[320,1024]{1,0:T(8,128)(2,1)}, bf16[320,1024]{1,0:T(8,128)(2,1)S(1)}, u32[]{:S(2)}, u32[]{:S(2)}) collective-permute-start(bf16[320,1024]{1,0:T(8,128)(2,1)} %bitcast.10), channel_id=1, source_target_pairs={{0,8},{4,12},{8,0},{12,4},{1,9},{5,13},{9,1},{13,5},{2,10},{6,14},... | collective-permute-start | bytes 1966088 | tf_op jit(solution)/shard_map/ppermute | solution.py:26
  3.7 1.1 copy-done.4
  5.0 1.6 %collective-permute-start.2 = (f32[8,384]{1,0:T(8,128)S(1)}, f32[8,384]{1,0:T(8,128)S(1)}, u32[]{:S(2)}, u32[]{:S(2)}) collective-permute-start(f32[8,384]{1,0:T(8,128)S(1)} %shard_map.68), channel_id=1, source_target_pairs={{0,16},{16,0},{1,17},{17,1},{2,18},{18,2},{3,19},{19,3},{4,20},{20... | collective-permute-start | bytes 36872 | tf_op jit(solution)/shard_map/ppermute | solution.py:26
  7.3 1.4 %collective-permute-done.2 = f32[8,384]{1,0:T(8,128)S(1)} collective-permute-done((f32[8,384]{1,0:T(8,128)S(1)}, f32[8,384]{1,0:T(8,128)S(1)}, u32[]{:S(2)}, u32[]{:S(2)}) %collective-permute-start.2) | collective-permute-done | bytes 12320 | tf_op jit(solution)/shard_map/ppermute | solution.py:26
  11.6 2.4 %copy-done = bf16[5,1280,384]{2,1,0:T(8,128)(2,1)S(1)} copy-done((bf16[5,1280,384]{2,1,0:T(8,128)(2,1)S(1)}, bf16[5,1280,384]{2,1,0:T(8,128)(2,1)}, u32[]{:S(2)}) %copy-start) | copy-done | bytes 4915224
  14.0 1.1 copy-done.5
  15.1 4.3 %shard_map.69 = (f32[512,384]{1,0:T(8,128)S(1)}, f32[512,384]{1,0:T(8,128)S(1)}) custom-call(s32[2]{0:T(128)S(1)} %pad_add_fusion.idx_ref, bf16[320,1024]{1,0:T(8,128)(2,1)S(1)} %bitcast.13, bf16[320,1024]{1,0:T(8,128)(2,1)S(1)} %collective-permute-done.1.refs_1_.refs_2_, f32[8,384]{1,0:T(8,128)S(1)} %maximum_maximum_fusion.refs_2_.refs_4_, ...), custom_call_target="tpu_custom_call" | custom-call | tf_op jit(solution)/shard_map/pallas_call | solution.py:187
  20.6 1.3 collective-permute-done.6.refs_3_
  21.9 1.1 copy-done.8
  23.0 1.1 copy-done.23
  24.1 6.2 %shard_map.70 = (bf16[512,384]{1,0:T(8,128)(2,1)S(1)}, f32[1040,384]{1,0:T(8,128)S(1)}, bf16[1280,1152]{1,0:T(8,128)(2,1)S(1)}, bf16[320,384]{1,0:T(8,128)(2,1)S(1)}) custom-call(s32[2]{0:T(128)S(1)} %pad_add_fusion.idx_ref, bf16[320,1024]{1,0:T(8,128)(2,1)S(1)} %bitcast.14, bf16[320,1024]{1,0:T(8,128)(2,1)S(1)} %copy-done.23, ...), custom_call_target="tpu_custom_call" | custom-call | tf_op jit(solution)/shard_map/pallas_call | solution.py:187
  30.3 1.8 %collective-permute-start.7 = (bf16[320,384]{1,0:T(8,128)(2,1)S(1)}, bf16[320,384]{1,0:T(8,128)(2,1)S(1)}, u32[]{:S(2)}, u32[]{:S(2)}) collective-permute-start(bf16[320,384]{1,0:T(8,128)(2,1)S(1)} %get-tuple-element.68), channel_id=1, source_target_pairs={{0,16},{16,0},{1,17},{17,1},{2,18},{18,2},{3,19},{19,3},{4,20},{20... | collective-permute-start | bytes 737288 | tf_op jit(solution)/shard_map/ppermute | solution.py:26
  32.1 3.0 %shard_map.71 = (bf16[640,384]{1,0:T(8,128)(2,1)S(1)}, bf16[320,384]{1,0:T(8,128)(2,1)}) custom-call(s32[2]{0:T(128)S(1)} %pad_add_fusion.idx_ref, bf16[1280,1152]{1,0:T(8,128)(2,1)S(1)} %get-tuple-element.65.all_ref, f32[1040,384]{1,0:T(8,128)S(1)} %get-tuple-element.66.p_ref), custom_call_target="tpu_custom_call" | custom-call | tf_op jit(solution)/shard_map/pallas_call | solution.py:187
  35.4 3.5 %shard_map.72 = (bf16[640,384]{1,0:T(8,128)(2,1)S(1)}, bf16[320,384]{1,0:T(8,128)(2,1)S(1)}, bf16[320,384]{1,0:T(8,128)(2,1)S(1)}, bf16[640,384]{1,0:T(8,128)(2,1)S(1)}, bf16[640,384]{1,0:T(8,128)(2,1)S(1)}) custom-call(s32[2]{0:T(128)S(1)} %pad_add_fusion.idx_ref, bf16[1280,1152]{1,0:T(8,128)(2,1)S(1)} %get-tuple-element.65.all_ref, ...), custom_call_target="tpu_custom_call" | custom-call | tf_op jit(solution)/shard_map/pallas_call | solution.py:187
  41.4 1.8 %collective-permute-start.8 = (bf16[320,384]{1,0:T(8,128)(2,1)}, bf16[320,384]{1,0:T(8,128)(2,1)}, u32[]{:S(2)}, u32[]{:S(2)}) collective-permute-start(bf16[320,384]{1,0:T(8,128)(2,1)} %add_convert_fusion.29), channel_id=1, source_target_pairs={{0,1},{1,0},{2,3},{3,2},{4,5},{5,4},{6,7},{7,6},{8,9},{9,8},{10,11... | collective-permute-start | bytes 737288 | tf_op jit(solution)/shard_map/ppermute | solution.py:290
  43.2 1.5 %collective-permute-start.10 = (bf16[512,384]{1,0:T(8,128)(2,1)}, bf16[512,384]{1,0:T(8,128)(2,1)S(1)}, u32[]{:S(2)}, u32[]{:S(2)}) collective-permute-start(bf16[512,384]{1,0:T(8,128)(2,1)} %copy-done.26), channel_id=1, source_target_pairs={{0,8},{4,12},{8,0},{12,4},{1,9},{5,13},{9,1},{13,5},{2,10},{6,14},... | collective-permute-start | bytes 1179656 | tf_op jit(solution)/shard_map/ppermute | solution.py:26
  44.7 1.5 %collective-permute-start.11 = (bf16[320,384]{1,0:T(8,128)(2,1)}, bf16[320,384]{1,0:T(8,128)(2,1)S(1)}, u32[]{:S(2)}, u32[]{:S(2)}) collective-permute-start(bf16[320,384]{1,0:T(8,128)(2,1)} %copy-done.32), channel_id=1, source_target_pairs={{0,16},{16,0},{1,17},{17,1},{2,18},{18,2},{3,19},{19,3},{4,20},{20... | collective-permute-start | bytes 737288 | tf_op jit(solution)/shard_map/ppermute | solution.py:26
  46.8 1.1 add_convert_fusion.28
  48.4 1.4 %collective-permute-done.8 = bf16[320,384]{1,0:T(8,128)(2,1)} collective-permute-done((bf16[320,384]{1,0:T(8,128)(2,1)}, bf16[320,384]{1,0:T(8,128)(2,1)}, u32[]{:S(2)}, u32[]{:S(2)}) %collective-permute-start.8) | collective-permute-done | bytes 245792 | tf_op jit(solution)/shard_map/ppermute | solution.py:290
  49.8 1.5 %collective-permute-start.13 = (bf16[640,384]{1,0:T(8,128)(2,1)}, bf16[640,384]{1,0:T(8,128)(2,1)S(1)}, u32[]{:S(2)}, u32[]{:S(2)}) collective-permute-start(bf16[640,384]{1,0:T(8,128)(2,1)} %copy-done.30), channel_id=1, source_target_pairs={{0,16},{16,0},{1,17},{17,1},{2,18},{18,2},{3,19},{19,3},{4,20},{20... | collective-permute-start | bytes 1474568 | tf_op jit(solution)/shard_map/ppermute | solution.py:26
  51.3 1.1 add_convert_fusion.27
  52.4 1.3 collective-permute-done.10.refs_1_
  54.4 1.4 %copy-done.3 = f32[1040,384]{1,0:T(8,128)S(1)} copy-done((f32[1040,384]{1,0:T(8,128)S(1)}, f32[1040,384]{1,0:T(8,128)}, u32[]{:S(2)}) %copy-start.3) | copy-done | bytes 1597464
  55.8 3.3 %shard_map.73 = (bf16[640,384]{1,0:T(8,128)(2,1)S(1)}, bf16[640,384]{1,0:T(8,128)(2,1)S(1)}, bf16[640,384]{1,0:T(8,128)(2,1)S(1)}, bf16[640,384]{1,0:T(8,128)(2,1)S(1)}) custom-call(s32[2]{0:T(128)S(1)} %pad_add_fusion.idx_ref, bf16[1280,1152]{1,0:T(8,128)(2,1)S(1)} %get-tuple-element.65.all_ref, f32[1040,384]{1,0:T(8,128)S(1)} %copy-done.3), custom_call_target="tpu_custom_call" | custom-call | tf_op jit(solution)/shard_map/pallas_call | solution.py:187
  59.2 4.5 %collective-permute-start.16 = (bf16[320,384]{1,0:T(8,128)(2,1)S(1)}, bf16[320,384]{1,0:T(8,128)(2,1)S(1)}, u32[]{:S(2)}, u32[]{:S(2)}) collective-permute-start(bf16[320,384]{1,0:T(8,128)(2,1)S(1)} %add_convert_fusion.26), channel_id=1, source_target_pairs={{0,1},{1,0},{2,3},{3,2},{4,5},{5,4},{6,7},{7,6},{8,9},{9,8},{10,11... | collective-permute-start | bytes 737288 | tf_op jit(solution)/shard_map/ppermute | solution.py:290
  64.5 1.6 %collective-permute-start.12 = (bf16[640,384]{1,0:T(8,128)(2,1)S(1)}, bf16[640,384]{1,0:T(8,128)(2,1)S(1)}, u32[]{:S(2)}, u32[]{:S(2)}) collective-permute-start(bf16[640,384]{1,0:T(8,128)(2,1)S(1)} %get-tuple-element.82), channel_id=1, source_target_pairs={{0,16},{16,0},{1,17},{17,1},{2,18},{18,2},{3,19},{19,3},{4,20},{20... | collective-permute-start | bytes 1474568 | tf_op jit(solution)/shard_map/ppermute | solution.py:26
  66.2 1.3 %collective-permute-start.21 = (bf16[320,384]{1,0:T(8,128)(2,1)S(1)}, bf16[320,384]{1,0:T(8,128)(2,1)S(1)}, u32[]{:S(2)}, u32[]{:S(2)}) collective-permute-start(bf16[320,384]{1,0:T(8,128)(2,1)S(1)} %broadcast_select_fusion.6), channel_id=1, source_target_pairs={{0,1},{1,0},{2,3},{3,2},{4,5},{5,4},{6,7},{7,6},{8,9},{9,8},{10,11... | collective-permute-start | bytes 737288 | tf_op jit(solution)/shard_map/ppermute | solution.py:290
  67.5 1.9 %collective-permute-done.16 = bf16[320,384]{1,0:T(8,128)(2,1)S(1)} collective-permute-done((bf16[320,384]{1,0:T(8,128)(2,1)S(1)}, bf16[320,384]{1,0:T(8,128)(2,1)S(1)}, u32[]{:S(2)}, u32[]{:S(2)}) %collective-permute-start.16) | collective-permute-done | bytes 245792 | tf_op jit(solution)/shard_map/ppermute | solution.py:290
  70.4 3.8 %collective-permute-start.19 = (bf16[320,384]{1,0:T(8,128)(2,1)S(1)}, bf16[320,384]{1,0:T(8,128)(2,1)S(1)}, u32[]{:S(2)}, u32[]{:S(2)}) collective-permute-start(bf16[320,384]{1,0:T(8,128)(2,1)S(1)} %broadcast_select_fusion.5), channel_id=1, source_target_pairs={{0,1},{1,0},{2,3},{3,2},{4,5},{5,4},{6,7},{7,6},{8,9},{9,8},{10,11... | collective-permute-start | bytes 737288 | tf_op jit(solution)/shard_map/ppermute | solution.py:290
  74.2 0.9 collective-permute-done.21.refs_0_
  76.3 6.2 %collective-permute-start.23 = (bf16[320,384]{1,0:T(8,128)(2,1)S(1)}, bf16[320,384]{1,0:T(8,128)(2,1)S(1)}, u32[]{:S(2)}, u32[]{:S(2)}) collective-permute-start(bf16[320,384]{1,0:T(8,128)(2,1)S(1)} %broadcast_select_fusion.4), channel_id=1, source_target_pairs={{0,1},{1,0},{2,3},{3,2},{4,5},{5,4},{6,7},{7,6},{8,9},{9,8},{10,11... | collective-permute-start | bytes 737288 | tf_op jit(solution)/shard_map/ppermute | solution.py:290
  83.2 1.4 %collective-permute-start.26 = (bf16[640,384]{1,0:T(8,128)(2,1)S(1)}, bf16[640,384]{1,0:T(8,128)(2,1)S(1)}, u32[]{:S(2)}, u32[]{:S(2)}) collective-permute-start(bf16[640,384]{1,0:T(8,128)(2,1)S(1)} %get-tuple-element.103), channel_id=1, source_target_pairs={{0,16},{16,0},{1,17},{17,1},{2,18},{18,2},{3,19},{19,3},{4,20},{20... | collective-permute-start | bytes 1474568 | tf_op jit(solution)/shard_map/ppermute | solution.py:26
  84.9 3.3 %collective-permute-start.28 = (bf16[320,384]{1,0:T(8,128)(2,1)S(1)}, bf16[320,384]{1,0:T(8,128)(2,1)S(1)}, u32[]{:S(2)}, u32[]{:S(2)}) collective-permute-start(bf16[320,384]{1,0:T(8,128)(2,1)S(1)} %broadcast_select_fusion.3), channel_id=1, source_target_pairs={{0,1},{1,0},{2,3},{3,2},{4,5},{5,4},{6,7},{7,6},{8,9},{9,8},{10,11... | collective-permute-start | bytes 737288 | tf_op jit(solution)/shard_map/ppermute | solution.py:290
  88.2 1.0 collective-permute-done.23.refs_4_
  90.2 3.3 %collective-permute-start.25 = (bf16[320,384]{1,0:T(8,128)(2,1)S(1)}, bf16[320,384]{1,0:T(8,128)(2,1)S(1)}, u32[]{:S(2)}, u32[]{:S(2)}) collective-permute-start(bf16[320,384]{1,0:T(8,128)(2,1)S(1)} %broadcast_select_fusion.2), channel_id=1, source_target_pairs={{0,1},{1,0},{2,3},{3,2},{4,5},{5,4},{6,7},{7,6},{8,9},{9,8},{10,11... | collective-permute-start | bytes 737288 | tf_op jit(solution)/shard_map/ppermute | solution.py:290
  96.0 5.4 %collective-permute-start.30 = (bf16[320,384]{1,0:T(8,128)(2,1)S(1)}, bf16[320,384]{1,0:T(8,128)(2,1)S(1)}, u32[]{:S(2)}, u32[]{:S(2)}) collective-permute-start(bf16[320,384]{1,0:T(8,128)(2,1)S(1)} %broadcast_select_fusion.1), channel_id=1, source_target_pairs={{0,1},{1,0},{2,3},{3,2},{4,5},{5,4},{6,7},{7,6},{8,9},{9,8},{10,11... | collective-permute-start | bytes 737288 | tf_op jit(solution)/shard_map/ppermute | solution.py:290
  102.5 2.0 %collective-permute-start.34 = (bf16[320,384]{1,0:T(8,128)(2,1)S(1)}, bf16[320,384]{1,0:T(8,128)(2,1)S(1)}, u32[]{:S(2)}, u32[]{:S(2)}) collective-permute-start(bf16[320,384]{1,0:T(8,128)(2,1)S(1)} %broadcast_select_fusion), channel_id=1, source_target_pairs={{0,1},{1,0},{2,3},{3,2},{4,5},{5,4},{6,7},{7,6},{8,9},{9,8},{10,11... | collective-permute-start | bytes 737288 | tf_op jit(solution)/shard_map/ppermute | solution.py:290
  104.6 3.6 %collective-permute-done.30.refs_10_ = bf16[320,384]{1,0:T(8,128)(2,1)S(1)} collective-permute-done((bf16[320,384]{1,0:T(8,128)(2,1)S(1)}, bf16[320,384]{1,0:T(8,128)(2,1)S(1)}, u32[]{:S(2)}, u32[]{:S(2)}) %collective-permute-start.30) | collective-permute-done | bytes 245792 | tf_op jit(solution)/shard_map/ppermute | solution.py:290
  109.0 3.7 %collective-permute-start.32 = (bf16[320,384]{1,0:T(8,128)(2,1)S(1)}, bf16[320,384]{1,0:T(8,128)(2,1)S(1)}, u32[]{:S(2)}, u32[]{:S(2)}) collective-permute-start(bf16[320,384]{1,0:T(8,128)(2,1)S(1)} %add_convert_fusion.3.refs_15_), channel_id=1, source_target_pairs={{0,1},{1,0},{2,3},{3,2},{4,5},{5,4},{6,7},{7,6},{8,9},{9,8},{10,11... | collective-permute-start | bytes 737288 | tf_op jit(solution)/shard_map/ppermute | solution.py:290
  114.3 4.3 %collective-permute-start.38 = (bf16[320,384]{1,0:T(8,128)(2,1)S(1)}, bf16[320,384]{1,0:T(8,128)(2,1)}, u32[]{:S(2)}, u32[]{:S(2)}) collective-permute-start(bf16[320,384]{1,0:T(8,128)(2,1)S(1)} %add_convert_fusion.1.refs_1_), channel_id=1, source_target_pairs={{0,1},{1,0},{2,3},{3,2},{4,5},{5,4},{6,7},{7,6},{8,9},{9,8},{10,11... | collective-permute-start | bytes 737288 | tf_op jit(solution)/shard_map/ppermute | solution.py:290
  119.3 3.6 %shard_map.74 = bf16[512,640]{1,0:T(8,128)(2,1)} custom-call(s32[2]{0:T(128)S(1)} %pad_add_fusion.idx_ref, bf16[512,384]{1,0:T(8,128)(2,1)S(1)} %copy-done.27, bf16[512,384]{1,0:T(8,128)(2,1)S(1)} %collective-permute-done.10.refs_1_, bf16[512,384]{1,0:T(8,128)(2,1)S(1)} %collective-permute-done.35.refs_2_, ...), custom_call_target="tpu_custom_call" | custom-call | tf_op jit(solution)/shard_map/pallas_call | solution.py:187
  122.9 1.8 %collective-permute-start.39 = (bf16[320,384]{1,0:T(8,128)(2,1)S(1)}, bf16[320,384]{1,0:T(8,128)(2,1)}, u32[]{:S(2)}, u32[]{:S(2)}) collective-permute-start(bf16[320,384]{1,0:T(8,128)(2,1)S(1)} %add_convert_fusion.refs_3_), channel_id=1, source_target_pairs={{0,1},{1,0},{2,3},{3,2},{4,5},{5,4},{6,7},{7,6},{8,9},{9,8},{10,11... | collective-permute-start | bytes 737288 | tf_op jit(solution)/shard_map/ppermute | solution.py:290
  124.7 0.9 copy-done.17
  125.7 0.9 copy-done.19
  126.6 0.9 copy-done.21
  127.6 0.9 copy-done.29
  128.5 2.2 %shard_map.75.b = f32[5,640,384]{2,1,0:T(8,128)} custom-call(s32[1]{0:T(128)} %bitcast.7.end_ref.end, bf16[320,384]{1,0:T(8,128)(2,1)S(1)} %collective-permute-done.21.refs_0_, bf16[320,384]{1,0:T(8,128)(2,1)S(1)} %add_convert_fusion.24.refs_1_, bf16[320,384]{1,0:T(8,128)(2,1)S(1)} %collective-permute-done.19.refs_2_, ...), custom_call_target="tpu_custom_call" | custom-call | tf_op jit(solution)/shard_map/pallas_call | solution.py:222
  130.8 2.1 %shard_map.76 = f32[5,640,384]{2,1,0:T(8,128)} custom-call(s32[1]{0:T(128)} %bitcast.7.end_ref.end, f32[5,640,384]{2,1,0:T(8,128)} %shard_map.75.b, bf16[320,384]{1,0:T(8,128)(2,1)} %collective-permute-done.38.refs_0_, bf16[320,384]{1,0:T(8,128)(2,1)S(1)} %add_convert_fusion.1.refs_1_, ...), custom_call_target="tpu_custom_call", output_to_operand_aliasing={{}: (1, {})} | custom-call | tf_op jit(solution)/shard_map/pallas_call | solution.py:222
  (146 shorter events, 21.5 us)
Async XLA Ops:
  0.6 10.9 %collective-permute-start.1 = (bf16[320,1024]{1,0:T(8,128)(2,1)}, bf16[320,1024]{1,0:T(8,128)(2,1)S(1)}, u32[]{:S(2)}, u32[]{:S(2)}) collective-permute-start(bf16[320,1024]{1,0:T(8,128)(2,1)} %bitcast.9), channel_id=1, source_target_pairs={{0,4},{4,0},{8,12},{12,8},{1,5},{5,1},{9,13},{13,9},{2,6},{6,2},{1... | collective-permute-start | bytes 1966088 | tf_op jit(solution)/shard_map/ppermute | solution.py:26
  1.1 18.7 %collective-permute-start = (bf16[320,1024]{1,0:T(8,128)(2,1)}, bf16[320,1024]{1,0:T(8,128)(2,1)S(1)}, u32[]{:S(2)}, u32[]{:S(2)}) collective-permute-start(bf16[320,1024]{1,0:T(8,128)(2,1)} %bitcast.10), channel_id=1, source_target_pairs={{0,8},{4,12},{8,0},{12,4},{1,9},{5,13},{9,1},{13,5},{2,10},{6,14},... | collective-permute-start | bytes 1966088 | tf_op jit(solution)/shard_map/ppermute | solution.py:26
  4.9 17.0 %copy-start.25 = (bf16[1,512,384]{2,1,0:T(8,128)(2,1)S(1)}, bf16[1,512,384]{2,1,0:T(8,128)(2,1)}, u32[]{:S(2)}) copy-start(bf16[1,512,384]{2,1,0:T(8,128)(2,1)} %param.9) | copy-start | bytes 1179652
  5.0 3.8 %collective-permute-start.2 = (f32[8,384]{1,0:T(8,128)S(1)}, f32[8,384]{1,0:T(8,128)S(1)}, u32[]{:S(2)}, u32[]{:S(2)}) collective-permute-start(f32[8,384]{1,0:T(8,128)S(1)} %shard_map.68), channel_id=1, source_target_pairs={{0,16},{16,0},{1,17},{17,1},{2,18},{18,2},{3,19},{19,3},{4,20},{20... | collective-permute-start | bytes 36872 | tf_op jit(solution)/shard_map/ppermute | solution.py:26
  8.9 10.5 %collective-permute-start.5 = (f32[8,384]{1,0:T(8,128)S(1)}, f32[8,384]{1,0:T(8,128)S(1)}, u32[]{:S(2)}, u32[]{:S(2)}) collective-permute-start(f32[8,384]{1,0:T(8,128)S(1)} %maximum_maximum_fusion.refs_2_.refs_4_), channel_id=1, source_target_pairs={{0,12},{4,8},{8,4},{12,0},{1,13},{5,9},{9,5},{13,1},{2,14},{6,10},... | collective-permute-start | bytes 36872 | tf_op jit(solution)/shard_map/ppermute | solution.py:26
  8.9 10.9 %collective-permute-start.4 = (f32[8,384]{1,0:T(8,128)S(1)}, f32[8,384]{1,0:T(8,128)S(1)}, u32[]{:S(2)}, u32[]{:S(2)}) collective-permute-start(f32[8,384]{1,0:T(8,128)S(1)} %maximum_maximum_fusion.refs_2_.refs_4_), channel_id=1, source_target_pairs={{0,8},{4,12},{8,0},{12,4},{1,9},{5,13},{9,1},{13,5},{2,10},{6,14},... | collective-permute-start | bytes 36872 | tf_op jit(solution)/shard_map/ppermute | solution.py:26
  9.8 1.8 %collective-permute-start.3 = (f32[8,384]{1,0:T(8,128)S(1)}, f32[8,384]{1,0:T(8,128)S(1)}, u32[]{:S(2)}, u32[]{:S(2)}) collective-permute-start(f32[8,384]{1,0:T(8,128)S(1)} %maximum_maximum_fusion.refs_2_.refs_4_), channel_id=1, source_target_pairs={{0,4},{4,0},{8,12},{12,8},{1,5},{5,1},{9,13},{13,9},{2,6},{6,2},{1... | collective-permute-start | bytes 36872 | tf_op jit(solution)/shard_map/ppermute | solution.py:26
  19.8 2.1 %collective-permute-start.6 = (bf16[320,1024]{1,0:T(8,128)(2,1)S(1)}, bf16[320,1024]{1,0:T(8,128)(2,1)S(1)}, u32[]{:S(2)}, u32[]{:S(2)}) collective-permute-start(bf16[320,1024]{1,0:T(8,128)(2,1)S(1)} %collective-permute-done.refs_1_), channel_id=1, source_target_pairs={{0,4},{4,0},{8,12},{12,8},{1,5},{5,1},{9,13},{13,9},{2,6},{6,2},{1... | collective-permute-start | bytes 1966088 | tf_op jit(solution)/shard_map/ppermute | solution.py:26
  30.3 11.0 %copy-start.2 = (f32[1040,384]{1,0:T(8,128)}, f32[1040,384]{1,0:T(8,128)S(1)}, u32[]{:S(2)}) copy-start(f32[1040,384]{1,0:T(8,128)S(1)} %get-tuple-element.66.p_ref) | copy-start | bytes 4792324
  30.3 11.0 %copy-start.26 = (bf16[512,384]{1,0:T(8,128)(2,1)}, bf16[512,384]{1,0:T(8,128)(2,1)S(1)}, u32[]{:S(2)}) copy-start(bf16[512,384]{1,0:T(8,128)(2,1)S(1)} %get-tuple-element.115.refs_0_) | copy-start | bytes 1179652
  30.3 10.1 %collective-permute-start.7 = (bf16[320,384]{1,0:T(8,128)(2,1)S(1)}, bf16[320,384]{1,0:T(8,128)(2,1)S(1)}, u32[]{:S(2)}, u32[]{:S(2)}) collective-permute-start(bf16[320,384]{1,0:T(8,128)(2,1)S(1)} %get-tuple-element.68), channel_id=1, source_target_pairs={{0,16},{16,0},{1,17},{17,1},{2,18},{18,2},{3,19},{19,3},{4,20},{20... | collective-permute-start | bytes 737288 | tf_op jit(solution)/shard_map/ppermute | solution.py:26
  35.1 11.6 %collective-permute-start.9 = (bf16[320,384]{1,0:T(8,128)(2,1)}, bf16[320,384]{1,0:T(8,128)(2,1)}, u32[]{:S(2)}, u32[]{:S(2)}) collective-permute-start(bf16[320,384]{1,0:T(8,128)(2,1)} %get-tuple-element.72), channel_id=1, source_target_pairs={{0,16},{16,0},{1,17},{17,1},{2,18},{18,2},{3,19},{19,3},{4,20},{20... | collective-permute-start | bytes 737288 | tf_op jit(solution)/shard_map/ppermute | solution.py:26
  41.4 8.4 %collective-permute-start.8 = (bf16[320,384]{1,0:T(8,128)(2,1)}, bf16[320,384]{1,0:T(8,128)(2,1)}, u32[]{:S(2)}, u32[]{:S(2)}) collective-permute-start(bf16[320,384]{1,0:T(8,128)(2,1)} %add_convert_fusion.29), channel_id=1, source_target_pairs={{0,1},{1,0},{2,3},{3,2},{4,5},{5,4},{6,7},{7,6},{8,9},{9,8},{10,11... | collective-permute-start | bytes 737288 | tf_op jit(solution)/shard_map/ppermute | solution.py:290
  43.2 16.0 %copy-start.11 = (bf16[640,384]{1,0:T(8,128)(2,1)S(1)}, bf16[640,384]{1,0:T(8,128)(2,1)}, u32[]{:S(2)}) copy-start(bf16[640,384]{1,0:T(8,128)(2,1)} %copy-done.10) | copy-start | bytes 1474564
  43.2 10.5 %collective-permute-start.10 = (bf16[512,384]{1,0:T(8,128)(2,1)}, bf16[512,384]{1,0:T(8,128)(2,1)S(1)}, u32[]{:S(2)}, u32[]{:S(2)}) collective-permute-start(bf16[512,384]{1,0:T(8,128)(2,1)} %copy-done.26), channel_id=1, source_target_pairs={{0,8},{4,12},{8,0},{12,4},{1,9},{5,13},{9,1},{13,5},{2,10},{6,14},... | collective-permute-start | bytes 1179656 | tf_op jit(solution)/shard_map/ppermute | solution.py:26
  44.7 14.4 %collective-permute-start.11 = (bf16[320,384]{1,0:T(8,128)(2,1)}, bf16[320,384]{1,0:T(8,128)(2,1)S(1)}, u32[]{:S(2)}, u32[]{:S(2)}) collective-permute-start(bf16[320,384]{1,0:T(8,128)(2,1)} %copy-done.32), channel_id=1, source_target_pairs={{0,16},{16,0},{1,17},{17,1},{2,18},{18,2},{3,19},{19,3},{4,20},{20... | collective-permute-start | bytes 737288 | tf_op jit(solution)/shard_map/ppermute | solution.py:26
  46.2 19.9 %collective-permute-start.17 = (bf16[320,384]{1,0:T(8,128)(2,1)}, bf16[320,384]{1,0:T(8,128)(2,1)S(1)}, u32[]{:S(2)}, u32[]{:S(2)}) collective-permute-start(bf16[320,384]{1,0:T(8,128)(2,1)} %copy-done.31), channel_id=1, source_target_pairs={{0,16},{16,0},{1,17},{17,1},{2,18},{18,2},{3,19},{19,3},{4,20},{20... | collective-permute-start | bytes 737288 | tf_op jit(solution)/shard_map/ppermute | solution.py:26
  47.9 15.8 %collective-permute-start.14 = (bf16[320,384]{1,0:T(8,128)(2,1)S(1)}, bf16[320,384]{1,0:T(8,128)(2,1)S(1)}, u32[]{:S(2)}, u32[]{:S(2)}) collective-permute-start(bf16[320,384]{1,0:T(8,128)(2,1)S(1)} %add_convert_fusion.28), channel_id=1, source_target_pairs={{0,1},{1,0},{2,3},{3,2},{4,5},{5,4},{6,7},{7,6},{8,9},{9,8},{10,11... | collective-permute-start | bytes 737288 | tf_op jit(solution)/shard_map/ppermute | solution.py:290
  49.8 20.5 %collective-permute-start.13 = (bf16[640,384]{1,0:T(8,128)(2,1)}, bf16[640,384]{1,0:T(8,128)(2,1)S(1)}, u32[]{:S(2)}, u32[]{:S(2)}) collective-permute-start(bf16[640,384]{1,0:T(8,128)(2,1)} %copy-done.30), channel_id=1, source_target_pairs={{0,16},{16,0},{1,17},{17,1},{2,18},{18,2},{3,19},{19,3},{4,20},{20... | collective-permute-start | bytes 1474568 | tf_op jit(solution)/shard_map/ppermute | solution.py:26
  53.7 10.7 %collective-permute-start.18 = (bf16[320,384]{1,0:T(8,128)(2,1)S(1)}, bf16[320,384]{1,0:T(8,128)(2,1)S(1)}, u32[]{:S(2)}, u32[]{:S(2)}) collective-permute-start(bf16[320,384]{1,0:T(8,128)(2,1)S(1)} %add_convert_fusion.27), channel_id=1, source_target_pairs={{1,2},{2,1},{5,6},{6,5},{9,10},{10,9},{13,14},{14,13},{17,18},{18,... | collective-permute-start | bytes 737288 | tf_op jit(solution)/shard_map/ppermute | solution.py:296
  59.2 10.2 %collective-permute-start.16 = (bf16[320,384]{1,0:T(8,128)(2,1)S(1)}, bf16[320,384]{1,0:T(8,128)(2,1)S(1)}, u32[]{:S(2)}, u32[]{:S(2)}) collective-permute-start(bf16[320,384]{1,0:T(8,128)(2,1)S(1)} %add_convert_fusion.26), channel_id=1, source_target_pairs={{0,1},{1,0},{2,3},{3,2},{4,5},{5,4},{6,7},{7,6},{8,9},{9,8},{10,11... | collective-permute-start | bytes 737288 | tf_op jit(solution)/shard_map/ppermute | solution.py:290
  63.8 6.4 %collective-permute-start.15 = (bf16[320,384]{1,0:T(8,128)(2,1)S(1)}, bf16[320,384]{1,0:T(8,128)(2,1)S(1)}, u32[]{:S(2)}, u32[]{:S(2)}) collective-permute-start(bf16[320,384]{1,0:T(8,128)(2,1)S(1)} %add_convert_fusion.25), channel_id=1, source_target_pairs={{1,2},{2,1},{5,6},{6,5},{9,10},{10,9},{13,14},{14,13},{17,18},{18,... | collective-permute-start | bytes 737288 | tf_op jit(solution)/shard_map/ppermute | solution.py:296
  64.5 20.2 %collective-permute-start.12 = (bf16[640,384]{1,0:T(8,128)(2,1)S(1)}, bf16[640,384]{1,0:T(8,128)(2,1)S(1)}, u32[]{:S(2)}, u32[]{:S(2)}) collective-permute-start(bf16[640,384]{1,0:T(8,128)(2,1)S(1)} %get-tuple-element.82), channel_id=1, source_target_pairs={{0,16},{16,0},{1,17},{17,1},{2,18},{18,2},{3,19},{19,3},{4,20},{20... | collective-permute-start | bytes 1474568 | tf_op jit(solution)/shard_map/ppermute | solution.py:26
  66.2 9.0 %collective-permute-start.21 = (bf16[320,384]{1,0:T(8,128)(2,1)S(1)}, bf16[320,384]{1,0:T(8,128)(2,1)S(1)}, u32[]{:S(2)}, u32[]{:S(2)}) collective-permute-start(bf16[320,384]{1,0:T(8,128)(2,1)S(1)} %broadcast_select_fusion.6), channel_id=1, source_target_pairs={{0,1},{1,0},{2,3},{3,2},{4,5},{5,4},{6,7},{7,6},{8,9},{9,8},{10,11... | collective-permute-start | bytes 737288 | tf_op jit(solution)/shard_map/ppermute | solution.py:290
  69.5 6.6 %collective-permute-start.20 = (bf16[320,384]{1,0:T(8,128)(2,1)S(1)}, bf16[320,384]{1,0:T(8,128)(2,1)S(1)}, u32[]{:S(2)}, u32[]{:S(2)}) collective-permute-start(bf16[320,384]{1,0:T(8,128)(2,1)S(1)} %add_convert_fusion.22), channel_id=1, source_target_pairs={{1,2},{2,1},{5,6},{6,5},{9,10},{10,9},{13,14},{14,13},{17,18},{18,... | collective-permute-start | bytes 737288 | tf_op jit(solution)/shard_map/ppermute | solution.py:296
  70.4 12.0 %collective-permute-start.19 = (bf16[320,384]{1,0:T(8,128)(2,1)S(1)}, bf16[320,384]{1,0:T(8,128)(2,1)S(1)}, u32[]{:S(2)}, u32[]{:S(2)}) collective-permute-start(bf16[320,384]{1,0:T(8,128)(2,1)S(1)} %broadcast_select_fusion.5), channel_id=1, source_target_pairs={{0,1},{1,0},{2,3},{3,2},{4,5},{5,4},{6,7},{7,6},{8,9},{9,8},{10,11... | collective-permute-start | bytes 737288 | tf_op jit(solution)/shard_map/ppermute | solution.py:290
  75.3 20.0 %copy-start.27 = (bf16[512,384]{1,0:T(8,128)(2,1)S(1)}, bf16[512,384]{1,0:T(8,128)(2,1)}, u32[]{:S(2)}) copy-start(bf16[512,384]{1,0:T(8,128)(2,1)} %copy-done.26) | copy-start | bytes 1179652
  75.3 9.4 %collective-permute-start.24 = (bf16[320,384]{1,0:T(8,128)(2,1)S(1)}, bf16[320,384]{1,0:T(8,128)(2,1)S(1)}, u32[]{:S(2)}, u32[]{:S(2)}) collective-permute-start(bf16[320,384]{1,0:T(8,128)(2,1)S(1)} %add_convert_fusion.19), channel_id=1, source_target_pairs={{1,2},{2,1},{5,6},{6,5},{9,10},{10,9},{13,14},{14,13},{17,18},{18,... | collective-permute-start | bytes 737288 | tf_op jit(solution)/shard_map/ppermute | solution.py:296
  76.3 13.0 %collective-permute-start.23 = (bf16[320,384]{1,0:T(8,128)(2,1)S(1)}, bf16[320,384]{1,0:T(8,128)(2,1)S(1)}, u32[]{:S(2)}, u32[]{:S(2)}) collective-permute-start(bf16[320,384]{1,0:T(8,128)(2,1)S(1)} %broadcast_select_fusion.4), channel_id=1, source_target_pairs={{0,1},{1,0},{2,3},{3,2},{4,5},{5,4},{6,7},{7,6},{8,9},{9,8},{10,11... | collective-permute-start | bytes 737288 | tf_op jit(solution)/shard_map/ppermute | solution.py:290
  82.5 7.5 %collective-permute-start.22 = (bf16[320,384]{1,0:T(8,128)(2,1)S(1)}, bf16[320,384]{1,0:T(8,128)(2,1)S(1)}, u32[]{:S(2)}, u32[]{:S(2)}) collective-permute-start(bf16[320,384]{1,0:T(8,128)(2,1)S(1)} %add_convert_fusion.16), channel_id=1, source_target_pairs={{1,2},{2,1},{5,6},{6,5},{9,10},{10,9},{13,14},{14,13},{17,18},{18,... | collective-permute-start | bytes 737288 | tf_op jit(solution)/shard_map/ppermute | solution.py:296
  83.2 12.6 %collective-permute-start.26 = (bf16[640,384]{1,0:T(8,128)(2,1)S(1)}, bf16[640,384]{1,0:T(8,128)(2,1)S(1)}, u32[]{:S(2)}, u32[]{:S(2)}) collective-permute-start(bf16[640,384]{1,0:T(8,128)(2,1)S(1)} %get-tuple-element.103), channel_id=1, source_target_pairs={{0,16},{16,0},{1,17},{17,1},{2,18},{18,2},{3,19},{19,3},{4,20},{20... | collective-permute-start | bytes 1474568 | tf_op jit(solution)/shard_map/ppermute | solution.py:26
  84.9 9.5 %collective-permute-start.28 = (bf16[320,384]{1,0:T(8,128)(2,1)S(1)}, bf16[320,384]{1,0:T(8,128)(2,1)S(1)}, u32[]{:S(2)}, u32[]{:S(2)}) collective-permute-start(bf16[320,384]{1,0:T(8,128)(2,1)S(1)} %broadcast_select_fusion.3), channel_id=1, source_target_pairs={{0,1},{1,0},{2,3},{3,2},{4,5},{5,4},{6,7},{7,6},{8,9},{9,8},{10,11... | collective-permute-start | bytes 737288 | tf_op jit(solution)/shard_map/ppermute | solution.py:290
  89.3 5.8 %collective-permute-start.27 = (bf16[320,384]{1,0:T(8,128)(2,1)S(1)}, bf16[320,384]{1,0:T(8,128)(2,1)S(1)}, u32[]{:S(2)}, u32[]{:S(2)}) collective-permute-start(bf16[320,384]{1,0:T(8,128)(2,1)S(1)} %add_convert_fusion.13), channel_id=1, source_target_pairs={{1,2},{2,1},{5,6},{6,5},{9,10},{10,9},{13,14},{14,13},{17,18},{18,... | collective-permute-start | bytes 737288 | tf_op jit(solution)/shard_map/ppermute | solution.py:296
  90.2 29.0 %copy-start.9 = (bf16[1536,640]{1,0:T(8,128)(2,1)S(1)}, bf16[1536,640]{1,0:T(8,128)(2,1)}, u32[]{:S(2)}) copy-start(bf16[1536,640]{1,0:T(8,128)(2,1)} %refs_8_.3) | copy-start | bytes 5898244
  90.2 11.2 %collective-permute-start.25 = (bf16[320,384]{1,0:T(8,128)(2,1)S(1)}, bf16[320,384]{1,0:T(8,128)(2,1)S(1)}, u32[]{:S(2)}, u32[]{:S(2)}) collective-permute-start(bf16[320,384]{1,0:T(8,128)(2,1)S(1)} %broadcast_select_fusion.2), channel_id=1, source_target_pairs={{0,1},{1,0},{2,3},{3,2},{4,5},{5,4},{6,7},{7,6},{8,9},{9,8},{10,11... | collective-permute-start | bytes 737288 | tf_op jit(solution)/shard_map/ppermute | solution.py:290
  94.5 7.9 %collective-permute-start.31 = (bf16[320,384]{1,0:T(8,128)(2,1)S(1)}, bf16[320,384]{1,0:T(8,128)(2,1)S(1)}, u32[]{:S(2)}, u32[]{:S(2)}) collective-permute-start(bf16[320,384]{1,0:T(8,128)(2,1)S(1)} %add_convert_fusion.10), channel_id=1, source_target_pairs={{1,2},{2,1},{5,6},{6,5},{9,10},{10,9},{13,14},{14,13},{17,18},{18,... | collective-permute-start | bytes 737288 | tf_op jit(solution)/shard_map/ppermute | solution.py:296
  95.3 24.0 %collective-permute-start.35 = (bf16[512,384]{1,0:T(8,128)(2,1)S(1)}, bf16[512,384]{1,0:T(8,128)(2,1)S(1)}, u32[]{:S(2)}, u32[]{:S(2)}) collective-permute-start(bf16[512,384]{1,0:T(8,128)(2,1)S(1)} %copy-done.27), channel_id=1, source_target_pairs={{0,4},{4,0},{8,12},{12,8},{1,5},{5,1},{9,13},{13,9},{2,6},{6,2},{1... | collective-permute-start | bytes 1179656 | tf_op jit(solution)/shard_map/ppermute | solution.py:26
  95.4 23.9 %collective-permute-start.36 = (bf16[512,384]{1,0:T(8,128)(2,1)S(1)}, bf16[512,384]{1,0:T(8,128)(2,1)S(1)}, u32[]{:S(2)}, u32[]{:S(2)}) collective-permute-start(bf16[512,384]{1,0:T(8,128)(2,1)S(1)} %collective-permute-done.10.refs_1_), channel_id=1, source_target_pairs={{0,4},{4,0},{8,12},{12,8},{1,5},{5,1},{9,13},{13,9},{2,6},{6,2},{1... | collective-permute-start | bytes 1179656 | tf_op jit(solution)/shard_map/ppermute | solution.py:26
  96.0 12.1 %collective-permute-start.30 = (bf16[320,384]{1,0:T(8,128)(2,1)S(1)}, bf16[320,384]{1,0:T(8,128)(2,1)S(1)}, u32[]{:S(2)}, u32[]{:S(2)}) collective-permute-start(bf16[320,384]{1,0:T(8,128)(2,1)S(1)} %broadcast_select_fusion.1), channel_id=1, source_target_pairs={{0,1},{1,0},{2,3},{3,2},{4,5},{5,4},{6,7},{7,6},{8,9},{9,8},{10,11... | collective-permute-start | bytes 737288 | tf_op jit(solution)/shard_map/ppermute | solution.py:290
  101.5 23.2 %copy-start.13 = (bf16[320,384]{1,0:T(8,128)(2,1)S(1)}, bf16[320,384]{1,0:T(8,128)(2,1)}, u32[]{:S(2)}) copy-start(bf16[320,384]{1,0:T(8,128)(2,1)} %copy-done.12) | copy-start | bytes 737284
  101.5 23.2 %copy-start.15 = (bf16[320,384]{1,0:T(8,128)(2,1)S(1)}, bf16[320,384]{1,0:T(8,128)(2,1)}, u32[]{:S(2)}) copy-start(bf16[320,384]{1,0:T(8,128)(2,1)} %copy-done.14) | copy-start | bytes 737284
  101.5 7.4 %collective-permute-start.29 = (bf16[320,384]{1,0:T(8,128)(2,1)S(1)}, bf16[320,384]{1,0:T(8,128)(2,1)S(1)}, u32[]{:S(2)}, u32[]{:S(2)}) collective-permute-start(bf16[320,384]{1,0:T(8,128)(2,1)S(1)} %add_convert_fusion.7), channel_id=1, source_target_pairs={{1,2},{2,1},{5,6},{6,5},{9,10},{10,9},{13,14},{14,13},{17,18},{18,... | collective-permute-start | bytes 737288 | tf_op jit(solution)/shard_map/ppermute | solution.py:296
  102.5 10.9 %collective-permute-start.34 = (bf16[320,384]{1,0:T(8,128)(2,1)S(1)}, bf16[320,384]{1,0:T(8,128)(2,1)S(1)}, u32[]{:S(2)}, u32[]{:S(2)}) collective-permute-start(bf16[320,384]{1,0:T(8,128)(2,1)S(1)} %broadcast_select_fusion), channel_id=1, source_target_pairs={{0,1},{1,0},{2,3},{3,2},{4,5},{5,4},{6,7},{7,6},{8,9},{9,8},{10,11... | collective-permute-start | bytes 737288 | tf_op jit(solution)/shard_map/ppermute | solution.py:290
  108.2 6.0 %collective-permute-start.33 = (bf16[320,384]{1,0:T(8,128)(2,1)S(1)}, bf16[320,384]{1,0:T(8,128)(2,1)S(1)}, u32[]{:S(2)}, u32[]{:S(2)}) collective-permute-start(bf16[320,384]{1,0:T(8,128)(2,1)S(1)} %add_convert_fusion.4), channel_id=1, source_target_pairs={{1,2},{2,1},{5,6},{6,5},{9,10},{10,9},{13,14},{14,13},{17,18},{18,... | collective-permute-start | bytes 737288 | tf_op jit(solution)/shard_map/ppermute | solution.py:296
  109.0 10.2 %collective-permute-start.32 = (bf16[320,384]{1,0:T(8,128)(2,1)S(1)}, bf16[320,384]{1,0:T(8,128)(2,1)S(1)}, u32[]{:S(2)}, u32[]{:S(2)}) collective-permute-start(bf16[320,384]{1,0:T(8,128)(2,1)S(1)} %add_convert_fusion.3.refs_15_), channel_id=1, source_target_pairs={{0,1},{1,0},{2,3},{3,2},{4,5},{5,4},{6,7},{7,6},{8,9},{9,8},{10,11... | collective-permute-start | bytes 737288 | tf_op jit(solution)/shard_map/ppermute | solution.py:290
  113.5 9.3 %collective-permute-start.37 = (bf16[320,384]{1,0:T(8,128)(2,1)S(1)}, bf16[320,384]{1,0:T(8,128)(2,1)S(1)}, u32[]{:S(2)}, u32[]{:S(2)}) collective-permute-start(bf16[320,384]{1,0:T(8,128)(2,1)S(1)} %add_convert_fusion.2), channel_id=1, source_target_pairs={{1,2},{2,1},{5,6},{6,5},{9,10},{10,9},{13,14},{14,13},{17,18},{18,... | collective-permute-start | bytes 737288 | tf_op jit(solution)/shard_map/ppermute | solution.py:296
  114.3 16.5 %collective-permute-start.38 = (bf16[320,384]{1,0:T(8,128)(2,1)S(1)}, bf16[320,384]{1,0:T(8,128)(2,1)}, u32[]{:S(2)}, u32[]{:S(2)}) collective-permute-start(bf16[320,384]{1,0:T(8,128)(2,1)S(1)} %add_convert_fusion.1.refs_1_), channel_id=1, source_target_pairs={{0,1},{1,0},{2,3},{3,2},{4,5},{5,4},{6,7},{7,6},{8,9},{9,8},{10,11... | collective-permute-start | bytes 737288 | tf_op jit(solution)/shard_map/ppermute | solution.py:290
  122.9 7.8 %collective-permute-start.39 = (bf16[320,384]{1,0:T(8,128)(2,1)S(1)}, bf16[320,384]{1,0:T(8,128)(2,1)}, u32[]{:S(2)}, u32[]{:S(2)}) collective-permute-start(bf16[320,384]{1,0:T(8,128)(2,1)S(1)} %add_convert_fusion.refs_3_), channel_id=1, source_target_pairs={{0,1},{1,0},{2,3},{3,2},{4,5},{5,4},{6,7},{7,6},{8,9},{9,8},{10,11... | collective-permute-start | bytes 737288 | tf_op jit(solution)/shard_map/ppermute | solution.py:290
  (25 other events, 49.6 us)

commit v14 on v10

--- a/solution.py
+++ b/solution.py
@@ -228,7 +228,7 @@
         + [pl.BlockSpec((rows, width), lambda i: (0, 0))] * len(parts),
         out_specs=pl.BlockSpec((taps, shape[1], width), lambda i: (at // taps, 0, 0)),
         input_output_aliases={1: 0} if extra else {},
-        compiler_params=pltpu.CompilerParams(vmem_limit_bytes=16 * 1024 * 1024),
+        compiler_params=pltpu.CompilerParams(vmem_limit_bytes=12 * 1024 * 1024),
     )(end, *extra, *parts)
 
 
@@ -338,7 +338,7 @@
         functools.partial(first_kernel, pick(offsets, near)),
         (part, part),
         scratch(near),
-        24,
+        14,
         idx, x, own, *pick(payloads, near), conv_weight,
     )
     hold = [even] + pick(payloads, far)
@@ -359,7 +359,7 @@
             pltpu.VMEM((width // LANES, length, LANES), F32),
             pltpu.VMEM((LANES, width), F32),
         ],
-        26,
+        16,
         idx, *blocks, *payloads, conv_weight, even, odd, encoder_grad[0],
     )
     encs = [encoded]
@@ -382,7 +382,7 @@
             functools.partial(grad_kernel, group, depth, per, pieces),
             tuple(o for tap in outs for o in tap),
             [pltpu.VMEM((LANES, width * min(len(group), 2)), F32)],
-            24 if len(group) > 2 else 16,
+            24 if len(group) > 2 else 8,
             after(idx, *hold) if hold else idx, joined, pre_grad,
         )
         flat = list(flat)
@@ -393,7 +393,7 @@
         functools.partial(qkv_kernel, offsets),
         jax.ShapeDtypeStruct((half, qkv_weight.shape[1]), BF16),
         [],
-        8,
+        5,
         idx, *encs, *payloads, qkv_weight,
     )
     if not pair:

time: 130 us -> 130 us (level)
    unnamed x46 -> x48, local copies, waits for them, and re-layouts: 14 us -> 14 us
where the time goes in v14:
time: 130 us; the launch traced here: 129 us
  starting transfers between devices  64.5 us (50%)
  Pallas kernels  28.4 us (22%)
  local copies, waits for them, and re-layouts  14.9 us (11%)
  waiting for transfers between devices  14.7 us (11%)
  other arithmetic  5.31 us (4%)
    ppermute x13, starting transfers between devices, chain_sums(): outer[r] = lax.ppermute(value, 'dp', outer_pairs)  40.5 us
    pallas_call x6, Pallas kernels, call(): pl.pallas_call(kernel, out_shape=out, in_specs=[pl.BlockSpec(memory_space...  23.9 us
    ppermute x17, starting transfers between devices, swap(): return lax.ppermute(value, axis, [(i, i ^ bit) for i in range(peers)])  17.1 us
    unnamed x48, local copies, waits for them, and re-layouts  14 us
    ppermute x17, waiting for transfers between devices, swap(): return lax.ppermute(value, axis, [(i, i ^ bit) for i in range(peers)])  8.64 us
    ppermute x10, starting transfers between devices, chain_sums(): middle[r - 1] = lax.ppermute(last, 'dp', middle_pairs)  6.89 us
    ppermute x13, waiting for transfers between devices, chain_sums(): outer[r] = lax.ppermute(value, 'dp', outer_pairs)  6.02 us
    convert_element_type x23, other arithmetic, added(): return (a.astype(F32) + b.astype(F32)).astype(BF16)  4.43 us
  transfers between devices with their start and end apart: 40, of which 9 were waited for; matrix products, arithmetic and copies ran while one was open for 5% of the time, Pallas kernels for 16%

profile of v14, /device:TPU:0, one launch (start us, length us, event | category | flops | bytes accessed | tf_op | source)
XLA Modules:
  0.0 128.9 jit_solution(7376625906690643461)
XLA Ops:
  1.1 2.6 %collective-permute-start = (bf16[320,1024]{1,0:T(8,128)(2,1)}, bf16[320,1024]{1,0:T(8,128)(2,1)S(1)}, u32[]{:S(2)}, u32[]{:S(2)}) collective-permute-start(bf16[320,1024]{1,0:T(8,128)(2,1)} %bitcast.10), channel_id=1, source_target_pairs={{0,8},{4,12},{8,0},{12,4},{1,9},{5,13},{9,1},{13,5},{2,10},{6,14},... | collective-permute-start | bytes 1966088 | tf_op jit(solution)/shard_map/ppermute | solution.py:26
  3.7 1.1 copy-done.5
  5.0 1.6 %collective-permute-start.2 = (f32[8,384]{1,0:T(8,128)S(1)}, f32[8,384]{1,0:T(8,128)S(1)}, u32[]{:S(2)}, u32[]{:S(2)}) collective-permute-start(f32[8,384]{1,0:T(8,128)S(1)} %shard_map.68), channel_id=1, source_target_pairs={{0,16},{16,0},{1,17},{17,1},{2,18},{18,2},{3,19},{19,3},{4,20},{20... | collective-permute-start | bytes 36872 | tf_op jit(solution)/shard_map/ppermute | solution.py:26
  7.3 1.4 %collective-permute-done.2 = f32[8,384]{1,0:T(8,128)S(1)} collective-permute-done((f32[8,384]{1,0:T(8,128)S(1)}, f32[8,384]{1,0:T(8,128)S(1)}, u32[]{:S(2)}, u32[]{:S(2)}) %collective-permute-start.2) | collective-permute-done | bytes 12320 | tf_op jit(solution)/shard_map/ppermute | solution.py:26
  8.9 0.9 collective-permute-start.4
  9.8 0.9 collective-permute-start.3
  11.6 2.4 %copy-done = bf16[5,1280,384]{2,1,0:T(8,128)(2,1)S(1)} copy-done((bf16[5,1280,384]{2,1,0:T(8,128)(2,1)S(1)}, bf16[5,1280,384]{2,1,0:T(8,128)(2,1)}, u32[]{:S(2)}) %copy-start) | copy-done | bytes 4915224
  14.0 1.1 copy-done.6
  15.1 4.3 %shard_map.69 = (f32[512,384]{1,0:T(8,128)S(1)}, f32[512,384]{1,0:T(8,128)S(1)}) custom-call(s32[2]{0:T(128)S(1)} %pad_add_fusion.idx_ref, bf16[320,1024]{1,0:T(8,128)(2,1)S(1)} %bitcast.13, bf16[320,1024]{1,0:T(8,128)(2,1)S(1)} %collective-permute-done.1.refs_1_.refs_2_, f32[8,384]{1,0:T(8,128)S(1)} %maximum_maximum_fusion.refs_2_.refs_4_, ...), custom_call_target="tpu_custom_call" | custom-call | tf_op jit(solution)/shard_map/pallas_call | solution.py:187
  20.6 1.3 collective-permute-done.6.refs_3_
  21.9 1.1 copy-done.9
  23.0 1.1 copy-done.18
  24.1 6.2 %shard_map.70 = (bf16[512,384]{1,0:T(8,128)(2,1)S(1)}, f32[1040,384]{1,0:T(8,128)S(1)}, bf16[1280,1152]{1,0:T(8,128)(2,1)S(1)}, bf16[320,384]{1,0:T(8,128)(2,1)S(1)}) custom-call(s32[2]{0:T(128)S(1)} %pad_add_fusion.idx_ref, bf16[320,1024]{1,0:T(8,128)(2,1)S(1)} %bitcast.14, bf16[320,1024]{1,0:T(8,128)(2,1)S(1)} %copy-done.18, ...), custom_call_target="tpu_custom_call" | custom-call | tf_op jit(solution)/shard_map/pallas_call | solution.py:187
  30.3 1.8 %collective-permute-start.7 = (bf16[320,384]{1,0:T(8,128)(2,1)S(1)}, bf16[320,384]{1,0:T(8,128)(2,1)S(1)}, u32[]{:S(2)}, u32[]{:S(2)}) collective-permute-start(bf16[320,384]{1,0:T(8,128)(2,1)S(1)} %get-tuple-element.67), channel_id=1, source_target_pairs={{0,16},{16,0},{1,17},{17,1},{2,18},{18,2},{3,19},{19,3},{4,20},{20... | collective-permute-start | bytes 737288 | tf_op jit(solution)/shard_map/ppermute | solution.py:26
  32.1 3.0 %shard_map.71 = (bf16[640,384]{1,0:T(8,128)(2,1)S(1)}, bf16[320,384]{1,0:T(8,128)(2,1)}) custom-call(s32[2]{0:T(128)S(1)} %pad_add_fusion.idx_ref, bf16[1280,1152]{1,0:T(8,128)(2,1)S(1)} %get-tuple-element.64.all_ref, f32[1040,384]{1,0:T(8,128)S(1)} %get-tuple-element.65.p_ref), custom_call_target="tpu_custom_call" | custom-call | tf_op jit(solution)/shard_map/pallas_call | solution.py:187
  35.1 1.1 copy-done.2
  36.6 1.8 %collective-permute-done.7 = bf16[320,384]{1,0:T(8,128)(2,1)S(1)} collective-permute-done((bf16[320,384]{1,0:T(8,128)(2,1)S(1)}, bf16[320,384]{1,0:T(8,128)(2,1)S(1)}, u32[]{:S(2)}, u32[]{:S(2)}) %collective-permute-start.7) | collective-permute-done | bytes 245792 | tf_op jit(solution)/shard_map/ppermute | solution.py:26
  39.2 1.8 %collective-permute-start.8 = (bf16[320,384]{1,0:T(8,128)(2,1)}, bf16[320,384]{1,0:T(8,128)(2,1)}, u32[]{:S(2)}, u32[]{:S(2)}) collective-permute-start(bf16[320,384]{1,0:T(8,128)(2,1)} %add_convert_fusion.29), channel_id=1, source_target_pairs={{0,1},{1,0},{2,3},{3,2},{4,5},{5,4},{6,7},{7,6},{8,9},{9,8},{10,11... | collective-permute-start | bytes 737288 | tf_op jit(solution)/shard_map/ppermute | solution.py:290
  40.9 1.5 %collective-permute-start.10 = (bf16[512,384]{1,0:T(8,128)(2,1)}, bf16[512,384]{1,0:T(8,128)(2,1)S(1)}, u32[]{:S(2)}, u32[]{:S(2)}) collective-permute-start(bf16[512,384]{1,0:T(8,128)(2,1)} %copy-done.20), channel_id=1, source_target_pairs={{0,8},{4,12},{8,0},{12,4},{1,9},{5,13},{9,1},{13,5},{2,10},{6,14},... | collective-permute-start | bytes 1179656 | tf_op jit(solution)/shard_map/ppermute | solution.py:26
  42.5 1.4 %copy-done.3 = f32[1040,384]{1,0:T(8,128)S(1)} copy-done((f32[1040,384]{1,0:T(8,128)S(1)}, f32[1040,384]{1,0:T(8,128)}, u32[]{:S(2)}) %copy-start.3) | copy-done | bytes 1597464
  43.9 3.5 %shard_map.73 = (bf16[640,384]{1,0:T(8,128)(2,1)S(1)}, bf16[320,384]{1,0:T(8,128)(2,1)S(1)}, bf16[320,384]{1,0:T(8,128)(2,1)S(1)}, bf16[640,384]{1,0:T(8,128)(2,1)S(1)}, bf16[640,384]{1,0:T(8,128)(2,1)S(1)}) custom-call(s32[2]{0:T(128)S(1)} %pad_add_fusion.idx_ref, bf16[1280,1152]{1,0:T(8,128)(2,1)S(1)} %get-tuple-element.64.all_ref, f32[1040,384]{1,0:T(8,128)S(1)} %copy-done.3), custom_call_target="tpu_custom_call" | custom-call | tf_op jit(solution)/shard_map/pallas_call | solution.py:187
  47.4 2.1 %collective-permute-start.11 = (bf16[320,384]{1,0:T(8,128)(2,1)S(1)}, bf16[320,384]{1,0:T(8,128)(2,1)S(1)}, u32[]{:S(2)}, u32[]{:S(2)}) collective-permute-start(bf16[320,384]{1,0:T(8,128)(2,1)S(1)} %get-tuple-element.77), channel_id=1, source_target_pairs={{0,16},{16,0},{1,17},{17,1},{2,18},{18,2},{3,19},{19,3},{4,20},{20... | collective-permute-start | bytes 737288 | tf_op jit(solution)/shard_map/ppermute | solution.py:26
  49.6 1.0 add_convert_fusion.28
  51.1 1.9 %collective-permute-start.13 = (bf16[640,384]{1,0:T(8,128)(2,1)S(1)}, bf16[640,384]{1,0:T(8,128)(2,1)S(1)}, u32[]{:S(2)}, u32[]{:S(2)}) collective-permute-start(bf16[640,384]{1,0:T(8,128)(2,1)S(1)} %get-tuple-element.83), channel_id=1, source_target_pairs={{0,16},{16,0},{1,17},{17,1},{2,18},{18,2},{3,19},{19,3},{4,20},{20... | collective-permute-start | bytes 1474568 | tf_op jit(solution)/shard_map/ppermute | solution.py:26
  53.1 1.1 add_convert_fusion.27
  54.9 3.3 %shard_map.72 = (bf16[640,384]{1,0:T(8,128)(2,1)S(1)}, bf16[640,384]{1,0:T(8,128)(2,1)S(1)}, bf16[640,384]{1,0:T(8,128)(2,1)S(1)}, bf16[640,384]{1,0:T(8,128)(2,1)S(1)}) custom-call(s32[2]{0:T(128)S(1)} %pad_add_fusion.idx_ref, bf16[1280,1152]{1,0:T(8,128)(2,1)S(1)} %get-tuple-element.64.all_ref, f32[1040,384]{1,0:T(8,128)S(1)} %copy-done.4), custom_call_target="tpu_custom_call" | custom-call | tf_op jit(solution)/shard_map/pallas_call | solution.py:187
  58.3 4.5 %collective-permute-start.16 = (bf16[320,384]{1,0:T(8,128)(2,1)S(1)}, bf16[320,384]{1,0:T(8,128)(2,1)S(1)}, u32[]{:S(2)}, u32[]{:S(2)}) collective-permute-start(bf16[320,384]{1,0:T(8,128)(2,1)S(1)} %add_convert_fusion.26), channel_id=1, source_target_pairs={{0,1},{1,0},{2,3},{3,2},{4,5},{5,4},{6,7},{7,6},{8,9},{9,8},{10,11... | collective-permute-start | bytes 737288 | tf_op jit(solution)/shard_map/ppermute | solution.py:290
  63.9 1.8 %collective-permute-start.21 = (bf16[320,384]{1,0:T(8,128)(2,1)S(1)}, bf16[320,384]{1,0:T(8,128)(2,1)S(1)}, u32[]{:S(2)}, u32[]{:S(2)}) collective-permute-start(bf16[320,384]{1,0:T(8,128)(2,1)S(1)} %broadcast_select_fusion.6), channel_id=1, source_target_pairs={{0,1},{1,0},{2,3},{3,2},{4,5},{5,4},{6,7},{7,6},{8,9},{9,8},{10,11... | collective-permute-start | bytes 737288 | tf_op jit(solution)/shard_map/ppermute | solution.py:290
  65.7 2.8 %collective-permute-done.16 = bf16[320,384]{1,0:T(8,128)(2,1)S(1)} collective-permute-done((bf16[320,384]{1,0:T(8,128)(2,1)S(1)}, bf16[320,384]{1,0:T(8,128)(2,1)S(1)}, u32[]{:S(2)}, u32[]{:S(2)}) %collective-permute-start.16) | collective-permute-done | bytes 245792 | tf_op jit(solution)/shard_map/ppermute | solution.py:290
  69.3 2.9 %collective-permute-done.13 = bf16[640,384]{1,0:T(8,128)(2,1)S(1)} collective-permute-done((bf16[640,384]{1,0:T(8,128)(2,1)S(1)}, bf16[640,384]{1,0:T(8,128)(2,1)S(1)}, u32[]{:S(2)}, u32[]{:S(2)}) %collective-permute-start.13) | collective-permute-done | bytes 491552 | tf_op jit(solution)/shard_map/ppermute | solution.py:26
  72.4 1.7 %collective-permute-start.19 = (bf16[320,384]{1,0:T(8,128)(2,1)S(1)}, bf16[320,384]{1,0:T(8,128)(2,1)S(1)}, u32[]{:S(2)}, u32[]{:S(2)}) collective-permute-start(bf16[320,384]{1,0:T(8,128)(2,1)S(1)} %broadcast_select_fusion.5), channel_id=1, source_target_pairs={{0,1},{1,0},{2,3},{3,2},{4,5},{5,4},{6,7},{7,6},{8,9},{9,8},{10,11... | collective-permute-start | bytes 737288 | tf_op jit(solution)/shard_map/ppermute | solution.py:290
  75.2 4.9 %collective-permute-start.23 = (bf16[320,384]{1,0:T(8,128)(2,1)S(1)}, bf16[320,384]{1,0:T(8,128)(2,1)S(1)}, u32[]{:S(2)}, u32[]{:S(2)}) collective-permute-start(bf16[320,384]{1,0:T(8,128)(2,1)S(1)} %broadcast_select_fusion.4), channel_id=1, source_target_pairs={{0,1},{1,0},{2,3},{3,2},{4,5},{5,4},{6,7},{7,6},{8,9},{9,8},{10,11... | collective-permute-start | bytes 737288 | tf_op jit(solution)/shard_map/ppermute | solution.py:290
  80.9 2.1 %collective-permute-start.26 = (bf16[640,384]{1,0:T(8,128)(2,1)S(1)}, bf16[640,384]{1,0:T(8,128)(2,1)S(1)}, u32[]{:S(2)}, u32[]{:S(2)}) collective-permute-start(bf16[640,384]{1,0:T(8,128)(2,1)S(1)} %get-tuple-element.101), channel_id=1, source_target_pairs={{0,16},{16,0},{1,17},{17,1},{2,18},{18,2},{3,19},{19,3},{4,20},{20... | collective-permute-start | bytes 1474568 | tf_op jit(solution)/shard_map/ppermute | solution.py:26
  83.2 3.0 %collective-permute-start.28 = (bf16[320,384]{1,0:T(8,128)(2,1)S(1)}, bf16[320,384]{1,0:T(8,128)(2,1)S(1)}, u32[]{:S(2)}, u32[]{:S(2)}) collective-permute-start(bf16[320,384]{1,0:T(8,128)(2,1)S(1)} %broadcast_select_fusion.3), channel_id=1, source_target_pairs={{0,1},{1,0},{2,3},{3,2},{4,5},{5,4},{6,7},{7,6},{8,9},{9,8},{10,11... | collective-permute-start | bytes 737288 | tf_op jit(solution)/shard_map/ppermute | solution.py:290
  87.3 4.4 %collective-permute-start.25 = (bf16[320,384]{1,0:T(8,128)(2,1)S(1)}, bf16[320,384]{1,0:T(8,128)(2,1)S(1)}, u32[]{:S(2)}, u32[]{:S(2)}) collective-permute-start(bf16[320,384]{1,0:T(8,128)(2,1)S(1)} %broadcast_select_fusion.2), channel_id=1, source_target_pairs={{0,1},{1,0},{2,3},{3,2},{4,5},{5,4},{6,7},{7,6},{8,9},{9,8},{10,11... | collective-permute-start | bytes 737288 | tf_op jit(solution)/shard_map/ppermute | solution.py:290
  93.4 4.8 %collective-permute-start.30 = (bf16[320,384]{1,0:T(8,128)(2,1)S(1)}, bf16[320,384]{1,0:T(8,128)(2,1)S(1)}, u32[]{:S(2)}, u32[]{:S(2)}) collective-permute-start(bf16[320,384]{1,0:T(8,128)(2,1)S(1)} %broadcast_select_fusion.1), channel_id=1, source_target_pairs={{0,1},{1,0},{2,3},{3,2},{4,5},{5,4},{6,7},{7,6},{8,9},{9,8},{10,11... | collective-permute-start | bytes 737288 | tf_op jit(solution)/shard_map/ppermute | solution.py:290
  99.1 2.8 %collective-permute-start.34 = (bf16[320,384]{1,0:T(8,128)(2,1)S(1)}, bf16[320,384]{1,0:T(8,128)(2,1)S(1)}, u32[]{:S(2)}, u32[]{:S(2)}) collective-permute-start(bf16[320,384]{1,0:T(8,128)(2,1)S(1)} %broadcast_select_fusion), channel_id=1, source_target_pairs={{0,1},{1,0},{2,3},{3,2},{4,5},{5,4},{6,7},{7,6},{8,9},{9,8},{10,11... | collective-permute-start | bytes 737288 | tf_op jit(solution)/shard_map/ppermute | solution.py:290
  101.9 3.0 %collective-permute-done.30.refs_10_ = bf16[320,384]{1,0:T(8,128)(2,1)S(1)} collective-permute-done((bf16[320,384]{1,0:T(8,128)(2,1)S(1)}, bf16[320,384]{1,0:T(8,128)(2,1)S(1)}, u32[]{:S(2)}, u32[]{:S(2)}) %collective-permute-start.30) | collective-permute-done | bytes 245792 | tf_op jit(solution)/shard_map/ppermute | solution.py:290
  105.8 4.3 %collective-permute-start.32 = (bf16[320,384]{1,0:T(8,128)(2,1)S(1)}, bf16[320,384]{1,0:T(8,128)(2,1)S(1)}, u32[]{:S(2)}, u32[]{:S(2)}) collective-permute-start(bf16[320,384]{1,0:T(8,128)(2,1)S(1)} %add_convert_fusion.3.refs_15_), channel_id=1, source_target_pairs={{0,1},{1,0},{2,3},{3,2},{4,5},{5,4},{6,7},{7,6},{8,9},{9,8},{10,11... | collective-permute-start | bytes 737288 | tf_op jit(solution)/shard_map/ppermute | solution.py:290
  111.0 4.3 %collective-permute-start.38 = (bf16[320,384]{1,0:T(8,128)(2,1)S(1)}, bf16[320,384]{1,0:T(8,128)(2,1)}, u32[]{:S(2)}, u32[]{:S(2)}) collective-permute-start(bf16[320,384]{1,0:T(8,128)(2,1)S(1)} %add_convert_fusion.1.refs_1_), channel_id=1, source_target_pairs={{0,1},{1,0},{2,3},{3,2},{4,5},{5,4},{6,7},{7,6},{8,9},{9,8},{10,11... | collective-permute-start | bytes 737288 | tf_op jit(solution)/shard_map/ppermute | solution.py:290
  115.4 3.5 %shard_map.74 = bf16[512,640]{1,0:T(8,128)(2,1)} custom-call(s32[2]{0:T(128)S(1)} %pad_add_fusion.idx_ref, bf16[512,384]{1,0:T(8,128)(2,1)S(1)} %copy-done.21, bf16[512,384]{1,0:T(8,128)(2,1)S(1)} %collective-permute-done.10.refs_1_, bf16[512,384]{1,0:T(8,128)(2,1)S(1)} %collective-permute-done.35.refs_2_, ...), custom_call_target="tpu_custom_call" | custom-call | tf_op jit(solution)/shard_map/pallas_call | solution.py:187
  119.0 1.8 %collective-permute-start.39 = (bf16[320,384]{1,0:T(8,128)(2,1)S(1)}, bf16[320,384]{1,0:T(8,128)(2,1)}, u32[]{:S(2)}, u32[]{:S(2)}) collective-permute-start(bf16[320,384]{1,0:T(8,128)(2,1)S(1)} %add_convert_fusion.refs_3_), channel_id=1, source_target_pairs={{0,1},{1,0},{2,3},{3,2},{4,5},{5,4},{6,7},{7,6},{8,9},{9,8},{10,11... | collective-permute-start | bytes 737288 | tf_op jit(solution)/shard_map/ppermute | solution.py:290
  120.8 0.9 copy-done.12
  121.8 0.9 copy-done.14
  122.7 0.9 copy-done.16
  123.6 0.9 copy-done.23
  124.6 2.2 %shard_map.75.b = f32[5,640,384]{2,1,0:T(8,128)} custom-call(s32[1]{0:T(128)} %bitcast.7.end_ref.end, bf16[320,384]{1,0:T(8,128)(2,1)S(1)} %collective-permute-done.21.refs_0_, bf16[320,384]{1,0:T(8,128)(2,1)S(1)} %add_convert_fusion.24.refs_1_, bf16[320,384]{1,0:T(8,128)(2,1)S(1)} %collective-permute-done.19.refs_2_, ...), custom_call_target="tpu_custom_call" | custom-call | tf_op jit(solution)/shard_map/pallas_call | solution.py:222
  126.8 2.1 %shard_map.76 = f32[5,640,384]{2,1,0:T(8,128)} custom-call(s32[1]{0:T(128)} %bitcast.7.end_ref.end, f32[5,640,384]{2,1,0:T(8,128)} %shard_map.75.b, bf16[320,384]{1,0:T(8,128)(2,1)} %collective-permute-done.38.refs_0_, bf16[320,384]{1,0:T(8,128)(2,1)S(1)} %add_convert_fusion.1.refs_1_, ...), custom_call_target="tpu_custom_call", output_to_operand_aliasing={{}: (1, {})} | custom-call | tf_op jit(solution)/shard_map/pallas_call | solution.py:222
  (128 shorter events, 15.6 us)
Async XLA Ops:
  0.6 10.9 %collective-permute-start.1 = (bf16[320,1024]{1,0:T(8,128)(2,1)}, bf16[320,1024]{1,0:T(8,128)(2,1)S(1)}, u32[]{:S(2)}, u32[]{:S(2)}) collective-permute-start(bf16[320,1024]{1,0:T(8,128)(2,1)} %bitcast.9), channel_id=1, source_target_pairs={{0,4},{4,0},{8,12},{12,8},{1,5},{5,1},{9,13},{13,9},{2,6},{6,2},{1... | collective-permute-start | bytes 1966088 | tf_op jit(solution)/shard_map/ppermute | solution.py:26
  1.1 18.7 %collective-permute-start = (bf16[320,1024]{1,0:T(8,128)(2,1)}, bf16[320,1024]{1,0:T(8,128)(2,1)S(1)}, u32[]{:S(2)}, u32[]{:S(2)}) collective-permute-start(bf16[320,1024]{1,0:T(8,128)(2,1)} %bitcast.10), channel_id=1, source_target_pairs={{0,8},{4,12},{8,0},{12,4},{1,9},{5,13},{9,1},{13,5},{2,10},{6,14},... | collective-permute-start | bytes 1966088 | tf_op jit(solution)/shard_map/ppermute | solution.py:26
  4.9 17.0 %copy-start.19 = (bf16[1,512,384]{2,1,0:T(8,128)(2,1)S(1)}, bf16[1,512,384]{2,1,0:T(8,128)(2,1)}, u32[]{:S(2)}) copy-start(bf16[1,512,384]{2,1,0:T(8,128)(2,1)} %param.9) | copy-start | bytes 1179652
  5.0 3.8 %collective-permute-start.2 = (f32[8,384]{1,0:T(8,128)S(1)}, f32[8,384]{1,0:T(8,128)S(1)}, u32[]{:S(2)}, u32[]{:S(2)}) collective-permute-start(f32[8,384]{1,0:T(8,128)S(1)} %shard_map.68), channel_id=1, source_target_pairs={{0,16},{16,0},{1,17},{17,1},{2,18},{18,2},{3,19},{19,3},{4,20},{20... | collective-permute-start | bytes 36872 | tf_op jit(solution)/shard_map/ppermute | solution.py:26
  8.9 10.5 %collective-permute-start.5 = (f32[8,384]{1,0:T(8,128)S(1)}, f32[8,384]{1,0:T(8,128)S(1)}, u32[]{:S(2)}, u32[]{:S(2)}) collective-permute-start(f32[8,384]{1,0:T(8,128)S(1)} %maximum_maximum_fusion.refs_2_.refs_4_), channel_id=1, source_target_pairs={{0,12},{4,8},{8,4},{12,0},{1,13},{5,9},{9,5},{13,1},{2,14},{6,10},... | collective-permute-start | bytes 36872 | tf_op jit(solution)/shard_map/ppermute | solution.py:26
  8.9 10.9 %collective-permute-start.4 = (f32[8,384]{1,0:T(8,128)S(1)}, f32[8,384]{1,0:T(8,128)S(1)}, u32[]{:S(2)}, u32[]{:S(2)}) collective-permute-start(f32[8,384]{1,0:T(8,128)S(1)} %maximum_maximum_fusion.refs_2_.refs_4_), channel_id=1, source_target_pairs={{0,8},{4,12},{8,0},{12,4},{1,9},{5,13},{9,1},{13,5},{2,10},{6,14},... | collective-permute-start | bytes 36872 | tf_op jit(solution)/shard_map/ppermute | solution.py:26
  9.8 1.8 %collective-permute-start.3 = (f32[8,384]{1,0:T(8,128)S(1)}, f32[8,384]{1,0:T(8,128)S(1)}, u32[]{:S(2)}, u32[]{:S(2)}) collective-permute-start(f32[8,384]{1,0:T(8,128)S(1)} %maximum_maximum_fusion.refs_2_.refs_4_), channel_id=1, source_target_pairs={{0,4},{4,0},{8,12},{12,8},{1,5},{5,1},{9,13},{13,9},{2,6},{6,2},{1... | collective-permute-start | bytes 36872 | tf_op jit(solution)/shard_map/ppermute | solution.py:26
  15.1 6.9 %copy-start.8 = (bf16[320,1024]{1,0:T(8,128)(2,1)}, bf16[320,1024]{1,0:T(8,128)(2,1)S(1)}, u32[]{:S(2)}) copy-start(bf16[320,1024]{1,0:T(8,128)(2,1)S(1)} %collective-permute-done.1.refs_1_.refs_2_) | copy-start | bytes 1966084
  15.1 6.9 %copy-start.1 = (bf16[5,1280,384]{2,1,0:T(8,128)(2,1)S(1)}, bf16[5,1280,384]{2,1,0:T(8,128)(2,1)}, u32[]{:S(2)}) copy-start(bf16[5,1280,384]{2,1,0:T(8,128)(2,1)} %refs_8_.2) | copy-start | bytes 14745604
  15.1 6.9 %copy-start.7 = (bf16[1,1024,320]{1,2,0:T(8,128)(2,1)S(1)}, bf16[1,1024,320]{1,2,0:T(8,128)(2,1)}, u32[]{:S(2)}) copy-start(bf16[1,1024,320]{1,2,0:T(8,128)(2,1)} %param.5) | copy-start | bytes 1966084
  19.8 2.1 %collective-permute-start.6 = (bf16[320,1024]{1,0:T(8,128)(2,1)S(1)}, bf16[320,1024]{1,0:T(8,128)(2,1)S(1)}, u32[]{:S(2)}, u32[]{:S(2)}) collective-permute-start(bf16[320,1024]{1,0:T(8,128)(2,1)S(1)} %collective-permute-done.refs_1_), channel_id=1, source_target_pairs={{0,4},{4,0},{8,12},{12,8},{1,5},{5,1},{9,13},{13,9},{2,6},{6,2},{1... | collective-permute-start | bytes 1966088 | tf_op jit(solution)/shard_map/ppermute | solution.py:26
  30.3 4.8 %copy-start.20 = (bf16[512,384]{1,0:T(8,128)(2,1)}, bf16[512,384]{1,0:T(8,128)(2,1)S(1)}, u32[]{:S(2)}) copy-start(bf16[512,384]{1,0:T(8,128)(2,1)S(1)} %get-tuple-element.113.refs_0_) | copy-start | bytes 1179652
  30.3 8.1 %collective-permute-start.7 = (bf16[320,384]{1,0:T(8,128)(2,1)S(1)}, bf16[320,384]{1,0:T(8,128)(2,1)S(1)}, u32[]{:S(2)}, u32[]{:S(2)}) collective-permute-start(bf16[320,384]{1,0:T(8,128)(2,1)S(1)} %get-tuple-element.67), channel_id=1, source_target_pairs={{0,16},{16,0},{1,17},{17,1},{2,18},{18,2},{3,19},{19,3},{4,20},{20... | collective-permute-start | bytes 737288 | tf_op jit(solution)/shard_map/ppermute | solution.py:26
  36.3 13.3 %collective-permute-start.9 = (bf16[320,384]{1,0:T(8,128)(2,1)}, bf16[320,384]{1,0:T(8,128)(2,1)}, u32[]{:S(2)}, u32[]{:S(2)}) collective-permute-start(bf16[320,384]{1,0:T(8,128)(2,1)} %get-tuple-element.68), channel_id=1, source_target_pairs={{0,16},{16,0},{1,17},{17,1},{2,18},{18,2},{3,19},{19,3},{4,20},{20... | collective-permute-start | bytes 737288 | tf_op jit(solution)/shard_map/ppermute | solution.py:26
  39.2 11.9 %collective-permute-start.8 = (bf16[320,384]{1,0:T(8,128)(2,1)}, bf16[320,384]{1,0:T(8,128)(2,1)}, u32[]{:S(2)}, u32[]{:S(2)}) collective-permute-start(bf16[320,384]{1,0:T(8,128)(2,1)} %add_convert_fusion.29), channel_id=1, source_target_pairs={{0,1},{1,0},{2,3},{3,2},{4,5},{5,4},{6,7},{7,6},{8,9},{9,8},{10,11... | collective-permute-start | bytes 737288 | tf_op jit(solution)/shard_map/ppermute | solution.py:290
  40.9 13.3 %collective-permute-start.10 = (bf16[512,384]{1,0:T(8,128)(2,1)}, bf16[512,384]{1,0:T(8,128)(2,1)S(1)}, u32[]{:S(2)}, u32[]{:S(2)}) collective-permute-start(bf16[512,384]{1,0:T(8,128)(2,1)} %copy-done.20), channel_id=1, source_target_pairs={{0,8},{4,12},{8,0},{12,4},{1,9},{5,13},{9,1},{13,5},{2,10},{6,14},... | collective-permute-start | bytes 1179656 | tf_op jit(solution)/shard_map/ppermute | solution.py:26
  43.9 11.0 %copy-start.4 = (f32[1040,384]{1,0:T(8,128)S(1)}, f32[1040,384]{1,0:T(8,128)}, u32[]{:S(2)}) copy-start(f32[1040,384]{1,0:T(8,128)} %copy-done.2) | copy-start | bytes 4792324
  47.4 10.8 %collective-permute-start.11 = (bf16[320,384]{1,0:T(8,128)(2,1)S(1)}, bf16[320,384]{1,0:T(8,128)(2,1)S(1)}, u32[]{:S(2)}, u32[]{:S(2)}) collective-permute-start(bf16[320,384]{1,0:T(8,128)(2,1)S(1)} %get-tuple-element.77), channel_id=1, source_target_pairs={{0,16},{16,0},{1,17},{17,1},{2,18},{18,2},{3,19},{19,3},{4,20},{20... | collective-permute-start | bytes 737288 | tf_op jit(solution)/shard_map/ppermute | solution.py:26
  49.5 14.2 %collective-permute-start.17 = (bf16[320,384]{1,0:T(8,128)(2,1)S(1)}, bf16[320,384]{1,0:T(8,128)(2,1)S(1)}, u32[]{:S(2)}, u32[]{:S(2)}) collective-permute-start(bf16[320,384]{1,0:T(8,128)(2,1)S(1)} %get-tuple-element.85), channel_id=1, source_target_pairs={{0,16},{16,0},{1,17},{17,1},{2,18},{18,2},{3,19},{19,3},{4,20},{20... | collective-permute-start | bytes 737288 | tf_op jit(solution)/shard_map/ppermute | solution.py:26
  50.6 12.2 %collective-permute-start.14 = (bf16[320,384]{1,0:T(8,128)(2,1)S(1)}, bf16[320,384]{1,0:T(8,128)(2,1)S(1)}, u32[]{:S(2)}, u32[]{:S(2)}) collective-permute-start(bf16[320,384]{1,0:T(8,128)(2,1)S(1)} %add_convert_fusion.28), channel_id=1, source_target_pairs={{0,1},{1,0},{2,3},{3,2},{4,5},{5,4},{6,7},{7,6},{8,9},{9,8},{10,11... | collective-permute-start | bytes 737288 | tf_op jit(solution)/shard_map/ppermute | solution.py:290
  51.1 21.1 %collective-permute-start.13 = (bf16[640,384]{1,0:T(8,128)(2,1)S(1)}, bf16[640,384]{1,0:T(8,128)(2,1)S(1)}, u32[]{:S(2)}, u32[]{:S(2)}) collective-permute-start(bf16[640,384]{1,0:T(8,128)(2,1)S(1)} %get-tuple-element.83), channel_id=1, source_target_pairs={{0,16},{16,0},{1,17},{17,1},{2,18},{18,2},{3,19},{19,3},{4,20},{20... | collective-permute-start | bytes 1474568 | tf_op jit(solution)/shard_map/ppermute | solution.py:26
  54.2 9.3 %collective-permute-start.18 = (bf16[320,384]{1,0:T(8,128)(2,1)S(1)}, bf16[320,384]{1,0:T(8,128)(2,1)S(1)}, u32[]{:S(2)}, u32[]{:S(2)}) collective-permute-start(bf16[320,384]{1,0:T(8,128)(2,1)S(1)} %add_convert_fusion.27), channel_id=1, source_target_pairs={{1,2},{2,1},{5,6},{6,5},{9,10},{10,9},{13,14},{14,13},{17,18},{18,... | collective-permute-start | bytes 737288 | tf_op jit(solution)/shard_map/ppermute | solution.py:296
  58.3 10.2 %collective-permute-start.16 = (bf16[320,384]{1,0:T(8,128)(2,1)S(1)}, bf16[320,384]{1,0:T(8,128)(2,1)S(1)}, u32[]{:S(2)}, u32[]{:S(2)}) collective-permute-start(bf16[320,384]{1,0:T(8,128)(2,1)S(1)} %add_convert_fusion.26), channel_id=1, source_target_pairs={{0,1},{1,0},{2,3},{3,2},{4,5},{5,4},{6,7},{7,6},{8,9},{9,8},{10,11... | collective-permute-start | bytes 737288 | tf_op jit(solution)/shard_map/ppermute | solution.py:290
  62.9 6.4 %collective-permute-start.15 = (bf16[320,384]{1,0:T(8,128)(2,1)S(1)}, bf16[320,384]{1,0:T(8,128)(2,1)S(1)}, u32[]{:S(2)}, u32[]{:S(2)}) collective-permute-start(bf16[320,384]{1,0:T(8,128)(2,1)S(1)} %add_convert_fusion.25), channel_id=1, source_target_pairs={{1,2},{2,1},{5,6},{6,5},{9,10},{10,9},{13,14},{14,13},{17,18},{18,... | collective-permute-start | bytes 737288 | tf_op jit(solution)/shard_map/ppermute | solution.py:296
  63.6 19.4 %collective-permute-start.12 = (bf16[640,384]{1,0:T(8,128)(2,1)S(1)}, bf16[640,384]{1,0:T(8,128)(2,1)S(1)}, u32[]{:S(2)}, u32[]{:S(2)}) collective-permute-start(bf16[640,384]{1,0:T(8,128)(2,1)S(1)} %get-tuple-element.80), channel_id=1, source_target_pairs={{0,16},{16,0},{1,17},{17,1},{2,18},{18,2},{3,19},{19,3},{4,20},{20... | collective-permute-start | bytes 1474568 | tf_op jit(solution)/shard_map/ppermute | solution.py:26
  63.9 10.2 %collective-permute-start.21 = (bf16[320,384]{1,0:T(8,128)(2,1)S(1)}, bf16[320,384]{1,0:T(8,128)(2,1)S(1)}, u32[]{:S(2)}, u32[]{:S(2)}) collective-permute-start(bf16[320,384]{1,0:T(8,128)(2,1)S(1)} %broadcast_select_fusion.6), channel_id=1, source_target_pairs={{0,1},{1,0},{2,3},{3,2},{4,5},{5,4},{6,7},{7,6},{8,9},{9,8},{10,11... | collective-permute-start | bytes 737288 | tf_op jit(solution)/shard_map/ppermute | solution.py:290
  68.6 6.5 %collective-permute-start.20 = (bf16[320,384]{1,0:T(8,128)(2,1)S(1)}, bf16[320,384]{1,0:T(8,128)(2,1)S(1)}, u32[]{:S(2)}, u32[]{:S(2)}) collective-permute-start(bf16[320,384]{1,0:T(8,128)(2,1)S(1)} %add_convert_fusion.22), channel_id=1, source_target_pairs={{1,2},{2,1},{5,6},{6,5},{9,10},{10,9},{13,14},{14,13},{17,18},{18,... | collective-permute-start | bytes 737288 | tf_op jit(solution)/shard_map/ppermute | solution.py:296
  72.4 7.7 %collective-permute-start.19 = (bf16[320,384]{1,0:T(8,128)(2,1)S(1)}, bf16[320,384]{1,0:T(8,128)(2,1)S(1)}, u32[]{:S(2)}, u32[]{:S(2)}) collective-permute-start(bf16[320,384]{1,0:T(8,128)(2,1)S(1)} %broadcast_select_fusion.5), channel_id=1, source_target_pairs={{0,1},{1,0},{2,3},{3,2},{4,5},{5,4},{6,7},{7,6},{8,9},{9,8},{10,11... | collective-permute-start | bytes 737288 | tf_op jit(solution)/shard_map/ppermute | solution.py:290
  74.2 18.5 %copy-start.21 = (bf16[512,384]{1,0:T(8,128)(2,1)S(1)}, bf16[512,384]{1,0:T(8,128)(2,1)}, u32[]{:S(2)}) copy-start(bf16[512,384]{1,0:T(8,128)(2,1)} %copy-done.20) | copy-start | bytes 1179652
  74.2 8.8 %collective-permute-start.24 = (bf16[320,384]{1,0:T(8,128)(2,1)S(1)}, bf16[320,384]{1,0:T(8,128)(2,1)S(1)}, u32[]{:S(2)}, u32[]{:S(2)}) collective-permute-start(bf16[320,384]{1,0:T(8,128)(2,1)S(1)} %add_convert_fusion.19), channel_id=1, source_target_pairs={{1,2},{2,1},{5,6},{6,5},{9,10},{10,9},{13,14},{14,13},{17,18},{18,... | collective-permute-start | bytes 737288 | tf_op jit(solution)/shard_map/ppermute | solution.py:296
  75.2 11.1 %collective-permute-start.23 = (bf16[320,384]{1,0:T(8,128)(2,1)S(1)}, bf16[320,384]{1,0:T(8,128)(2,1)S(1)}, u32[]{:S(2)}, u32[]{:S(2)}) collective-permute-start(bf16[320,384]{1,0:T(8,128)(2,1)S(1)} %broadcast_select_fusion.4), channel_id=1, source_target_pairs={{0,1},{1,0},{2,3},{3,2},{4,5},{5,4},{6,7},{7,6},{8,9},{9,8},{10,11... | collective-permute-start | bytes 737288 | tf_op jit(solution)/shard_map/ppermute | solution.py:290
  80.2 6.9 %collective-permute-start.22 = (bf16[320,384]{1,0:T(8,128)(2,1)S(1)}, bf16[320,384]{1,0:T(8,128)(2,1)S(1)}, u32[]{:S(2)}, u32[]{:S(2)}) collective-permute-start(bf16[320,384]{1,0:T(8,128)(2,1)S(1)} %add_convert_fusion.16), channel_id=1, source_target_pairs={{1,2},{2,1},{5,6},{6,5},{9,10},{10,9},{13,14},{14,13},{17,18},{18,... | collective-permute-start | bytes 737288 | tf_op jit(solution)/shard_map/ppermute | solution.py:296
  80.9 12.3 %collective-permute-start.26 = (bf16[640,384]{1,0:T(8,128)(2,1)S(1)}, bf16[640,384]{1,0:T(8,128)(2,1)S(1)}, u32[]{:S(2)}, u32[]{:S(2)}) collective-permute-start(bf16[640,384]{1,0:T(8,128)(2,1)S(1)} %get-tuple-element.101), channel_id=1, source_target_pairs={{0,16},{16,0},{1,17},{17,1},{2,18},{18,2},{3,19},{19,3},{4,20},{20... | collective-permute-start | bytes 1474568 | tf_op jit(solution)/shard_map/ppermute | solution.py:26
  83.2 8.5 %collective-permute-start.28 = (bf16[320,384]{1,0:T(8,128)(2,1)S(1)}, bf16[320,384]{1,0:T(8,128)(2,1)S(1)}, u32[]{:S(2)}, u32[]{:S(2)}) collective-permute-start(bf16[320,384]{1,0:T(8,128)(2,1)S(1)} %broadcast_select_fusion.3), channel_id=1, source_target_pairs={{0,1},{1,0},{2,3},{3,2},{4,5},{5,4},{6,7},{7,6},{8,9},{9,8},{10,11... | collective-permute-start | bytes 737288 | tf_op jit(solution)/shard_map/ppermute | solution.py:290
  86.4 6.1 %collective-permute-start.27 = (bf16[320,384]{1,0:T(8,128)(2,1)S(1)}, bf16[320,384]{1,0:T(8,128)(2,1)S(1)}, u32[]{:S(2)}, u32[]{:S(2)}) collective-permute-start(bf16[320,384]{1,0:T(8,128)(2,1)S(1)} %add_convert_fusion.13), channel_id=1, source_target_pairs={{1,2},{2,1},{5,6},{6,5},{9,10},{10,9},{13,14},{14,13},{17,18},{18,... | collective-permute-start | bytes 737288 | tf_op jit(solution)/shard_map/ppermute | solution.py:296
  87.3 28.1 %copy-start.10 = (bf16[1536,640]{1,0:T(8,128)(2,1)S(1)}, bf16[1536,640]{1,0:T(8,128)(2,1)}, u32[]{:S(2)}) copy-start(bf16[1536,640]{1,0:T(8,128)(2,1)} %refs_8_.3) | copy-start | bytes 5898244
  87.3 10.8 %collective-permute-start.25 = (bf16[320,384]{1,0:T(8,128)(2,1)S(1)}, bf16[320,384]{1,0:T(8,128)(2,1)S(1)}, u32[]{:S(2)}, u32[]{:S(2)}) collective-permute-start(bf16[320,384]{1,0:T(8,128)(2,1)S(1)} %broadcast_select_fusion.2), channel_id=1, source_target_pairs={{0,1},{1,0},{2,3},{3,2},{4,5},{5,4},{6,7},{7,6},{8,9},{9,8},{10,11... | collective-permute-start | bytes 737288 | tf_op jit(solution)/shard_map/ppermute | solution.py:290
  91.9 7.1 %collective-permute-start.31 = (bf16[320,384]{1,0:T(8,128)(2,1)S(1)}, bf16[320,384]{1,0:T(8,128)(2,1)S(1)}, u32[]{:S(2)}, u32[]{:S(2)}) collective-permute-start(bf16[320,384]{1,0:T(8,128)(2,1)S(1)} %add_convert_fusion.10), channel_id=1, source_target_pairs={{1,2},{2,1},{5,6},{6,5},{9,10},{10,9},{13,14},{14,13},{17,18},{18,... | collective-permute-start | bytes 737288 | tf_op jit(solution)/shard_map/ppermute | solution.py:296
  92.6 22.7 %collective-permute-start.35 = (bf16[512,384]{1,0:T(8,128)(2,1)S(1)}, bf16[512,384]{1,0:T(8,128)(2,1)S(1)}, u32[]{:S(2)}, u32[]{:S(2)}) collective-permute-start(bf16[512,384]{1,0:T(8,128)(2,1)S(1)} %copy-done.21), channel_id=1, source_target_pairs={{0,4},{4,0},{8,12},{12,8},{1,5},{5,1},{9,13},{13,9},{2,6},{6,2},{1... | collective-permute-start | bytes 1179656 | tf_op jit(solution)/shard_map/ppermute | solution.py:26
  92.7 22.6 %collective-permute-start.36 = (bf16[512,384]{1,0:T(8,128)(2,1)S(1)}, bf16[512,384]{1,0:T(8,128)(2,1)S(1)}, u32[]{:S(2)}, u32[]{:S(2)}) collective-permute-start(bf16[512,384]{1,0:T(8,128)(2,1)S(1)} %collective-permute-done.10.refs_1_), channel_id=1, source_target_pairs={{0,4},{4,0},{8,12},{12,8},{1,5},{5,1},{9,13},{13,9},{2,6},{6,2},{1... | collective-permute-start | bytes 1179656 | tf_op jit(solution)/shard_map/ppermute | solution.py:26
  93.4 11.5 %collective-permute-start.30 = (bf16[320,384]{1,0:T(8,128)(2,1)S(1)}, bf16[320,384]{1,0:T(8,128)(2,1)S(1)}, u32[]{:S(2)}, u32[]{:S(2)}) collective-permute-start(bf16[320,384]{1,0:T(8,128)(2,1)S(1)} %broadcast_select_fusion.1), channel_id=1, source_target_pairs={{0,1},{1,0},{2,3},{3,2},{4,5},{5,4},{6,7},{7,6},{8,9},{9,8},{10,11... | collective-permute-start | bytes 737288 | tf_op jit(solution)/shard_map/ppermute | solution.py:290
  98.3 7.4 %collective-permute-start.29 = (bf16[320,384]{1,0:T(8,128)(2,1)S(1)}, bf16[320,384]{1,0:T(8,128)(2,1)S(1)}, u32[]{:S(2)}, u32[]{:S(2)}) collective-permute-start(bf16[320,384]{1,0:T(8,128)(2,1)S(1)} %add_convert_fusion.7), channel_id=1, source_target_pairs={{1,2},{2,1},{5,6},{6,5},{9,10},{10,9},{13,14},{14,13},{17,18},{18,... | collective-permute-start | bytes 737288 | tf_op jit(solution)/shard_map/ppermute | solution.py:296
  99.1 11.0 %collective-permute-start.34 = (bf16[320,384]{1,0:T(8,128)(2,1)S(1)}, bf16[320,384]{1,0:T(8,128)(2,1)S(1)}, u32[]{:S(2)}, u32[]{:S(2)}) collective-permute-start(bf16[320,384]{1,0:T(8,128)(2,1)S(1)} %broadcast_select_fusion), channel_id=1, source_target_pairs={{0,1},{1,0},{2,3},{3,2},{4,5},{5,4},{6,7},{7,6},{8,9},{9,8},{10,11... | collective-permute-start | bytes 737288 | tf_op jit(solution)/shard_map/ppermute | solution.py:290
  105.0 5.9 %collective-permute-start.33 = (bf16[320,384]{1,0:T(8,128)(2,1)S(1)}, bf16[320,384]{1,0:T(8,128)(2,1)S(1)}, u32[]{:S(2)}, u32[]{:S(2)}) collective-permute-start(bf16[320,384]{1,0:T(8,128)(2,1)S(1)} %add_convert_fusion.4), channel_id=1, source_target_pairs={{1,2},{2,1},{5,6},{6,5},{9,10},{10,9},{13,14},{14,13},{17,18},{18,... | collective-permute-start | bytes 737288 | tf_op jit(solution)/shard_map/ppermute | solution.py:296
  105.8 9.6 %collective-permute-start.32 = (bf16[320,384]{1,0:T(8,128)(2,1)S(1)}, bf16[320,384]{1,0:T(8,128)(2,1)S(1)}, u32[]{:S(2)}, u32[]{:S(2)}) collective-permute-start(bf16[320,384]{1,0:T(8,128)(2,1)S(1)} %add_convert_fusion.3.refs_15_), channel_id=1, source_target_pairs={{0,1},{1,0},{2,3},{3,2},{4,5},{5,4},{6,7},{7,6},{8,9},{9,8},{10,11... | collective-permute-start | bytes 737288 | tf_op jit(solution)/shard_map/ppermute | solution.py:290
  110.2 8.7 %collective-permute-start.37 = (bf16[320,384]{1,0:T(8,128)(2,1)S(1)}, bf16[320,384]{1,0:T(8,128)(2,1)S(1)}, u32[]{:S(2)}, u32[]{:S(2)}) collective-permute-start(bf16[320,384]{1,0:T(8,128)(2,1)S(1)} %add_convert_fusion.2), channel_id=1, source_target_pairs={{1,2},{2,1},{5,6},{6,5},{9,10},{10,9},{13,14},{14,13},{17,18},{18,... | collective-permute-start | bytes 737288 | tf_op jit(solution)/shard_map/ppermute | solution.py:296
  111.0 15.8 %collective-permute-start.38 = (bf16[320,384]{1,0:T(8,128)(2,1)S(1)}, bf16[320,384]{1,0:T(8,128)(2,1)}, u32[]{:S(2)}, u32[]{:S(2)}) collective-permute-start(bf16[320,384]{1,0:T(8,128)(2,1)S(1)} %add_convert_fusion.1.refs_1_), channel_id=1, source_target_pairs={{0,1},{1,0},{2,3},{3,2},{4,5},{5,4},{6,7},{7,6},{8,9},{9,8},{10,11... | collective-permute-start | bytes 737288 | tf_op jit(solution)/shard_map/ppermute | solution.py:290
  119.0 7.8 %collective-permute-start.39 = (bf16[320,384]{1,0:T(8,128)(2,1)S(1)}, bf16[320,384]{1,0:T(8,128)(2,1)}, u32[]{:S(2)}, u32[]{:S(2)}) collective-permute-start(bf16[320,384]{1,0:T(8,128)(2,1)S(1)} %add_convert_fusion.refs_3_), channel_id=1, source_target_pairs={{0,1},{1,0},{2,3},{3,2},{4,5},{5,4},{6,7},{7,6},{8,9},{9,8},{10,11... | collective-permute-start | bytes 737288 | tf_op jit(solution)/shard_map/ppermute | solution.py:290
  (16 other events, 19.9 us)

commit v15 on v10

--- a/solution.py
+++ b/solution.py
@@ -198,13 +198,16 @@
     return lax.optimization_barrier((value, *others))[0]
 
 
-def write_kernel(end_ref, *refs):
+def write_kernel(each, end_ref, *refs):
     *part_refs, out_ref = refs
-    count = len(part_refs) // 2
+    count = len(part_refs) // each
     pieces = count // out_ref.shape[0]
     rows = part_refs[0].shape[0]
     for i in range(count):
         tap, r = i // pieces, i % pieces
+        if each == 1:
+            out_ref[tap, r * rows : (r + 1) * rows, :] = part_refs[i][...].astype(F32)
+            continue
         for ref, here in ((part_refs[2 * i], end_ref[0] > 0), (part_refs[2 * i + 1], end_ref[0] == 0)):
 
             @pl.when(here)
@@ -215,10 +218,13 @@
 def written(parts, taps, at, buffer, shape):
     me = lax.axis_index("dp")
     end = jnp.logical_or(me == 0, me == lax.axis_size("dp") - 1).astype(jnp.int32).reshape(1)
-    parts = [v for pair in parts for v in pair]
+    each = len(parts[0])
+    parts = [v for part in parts for v in part]
     rows, width = parts[0].shape
     extra = [] if buffer is None else [buffer]
-    kernel = write_kernel if buffer is None else lambda end, b, *refs: write_kernel(end, *refs)
+    kernel = functools.partial(write_kernel, each)
+    if buffer is not None:
+        kernel = lambda end, b, *refs: write_kernel(each, end, *refs)
     return pl.pallas_call(
         kernel,
         out_shape=jax.ShapeDtypeStruct(shape, F32),
@@ -455,8 +461,11 @@
     sums = chain_sums(chunks, share, sent, idle)
     shape = (taps, per * depth, width)
     conv_grad, early = done["early"], done["at"]
+    me = lax.axis_index("dp")
+    end = jnp.logical_or(me == 0, me == lax.axis_size("dp") - 1)
     for k in range(early, taps):
-        conv_grad = written(sums[k * per : (k + 1) * per], 1, k, conv_grad, shape)
+        parts = [(jnp.where(end, got, own),) for got, own in sums[k * per : (k + 1) * per]]
+        conv_grad = written(parts, 1, k, conv_grad, shape)
     return (done["qkv"][None], jnp.swapaxes(conv_grad, 0, 1))
 
 

time: 130 us -> 130 us (level)
  other arithmetic: 5.25 us -> 7.76 us
  local copies, waits for them, and re-layouts: 14.9 us -> 13 us
  waiting for transfers between devices: 14.7 us -> 16.1 us
    unnamed x46 -> x38, local copies, waits for them, and re-layouts: 14 us -> 12.1 us
    ppermute x13, waiting for transfers between devices: 6.02 us -> 7.43 us  [chain_sums(): outer[r] = lax.ppermute(value, 'dp', outer_pairs)]
    convert_element_type x23, other arithmetic: 4.42 us -> 5.81 us  [added(): return (a.astype(F32) + b.astype(F32)).astype(BF16)]
  transfers between devices with their start and end apart: 40 -> 40, of which waited for: 9 -> 10; matrix products, arithmetic and copies ran while one was open for 5% -> 6% of each run, Pallas kernels for 16% -> 16%
where the time goes in v15:
time: 130 us; the launch traced here: 129 us
  starting transfers between devices  63.6 us (49%)
  Pallas kernels  27.3 us (21%)
  waiting for transfers between devices  16.1 us (12%)
  local copies, waits for them, and re-layouts  13 us (10%)
  other arithmetic  7.76 us (6%)
    ppermute x13, starting transfers between devices, chain_sums(): outer[r] = lax.ppermute(value, 'dp', outer_pairs)  39.6 us
    pallas_call x6, Pallas kernels, call(): pl.pallas_call(kernel, out_shape=out, in_specs=[pl.BlockSpec(memory_space...  23.9 us
    ppermute x17, starting transfers between devices, swap(): return lax.ppermute(value, axis, [(i, i ^ bit) for i in range(peers)])  17.1 us
    unnamed x38, local copies, waits for them, and re-layouts  12.1 us
    ppermute x17, waiting for transfers between devices, swap(): return lax.ppermute(value, axis, [(i, i ^ bit) for i in range(peers)])  8.67 us
    ppermute x13, waiting for transfers between devices, chain_sums(): outer[r] = lax.ppermute(value, 'dp', outer_pairs)  7.43 us
    ppermute x10, starting transfers between devices, chain_sums(): middle[r - 1] = lax.ppermute(last, 'dp', middle_pairs)  6.89 us
    convert_element_type x23, other arithmetic, added(): return (a.astype(F32) + b.astype(F32)).astype(BF16)  5.81 us
  transfers between devices with their start and end apart: 40, of which 10 were waited for; matrix products, arithmetic and copies ran while one was open for 6% of the time, Pallas kernels for 16%

profile of v15, /device:TPU:0, one launch (start us, length us, event | category | flops | bytes accessed | tf_op | source)
XLA Modules:
  0.0 128.9 jit_solution(11612286041427982901)
XLA Ops:
  1.1 2.6 %collective-permute-start = (bf16[320,1024]{1,0:T(8,128)(2,1)}, bf16[320,1024]{1,0:T(8,128)(2,1)S(1)}, u32[]{:S(2)}, u32[]{:S(2)}) collective-permute-start(bf16[320,1024]{1,0:T(8,128)(2,1)} %bitcast.10), channel_id=1, source_target_pairs={{0,8},{4,12},{8,0},{12,4},{1,9},{5,13},{9,1},{13,5},{2,10},{6,14},... | collective-permute-start | bytes 1966088 | tf_op jit(solution)/shard_map/ppermute | solution.py:26
  3.7 1.1 copy-done.4
  5.0 1.6 %collective-permute-start.2 = (f32[8,384]{1,0:T(8,128)S(1)}, f32[8,384]{1,0:T(8,128)S(1)}, u32[]{:S(2)}, u32[]{:S(2)}) collective-permute-start(f32[8,384]{1,0:T(8,128)S(1)} %shard_map.68), channel_id=1, source_target_pairs={{0,16},{16,0},{1,17},{17,1},{2,18},{18,2},{3,19},{19,3},{4,20},{20... | collective-permute-start | bytes 36872 | tf_op jit(solution)/shard_map/ppermute | solution.py:26
  7.3 1.4 %collective-permute-done.2 = f32[8,384]{1,0:T(8,128)S(1)} collective-permute-done((f32[8,384]{1,0:T(8,128)S(1)}, f32[8,384]{1,0:T(8,128)S(1)}, u32[]{:S(2)}, u32[]{:S(2)}) %collective-permute-start.2) | collective-permute-done | bytes 12320 | tf_op jit(solution)/shard_map/ppermute | solution.py:26
  8.9 0.9 collective-permute-start.4
  9.8 0.9 collective-permute-start.3
  11.6 2.4 %copy-done = bf16[5,1280,384]{2,1,0:T(8,128)(2,1)S(1)} copy-done((bf16[5,1280,384]{2,1,0:T(8,128)(2,1)S(1)}, bf16[5,1280,384]{2,1,0:T(8,128)(2,1)}, u32[]{:S(2)}) %copy-start) | copy-done | bytes 4915224
  14.0 1.1 copy-done.5
  15.1 4.3 %shard_map.69 = (f32[512,384]{1,0:T(8,128)S(1)}, f32[512,384]{1,0:T(8,128)S(1)}) custom-call(s32[2]{0:T(128)S(1)} %pad_add_fusion.idx_ref, bf16[320,1024]{1,0:T(8,128)(2,1)S(1)} %bitcast.13, bf16[320,1024]{1,0:T(8,128)(2,1)S(1)} %collective-permute-done.1.refs_1_.refs_2_, f32[8,384]{1,0:T(8,128)S(1)} %maximum_maximum_fusion.refs_2_.refs_4_, ...), custom_call_target="tpu_custom_call" | custom-call | tf_op jit(solution)/shard_map/pallas_call | solution.py:187
  20.6 1.3 collective-permute-done.6.refs_3_
  21.9 1.1 copy-done.8
  23.0 1.1 copy-done.13
  24.1 6.2 %shard_map.70 = (bf16[512,384]{1,0:T(8,128)(2,1)S(1)}, f32[1040,384]{1,0:T(8,128)S(1)}, bf16[1280,1152]{1,0:T(8,128)(2,1)S(1)}, bf16[320,384]{1,0:T(8,128)(2,1)S(1)}) custom-call(s32[2]{0:T(128)S(1)} %pad_add_fusion.idx_ref, bf16[320,1024]{1,0:T(8,128)(2,1)S(1)} %bitcast.14, bf16[320,1024]{1,0:T(8,128)(2,1)S(1)} %copy-done.13, ...), custom_call_target="tpu_custom_call" | custom-call | tf_op jit(solution)/shard_map/pallas_call | solution.py:187
  30.3 1.8 %collective-permute-start.7 = (bf16[320,384]{1,0:T(8,128)(2,1)S(1)}, bf16[320,384]{1,0:T(8,128)(2,1)S(1)}, u32[]{:S(2)}, u32[]{:S(2)}) collective-permute-start(bf16[320,384]{1,0:T(8,128)(2,1)S(1)} %get-tuple-element.67), channel_id=1, source_target_pairs={{0,16},{16,0},{1,17},{17,1},{2,18},{18,2},{3,19},{19,3},{4,20},{20... | collective-permute-start | bytes 737288 | tf_op jit(solution)/shard_map/ppermute | solution.py:26
  32.1 3.0 %shard_map.71 = (bf16[640,384]{1,0:T(8,128)(2,1)S(1)}, bf16[320,384]{1,0:T(8,128)(2,1)}) custom-call(s32[2]{0:T(128)S(1)} %pad_add_fusion.idx_ref, bf16[1280,1152]{1,0:T(8,128)(2,1)S(1)} %get-tuple-element.64.all_ref, f32[1040,384]{1,0:T(8,128)S(1)} %get-tuple-element.65.p_ref), custom_call_target="tpu_custom_call" | custom-call | tf_op jit(solution)/shard_map/pallas_call | solution.py:187
  35.1 1.1 copy-done.2
  36.6 1.9 %collective-permute-done.7 = bf16[320,384]{1,0:T(8,128)(2,1)S(1)} collective-permute-done((bf16[320,384]{1,0:T(8,128)(2,1)S(1)}, bf16[320,384]{1,0:T(8,128)(2,1)S(1)}, u32[]{:S(2)}, u32[]{:S(2)}) %collective-permute-start.7) | collective-permute-done | bytes 245792 | tf_op jit(solution)/shard_map/ppermute | solution.py:26
  39.2 1.8 %collective-permute-start.8 = (bf16[320,384]{1,0:T(8,128)(2,1)}, bf16[320,384]{1,0:T(8,128)(2,1)}, u32[]{:S(2)}, u32[]{:S(2)}) collective-permute-start(bf16[320,384]{1,0:T(8,128)(2,1)} %add_convert_fusion.29), channel_id=1, source_target_pairs={{0,1},{1,0},{2,3},{3,2},{4,5},{5,4},{6,7},{7,6},{8,9},{9,8},{10,11... | collective-permute-start | bytes 737288 | tf_op jit(solution)/shard_map/ppermute | solution.py:296
  41.0 1.5 %collective-permute-start.10 = (bf16[512,384]{1,0:T(8,128)(2,1)}, bf16[512,384]{1,0:T(8,128)(2,1)S(1)}, u32[]{:S(2)}, u32[]{:S(2)}) collective-permute-start(bf16[512,384]{1,0:T(8,128)(2,1)} %copy-done.15), channel_id=1, source_target_pairs={{0,8},{4,12},{8,0},{12,4},{1,9},{5,13},{9,1},{13,5},{2,10},{6,14},... | collective-permute-start | bytes 1179656 | tf_op jit(solution)/shard_map/ppermute | solution.py:26
  42.5 1.4 %copy-done.3 = f32[1040,384]{1,0:T(8,128)S(1)} copy-done((f32[1040,384]{1,0:T(8,128)S(1)}, f32[1040,384]{1,0:T(8,128)}, u32[]{:S(2)}) %copy-start.3) | copy-done | bytes 1597464
  43.9 3.5 %shard_map.73 = (bf16[640,384]{1,0:T(8,128)(2,1)S(1)}, bf16[320,384]{1,0:T(8,128)(2,1)S(1)}, bf16[320,384]{1,0:T(8,128)(2,1)S(1)}, bf16[640,384]{1,0:T(8,128)(2,1)S(1)}, bf16[640,384]{1,0:T(8,128)(2,1)S(1)}) custom-call(s32[2]{0:T(128)S(1)} %pad_add_fusion.idx_ref, bf16[1280,1152]{1,0:T(8,128)(2,1)S(1)} %get-tuple-element.64.all_ref, f32[1040,384]{1,0:T(8,128)S(1)} %copy-done.3), custom_call_target="tpu_custom_call" | custom-call | tf_op jit(solution)/shard_map/pallas_call | solution.py:187
  47.4 2.1 %collective-permute-start.11 = (bf16[320,384]{1,0:T(8,128)(2,1)S(1)}, bf16[320,384]{1,0:T(8,128)(2,1)S(1)}, u32[]{:S(2)}, u32[]{:S(2)}) collective-permute-start(bf16[320,384]{1,0:T(8,128)(2,1)S(1)} %get-tuple-element.77), channel_id=1, source_target_pairs={{0,16},{16,0},{1,17},{17,1},{2,18},{18,2},{3,19},{19,3},{4,20},{20... | collective-permute-start | bytes 737288 | tf_op jit(solution)/shard_map/ppermute | solution.py:26
  49.6 1.0 add_convert_fusion.28
  51.1 1.9 %collective-permute-start.13 = (bf16[640,384]{1,0:T(8,128)(2,1)S(1)}, bf16[640,384]{1,0:T(8,128)(2,1)S(1)}, u32[]{:S(2)}, u32[]{:S(2)}) collective-permute-start(bf16[640,384]{1,0:T(8,128)(2,1)S(1)} %get-tuple-element.83), channel_id=1, source_target_pairs={{0,16},{16,0},{1,17},{17,1},{2,18},{18,2},{3,19},{19,3},{4,20},{20... | collective-permute-start | bytes 1474568 | tf_op jit(solution)/shard_map/ppermute | solution.py:26
  53.1 1.1 add_convert_fusion.27
  54.9 3.3 %shard_map.72 = (bf16[640,384]{1,0:T(8,128)(2,1)S(1)}, bf16[640,384]{1,0:T(8,128)(2,1)S(1)}, bf16[640,384]{1,0:T(8,128)(2,1)S(1)}, bf16[640,384]{1,0:T(8,128)(2,1)S(1)}) custom-call(s32[2]{0:T(128)S(1)} %pad_add_fusion.idx_ref, bf16[1280,1152]{1,0:T(8,128)(2,1)S(1)} %get-tuple-element.64.all_ref, f32[1040,384]{1,0:T(8,128)S(1)} %copy-done.3), custom_call_target="tpu_custom_call" | custom-call | tf_op jit(solution)/shard_map/pallas_call | solution.py:187
  58.3 4.5 %collective-permute-start.16 = (bf16[320,384]{1,0:T(8,128)(2,1)S(1)}, bf16[320,384]{1,0:T(8,128)(2,1)S(1)}, u32[]{:S(2)}, u32[]{:S(2)}) collective-permute-start(bf16[320,384]{1,0:T(8,128)(2,1)S(1)} %add_convert_fusion.26), channel_id=1, source_target_pairs={{0,1},{1,0},{2,3},{3,2},{4,5},{5,4},{6,7},{7,6},{8,9},{9,8},{10,11... | collective-permute-start | bytes 737288 | tf_op jit(solution)/shard_map/ppermute | solution.py:296
  63.9 1.8 %collective-permute-start.21 = (bf16[320,384]{1,0:T(8,128)(2,1)S(1)}, bf16[320,384]{1,0:T(8,128)(2,1)S(1)}, u32[]{:S(2)}, u32[]{:S(2)}) collective-permute-start(bf16[320,384]{1,0:T(8,128)(2,1)S(1)} %broadcast_select_fusion.8), channel_id=1, source_target_pairs={{0,1},{1,0},{2,3},{3,2},{4,5},{5,4},{6,7},{7,6},{8,9},{9,8},{10,11... | collective-permute-start | bytes 737288 | tf_op jit(solution)/shard_map/ppermute | solution.py:296
  65.7 2.8 %collective-permute-done.16 = bf16[320,384]{1,0:T(8,128)(2,1)S(1)} collective-permute-done((bf16[320,384]{1,0:T(8,128)(2,1)S(1)}, bf16[320,384]{1,0:T(8,128)(2,1)S(1)}, u32[]{:S(2)}, u32[]{:S(2)}) %collective-permute-start.16) | collective-permute-done | bytes 245792 | tf_op jit(solution)/shard_map/ppermute | solution.py:296
  69.3 2.9 %collective-permute-done.13 = bf16[640,384]{1,0:T(8,128)(2,1)S(1)} collective-permute-done((bf16[640,384]{1,0:T(8,128)(2,1)S(1)}, bf16[640,384]{1,0:T(8,128)(2,1)S(1)}, u32[]{:S(2)}, u32[]{:S(2)}) %collective-permute-start.13) | collective-permute-done | bytes 491552 | tf_op jit(solution)/shard_map/ppermute | solution.py:26
  72.4 1.7 %collective-permute-start.19 = (bf16[320,384]{1,0:T(8,128)(2,1)S(1)}, bf16[320,384]{1,0:T(8,128)(2,1)S(1)}, u32[]{:S(2)}, u32[]{:S(2)}) collective-permute-start(bf16[320,384]{1,0:T(8,128)(2,1)S(1)} %broadcast_select_fusion.7), channel_id=1, source_target_pairs={{0,1},{1,0},{2,3},{3,2},{4,5},{5,4},{6,7},{7,6},{8,9},{9,8},{10,11... | collective-permute-start | bytes 737288 | tf_op jit(solution)/shard_map/ppermute | solution.py:296
  75.2 4.9 %collective-permute-start.23 = (bf16[320,384]{1,0:T(8,128)(2,1)S(1)}, bf16[320,384]{1,0:T(8,128)(2,1)S(1)}, u32[]{:S(2)}, u32[]{:S(2)}) collective-permute-start(bf16[320,384]{1,0:T(8,128)(2,1)S(1)} %broadcast_select_fusion.6), channel_id=1, source_target_pairs={{0,1},{1,0},{2,3},{3,2},{4,5},{5,4},{6,7},{7,6},{8,9},{9,8},{10,11... | collective-permute-start | bytes 737288 | tf_op jit(solution)/shard_map/ppermute | solution.py:296
  80.9 2.1 %collective-permute-start.26 = (bf16[640,384]{1,0:T(8,128)(2,1)S(1)}, bf16[640,384]{1,0:T(8,128)(2,1)S(1)}, u32[]{:S(2)}, u32[]{:S(2)}) collective-permute-start(bf16[640,384]{1,0:T(8,128)(2,1)S(1)} %get-tuple-element.101), channel_id=1, source_target_pairs={{0,16},{16,0},{1,17},{17,1},{2,18},{18,2},{3,19},{19,3},{4,20},{20... | collective-permute-start | bytes 1474568 | tf_op jit(solution)/shard_map/ppermute | solution.py:26
  83.2 3.0 %collective-permute-start.28 = (bf16[320,384]{1,0:T(8,128)(2,1)S(1)}, bf16[320,384]{1,0:T(8,128)(2,1)S(1)}, u32[]{:S(2)}, u32[]{:S(2)}) collective-permute-start(bf16[320,384]{1,0:T(8,128)(2,1)S(1)} %broadcast_select_fusion.5), channel_id=1, source_target_pairs={{0,1},{1,0},{2,3},{3,2},{4,5},{5,4},{6,7},{7,6},{8,9},{9,8},{10,11... | collective-permute-start | bytes 737288 | tf_op jit(solution)/shard_map/ppermute | solution.py:296
  87.3 4.4 %collective-permute-start.25 = (bf16[320,384]{1,0:T(8,128)(2,1)S(1)}, bf16[320,384]{1,0:T(8,128)(2,1)S(1)}, u32[]{:S(2)}, u32[]{:S(2)}) collective-permute-start(bf16[320,384]{1,0:T(8,128)(2,1)S(1)} %broadcast_select_fusion.4), channel_id=1, source_target_pairs={{0,1},{1,0},{2,3},{3,2},{4,5},{5,4},{6,7},{7,6},{8,9},{9,8},{10,11... | collective-permute-start | bytes 737288 | tf_op jit(solution)/shard_map/ppermute | solution.py:296
  93.4 4.8 %collective-permute-start.30 = (bf16[320,384]{1,0:T(8,128)(2,1)S(1)}, bf16[320,384]{1,0:T(8,128)(2,1)S(1)}, u32[]{:S(2)}, u32[]{:S(2)}) collective-permute-start(bf16[320,384]{1,0:T(8,128)(2,1)S(1)} %broadcast_select_fusion.3), channel_id=1, source_target_pairs={{0,1},{1,0},{2,3},{3,2},{4,5},{5,4},{6,7},{7,6},{8,9},{9,8},{10,11... | collective-permute-start | bytes 737288 | tf_op jit(solution)/shard_map/ppermute | solution.py:296
  99.1 2.8 %collective-permute-start.34 = (bf16[320,384]{1,0:T(8,128)(2,1)S(1)}, bf16[320,384]{1,0:T(8,128)(2,1)S(1)}, u32[]{:S(2)}, u32[]{:S(2)}) collective-permute-start(bf16[320,384]{1,0:T(8,128)(2,1)S(1)} %broadcast_select_fusion.2), channel_id=1, source_target_pairs={{0,1},{1,0},{2,3},{3,2},{4,5},{5,4},{6,7},{7,6},{8,9},{9,8},{10,11... | collective-permute-start | bytes 737288 | tf_op jit(solution)/shard_map/ppermute | solution.py:296
  101.9 3.0 %collective-permute-done.30.refs_10_ = bf16[320,384]{1,0:T(8,128)(2,1)S(1)} collective-permute-done((bf16[320,384]{1,0:T(8,128)(2,1)S(1)}, bf16[320,384]{1,0:T(8,128)(2,1)S(1)}, u32[]{:S(2)}, u32[]{:S(2)}) %collective-permute-start.30) | collective-permute-done | bytes 245792 | tf_op jit(solution)/shard_map/ppermute | solution.py:296
  105.8 4.4 %collective-permute-start.32 = (bf16[320,384]{1,0:T(8,128)(2,1)S(1)}, bf16[320,384]{1,0:T(8,128)(2,1)S(1)}, u32[]{:S(2)}, u32[]{:S(2)}) collective-permute-start(bf16[320,384]{1,0:T(8,128)(2,1)S(1)} %add_convert_fusion.3.refs_15_), channel_id=1, source_target_pairs={{0,1},{1,0},{2,3},{3,2},{4,5},{5,4},{6,7},{7,6},{8,9},{9,8},{10,11... | collective-permute-start | bytes 737288 | tf_op jit(solution)/shard_map/ppermute | solution.py:296
  111.7 4.3 %collective-permute-start.38 = (bf16[320,384]{1,0:T(8,128)(2,1)}, bf16[320,384]{1,0:T(8,128)(2,1)}, u32[]{:S(2)}, u32[]{:S(2)}) collective-permute-start(bf16[320,384]{1,0:T(8,128)(2,1)} %add_convert_fusion.1), channel_id=1, source_target_pairs={{0,1},{1,0},{2,3},{3,2},{4,5},{5,4},{6,7},{7,6},{8,9},{9,8},{10,11... | collective-permute-start | bytes 737288 | tf_op jit(solution)/shard_map/ppermute | solution.py:296
  115.9 3.6 %shard_map.74 = bf16[512,640]{1,0:T(8,128)(2,1)} custom-call(s32[2]{0:T(128)S(1)} %pad_add_fusion.idx_ref, bf16[512,384]{1,0:T(8,128)(2,1)S(1)} %copy-done.16, bf16[512,384]{1,0:T(8,128)(2,1)S(1)} %collective-permute-done.10.refs_1_, bf16[512,384]{1,0:T(8,128)(2,1)S(1)} %collective-permute-done.35.refs_2_, ...), custom_call_target="tpu_custom_call" | custom-call | tf_op jit(solution)/shard_map/pallas_call | solution.py:187
  120.3 0.9 collective-permute-start.39
  121.2 0.9 copy-done.11
  122.1 0.9 copy-done.18
  123.1 2.2 %shard_map.75.b = f32[5,640,384]{2,1,0:T(8,128)} custom-call(s32[1]{0:T(128)} %bitcast.7.end_ref.end, bf16[320,384]{1,0:T(8,128)(2,1)S(1)} %collective-permute-done.21.refs_0_, bf16[320,384]{1,0:T(8,128)(2,1)S(1)} %add_convert_fusion.24.refs_1_, bf16[320,384]{1,0:T(8,128)(2,1)S(1)} %collective-permute-done.19.refs_2_, ...), custom_call_target="tpu_custom_call" | custom-call | tf_op jit(solution)/shard_map/pallas_call | solution.py:228
  125.3 1.4 %collective-permute-done.39 = bf16[320,384]{1,0:T(8,128)(2,1)} collective-permute-done((bf16[320,384]{1,0:T(8,128)(2,1)}, bf16[320,384]{1,0:T(8,128)(2,1)}, u32[]{:S(2)}, u32[]{:S(2)}) %collective-permute-start.39) | collective-permute-done | bytes 245792 | tf_op jit(solution)/shard_map/ppermute | solution.py:296
  126.8 1.1 broadcast_select_fusion
  127.9 1.0 shard_map.76
  (119 shorter events, 16.9 us)
Async XLA Ops:
  0.6 10.9 %collective-permute-start.1 = (bf16[320,1024]{1,0:T(8,128)(2,1)}, bf16[320,1024]{1,0:T(8,128)(2,1)S(1)}, u32[]{:S(2)}, u32[]{:S(2)}) collective-permute-start(bf16[320,1024]{1,0:T(8,128)(2,1)} %bitcast.9), channel_id=1, source_target_pairs={{0,4},{4,0},{8,12},{12,8},{1,5},{5,1},{9,13},{13,9},{2,6},{6,2},{1... | collective-permute-start | bytes 1966088 | tf_op jit(solution)/shard_map/ppermute | solution.py:26
  1.1 18.7 %collective-permute-start = (bf16[320,1024]{1,0:T(8,128)(2,1)}, bf16[320,1024]{1,0:T(8,128)(2,1)S(1)}, u32[]{:S(2)}, u32[]{:S(2)}) collective-permute-start(bf16[320,1024]{1,0:T(8,128)(2,1)} %bitcast.10), channel_id=1, source_target_pairs={{0,8},{4,12},{8,0},{12,4},{1,9},{5,13},{9,1},{13,5},{2,10},{6,14},... | collective-permute-start | bytes 1966088 | tf_op jit(solution)/shard_map/ppermute | solution.py:26
  4.9 17.0 %copy-start.14 = (bf16[1,512,384]{2,1,0:T(8,128)(2,1)S(1)}, bf16[1,512,384]{2,1,0:T(8,128)(2,1)}, u32[]{:S(2)}) copy-start(bf16[1,512,384]{2,1,0:T(8,128)(2,1)} %param.9) | copy-start | bytes 1179652
  5.0 3.8 %collective-permute-start.2 = (f32[8,384]{1,0:T(8,128)S(1)}, f32[8,384]{1,0:T(8,128)S(1)}, u32[]{:S(2)}, u32[]{:S(2)}) collective-permute-start(f32[8,384]{1,0:T(8,128)S(1)} %shard_map.68), channel_id=1, source_target_pairs={{0,16},{16,0},{1,17},{17,1},{2,18},{18,2},{3,19},{19,3},{4,20},{20... | collective-permute-start | bytes 36872 | tf_op jit(solution)/shard_map/ppermute | solution.py:26
  8.9 10.5 %collective-permute-start.5 = (f32[8,384]{1,0:T(8,128)S(1)}, f32[8,384]{1,0:T(8,128)S(1)}, u32[]{:S(2)}, u32[]{:S(2)}) collective-permute-start(f32[8,384]{1,0:T(8,128)S(1)} %maximum_maximum_fusion.refs_2_.refs_4_), channel_id=1, source_target_pairs={{0,12},{4,8},{8,4},{12,0},{1,13},{5,9},{9,5},{13,1},{2,14},{6,10},... | collective-permute-start | bytes 36872 | tf_op jit(solution)/shard_map/ppermute | solution.py:26
  8.9 10.9 %collective-permute-start.4 = (f32[8,384]{1,0:T(8,128)S(1)}, f32[8,384]{1,0:T(8,128)S(1)}, u32[]{:S(2)}, u32[]{:S(2)}) collective-permute-start(f32[8,384]{1,0:T(8,128)S(1)} %maximum_maximum_fusion.refs_2_.refs_4_), channel_id=1, source_target_pairs={{0,8},{4,12},{8,0},{12,4},{1,9},{5,13},{9,1},{13,5},{2,10},{6,14},... | collective-permute-start | bytes 36872 | tf_op jit(solution)/shard_map/ppermute | solution.py:26
  9.8 1.8 %collective-permute-start.3 = (f32[8,384]{1,0:T(8,128)S(1)}, f32[8,384]{1,0:T(8,128)S(1)}, u32[]{:S(2)}, u32[]{:S(2)}) collective-permute-start(f32[8,384]{1,0:T(8,128)S(1)} %maximum_maximum_fusion.refs_2_.refs_4_), channel_id=1, source_target_pairs={{0,4},{4,0},{8,12},{12,8},{1,5},{5,1},{9,13},{13,9},{2,6},{6,2},{1... | collective-permute-start | bytes 36872 | tf_op jit(solution)/shard_map/ppermute | solution.py:26
  15.1 6.9 %copy-start.7 = (bf16[320,1024]{1,0:T(8,128)(2,1)}, bf16[320,1024]{1,0:T(8,128)(2,1)S(1)}, u32[]{:S(2)}) copy-start(bf16[320,1024]{1,0:T(8,128)(2,1)S(1)} %collective-permute-done.1.refs_1_.refs_2_) | copy-start | bytes 1966084
  15.1 6.9 %copy-start.1 = (bf16[5,1280,384]{2,1,0:T(8,128)(2,1)S(1)}, bf16[5,1280,384]{2,1,0:T(8,128)(2,1)}, u32[]{:S(2)}) copy-start(bf16[5,1280,384]{2,1,0:T(8,128)(2,1)} %refs_8_.2) | copy-start | bytes 14745604
  15.1 6.9 %copy-start.6 = (bf16[1,1024,320]{1,2,0:T(8,128)(2,1)S(1)}, bf16[1,1024,320]{1,2,0:T(8,128)(2,1)}, u32[]{:S(2)}) copy-start(bf16[1,1024,320]{1,2,0:T(8,128)(2,1)} %param.5) | copy-start | bytes 1966084
  19.8 2.1 %collective-permute-start.6 = (bf16[320,1024]{1,0:T(8,128)(2,1)S(1)}, bf16[320,1024]{1,0:T(8,128)(2,1)S(1)}, u32[]{:S(2)}, u32[]{:S(2)}) collective-permute-start(bf16[320,1024]{1,0:T(8,128)(2,1)S(1)} %collective-permute-done.refs_1_), channel_id=1, source_target_pairs={{0,4},{4,0},{8,12},{12,8},{1,5},{5,1},{9,13},{13,9},{2,6},{6,2},{1... | collective-permute-start | bytes 1966088 | tf_op jit(solution)/shard_map/ppermute | solution.py:26
  30.3 4.8 %copy-start.15 = (bf16[512,384]{1,0:T(8,128)(2,1)}, bf16[512,384]{1,0:T(8,128)(2,1)S(1)}, u32[]{:S(2)}) copy-start(bf16[512,384]{1,0:T(8,128)(2,1)S(1)} %get-tuple-element.113.refs_0_) | copy-start | bytes 1179652
  30.3 8.1 %collective-permute-start.7 = (bf16[320,384]{1,0:T(8,128)(2,1)S(1)}, bf16[320,384]{1,0:T(8,128)(2,1)S(1)}, u32[]{:S(2)}, u32[]{:S(2)}) collective-permute-start(bf16[320,384]{1,0:T(8,128)(2,1)S(1)} %get-tuple-element.67), channel_id=1, source_target_pairs={{0,16},{16,0},{1,17},{17,1},{2,18},{18,2},{3,19},{19,3},{4,20},{20... | collective-permute-start | bytes 737288 | tf_op jit(solution)/shard_map/ppermute | solution.py:26
  36.3 13.3 %collective-permute-start.9 = (bf16[320,384]{1,0:T(8,128)(2,1)}, bf16[320,384]{1,0:T(8,128)(2,1)}, u32[]{:S(2)}, u32[]{:S(2)}) collective-permute-start(bf16[320,384]{1,0:T(8,128)(2,1)} %get-tuple-element.68), channel_id=1, source_target_pairs={{0,16},{16,0},{1,17},{17,1},{2,18},{18,2},{3,19},{19,3},{4,20},{20... | collective-permute-start | bytes 737288 | tf_op jit(solution)/shard_map/ppermute | solution.py:26
  39.2 11.9 %collective-permute-start.8 = (bf16[320,384]{1,0:T(8,128)(2,1)}, bf16[320,384]{1,0:T(8,128)(2,1)}, u32[]{:S(2)}, u32[]{:S(2)}) collective-permute-start(bf16[320,384]{1,0:T(8,128)(2,1)} %add_convert_fusion.29), channel_id=1, source_target_pairs={{0,1},{1,0},{2,3},{3,2},{4,5},{5,4},{6,7},{7,6},{8,9},{9,8},{10,11... | collective-permute-start | bytes 737288 | tf_op jit(solution)/shard_map/ppermute | solution.py:296
  41.0 13.3 %collective-permute-start.10 = (bf16[512,384]{1,0:T(8,128)(2,1)}, bf16[512,384]{1,0:T(8,128)(2,1)S(1)}, u32[]{:S(2)}, u32[]{:S(2)}) collective-permute-start(bf16[512,384]{1,0:T(8,128)(2,1)} %copy-done.15), channel_id=1, source_target_pairs={{0,8},{4,12},{8,0},{12,4},{1,9},{5,13},{9,1},{13,5},{2,10},{6,14},... | collective-permute-start | bytes 1179656 | tf_op jit(solution)/shard_map/ppermute | solution.py:26
  47.4 10.8 %collective-permute-start.11 = (bf16[320,384]{1,0:T(8,128)(2,1)S(1)}, bf16[320,384]{1,0:T(8,128)(2,1)S(1)}, u32[]{:S(2)}, u32[]{:S(2)}) collective-permute-start(bf16[320,384]{1,0:T(8,128)(2,1)S(1)} %get-tuple-element.77), channel_id=1, source_target_pairs={{0,16},{16,0},{1,17},{17,1},{2,18},{18,2},{3,19},{19,3},{4,20},{20... | collective-permute-start | bytes 737288 | tf_op jit(solution)/shard_map/ppermute | solution.py:26
  49.5 14.2 %collective-permute-start.17 = (bf16[320,384]{1,0:T(8,128)(2,1)S(1)}, bf16[320,384]{1,0:T(8,128)(2,1)S(1)}, u32[]{:S(2)}, u32[]{:S(2)}) collective-permute-start(bf16[320,384]{1,0:T(8,128)(2,1)S(1)} %get-tuple-element.85), channel_id=1, source_target_pairs={{0,16},{16,0},{1,17},{17,1},{2,18},{18,2},{3,19},{19,3},{4,20},{20... | collective-permute-start | bytes 737288 | tf_op jit(solution)/shard_map/ppermute | solution.py:26
  50.6 12.2 %collective-permute-start.14 = (bf16[320,384]{1,0:T(8,128)(2,1)S(1)}, bf16[320,384]{1,0:T(8,128)(2,1)S(1)}, u32[]{:S(2)}, u32[]{:S(2)}) collective-permute-start(bf16[320,384]{1,0:T(8,128)(2,1)S(1)} %add_convert_fusion.28), channel_id=1, source_target_pairs={{0,1},{1,0},{2,3},{3,2},{4,5},{5,4},{6,7},{7,6},{8,9},{9,8},{10,11... | collective-permute-start | bytes 737288 | tf_op jit(solution)/shard_map/ppermute | solution.py:296
  51.1 21.1 %collective-permute-start.13 = (bf16[640,384]{1,0:T(8,128)(2,1)S(1)}, bf16[640,384]{1,0:T(8,128)(2,1)S(1)}, u32[]{:S(2)}, u32[]{:S(2)}) collective-permute-start(bf16[640,384]{1,0:T(8,128)(2,1)S(1)} %get-tuple-element.83), channel_id=1, source_target_pairs={{0,16},{16,0},{1,17},{17,1},{2,18},{18,2},{3,19},{19,3},{4,20},{20... | collective-permute-start | bytes 1474568 | tf_op jit(solution)/shard_map/ppermute | solution.py:26
  54.2 9.3 %collective-permute-start.18 = (bf16[320,384]{1,0:T(8,128)(2,1)S(1)}, bf16[320,384]{1,0:T(8,128)(2,1)S(1)}, u32[]{:S(2)}, u32[]{:S(2)}) collective-permute-start(bf16[320,384]{1,0:T(8,128)(2,1)S(1)} %add_convert_fusion.27), channel_id=1, source_target_pairs={{1,2},{2,1},{5,6},{6,5},{9,10},{10,9},{13,14},{14,13},{17,18},{18,... | collective-permute-start | bytes 737288 | tf_op jit(solution)/shard_map/ppermute | solution.py:302
  58.3 10.2 %collective-permute-start.16 = (bf16[320,384]{1,0:T(8,128)(2,1)S(1)}, bf16[320,384]{1,0:T(8,128)(2,1)S(1)}, u32[]{:S(2)}, u32[]{:S(2)}) collective-permute-start(bf16[320,384]{1,0:T(8,128)(2,1)S(1)} %add_convert_fusion.26), channel_id=1, source_target_pairs={{0,1},{1,0},{2,3},{3,2},{4,5},{5,4},{6,7},{7,6},{8,9},{9,8},{10,11... | collective-permute-start | bytes 737288 | tf_op jit(solution)/shard_map/ppermute | solution.py:296
  62.9 6.4 %collective-permute-start.15 = (bf16[320,384]{1,0:T(8,128)(2,1)S(1)}, bf16[320,384]{1,0:T(8,128)(2,1)S(1)}, u32[]{:S(2)}, u32[]{:S(2)}) collective-permute-start(bf16[320,384]{1,0:T(8,128)(2,1)S(1)} %add_convert_fusion.25), channel_id=1, source_target_pairs={{1,2},{2,1},{5,6},{6,5},{9,10},{10,9},{13,14},{14,13},{17,18},{18,... | collective-permute-start | bytes 737288 | tf_op jit(solution)/shard_map/ppermute | solution.py:302
  63.6 19.4 %collective-permute-start.12 = (bf16[640,384]{1,0:T(8,128)(2,1)S(1)}, bf16[640,384]{1,0:T(8,128)(2,1)S(1)}, u32[]{:S(2)}, u32[]{:S(2)}) collective-permute-start(bf16[640,384]{1,0:T(8,128)(2,1)S(1)} %get-tuple-element.80), channel_id=1, source_target_pairs={{0,16},{16,0},{1,17},{17,1},{2,18},{18,2},{3,19},{19,3},{4,20},{20... | collective-permute-start | bytes 1474568 | tf_op jit(solution)/shard_map/ppermute | solution.py:26
  63.9 10.2 %collective-permute-start.21 = (bf16[320,384]{1,0:T(8,128)(2,1)S(1)}, bf16[320,384]{1,0:T(8,128)(2,1)S(1)}, u32[]{:S(2)}, u32[]{:S(2)}) collective-permute-start(bf16[320,384]{1,0:T(8,128)(2,1)S(1)} %broadcast_select_fusion.8), channel_id=1, source_target_pairs={{0,1},{1,0},{2,3},{3,2},{4,5},{5,4},{6,7},{7,6},{8,9},{9,8},{10,11... | collective-permute-start | bytes 737288 | tf_op jit(solution)/shard_map/ppermute | solution.py:296
  68.6 6.4 %collective-permute-start.20 = (bf16[320,384]{1,0:T(8,128)(2,1)S(1)}, bf16[320,384]{1,0:T(8,128)(2,1)S(1)}, u32[]{:S(2)}, u32[]{:S(2)}) collective-permute-start(bf16[320,384]{1,0:T(8,128)(2,1)S(1)} %add_convert_fusion.22), channel_id=1, source_target_pairs={{1,2},{2,1},{5,6},{6,5},{9,10},{10,9},{13,14},{14,13},{17,18},{18,... | collective-permute-start | bytes 737288 | tf_op jit(solution)/shard_map/ppermute | solution.py:302
  72.4 7.7 %collective-permute-start.19 = (bf16[320,384]{1,0:T(8,128)(2,1)S(1)}, bf16[320,384]{1,0:T(8,128)(2,1)S(1)}, u32[]{:S(2)}, u32[]{:S(2)}) collective-permute-start(bf16[320,384]{1,0:T(8,128)(2,1)S(1)} %broadcast_select_fusion.7), channel_id=1, source_target_pairs={{0,1},{1,0},{2,3},{3,2},{4,5},{5,4},{6,7},{7,6},{8,9},{9,8},{10,11... | collective-permute-start | bytes 737288 | tf_op jit(solution)/shard_map/ppermute | solution.py:296
  74.2 18.4 %copy-start.16 = (bf16[512,384]{1,0:T(8,128)(2,1)S(1)}, bf16[512,384]{1,0:T(8,128)(2,1)}, u32[]{:S(2)}) copy-start(bf16[512,384]{1,0:T(8,128)(2,1)} %copy-done.15) | copy-start | bytes 1179652
  74.2 8.8 %collective-permute-start.24 = (bf16[320,384]{1,0:T(8,128)(2,1)S(1)}, bf16[320,384]{1,0:T(8,128)(2,1)S(1)}, u32[]{:S(2)}, u32[]{:S(2)}) collective-permute-start(bf16[320,384]{1,0:T(8,128)(2,1)S(1)} %add_convert_fusion.19), channel_id=1, source_target_pairs={{1,2},{2,1},{5,6},{6,5},{9,10},{10,9},{13,14},{14,13},{17,18},{18,... | collective-permute-start | bytes 737288 | tf_op jit(solution)/shard_map/ppermute | solution.py:302
  75.2 11.1 %collective-permute-start.23 = (bf16[320,384]{1,0:T(8,128)(2,1)S(1)}, bf16[320,384]{1,0:T(8,128)(2,1)S(1)}, u32[]{:S(2)}, u32[]{:S(2)}) collective-permute-start(bf16[320,384]{1,0:T(8,128)(2,1)S(1)} %broadcast_select_fusion.6), channel_id=1, source_target_pairs={{0,1},{1,0},{2,3},{3,2},{4,5},{5,4},{6,7},{7,6},{8,9},{9,8},{10,11... | collective-permute-start | bytes 737288 | tf_op jit(solution)/shard_map/ppermute | solution.py:296
  80.2 6.9 %collective-permute-start.22 = (bf16[320,384]{1,0:T(8,128)(2,1)S(1)}, bf16[320,384]{1,0:T(8,128)(2,1)S(1)}, u32[]{:S(2)}, u32[]{:S(2)}) collective-permute-start(bf16[320,384]{1,0:T(8,128)(2,1)S(1)} %add_convert_fusion.16), channel_id=1, source_target_pairs={{1,2},{2,1},{5,6},{6,5},{9,10},{10,9},{13,14},{14,13},{17,18},{18,... | collective-permute-start | bytes 737288 | tf_op jit(solution)/shard_map/ppermute | solution.py:302
  80.9 12.3 %collective-permute-start.26 = (bf16[640,384]{1,0:T(8,128)(2,1)S(1)}, bf16[640,384]{1,0:T(8,128)(2,1)S(1)}, u32[]{:S(2)}, u32[]{:S(2)}) collective-permute-start(bf16[640,384]{1,0:T(8,128)(2,1)S(1)} %get-tuple-element.101), channel_id=1, source_target_pairs={{0,16},{16,0},{1,17},{17,1},{2,18},{18,2},{3,19},{19,3},{4,20},{20... | collective-permute-start | bytes 1474568 | tf_op jit(solution)/shard_map/ppermute | solution.py:26
  83.2 8.6 %collective-permute-start.28 = (bf16[320,384]{1,0:T(8,128)(2,1)S(1)}, bf16[320,384]{1,0:T(8,128)(2,1)S(1)}, u32[]{:S(2)}, u32[]{:S(2)}) collective-permute-start(bf16[320,384]{1,0:T(8,128)(2,1)S(1)} %broadcast_select_fusion.5), channel_id=1, source_target_pairs={{0,1},{1,0},{2,3},{3,2},{4,5},{5,4},{6,7},{7,6},{8,9},{9,8},{10,11... | collective-permute-start | bytes 737288 | tf_op jit(solution)/shard_map/ppermute | solution.py:296
  86.4 6.1 %collective-permute-start.27 = (bf16[320,384]{1,0:T(8,128)(2,1)S(1)}, bf16[320,384]{1,0:T(8,128)(2,1)S(1)}, u32[]{:S(2)}, u32[]{:S(2)}) collective-permute-start(bf16[320,384]{1,0:T(8,128)(2,1)S(1)} %add_convert_fusion.13), channel_id=1, source_target_pairs={{1,2},{2,1},{5,6},{6,5},{9,10},{10,9},{13,14},{14,13},{17,18},{18,... | collective-permute-start | bytes 737288 | tf_op jit(solution)/shard_map/ppermute | solution.py:302
  87.3 28.6 %copy-start.9 = (bf16[1536,640]{1,0:T(8,128)(2,1)S(1)}, bf16[1536,640]{1,0:T(8,128)(2,1)}, u32[]{:S(2)}) copy-start(bf16[1536,640]{1,0:T(8,128)(2,1)} %refs_8_.3) | copy-start | bytes 5898244
  87.3 10.8 %collective-permute-start.25 = (bf16[320,384]{1,0:T(8,128)(2,1)S(1)}, bf16[320,384]{1,0:T(8,128)(2,1)S(1)}, u32[]{:S(2)}, u32[]{:S(2)}) collective-permute-start(bf16[320,384]{1,0:T(8,128)(2,1)S(1)} %broadcast_select_fusion.4), channel_id=1, source_target_pairs={{0,1},{1,0},{2,3},{3,2},{4,5},{5,4},{6,7},{7,6},{8,9},{9,8},{10,11... | collective-permute-start | bytes 737288 | tf_op jit(solution)/shard_map/ppermute | solution.py:296
  91.9 7.1 %collective-permute-start.31 = (bf16[320,384]{1,0:T(8,128)(2,1)S(1)}, bf16[320,384]{1,0:T(8,128)(2,1)S(1)}, u32[]{:S(2)}, u32[]{:S(2)}) collective-permute-start(bf16[320,384]{1,0:T(8,128)(2,1)S(1)} %add_convert_fusion.10), channel_id=1, source_target_pairs={{1,2},{2,1},{5,6},{6,5},{9,10},{10,9},{13,14},{14,13},{17,18},{18,... | collective-permute-start | bytes 737288 | tf_op jit(solution)/shard_map/ppermute | solution.py:302
  92.6 23.3 %collective-permute-start.35 = (bf16[512,384]{1,0:T(8,128)(2,1)S(1)}, bf16[512,384]{1,0:T(8,128)(2,1)S(1)}, u32[]{:S(2)}, u32[]{:S(2)}) collective-permute-start(bf16[512,384]{1,0:T(8,128)(2,1)S(1)} %copy-done.16), channel_id=1, source_target_pairs={{0,4},{4,0},{8,12},{12,8},{1,5},{5,1},{9,13},{13,9},{2,6},{6,2},{1... | collective-permute-start | bytes 1179656 | tf_op jit(solution)/shard_map/ppermute | solution.py:26
  92.7 23.2 %collective-permute-start.36 = (bf16[512,384]{1,0:T(8,128)(2,1)S(1)}, bf16[512,384]{1,0:T(8,128)(2,1)S(1)}, u32[]{:S(2)}, u32[]{:S(2)}) collective-permute-start(bf16[512,384]{1,0:T(8,128)(2,1)S(1)} %collective-permute-done.10.refs_1_), channel_id=1, source_target_pairs={{0,4},{4,0},{8,12},{12,8},{1,5},{5,1},{9,13},{13,9},{2,6},{6,2},{1... | collective-permute-start | bytes 1179656 | tf_op jit(solution)/shard_map/ppermute | solution.py:26
  93.4 11.5 %collective-permute-start.30 = (bf16[320,384]{1,0:T(8,128)(2,1)S(1)}, bf16[320,384]{1,0:T(8,128)(2,1)S(1)}, u32[]{:S(2)}, u32[]{:S(2)}) collective-permute-start(bf16[320,384]{1,0:T(8,128)(2,1)S(1)} %broadcast_select_fusion.3), channel_id=1, source_target_pairs={{0,1},{1,0},{2,3},{3,2},{4,5},{5,4},{6,7},{7,6},{8,9},{9,8},{10,11... | collective-permute-start | bytes 737288 | tf_op jit(solution)/shard_map/ppermute | solution.py:296
  98.2 7.4 %collective-permute-start.29 = (bf16[320,384]{1,0:T(8,128)(2,1)S(1)}, bf16[320,384]{1,0:T(8,128)(2,1)S(1)}, u32[]{:S(2)}, u32[]{:S(2)}) collective-permute-start(bf16[320,384]{1,0:T(8,128)(2,1)S(1)} %add_convert_fusion.7), channel_id=1, source_target_pairs={{1,2},{2,1},{5,6},{6,5},{9,10},{10,9},{13,14},{14,13},{17,18},{18,... | collective-permute-start | bytes 737288 | tf_op jit(solution)/shard_map/ppermute | solution.py:302
  99.1 11.0 %collective-permute-start.34 = (bf16[320,384]{1,0:T(8,128)(2,1)S(1)}, bf16[320,384]{1,0:T(8,128)(2,1)S(1)}, u32[]{:S(2)}, u32[]{:S(2)}) collective-permute-start(bf16[320,384]{1,0:T(8,128)(2,1)S(1)} %broadcast_select_fusion.2), channel_id=1, source_target_pairs={{0,1},{1,0},{2,3},{3,2},{4,5},{5,4},{6,7},{7,6},{8,9},{9,8},{10,11... | collective-permute-start | bytes 737288 | tf_op jit(solution)/shard_map/ppermute | solution.py:296
  105.0 5.9 %collective-permute-start.33 = (bf16[320,384]{1,0:T(8,128)(2,1)S(1)}, bf16[320,384]{1,0:T(8,128)(2,1)S(1)}, u32[]{:S(2)}, u32[]{:S(2)}) collective-permute-start(bf16[320,384]{1,0:T(8,128)(2,1)S(1)} %add_convert_fusion.4), channel_id=1, source_target_pairs={{1,2},{2,1},{5,6},{6,5},{9,10},{10,9},{13,14},{14,13},{17,18},{18,... | collective-permute-start | bytes 737288 | tf_op jit(solution)/shard_map/ppermute | solution.py:302
  105.8 10.2 %collective-permute-start.32 = (bf16[320,384]{1,0:T(8,128)(2,1)S(1)}, bf16[320,384]{1,0:T(8,128)(2,1)S(1)}, u32[]{:S(2)}, u32[]{:S(2)}) collective-permute-start(bf16[320,384]{1,0:T(8,128)(2,1)S(1)} %add_convert_fusion.3.refs_15_), channel_id=1, source_target_pairs={{0,1},{1,0},{2,3},{3,2},{4,5},{5,4},{6,7},{7,6},{8,9},{9,8},{10,11... | collective-permute-start | bytes 737288 | tf_op jit(solution)/shard_map/ppermute | solution.py:296
  110.1 9.4 %copy-start.10 = (bf16[320,384]{1,0:T(8,128)(2,1)}, bf16[320,384]{1,0:T(8,128)(2,1)S(1)}, u32[]{:S(2)}) copy-start(bf16[320,384]{1,0:T(8,128)(2,1)S(1)} %collective-permute-done.34.refs_12_) | copy-start | bytes 737284
  110.2 9.3 %collective-permute-start.37 = (bf16[320,384]{1,0:T(8,128)(2,1)S(1)}, bf16[320,384]{1,0:T(8,128)(2,1)S(1)}, u32[]{:S(2)}, u32[]{:S(2)}) collective-permute-start(bf16[320,384]{1,0:T(8,128)(2,1)S(1)} %add_convert_fusion.2), channel_id=1, source_target_pairs={{1,2},{2,1},{5,6},{6,5},{9,10},{10,9},{13,14},{14,13},{17,18},{18,... | collective-permute-start | bytes 737288 | tf_op jit(solution)/shard_map/ppermute | solution.py:302
  111.7 13.7 %collective-permute-start.38 = (bf16[320,384]{1,0:T(8,128)(2,1)}, bf16[320,384]{1,0:T(8,128)(2,1)}, u32[]{:S(2)}, u32[]{:S(2)}) collective-permute-start(bf16[320,384]{1,0:T(8,128)(2,1)} %add_convert_fusion.1), channel_id=1, source_target_pairs={{0,1},{1,0},{2,3},{3,2},{4,5},{5,4},{6,7},{7,6},{8,9},{9,8},{10,11... | collective-permute-start | bytes 737288 | tf_op jit(solution)/shard_map/ppermute | solution.py:296
  120.3 6.5 %collective-permute-start.39 = (bf16[320,384]{1,0:T(8,128)(2,1)}, bf16[320,384]{1,0:T(8,128)(2,1)}, u32[]{:S(2)}, u32[]{:S(2)}) collective-permute-start(bf16[320,384]{1,0:T(8,128)(2,1)} %add_convert_fusion), channel_id=1, source_target_pairs={{0,1},{1,0},{2,3},{3,2},{4,5},{5,4},{6,7},{7,6},{8,9},{9,8},{10,11... | collective-permute-start | bytes 737288 | tf_op jit(solution)/shard_map/ppermute | solution.py:296
  (11 other events, 15.7 us)

commit v16 on v15

--- a/solution.py
+++ b/solution.py
@@ -448,7 +448,7 @@
         return last
 
     def idle(c, last, sums):
-        if c == per + 4:
+        if c == per + 5:
             held = encs[1:]
             relays.extend([swap(after(e, last, *held), "mp", bits[-1]) for e in encs])
         if c == 0:

time: 130 us -> 130 us (level)
  transfers between devices with their start and end apart: 40 -> 40, of which waited for: 10 -> 11; matrix products, arithmetic and copies ran while one was open for 6% -> 6% of each run, Pallas kernels for 16% -> 16%
where the time goes in v16:
time: 130 us; the launch traced here: 129 us
  starting transfers between devices  63.2 us (49%)
  Pallas kernels  27.3 us (21%)
  waiting for transfers between devices  16.9 us (13%)
  local copies, waits for them, and re-layouts  13 us (10%)
  other arithmetic  7.76 us (6%)
    ppermute x13, starting transfers between devices, chain_sums(): outer[r] = lax.ppermute(value, 'dp', outer_pairs)  39.5 us
    pallas_call x6, Pallas kernels, call(): pl.pallas_call(kernel, out_shape=out, in_specs=[pl.BlockSpec(memory_space...  23.9 us
    ppermute x17, starting transfers between devices, swap(): return lax.ppermute(value, axis, [(i, i ^ bit) for i in range(peers)])  16.9 us
    unnamed x38, local copies, waits for them, and re-layouts  12.1 us
    ppermute x17, waiting for transfers between devices, swap(): return lax.ppermute(value, axis, [(i, i ^ bit) for i in range(peers)])  8.67 us
    ppermute x13, waiting for transfers between devices, chain_sums(): outer[r] = lax.ppermute(value, 'dp', outer_pairs)  8.22 us
    ppermute x10, starting transfers between devices, chain_sums(): middle[r - 1] = lax.ppermute(last, 'dp', middle_pairs)  6.89 us
    convert_element_type x23, other arithmetic, added(): return (a.astype(F32) + b.astype(F32)).astype(BF16)  5.81 us
  transfers between devices with their start and end apart: 40, of which 11 were waited for; matrix products, arithmetic and copies ran while one was open for 6% of the time, Pallas kernels for 16%

profile of v16, /device:TPU:0, one launch (start us, length us, event | category | flops | bytes accessed | tf_op | source)
XLA Modules:
  0.0 129.4 jit_solution(2350190640672627019)
XLA Ops:
  1.1 2.6 %collective-permute-start = (bf16[320,1024]{1,0:T(8,128)(2,1)}, bf16[320,1024]{1,0:T(8,128)(2,1)S(1)}, u32[]{:S(2)}, u32[]{:S(2)}) collective-permute-start(bf16[320,1024]{1,0:T(8,128)(2,1)} %bitcast.10), channel_id=1, source_target_pairs={{0,8},{4,12},{8,0},{12,4},{1,9},{5,13},{9,1},{13,5},{2,10},{6,14},... | collective-permute-start | bytes 1966088 | tf_op jit(solution)/shard_map/ppermute | solution.py:26
  3.7 1.1 copy-done.4
  5.0 1.6 %collective-permute-start.2 = (f32[8,384]{1,0:T(8,128)S(1)}, f32[8,384]{1,0:T(8,128)S(1)}, u32[]{:S(2)}, u32[]{:S(2)}) collective-permute-start(f32[8,384]{1,0:T(8,128)S(1)} %shard_map.68), channel_id=1, source_target_pairs={{0,16},{16,0},{1,17},{17,1},{2,18},{18,2},{3,19},{19,3},{4,20},{20... | collective-permute-start | bytes 36872 | tf_op jit(solution)/shard_map/ppermute | solution.py:26
  7.3 1.4 %collective-permute-done.2 = f32[8,384]{1,0:T(8,128)S(1)} collective-permute-done((f32[8,384]{1,0:T(8,128)S(1)}, f32[8,384]{1,0:T(8,128)S(1)}, u32[]{:S(2)}, u32[]{:S(2)}) %collective-permute-start.2) | collective-permute-done | bytes 12320 | tf_op jit(solution)/shard_map/ppermute | solution.py:26
  8.9 0.9 collective-permute-start.4
  9.8 0.9 collective-permute-start.3
  11.6 2.4 %copy-done = bf16[5,1280,384]{2,1,0:T(8,128)(2,1)S(1)} copy-done((bf16[5,1280,384]{2,1,0:T(8,128)(2,1)S(1)}, bf16[5,1280,384]{2,1,0:T(8,128)(2,1)}, u32[]{:S(2)}) %copy-start) | copy-done | bytes 4915224
  14.0 1.1 copy-done.5
  15.1 4.3 %shard_map.69 = (f32[512,384]{1,0:T(8,128)S(1)}, f32[512,384]{1,0:T(8,128)S(1)}) custom-call(s32[2]{0:T(128)S(1)} %pad_add_fusion.idx_ref, bf16[320,1024]{1,0:T(8,128)(2,1)S(1)} %bitcast.13, bf16[320,1024]{1,0:T(8,128)(2,1)S(1)} %collective-permute-done.1.refs_1_.refs_2_, f32[8,384]{1,0:T(8,128)S(1)} %maximum_maximum_fusion.refs_2_.refs_4_, ...), custom_call_target="tpu_custom_call" | custom-call | tf_op jit(solution)/shard_map/pallas_call | solution.py:187
  19.8 0.8 copy-done.12
  20.6 1.3 collective-permute-done.6.refs_3_
  21.9 1.1 copy-done.8
  23.0 1.1 copy-done.13
  24.1 6.2 %shard_map.70 = (bf16[512,384]{1,0:T(8,128)(2,1)S(1)}, f32[1040,384]{1,0:T(8,128)S(1)}, bf16[1280,1152]{1,0:T(8,128)(2,1)S(1)}, bf16[320,384]{1,0:T(8,128)(2,1)S(1)}) custom-call(s32[2]{0:T(128)S(1)} %pad_add_fusion.idx_ref, bf16[320,1024]{1,0:T(8,128)(2,1)S(1)} %bitcast.14, bf16[320,1024]{1,0:T(8,128)(2,1)S(1)} %copy-done.13, ...), custom_call_target="tpu_custom_call" | custom-call | tf_op jit(solution)/shard_map/pallas_call | solution.py:187
  30.3 1.8 %collective-permute-start.7 = (bf16[320,384]{1,0:T(8,128)(2,1)S(1)}, bf16[320,384]{1,0:T(8,128)(2,1)S(1)}, u32[]{:S(2)}, u32[]{:S(2)}) collective-permute-start(bf16[320,384]{1,0:T(8,128)(2,1)S(1)} %get-tuple-element.67), channel_id=1, source_target_pairs={{0,16},{16,0},{1,17},{17,1},{2,18},{18,2},{3,19},{19,3},{4,20},{20... | collective-permute-start | bytes 737288 | tf_op jit(solution)/shard_map/ppermute | solution.py:26
  32.1 3.0 %shard_map.71 = (bf16[640,384]{1,0:T(8,128)(2,1)S(1)}, bf16[320,384]{1,0:T(8,128)(2,1)}) custom-call(s32[2]{0:T(128)S(1)} %pad_add_fusion.idx_ref, bf16[1280,1152]{1,0:T(8,128)(2,1)S(1)} %get-tuple-element.64.all_ref, f32[1040,384]{1,0:T(8,128)S(1)} %get-tuple-element.65.p_ref), custom_call_target="tpu_custom_call" | custom-call | tf_op jit(solution)/shard_map/pallas_call | solution.py:187
  35.1 1.1 copy-done.2
  36.6 1.9 %collective-permute-done.7 = bf16[320,384]{1,0:T(8,128)(2,1)S(1)} collective-permute-done((bf16[320,384]{1,0:T(8,128)(2,1)S(1)}, bf16[320,384]{1,0:T(8,128)(2,1)S(1)}, u32[]{:S(2)}, u32[]{:S(2)}) %collective-permute-start.7) | collective-permute-done | bytes 245792 | tf_op jit(solution)/shard_map/ppermute | solution.py:26
  39.2 1.8 %collective-permute-start.8 = (bf16[320,384]{1,0:T(8,128)(2,1)}, bf16[320,384]{1,0:T(8,128)(2,1)}, u32[]{:S(2)}, u32[]{:S(2)}) collective-permute-start(bf16[320,384]{1,0:T(8,128)(2,1)} %add_convert_fusion.29), channel_id=1, source_target_pairs={{0,1},{1,0},{2,3},{3,2},{4,5},{5,4},{6,7},{7,6},{8,9},{9,8},{10,11... | collective-permute-start | bytes 737288 | tf_op jit(solution)/shard_map/ppermute | solution.py:296
  41.0 1.5 %collective-permute-start.10 = (bf16[512,384]{1,0:T(8,128)(2,1)}, bf16[512,384]{1,0:T(8,128)(2,1)S(1)}, u32[]{:S(2)}, u32[]{:S(2)}) collective-permute-start(bf16[512,384]{1,0:T(8,128)(2,1)} %copy-done.15), channel_id=1, source_target_pairs={{0,8},{4,12},{8,0},{12,4},{1,9},{5,13},{9,1},{13,5},{2,10},{6,14},... | collective-permute-start | bytes 1179656 | tf_op jit(solution)/shard_map/ppermute | solution.py:26
  42.5 1.4 %copy-done.3 = f32[1040,384]{1,0:T(8,128)S(1)} copy-done((f32[1040,384]{1,0:T(8,128)S(1)}, f32[1040,384]{1,0:T(8,128)}, u32[]{:S(2)}) %copy-start.3) | copy-done | bytes 1597464
  43.9 3.5 %shard_map.73 = (bf16[640,384]{1,0:T(8,128)(2,1)S(1)}, bf16[320,384]{1,0:T(8,128)(2,1)S(1)}, bf16[320,384]{1,0:T(8,128)(2,1)S(1)}, bf16[640,384]{1,0:T(8,128)(2,1)S(1)}, bf16[640,384]{1,0:T(8,128)(2,1)S(1)}) custom-call(s32[2]{0:T(128)S(1)} %pad_add_fusion.idx_ref, bf16[1280,1152]{1,0:T(8,128)(2,1)S(1)} %get-tuple-element.64.all_ref, f32[1040,384]{1,0:T(8,128)S(1)} %copy-done.3), custom_call_target="tpu_custom_call" | custom-call | tf_op jit(solution)/shard_map/pallas_call | solution.py:187
  47.4 2.1 %collective-permute-start.11 = (bf16[320,384]{1,0:T(8,128)(2,1)S(1)}, bf16[320,384]{1,0:T(8,128)(2,1)S(1)}, u32[]{:S(2)}, u32[]{:S(2)}) collective-permute-start(bf16[320,384]{1,0:T(8,128)(2,1)S(1)} %get-tuple-element.77), channel_id=1, source_target_pairs={{0,16},{16,0},{1,17},{17,1},{2,18},{18,2},{3,19},{19,3},{4,20},{20... | collective-permute-start | bytes 737288 | tf_op jit(solution)/shard_map/ppermute | solution.py:26
  49.6 1.0 add_convert_fusion.28
  51.1 1.9 %collective-permute-start.13 = (bf16[640,384]{1,0:T(8,128)(2,1)S(1)}, bf16[640,384]{1,0:T(8,128)(2,1)S(1)}, u32[]{:S(2)}, u32[]{:S(2)}) collective-permute-start(bf16[640,384]{1,0:T(8,128)(2,1)S(1)} %get-tuple-element.83), channel_id=1, source_target_pairs={{0,16},{16,0},{1,17},{17,1},{2,18},{18,2},{3,19},{19,3},{4,20},{20... | collective-permute-start | bytes 1474568 | tf_op jit(solution)/shard_map/ppermute | solution.py:26
  53.1 1.1 add_convert_fusion.27
  54.9 3.3 %shard_map.72 = (bf16[640,384]{1,0:T(8,128)(2,1)S(1)}, bf16[640,384]{1,0:T(8,128)(2,1)S(1)}, bf16[640,384]{1,0:T(8,128)(2,1)S(1)}, bf16[640,384]{1,0:T(8,128)(2,1)S(1)}) custom-call(s32[2]{0:T(128)S(1)} %pad_add_fusion.idx_ref, bf16[1280,1152]{1,0:T(8,128)(2,1)S(1)} %get-tuple-element.64.all_ref, f32[1040,384]{1,0:T(8,128)S(1)} %copy-done.3), custom_call_target="tpu_custom_call" | custom-call | tf_op jit(solution)/shard_map/pallas_call | solution.py:187
  58.3 4.5 %collective-permute-start.16 = (bf16[320,384]{1,0:T(8,128)(2,1)S(1)}, bf16[320,384]{1,0:T(8,128)(2,1)S(1)}, u32[]{:S(2)}, u32[]{:S(2)}) collective-permute-start(bf16[320,384]{1,0:T(8,128)(2,1)S(1)} %add_convert_fusion.26), channel_id=1, source_target_pairs={{0,1},{1,0},{2,3},{3,2},{4,5},{5,4},{6,7},{7,6},{8,9},{9,8},{10,11... | collective-permute-start | bytes 737288 | tf_op jit(solution)/shard_map/ppermute | solution.py:296
  63.9 1.8 %collective-permute-start.21 = (bf16[320,384]{1,0:T(8,128)(2,1)S(1)}, bf16[320,384]{1,0:T(8,128)(2,1)S(1)}, u32[]{:S(2)}, u32[]{:S(2)}) collective-permute-start(bf16[320,384]{1,0:T(8,128)(2,1)S(1)} %broadcast_select_fusion.8), channel_id=1, source_target_pairs={{0,1},{1,0},{2,3},{3,2},{4,5},{5,4},{6,7},{7,6},{8,9},{9,8},{10,11... | collective-permute-start | bytes 737288 | tf_op jit(solution)/shard_map/ppermute | solution.py:296
  65.7 2.8 %collective-permute-done.16 = bf16[320,384]{1,0:T(8,128)(2,1)S(1)} collective-permute-done((bf16[320,384]{1,0:T(8,128)(2,1)S(1)}, bf16[320,384]{1,0:T(8,128)(2,1)S(1)}, u32[]{:S(2)}, u32[]{:S(2)}) %collective-permute-start.16) | collective-permute-done | bytes 245792 | tf_op jit(solution)/shard_map/ppermute | solution.py:296
  69.3 2.9 %collective-permute-done.13 = bf16[640,384]{1,0:T(8,128)(2,1)S(1)} collective-permute-done((bf16[640,384]{1,0:T(8,128)(2,1)S(1)}, bf16[640,384]{1,0:T(8,128)(2,1)S(1)}, u32[]{:S(2)}, u32[]{:S(2)}) %collective-permute-start.13) | collective-permute-done | bytes 491552 | tf_op jit(solution)/shard_map/ppermute | solution.py:26
  72.4 1.7 %collective-permute-start.19 = (bf16[320,384]{1,0:T(8,128)(2,1)S(1)}, bf16[320,384]{1,0:T(8,128)(2,1)S(1)}, u32[]{:S(2)}, u32[]{:S(2)}) collective-permute-start(bf16[320,384]{1,0:T(8,128)(2,1)S(1)} %broadcast_select_fusion.7), channel_id=1, source_target_pairs={{0,1},{1,0},{2,3},{3,2},{4,5},{5,4},{6,7},{7,6},{8,9},{9,8},{10,11... | collective-permute-start | bytes 737288 | tf_op jit(solution)/shard_map/ppermute | solution.py:296
  75.1 4.9 %collective-permute-start.23 = (bf16[320,384]{1,0:T(8,128)(2,1)S(1)}, bf16[320,384]{1,0:T(8,128)(2,1)S(1)}, u32[]{:S(2)}, u32[]{:S(2)}) collective-permute-start(bf16[320,384]{1,0:T(8,128)(2,1)S(1)} %broadcast_select_fusion.6), channel_id=1, source_target_pairs={{0,1},{1,0},{2,3},{3,2},{4,5},{5,4},{6,7},{7,6},{8,9},{9,8},{10,11... | collective-permute-start | bytes 737288 | tf_op jit(solution)/shard_map/ppermute | solution.py:296
  81.0 1.9 %collective-permute-start.26 = (bf16[640,384]{1,0:T(8,128)(2,1)S(1)}, bf16[640,384]{1,0:T(8,128)(2,1)S(1)}, u32[]{:S(2)}, u32[]{:S(2)}) collective-permute-start(bf16[640,384]{1,0:T(8,128)(2,1)S(1)} %get-tuple-element.101), channel_id=1, source_target_pairs={{0,16},{16,0},{1,17},{17,1},{2,18},{18,2},{3,19},{19,3},{4,20},{20... | collective-permute-start | bytes 1474568 | tf_op jit(solution)/shard_map/ppermute | solution.py:26
  83.1 3.2 %collective-permute-start.28 = (bf16[320,384]{1,0:T(8,128)(2,1)S(1)}, bf16[320,384]{1,0:T(8,128)(2,1)S(1)}, u32[]{:S(2)}, u32[]{:S(2)}) collective-permute-start(bf16[320,384]{1,0:T(8,128)(2,1)S(1)} %broadcast_select_fusion.5), channel_id=1, source_target_pairs={{0,1},{1,0},{2,3},{3,2},{4,5},{5,4},{6,7},{7,6},{8,9},{9,8},{10,11... | collective-permute-start | bytes 737288 | tf_op jit(solution)/shard_map/ppermute | solution.py:296
  87.3 4.4 %collective-permute-start.25 = (bf16[320,384]{1,0:T(8,128)(2,1)S(1)}, bf16[320,384]{1,0:T(8,128)(2,1)S(1)}, u32[]{:S(2)}, u32[]{:S(2)}) collective-permute-start(bf16[320,384]{1,0:T(8,128)(2,1)S(1)} %broadcast_select_fusion.4), channel_id=1, source_target_pairs={{0,1},{1,0},{2,3},{3,2},{4,5},{5,4},{6,7},{7,6},{8,9},{9,8},{10,11... | collective-permute-start | bytes 737288 | tf_op jit(solution)/shard_map/ppermute | solution.py:296
  93.3 4.6 %collective-permute-start.30 = (bf16[320,384]{1,0:T(8,128)(2,1)S(1)}, bf16[320,384]{1,0:T(8,128)(2,1)S(1)}, u32[]{:S(2)}, u32[]{:S(2)}) collective-permute-start(bf16[320,384]{1,0:T(8,128)(2,1)S(1)} %broadcast_select_fusion.3), channel_id=1, source_target_pairs={{0,1},{1,0},{2,3},{3,2},{4,5},{5,4},{6,7},{7,6},{8,9},{9,8},{10,11... | collective-permute-start | bytes 737288 | tf_op jit(solution)/shard_map/ppermute | solution.py:296
  99.5 3.8 %collective-permute-start.34 = (bf16[320,384]{1,0:T(8,128)(2,1)S(1)}, bf16[320,384]{1,0:T(8,128)(2,1)S(1)}, u32[]{:S(2)}, u32[]{:S(2)}) collective-permute-start(bf16[320,384]{1,0:T(8,128)(2,1)S(1)} %broadcast_select_fusion.2), channel_id=1, source_target_pairs={{0,1},{1,0},{2,3},{3,2},{4,5},{5,4},{6,7},{7,6},{8,9},{9,8},{10,11... | collective-permute-start | bytes 737288 | tf_op jit(solution)/shard_map/ppermute | solution.py:296
  104.1 3.2 %collective-permute-start.32 = (bf16[320,384]{1,0:T(8,128)(2,1)S(1)}, bf16[320,384]{1,0:T(8,128)(2,1)S(1)}, u32[]{:S(2)}, u32[]{:S(2)}) collective-permute-start(bf16[320,384]{1,0:T(8,128)(2,1)S(1)} %add_convert_fusion.3.refs_15_), channel_id=1, source_target_pairs={{0,1},{1,0},{2,3},{3,2},{4,5},{5,4},{6,7},{7,6},{8,9},{9,8},{10,11... | collective-permute-start | bytes 737288 | tf_op jit(solution)/shard_map/ppermute | solution.py:296
  107.3 2.7 %collective-permute-done.34.refs_12_ = bf16[320,384]{1,0:T(8,128)(2,1)S(1)} collective-permute-done((bf16[320,384]{1,0:T(8,128)(2,1)S(1)}, bf16[320,384]{1,0:T(8,128)(2,1)S(1)}, u32[]{:S(2)}, u32[]{:S(2)}) %collective-permute-start.34) | collective-permute-done | bytes 245792 | tf_op jit(solution)/shard_map/ppermute | solution.py:296
  111.5 4.8 %collective-permute-start.38 = (bf16[320,384]{1,0:T(8,128)(2,1)}, bf16[320,384]{1,0:T(8,128)(2,1)}, u32[]{:S(2)}, u32[]{:S(2)}) collective-permute-start(bf16[320,384]{1,0:T(8,128)(2,1)} %add_convert_fusion.1), channel_id=1, source_target_pairs={{0,1},{1,0},{2,3},{3,2},{4,5},{5,4},{6,7},{7,6},{8,9},{9,8},{10,11... | collective-permute-start | bytes 737288 | tf_op jit(solution)/shard_map/ppermute | solution.py:296
  116.4 3.6 %shard_map.74 = bf16[512,640]{1,0:T(8,128)(2,1)} custom-call(s32[2]{0:T(128)S(1)} %pad_add_fusion.idx_ref, bf16[512,384]{1,0:T(8,128)(2,1)S(1)} %copy-done.16, bf16[512,384]{1,0:T(8,128)(2,1)S(1)} %collective-permute-done.10.refs_1_, bf16[512,384]{1,0:T(8,128)(2,1)S(1)} %collective-permute-done.35.refs_2_, ...), custom_call_target="tpu_custom_call" | custom-call | tf_op jit(solution)/shard_map/pallas_call | solution.py:187
  121.2 0.9 copy-done.11
  122.1 0.9 copy-done.18
  123.0 2.2 %shard_map.75.b = f32[5,640,384]{2,1,0:T(8,128)} custom-call(s32[1]{0:T(128)} %bitcast.7.end_ref.end, bf16[320,384]{1,0:T(8,128)(2,1)S(1)} %collective-permute-done.21.refs_0_, bf16[320,384]{1,0:T(8,128)(2,1)S(1)} %add_convert_fusion.24.refs_1_, bf16[320,384]{1,0:T(8,128)(2,1)S(1)} %collective-permute-done.19.refs_2_, ...), custom_call_target="tpu_custom_call" | custom-call | tf_op jit(solution)/shard_map/pallas_call | solution.py:228
  125.3 1.9 %collective-permute-done.39 = bf16[320,384]{1,0:T(8,128)(2,1)} collective-permute-done((bf16[320,384]{1,0:T(8,128)(2,1)}, bf16[320,384]{1,0:T(8,128)(2,1)}, u32[]{:S(2)}, u32[]{:S(2)}) %collective-permute-start.39) | collective-permute-done | bytes 245792 | tf_op jit(solution)/shard_map/ppermute | solution.py:296
  127.2 1.1 broadcast_select_fusion
  128.4 1.0 shard_map.76
  (119 shorter events, 17.0 us)
Async XLA Ops:
  0.6 10.9 %collective-permute-start.1 = (bf16[320,1024]{1,0:T(8,128)(2,1)}, bf16[320,1024]{1,0:T(8,128)(2,1)S(1)}, u32[]{:S(2)}, u32[]{:S(2)}) collective-permute-start(bf16[320,1024]{1,0:T(8,128)(2,1)} %bitcast.9), channel_id=1, source_target_pairs={{0,4},{4,0},{8,12},{12,8},{1,5},{5,1},{9,13},{13,9},{2,6},{6,2},{1... | collective-permute-start | bytes 1966088 | tf_op jit(solution)/shard_map/ppermute | solution.py:26
  1.1 18.7 %collective-permute-start = (bf16[320,1024]{1,0:T(8,128)(2,1)}, bf16[320,1024]{1,0:T(8,128)(2,1)S(1)}, u32[]{:S(2)}, u32[]{:S(2)}) collective-permute-start(bf16[320,1024]{1,0:T(8,128)(2,1)} %bitcast.10), channel_id=1, source_target_pairs={{0,8},{4,12},{8,0},{12,4},{1,9},{5,13},{9,1},{13,5},{2,10},{6,14},... | collective-permute-start | bytes 1966088 | tf_op jit(solution)/shard_map/ppermute | solution.py:26
  4.9 17.0 %copy-start.14 = (bf16[1,512,384]{2,1,0:T(8,128)(2,1)S(1)}, bf16[1,512,384]{2,1,0:T(8,128)(2,1)}, u32[]{:S(2)}) copy-start(bf16[1,512,384]{2,1,0:T(8,128)(2,1)} %param.9) | copy-start | bytes 1179652
  5.0 3.8 %collective-permute-start.2 = (f32[8,384]{1,0:T(8,128)S(1)}, f32[8,384]{1,0:T(8,128)S(1)}, u32[]{:S(2)}, u32[]{:S(2)}) collective-permute-start(f32[8,384]{1,0:T(8,128)S(1)} %shard_map.68), channel_id=1, source_target_pairs={{0,16},{16,0},{1,17},{17,1},{2,18},{18,2},{3,19},{19,3},{4,20},{20... | collective-permute-start | bytes 36872 | tf_op jit(solution)/shard_map/ppermute | solution.py:26
  8.9 10.5 %collective-permute-start.5 = (f32[8,384]{1,0:T(8,128)S(1)}, f32[8,384]{1,0:T(8,128)S(1)}, u32[]{:S(2)}, u32[]{:S(2)}) collective-permute-start(f32[8,384]{1,0:T(8,128)S(1)} %maximum_maximum_fusion.refs_2_.refs_4_), channel_id=1, source_target_pairs={{0,12},{4,8},{8,4},{12,0},{1,13},{5,9},{9,5},{13,1},{2,14},{6,10},... | collective-permute-start | bytes 36872 | tf_op jit(solution)/shard_map/ppermute | solution.py:26
  8.9 10.9 %collective-permute-start.4 = (f32[8,384]{1,0:T(8,128)S(1)}, f32[8,384]{1,0:T(8,128)S(1)}, u32[]{:S(2)}, u32[]{:S(2)}) collective-permute-start(f32[8,384]{1,0:T(8,128)S(1)} %maximum_maximum_fusion.refs_2_.refs_4_), channel_id=1, source_target_pairs={{0,8},{4,12},{8,0},{12,4},{1,9},{5,13},{9,1},{13,5},{2,10},{6,14},... | collective-permute-start | bytes 36872 | tf_op jit(solution)/shard_map/ppermute | solution.py:26
  9.8 1.8 %collective-permute-start.3 = (f32[8,384]{1,0:T(8,128)S(1)}, f32[8,384]{1,0:T(8,128)S(1)}, u32[]{:S(2)}, u32[]{:S(2)}) collective-permute-start(f32[8,384]{1,0:T(8,128)S(1)} %maximum_maximum_fusion.refs_2_.refs_4_), channel_id=1, source_target_pairs={{0,4},{4,0},{8,12},{12,8},{1,5},{5,1},{9,13},{13,9},{2,6},{6,2},{1... | collective-permute-start | bytes 36872 | tf_op jit(solution)/shard_map/ppermute | solution.py:26
  15.1 6.9 %copy-start.7 = (bf16[320,1024]{1,0:T(8,128)(2,1)}, bf16[320,1024]{1,0:T(8,128)(2,1)S(1)}, u32[]{:S(2)}) copy-start(bf16[320,1024]{1,0:T(8,128)(2,1)S(1)} %collective-permute-done.1.refs_1_.refs_2_) | copy-start | bytes 1966084
  15.1 6.9 %copy-start.1 = (bf16[5,1280,384]{2,1,0:T(8,128)(2,1)S(1)}, bf16[5,1280,384]{2,1,0:T(8,128)(2,1)}, u32[]{:S(2)}) copy-start(bf16[5,1280,384]{2,1,0:T(8,128)(2,1)} %refs_8_.2) | copy-start | bytes 14745604
  15.1 6.9 %copy-start.6 = (bf16[1,1024,320]{1,2,0:T(8,128)(2,1)S(1)}, bf16[1,1024,320]{1,2,0:T(8,128)(2,1)}, u32[]{:S(2)}) copy-start(bf16[1,1024,320]{1,2,0:T(8,128)(2,1)} %param.5) | copy-start | bytes 1966084
  19.8 2.1 %collective-permute-start.6 = (bf16[320,1024]{1,0:T(8,128)(2,1)S(1)}, bf16[320,1024]{1,0:T(8,128)(2,1)S(1)}, u32[]{:S(2)}, u32[]{:S(2)}) collective-permute-start(bf16[320,1024]{1,0:T(8,128)(2,1)S(1)} %collective-permute-done.refs_1_), channel_id=1, source_target_pairs={{0,4},{4,0},{8,12},{12,8},{1,5},{5,1},{9,13},{13,9},{2,6},{6,2},{1... | collective-permute-start | bytes 1966088 | tf_op jit(solution)/shard_map/ppermute | solution.py:26
  30.3 4.8 %copy-start.15 = (bf16[512,384]{1,0:T(8,128)(2,1)}, bf16[512,384]{1,0:T(8,128)(2,1)S(1)}, u32[]{:S(2)}) copy-start(bf16[512,384]{1,0:T(8,128)(2,1)S(1)} %get-tuple-element.113.refs_0_) | copy-start | bytes 1179652
  30.3 8.1 %collective-permute-start.7 = (bf16[320,384]{1,0:T(8,128)(2,1)S(1)}, bf16[320,384]{1,0:T(8,128)(2,1)S(1)}, u32[]{:S(2)}, u32[]{:S(2)}) collective-permute-start(bf16[320,384]{1,0:T(8,128)(2,1)S(1)} %get-tuple-element.67), channel_id=1, source_target_pairs={{0,16},{16,0},{1,17},{17,1},{2,18},{18,2},{3,19},{19,3},{4,20},{20... | collective-permute-start | bytes 737288 | tf_op jit(solution)/shard_map/ppermute | solution.py:26
  36.3 13.3 %collective-permute-start.9 = (bf16[320,384]{1,0:T(8,128)(2,1)}, bf16[320,384]{1,0:T(8,128)(2,1)}, u32[]{:S(2)}, u32[]{:S(2)}) collective-permute-start(bf16[320,384]{1,0:T(8,128)(2,1)} %get-tuple-element.68), channel_id=1, source_target_pairs={{0,16},{16,0},{1,17},{17,1},{2,18},{18,2},{3,19},{19,3},{4,20},{20... | collective-permute-start | bytes 737288 | tf_op jit(solution)/shard_map/ppermute | solution.py:26
  39.2 11.9 %collective-permute-start.8 = (bf16[320,384]{1,0:T(8,128)(2,1)}, bf16[320,384]{1,0:T(8,128)(2,1)}, u32[]{:S(2)}, u32[]{:S(2)}) collective-permute-start(bf16[320,384]{1,0:T(8,128)(2,1)} %add_convert_fusion.29), channel_id=1, source_target_pairs={{0,1},{1,0},{2,3},{3,2},{4,5},{5,4},{6,7},{7,6},{8,9},{9,8},{10,11... | collective-permute-start | bytes 737288 | tf_op jit(solution)/shard_map/ppermute | solution.py:296
  41.0 13.3 %collective-permute-start.10 = (bf16[512,384]{1,0:T(8,128)(2,1)}, bf16[512,384]{1,0:T(8,128)(2,1)S(1)}, u32[]{:S(2)}, u32[]{:S(2)}) collective-permute-start(bf16[512,384]{1,0:T(8,128)(2,1)} %copy-done.15), channel_id=1, source_target_pairs={{0,8},{4,12},{8,0},{12,4},{1,9},{5,13},{9,1},{13,5},{2,10},{6,14},... | collective-permute-start | bytes 1179656 | tf_op jit(solution)/shard_map/ppermute | solution.py:26
  47.4 10.8 %collective-permute-start.11 = (bf16[320,384]{1,0:T(8,128)(2,1)S(1)}, bf16[320,384]{1,0:T(8,128)(2,1)S(1)}, u32[]{:S(2)}, u32[]{:S(2)}) collective-permute-start(bf16[320,384]{1,0:T(8,128)(2,1)S(1)} %get-tuple-element.77), channel_id=1, source_target_pairs={{0,16},{16,0},{1,17},{17,1},{2,18},{18,2},{3,19},{19,3},{4,20},{20... | collective-permute-start | bytes 737288 | tf_op jit(solution)/shard_map/ppermute | solution.py:26
  49.5 14.2 %collective-permute-start.17 = (bf16[320,384]{1,0:T(8,128)(2,1)S(1)}, bf16[320,384]{1,0:T(8,128)(2,1)S(1)}, u32[]{:S(2)}, u32[]{:S(2)}) collective-permute-start(bf16[320,384]{1,0:T(8,128)(2,1)S(1)} %get-tuple-element.85), channel_id=1, source_target_pairs={{0,16},{16,0},{1,17},{17,1},{2,18},{18,2},{3,19},{19,3},{4,20},{20... | collective-permute-start | bytes 737288 | tf_op jit(solution)/shard_map/ppermute | solution.py:26
  50.6 12.2 %collective-permute-start.14 = (bf16[320,384]{1,0:T(8,128)(2,1)S(1)}, bf16[320,384]{1,0:T(8,128)(2,1)S(1)}, u32[]{:S(2)}, u32[]{:S(2)}) collective-permute-start(bf16[320,384]{1,0:T(8,128)(2,1)S(1)} %add_convert_fusion.28), channel_id=1, source_target_pairs={{0,1},{1,0},{2,3},{3,2},{4,5},{5,4},{6,7},{7,6},{8,9},{9,8},{10,11... | collective-permute-start | bytes 737288 | tf_op jit(solution)/shard_map/ppermute | solution.py:296
  51.1 21.1 %collective-permute-start.13 = (bf16[640,384]{1,0:T(8,128)(2,1)S(1)}, bf16[640,384]{1,0:T(8,128)(2,1)S(1)}, u32[]{:S(2)}, u32[]{:S(2)}) collective-permute-start(bf16[640,384]{1,0:T(8,128)(2,1)S(1)} %get-tuple-element.83), channel_id=1, source_target_pairs={{0,16},{16,0},{1,17},{17,1},{2,18},{18,2},{3,19},{19,3},{4,20},{20... | collective-permute-start | bytes 1474568 | tf_op jit(solution)/shard_map/ppermute | solution.py:26
  54.2 9.3 %collective-permute-start.18 = (bf16[320,384]{1,0:T(8,128)(2,1)S(1)}, bf16[320,384]{1,0:T(8,128)(2,1)S(1)}, u32[]{:S(2)}, u32[]{:S(2)}) collective-permute-start(bf16[320,384]{1,0:T(8,128)(2,1)S(1)} %add_convert_fusion.27), channel_id=1, source_target_pairs={{1,2},{2,1},{5,6},{6,5},{9,10},{10,9},{13,14},{14,13},{17,18},{18,... | collective-permute-start | bytes 737288 | tf_op jit(solution)/shard_map/ppermute | solution.py:302
  58.3 10.2 %collective-permute-start.16 = (bf16[320,384]{1,0:T(8,128)(2,1)S(1)}, bf16[320,384]{1,0:T(8,128)(2,1)S(1)}, u32[]{:S(2)}, u32[]{:S(2)}) collective-permute-start(bf16[320,384]{1,0:T(8,128)(2,1)S(1)} %add_convert_fusion.26), channel_id=1, source_target_pairs={{0,1},{1,0},{2,3},{3,2},{4,5},{5,4},{6,7},{7,6},{8,9},{9,8},{10,11... | collective-permute-start | bytes 737288 | tf_op jit(solution)/shard_map/ppermute | solution.py:296
  62.9 6.4 %collective-permute-start.15 = (bf16[320,384]{1,0:T(8,128)(2,1)S(1)}, bf16[320,384]{1,0:T(8,128)(2,1)S(1)}, u32[]{:S(2)}, u32[]{:S(2)}) collective-permute-start(bf16[320,384]{1,0:T(8,128)(2,1)S(1)} %add_convert_fusion.25), channel_id=1, source_target_pairs={{1,2},{2,1},{5,6},{6,5},{9,10},{10,9},{13,14},{14,13},{17,18},{18,... | collective-permute-start | bytes 737288 | tf_op jit(solution)/shard_map/ppermute | solution.py:302
  63.6 19.3 %collective-permute-start.12 = (bf16[640,384]{1,0:T(8,128)(2,1)S(1)}, bf16[640,384]{1,0:T(8,128)(2,1)S(1)}, u32[]{:S(2)}, u32[]{:S(2)}) collective-permute-start(bf16[640,384]{1,0:T(8,128)(2,1)S(1)} %get-tuple-element.80), channel_id=1, source_target_pairs={{0,16},{16,0},{1,17},{17,1},{2,18},{18,2},{3,19},{19,3},{4,20},{20... | collective-permute-start | bytes 1474568 | tf_op jit(solution)/shard_map/ppermute | solution.py:26
  63.9 10.2 %collective-permute-start.21 = (bf16[320,384]{1,0:T(8,128)(2,1)S(1)}, bf16[320,384]{1,0:T(8,128)(2,1)S(1)}, u32[]{:S(2)}, u32[]{:S(2)}) collective-permute-start(bf16[320,384]{1,0:T(8,128)(2,1)S(1)} %broadcast_select_fusion.8), channel_id=1, source_target_pairs={{0,1},{1,0},{2,3},{3,2},{4,5},{5,4},{6,7},{7,6},{8,9},{9,8},{10,11... | collective-permute-start | bytes 737288 | tf_op jit(solution)/shard_map/ppermute | solution.py:296
  68.6 6.3 %collective-permute-start.20 = (bf16[320,384]{1,0:T(8,128)(2,1)S(1)}, bf16[320,384]{1,0:T(8,128)(2,1)S(1)}, u32[]{:S(2)}, u32[]{:S(2)}) collective-permute-start(bf16[320,384]{1,0:T(8,128)(2,1)S(1)} %add_convert_fusion.22), channel_id=1, source_target_pairs={{1,2},{2,1},{5,6},{6,5},{9,10},{10,9},{13,14},{14,13},{17,18},{18,... | collective-permute-start | bytes 737288 | tf_op jit(solution)/shard_map/ppermute | solution.py:302
  72.4 7.7 %collective-permute-start.19 = (bf16[320,384]{1,0:T(8,128)(2,1)S(1)}, bf16[320,384]{1,0:T(8,128)(2,1)S(1)}, u32[]{:S(2)}, u32[]{:S(2)}) collective-permute-start(bf16[320,384]{1,0:T(8,128)(2,1)S(1)} %broadcast_select_fusion.7), channel_id=1, source_target_pairs={{0,1},{1,0},{2,3},{3,2},{4,5},{5,4},{6,7},{7,6},{8,9},{9,8},{10,11... | collective-permute-start | bytes 737288 | tf_op jit(solution)/shard_map/ppermute | solution.py:296
  74.2 8.8 %collective-permute-start.24 = (bf16[320,384]{1,0:T(8,128)(2,1)S(1)}, bf16[320,384]{1,0:T(8,128)(2,1)S(1)}, u32[]{:S(2)}, u32[]{:S(2)}) collective-permute-start(bf16[320,384]{1,0:T(8,128)(2,1)S(1)} %add_convert_fusion.19), channel_id=1, source_target_pairs={{1,2},{2,1},{5,6},{6,5},{9,10},{10,9},{13,14},{14,13},{17,18},{18,... | collective-permute-start | bytes 737288 | tf_op jit(solution)/shard_map/ppermute | solution.py:302
  75.1 11.3 %collective-permute-start.23 = (bf16[320,384]{1,0:T(8,128)(2,1)S(1)}, bf16[320,384]{1,0:T(8,128)(2,1)S(1)}, u32[]{:S(2)}, u32[]{:S(2)}) collective-permute-start(bf16[320,384]{1,0:T(8,128)(2,1)S(1)} %broadcast_select_fusion.6), channel_id=1, source_target_pairs={{0,1},{1,0},{2,3},{3,2},{4,5},{5,4},{6,7},{7,6},{8,9},{9,8},{10,11... | collective-permute-start | bytes 737288 | tf_op jit(solution)/shard_map/ppermute | solution.py:296
  80.2 18.5 %copy-start.16 = (bf16[512,384]{1,0:T(8,128)(2,1)S(1)}, bf16[512,384]{1,0:T(8,128)(2,1)}, u32[]{:S(2)}) copy-start(bf16[512,384]{1,0:T(8,128)(2,1)} %copy-done.15) | copy-start | bytes 1179652
  80.2 6.9 %collective-permute-start.22 = (bf16[320,384]{1,0:T(8,128)(2,1)S(1)}, bf16[320,384]{1,0:T(8,128)(2,1)S(1)}, u32[]{:S(2)}, u32[]{:S(2)}) collective-permute-start(bf16[320,384]{1,0:T(8,128)(2,1)S(1)} %add_convert_fusion.16), channel_id=1, source_target_pairs={{1,2},{2,1},{5,6},{6,5},{9,10},{10,9},{13,14},{14,13},{17,18},{18,... | collective-permute-start | bytes 737288 | tf_op jit(solution)/shard_map/ppermute | solution.py:302
  81.0 12.1 %collective-permute-start.26 = (bf16[640,384]{1,0:T(8,128)(2,1)S(1)}, bf16[640,384]{1,0:T(8,128)(2,1)S(1)}, u32[]{:S(2)}, u32[]{:S(2)}) collective-permute-start(bf16[640,384]{1,0:T(8,128)(2,1)S(1)} %get-tuple-element.101), channel_id=1, source_target_pairs={{0,16},{16,0},{1,17},{17,1},{2,18},{18,2},{3,19},{19,3},{4,20},{20... | collective-permute-start | bytes 1474568 | tf_op jit(solution)/shard_map/ppermute | solution.py:26
  83.1 9.2 %collective-permute-start.28 = (bf16[320,384]{1,0:T(8,128)(2,1)S(1)}, bf16[320,384]{1,0:T(8,128)(2,1)S(1)}, u32[]{:S(2)}, u32[]{:S(2)}) collective-permute-start(bf16[320,384]{1,0:T(8,128)(2,1)S(1)} %broadcast_select_fusion.5), channel_id=1, source_target_pairs={{0,1},{1,0},{2,3},{3,2},{4,5},{5,4},{6,7},{7,6},{8,9},{9,8},{10,11... | collective-permute-start | bytes 737288 | tf_op jit(solution)/shard_map/ppermute | solution.py:296
  86.4 6.6 %collective-permute-start.27 = (bf16[320,384]{1,0:T(8,128)(2,1)S(1)}, bf16[320,384]{1,0:T(8,128)(2,1)S(1)}, u32[]{:S(2)}, u32[]{:S(2)}) collective-permute-start(bf16[320,384]{1,0:T(8,128)(2,1)S(1)} %add_convert_fusion.13), channel_id=1, source_target_pairs={{1,2},{2,1},{5,6},{6,5},{9,10},{10,9},{13,14},{14,13},{17,18},{18,... | collective-permute-start | bytes 737288 | tf_op jit(solution)/shard_map/ppermute | solution.py:302
  87.3 29.1 %copy-start.9 = (bf16[1536,640]{1,0:T(8,128)(2,1)S(1)}, bf16[1536,640]{1,0:T(8,128)(2,1)}, u32[]{:S(2)}) copy-start(bf16[1536,640]{1,0:T(8,128)(2,1)} %refs_8_.3) | copy-start | bytes 5898244
  87.3 10.6 %collective-permute-start.25 = (bf16[320,384]{1,0:T(8,128)(2,1)S(1)}, bf16[320,384]{1,0:T(8,128)(2,1)S(1)}, u32[]{:S(2)}, u32[]{:S(2)}) collective-permute-start(bf16[320,384]{1,0:T(8,128)(2,1)S(1)} %broadcast_select_fusion.4), channel_id=1, source_target_pairs={{0,1},{1,0},{2,3},{3,2},{4,5},{5,4},{6,7},{7,6},{8,9},{9,8},{10,11... | collective-permute-start | bytes 737288 | tf_op jit(solution)/shard_map/ppermute | solution.py:296
  92.4 6.9 %collective-permute-start.31 = (bf16[320,384]{1,0:T(8,128)(2,1)S(1)}, bf16[320,384]{1,0:T(8,128)(2,1)S(1)}, u32[]{:S(2)}, u32[]{:S(2)}) collective-permute-start(bf16[320,384]{1,0:T(8,128)(2,1)S(1)} %add_convert_fusion.10), channel_id=1, source_target_pairs={{1,2},{2,1},{5,6},{6,5},{9,10},{10,9},{13,14},{14,13},{17,18},{18,... | collective-permute-start | bytes 737288 | tf_op jit(solution)/shard_map/ppermute | solution.py:302
  93.3 9.9 %collective-permute-start.30 = (bf16[320,384]{1,0:T(8,128)(2,1)S(1)}, bf16[320,384]{1,0:T(8,128)(2,1)S(1)}, u32[]{:S(2)}, u32[]{:S(2)}) collective-permute-start(bf16[320,384]{1,0:T(8,128)(2,1)S(1)} %broadcast_select_fusion.3), channel_id=1, source_target_pairs={{0,1},{1,0},{2,3},{3,2},{4,5},{5,4},{6,7},{7,6},{8,9},{9,8},{10,11... | collective-permute-start | bytes 737288 | tf_op jit(solution)/shard_map/ppermute | solution.py:296
  98.0 6.0 %collective-permute-start.29 = (bf16[320,384]{1,0:T(8,128)(2,1)S(1)}, bf16[320,384]{1,0:T(8,128)(2,1)S(1)}, u32[]{:S(2)}, u32[]{:S(2)}) collective-permute-start(bf16[320,384]{1,0:T(8,128)(2,1)S(1)} %add_convert_fusion.7), channel_id=1, source_target_pairs={{1,2},{2,1},{5,6},{6,5},{9,10},{10,9},{13,14},{14,13},{17,18},{18,... | collective-permute-start | bytes 737288 | tf_op jit(solution)/shard_map/ppermute | solution.py:302
  98.7 17.7 %collective-permute-start.35 = (bf16[512,384]{1,0:T(8,128)(2,1)S(1)}, bf16[512,384]{1,0:T(8,128)(2,1)S(1)}, u32[]{:S(2)}, u32[]{:S(2)}) collective-permute-start(bf16[512,384]{1,0:T(8,128)(2,1)S(1)} %copy-done.16), channel_id=1, source_target_pairs={{0,4},{4,0},{8,12},{12,8},{1,5},{5,1},{9,13},{13,9},{2,6},{6,2},{1... | collective-permute-start | bytes 1179656 | tf_op jit(solution)/shard_map/ppermute | solution.py:26
  98.8 17.6 %collective-permute-start.36 = (bf16[512,384]{1,0:T(8,128)(2,1)S(1)}, bf16[512,384]{1,0:T(8,128)(2,1)S(1)}, u32[]{:S(2)}, u32[]{:S(2)}) collective-permute-start(bf16[512,384]{1,0:T(8,128)(2,1)S(1)} %collective-permute-done.10.refs_1_), channel_id=1, source_target_pairs={{0,4},{4,0},{8,12},{12,8},{1,5},{5,1},{9,13},{13,9},{2,6},{6,2},{1... | collective-permute-start | bytes 1179656 | tf_op jit(solution)/shard_map/ppermute | solution.py:26
  99.5 10.5 %collective-permute-start.34 = (bf16[320,384]{1,0:T(8,128)(2,1)S(1)}, bf16[320,384]{1,0:T(8,128)(2,1)S(1)}, u32[]{:S(2)}, u32[]{:S(2)}) collective-permute-start(bf16[320,384]{1,0:T(8,128)(2,1)S(1)} %broadcast_select_fusion.2), channel_id=1, source_target_pairs={{0,1},{1,0},{2,3},{3,2},{4,5},{5,4},{6,7},{7,6},{8,9},{9,8},{10,11... | collective-permute-start | bytes 737288 | tf_op jit(solution)/shard_map/ppermute | solution.py:296
  103.3 7.4 %collective-permute-start.33 = (bf16[320,384]{1,0:T(8,128)(2,1)S(1)}, bf16[320,384]{1,0:T(8,128)(2,1)S(1)}, u32[]{:S(2)}, u32[]{:S(2)}) collective-permute-start(bf16[320,384]{1,0:T(8,128)(2,1)S(1)} %add_convert_fusion.4), channel_id=1, source_target_pairs={{1,2},{2,1},{5,6},{6,5},{9,10},{10,9},{13,14},{14,13},{17,18},{18,... | collective-permute-start | bytes 737288 | tf_op jit(solution)/shard_map/ppermute | solution.py:302
  104.1 12.3 %collective-permute-start.32 = (bf16[320,384]{1,0:T(8,128)(2,1)S(1)}, bf16[320,384]{1,0:T(8,128)(2,1)S(1)}, u32[]{:S(2)}, u32[]{:S(2)}) collective-permute-start(bf16[320,384]{1,0:T(8,128)(2,1)S(1)} %add_convert_fusion.3.refs_15_), channel_id=1, source_target_pairs={{0,1},{1,0},{2,3},{3,2},{4,5},{5,4},{6,7},{7,6},{8,9},{9,8},{10,11... | collective-permute-start | bytes 737288 | tf_op jit(solution)/shard_map/ppermute | solution.py:296
  110.0 10.0 %copy-start.10 = (bf16[320,384]{1,0:T(8,128)(2,1)}, bf16[320,384]{1,0:T(8,128)(2,1)S(1)}, u32[]{:S(2)}) copy-start(bf16[320,384]{1,0:T(8,128)(2,1)S(1)} %collective-permute-done.34.refs_12_) | copy-start | bytes 737284
  110.1 9.9 %collective-permute-start.37 = (bf16[320,384]{1,0:T(8,128)(2,1)S(1)}, bf16[320,384]{1,0:T(8,128)(2,1)S(1)}, u32[]{:S(2)}, u32[]{:S(2)}) collective-permute-start(bf16[320,384]{1,0:T(8,128)(2,1)S(1)} %add_convert_fusion.2), channel_id=1, source_target_pairs={{1,2},{2,1},{5,6},{6,5},{9,10},{10,9},{13,14},{14,13},{17,18},{18,... | collective-permute-start | bytes 737288 | tf_op jit(solution)/shard_map/ppermute | solution.py:302
  111.5 13.8 %collective-permute-start.38 = (bf16[320,384]{1,0:T(8,128)(2,1)}, bf16[320,384]{1,0:T(8,128)(2,1)}, u32[]{:S(2)}, u32[]{:S(2)}) collective-permute-start(bf16[320,384]{1,0:T(8,128)(2,1)} %add_convert_fusion.1), channel_id=1, source_target_pairs={{0,1},{1,0},{2,3},{3,2},{4,5},{5,4},{6,7},{7,6},{8,9},{9,8},{10,11... | collective-permute-start | bytes 737288 | tf_op jit(solution)/shard_map/ppermute | solution.py:296
  120.7 6.5 %collective-permute-start.39 = (bf16[320,384]{1,0:T(8,128)(2,1)}, bf16[320,384]{1,0:T(8,128)(2,1)}, u32[]{:S(2)}, u32[]{:S(2)}) collective-permute-start(bf16[320,384]{1,0:T(8,128)(2,1)} %add_convert_fusion), channel_id=1, source_target_pairs={{0,1},{1,0},{2,3},{3,2},{4,5},{5,4},{6,7},{7,6},{8,9},{9,8},{10,11... | collective-permute-start | bytes 737288 | tf_op jit(solution)/shard_map/ppermute | solution.py:296
  (11 other events, 15.7 us)
